TPU v7x, 32 devices: a whole 2x2x4 slice. The times are simulated.
32 devices in a mesh: pipe: 2 (over y), seq: 4 (over x, core), dp: 4 (over z).
Axes of the slice: x: 2, y: 2, z: 4, core: 2. Of those that a mesh axis runs over, the one named last changes fastest.
Arguments:
- incoming: bfloat16 [2, 3, 4, 512, 1536], P('pipe', None, 'dp', 'seq'), may hold values from -9 to 9, as said below
- contacts: int32 [4, 4, 512], P(None, 'dp', 'seq'), may hold values from 0 to 15
- keyframes: int32 [4, 4, 512], P(None, 'dp'), may hold values 0 or 1
- timesteps: int32 [4, 4], P(None, 'dp'), may hold values from 0 to 999
- w_query: bfloat16 [2, 1536, 1536], P('pipe', ('seq', 'dp')), may hold values from -1 to 1, as said below
- w_keyval: bfloat16 [2, 1536, 1536], P('pipe', ('seq', 'dp')), may hold values from -1 to 1, as said below
- norm_gain: float32 [2, 1536], P('pipe'), may hold values from 0.5 to 1.5
- time_freq: float32 [2, 1536], P('pipe'), may hold values from 0.0005 to 0.05
- contact_table: bfloat16 [2, 16, 1536], P('pipe'), may hold values from -3 to 3
- key_bias: float32 [2, 16], P('pipe'), may hold values from 0.5 to 4
- attn_gate: float32 [2, 1536], P('pipe'), may hold values from 1 to 4
- head_cotangent: bfloat16 [2, 3, 4, 512, 256], P('pipe', None, 'dp', 'seq'), may hold values from -6 to 6
Outputs:
- section_out: bfloat16 [2, 3, 4, 512, 1536], P('pipe', None, 'dp', 'seq')
- head_grad: float32 [2, 1536, 256], P('pipe', ('seq', 'dp'))
Inputs may be any that keep to these rules, and one draw needn't show every extreme that they name: `contacts`: each frame's contact state, four limbs as bits. `incoming`: activations of order one. `w_query`: entries of about 1536 ** -0.5. `w_keyval`: entries of about 1536 ** -0.5.
All inputs are finite; a program needn't handle non-finite values. No bound on the sum of `keyframes` on one device may be relied on, other than what follows from the above.
Results may differ from a plain program's by a relative error of at most 0.014.
Values may be sent and summed in bfloat16 or wider, within the bound.
No kernel may reach another device: no remote copies, remote signals or barrier semaphores. Data moves between devices by JAX's collectives and lax.ppermute only.
A program may use at most 64 MiB of HBM per device.

v0:
```python
import jax
import jax.numpy as jnp
from jax import lax
from jax.sharding import PartitionSpec as P

epsilon = 1e-06


def passed_along(value, axis, steps):
    count = lax.axis_size(axis)
    first, last = (max(0, -steps), min(count, count - steps))
    return lax.ppermute(value, axis, [(source, source + steps) for source in range(first, last)])


def body(
    incoming,
    contacts,
    keyframes,
    timesteps,
    w_query,
    w_keyval,
    norm_gain,
    time_freq,
    contact_table,
    key_bias,
    attn_gate,
    head_cotangent,
):
    section_idx = lax.axis_index("pipe")
    seq_idx = lax.axis_index("seq")
    seq_count = lax.axis_size("seq")
    section_count = lax.axis_size("pipe")
    rep_count = lax.axis_size("dp")
    tok_rows = incoming.shape[3]
    width = incoming.shape[4]
    turns = incoming.shape[1]
    frames = tok_rows * seq_count
    heads_all = key_bias.shape[1]
    head_size = width // heads_all
    heads_local = heads_all // seq_count
    kv_width = w_keyval.shape[2]
    kv_local = kv_width // (2 * head_size * seq_count)
    group_size = heads_local // kv_local
    feat_count = head_cotangent.shape[4]
    score_scale = head_size ** (-0.5)
    gathered = (
        lax.all_gather(w_query, ("seq", "dp"), axis=1, tiled=True),
        lax.all_gather(w_keyval, ("seq", "dp"), axis=1, tiled=True),
    )
    wquery = gathered[0][0]
    wkeyval = gathered[1][0]
    gain_row = norm_gain[0]
    freq_row = time_freq[0]
    table = contact_table[0]
    gate_row = attn_gate[0]
    bias_local = lax.dynamic_slice_in_dim(key_bias[0], seq_idx * heads_local, heads_local)
    contact_all = contacts[:, 0, :]
    key_all = keyframes[:, 0, :]
    step_all = timesteps[:, 0]
    labels = jnp.arange(table.shape[0], dtype=jnp.int32)
    outputs = []
    handed = None
    for turn in range(turns):
        fresh_rows = incoming[0, turn, 0]
        if turn == 0:
            current = fresh_rows
        else:
            current = jnp.where(section_idx == 0, fresh_rows, handed)
        batch_idx = turn - section_idx + section_count - 1
        contact_rows = lax.dynamic_index_in_dim(contact_all, batch_idx, 0, keepdims=False)
        key_flags = lax.dynamic_index_in_dim(key_all, batch_idx, 0, keepdims=False).astype(
            jnp.float32
        )
        timestep = lax.dynamic_index_in_dim(step_all, batch_idx, 0, keepdims=False).astype(
            jnp.float32
        )
        onehot = (contact_rows[:, None] == labels[None, :]).astype(jnp.bfloat16)
        embedded = jnp.dot(onehot, table, preferred_element_type=jnp.float32)
        hidden = current.astype(jnp.float32) + embedded
        root_mean = jnp.sqrt(jnp.mean(hidden * hidden, axis=-1, keepdims=True) + epsilon)
        modulation = gain_row * (1.0 + 0.5 * jnp.sin(timestep * freq_row))
        normed = (hidden / root_mean * modulation[None, :]).astype(jnp.bfloat16)
        queries = jnp.dot(normed, wquery, preferred_element_type=jnp.float32).astype(jnp.bfloat16)
        keyval = jnp.dot(normed, wkeyval, preferred_element_type=jnp.float32).astype(jnp.bfloat16)
        query_parts = queries.reshape(tok_rows, seq_count, width // seq_count)
        keyval_parts = keyval.reshape(tok_rows, seq_count, kv_width // seq_count)
        regrouped = (
            lax.all_to_all(query_parts, "seq", split_axis=1, concat_axis=0, tiled=True),
            lax.all_to_all(keyval_parts, "seq", split_axis=1, concat_axis=0, tiled=True),
        )
        query_heads = regrouped[0].reshape(frames, heads_local, head_size)
        keyval_heads = regrouped[1].reshape(frames, kv_local, 2, head_size)
        head_outputs = []
        for head in range(heads_local):
            key_rows = keyval_heads[:, head // group_size, 0]
            value_rows = keyval_heads[:, head // group_size, 1]
            scores = (
                lax.dot_general(
                    query_heads[:, head],
                    key_rows,
                    (((1,), (1,)), ((), ())),
                    preferred_element_type=jnp.float32,
                )
                * score_scale
            )
            scores = scores + bias_local[head] * key_flags[None, :]
            row_max = jnp.max(scores, axis=-1, keepdims=True)
            exponent = jnp.exp(scores - row_max)
            probabilities = (exponent / jnp.sum(exponent, axis=-1, keepdims=True)).astype(
                jnp.bfloat16
            )
            head_outputs.append(
                jnp.dot(probabilities, value_rows, preferred_element_type=jnp.float32).astype(
                    jnp.bfloat16
                )
            )
        attended = jnp.stack(head_outputs, axis=1).reshape(frames, heads_local * head_size)
        returned = lax.all_to_all(attended, "seq", split_axis=0, concat_axis=1, tiled=True)
        output = (hidden + gate_row[None, :] * returned.astype(jnp.float32)).astype(jnp.bfloat16)
        outputs.append(output)
        if turn + 1 < turns:
            handed = passed_along(output, "pipe", 1)
    stacked = jnp.stack(outputs)
    section_out = stacked[None, :, None]
    flat_out = stacked.reshape(turns * tok_rows, width)
    flat_cot = head_cotangent[0, :, 0].reshape(turns * tok_rows, feat_count)
    factor = float(turns * rep_count * frames) ** (-0.5)
    grad_rows = lax.psum_scatter(
        lax.dot_general(
            flat_out, flat_cot, (((0,), (0,)), ((), ())), preferred_element_type=jnp.float32
        )
        * factor,
        ("seq", "dp"),
        scatter_dimension=0,
        tiled=True,
    )
    return (section_out, grad_rows[None])


def solution(mesh):
    in_specs = (
        P("pipe", None, "dp", "seq", None),
        P(None, "dp", "seq"),
        P(None, "dp", None),
        P(None, "dp"),
        P("pipe", ("seq", "dp"), None),
        P("pipe", ("seq", "dp"), None),
        P("pipe", None),
        P("pipe", None),
        P("pipe", None, None),
        P("pipe", None),
        P("pipe", None),
        P("pipe", None, "dp", "seq", None),
    )
    out_specs = (P("pipe", None, "dp", "seq", None), P("pipe", ("seq", "dp"), None))
    return jax.shard_map(body, mesh=mesh, in_specs=in_specs, out_specs=out_specs, check_vma=False)
```

profile of v0, /device:TPU:0, one launch (start us, length us, event | category | flops | bytes accessed | tf_op | source)
XLA Modules:
  0.0 329.8 jit_solution(3384821927798843113)
XLA Ops:
  7.2 0.7 all-gather.3.cloned.1.call-update
  8.0 0.7 all-gather.5.cloned.1.call-update
  8.7 1.4 constant_dynamic-slice_fusion.4
  12.0 0.7 fusion.79
  12.7 1.2 multiply_reduce_fusion.3
  14.0 1.4 multiply_reduce_fusion.2
  15.4 51.0 %all-gather.3.cloned.1.call-done = bf16[1,1536,1536]{2,1,0:T(8,128)(2,1)} async-done(((bf16[1,96,1536]{2,1,0:T(8,128)(2,1)}), bf16[1,1536,1536]{2,1,0:T(8,128)(2,1)}) %all-gather.3.cloned.1.call-update) | async-done | bytes 4718608 | tf_op jit(solution)/shard_map/all_gather | solution.py:47
  66.4 3.2 fusion.12
  69.6 0.9 copy.47
  70.5 3.6 %all-to-all-start = ((bf16[128,4,384]{0,2,1:T(8,128)(2,1)}), bf16[128,4,384]{0,2,1:T(8,128)(2,1)S(1)}, u32[]{:S(2)}, u32[]{:S(2)}) async-start(bf16[128,4,384]{0,2,1:T(8,128)(2,1)} %bitcast.5), calls=%async_computation | async-start | bytes 786432 | tf_op jit(solution)/shard_map/all_to_all | solution.py:88
  74.1 48.0 %all-gather.5.cloned.1.call-done = bf16[1,1536,1536]{2,1,0:T(8,128)(2,1)} async-done(((bf16[1,96,1536]{2,1,0:T(8,128)(2,1)}), bf16[1,1536,1536]{2,1,0:T(8,128)(2,1)}) %all-gather.5.cloned.1.call-update) | async-done | bytes 4718608 | tf_op jit(solution)/shard_map/all_gather | solution.py:48
  122.1 3.2 fusion.21
  125.3 0.9 copy.48
  126.2 3.5 %all-to-all-start.1 = ((bf16[128,4,384]{0,2,1:T(8,128)(2,1)}), bf16[128,4,384]{0,2,1:T(8,128)(2,1)S(1)}, u32[]{:S(2)}, u32[]{:S(2)}) async-start(bf16[128,4,384]{0,2,1:T(8,128)(2,1)} %bitcast.10), calls=%async_computation.1 | async-start | bytes 786432 | tf_op jit(solution)/shard_map/all_to_all | solution.py:89
  129.8 0.7 fusion.82
  130.5 2.6 broadcast_multiply_fusion.9
  133.5 3.6 %all-to-all-done.1 = bf16[128,4,384]{0,2,1:T(8,128)(2,1)S(1)} async-done(((bf16[128,4,384]{0,2,1:T(8,128)(2,1)}), bf16[128,4,384]{0,2,1:T(8,128)(2,1)S(1)}, u32[]{:S(2)}, u32[]{:S(2)}) %all-to-all-start.1) | async-done | bytes 393248 | tf_op jit(solution)/shard_map/all_to_all | solution.py:89
  137.6 0.4 fusion.86
  138.5 0.4 fusion.85
  139.4 0.4 fusion.84
  140.3 0.4 fusion.83
  141.4 1.0 copy.32
  142.4 3.5 %all-to-all-start.2 = ((bf16[4,128,384]{2,1,0:T(8,128)(2,1)}), bf16[4,128,384]{2,1,0:T(8,128)(2,1)S(1)}, u32[]{:S(2)}, u32[]{:S(2)}) async-start(bf16[4,128,384]{2,1,0:T(8,128)(2,1)} %copy.32), calls=%async_computation.2 | async-start | bytes 786432 | tf_op jit(solution)/shard_map/all_to_all | solution.py:118
  145.9 7.4 %all-to-all-done.2 = bf16[4,128,384]{2,1,0:T(8,128)(2,1)S(1)} async-done(((bf16[4,128,384]{2,1,0:T(8,128)(2,1)}), bf16[4,128,384]{2,1,0:T(8,128)(2,1)S(1)}, u32[]{:S(2)}, u32[]{:S(2)}) %all-to-all-start.2) | async-done | bytes 393248 | tf_op jit(solution)/shard_map/all_to_all | solution.py:118
  153.5 3.4 %collective-permute-start = (bf16[128,1536]{1,0:T(8,128)(2,1)S(1)}, bf16[128,1536]{1,0:T(8,128)(2,1)S(1)}, u32[]{:S(2)}, u32[]{:S(2)}) collective-permute-start(bf16[128,1536]{1,0:T(8,128)(2,1)S(1)} %add_convert_fusion.2), channel_id=1, source_target_pairs={{0,16},{1,17},{2,18},{3,19},{4,20},{5,21},{6,22},{7,23},{8,24},{9,... | collective-permute-start | bytes 1179656 | tf_op jit(solution)/shard_map/ppermute | solution.py:12
  156.9 8.1 %collective-permute-done = bf16[128,1536]{1,0:T(8,128)(2,1)S(1)} collective-permute-done((bf16[128,1536]{1,0:T(8,128)(2,1)S(1)}, bf16[128,1536]{1,0:T(8,128)(2,1)S(1)}, u32[]{:S(2)}, u32[]{:S(2)}) %collective-permute-start) | collective-permute-done | bytes 393248 | tf_op jit(solution)/shard_map/ppermute | solution.py:12
  165.1 1.4 multiply_reduce_fusion.1
  166.5 3.2 fusion.15
  169.7 0.9 copy.49
  170.6 3.5 %all-to-all-start.3 = ((bf16[128,4,384]{0,2,1:T(8,128)(2,1)}), bf16[128,4,384]{0,2,1:T(8,128)(2,1)S(1)}, u32[]{:S(2)}, u32[]{:S(2)}) async-start(bf16[128,4,384]{0,2,1:T(8,128)(2,1)} %bitcast.37), calls=%async_computation.3 | async-start | bytes 786432 | tf_op jit(solution)/shard_map/all_to_all | solution.py:88
  174.1 3.2 fusion.24
  177.3 0.9 copy.50
  178.2 3.3 all-to-all-done.3
  181.5 3.6 %all-to-all-start.4 = ((bf16[128,4,384]{0,2,1:T(8,128)(2,1)}), bf16[128,4,384]{0,2,1:T(8,128)(2,1)S(1)}, u32[]{:S(2)}, u32[]{:S(2)}) async-start(bf16[128,4,384]{0,2,1:T(8,128)(2,1)} %bitcast.41), calls=%async_computation.4 | async-start | bytes 786432 | tf_op jit(solution)/shard_map/all_to_all | solution.py:89
  185.6 6.8 %all-to-all-done.4 = bf16[128,4,384]{0,2,1:T(8,128)(2,1)S(1)} async-done(((bf16[128,4,384]{0,2,1:T(8,128)(2,1)}), bf16[128,4,384]{0,2,1:T(8,128)(2,1)S(1)}, u32[]{:S(2)}, u32[]{:S(2)}) %all-to-all-start.4) | async-done | bytes 393248 | tf_op jit(solution)/shard_map/all_to_all | solution.py:89
  192.8 0.4 fusion.90
  193.4 0.3 fusion.46
  193.7 0.4 fusion.89
  194.6 0.4 fusion.88
  195.2 0.3 fusion.48
  195.5 0.4 fusion.87
  196.1 0.3 fusion.49
  196.9 9.8 %all_to_all.129 = bf16[4,128,384]{2,1,0:T(8,128)(2,1)S(1)} all-to-all(bf16[4,128,384]{2,1,0:T(8,128)(2,1)S(1)} %copy.38), channel_id=1, replica_groups=mesh['pipe'=2,'seq'=4,'dp'=4] {'seq'}, dimensions={0} | all-to-all | bytes 786432 | tf_op jit(solution)/shard_map/all_to_all | solution.py:118
  207.0 4.4 %collective-permute-start.1 = (bf16[128,1536]{1,0:T(8,128)(2,1)S(1)}, bf16[128,1536]{1,0:T(8,128)(2,1)S(1)}, u32[]{:S(2)}, u32[]{:S(2)}) collective-permute-start(bf16[128,1536]{1,0:T(8,128)(2,1)S(1)} %add_convert_fusion.1), channel_id=1, source_target_pairs={{0,16},{1,17},{2,18},{3,19},{4,20},{5,21},{6,22},{7,23},{8,24},{9,... | collective-permute-start | bytes 1179656 | tf_op jit(solution)/shard_map/ppermute | solution.py:12
  211.7 7.7 %collective-permute-done.1 = bf16[128,1536]{1,0:T(8,128)(2,1)S(1)} collective-permute-done((bf16[128,1536]{1,0:T(8,128)(2,1)S(1)}, bf16[128,1536]{1,0:T(8,128)(2,1)S(1)}, u32[]{:S(2)}, u32[]{:S(2)}) %collective-permute-start.1) | collective-permute-done | bytes 393248 | tf_op jit(solution)/shard_map/ppermute | solution.py:12
  219.4 1.2 multiply_reduce_fusion
  220.7 3.2 fusion.18
  223.9 0.9 copy.51
  224.8 3.5 %all-to-all-start.6 = ((bf16[128,4,384]{0,2,1:T(8,128)(2,1)}), bf16[128,4,384]{0,2,1:T(8,128)(2,1)S(1)}, u32[]{:S(2)}, u32[]{:S(2)}) async-start(bf16[128,4,384]{0,2,1:T(8,128)(2,1)} %bitcast.64), calls=%async_computation.6 | async-start | bytes 786432 | tf_op jit(solution)/shard_map/all_to_all | solution.py:88
  228.3 3.2 fusion.27
  231.5 0.9 copy.52
  232.4 3.3 all-to-all-done.6
  235.7 3.5 %all-to-all-start.7 = ((bf16[128,4,384]{0,2,1:T(8,128)(2,1)}), bf16[128,4,384]{0,2,1:T(8,128)(2,1)S(1)}, u32[]{:S(2)}, u32[]{:S(2)}) async-start(bf16[128,4,384]{0,2,1:T(8,128)(2,1)} %bitcast.68), calls=%async_computation.7 | async-start | bytes 786432 | tf_op jit(solution)/shard_map/all_to_all | solution.py:89
  239.7 6.9 %all-to-all-done.7 = bf16[128,4,384]{0,2,1:T(8,128)(2,1)S(1)} async-done(((bf16[128,4,384]{0,2,1:T(8,128)(2,1)}), bf16[128,4,384]{0,2,1:T(8,128)(2,1)S(1)}, u32[]{:S(2)}, u32[]{:S(2)}) %all-to-all-start.7) | async-done | bytes 393248 | tf_op jit(solution)/shard_map/all_to_all | solution.py:89
  247.0 0.4 fusion.94
  247.9 0.4 fusion.93
  248.5 0.3 fusion.51
  248.8 0.4 fusion.92
  249.4 0.3 fusion.52
  249.7 0.4 fusion.91
  251.1 9.8 %all_to_all.130 = bf16[4,128,384]{2,1,0:T(8,128)(2,1)S(1)} all-to-all(bf16[4,128,384]{2,1,0:T(8,128)(2,1)S(1)} %copy.44), channel_id=1, replica_groups=mesh['pipe'=2,'seq'=4,'dp'=4] {'seq'}, dimensions={0} | all-to-all | bytes 786432 | tf_op jit(solution)/shard_map/all_to_all | solution.py:118
  261.2 1.2 pad_maximum_fusion
  262.4 1.8 convolution_multiply_fusion
  264.2 59.1 %reduce-scatter.2.cloned.1.call-done = f32[96,256]{1,0:T(8,128)} async-done(((f32[1536,256]{1,0:T(8,128)}), f32[96,256]{1,0:T(8,128)}) %reduce-scatter.2.cloned.1.call-update) | async-done | bytes 98320 | tf_op jit(solution)/shard_map/reduce_scatter | solution.py:128
  (69 shorter events, 9.8 us)
Async XLA Ops:
  7.2 255.2 %copy-start = (bf16[1,3,1,128,256]{4,3,2,1,0:T(8,128)(2,1)S(1)}, bf16[1,3,1,128,256]{4,3,2,1,0:T(8,128)(2,1)}, u32[]{:S(2)}) copy-start(bf16[1,3,1,128,256]{4,3,2,1,0:T(8,128)(2,1)} %param.23) | copy-start | bytes 589828
  7.2 59.3 %all-gather.3.cloned.1.call-start = ((), (), s32[]{:S(2)}) async-start(), calls=%async_computation.10 | async-start | bytes 5013504 | tf_op jit(solution)/shard_map/all_gather | solution.py:47
  7.9 114.2 %all-gather.5.cloned.1.call-start = ((), (), s32[]{:S(2)}) async-start(), calls=%async_computation.11 | async-start | bytes 5013504 | tf_op jit(solution)/shard_map/all_gather | solution.py:48
  70.5 59.2 %copy-start.4 = (f32[1,16]{1,0:T(1,128)S(1)}, f32[1,16]{1,0:T(1,128)}, u32[]{:S(2)}) copy-start(f32[1,16]{1,0:T(1,128)} %param.21) | copy-start | bytes 196
  70.5 59.9 %copy-start.3 = (s32[4,1,512]{2,1,0:T(1,128)S(1)}, s32[4,1,512]{2,1,0:T(1,128)}, u32[]{:S(2)}) copy-start(s32[4,1,512]{2,1,0:T(1,128)} %param.14) | copy-start | bytes 24580
  70.5 55.7 %all-to-all-start = ((bf16[128,4,384]{0,2,1:T(8,128)(2,1)}), bf16[128,4,384]{0,2,1:T(8,128)(2,1)S(1)}, u32[]{:S(2)}, u32[]{:S(2)}) async-start(bf16[128,4,384]{0,2,1:T(8,128)(2,1)} %bitcast.5), calls=%async_computation | async-start | bytes 786432 | tf_op jit(solution)/shard_map/all_to_all | solution.py:88
  126.2 10.9 %all-to-all-start.1 = ((bf16[128,4,384]{0,2,1:T(8,128)(2,1)}), bf16[128,4,384]{0,2,1:T(8,128)(2,1)S(1)}, u32[]{:S(2)}, u32[]{:S(2)}) async-start(bf16[128,4,384]{0,2,1:T(8,128)(2,1)} %bitcast.10), calls=%async_computation.1 | async-start | bytes 786432 | tf_op jit(solution)/shard_map/all_to_all | solution.py:89
  140.3 5.6 %copy-start.2 = (f32[1,1536]{1,0:T(1,128)S(1)}, f32[1,1536]{1,0:T(1,128)}, u32[]{:S(2)}) copy-start(f32[1,1536]{1,0:T(1,128)} %param.22) | copy-start | bytes 18436
  141.2 23.9 %copy-start.1 = (bf16[1,16,1536]{2,1,0:T(8,128)(2,1)S(1)}, bf16[1,16,1536]{2,1,0:T(8,128)(2,1)}, u32[]{:S(2)}) copy-start(bf16[1,16,1536]{2,1,0:T(8,128)(2,1)} %param.20) | copy-start | bytes 147460
  142.4 10.9 %all-to-all-start.2 = ((bf16[4,128,384]{2,1,0:T(8,128)(2,1)}), bf16[4,128,384]{2,1,0:T(8,128)(2,1)S(1)}, u32[]{:S(2)}, u32[]{:S(2)}) async-start(bf16[4,128,384]{2,1,0:T(8,128)(2,1)} %copy.32), calls=%async_computation.2 | async-start | bytes 786432 | tf_op jit(solution)/shard_map/all_to_all | solution.py:118
  153.5 11.5 %collective-permute-start = (bf16[128,1536]{1,0:T(8,128)(2,1)S(1)}, bf16[128,1536]{1,0:T(8,128)(2,1)S(1)}, u32[]{:S(2)}, u32[]{:S(2)}) collective-permute-start(bf16[128,1536]{1,0:T(8,128)(2,1)S(1)} %add_convert_fusion.2), channel_id=1, source_target_pairs={{0,16},{1,17},{2,18},{3,19},{4,20},{5,21},{6,22},{7,23},{8,24},{9,... | collective-permute-start | bytes 1179656 | tf_op jit(solution)/shard_map/ppermute | solution.py:12
  170.6 10.9 %all-to-all-start.3 = ((bf16[128,4,384]{0,2,1:T(8,128)(2,1)}), bf16[128,4,384]{0,2,1:T(8,128)(2,1)S(1)}, u32[]{:S(2)}, u32[]{:S(2)}) async-start(bf16[128,4,384]{0,2,1:T(8,128)(2,1)} %bitcast.37), calls=%async_computation.3 | async-start | bytes 786432 | tf_op jit(solution)/shard_map/all_to_all | solution.py:88
  181.5 10.9 %all-to-all-start.4 = ((bf16[128,4,384]{0,2,1:T(8,128)(2,1)}), bf16[128,4,384]{0,2,1:T(8,128)(2,1)S(1)}, u32[]{:S(2)}, u32[]{:S(2)}) async-start(bf16[128,4,384]{0,2,1:T(8,128)(2,1)} %bitcast.41), calls=%async_computation.4 | async-start | bytes 786432 | tf_op jit(solution)/shard_map/all_to_all | solution.py:89
  207.0 12.4 %collective-permute-start.1 = (bf16[128,1536]{1,0:T(8,128)(2,1)S(1)}, bf16[128,1536]{1,0:T(8,128)(2,1)S(1)}, u32[]{:S(2)}, u32[]{:S(2)}) collective-permute-start(bf16[128,1536]{1,0:T(8,128)(2,1)S(1)} %add_convert_fusion.1), channel_id=1, source_target_pairs={{0,16},{1,17},{2,18},{3,19},{4,20},{5,21},{6,22},{7,23},{8,24},{9,... | collective-permute-start | bytes 1179656 | tf_op jit(solution)/shard_map/ppermute | solution.py:12
  224.8 10.9 %all-to-all-start.6 = ((bf16[128,4,384]{0,2,1:T(8,128)(2,1)}), bf16[128,4,384]{0,2,1:T(8,128)(2,1)S(1)}, u32[]{:S(2)}, u32[]{:S(2)}) async-start(bf16[128,4,384]{0,2,1:T(8,128)(2,1)} %bitcast.64), calls=%async_computation.6 | async-start | bytes 786432 | tf_op jit(solution)/shard_map/all_to_all | solution.py:88
  235.7 10.9 %all-to-all-start.7 = ((bf16[128,4,384]{0,2,1:T(8,128)(2,1)}), bf16[128,4,384]{0,2,1:T(8,128)(2,1)S(1)}, u32[]{:S(2)}, u32[]{:S(2)}) async-start(bf16[128,4,384]{0,2,1:T(8,128)(2,1)} %bitcast.68), calls=%async_computation.7 | async-start | bytes 786432 | tf_op jit(solution)/shard_map/all_to_all | solution.py:89
  239.1 84.2 %reduce-scatter.2.cloned.1.call-start = ((), (), s32[]{:S(2)}) async-start(), calls=%async_computation.12 | async-start | bytes 1671168 | tf_op jit(solution)/shard_map/reduce_scatter | solution.py:128
Sparse Core Ops, SparseCore 0:
  10.3 56.0 all-gather.2
  68.7 53.3 all-gather.4
  264.3 58.9 reduce-scatter.1
where the time goes:
time: 331 us; the launch traced here: 330 us
  waiting for transfers between devices  206 us (62%)
  starting transfers between devices  32.5 us (10%)
  matrix products  32.4 us (10%)
  blocking collectives  19.7 us (6%)
  between operations  16.2 us (5%)
  local copies, waits for them, and re-layouts  13.3 us (4%)
  other arithmetic  9.34 us (3%)
    reduce_scatter x1, waiting for transfers between devices, body(): lax.psum_scatter(lax.dot_general(flat_out, flat_cot, (((0,), (0,)), ((),...  59.1 us
    all_gather x1, waiting for transfers between devices, body(): lax.all_gather(w_query, ('seq', 'dp'), axis=1, tiled=True)  51 us
    all_gather x1, waiting for transfers between devices, body(): lax.all_gather(w_keyval, ('seq', 'dp'), axis=1, tiled=True)  48 us
    all_to_all x2, blocking collectives, body(): lax.all_to_all(attended, 'seq', split_axis=0, concat_axis=1, tiled=True)  19.7 us
    all_to_all x3, waiting for transfers between devices, body(): lax.all_to_all(keyval_parts, 'seq', split_axis=1, concat_axis=0, tiled=True)  17.2 us
    ppermute x2, waiting for transfers between devices, passed_along(): lax.ppermute(value, axis, [(source, source + steps) for source in range(f...  15.8 us
    all_to_all x3, starting transfers between devices, body(): lax.all_to_all(keyval_parts, 'seq', split_axis=1, concat_axis=0, tiled=True)  10.6 us
    all_to_all x3, starting transfers between devices, body(): lax.all_to_all(query_parts, 'seq', split_axis=1, concat_axis=0, tiled=True)  10.5 us
  transfers between devices with their start and end apart: 12, of which 11 were waited for; matrix products, arithmetic and copies ran while one was open for 8% of the time, Pallas kernels for 0%

commit v1 on v0

v1 whole, which is shorter than its diff:
```python
import jax
import jax.numpy as jnp
from jax import lax
from jax.sharding import PartitionSpec as P

epsilon = 1e-06


def passed_along(value, axis, steps):
    count = lax.axis_size(axis)
    first, last = (max(0, -steps), min(count, count - steps))
    return lax.ppermute(value, axis, [(source, source + steps) for source in range(first, last)])


def ring(value, axis):
    count = lax.axis_size(axis)
    return lax.ppermute(value, axis, [(source, (source + 1) % count) for source in range(count)])


def body(
    incoming,
    contacts,
    keyframes,
    timesteps,
    w_query,
    w_keyval,
    norm_gain,
    time_freq,
    contact_table,
    key_bias,
    attn_gate,
    head_cotangent,
):
    section_idx = lax.axis_index("pipe")
    seq_idx = lax.axis_index("seq")
    rep_idx = lax.axis_index("dp")
    seq_count = lax.axis_size("seq")
    section_count = lax.axis_size("pipe")
    rep_count = lax.axis_size("dp")
    tok_rows = incoming.shape[3]
    width = incoming.shape[4]
    turns = incoming.shape[1]
    frames = tok_rows * seq_count
    heads_all = key_bias.shape[1]
    head_size = width // heads_all
    heads_local = heads_all // seq_count
    kv_width = w_keyval.shape[2]
    kv_local = kv_width // (2 * head_size * seq_count)
    group_size = heads_local // kv_local
    feat_count = head_cotangent.shape[4]
    score_scale = head_size ** (-0.5)
    q_cols = width // seq_count
    kv_cols = kv_width // seq_count
    w_rows = w_query.shape[1]

    w_parts = jnp.concatenate(
        [
            w_query[0].reshape(w_rows, seq_count, q_cols),
            w_keyval[0].reshape(w_rows, seq_count, kv_cols),
        ],
        axis=2,
    ).transpose(1, 0, 2)
    block = lax.all_to_all(w_parts, "seq", split_axis=0, concat_axis=0, tiled=True)
    weights = jnp.zeros((seq_count, rep_count, w_rows, q_cols + kv_cols), jnp.bfloat16)
    for hop in range(rep_count):
        owner = lax.rem(rep_idx + rep_count - hop, rep_count)
        weights = lax.dynamic_update_slice_in_dim(weights, block[:, None], owner, 1)
        if hop + 1 < rep_count:
            block = ring(block, "dp")
    weights = weights.reshape(width, q_cols + kv_cols)

    gain_row = norm_gain[0]
    freq_row = time_freq[0]
    table = contact_table[0]
    gate_local = lax.dynamic_slice_in_dim(attn_gate[0], seq_idx * q_cols, q_cols)
    table_local = lax.dynamic_slice_in_dim(table, seq_idx * q_cols, q_cols, 1)
    bias_local = lax.dynamic_slice_in_dim(key_bias[0], seq_idx * heads_local, heads_local)
    contact_all = lax.all_gather(contacts[:, 0, :], "seq", axis=1, tiled=True)
    key_all = keyframes[:, 0, :]
    step_all = timesteps[:, 0]
    labels = jnp.arange(table.shape[0], dtype=jnp.int32)
    cot_all = lax.all_gather(head_cotangent[0, :, 0], "seq", axis=1, tiled=True)

    lag = 2 if section_count == 2 else 1
    if lag == 2:
        steps = turns + 1
    else:
        steps = turns

    def turn_at(step):
        if lag == 1:
            return jnp.int32(step)
        return jnp.clip(step - section_idx, 0, turns - 1)

    outputs = []
    handed = {}
    for step in range(steps):
        turn = turn_at(step)
        fresh = lax.dynamic_index_in_dim(incoming[0, :, 0], turn, 0, keepdims=False)
        current = lax.all_gather(fresh, "seq", axis=0, tiled=True)
        if step in handed:
            current = jnp.where((section_idx == 0) | (turn == 0), current, handed[step])
        batch_idx = turn - section_idx + section_count - 1
        contact_rows = lax.dynamic_index_in_dim(contact_all, batch_idx, 0, keepdims=False)
        key_flags = lax.dynamic_index_in_dim(key_all, batch_idx, 0, keepdims=False).astype(
            jnp.float32
        )
        timestep = lax.dynamic_index_in_dim(step_all, batch_idx, 0, keepdims=False).astype(
            jnp.float32
        )
        onehot = (contact_rows[:, None] == labels[None, :]).astype(jnp.bfloat16)
        hidden = current.astype(jnp.float32) + jnp.dot(
            onehot, table, preferred_element_type=jnp.float32
        )
        root_mean = jnp.sqrt(jnp.mean(hidden * hidden, axis=-1, keepdims=True) + epsilon)
        modulation = gain_row * (1.0 + 0.5 * jnp.sin(timestep * freq_row))
        normed = (hidden / root_mean * modulation[None, :]).astype(jnp.bfloat16)
        projected = jnp.dot(normed, weights, preferred_element_type=jnp.float32).astype(
            jnp.bfloat16
        )
        query_heads = projected[:, :q_cols].reshape(frames, heads_local, head_size)
        keyval_heads = projected[:, q_cols:].reshape(frames, kv_local, 2, head_size)
        head_outputs = []
        for head in range(heads_local):
            key_rows = keyval_heads[:, head // group_size, 0]
            value_rows = keyval_heads[:, head // group_size, 1]
            scores = (
                lax.dot_general(
                    query_heads[:, head],
                    key_rows,
                    (((1,), (1,)), ((), ())),
                    preferred_element_type=jnp.float32,
                )
                * score_scale
            )
            scores = scores + bias_local[head] * key_flags[None, :]
            row_max = jnp.max(scores, axis=-1, keepdims=True)
            exponent = jnp.exp(scores - row_max)
            probabilities = (exponent / jnp.sum(exponent, axis=-1, keepdims=True)).astype(
                jnp.bfloat16
            )
            head_outputs.append(
                jnp.dot(probabilities, value_rows, preferred_element_type=jnp.float32).astype(
                    jnp.bfloat16
                )
            )
        attended = jnp.concatenate(head_outputs, axis=1)
        hidden_local = lax.dynamic_slice_in_dim(current, seq_idx * q_cols, q_cols, 1).astype(
            jnp.float32
        ) + jnp.dot(onehot, table_local, preferred_element_type=jnp.float32)
        output = (hidden_local + gate_local[None, :] * attended.astype(jnp.float32)).astype(
            jnp.bfloat16
        )
        outputs.append(output)
        if step + lag < steps:
            piece = passed_along(output, "pipe", 1)
            handed[step + lag] = lax.all_gather(piece, "seq", axis=1, tiled=True)

    factor = float(turns * rep_count * frames) ** (-0.5)
    total = None
    rows_out = []
    for turn in range(turns):
        if lag == 2:
            own = jnp.where(section_idx == 0, outputs[turn], outputs[turn + 1])
        else:
            own = outputs[turn]
        term = lax.dot_general(
            own, cot_all[turn], (((0,), (0,)), ((), ())), preferred_element_type=jnp.float32
        )
        total = term if total is None else total + term
        rows_out.append(lax.all_to_all(own, "seq", split_axis=0, concat_axis=1, tiled=True))
    section_out = jnp.stack(rows_out)[None, :, None]
    grad_parts = lax.all_to_all(
        (total * factor).astype(jnp.bfloat16).reshape(rep_count, q_cols // rep_count, feat_count),
        "dp",
        split_axis=0,
        concat_axis=0,
        tiled=True,
    )
    grad_rows = jnp.sum(grad_parts.astype(jnp.float32), axis=0)
    return (section_out, grad_rows[None])


def solution(mesh):
    in_specs = (
        P("pipe", None, "dp", "seq", None),
        P(None, "dp", "seq"),
        P(None, "dp", None),
        P(None, "dp"),
        P("pipe", ("seq", "dp"), None),
        P("pipe", ("seq", "dp"), None),
        P("pipe", None),
        P("pipe", None),
        P("pipe", None, None),
        P("pipe", None),
        P("pipe", None),
        P("pipe", None, "dp", "seq", None),
    )
    out_specs = (P("pipe", None, "dp", "seq", None), P("pipe", ("seq", "dp"), None))
    return jax.shard_map(body, mesh=mesh, in_specs=in_specs, out_specs=out_specs, check_vma=False)
```

time: 331 us -> 238 us (0.72)
  waiting for transfers between devices: 206 us -> 80.5 us
  blocking collectives: 19.7 us -> 34.1 us
  local copies, waits for them, and re-layouts: 13.3 us -> 24.2 us
  starting transfers between devices: 32.5 us -> 25.8 us
  matrix products: 32.4 us -> 38.9 us
  other arithmetic: 9.34 us -> 15.3 us
    all_gather x2 -> x6, waiting for transfers between devices: 99.1 us -> 25.1 us  [the longest x2 21.1 us: body(): handed[step + lag] = lax.all_gather(piece, 'seq', axis=1, tiled=True)]
    reduce_scatter x1 -> x0, waiting for transfers between devices: 59.1 us -> none  [body(): lax.psum_scatter(lax.dot_general(flat_out, flat_cot, (((0,), (0,)), ((),...]
    ppermute x0 -> x3, waiting for transfers between devices: none -> 31.1 us  [ring(): lax.ppermute(value, axis, [(source, (source + 1) % count) for source in r...]
    all_gather x0 -> x2, blocking collectives: none -> 17.6 us  [the longest x1 12.5 us: body(): cot_all = lax.all_gather(head_cotangent[0, :, 0], 'seq', axis=1, tiled=True)]
    all_to_all x7 -> x4, waiting for transfers between devices: 31.1 us -> 16.2 us  [the longest x3 10.6 us: body(): lax.all_to_all(own, 'seq', split_axis=0, concat_axis=1, tiled=True)]
    all_to_all x7 -> x4, starting transfers between devices: 24.5 us -> 15.1 us  [the longest x3 10.5 us: body(): lax.all_to_all(own, 'seq', split_axis=0, concat_axis=1, tiled=True)]
    slice x0 -> x12, local copies, waits for them, and re-layouts: none -> 7.93 us  [the longest x8 4.46 us: body(): keyval_heads = projected[:, q_cols:].reshape(frames, kv_local, 2, head_size)]
    ppermute x2, waiting for transfers between devices: 15.8 us -> 8.07 us  [passed_along(): lax.ppermute(value, axis, [(source, source + steps) for source in range(f...]
  transfers between devices with their start and end apart: 12 -> 15, of which waited for: 11 -> 10; matrix products, arithmetic and copies ran while one was open for 8% -> 25% of each run, Pallas kernels for 0% -> 0%
where the time goes in v1:
time: 238 us; the launch traced here: 236 us
  waiting for transfers between devices  80.5 us (34%)
  matrix products  38.9 us (16%)
  blocking collectives  34.1 us (14%)
  starting transfers between devices  25.8 us (11%)
  local copies, waits for them, and re-layouts  24.2 us (10%)
  between operations  17.4 us (7%)
  other arithmetic  15.3 us (6%)
    ppermute x3, waiting for transfers between devices, ring(): lax.ppermute(value, axis, [(source, (source + 1) % count) for source in r...  31.1 us
    all_gather x2, waiting for transfers between devices, body(): handed[step + lag] = lax.all_gather(piece, 'seq', axis=1, tiled=True)  21.1 us
    all_to_all x1, blocking collectives, body(): lax.all_to_all(w_parts, 'seq', split_axis=0, concat_axis=0, tiled=True)  16.5 us
    all_gather x1, blocking collectives, body(): cot_all = lax.all_gather(head_cotangent[0, :, 0], 'seq', axis=1, tiled=True)  12.5 us
    all_to_all x3, waiting for transfers between devices, body(): lax.all_to_all(own, 'seq', split_axis=0, concat_axis=1, tiled=True)  10.6 us
    all_to_all x3, starting transfers between devices, body(): lax.all_to_all(own, 'seq', split_axis=0, concat_axis=1, tiled=True)  10.5 us
    ppermute x2, starting transfers between devices, passed_along(): lax.ppermute(value, axis, [(source, source + steps) for source in range(f...  8.62 us
    dot_general x4, matrix products, body(): jnp.dot(onehot, table, preferred_element_type=jnp.float32)  8.13 us
  transfers between devices with their start and end apart: 15, of which 10 were waited for; matrix products, arithmetic and copies ran while one was open for 25% of the time, Pallas kernels for 0%

profile of v1, /device:TPU:0, one launch (start us, length us, event | category | flops | bytes accessed | tf_op | source)
XLA Modules:
  0.0 236.3 jit_solution(1624286467502183438)
XLA Ops:
  7.3 2.3 constant_dynamic-slice_fusion.2
  9.6 0.9 copy.187
  10.6 0.9 copy.188
  12.2 16.5 %all_to_all.58 = bf16[4,96,768]{2,1,0:T(8,128)(2,1)S(1)} all-to-all(bf16[4,96,768]{2,1,0:T(8,128)(2,1)S(1)} %copy.153), channel_id=1, replica_groups=mesh['pipe'=2,'seq'=4,'dp'=4] {'seq'}, dimensions={0} | all-to-all | bytes 1179648 | tf_op jit(solution)/shard_map/all_to_all | solution.py:63
  28.7 1.7 collective-permute-start
  30.4 15.4 %collective-permute-done = bf16[4,96,768]{2,1,0:T(8,128)(2,1)S(1)} collective-permute-done((bf16[4,96,768]{2,1,0:T(8,128)(2,1)S(1)}, bf16[4,96,768]{2,1,0:T(8,128)(2,1)S(1)}, u32[]{:S(2)}, u32[]{:S(2)}) %collective-permute-start) | collective-permute-done | bytes 589856 | tf_op jit(solution)/shard_map/ppermute | solution.py:17
  45.8 0.9 copy.189
  50.0 0.7 fusion.82
  50.7 5.1 %all-gather.1 = s32[4,1,512]{2,1,0:T(1,128)S(1)} all-gather(s32[4,1,128]{2,1,0:T(1,128)S(1)} %copy-done.22), channel_id=3, replica_groups=mesh['pipe'=2,'seq'=4,'dp'=4] {'seq'}, dimensions={2}, use_global_device_ids=true | all-gather | bytes 10240 | tf_op jit(solution)/shard_map/all_gather | solution.py:78
  56.6 2.7 %broadcast_multiply_fusion.12 = (f32[1,1,512]{2,1,0:T(1,128)S(1)}, f32[1,1,512]{2,1,0:T(1,128)S(1)}, f32[1,1,512]{2,1,0:T(1,128)S(1)}, f32[1,1,512]{2,1,0:T(1,12...) fusion(f32[]{:T(128)} %bitcast.18, ...), kind=kLoop, calls=%fused_computation.256 | loop fusion | flops 10240 | bytes 40992 | tf_op jit(solution)/shard_map/mul | solution.py:136
  59.3 0.7 multiply_reduce_fusion.4
  60.0 2.0 collective-permute-done.1
  62.3 0.8 copy-done.13
  63.1 1.1 bitcast_dynamic-update-slice_fusion
  64.2 13.7 %collective-permute-done.2 = bf16[4,96,768]{2,1,0:T(8,128)(2,1)S(1)} collective-permute-done((bf16[4,96,768]{2,1,0:T(8,128)(2,1)}, bf16[4,96,768]{2,1,0:T(8,128)(2,1)S(1)}, u32[]{:S(2)}, u32[]{:S(2)}) %collective-permute-start.2) | collective-permute-done | bytes 589856 | tf_op jit(solution)/shard_map/ppermute | solution.py:17
  78.0 3.0 %multiply_reduce_fusion.3 = (f32[512]{0:T(512)S(1)}, f32[512,1536]{0,1:T(8,128)S(1)}) fusion(bf16[1,16,1536]{2,1,0:T(8,128)(2,1)S(1)} %copy-done, s32[512]{0:T(512)S(1)} %bitcast.379, bf16[1,1,1,512,1536]{3,4,2,1,0:T(8,128)(2,1)} %all-gather.17.cloned.1.call-done), kind=kOutput, calls=%fused_computation.11 | convolution fusion | flops 28319232 | bytes 4771840 | tf_op jit(solution)/shard_map/dot_general | solution.py:112
  81.0 1.7 fusion.7
  82.7 0.8 fusion.86
  83.7 1.2 copy.156
  88.5 1.5 fusion.26
  89.9 0.8 copy-done.9
  90.7 3.5 %collective-permute-start.3 = (bf16[512,384]{0,1:T(8,128)(2,1)S(1)}, bf16[512,384]{0,1:T(8,128)(2,1)S(1)}, u32[]{:S(2)}, u32[]{:S(2)}) collective-permute-start(bf16[512,384]{0,1:T(8,128)(2,1)S(1)} %fusion.26), channel_id=1, source_target_pairs={{0,16},{1,17},{2,18},{3,19},{4,20},{5,21},{6,22},{7,23},{8,24},{9,... | collective-permute-start | bytes 1179656 | tf_op jit(solution)/shard_map/ppermute | solution.py:12
  94.2 6.2 %collective-permute-done.3 = bf16[512,384]{0,1:T(8,128)(2,1)S(1)} collective-permute-done((bf16[512,384]{0,1:T(8,128)(2,1)S(1)}, bf16[512,384]{0,1:T(8,128)(2,1)S(1)}, u32[]{:S(2)}, u32[]{:S(2)}) %collective-permute-start.3) | collective-permute-done | bytes 393248 | tf_op jit(solution)/shard_map/ppermute | solution.py:12
  100.4 0.7 copy-done.14
  101.2 1.0 copy.190
  102.5 2.1 multiply_reduce_fusion.2
  104.6 1.7 fusion.6
  110.4 2.2 fusion.27
  112.6 5.1 %collective-permute-start.4 = (bf16[512,384]{0,1:T(8,128)(2,1)}, bf16[512,384]{0,1:T(8,128)(2,1)}, u32[]{:S(2)}, u32[]{:S(2)}) collective-permute-start(bf16[512,384]{0,1:T(8,128)(2,1)} %fusion.27), channel_id=1, source_target_pairs={{0,16},{1,17},{2,18},{3,19},{4,20},{5,21},{6,22},{7,23},{8,24},{9,... | collective-permute-start | bytes 1179656 | tf_op jit(solution)/shard_map/ppermute | solution.py:12
  117.7 2.4 fusion.50
  120.1 0.7 fusion.48
  120.8 1.8 collective-permute-done.4
  122.7 3.3 %multiply_reduce_fusion.1 = (f32[512]{0:T(512)S(1)}, bf16[512,1536]{0,1:T(8,128)(2,1)S(1)}) fusion(f32[512,1536]{0,1:T(8,128)} %fusion.50, bf16[512,1536]{0,1:T(8,128)(2,1)} %all-gather.13.cloned.1.call-done, bf16[1,1,1,512,1536]{3,4,2,1,0:T(8,128)(2,1)} %all-gather.21.cloned.1.call-done, pred[]{:T(512)S(6)} %or.6), kind=kLoop, calls=%fused_computation.6 | loop fusion | flops 3931648 | bytes 7866369 | tf_op jit(solution)/shard_map/reduce_sum | solution.py:115
  126.0 0.7 copy-done.3
  126.7 1.6 fusion.5
  128.4 0.9 fusion.85
  129.3 2.0 copy.168
  131.3 1.9 copy.167
  133.2 1.4 fusion.92
  136.8 1.0 convolution_convert_fusion.5
  137.8 1.0 convolution_convert_fusion.6
  138.8 1.0 convolution_convert_fusion.7
  139.7 3.9 %all-gather.23.cloned.1.call-done = bf16[1,1,1,512,1536]{3,4,2,1,0:T(8,128)(2,1)} async-done(((bf16[1,1,1,128,1536]{3,4,2,1,0:T(8,128)(2,1)}), bf16[1,1,1,512,1536]{3,4,2,1,0:T(8,128)(2,1)}) %all-gather.23.cloned.1.call-update) | async-done | bytes 1572880 | tf_op jit(solution)/shard_map/all_gather | solution.py:100
  143.6 21.1 %all-gather.15.cloned.1.call-done = bf16[512,1536]{0,1:T(8,128)(2,1)} async-done(((bf16[512,384]{0,1:T(8,128)(2,1)}), bf16[512,1536]{0,1:T(8,128)(2,1)}) %all-gather.15.cloned.1.call-update) | async-done | bytes 1572880 | tf_op jit(solution)/shard_map/all_gather | solution.py:157
  164.7 2.3 multiply_reduce_fusion
  167.1 1.6 fusion.4
  173.5 1.4 add_convert_fusion.1
  174.9 1.5 fusion.46
  176.4 0.8 copy_bitcast_fusion
  177.2 3.6 %all-to-all-start.3 = ((bf16[4,128,384]{1,2,0:T(8,128)(2,1)}), bf16[4,128,384]{1,2,0:T(8,128)(2,1)S(1)}, u32[]{:S(2)}, u32[]{:S(2)}) async-start(bf16[4,128,384]{1,2,0:T(8,128)(2,1)} %copy_bitcast_fusion), calls=%async_computation.3 | async-start | bytes 786432 | tf_op jit(solution)/shard_map/all_to_all | solution.py:171
  180.9 1.1 fusion.52
  181.9 0.8 copy.197
  182.7 5.5 %all-to-all-done.3 = bf16[4,128,384]{1,2,0:T(8,128)(2,1)S(1)} async-done(((bf16[4,128,384]{1,2,0:T(8,128)(2,1)}), bf16[4,128,384]{1,2,0:T(8,128)(2,1)S(1)}, u32[]{:S(2)}, u32[]{:S(2)}) %all-to-all-start.3) | async-done | bytes 393248 | tf_op jit(solution)/shard_map/all_to_all | solution.py:171
  188.2 3.5 %all-to-all-start.2 = ((bf16[4,128,384]{1,2,0:T(8,128)(2,1)}), bf16[4,128,384]{1,2,0:T(8,128)(2,1)S(1)}, u32[]{:S(2)}, u32[]{:S(2)}) async-start(bf16[4,128,384]{1,2,0:T(8,128)(2,1)} %bitcast.307), calls=%async_computation.2 | async-start | bytes 786432 | tf_op jit(solution)/shard_map/all_to_all | solution.py:171
  191.7 12.5 %all-gather.5 = bf16[1,3,1,512,256]{4,3,2,1,0:T(8,128)(2,1)S(1)} all-gather(bf16[1,3,1,128,256]{4,3,2,1,0:T(8,128)(2,1)S(1)} %copy-done.17), channel_id=7, replica_groups=mesh['pipe'=2,'seq'=4,'dp'=4] {'seq'}, dimensions={3}, use_global_device_ids=true | all-gather | bytes 983040 | tf_op jit(solution)/shard_map/all_gather | solution.py:82
  204.2 1.0 fusion.47
  205.2 0.8 copy.198
  206.0 3.5 %all-to-all-start.1 = ((bf16[4,128,384]{1,2,0:T(8,128)(2,1)}), bf16[4,128,384]{1,2,0:T(8,128)(2,1)S(1)}, u32[]{:S(2)}, u32[]{:S(2)}) async-start(bf16[4,128,384]{1,2,0:T(8,128)(2,1)} %bitcast.308), calls=%async_computation.1 | async-start | bytes 786432 | tf_op jit(solution)/shard_map/all_to_all | solution.py:171
  209.5 1.4 convolution_add_fusion.5
  210.9 0.9 fusion.29
  211.8 5.1 %all-to-all-done.1 = bf16[4,128,384]{1,2,0:T(8,128)(2,1)S(1)} async-done(((bf16[4,128,384]{1,2,0:T(8,128)(2,1)}), bf16[4,128,384]{1,2,0:T(8,128)(2,1)S(1)}, u32[]{:S(2)}, u32[]{:S(2)}) %all-to-all-start.1) | async-done | bytes 393248 | tf_op jit(solution)/shard_map/all_to_all | solution.py:171
  216.9 4.6 %all-to-all-start.4 = ((bf16[4,96,256]{2,1,0:T(8,128)(2,1)}), bf16[4,96,256]{2,1,0:T(8,128)(2,1)S(1)}, u32[]{:S(2)}, u32[]{:S(2)}) async-start(bf16[4,96,256]{2,1,0:T(8,128)(2,1)} %bitcast.94), calls=%async_computation.4 | async-start | bytes 393216 | tf_op jit(solution)/shard_map/all_to_all | solution.py:173
  222.1 1.1 maximum_bitcast_fusion
  223.2 5.6 %all-to-all-done.4 = bf16[4,96,256]{2,1,0:T(8,128)(2,1)S(1)} async-done(((bf16[4,96,256]{2,1,0:T(8,128)(2,1)}), bf16[4,96,256]{2,1,0:T(8,128)(2,1)S(1)}, u32[]{:S(2)}, u32[]{:S(2)}) %all-to-all-start.4) | async-done | bytes 196640 | tf_op jit(solution)/shard_map/all_to_all | solution.py:173
  (140 shorter events, 18.8 us)
Async XLA Ops:
  7.2 70.8 %copy-start = (bf16[1,16,1536]{2,1,0:T(8,128)(2,1)S(1)}, bf16[1,16,1536]{2,1,0:T(8,128)(2,1)}, u32[]{:S(2)}) copy-start(bf16[1,16,1536]{2,1,0:T(8,128)(2,1)} %param.20) | copy-start | bytes 147460
  7.2 70.8 %all-gather.17.cloned.1.call-start = ((), (), s32[]{:S(2)}) async-start(), calls=%async_computation.7 | async-start | bytes 1966080 | tf_op jit(solution)/shard_map/all_gather | solution.py:100
  7.2 4.3 %copy-start.15 = (bf16[1,96,1536]{2,1,0:T(8,128)(2,1)S(1)}, bf16[1,96,1536]{2,1,0:T(8,128)(2,1)}, u32[]{:S(2)}) copy-start(bf16[1,96,1536]{2,1,0:T(8,128)(2,1)} %param.17) | copy-start | bytes 884740
  7.2 4.4 %copy-start.16 = (bf16[1,96,1536]{2,1,0:T(8,128)(2,1)S(1)}, bf16[1,96,1536]{2,1,0:T(8,128)(2,1)}, u32[]{:S(2)}) copy-start(bf16[1,96,1536]{2,1,0:T(8,128)(2,1)} %param.16) | copy-start | bytes 884740
  10.5 91.9 %all-gather.19.cloned.1.call-start = ((), (), s32[]{:S(2)}) async-start(), calls=%async_computation.8 | async-start | bytes 1966080 | tf_op jit(solution)/shard_map/all_gather | solution.py:100
  11.5 111.1 %all-gather.21.cloned.1.call-start = ((), (), s32[]{:S(2)}) async-start(), calls=%async_computation.9 | async-start | bytes 1966080 | tf_op jit(solution)/shard_map/all_gather | solution.py:100
  11.8 35.0 %copy-start.18 = (s32[4,1]{0,1:T(1,128)S(1)}, s32[4,1]{0,1:T(1,128)}, u32[]{:S(2)}) copy-start(s32[4,1]{0,1:T(1,128)} %param.15) | copy-start | bytes 52
  11.8 39.0 %copy-start.22 = (s32[4,1,128]{2,1,0:T(1,128)S(1)}, s32[4,1,128]{2,1,0:T(1,128)}, u32[]{:S(2)}) copy-start(s32[4,1,128]{2,1,0:T(1,128)} %param.13) | copy-start | bytes 6148
  11.8 44.0 %copy-start.23 = (f32[1,16]{1,0:T(1,128)S(1)}, f32[1,16]{1,0:T(1,128)}, u32[]{:S(2)}) copy-start(f32[1,16]{1,0:T(1,128)} %param.21) | copy-start | bytes 196
  11.8 44.8 %copy-start.19 = (s32[4,1,512]{2,1,0:T(1,128)S(1)}, s32[4,1,512]{2,1,0:T(1,128)}, u32[]{:S(2)}) copy-start(s32[4,1,512]{2,1,0:T(1,128)} %param.14) | copy-start | bytes 24580
  11.8 47.5 %copy-start.20 = (f32[1,1536]{1,0:T(1,128)S(1)}, f32[1,1536]{1,0:T(1,128)}, u32[]{:S(2)}) copy-start(f32[1,1536]{1,0:T(1,128)} %param.18) | copy-start | bytes 18436
  11.8 47.5 %copy-start.21 = (f32[1,1536]{1,0:T(1,128)S(1)}, f32[1,1536]{1,0:T(1,128)}, u32[]{:S(2)}) copy-start(f32[1,1536]{1,0:T(1,128)} %param.19) | copy-start | bytes 18436
  28.7 17.1 %collective-permute-start = (bf16[4,96,768]{2,1,0:T(8,128)(2,1)S(1)}, bf16[4,96,768]{2,1,0:T(8,128)(2,1)S(1)}, u32[]{:S(2)}, u32[]{:S(2)}) collective-permute-start(bf16[4,96,768]{2,1,0:T(8,128)(2,1)S(1)} %all_to_all.58), channel_id=1, source_target_pairs={{0,1},{1,2},{2,3},{3,0},{4,5},{5,6},{6,7},{7,4},{8,9},{9,10},{10,1... | collective-permute-start | bytes 1769480 | tf_op jit(solution)/shard_map/ppermute | solution.py:17
  45.8 16.3 %copy-start.12 = (bf16[4,96,768]{2,1,0:T(8,128)(2,1)}, bf16[4,96,768]{2,1,0:T(8,128)(2,1)S(1)}, u32[]{:S(2)}) copy-start(bf16[4,96,768]{2,1,0:T(8,128)(2,1)S(1)} %collective-permute-done) | copy-start | bytes 1769476
  45.8 16.3 %collective-permute-start.1 = (bf16[4,96,768]{2,1,0:T(8,128)(2,1)S(1)}, bf16[4,96,768]{2,1,0:T(8,128)(2,1)}, u32[]{:S(2)}, u32[]{:S(2)}) collective-permute-start(bf16[4,96,768]{2,1,0:T(8,128)(2,1)S(1)} %collective-permute-done), channel_id=1, source_target_pairs={{0,1},{1,2},{2,3},{3,0},{4,5},{5,6},{6,7},{7,4},{8,9},{9,10},{10,1... | collective-permute-start | bytes 1769480 | tf_op jit(solution)/shard_map/ppermute | solution.py:17
  46.7 76.0 %all-gather.13.cloned.1.call-start = ((), (), s32[]{:S(2)}) async-start(), calls=%async_computation.5 | async-start | bytes 1966080 | tf_op jit(solution)/shard_map/all_gather | solution.py:157
  62.0 15.9 %collective-permute-start.2 = (bf16[4,96,768]{2,1,0:T(8,128)(2,1)}, bf16[4,96,768]{2,1,0:T(8,128)(2,1)S(1)}, u32[]{:S(2)}, u32[]{:S(2)}) collective-permute-start(bf16[4,96,768]{2,1,0:T(8,128)(2,1)} %collective-permute-done.1), channel_id=1, source_target_pairs={{0,1},{1,2},{2,3},{3,0},{4,5},{5,6},{6,7},{7,4},{8,9},{9,10},{10,1... | collective-permute-start | bytes 1769480 | tf_op jit(solution)/shard_map/ppermute | solution.py:17
  62.0 1.1 copy-start.13
  78.0 26.6 %copy-start.2 = (bf16[4,4,96,768]{3,2,1,0:T(8,128)(2,1)}, bf16[4,4,96,768]{3,2,1,0:T(8,128)(2,1)S(1)}, u32[]{:S(2)}) copy-start(bf16[4,4,96,768]{3,2,1,0:T(8,128)(2,1)S(1)} %bitcast_dynamic-update-slice_fusion.2) | copy-start | bytes 7077892
  88.5 12.8 %copy-start.11 = (bf16[1,1,1,128,1536]{4,3,2,1,0:T(8,128)(2,1)S(1)}, bf16[1,1,1,128,1536]{4,3,2,1,0:T(8,128)(2,1)}, u32[]{:S(2)}) copy-start(bf16[1,1,1,128,1536]{4,3,2,1,0:T(8,128)(2,1)} %get-tuple-element.10) | copy-start | bytes 1179652
  89.9 0.8 copy-start.9
  90.7 9.7 %collective-permute-start.3 = (bf16[512,384]{0,1:T(8,128)(2,1)S(1)}, bf16[512,384]{0,1:T(8,128)(2,1)S(1)}, u32[]{:S(2)}, u32[]{:S(2)}) collective-permute-start(bf16[512,384]{0,1:T(8,128)(2,1)S(1)} %fusion.26), channel_id=1, source_target_pairs={{0,16},{1,17},{2,18},{3,19},{4,20},{5,21},{6,22},{7,23},{8,24},{9,... | collective-permute-start | bytes 1179656 | tf_op jit(solution)/shard_map/ppermute | solution.py:12
  100.4 0.7 copy-start.14
  101.2 42.4 %all-gather.23.cloned.1.call-start = ((), (), s32[]{:S(2)}) async-start(), calls=%async_computation.10 | async-start | bytes 1966080 | tf_op jit(solution)/shard_map/all_gather | solution.py:100
  102.2 62.5 %all-gather.15.cloned.1.call-start = ((), (), s32[]{:S(2)}) async-start(), calls=%async_computation.6 | async-start | bytes 1966080 | tf_op jit(solution)/shard_map/all_gather | solution.py:157
  112.6 10.0 %collective-permute-start.4 = (bf16[512,384]{0,1:T(8,128)(2,1)}, bf16[512,384]{0,1:T(8,128)(2,1)}, u32[]{:S(2)}, u32[]{:S(2)}) collective-permute-start(bf16[512,384]{0,1:T(8,128)(2,1)} %fusion.27), channel_id=1, source_target_pairs={{0,16},{1,17},{2,18},{3,19},{4,20},{5,21},{6,22},{7,23},{8,24},{9,... | collective-permute-start | bytes 1179656 | tf_op jit(solution)/shard_map/ppermute | solution.py:12
  122.7 3.3 %copy-start.1 = (f32[512,1536]{0,1:T(8,128)S(1)}, f32[512,1536]{0,1:T(8,128)}, u32[]{:S(2)}) copy-start(f32[512,1536]{0,1:T(8,128)} %fusion.50) | copy-start | bytes 9437188
  122.7 4.0 %copy-start.3 = (bf16[4,4,96,768]{3,2,1,0:T(8,128)(2,1)S(1)}, bf16[4,4,96,768]{3,2,1,0:T(8,128)(2,1)}, u32[]{:S(2)}) copy-start(bf16[4,4,96,768]{3,2,1,0:T(8,128)(2,1)} %copy-done.2) | copy-start | bytes 7077892
  126.0 2.4 copy-start.7
  133.2 1.6 copy-start.5
  133.2 1.6 copy-start.6
  164.7 2.4 copy-start.4
  167.1 1.7 copy-start.8
  172.5 0.9 copy-start.24
  172.5 0.9 copy-start.25
  172.5 1.0 copy-start.26
  174.9 5.9 %copy-start.10 = (bf16[512,384]{0,1:T(8,128)(2,1)S(1)}, bf16[512,384]{0,1:T(8,128)(2,1)}, u32[]{:S(2)}) copy-start(bf16[512,384]{0,1:T(8,128)(2,1)} %copy-done.9) | copy-start | bytes 1179652
  177.2 14.5 %copy-start.17 = (bf16[1,3,1,128,256]{4,3,2,1,0:T(8,128)(2,1)S(1)}, bf16[1,3,1,128,256]{4,3,2,1,0:T(8,128)(2,1)}, u32[]{:S(2)}) copy-start(bf16[1,3,1,128,256]{4,3,2,1,0:T(8,128)(2,1)} %param.23) | copy-start | bytes 589828
  177.2 11.0 %all-to-all-start.3 = ((bf16[4,128,384]{1,2,0:T(8,128)(2,1)}), bf16[4,128,384]{1,2,0:T(8,128)(2,1)S(1)}, u32[]{:S(2)}, u32[]{:S(2)}) async-start(bf16[4,128,384]{1,2,0:T(8,128)(2,1)} %copy_bitcast_fusion), calls=%async_computation.3 | async-start | bytes 786432 | tf_op jit(solution)/shard_map/all_to_all | solution.py:171
  188.2 17.8 %all-to-all-start.2 = ((bf16[4,128,384]{1,2,0:T(8,128)(2,1)}), bf16[4,128,384]{1,2,0:T(8,128)(2,1)S(1)}, u32[]{:S(2)}, u32[]{:S(2)}) async-start(bf16[4,128,384]{1,2,0:T(8,128)(2,1)} %bitcast.307), calls=%async_computation.2 | async-start | bytes 786432 | tf_op jit(solution)/shard_map/all_to_all | solution.py:171
  206.0 10.9 %all-to-all-start.1 = ((bf16[4,128,384]{1,2,0:T(8,128)(2,1)}), bf16[4,128,384]{1,2,0:T(8,128)(2,1)S(1)}, u32[]{:S(2)}, u32[]{:S(2)}) async-start(bf16[4,128,384]{1,2,0:T(8,128)(2,1)} %bitcast.308), calls=%async_computation.1 | async-start | bytes 786432 | tf_op jit(solution)/shard_map/all_to_all | solution.py:171
  216.9 11.9 %all-to-all-start.4 = ((bf16[4,96,256]{2,1,0:T(8,128)(2,1)}), bf16[4,96,256]{2,1,0:T(8,128)(2,1)S(1)}, u32[]{:S(2)}, u32[]{:S(2)}) async-start(bf16[4,96,256]{2,1,0:T(8,128)(2,1)} %bitcast.94), calls=%async_computation.4 | async-start | bytes 393216 | tf_op jit(solution)/shard_map/all_to_all | solution.py:173
Sparse Core Ops, SparseCore 0:
  10.6 25.1 all-gather.16
  37.4 20.1 all-gather.18
  59.2 19.8 all-gather.20
  101.3 20.9 all-gather.12
  123.7 19.8 all-gather.22
  145.0 19.6 all-gather.14

commit v2 on v1

--- a/solution.py
+++ b/solution.py
@@ -1,6 +1,11 @@
+import functools
+import math
+
 import jax
 import jax.numpy as jnp
 from jax import lax
+from jax.experimental import pallas as pl
+from jax.experimental.pallas import tpu as pltpu
 from jax.sharding import PartitionSpec as P
 
 epsilon = 1e-06
@@ -17,7 +22,397 @@
     return lax.ppermute(value, axis, [(source, (source + 1) % count) for source in range(count)])
 
 
-def body(
+def swap(value, bit):
+    count = lax.axis_size("seq")
+    return lax.ppermute(value, "seq", [(source, source ^ bit) for source in range(count)])
+
+
+def offsets_of(count):
+    offsets = [0]
+    bit = count // 2
+    while bit:
+        offsets = offsets + [offset ^ bit for offset in offsets]
+        bit //= 2
+    return offsets
+
+
+def gathered_pieces(value):
+    pieces = [value]
+    bit = lax.axis_size("seq") // 2
+    while bit:
+        pieces = pieces + [swap(piece, bit) for piece in pieces]
+        bit //= 2
+    return pieces
+
+
+def pack_kernel(offsets, meta, wq, wkv, *outs):
+    q_cols = outs[0].shape[1] // 2
+    for offset, out in zip(offsets, outs):
+        start = pl.multiple_of((meta[0] ^ offset) * q_cols, 128)
+        out[:, :q_cols] = wq[0, :, pl.ds(start, q_cols)]
+        out[:, q_cols:] = wkv[0, :, pl.ds(start, q_cols)]
+
+
+def step_kernel(cfg, *refs):
+    step, has_relay, has_prev, last = cfg["step"], cfg["has_relay"], cfg["has_prev"], cfg["last"]
+    pieces, hops, head = cfg["pieces"], cfg["hops"], cfg["head"]
+    heads, group = cfg["heads"], cfg["group"]
+    refs = list(refs)
+
+    def take(count):
+        taken, refs[:count] = refs[:count], []
+        return taken
+
+    meta, bias, table, mod, gate, flags = take(6)
+    prev = take(1)[0] if has_prev else None
+    inc = take(pieces)
+    side = take(pieces)
+    chunks = take(2 * hops)
+    relay = take(pieces) if has_relay else None
+    out, grad = take(2)
+    xs, cot, ids, w, normed, proj, att, sem_x, sem_c, sem_w = take(10)
+    offsets = offsets_of(pieces)
+    rows, width = xs.shape[1], xs.shape[2]
+    cols = out.shape[2]
+    w_rows = chunks[0].shape[1]
+    frames = pieces * rows
+    seq, rep = meta[0], meta[1]
+    turn = meta[8 + step]
+
+    def fresh_copies():
+        return [
+            pltpu.make_async_copy(inc[i].at[turn], xs.at[seq ^ offsets[i]], sem_x.at[i])
+            for i in range(pieces)
+        ]
+
+    def relay_copies():
+        return [
+            pltpu.make_async_copy(
+                relay[i],
+                xs.at[:, :, pl.ds(pl.multiple_of((seq ^ offsets[i]) * cols, 128), cols)],
+                sem_x.at[i],
+            )
+            for i in range(pieces)
+        ]
+
+    def either(act):
+        if has_relay:
+            relayed = meta[16 + step]
+
+            @pl.when(relayed == 0)
+            def _():
+                for copy in fresh_copies():
+                    act(copy)
+
+            @pl.when(relayed != 0)
+            def _():
+                for copy in relay_copies():
+                    act(copy)
+        else:
+            for copy in fresh_copies():
+                act(copy)
+
+    turns_rows = cfg["turns"] * rows
+    side_copies = []
+    for i in range(pieces):
+        side_copies.append(
+            pltpu.make_async_copy(
+                side[i].at[pl.ds(turns_rows, 16)], ids.at[seq ^ offsets[i]], sem_c.at[i]
+            )
+        )
+    cot_copies = []
+    for i in range(pieces):
+        cot_copies.append(
+            pltpu.make_async_copy(
+                side[i].at[pl.ds(pl.multiple_of(turn * rows, 128), rows)],
+                cot.at[seq ^ offsets[i]],
+                sem_c.at[pieces + i],
+            )
+        )
+    w_copies = []
+    for half in range(2):
+        for hop in range(hops):
+            owner = lax.rem(rep + hops - hop, hops)
+            for j in range(pieces // 2):
+                offset = half * (pieces // 2) + j
+                block = (seq ^ offset) * hops + owner
+                w_copies.append(
+                    pltpu.make_async_copy(
+                        chunks[half * hops + hop].at[j],
+                        w.at[pl.ds(pl.multiple_of(block * w_rows, 16), w_rows)],
+                        sem_w.at[len(w_copies)],
+                    )
+                )
+    either(lambda copy: copy.start())
+    for copy in side_copies + w_copies + cot_copies:
+        copy.start()
+    for copy in side_copies:
+        copy.wait()
+    either(lambda copy: copy.wait())
+
+    def onehot_of(block):
+        state = ids[block, step : step + 1, :rows].astype(jnp.float32).astype(jnp.int32)
+        labels = lax.broadcasted_iota(jnp.int32, (table.shape[0], rows), 0)
+        return jnp.where(labels == state, 1.0, 0.0).T.astype(jnp.bfloat16)
+
+    mod_row = mod[step]
+    for block in range(pieces):
+        hidden = xs[block].astype(jnp.float32) + jnp.dot(
+            onehot_of(block), table[...], preferred_element_type=jnp.float32
+        )
+        square = jnp.sum(hidden * hidden, axis=1, keepdims=True) * (1.0 / width)
+        scale = lax.rsqrt(square + epsilon)
+        normed[block] = (hidden * scale * mod_row).astype(jnp.bfloat16)
+    for copy in w_copies:
+        copy.wait()
+    for block in range(pieces):
+        proj[pl.ds(block * rows, rows), : 2 * cols] = jnp.dot(
+            normed[block], w[...], preferred_element_type=jnp.float32
+        ).astype(jnp.bfloat16)
+    score_scale = head ** (-0.5) * math.log2(math.e)
+    lanes = lax.broadcasted_iota(jnp.int32, (frames, 128), 1)
+    flag_row = flags[step] * math.log2(math.e)
+    for kv in range(heads // group):
+        base = cols + kv * 2 * head
+        keys = proj[:, base : base + head]
+        values = proj[:, base + head : base + head + 128].astype(jnp.float32)
+        values = jnp.where(lanes < head, values, jnp.where(lanes == head, 1.0, 0.0)).astype(
+            jnp.bfloat16
+        )
+        for h in range(kv * group, (kv + 1) * group):
+            bias_row = flag_row * bias[h]
+            for block in range(pieces):
+                queries = proj[block * rows : (block + 1) * rows, h * head : (h + 1) * head]
+                scores = lax.dot_general(
+                    queries, keys, (((1,), (1,)), ((), ())), preferred_element_type=jnp.float32
+                )
+                scores = scores * score_scale + bias_row
+                top = jnp.max(scores, axis=1, keepdims=True)
+                weight = jnp.exp2(scores - top).astype(jnp.bfloat16)
+                mixed = jnp.dot(weight, values, preferred_element_type=jnp.float32)
+                att[block, :, h * head : (h + 1) * head] = (
+                    mixed[:, :head] / mixed[:, head : head + 1]
+                )
+    start = pl.multiple_of(seq * cols, 128)
+    for block in range(pieces):
+        hidden = xs[block, :, pl.ds(start, cols)].astype(jnp.float32) + jnp.dot(
+            onehot_of(block), table[:, pl.ds(start, cols)], preferred_element_type=jnp.float32
+        )
+        attended = att[block].astype(jnp.bfloat16).astype(jnp.float32)
+        out[block] = (hidden + gate[...] * attended).astype(jnp.bfloat16)
+    for copy in cot_copies:
+        copy.wait()
+    total = lax.dot_general(
+        out[...].reshape(frames, cols),
+        cot[...].reshape(frames, cot.shape[2]),
+        (((0,), (0,)), ((), ())),
+        preferred_element_type=jnp.float32,
+    )
+    total = total * meta[24 + step].astype(jnp.float32)
+    if has_prev:
+        total = total + prev[...]
+    if last:
+        factor = float(cfg["turns"] * hops * frames) ** (-0.5)
+        grad[...] = (total * factor).astype(jnp.bfloat16)
+    else:
+        grad[...] = total
+
+
+def finish_kernel(early, late, parts, section_out, grad):
+    count, turns_early, _, cols = early.shape
+    for source in range(count):
+        lanes = pl.ds(source * cols, cols)
+        for turn in range(turns_early):
+            section_out[turn, :, lanes] = early[source, turn]
+        section_out[turns_early, :, lanes] = late[source]
+    total = parts[0].astype(jnp.float32)
+    for source in range(1, parts.shape[0]):
+        total = total + parts[source].astype(jnp.float32)
+    grad[...] = total
+
+
+VMEM_LIMIT = 40 * 1024 * 1024
+
+
+def paired_body(
+    incoming,
+    contacts,
+    keyframes,
+    timesteps,
+    w_query,
+    w_keyval,
+    norm_gain,
+    time_freq,
+    contact_table,
+    key_bias,
+    attn_gate,
+    head_cotangent,
+):
+    section_idx = lax.axis_index("pipe")
+    seq_idx = lax.axis_index("seq")
+    rep_idx = lax.axis_index("dp")
+    seq_count = lax.axis_size("seq")
+    hops = lax.axis_size("dp")
+    rows, width, turns = incoming.shape[3], incoming.shape[4], incoming.shape[1]
+    frames = rows * seq_count
+    heads_all = key_bias.shape[1]
+    head = width // heads_all
+    heads = heads_all // seq_count
+    kv_heads = w_keyval.shape[2] // (2 * head * seq_count)
+    feats = head_cotangent.shape[4]
+    cols = width // seq_count
+    w_rows = w_query.shape[1]
+    steps = turns + 1
+    contact_states = contact_table.shape[1]
+
+    step_ids = jnp.arange(8, dtype=jnp.int32)
+    turn_ids = jnp.clip(step_ids - section_idx, 0, turns - 1)
+    batch_ids = (turn_ids - section_idx + 1)[:steps]
+    meta = jnp.concatenate(
+        [
+            jnp.stack([seq_idx, rep_idx] + [jnp.int32(0)] * 6).astype(jnp.int32),
+            turn_ids,
+            jnp.where((section_idx > 0) & (turn_ids > 0), 1, 0).astype(jnp.int32),
+            jnp.where((step_ids >= section_idx) & (step_ids < turns + section_idx), 1, 0).astype(
+                jnp.int32
+            ),
+        ]
+    )
+
+    smem = pl.BlockSpec(memory_space=pltpu.SMEM)
+    vmem = pl.BlockSpec(memory_space=pltpu.VMEM)
+    anywhere = pl.BlockSpec(memory_space=pl.ANY)
+    parts = pl.pallas_call(
+        functools.partial(pack_kernel, range(seq_count)),
+        out_shape=[jax.ShapeDtypeStruct((w_rows, 2 * cols), jnp.bfloat16)] * seq_count,
+        in_specs=[smem, vmem, vmem],
+        out_specs=[vmem] * seq_count,
+        name="pack",
+    )(meta, w_query, w_keyval)
+    arrived = [parts[0]] + [
+        lax.ppermute(parts[m], "seq", [(i, i ^ m) for i in range(seq_count)])
+        for m in range(1, seq_count)
+    ]
+    half = seq_count // 2
+    rings = [jnp.stack(arrived[:half]), jnp.stack(arrived[half:])]
+    chunks = [[rings[0]], [rings[1]]]
+    for hop in range(1, hops):
+        for which in range(2):
+            chunks[which].append(ring(chunks[which][-1], "dp"))
+
+    contact_steps = jnp.take(contacts[:, 0, :], batch_ids, axis=0).astype(jnp.bfloat16)
+    side = jnp.concatenate(
+        [
+            head_cotangent[0, :, 0].reshape(turns * rows, feats),
+            jnp.pad(contact_steps, ((0, 16 - steps), (0, feats - rows))),
+        ]
+    )
+    side_pieces = gathered_pieces(side)
+    fresh_pieces = gathered_pieces(incoming[0, :, 0])
+
+    flag_steps = jnp.take(keyframes[:, 0, :], batch_ids, axis=0).astype(jnp.float32)[:, None, :]
+    time_steps = jnp.take(timesteps[:, 0], batch_ids, axis=0).astype(jnp.float32)
+    mod_steps = (
+        norm_gain[0][None] * (1.0 + 0.5 * jnp.sin(time_steps[:, None] * time_freq[0][None]))
+    )[:, None, :]
+    gate_local = lax.dynamic_slice_in_dim(attn_gate[0], seq_idx * cols, cols)[None]
+    bias_local = lax.dynamic_slice_in_dim(key_bias[0], seq_idx * heads, heads)
+
+    outputs = []
+    relayed = {}
+    grad = None
+    for step in range(steps):
+        last = step + 1 == steps
+        cfg = {
+            "step": step,
+            "has_relay": step in relayed,
+            "has_prev": grad is not None,
+            "last": last,
+            "pieces": seq_count,
+            "hops": hops,
+            "head": head,
+            "heads": heads,
+            "group": heads // kv_heads,
+            "turns": turns,
+        }
+        operands = [meta, bias_local, contact_table[0], mod_steps, gate_local, flag_steps]
+        specs = [smem, smem, vmem, vmem, vmem, vmem]
+        if grad is not None:
+            operands.append(grad)
+            specs.append(vmem)
+        loose = fresh_pieces + side_pieces + chunks[0] + chunks[1] + relayed.get(step, [])
+        operands += loose
+        specs += [anywhere] * len(loose)
+        output, grad = pl.pallas_call(
+            functools.partial(step_kernel, cfg),
+            out_shape=[
+                jax.ShapeDtypeStruct((seq_count, rows, cols), jnp.bfloat16),
+                jax.ShapeDtypeStruct((cols, feats), jnp.bfloat16 if last else jnp.float32),
+            ],
+            in_specs=specs,
+            out_specs=[vmem, vmem],
+            scratch_shapes=[
+                pltpu.VMEM((seq_count, rows, width), jnp.bfloat16),
+                pltpu.VMEM((seq_count, rows, feats), jnp.bfloat16),
+                pltpu.VMEM((seq_count, 16, feats), jnp.bfloat16),
+                pltpu.VMEM((width, 2 * cols), jnp.bfloat16),
+                pltpu.VMEM((seq_count, rows, width), jnp.bfloat16),
+                pltpu.VMEM((frames, 2 * cols + 128), jnp.bfloat16),
+                pltpu.VMEM((seq_count, rows, cols), jnp.float32),
+                pltpu.SemaphoreType.DMA((seq_count,)),
+                pltpu.SemaphoreType.DMA((2 * seq_count,)),
+                pltpu.SemaphoreType.DMA((seq_count * hops,)),
+            ],
+            compiler_params=pltpu.CompilerParams(vmem_limit_bytes=VMEM_LIMIT),
+            cost_estimate=pl.CostEstimate(
+                flops=2 * frames * width * 2 * cols + 4 * heads * frames * frames * head,
+                bytes_accessed=6 * frames * width,
+                transcendentals=heads * frames * frames,
+            ),
+            name="step%d" % step,
+        )(*operands)
+        outputs.append(output)
+        if step + 2 < steps:
+            relayed[step + 2] = gathered_pieces(passed_along(output, "pipe", 1))
+
+    first_section = section_idx == 0
+    own = [jnp.where(first_section, outputs[t], outputs[t + 1]) for t in range(turns)]
+    early = lax.all_to_all(
+        jnp.stack(own[:-1], axis=1), "seq", split_axis=0, concat_axis=0, tiled=True
+    )
+    late = lax.all_to_all(own[-1], "seq", split_axis=0, concat_axis=0, tiled=True)
+    grad_parts = lax.all_to_all(
+        grad.reshape(hops, cols // hops, feats), "dp", split_axis=0, concat_axis=0, tiled=True
+    )
+    section_out, grad_rows = pl.pallas_call(
+        finish_kernel,
+        out_shape=[
+            jax.ShapeDtypeStruct((turns, rows, width), jnp.bfloat16),
+            jax.ShapeDtypeStruct((cols // hops, feats), jnp.float32),
+        ],
+        in_specs=[vmem] * 3,
+        out_specs=[vmem] * 2,
+        name="finish",
+    )(early, late, grad_parts)
+    return (section_out[None, :, None], grad_rows[None])
+
+
+def body(incoming, contacts, keyframes, timesteps, w_query, *others):
+    count = lax.axis_size("seq")
+    cols = w_query.shape[2] // count
+    paired = (
+        lax.axis_size("pipe") == 2
+        and count in (2, 4, 8)
+        and cols % 128 == 0
+        and w_query.shape[1] % 16 == 0
+        and incoming.shape[3] == 128
+        and incoming.shape[1] < 8
+    )
+    chosen = paired_body if paired else general_body
+    return chosen(incoming, contacts, keyframes, timesteps, w_query, *others)
+
+
+def general_body(
     incoming,
     contacts,
     keyframes,

time: 238 us -> 197 us (0.83)
  Pallas kernels: 0 us -> 46.9 us
  matrix products: 38.9 us -> 0 us
  between operations: 17.4 us -> 0.98 us
  waiting for transfers between devices: 80.5 us -> 67 us
  blocking collectives: 34.1 us -> 25.3 us
  local copies, waits for them, and re-layouts: 24.2 us -> 18 us
    pallas_call x0 -> x6, Pallas kernels: none -> 46.9 us  [the longest x4 42.6 us: paired_body(): pl.pallas_call(functools.partial(step_kernel, cfg), out_shape=[jax.ShapeD...]
    dot_general x47 -> x0, matrix products: 38.9 us -> none  [the longest x4 8.13 us: body(): jnp.dot(onehot, table, preferred_element_type=jnp.float32)]
    ppermute x0 -> x15, waiting for transfers between devices: none -> 32.9 us  [the longest x3 21.3 us: paired_body(): lax.ppermute(parts[m], 'seq', [(i, i ^ m) for i in range(seq_count)])]
    all_gather x6 -> x0, waiting for transfers between devices: 25.1 us -> none  [the longest x2 21.1 us: body(): handed[step + lag] = lax.all_gather(piece, 'seq', axis=1, tiled=True)]
    all_gather x2 -> x0, blocking collectives: 17.6 us -> none  [the longest x1 12.5 us: body(): cot_all = lax.all_gather(head_cotangent[0, :, 0], 'seq', axis=1, tiled=True)]
    all_to_all x4 -> x1, starting transfers between devices: 15.1 us -> 3.37 us  [paired_body(): lax.all_to_all(grad.reshape(hops, cols // hops, feats), 'dp', split_axis=...]
    ppermute x3 -> x6, waiting for transfers between devices: 31.1 us -> 20.4 us  [ring(): lax.ppermute(value, axis, [(source, (source + 1) % count) for source in r...]
    reduce_sum x19 -> x0, other arithmetic: 9.45 us -> none  [the longest x2 5.64 us: body(): jnp.mean(hidden * hidden, axis=-1, keepdims=True) + epsilon]
  transfers between devices with their start and end apart: 15 -> 24, of which waited for: 10 -> 11; matrix products, arithmetic and copies ran while one was open for 25% -> 10% of each run, Pallas kernels for 0% -> 12%
where the time goes in v2:
time: 197 us; the launch traced here: 196 us
  waiting for transfers between devices  67 us (34%)
  Pallas kernels  46.9 us (24%)
  blocking collectives  25.3 us (13%)
  starting transfers between devices  24.5 us (12%)
  local copies, waits for them, and re-layouts  18 us (9%)
  other arithmetic  13.3 us (7%)
    pallas_call x4, Pallas kernels, paired_body(): pl.pallas_call(functools.partial(step_kernel, cfg), out_shape=[jax.ShapeD...  42.6 us
    ppermute x3, waiting for transfers between devices, paired_body(): lax.ppermute(parts[m], 'seq', [(i, i ^ m) for i in range(seq_count)])  21.3 us
    ppermute x6, waiting for transfers between devices, ring(): lax.ppermute(value, axis, [(source, (source + 1) % count) for source in r...  20.4 us
    all_to_all x1, blocking collectives, paired_body(): lax.all_to_all(jnp.stack(own[:-1], axis=1), 'seq', split_axis=0, concat_a...  14.8 us
    unnamed x71, local copies, waits for them, and re-layouts  12.6 us
    ppermute x12, waiting for transfers between devices, swap(): lax.ppermute(value, 'seq', [(source, source ^ bit) for source in range(co...  11.5 us
    all_to_all x1, blocking collectives, paired_body(): lax.all_to_all(own[-1], 'seq', split_axis=0, concat_axis=0, tiled=True)  10.5 us
    all_to_all x1, waiting for transfers between devices, paired_body(): lax.all_to_all(grad.reshape(hops, cols // hops, feats), 'dp', split_axis=...  7.16 us
  transfers between devices with their start and end apart: 24, of which 11 were waited for; matrix products, arithmetic and copies ran while one was open for 10% of the time, Pallas kernels for 12%

profile of v2, /device:TPU:0, one launch (start us, length us, event | category | flops | bytes accessed | tf_op | source)
XLA Modules:
  0.0 195.9 jit_solution(4208742766491021180)
XLA Ops:
  0.7 3.0 %collective-permute-start = (bf16[3,128,1536]{2,1,0:T(8,128)(2,1)}, bf16[3,128,1536]{2,1,0:T(8,128)(2,1)S(1)}, u32[]{:S(2)}, u32[]{:S(2)}) collective-permute-start(bf16[3,128,1536]{2,1,0:T(8,128)(2,1)} %bitcast.25), channel_id=1, source_target_pairs={{0,8},{4,12},{8,0},{12,4},{1,9},{5,13},{9,1},{13,5},{2,10},{6,14},... | collective-permute-start | bytes 3538952 | tf_op jit(solution)/shard_map/ppermute | solution.py:27
  3.7 0.7 concatenate.6.meta.refs_0_
  4.4 1.9 pack.1
  6.3 0.5 collective-permute-start.6
  6.8 1.6 collective-permute-start.10
  8.5 0.5 compare_and_fusion
  9.0 0.6 pad_clamp_fusion
  9.6 1.4 gather_fusion.2
  11.0 0.7 select_convert_fusion
  11.6 1.7 pad_maximum_fusion.1.refs_14_.refs_15_
  13.4 1.6 collective-permute-start.7
  14.9 18.6 %collective-permute-done.11 = bf16[96,768]{1,0:T(8,128)(2,1)} collective-permute-done((bf16[96,768]{1,0:T(8,128)(2,1)}, bf16[96,768]{1,0:T(8,128)(2,1)}, u32[]{:S(2)}, u32[]{:S(2)}) %collective-permute-start.11) | collective-permute-done | bytes 147488 | tf_op jit(solution)/shard_map/ppermute | solution.py:293
  33.5 2.8 %collective-permute-done.10 = bf16[96,768]{1,0:T(8,128)(2,1)} collective-permute-done((bf16[96,768]{1,0:T(8,128)(2,1)}, bf16[96,768]{1,0:T(8,128)(2,1)}, u32[]{:S(2)}, u32[]{:S(2)}) %collective-permute-start.10) | collective-permute-done | bytes 147488 | tf_op jit(solution)/shard_map/ppermute | solution.py:293
  36.3 1.7 pad_maximum_fusion.2.refs_18_.refs_19_
  38.0 1.8 collective-permute-start.12
  39.8 1.6 fusion.1.refs_10_.refs_11_
  41.5 1.5 collective-permute-start.3
  42.9 1.3 reduce.1
  44.3 1.3 reduce
  45.6 1.3 gather_fusion
  46.8 0.7 select_convert_fusion.1
  47.5 1.6 collective-permute-start.8
  49.1 1.6 collective-permute-start.13
  50.7 2.1 %add_multiply_fusion.refs_3_ = f32[4,1,1536]{2,1,0:T(1,128)} fusion(f32[1536]{0:T(1024)} %reduce.1, f32[1536]{0:T(1024)} %reduce, f32[4]{0:T(128)S(1)} %select_convert_fusion.1), kind=kLoop, calls=%fused_computation.12 | loop fusion | flops 24576 | bytes 36880 | tf_op jit(solution)/shard_map/mul | solution.py:316
  52.7 0.7 copy.22
  53.4 1.3 gather_fusion.1
  54.7 4.7 %collective-permute-done.8.refs_16_.refs_17_ = bf16[2,96,768]{2,1,0:T(8,128)(2,1)} collective-permute-done((bf16[2,96,768]{2,1,0:T(8,128)(2,1)}, bf16[2,96,768]{2,1,0:T(8,128)(2,1)}, u32[]{:S(2)}, u32[]{:S(2)}) %collective-permute-start.8) | collective-permute-done | bytes 294944 | tf_op jit(solution)/shard_map/ppermute | solution.py:22
  59.5 6.3 %collective-permute-done.13.refs_20_.refs_21_ = bf16[2,96,768]{2,1,0:T(8,128)(2,1)} collective-permute-done((bf16[2,96,768]{2,1,0:T(8,128)(2,1)}, bf16[2,96,768]{2,1,0:T(8,128)(2,1)}, u32[]{:S(2)}, u32[]{:S(2)}) %collective-permute-start.13) | collective-permute-done | bytes 294944 | tf_op jit(solution)/shard_map/ppermute | solution.py:22
  65.8 0.7 dynamic-slice_bitcast_fusion.refs_1_
  66.6 0.8 fusion.2.refs_5_
  67.4 0.8 collective-permute-done.5.refs_13_.refs_14_
  68.2 3.8 %collective-permute-done.9.refs_17_.refs_18_ = bf16[2,96,768]{2,1,0:T(8,128)(2,1)S(1)} collective-permute-done((bf16[2,96,768]{2,1,0:T(8,128)(2,1)}, bf16[2,96,768]{2,1,0:T(8,128)(2,1)S(1)}, u32[]{:S(2)}, u32[]{:S(2)}) %collective-permute-start.9) | collective-permute-done | bytes 294944 | tf_op jit(solution)/shard_map/ppermute | solution.py:22
  72.0 5.6 %collective-permute-done.14.refs_21_.refs_22_ = bf16[2,96,768]{2,1,0:T(8,128)(2,1)S(1)} collective-permute-done((bf16[2,96,768]{2,1,0:T(8,128)(2,1)}, bf16[2,96,768]{2,1,0:T(8,128)(2,1)S(1)}, u32[]{:S(2)}, u32[]{:S(2)}) %collective-permute-start.14) | collective-permute-done | bytes 294944 | tf_op jit(solution)/shard_map/ppermute | solution.py:22
  77.6 0.9 copy-done.10
  78.5 0.7 copy-done.12
  79.2 0.7 copy-done.24
  79.9 10.5 %step0.1 = (bf16[4,128,384]{2,1,0:T(8,128)(2,1)S(1)}, f32[384,256]{1,0:T(8,128)S(1)}) custom-call(s32[32]{0:T(128)S(1)} %copy-done.24, f32[4]{0:T(128)S(1)} %dynamic-slice_bitcast_fusion.refs_1_, bf16[16,1536]{1,0:T(8,128)(2,1)S(1)} %bitcast.31, f32[4,1,1536]{2,1,0:T(1,128)S(1)} %copy-done.12, f32[1,384]{1,0:T(1,128)S(1)} %constant_dynamic-slice_fusion.refs_4_, ...), custom_call_target="tpu_custom_call" | custom-call | flops 1610612736 | bytes 4718592 | tf_op jit(solution)/shard_map/step0/pallas_call | solution.py:346
  90.4 4.2 %collective-permute-start.15 = (bf16[4,128,384]{2,1,0:T(8,128)(2,1)S(1)}, bf16[4,128,384]{2,1,0:T(8,128)(2,1)}, u32[]{:S(2)}, u32[]{:S(2)}) collective-permute-start(bf16[4,128,384]{2,1,0:T(8,128)(2,1)S(1)} %get-tuple-element.20), channel_id=1, source_target_pairs={{0,16},{1,17},{2,18},{3,19},{4,20},{5,21},{6,22},{7,23},{8,24},{9,... | collective-permute-start | bytes 1179656 | tf_op jit(solution)/shard_map/ppermute | solution.py:17
  94.6 10.5 %step1.1 = (bf16[4,128,384]{2,1,0:T(8,128)(2,1)S(1)}, f32[384,256]{1,0:T(8,128)S(1)}) custom-call(s32[32]{0:T(128)S(1)} %copy-done.25, f32[4]{0:T(128)S(1)} %dynamic-slice_bitcast_fusion.refs_1_, bf16[16,1536]{1,0:T(8,128)(2,1)S(1)} %bitcast.32, f32[4,1,1536]{2,1,0:T(1,128)S(1)} %copy-done.12, f32[1,384]{1,0:T(1,128)S(1)} %constant_dynamic-slice_fusion.refs_4_, ...), custom_call_target="tpu_custom_call" | custom-call | flops 1610612736 | bytes 4718592 | tf_op jit(solution)/shard_map/step1/pallas_call | solution.py:346
  105.2 0.7 copy-done.14
  105.9 2.1 %collective-permute-start.19 = (bf16[4,128,384]{2,1,0:T(8,128)(2,1)S(1)}, bf16[4,128,384]{2,1,0:T(8,128)(2,1)}, u32[]{:S(2)}, u32[]{:S(2)}) collective-permute-start(bf16[4,128,384]{2,1,0:T(8,128)(2,1)S(1)} %get-tuple-element.22), channel_id=1, source_target_pairs={{0,16},{1,17},{2,18},{3,19},{4,20},{5,21},{6,22},{7,23},{8,24},{9,... | collective-permute-start | bytes 1179656 | tf_op jit(solution)/shard_map/ppermute | solution.py:17
  108.0 0.5 collective-permute-start.16
  108.5 6.6 %collective-permute-done.19.refs_23_ = bf16[4,128,384]{2,1,0:T(8,128)(2,1)} collective-permute-done((bf16[4,128,384]{2,1,0:T(8,128)(2,1)S(1)}, bf16[4,128,384]{2,1,0:T(8,128)(2,1)}, u32[]{:S(2)}, u32[]{:S(2)}) %collective-permute-start.19) | collective-permute-done | bytes 393248 | tf_op jit(solution)/shard_map/ppermute | solution.py:17
  115.1 0.6 collective-permute-start.20
  115.7 4.6 %collective-permute-done.16.refs_24_ = bf16[4,128,384]{2,1,0:T(8,128)(2,1)} collective-permute-done((bf16[4,128,384]{2,1,0:T(8,128)(2,1)}, bf16[4,128,384]{2,1,0:T(8,128)(2,1)}, u32[]{:S(2)}, u32[]{:S(2)}) %collective-permute-start.16) | collective-permute-done | bytes 393248 | tf_op jit(solution)/shard_map/ppermute | solution.py:27
  120.4 0.5 collective-permute-start.21
  120.9 6.0 %collective-permute-done.20.refs_24_ = bf16[4,128,384]{2,1,0:T(8,128)(2,1)} collective-permute-done((bf16[4,128,384]{2,1,0:T(8,128)(2,1)}, bf16[4,128,384]{2,1,0:T(8,128)(2,1)}, u32[]{:S(2)}, u32[]{:S(2)}) %collective-permute-start.20) | collective-permute-done | bytes 393248 | tf_op jit(solution)/shard_map/ppermute | solution.py:27
  126.9 1.0 copy-done.3
  127.9 1.0 copy-done.5
  128.8 0.9 copy-done.7
  129.7 0.9 copy-done.9
  130.7 0.8 copy-done.11
  131.5 0.7 copy-done.13
  132.2 1.0 copy-done.15
  133.2 0.7 copy-done.22
  133.9 0.7 copy-done.26
  134.6 0.7 copy-done.29
  135.2 10.7 %step2.1 = (bf16[4,128,384]{2,1,0:T(8,128)(2,1)S(1)}, f32[384,256]{1,0:T(8,128)S(1)}) custom-call(s32[32]{0:T(128)S(1)} %copy-done.26, f32[4]{0:T(128)S(1)} %copy-done.29, bf16[16,1536]{1,0:T(8,128)(2,1)S(1)} %bitcast.33, f32[4,1,1536]{2,1,0:T(1,128)S(1)} %copy-done.13, f32[1,384]{1,0:T(1,128)S(1)} %copy-done.22, f32[4,1,512]{2,1,0:T(1,128)S(1)} %fusion.2.refs_5_, ...), custom_call_target="tpu_custom_call" | custom-call | flops 1610612736 | bytes 4718592 | tf_op jit(solution)/shard_map/step2/pallas_call | solution.py:346
  146.1 10.8 %step3.1 = (bf16[4,128,384]{2,1,0:T(8,128)(2,1)S(1)}, bf16[384,256]{1,0:T(8,128)(2,1)S(1)}) custom-call(s32[32]{0:T(128)S(1)} %copy-done.27, f32[4]{0:T(128)S(1)} %copy-done.30, bf16[16,1536]{1,0:T(8,128)(2,1)S(1)} %bitcast.34, f32[4,1,1536]{2,1,0:T(1,128)S(1)} %copy-done.13, f32[1,384]{1,0:T(1,128)S(1)} %copy-done.23, f32[4,1,512]{2,1,0:T(1,128)S(1)} %fusion.2.refs_5_, ...), custom_call_target="tpu_custom_call" | custom-call | flops 1610612736 | bytes 4718592 | tf_op jit(solution)/shard_map/step3/pallas_call | solution.py:346
  157.5 10.5 %all_to_all.15.late = bf16[4,128,384]{2,1,0:T(8,128)(2,1)} all-to-all(bf16[4,128,384]{2,1,0:T(8,128)(2,1)S(1)} %get-tuple-element.38), channel_id=1, replica_groups=mesh['pipe'=2,'seq'=4,'dp'=4] {'seq'}, dimensions={0} | all-to-all | bytes 786432 | tf_op jit(solution)/shard_map/all_to_all | solution.py:383
  168.0 3.4 %all-to-all-start.2 = ((bf16[4,96,256]{2,1,0:T(8,128)(2,1)}), bf16[4,96,256]{2,1,0:T(8,128)(2,1)S(1)}, u32[]{:S(2)}, u32[]{:S(2)}) async-start(bf16[4,96,256]{2,1,0:T(8,128)(2,1)} %bitcast.35), calls=%async_computation.2 | async-start | bytes 393216 | tf_op jit(solution)/shard_map/all_to_all | solution.py:384
  171.6 7.2 %all-to-all-done.2.parts = bf16[4,96,256]{2,1,0:T(8,128)(2,1)S(1)} async-done(((bf16[4,96,256]{2,1,0:T(8,128)(2,1)}), bf16[4,96,256]{2,1,0:T(8,128)(2,1)S(1)}, u32[]{:S(2)}, u32[]{:S(2)}) %all-to-all-start.2) | async-done | bytes 196640 | tf_op jit(solution)/shard_map/all_to_all | solution.py:384
  178.8 14.8 %all_to_all.16.early = bf16[4,2,128,384]{3,2,1,0:T(8,128)(2,1)} all-to-all(bf16[4,2,128,384]{3,2,1,0:T(8,128)(2,1)S(1)} %copy.18), channel_id=1, replica_groups=mesh['pipe'=2,'seq'=4,'dp'=4] {'seq'}, dimensions={0} | all-to-all | bytes 1572864 | tf_op jit(solution)/shard_map/all_to_all | solution.py:380
  193.5 2.4 %finish.1 = (bf16[3,128,1536]{2,1,0:T(8,128)(2,1)}, f32[96,256]{1,0:T(8,128)}) custom-call(bf16[4,2,128,384]{3,2,1,0:T(8,128)(2,1)} %all_to_all.16.early, bf16[4,128,384]{2,1,0:T(8,128)(2,1)} %all_to_all.15.late, bf16[4,96,256]{2,1,0:T(8,128)(2,1)} %copy-done.32), custom_call_target="tpu_custom_call" | custom-call | tf_op jit(solution)/shard_map/finish/pallas_call | solution.py:387
  (88 shorter events, 1.1 us)
Async XLA Ops:
  0.6 54.1 %copy-start = (f32[1,1536]{1,0:T(1,128)S(1)}, f32[1,1536]{1,0:T(1,128)}, u32[]{:S(2)}) copy-start(f32[1,1536]{1,0:T(1,128)} %param.22) | copy-start | bytes 18436
  0.6 44.9 %copy-start.31 = (s32[4,1]{0,1:T(1,128)S(1)}, s32[4,1]{0,1:T(1,128)}, u32[]{:S(2)}) copy-start(s32[4,1]{0,1:T(1,128)} %param.15) | copy-start | bytes 52
  0.7 39.2 %collective-permute-start = (bf16[3,128,1536]{2,1,0:T(8,128)(2,1)}, bf16[3,128,1536]{2,1,0:T(8,128)(2,1)S(1)}, u32[]{:S(2)}, u32[]{:S(2)}) collective-permute-start(bf16[3,128,1536]{2,1,0:T(8,128)(2,1)} %bitcast.25), channel_id=1, source_target_pairs={{0,8},{4,12},{8,0},{12,4},{1,9},{5,13},{9,1},{13,5},{2,10},{6,14},... | collective-permute-start | bytes 3538952 | tf_op jit(solution)/shard_map/ppermute | solution.py:27
  3.7 73.9 %collective-permute-start.1 = (bf16[3,128,1536]{2,1,0:T(8,128)(2,1)}, bf16[3,128,1536]{2,1,0:T(8,128)(2,1)S(1)}, u32[]{:S(2)}, u32[]{:S(2)}) collective-permute-start(bf16[3,128,1536]{2,1,0:T(8,128)(2,1)} %bitcast.26), channel_id=1, source_target_pairs={{0,4},{4,0},{8,12},{12,8},{1,5},{5,1},{9,13},{13,9},{2,6},{6,2},{1... | collective-permute-start | bytes 3538952 | tf_op jit(solution)/shard_map/ppermute | solution.py:27
  6.3 5.3 %collective-permute-start.6 = (bf16[96,768]{1,0:T(8,128)(2,1)}, bf16[96,768]{1,0:T(8,128)(2,1)}, u32[]{:S(2)}, u32[]{:S(2)}) collective-permute-start(bf16[96,768]{1,0:T(8,128)(2,1)} %get-tuple-element.17), channel_id=1, source_target_pairs={{0,4},{4,0},{8,12},{12,8},{1,5},{5,1},{9,13},{13,9},{2,6},{6,2},{1... | collective-permute-start | bytes 442376 | tf_op jit(solution)/shard_map/ppermute | solution.py:293
  6.8 26.7 %collective-permute-start.11 = (bf16[96,768]{1,0:T(8,128)(2,1)}, bf16[96,768]{1,0:T(8,128)(2,1)}, u32[]{:S(2)}, u32[]{:S(2)}) collective-permute-start(bf16[96,768]{1,0:T(8,128)(2,1)} %get-tuple-element.19), channel_id=1, source_target_pairs={{0,12},{4,8},{8,4},{12,0},{1,13},{5,9},{9,5},{13,1},{2,14},{6,10},... | collective-permute-start | bytes 442376 | tf_op jit(solution)/shard_map/ppermute | solution.py:293
  6.8 29.5 %collective-permute-start.10 = (bf16[96,768]{1,0:T(8,128)(2,1)}, bf16[96,768]{1,0:T(8,128)(2,1)}, u32[]{:S(2)}, u32[]{:S(2)}) collective-permute-start(bf16[96,768]{1,0:T(8,128)(2,1)} %get-tuple-element.18), channel_id=1, source_target_pairs={{0,8},{4,12},{8,0},{12,4},{1,9},{5,13},{9,1},{13,5},{2,10},{6,14},... | collective-permute-start | bytes 442376 | tf_op jit(solution)/shard_map/ppermute | solution.py:293
  9.0 0.6 copy-start.33
  9.0 68.6 %copy-start.1 = (bf16[1,3,1,128,1536]{4,3,2,1,0:T(8,128)(2,1)S(1)}, bf16[1,3,1,128,1536]{4,3,2,1,0:T(8,128)(2,1)}, u32[]{:S(2)}) copy-start(bf16[1,3,1,128,1536]{4,3,2,1,0:T(8,128)(2,1)} %param.12) | copy-start | bytes 3538948
  11.6 35.2 %copy-start.34 = (s32[4]{0:T(128)S(1)}, s32[4]{0:T(128)}, u32[]{:S(2)}) copy-start(s32[4]{0:T(128)} %copy-done.33) | copy-start | bytes 52
  13.4 34.1 %collective-permute-start.7 = (bf16[2,96,768]{2,1,0:T(8,128)(2,1)}, bf16[2,96,768]{2,1,0:T(8,128)(2,1)}, u32[]{:S(2)}, u32[]{:S(2)}) collective-permute-start(bf16[2,96,768]{2,1,0:T(8,128)(2,1)} %pad_maximum_fusion.1.refs_14_.refs_15_), channel_id=1, source_target_pairs={{0,1},{1,2},{2,3},{3,0},{4,5},{5,6},{6,7},{7,4},{8,9},{9,10},{10,1... | collective-permute-start | bytes 884744 | tf_op jit(solution)/shard_map/ppermute | solution.py:22
  38.0 11.1 %collective-permute-start.12 = (bf16[2,96,768]{2,1,0:T(8,128)(2,1)}, bf16[2,96,768]{2,1,0:T(8,128)(2,1)}, u32[]{:S(2)}, u32[]{:S(2)}) collective-permute-start(bf16[2,96,768]{2,1,0:T(8,128)(2,1)} %pad_maximum_fusion.2.refs_18_.refs_19_), channel_id=1, source_target_pairs={{0,1},{1,2},{2,3},{3,0},{4,5},{5,6},{6,7},{7,4},{8,9},{9,10},{10,1... | collective-permute-start | bytes 884744 | tf_op jit(solution)/shard_map/ppermute | solution.py:22
  39.8 37.8 %collective-permute-start.2 = (bf16[3,128,1536]{2,1,0:T(8,128)(2,1)S(1)}, bf16[3,128,1536]{2,1,0:T(8,128)(2,1)}, u32[]{:S(2)}, u32[]{:S(2)}) collective-permute-start(bf16[3,128,1536]{2,1,0:T(8,128)(2,1)S(1)} %collective-permute-done.refs_7_.refs_8_), channel_id=1, source_target_pairs={{0,4},{4,0},{8,12},{12,8},{1,5},{5,1},{9,13},{13,9},{2,6},{6,2},{1... | collective-permute-start | bytes 3538952 | tf_op jit(solution)/shard_map/ppermute | solution.py:27
  41.5 13.2 %collective-permute-start.3 = (bf16[400,256]{1,0:T(8,128)(2,1)}, bf16[400,256]{1,0:T(8,128)(2,1)}, u32[]{:S(2)}, u32[]{:S(2)}) collective-permute-start(bf16[400,256]{1,0:T(8,128)(2,1)} %fusion.1.refs_10_.refs_11_), channel_id=1, source_target_pairs={{0,8},{4,12},{8,0},{12,4},{1,9},{5,13},{9,1},{13,5},{2,10},{6,14},... | collective-permute-start | bytes 614408 | tf_op jit(solution)/shard_map/ppermute | solution.py:27
  47.5 12.0 %collective-permute-start.8 = (bf16[2,96,768]{2,1,0:T(8,128)(2,1)}, bf16[2,96,768]{2,1,0:T(8,128)(2,1)}, u32[]{:S(2)}, u32[]{:S(2)}) collective-permute-start(bf16[2,96,768]{2,1,0:T(8,128)(2,1)} %collective-permute-done.7.refs_15_.refs_16_), channel_id=1, source_target_pairs={{0,1},{1,2},{2,3},{3,0},{4,5},{5,6},{6,7},{7,4},{8,9},{9,10},{10,1... | collective-permute-start | bytes 884744 | tf_op jit(solution)/shard_map/ppermute | solution.py:22
  49.1 16.7 %collective-permute-start.13 = (bf16[2,96,768]{2,1,0:T(8,128)(2,1)}, bf16[2,96,768]{2,1,0:T(8,128)(2,1)}, u32[]{:S(2)}, u32[]{:S(2)}) collective-permute-start(bf16[2,96,768]{2,1,0:T(8,128)(2,1)} %collective-permute-done.12.refs_19_.refs_20_), channel_id=1, source_target_pairs={{0,1},{1,2},{2,3},{3,0},{4,5},{5,6},{6,7},{7,4},{8,9},{9,10},{10,1... | collective-permute-start | bytes 884744 | tf_op jit(solution)/shard_map/ppermute | solution.py:22
  54.7 11.8 %collective-permute-start.4 = (bf16[400,256]{1,0:T(8,128)(2,1)}, bf16[400,256]{1,0:T(8,128)(2,1)S(1)}, u32[]{:S(2)}, u32[]{:S(2)}) collective-permute-start(bf16[400,256]{1,0:T(8,128)(2,1)} %fusion.1.refs_10_.refs_11_), channel_id=1, source_target_pairs={{0,4},{4,0},{8,12},{12,8},{1,5},{5,1},{9,13},{13,9},{2,6},{6,2},{1... | collective-permute-start | bytes 614408 | tf_op jit(solution)/shard_map/ppermute | solution.py:27
  54.7 39.9 %copy-start.21 = (f32[1,384]{1,0:T(1,128)}, f32[1,384]{1,0:T(1,128)S(1)}, u32[]{:S(2)}) copy-start(f32[1,384]{1,0:T(1,128)S(1)} %constant_dynamic-slice_fusion.refs_4_) | copy-start | bytes 4612
  59.4 12.5 %collective-permute-start.9 = (bf16[2,96,768]{2,1,0:T(8,128)(2,1)}, bf16[2,96,768]{2,1,0:T(8,128)(2,1)S(1)}, u32[]{:S(2)}, u32[]{:S(2)}) collective-permute-start(bf16[2,96,768]{2,1,0:T(8,128)(2,1)} %collective-permute-done.8.refs_16_.refs_17_), channel_id=1, source_target_pairs={{0,1},{1,2},{2,3},{3,0},{4,5},{5,6},{6,7},{7,4},{8,9},{9,10},{10,1... | collective-permute-start | bytes 884744 | tf_op jit(solution)/shard_map/ppermute | solution.py:22
  65.8 11.8 %collective-permute-start.14 = (bf16[2,96,768]{2,1,0:T(8,128)(2,1)}, bf16[2,96,768]{2,1,0:T(8,128)(2,1)S(1)}, u32[]{:S(2)}, u32[]{:S(2)}) collective-permute-start(bf16[2,96,768]{2,1,0:T(8,128)(2,1)} %collective-permute-done.13.refs_20_.refs_21_), channel_id=1, source_target_pairs={{0,1},{1,2},{2,3},{3,0},{4,5},{5,6},{6,7},{7,4},{8,9},{9,10},{10,1... | collective-permute-start | bytes 884744 | tf_op jit(solution)/shard_map/ppermute | solution.py:22
  66.5 28.1 %copy-start.28 = (f32[4]{0:T(128)}, f32[4]{0:T(128)S(1)}, u32[]{:S(2)}) copy-start(f32[4]{0:T(128)S(1)} %dynamic-slice_bitcast_fusion.refs_1_) | copy-start | bytes 52
  66.5 28.1 %copy-start.6 = (bf16[400,256]{1,0:T(8,128)(2,1)}, bf16[400,256]{1,0:T(8,128)(2,1)S(1)}, u32[]{:S(2)}) copy-start(bf16[400,256]{1,0:T(8,128)(2,1)S(1)} %collective-permute-done.4.refs_12_.refs_13_) | copy-start | bytes 614404
  66.5 1.7 collective-permute-start.5
  68.2 26.4 %copy-start.8 = (bf16[400,256]{1,0:T(8,128)(2,1)}, bf16[400,256]{1,0:T(8,128)(2,1)S(1)}, u32[]{:S(2)}) copy-start(bf16[400,256]{1,0:T(8,128)(2,1)S(1)} %collective-permute-done.5.refs_13_.refs_14_) | copy-start | bytes 614404
  72.0 22.6 %copy-start.2 = (bf16[2,96,768]{2,1,0:T(8,128)(2,1)}, bf16[2,96,768]{2,1,0:T(8,128)(2,1)S(1)}, u32[]{:S(2)}) copy-start(bf16[2,96,768]{2,1,0:T(8,128)(2,1)S(1)} %collective-permute-done.9.refs_17_.refs_18_) | copy-start | bytes 884740
  77.6 17.0 %copy-start.4 = (bf16[2,96,768]{2,1,0:T(8,128)(2,1)}, bf16[2,96,768]{2,1,0:T(8,128)(2,1)S(1)}, u32[]{:S(2)}) copy-start(bf16[2,96,768]{2,1,0:T(8,128)(2,1)S(1)} %collective-permute-done.14.refs_21_.refs_22_) | copy-start | bytes 884740
  77.6 0.9 copy-start.10
  78.5 0.7 copy-start.12
  79.2 0.7 copy-start.24
  79.9 14.7 %copy-start.25 = (s32[32]{0:T(128)S(1)}, s32[32]{0:T(128)}, u32[]{:S(2)}) copy-start(s32[32]{0:T(128)} %concatenate.6.meta.refs_0_) | copy-start | bytes 388
  90.4 14.8 %copy-start.16 = (bf16[4,128,384]{2,1,0:T(8,128)(2,1)}, bf16[4,128,384]{2,1,0:T(8,128)(2,1)S(1)}, u32[]{:S(2)}) copy-start(bf16[4,128,384]{2,1,0:T(8,128)(2,1)S(1)} %get-tuple-element.20) | copy-start | bytes 1179652
  90.4 17.6 %collective-permute-start.15 = (bf16[4,128,384]{2,1,0:T(8,128)(2,1)S(1)}, bf16[4,128,384]{2,1,0:T(8,128)(2,1)}, u32[]{:S(2)}, u32[]{:S(2)}) collective-permute-start(bf16[4,128,384]{2,1,0:T(8,128)(2,1)S(1)} %get-tuple-element.20), channel_id=1, source_target_pairs={{0,16},{1,17},{2,18},{3,19},{4,20},{5,21},{6,22},{7,23},{8,24},{9,... | collective-permute-start | bytes 1179656 | tf_op jit(solution)/shard_map/ppermute | solution.py:17
  105.2 0.7 copy-start.14
  105.9 2.1 %copy-start.18 = (bf16[4,128,384]{2,1,0:T(8,128)(2,1)}, bf16[4,128,384]{2,1,0:T(8,128)(2,1)S(1)}, u32[]{:S(2)}) copy-start(bf16[4,128,384]{2,1,0:T(8,128)(2,1)S(1)} %get-tuple-element.22) | copy-start | bytes 1179652
  105.9 9.2 %collective-permute-start.19 = (bf16[4,128,384]{2,1,0:T(8,128)(2,1)S(1)}, bf16[4,128,384]{2,1,0:T(8,128)(2,1)}, u32[]{:S(2)}, u32[]{:S(2)}) collective-permute-start(bf16[4,128,384]{2,1,0:T(8,128)(2,1)S(1)} %get-tuple-element.22), channel_id=1, source_target_pairs={{0,16},{1,17},{2,18},{3,19},{4,20},{5,21},{6,22},{7,23},{8,24},{9,... | collective-permute-start | bytes 1179656 | tf_op jit(solution)/shard_map/ppermute | solution.py:17
  108.0 12.4 %collective-permute-start.16 = (bf16[4,128,384]{2,1,0:T(8,128)(2,1)}, bf16[4,128,384]{2,1,0:T(8,128)(2,1)}, u32[]{:S(2)}, u32[]{:S(2)}) collective-permute-start(bf16[4,128,384]{2,1,0:T(8,128)(2,1)} %collective-permute-done.15.refs_23_), channel_id=1, source_target_pairs={{0,8},{4,12},{8,0},{12,4},{1,9},{5,13},{9,1},{13,5},{2,10},{6,14},... | collective-permute-start | bytes 1179656 | tf_op jit(solution)/shard_map/ppermute | solution.py:27
  115.1 11.7 %collective-permute-start.20 = (bf16[4,128,384]{2,1,0:T(8,128)(2,1)}, bf16[4,128,384]{2,1,0:T(8,128)(2,1)}, u32[]{:S(2)}, u32[]{:S(2)}) collective-permute-start(bf16[4,128,384]{2,1,0:T(8,128)(2,1)} %collective-permute-done.19.refs_23_), channel_id=1, source_target_pairs={{0,8},{4,12},{8,0},{12,4},{1,9},{5,13},{9,1},{13,5},{2,10},{6,14},... | collective-permute-start | bytes 1179656 | tf_op jit(solution)/shard_map/ppermute | solution.py:27
  115.7 11.2 %collective-permute-start.17 = (bf16[4,128,384]{2,1,0:T(8,128)(2,1)}, bf16[4,128,384]{2,1,0:T(8,128)(2,1)}, u32[]{:S(2)}, u32[]{:S(2)}) collective-permute-start(bf16[4,128,384]{2,1,0:T(8,128)(2,1)} %collective-permute-done.15.refs_23_), channel_id=1, source_target_pairs={{0,4},{4,0},{8,12},{12,8},{1,5},{5,1},{9,13},{13,9},{2,6},{6,2},{1... | collective-permute-start | bytes 1179656 | tf_op jit(solution)/shard_map/ppermute | solution.py:27
  120.4 6.5 %collective-permute-start.18 = (bf16[4,128,384]{2,1,0:T(8,128)(2,1)}, bf16[4,128,384]{2,1,0:T(8,128)(2,1)}, u32[]{:S(2)}, u32[]{:S(2)}) collective-permute-start(bf16[4,128,384]{2,1,0:T(8,128)(2,1)} %collective-permute-done.16.refs_24_), channel_id=1, source_target_pairs={{0,4},{4,0},{8,12},{12,8},{1,5},{5,1},{9,13},{13,9},{2,6},{6,2},{1... | collective-permute-start | bytes 1179656 | tf_op jit(solution)/shard_map/ppermute | solution.py:27
  120.4 25.6 %collective-permute-start.21 = (bf16[4,128,384]{2,1,0:T(8,128)(2,1)}, bf16[4,128,384]{2,1,0:T(8,128)(2,1)}, u32[]{:S(2)}, u32[]{:S(2)}) collective-permute-start(bf16[4,128,384]{2,1,0:T(8,128)(2,1)} %collective-permute-done.19.refs_23_), channel_id=1, source_target_pairs={{0,4},{4,0},{8,12},{12,8},{1,5},{5,1},{9,13},{13,9},{2,6},{6,2},{1... | collective-permute-start | bytes 1179656 | tf_op jit(solution)/shard_map/ppermute | solution.py:27
  126.9 19.1 %collective-permute-start.22 = (bf16[4,128,384]{2,1,0:T(8,128)(2,1)}, bf16[4,128,384]{2,1,0:T(8,128)(2,1)}, u32[]{:S(2)}, u32[]{:S(2)}) collective-permute-start(bf16[4,128,384]{2,1,0:T(8,128)(2,1)} %collective-permute-done.20.refs_24_), channel_id=1, source_target_pairs={{0,4},{4,0},{8,12},{12,8},{1,5},{5,1},{9,13},{13,9},{2,6},{6,2},{1... | collective-permute-start | bytes 1179656 | tf_op jit(solution)/shard_map/ppermute | solution.py:27
  126.9 1.0 copy-start.3
  127.8 1.0 copy-start.5
  128.8 0.9 copy-start.7
  129.7 0.9 copy-start.9
  130.7 0.8 copy-start.11
  131.5 0.7 copy-start.13
  132.2 1.0 copy-start.15
  133.2 0.7 copy-start.22
  133.9 0.7 copy-start.26
  134.6 0.7 copy-start.29
  135.2 10.8 %copy-start.23 = (f32[1,384]{1,0:T(1,128)S(1)}, f32[1,384]{1,0:T(1,128)}, u32[]{:S(2)}) copy-start(f32[1,384]{1,0:T(1,128)} %copy-done.21) | copy-start | bytes 4612
  135.2 10.8 %copy-start.27 = (s32[32]{0:T(128)S(1)}, s32[32]{0:T(128)}, u32[]{:S(2)}) copy-start(s32[32]{0:T(128)} %concatenate.6.meta.refs_0_) | copy-start | bytes 388
  135.2 10.8 %copy-start.30 = (f32[4]{0:T(128)S(1)}, f32[4]{0:T(128)}, u32[]{:S(2)}) copy-start(f32[4]{0:T(128)} %copy-done.28) | copy-start | bytes 52
  146.0 10.8 %copy-start.17 = (bf16[4,128,384]{2,1,0:T(8,128)(2,1)S(1)}, bf16[4,128,384]{2,1,0:T(8,128)(2,1)}, u32[]{:S(2)}) copy-start(bf16[4,128,384]{2,1,0:T(8,128)(2,1)} %copy-done.16) | copy-start | bytes 1179652
  146.0 10.8 %copy-start.19 = (bf16[4,128,384]{2,1,0:T(8,128)(2,1)S(1)}, bf16[4,128,384]{2,1,0:T(8,128)(2,1)}, u32[]{:S(2)}) copy-start(bf16[4,128,384]{2,1,0:T(8,128)(2,1)} %copy-done.18) | copy-start | bytes 1179652
  156.9 0.7 copy-start.20
  168.0 10.7 %all-to-all-start.2 = ((bf16[4,96,256]{2,1,0:T(8,128)(2,1)}), bf16[4,96,256]{2,1,0:T(8,128)(2,1)S(1)}, u32[]{:S(2)}, u32[]{:S(2)}) async-start(bf16[4,96,256]{2,1,0:T(8,128)(2,1)} %bitcast.35), calls=%async_computation.2 | async-start | bytes 393216 | tf_op jit(solution)/shard_map/all_to_all | solution.py:384
  178.8 14.8 %copy-start.32 = (bf16[4,96,256]{2,1,0:T(8,128)(2,1)}, bf16[4,96,256]{2,1,0:T(8,128)(2,1)S(1)}, u32[]{:S(2)}) copy-start(bf16[4,96,256]{2,1,0:T(8,128)(2,1)S(1)} %all-to-all-done.2.parts) | copy-start | bytes 589828

commit v3 on v1

--- a/solution.py
+++ b/solution.py
@@ -1,6 +1,11 @@
+import functools
+import math
+
 import jax
 import jax.numpy as jnp
 from jax import lax
+from jax.experimental import pallas as pl
+from jax.experimental.pallas import tpu as pltpu
 from jax.sharding import PartitionSpec as P
 
 epsilon = 1e-06
@@ -17,7 +22,511 @@
     return lax.ppermute(value, axis, [(source, (source + 1) % count) for source in range(count)])
 
 
-def body(
+def swap(value, bit):
+    count = lax.axis_size("seq")
+    return lax.ppermute(value, "seq", [(source, source ^ bit) for source in range(count)])
+
+
+def shifted(value, axis, shift):
+    count = lax.axis_size(axis)
+    return lax.ppermute(value, axis, [(source, (source + shift) % count) for source in range(count)])
+
+
+def offsets_of(count):
+    offsets = [0]
+    bit = count // 2
+    while bit:
+        offsets = offsets + [offset ^ bit for offset in offsets]
+        bit //= 2
+    return offsets
+
+
+def gathered_pieces(value):
+    pieces = [value]
+    bit = lax.axis_size("seq") // 2
+    while bit:
+        pieces = pieces + [swap(piece, bit) for piece in pieces]
+        bit //= 2
+    return pieces
+
+
+def turn_and_batch(step, turns):
+    section = lax.axis_index("pipe")
+    turn = jnp.clip(step - section, 0, turns - 1)
+    return turn, turn - section + 1
+
+
+def pack_kernel(wq, wkv, *outs):
+    cols = outs[0].shape[1] // 2
+    seq = lax.axis_index("seq")
+    for m, out in enumerate(outs):
+        start = pl.multiple_of((seq ^ m) * cols, 128)
+        out[:, :cols] = wq[0, :, pl.ds(start, cols)]
+        out[:, cols:] = wkv[0, :, pl.ds(start, cols)]
+
+
+def prep_kernel(turns, *refs):
+    incoming, contacts, cotangent, first, second, states = refs[-6:]
+    steps = turns + 1
+    rows, feats = cotangent.shape[3:]
+    base = (turns - 2) * rows
+    for turn in range(turns):
+        if turn < 2:
+            first[turn] = incoming[0, turn, 0]
+        else:
+            second[(turn - 2) * rows : (turn - 1) * rows] = incoming[0, turn, 0]
+        second[base : base + rows, turn * feats : (turn + 1) * feats] = cotangent[0, turn, 0]
+    states[...] = jnp.zeros_like(states)
+    for step in range(steps):
+        _, batch = turn_and_batch(step, turns)
+        states[step : step + 1, :rows] = contacts[batch].astype(jnp.float32)
+    second[base + rows :, : states.shape[1]] = states[...].astype(jnp.bfloat16)
+
+
+def step_kernel(cfg, *refs):
+    step, has_relay, has_prev, last = cfg["step"], cfg["has_relay"], cfg["has_prev"], cfg["last"]
+    pieces, hops, head, turns = cfg["pieces"], cfg["hops"], cfg["head"], cfg["turns"]
+    heads, group, halves = cfg["heads"], cfg["group"], cfg["halves"]
+    refs = list(refs)
+
+    def take(count):
+        taken, refs[:count] = refs[:count], []
+        return taken
+
+    bias, times, table, gain, freq, gate, flags = take(7)
+    prev = take(1)[0] if has_prev else None
+    first, second = take(pieces), take(pieces)
+    chunks = take(pieces * hops)
+    relay = take(pieces * halves) if has_relay else None
+    before = take(halves) if last else None
+    if last:
+        take(pieces)
+        late = take(pieces)
+        own_grad = take(1)[0]
+        grads = take(hops - 1)
+    else:
+        outs = take(halves)
+        grad = take(1)[0]
+    xs, cot, ids, w, scaled, proj, att, keep, total, sem_x, sem_c, sem_w, sem_k = take(13)
+    offsets = offsets_of(pieces)
+    rows, width = xs.shape[1], xs.shape[2]
+    cols = att.shape[1]
+    feats = cot.shape[2]
+    w_rows = chunks[0].shape[0]
+    frames = pieces * rows
+    part = pieces // halves
+    seq, rep, section = lax.axis_index("seq"), lax.axis_index("dp"), lax.axis_index("pipe")
+    turn, batch = turn_and_batch(step, turns)
+    base = (turns - 2) * rows
+
+    def copy_of(source, target, sems, index):
+        return pltpu.make_async_copy(source, target, sems.at[index])
+
+    fresh = []
+    for i in range(pieces):
+        target = xs.at[seq ^ offsets[i]]
+        if step < 2:
+            source = first[i].at[jnp.minimum(turn, 1)]
+        else:
+            at = pl.multiple_of(jnp.clip(turn - 2, 0, turns - 3) * rows, 128)
+            source = second[i].at[pl.ds(at, rows)]
+        fresh.append(copy_of(source, target, sem_x, i * halves))
+    arrived = []
+    if has_relay:
+        for i in range(pieces):
+            lanes = pl.ds(pl.multiple_of((seq ^ offsets[i]) * cols, 128), cols)
+            for k in range(halves):
+                arrived.append(
+                    copy_of(
+                        relay[k * pieces + i],
+                        xs.at[pl.ds(k * part, part), :, lanes],
+                        sem_x,
+                        i * halves + k,
+                    )
+                )
+
+    def current(act):
+        if has_relay:
+
+            @pl.when(section == 0)
+            def _():
+                for copy in fresh:
+                    act(copy)
+
+            @pl.when(section != 0)
+            def _():
+                for copy in arrived:
+                    act(copy)
+        else:
+            for copy in fresh:
+                act(copy)
+
+    state_copies, cot_copies, w_copies, keep_copies = [], [], [], []
+    for i in range(pieces):
+        state_copies.append(
+            copy_of(
+                second[i].at[pl.ds(base + rows, 16), pl.ds(0, 128)],
+                ids.at[seq ^ offsets[i]],
+                sem_c,
+                i,
+            )
+        )
+        cot_copies.append(
+            copy_of(
+                second[i].at[pl.ds(base, rows), pl.ds(pl.multiple_of(turn * feats, 128), feats)],
+                cot.at[seq ^ offsets[i]],
+                sem_c,
+                pieces + i,
+            )
+        )
+    for m in range(pieces):
+        for hop in range(hops):
+            block = (seq ^ m) * hops + lax.rem(rep + hops - hop, hops)
+            w_copies.append(
+                copy_of(
+                    chunks[m * hops + hop],
+                    w.at[pl.ds(pl.multiple_of(block * w_rows, 16), w_rows)],
+                    sem_w,
+                    m * hops + hop,
+                )
+            )
+    if last:
+        for k in range(halves):
+            keep_copies.append(copy_of(before[k], keep.at[pl.ds(k * part, part)], sem_k, k))
+    for copy in state_copies:
+        copy.start()
+    current(lambda copy: copy.start())
+    for copy in w_copies + cot_copies + keep_copies:
+        copy.start()
+    for copy in state_copies:
+        copy.wait()
+    current(lambda copy: copy.wait())
+
+    labels = lax.broadcasted_iota(jnp.int32, (table.shape[1], rows), 0)
+    onehots = []
+    for block in range(pieces):
+        state = ids[block, step : step + 1, :].astype(jnp.float32).astype(jnp.int32)
+        onehots.append(jnp.where(labels == state, 1.0, 0.0).T.astype(jnp.bfloat16))
+    onehot = jnp.concatenate(onehots, axis=0)
+    time = times[batch, 0].astype(jnp.float32)
+    mod = gain[...] * (1.0 + 0.5 * jnp.sin(time * freq[...]))
+    tile = 256
+    square = jnp.zeros((frames, 128), jnp.float32)
+    for at in range(0, width, tile):
+        hidden = xs[:, :, at : at + tile].reshape(frames, tile).astype(jnp.float32) + jnp.dot(
+            onehot, table[0, :, at : at + tile], preferred_element_type=jnp.float32
+        )
+        for lane in range(0, tile, 128):
+            piece = hidden[:, lane : lane + 128]
+            square = square + piece * piece
+        scaled[:, at : at + tile] = (hidden * mod[:, at : at + tile]).astype(jnp.bfloat16)
+    scale = lax.rsqrt(jnp.sum(square, axis=1, keepdims=True) * (1.0 / width) + epsilon)
+    for copy in w_copies:
+        copy.wait()
+    for at in range(0, 2 * cols, tile):
+        proj[:, at : at + tile] = (
+            jnp.dot(scaled[...], w[:, at : at + tile], preferred_element_type=jnp.float32) * scale
+        ).astype(jnp.bfloat16)
+    score_scale = head ** (-0.5) * math.log2(math.e)
+    lanes = lax.broadcasted_iota(jnp.int32, (frames, 128), 1)
+    flag_row = flags[batch].astype(jnp.float32) * math.log2(math.e)
+    for kv in range(heads // group):
+        base = cols + kv * 2 * head
+        keys = proj[:, base : base + head]
+        values = proj[:, base + head : base + head + 128].astype(jnp.float32)
+        values = jnp.where(lanes < head, values, jnp.where(lanes == head, 1.0, 0.0)).astype(
+            jnp.bfloat16
+        )
+        for h in range(kv * group, (kv + 1) * group):
+            queries = proj[:, h * head : (h + 1) * head]
+            scores = lax.dot_general(
+                queries, keys, (((1,), (1,)), ((), ())), preferred_element_type=jnp.float32
+            )
+            scores = scores * score_scale + flag_row * bias[0, seq * heads + h]
+            top = jnp.max(scores, axis=1, keepdims=True)
+            weight = jnp.exp2(scores - top).astype(jnp.bfloat16)
+            mixed = jnp.dot(weight, values, preferred_element_type=jnp.float32)
+            att[:, h * head : (h + 1) * head] = mixed[:, :head] / mixed[:, head : head + 1]
+    own = pl.ds(pl.multiple_of(seq * cols, 128), cols)
+    hidden = xs[:, :, own].reshape(frames, cols).astype(jnp.float32) + jnp.dot(
+        onehot, table[0, :, own], preferred_element_type=jnp.float32
+    )
+    attended = att[...].astype(jnp.bfloat16).astype(jnp.float32)
+    output = (hidden + gate[:, own] * attended).astype(jnp.bfloat16)
+    for copy in cot_copies:
+        copy.wait()
+    share = lax.dot_general(
+        output,
+        cot[...].reshape(frames, feats),
+        (((0,), (0,)), ((), ())),
+        preferred_element_type=jnp.float32,
+    )
+    valid = jnp.logical_and(step >= section, step < turns + section)
+    share = jnp.where(valid, share, 0.0)
+    if has_prev:
+        share = share + prev[...]
+    blocks = output.reshape(pieces, rows, cols)
+    if not last:
+        for k in range(halves):
+            outs[k][...] = blocks[k * part : (k + 1) * part]
+        grad[...] = share
+        return
+    for copy in keep_copies:
+        copy.wait()
+
+    @pl.when(section != 0)
+    def _():
+        keep[...] = blocks
+
+    for m in range(pieces):
+        late[m][...] = keep[seq ^ m]
+    total[...] = share * float(turns * hops * frames) ** (-0.5)
+    g_rows = cols // hops
+    own_grad[...] = total[pl.ds(pl.multiple_of(rep * g_rows, 8), g_rows)]
+    for shift in range(1, hops):
+        at = pl.multiple_of(lax.rem(rep + shift, hops) * g_rows, 8)
+        grads[shift - 1][...] = total[pl.ds(at, g_rows)].astype(jnp.bfloat16)
+
+
+def early_kernel(turns, pieces, halves, *refs):
+    outs, sends = refs[: turns * halves], refs[turns * halves : turns * halves + pieces]
+    keep, sems = refs[turns * halves + pieces :]
+    section, seq = lax.axis_index("pipe"), lax.axis_index("seq")
+    part = pieces // halves
+
+    def copies(skew):
+        return [
+            pltpu.make_async_copy(
+                outs[(turn + skew) * halves + k],
+                keep.at[turn, pl.ds(k * part, part)],
+                sems.at[turn * halves + k],
+            )
+            for turn in range(turns - 1)
+            for k in range(halves)
+        ]
+
+    @pl.when(section == 0)
+    def _():
+        for copy in copies(0):
+            copy.start()
+        for copy in copies(0):
+            copy.wait()
+
+    @pl.when(section != 0)
+    def _():
+        for copy in copies(1):
+            copy.start()
+        for copy in copies(1):
+            copy.wait()
+
+    for m in range(pieces):
+        for turn in range(turns - 1):
+            sends[m][turn] = keep[turn, seq ^ m]
+
+
+def finish_kernel(pieces, hops, *refs):
+    early, late, refs = refs[:pieces], refs[pieces : 2 * pieces], refs[2 * pieces :]
+    own_grad, parts, (section_out, grad) = refs[0], refs[1:hops], refs[hops:]
+    seq = lax.axis_index("seq")
+    turns_early, _, cols = early[0].shape
+    for m in range(pieces):
+        lanes = pl.ds(pl.multiple_of((seq ^ m) * cols, 128), cols)
+        for turn in range(turns_early):
+            section_out[turn, :, lanes] = early[m][turn]
+        section_out[turns_early, :, lanes] = late[m][...]
+    total = own_grad[...]
+    for part in parts:
+        total = total + part[...].astype(jnp.float32)
+    grad[...] = total
+
+
+VMEM_LIMIT = 40 * 1024 * 1024
+HALVES = 2
+
+
+def paired_body(
+    incoming,
+    contacts,
+    keyframes,
+    timesteps,
+    w_query,
+    w_keyval,
+    norm_gain,
+    time_freq,
+    contact_table,
+    key_bias,
+    attn_gate,
+    head_cotangent,
+):
+    seq_count = lax.axis_size("seq")
+    hops = lax.axis_size("dp")
+    rows, width, turns = incoming.shape[3], incoming.shape[4], incoming.shape[1]
+    frames = rows * seq_count
+    heads_all = key_bias.shape[1]
+    head = width // heads_all
+    heads = heads_all // seq_count
+    kv_heads = w_keyval.shape[2] // (2 * head * seq_count)
+    feats = head_cotangent.shape[4]
+    cols = width // seq_count
+    w_rows = w_query.shape[1]
+    steps = turns + 1
+    part = seq_count // HALVES
+    kind = jnp.bfloat16
+    smem = pl.BlockSpec(memory_space=pltpu.SMEM)
+    vmem = pl.BlockSpec(memory_space=pltpu.VMEM)
+    hbm = pl.BlockSpec(memory_space=pltpu.HBM)
+    params = pltpu.CompilerParams(vmem_limit_bytes=VMEM_LIMIT)
+    shape = jax.ShapeDtypeStruct
+
+    packed = pl.pallas_call(
+        pack_kernel,
+        out_shape=[shape((w_rows, 2 * cols), kind)] * seq_count,
+        in_specs=[vmem, vmem],
+        out_specs=[vmem] * seq_count,
+        name="pack",
+    )(w_query, w_keyval)
+    blocks = [packed[0]] + [swap(packed[m], m) for m in range(1, seq_count)]
+    chunks = [[block] for block in blocks]
+    for hop in range(1, hops):
+        for m in range(seq_count):
+            chunks[m].append(shifted(chunks[m][-1], "dp", 1))
+
+    waits = blocks[seq_count // 2 :] + [ring[1] for ring in chunks[: seq_count // 2]]
+    first, second = pl.pallas_call(
+        functools.partial(prep_kernel, turns),
+        out_shape=[
+            shape((2, rows, width), kind),
+            shape(((turns - 1) * rows + 16, width), kind),
+        ],
+        in_specs=[hbm] * len(waits) + [vmem] * 3,
+        out_specs=[vmem] * 2,
+        scratch_shapes=[pltpu.VMEM((16, 128), jnp.float32)],
+        compiler_params=params,
+        name="prep",
+    )(*waits, incoming, contacts, head_cotangent)
+    loose = gathered_pieces(first) + gathered_pieces(second)
+    loose = loose + [chunk for ring in chunks for chunk in ring]
+
+    outputs = []
+    relayed = {}
+    grad = None
+    for step in range(steps):
+        last = step + 1 == steps
+        cfg = {
+            "step": step,
+            "has_relay": step in relayed,
+            "has_prev": grad is not None,
+            "last": last,
+            "pieces": seq_count,
+            "hops": hops,
+            "head": head,
+            "heads": heads,
+            "group": heads // kv_heads,
+            "turns": turns,
+            "halves": HALVES,
+        }
+        operands = [key_bias, timesteps, contact_table, norm_gain, time_freq, attn_gate, keyframes]
+        specs = [smem, smem] + [vmem] * 5
+        if grad is not None:
+            operands.append(grad)
+            specs.append(vmem)
+        pieces = loose + relayed.get(step, [])
+        if last:
+            early = pl.pallas_call(
+                functools.partial(early_kernel, turns, seq_count, HALVES),
+                out_shape=[shape((turns - 1, rows, cols), kind)] * seq_count,
+                in_specs=[hbm] * (turns * HALVES),
+                out_specs=[vmem] * seq_count,
+                scratch_shapes=[
+                    pltpu.VMEM((turns - 1, seq_count, rows, cols), kind),
+                    pltpu.SemaphoreType.DMA(((turns - 1) * HALVES,)),
+                ],
+                compiler_params=params,
+                name="early",
+            )(*[half for output in outputs for half in output])
+            pieces = pieces + list(outputs[-1]) + list(early)
+        if last:
+            out_shape = [shape((rows, cols), kind)] * seq_count
+            out_shape += [shape((cols // hops, feats), jnp.float32)]
+            out_shape += [shape((cols // hops, feats), kind)] * (hops - 1)
+        else:
+            out_shape = [shape((part, rows, cols), kind)] * HALVES
+            out_shape += [shape((cols, feats), jnp.float32)]
+        results = pl.pallas_call(
+            functools.partial(step_kernel, cfg),
+            out_shape=out_shape,
+            in_specs=specs + [hbm] * len(pieces),
+            out_specs=[vmem] * len(out_shape),
+            scratch_shapes=[
+                pltpu.VMEM((seq_count, rows, width), kind),
+                pltpu.VMEM((seq_count, rows, feats), kind),
+                pltpu.VMEM((seq_count, 16, 128), kind),
+                pltpu.VMEM((width, 2 * cols), kind),
+                pltpu.VMEM((frames, width), kind),
+                pltpu.VMEM((frames, 2 * cols + 128), kind),
+                pltpu.VMEM((frames, cols), jnp.float32),
+                pltpu.VMEM((seq_count, rows, cols), kind),
+                pltpu.VMEM((cols, feats), jnp.float32),
+                pltpu.SemaphoreType.DMA((seq_count * HALVES,)),
+                pltpu.SemaphoreType.DMA((2 * seq_count,)),
+                pltpu.SemaphoreType.DMA((seq_count * hops,)),
+                pltpu.SemaphoreType.DMA((HALVES,)),
+            ],
+            compiler_params=params,
+            cost_estimate=pl.CostEstimate(
+                flops=2 * frames * width * 2 * cols + 4 * heads * frames * frames * head,
+                bytes_accessed=6 * frames * width,
+                transcendentals=heads * frames * frames,
+            ),
+            name="step%d" % step,
+        )(*operands, *pieces)
+        results = list(results)
+        if last:
+            break
+        outputs.append(results[:HALVES])
+        grad = results[HALVES]
+        if step + 2 < steps:
+            relayed[step + 2] = [
+                piece
+                for half in outputs[-1]
+                for piece in gathered_pieces(passed_along(half, "pipe", 1))
+            ]
+
+    early = [early[0]] + [swap(early[m], m) for m in range(1, seq_count)]
+    late = results[:seq_count]
+    late = [late[0]] + [swap(late[m], m) for m in range(1, seq_count)]
+    grads = results[seq_count:]
+    grads = [grads[0]] + [shifted(grads[k], "dp", k) for k in range(1, hops)]
+    section_out, grad_rows = pl.pallas_call(
+        functools.partial(finish_kernel, seq_count, hops),
+        out_shape=[
+            shape((turns, rows, width), kind),
+            shape((cols // hops, feats), jnp.float32),
+        ],
+        in_specs=[vmem] * (2 * seq_count + hops),
+        out_specs=[vmem] * 2,
+        compiler_params=params,
+        name="finish",
+    )(*early, *late, *grads)
+    return (section_out[None, :, None], grad_rows[None])
+
+
+def body(incoming, contacts, keyframes, timesteps, w_query, *others):
+    count = lax.axis_size("seq")
+    cols = w_query.shape[2] // count
+    paired = (
+        lax.axis_size("pipe") == 2
+        and count in (2, 4, 8)
+        and cols % 128 == 0
+        and w_query.shape[1] % 16 == 0
+        and incoming.shape[3] == 128
+        and incoming.shape[1] < 8
+    )
+    chosen = paired_body if paired else general_body
+    return chosen(incoming, contacts, keyframes, timesteps, w_query, *others)
+
+
+def general_body(
     incoming,
     contacts,
     keyframes,

time: 238 us -> 198 us (0.83)
  Pallas kernels: 0 us -> 47.4 us
  matrix products: 38.9 us -> 0 us
  blocking collectives: 34.1 us -> 0 us
  between operations: 17.4 us -> 1.05 us
  other arithmetic: 15.3 us -> 0 us
  waiting for transfers between devices: 80.5 us -> 92.2 us
  starting transfers between devices: 25.8 us -> 32.2 us
    ppermute x3 -> x42, waiting for transfers between devices: 31.1 us -> 90.8 us  [the longest x15 55.5 us: shifted(): lax.ppermute(value, axis, [(source, (source + shift) % count) for source...]
    pallas_call x0 -> x8, Pallas kernels: none -> 47.4 us  [the longest x4 42.2 us: paired_body(): pl.pallas_call(functools.partial(step_kernel, cfg), out_shape=out_shape,...]
    dot_general x47 -> x0, matrix products: 38.9 us -> none  [the longest x4 8.13 us: body(): jnp.dot(onehot, table, preferred_element_type=jnp.float32)]
    all_gather x6 -> x0, waiting for transfers between devices: 25.1 us -> none  [the longest x2 21.1 us: body(): handed[step + lag] = lax.all_gather(piece, 'seq', axis=1, tiled=True)]
    ppermute x3 -> x42, starting transfers between devices: 1.67 us -> 24.6 us  [the longest x27 14.7 us: swap(): lax.ppermute(value, 'seq', [(source, source ^ bit) for source in range(co...]
    all_gather x2 -> x0, blocking collectives: 17.6 us -> none  [the longest x1 12.5 us: body(): cot_all = lax.all_gather(head_cotangent[0, :, 0], 'seq', axis=1, tiled=True)]
    unnamed x58 -> x89, local copies, waits for them, and re-layouts: 7.22 us -> 24.1 us
    all_to_all x1 -> x0, blocking collectives: 16.5 us -> none  [body(): lax.all_to_all(w_parts, 'seq', split_axis=0, concat_axis=0, tiled=True)]
  transfers between devices with their start and end apart: 15 -> 46, of which waited for: 10 -> 23; matrix products, arithmetic and copies ran while one was open for 25% -> 1% of each run, Pallas kernels for 0% -> 11%
where the time goes in v3:
time: 198 us; the launch traced here: 197 us
  waiting for transfers between devices  92.2 us (47%)
  Pallas kernels  47.4 us (24%)
  starting transfers between devices  32.2 us (16%)
  local copies, waits for them, and re-layouts  24.1 us (12%)
    ppermute x15, waiting for transfers between devices, shifted(): lax.ppermute(value, axis, [(source, (source + shift) % count) for source...  55.5 us
    pallas_call x4, Pallas kernels, paired_body(): pl.pallas_call(functools.partial(step_kernel, cfg), out_shape=out_shape,...  42.2 us
    ppermute x27, waiting for transfers between devices, swap(): lax.ppermute(value, 'seq', [(source, source ^ bit) for source in range(co...  35.3 us
    unnamed x89, local copies, waits for them, and re-layouts  24.1 us
    ppermute x27, starting transfers between devices, swap(): lax.ppermute(value, 'seq', [(source, source ^ bit) for source in range(co...  14.7 us
    ppermute x15, starting transfers between devices, shifted(): lax.ppermute(value, axis, [(source, (source + shift) % count) for source...  9.93 us
    ppermute x4, starting transfers between devices, passed_along(): lax.ppermute(value, axis, [(source, source + steps) for source in range(f...  7.59 us
  transfers between devices with their start and end apart: 46, of which 23 were waited for; matrix products, arithmetic and copies ran while one was open for 1% of the time, Pallas kernels for 11%

profile of v3, /device:TPU:0, one launch (start us, length us, event | category | flops | bytes accessed | tf_op | source)
XLA Modules:
  0.0 196.9 jit_solution(2150266534126424765)
XLA Ops:
  0.7 1.9 pack.1
  3.0 2.6 %collective-permute-start.2 = (bf16[96,768]{1,0:T(8,128)(2,1)}, bf16[96,768]{1,0:T(8,128)(2,1)S(1)}, u32[]{:S(2)}, u32[]{:S(2)}) collective-permute-start(bf16[96,768]{1,0:T(8,128)(2,1)} %get-tuple-element.33.refs_15_.refs_16_), channel_id=1, source_target_pairs={{0,1},{1,2},{2,3},{3,0},{4,5},{5,6},{6,7},{7,4},{8,9},{9,10},{10,1... | collective-permute-start | bytes 442376 | tf_op jit(solution)/shard_map/ppermute | solution.py:32
  5.6 1.5 collective-permute-start
  7.2 1.6 collective-permute-start.4
  8.8 3.8 %collective-permute-done.2.refs_2_.refs_16_.refs_17_ = bf16[96,768]{1,0:T(8,128)(2,1)S(1)} collective-permute-done((bf16[96,768]{1,0:T(8,128)(2,1)}, bf16[96,768]{1,0:T(8,128)(2,1)S(1)}, u32[]{:S(2)}, u32[]{:S(2)}) %collective-permute-start.2) | collective-permute-done | bytes 147488 | tf_op jit(solution)/shard_map/ppermute | solution.py:32
  12.6 1.7 collective-permute-done.1.refs_1_.refs_27_.refs_28_
  14.3 1.3 collective-permute-done.4.refs_3_.refs_20_.refs_21_
  15.5 1.3 copy-done.34
  16.8 0.9 copy-done.36
  18.4 1.0 prep.1
  19.4 1.5 collective-permute-start.8
  21.8 1.6 collective-permute-start.18
  23.4 0.9 collective-permute-start.11
  24.3 5.7 %collective-permute-done.15.refs_24_.refs_25_ = bf16[96,768]{1,0:T(8,128)(2,1)S(1)} collective-permute-done((bf16[96,768]{1,0:T(8,128)(2,1)S(1)}, bf16[96,768]{1,0:T(8,128)(2,1)S(1)}, u32[]{:S(2)}, u32[]{:S(2)}) %collective-permute-start.15) | collective-permute-done | bytes 147488 | tf_op jit(solution)/shard_map/ppermute | solution.py:32
  30.0 3.2 %collective-permute-done.18.refs_28_.refs_29_ = bf16[96,768]{1,0:T(8,128)(2,1)S(1)} collective-permute-done((bf16[96,768]{1,0:T(8,128)(2,1)S(1)}, bf16[96,768]{1,0:T(8,128)(2,1)S(1)}, u32[]{:S(2)}, u32[]{:S(2)}) %collective-permute-start.18) | collective-permute-done | bytes 147488 | tf_op jit(solution)/shard_map/ppermute | solution.py:32
  33.8 2.5 %collective-permute-done.11.refs_17_.refs_18_ = bf16[96,768]{1,0:T(8,128)(2,1)S(1)} collective-permute-done((bf16[96,768]{1,0:T(8,128)(2,1)S(1)}, bf16[96,768]{1,0:T(8,128)(2,1)S(1)}, u32[]{:S(2)}, u32[]{:S(2)}) %collective-permute-start.11) | collective-permute-done | bytes 147488 | tf_op jit(solution)/shard_map/ppermute | solution.py:32
  36.3 4.5 %collective-permute-done.8.refs_12_.refs_13_ = bf16[272,1536]{1,0:T(8,128)(2,1)S(1)} collective-permute-done((bf16[272,1536]{1,0:T(8,128)(2,1)S(1)}, bf16[272,1536]{1,0:T(8,128)(2,1)S(1)}, u32[]{:S(2)}, u32[]{:S(2)}) %collective-permute-start.8) | collective-permute-done | bytes 835616 | tf_op jit(solution)/shard_map/ppermute | solution.py:27
  41.5 15.2 %collective-permute-done.5.refs_8_.refs_9_ = bf16[2,128,1536]{2,1,0:T(8,128)(2,1)} collective-permute-done((bf16[2,128,1536]{2,1,0:T(8,128)(2,1)}, bf16[2,128,1536]{2,1,0:T(8,128)(2,1)}, u32[]{:S(2)}, u32[]{:S(2)}) %collective-permute-start.5) | collective-permute-done | bytes 786464 | tf_op jit(solution)/shard_map/ppermute | solution.py:27
  56.7 1.0 collective-permute-start.19
  58.4 6.5 %collective-permute-done.19.refs_29_.refs_30_ = bf16[96,768]{1,0:T(8,128)(2,1)} collective-permute-done((bf16[96,768]{1,0:T(8,128)(2,1)S(1)}, bf16[96,768]{1,0:T(8,128)(2,1)}, u32[]{:S(2)}, u32[]{:S(2)}) %collective-permute-start.19) | collective-permute-done | bytes 147488 | tf_op jit(solution)/shard_map/ppermute | solution.py:32
  65.5 6.6 %collective-permute-done.12.refs_18_.refs_19_ = bf16[96,768]{1,0:T(8,128)(2,1)S(1)} collective-permute-done((bf16[96,768]{1,0:T(8,128)(2,1)S(1)}, bf16[96,768]{1,0:T(8,128)(2,1)S(1)}, u32[]{:S(2)}, u32[]{:S(2)}) %collective-permute-start.12) | collective-permute-done | bytes 147488 | tf_op jit(solution)/shard_map/ppermute | solution.py:32
  73.5 6.3 %collective-permute-done.14.refs_22_.refs_23_ = bf16[96,768]{1,0:T(8,128)(2,1)S(1)} collective-permute-done((bf16[96,768]{1,0:T(8,128)(2,1)S(1)}, bf16[96,768]{1,0:T(8,128)(2,1)S(1)}, u32[]{:S(2)}, u32[]{:S(2)}) %collective-permute-start.14) | collective-permute-done | bytes 147488 | tf_op jit(solution)/shard_map/ppermute | solution.py:32
  81.0 6.3 %collective-permute-done.17.refs_26_.refs_27_ = bf16[96,768]{1,0:T(8,128)(2,1)S(1)} collective-permute-done((bf16[96,768]{1,0:T(8,128)(2,1)S(1)}, bf16[96,768]{1,0:T(8,128)(2,1)S(1)}, u32[]{:S(2)}, u32[]{:S(2)}) %collective-permute-start.17) | collective-permute-done | bytes 147488 | tf_op jit(solution)/shard_map/ppermute | solution.py:32
  88.0 1.3 copy.14.refs_1_
  89.3 5.9 %collective-permute-done.20.refs_30_.refs_31_ = bf16[96,768]{1,0:T(8,128)(2,1)} collective-permute-done((bf16[96,768]{1,0:T(8,128)(2,1)}, bf16[96,768]{1,0:T(8,128)(2,1)}, u32[]{:S(2)}, u32[]{:S(2)}) %collective-permute-start.20) | collective-permute-done | bytes 147488 | tf_op jit(solution)/shard_map/ppermute | solution.py:32
  95.3 0.9 copy-done.1
  96.2 0.9 copy-done.4
  97.1 0.9 copy-done.7
  98.0 0.9 copy-done.9
  99.0 0.9 copy-done.12
  99.9 0.9 copy-done.15
  100.8 0.9 copy-done.18
  101.7 0.9 copy-done.21
  102.6 0.9 copy-done.24
  103.5 0.9 copy-done.26
  104.4 0.9 copy-done.28
  105.3 0.9 copy-done.31
  106.2 0.9 copy-done.33
  107.8 0.7 copy-done.40
  109.9 9.9 %step0.1 = (bf16[2,128,384]{2,1,0:T(8,128)(2,1)S(1)}, bf16[2,128,384]{2,1,0:T(8,128)(2,1)S(1)}, f32[384,256]{1,0:T(8,128)S(1)}) custom-call(f32[1,16]{1,0:T(1,128)S(1)} %copy-done.42, s32[4,1]{1,0:T(4,128)S(1)} %copy-done.41, bf16[1,16,1536]{2,1,0:T(8,128)(2,1)S(1)} %copy-done.35, f32[1,1536]{1,0:T(1,128)S(1)} %copy-done.38, f32[1,1536]{1,0:T(1,128)S(1)} %copy-done.39, ...), custom_call_target="tpu_custom_call" | custom-call | flops 1610612736 | bytes 4718592 | tf_op jit(solution)/shard_map/step0/pallas_call | solution.py:455
  119.8 3.5 %collective-permute-start.21 = (bf16[2,128,384]{2,1,0:T(8,128)(2,1)S(1)}, bf16[2,128,384]{2,1,0:T(8,128)(2,1)S(1)}, u32[]{:S(2)}, u32[]{:S(2)}) collective-permute-start(bf16[2,128,384]{2,1,0:T(8,128)(2,1)S(1)} %get-tuple-element.37.refs_0_), channel_id=1, source_target_pairs={{0,16},{1,17},{2,18},{3,19},{4,20},{5,21},{6,22},{7,23},{8,24},{9,... | collective-permute-start | bytes 589832 | tf_op jit(solution)/shard_map/ppermute | solution.py:17
  123.3 1.5 collective-permute-start.25
  124.8 10.0 %step1.1 = (bf16[2,128,384]{2,1,0:T(8,128)(2,1)S(1)}, bf16[2,128,384]{2,1,0:T(8,128)(2,1)S(1)}, f32[384,256]{1,0:T(8,128)S(1)}) custom-call(f32[1,16]{1,0:T(1,128)S(1)} %copy-done.42, s32[4,1]{1,0:T(4,128)S(1)} %copy-done.41, bf16[1,16,1536]{2,1,0:T(8,128)(2,1)S(1)} %copy-done.35, f32[1,1536]{1,0:T(1,128)S(1)} %copy-done.38, f32[1,1536]{1,0:T(1,128)S(1)} %copy-done.39, ...), custom_call_target="tpu_custom_call" | custom-call | flops 1610612736 | bytes 4718592 | tf_op jit(solution)/shard_map/step1/pallas_call | solution.py:455
  134.8 1.3 collective-permute-start.32
  136.1 1.3 collective-permute-start.36
  137.4 1.6 collective-permute-start.22
  140.0 1.3 collective-permute-done.36.refs_36_
  141.4 1.5 collective-permute-start.33
  143.5 1.5 collective-permute-start.37
  145.0 2.7 %collective-permute-done.26.refs_37_ = bf16[2,128,384]{2,1,0:T(8,128)(2,1)S(1)} collective-permute-done((bf16[2,128,384]{2,1,0:T(8,128)(2,1)S(1)}, bf16[2,128,384]{2,1,0:T(8,128)(2,1)S(1)}, u32[]{:S(2)}, u32[]{:S(2)}) %collective-permute-start.26) | collective-permute-done | bytes 196640 | tf_op jit(solution)/shard_map/ppermute | solution.py:27
  148.3 3.2 %collective-permute-done.33.refs_33_ = bf16[2,128,384]{2,1,0:T(8,128)(2,1)S(1)} collective-permute-done((bf16[2,128,384]{2,1,0:T(8,128)(2,1)S(1)}, bf16[2,128,384]{2,1,0:T(8,128)(2,1)S(1)}, u32[]{:S(2)}, u32[]{:S(2)}) %collective-permute-start.33) | collective-permute-done | bytes 196640 | tf_op jit(solution)/shard_map/ppermute | solution.py:27
  151.6 2.1 %collective-permute-done.37.refs_37_ = bf16[2,128,384]{2,1,0:T(8,128)(2,1)S(1)} collective-permute-done((bf16[2,128,384]{2,1,0:T(8,128)(2,1)S(1)}, bf16[2,128,384]{2,1,0:T(8,128)(2,1)S(1)}, u32[]{:S(2)}, u32[]{:S(2)}) %collective-permute-start.37) | collective-permute-done | bytes 196640 | tf_op jit(solution)/shard_map/ppermute | solution.py:27
  154.2 10.7 %step2.1 = (bf16[2,128,384]{2,1,0:T(8,128)(2,1)S(1)}, bf16[2,128,384]{2,1,0:T(8,128)(2,1)S(1)}, f32[384,256]{1,0:T(8,128)S(1)}) custom-call(f32[1,16]{1,0:T(1,128)S(1)} %copy-done.42, s32[4,1]{1,0:T(4,128)S(1)} %copy-done.41, bf16[1,16,1536]{2,1,0:T(8,128)(2,1)S(1)} %copy-done.35, f32[1,1536]{1,0:T(1,128)S(1)} %copy-done.38, f32[1,1536]{1,0:T(1,128)S(1)} %copy-done.39, ...), custom_call_target="tpu_custom_call" | custom-call | flops 1610612736 | bytes 4718592 | tf_op jit(solution)/shard_map/step2/pallas_call | solution.py:455
  165.0 1.1 early.1
  166.2 11.6 %step3.1 = (bf16[128,384]{1,0:T(8,128)(2,1)S(1)}, bf16[128,384]{1,0:T(8,128)(2,1)S(1)}, bf16[128,384]{1,0:T(8,128)(2,1)S(1)}, bf16[128,384]{1,0:T(8,128)(2,1)S(1...) custom-call(f32[1,16]{1,0:T(1,128)S(1)} %copy-done.42, ...), custom_call_target="tpu_custom_call" | custom-call | flops 1610612736 | bytes 4718592 | tf_op jit(solution)/shard_map/step3/pallas_call | solution.py:455
  178.6 1.5 collective-permute-start.30
  180.1 4.0 %collective-permute-done.43.refs_9_ = bf16[96,256]{1,0:T(8,128)(2,1)S(1)} collective-permute-done((bf16[96,256]{1,0:T(8,128)(2,1)S(1)}, bf16[96,256]{1,0:T(8,128)(2,1)S(1)}, u32[]{:S(2)}, u32[]{:S(2)}) %collective-permute-start.43) | collective-permute-done | bytes 49184 | tf_op jit(solution)/shard_map/ppermute | solution.py:32
  184.1 1.0 collective-permute-done.44.refs_10_
  185.0 1.7 collective-permute-start.45
  186.7 2.6 %collective-permute-done.45.refs_11_ = bf16[96,256]{1,0:T(8,128)(2,1)S(1)} collective-permute-done((bf16[96,256]{1,0:T(8,128)(2,1)S(1)}, bf16[96,256]{1,0:T(8,128)(2,1)S(1)}, u32[]{:S(2)}, u32[]{:S(2)}) %collective-permute-start.45) | collective-permute-done | bytes 49184 | tf_op jit(solution)/shard_map/ppermute | solution.py:32
  189.4 1.3 collective-permute-start.41
  190.7 3.7 %collective-permute-done.41.refs_6_ = bf16[128,384]{1,0:T(8,128)(2,1)S(1)} collective-permute-done((bf16[128,384]{1,0:T(8,128)(2,1)S(1)}, bf16[128,384]{1,0:T(8,128)(2,1)S(1)}, u32[]{:S(2)}, u32[]{:S(2)}) %collective-permute-start.41) | collective-permute-done | bytes 98336 | tf_op jit(solution)/shard_map/ppermute | solution.py:27
  194.4 1.3 collective-permute-done.42.refs_7_
  195.7 1.2 finish.1
  (125 shorter events, 13.7 us)
Async XLA Ops:
  0.6 94.6 %copy-start.37 = (s32[4,1,512]{2,1,0:T(1,128)S(1)}, s32[4,1,512]{2,1,0:T(1,128)}, u32[]{:S(2)}) copy-start(s32[4,1,512]{2,1,0:T(1,128)} %refs_6_.9) | copy-start | bytes 24580
  0.6 94.6 %copy-start.38 = (f32[1,1536]{1,0:T(1,128)S(1)}, f32[1,1536]{1,0:T(1,128)}, u32[]{:S(2)}) copy-start(f32[1,1536]{1,0:T(1,128)} %refs_3_.7) | copy-start | bytes 18436
  0.7 94.6 %copy-start.35 = (bf16[1,16,1536]{2,1,0:T(8,128)(2,1)S(1)}, bf16[1,16,1536]{2,1,0:T(8,128)(2,1)}, u32[]{:S(2)}) copy-start(bf16[1,16,1536]{2,1,0:T(8,128)(2,1)} %refs_2_.7) | copy-start | bytes 147460
  2.6 4.6 %collective-permute-start.3 = (bf16[96,768]{1,0:T(8,128)(2,1)}, bf16[96,768]{1,0:T(8,128)(2,1)S(1)}, u32[]{:S(2)}, u32[]{:S(2)}) collective-permute-start(bf16[96,768]{1,0:T(8,128)(2,1)} %get-tuple-element.34), channel_id=1, source_target_pairs={{0,4},{4,0},{8,12},{12,8},{1,5},{5,1},{9,13},{13,9},{2,6},{6,2},{1... | collective-permute-start | bytes 442376 | tf_op jit(solution)/shard_map/ppermute | solution.py:27
  3.0 9.5 %collective-permute-start.2 = (bf16[96,768]{1,0:T(8,128)(2,1)}, bf16[96,768]{1,0:T(8,128)(2,1)S(1)}, u32[]{:S(2)}, u32[]{:S(2)}) collective-permute-start(bf16[96,768]{1,0:T(8,128)(2,1)} %get-tuple-element.33.refs_15_.refs_16_), channel_id=1, source_target_pairs={{0,1},{1,2},{2,3},{3,0},{4,5},{5,6},{6,7},{7,4},{8,9},{9,10},{10,1... | collective-permute-start | bytes 442376 | tf_op jit(solution)/shard_map/ppermute | solution.py:32
  5.6 6.9 %collective-permute-start = (bf16[96,768]{1,0:T(8,128)(2,1)}, bf16[96,768]{1,0:T(8,128)(2,1)S(1)}, u32[]{:S(2)}, u32[]{:S(2)}) collective-permute-start(bf16[96,768]{1,0:T(8,128)(2,1)} %get-tuple-element.31), channel_id=1, source_target_pairs={{0,8},{4,12},{8,0},{12,4},{1,9},{5,13},{9,1},{13,5},{2,10},{6,14},... | collective-permute-start | bytes 442376 | tf_op jit(solution)/shard_map/ppermute | solution.py:27
  7.1 7.2 %collective-permute-start.1 = (bf16[96,768]{1,0:T(8,128)(2,1)}, bf16[96,768]{1,0:T(8,128)(2,1)S(1)}, u32[]{:S(2)}, u32[]{:S(2)}) collective-permute-start(bf16[96,768]{1,0:T(8,128)(2,1)} %get-tuple-element.32), channel_id=1, source_target_pairs={{0,12},{4,8},{8,4},{12,0},{1,13},{5,9},{9,5},{13,1},{2,14},{6,10},... | collective-permute-start | bytes 442376 | tf_op jit(solution)/shard_map/ppermute | solution.py:27
  7.2 34.3 %copy-start.11 = (bf16[96,768]{1,0:T(8,128)(2,1)}, bf16[96,768]{1,0:T(8,128)(2,1)S(1)}, u32[]{:S(2)}) copy-start(bf16[96,768]{1,0:T(8,128)(2,1)S(1)} %collective-permute-done.3.refs_19_.refs_20_) | copy-start | bytes 442372
  7.2 8.3 %collective-permute-start.4 = (bf16[96,768]{1,0:T(8,128)(2,1)S(1)}, bf16[96,768]{1,0:T(8,128)(2,1)S(1)}, u32[]{:S(2)}, u32[]{:S(2)}) collective-permute-start(bf16[96,768]{1,0:T(8,128)(2,1)S(1)} %collective-permute-done.3.refs_19_.refs_20_), channel_id=1, source_target_pairs={{0,1},{1,2},{2,3},{3,0},{4,5},{5,6},{6,7},{7,4},{8,9},{9,10},{10,1... | collective-permute-start | bytes 442376 | tf_op jit(solution)/shard_map/ppermute | solution.py:32
  12.5 28.3 %copy-start = (bf16[96,768]{1,0:T(8,128)(2,1)}, bf16[96,768]{1,0:T(8,128)(2,1)S(1)}, u32[]{:S(2)}) copy-start(bf16[96,768]{1,0:T(8,128)(2,1)S(1)} %collective-permute-done.refs_0_.refs_23_.refs_24_) | copy-start | bytes 442372
  14.3 26.6 %copy-start.3 = (bf16[96,768]{1,0:T(8,128)(2,1)}, bf16[96,768]{1,0:T(8,128)(2,1)S(1)}, u32[]{:S(2)}) copy-start(bf16[96,768]{1,0:T(8,128)(2,1)S(1)} %collective-permute-done.1.refs_1_.refs_27_.refs_28_) | copy-start | bytes 442372
  15.5 1.3 copy-start.34
  16.8 0.9 copy-start.36
  18.4 22.5 %copy-start.6 = (bf16[96,768]{1,0:T(8,128)(2,1)}, bf16[96,768]{1,0:T(8,128)(2,1)S(1)}, u32[]{:S(2)}) copy-start(bf16[96,768]{1,0:T(8,128)(2,1)S(1)} %collective-permute-done.4.refs_3_.refs_20_.refs_21_) | copy-start | bytes 442372
  19.4 21.5 %collective-permute-start.8 = (bf16[272,1536]{1,0:T(8,128)(2,1)S(1)}, bf16[272,1536]{1,0:T(8,128)(2,1)S(1)}, u32[]{:S(2)}, u32[]{:S(2)}) collective-permute-start(bf16[272,1536]{1,0:T(8,128)(2,1)S(1)} %get-tuple-element.36.refs_11_.refs_12_), channel_id=1, source_target_pairs={{0,8},{4,12},{8,0},{12,4},{1,9},{5,13},{9,1},{13,5},{2,10},{6,14},... | collective-permute-start | bytes 2506760 | tf_op jit(solution)/shard_map/ppermute | solution.py:27
  20.9 35.8 %collective-permute-start.5 = (bf16[2,128,1536]{2,1,0:T(8,128)(2,1)}, bf16[2,128,1536]{2,1,0:T(8,128)(2,1)}, u32[]{:S(2)}, u32[]{:S(2)}) collective-permute-start(bf16[2,128,1536]{2,1,0:T(8,128)(2,1)} %get-tuple-element.35.refs_7_.refs_8_), channel_id=1, source_target_pairs={{0,8},{4,12},{8,0},{12,4},{1,9},{5,13},{9,1},{13,5},{2,10},{6,14},... | collective-permute-start | bytes 2359304 | tf_op jit(solution)/shard_map/ppermute | solution.py:27
  21.4 8.6 %collective-permute-start.15 = (bf16[96,768]{1,0:T(8,128)(2,1)S(1)}, bf16[96,768]{1,0:T(8,128)(2,1)S(1)}, u32[]{:S(2)}, u32[]{:S(2)}) collective-permute-start(bf16[96,768]{1,0:T(8,128)(2,1)S(1)} %collective-permute-done.refs_0_.refs_23_.refs_24_), channel_id=1, source_target_pairs={{0,1},{1,2},{2,3},{3,0},{4,5},{5,6},{6,7},{7,4},{8,9},{9,10},{10,1... | collective-permute-start | bytes 442376 | tf_op jit(solution)/shard_map/ppermute | solution.py:32
  21.8 11.4 %collective-permute-start.18 = (bf16[96,768]{1,0:T(8,128)(2,1)S(1)}, bf16[96,768]{1,0:T(8,128)(2,1)S(1)}, u32[]{:S(2)}, u32[]{:S(2)}) collective-permute-start(bf16[96,768]{1,0:T(8,128)(2,1)S(1)} %collective-permute-done.1.refs_1_.refs_27_.refs_28_), channel_id=1, source_target_pairs={{0,1},{1,2},{2,3},{3,0},{4,5},{5,6},{6,7},{7,4},{8,9},{9,10},{10,1... | collective-permute-start | bytes 442376 | tf_op jit(solution)/shard_map/ppermute | solution.py:32
  23.4 13.0 %collective-permute-start.11 = (bf16[96,768]{1,0:T(8,128)(2,1)S(1)}, bf16[96,768]{1,0:T(8,128)(2,1)S(1)}, u32[]{:S(2)}, u32[]{:S(2)}) collective-permute-start(bf16[96,768]{1,0:T(8,128)(2,1)S(1)} %collective-permute-done.2.refs_2_.refs_16_.refs_17_), channel_id=1, source_target_pairs={{0,1},{1,2},{2,3},{3,0},{4,5},{5,6},{6,7},{7,4},{8,9},{9,10},{10,1... | collective-permute-start | bytes 442376 | tf_op jit(solution)/shard_map/ppermute | solution.py:32
  30.0 10.9 %collective-permute-start.13 = (bf16[96,768]{1,0:T(8,128)(2,1)S(1)}, bf16[96,768]{1,0:T(8,128)(2,1)S(1)}, u32[]{:S(2)}, u32[]{:S(2)}) collective-permute-start(bf16[96,768]{1,0:T(8,128)(2,1)S(1)} %collective-permute-done.4.refs_3_.refs_20_.refs_21_), channel_id=1, source_target_pairs={{0,1},{1,2},{2,3},{3,0},{4,5},{5,6},{6,7},{7,4},{8,9},{9,10},{10,1... | collective-permute-start | bytes 442376 | tf_op jit(solution)/shard_map/ppermute | solution.py:32
  33.1 23.5 %collective-permute-start.16 = (bf16[96,768]{1,0:T(8,128)(2,1)S(1)}, bf16[96,768]{1,0:T(8,128)(2,1)S(1)}, u32[]{:S(2)}, u32[]{:S(2)}) collective-permute-start(bf16[96,768]{1,0:T(8,128)(2,1)S(1)} %collective-permute-done.15.refs_24_.refs_25_), channel_id=1, source_target_pairs={{0,1},{1,2},{2,3},{3,0},{4,5},{5,6},{6,7},{7,4},{8,9},{9,10},{10,1... | collective-permute-start | bytes 442376 | tf_op jit(solution)/shard_map/ppermute | solution.py:32
  36.3 59.0 %collective-permute-start.9 = (bf16[272,1536]{1,0:T(8,128)(2,1)S(1)}, bf16[272,1536]{1,0:T(8,128)(2,1)S(1)}, u32[]{:S(2)}, u32[]{:S(2)}) collective-permute-start(bf16[272,1536]{1,0:T(8,128)(2,1)S(1)} %get-tuple-element.36.refs_11_.refs_12_), channel_id=1, source_target_pairs={{0,4},{4,0},{8,12},{12,8},{1,5},{5,1},{9,13},{13,9},{2,6},{6,2},{1... | collective-permute-start | bytes 2506760 | tf_op jit(solution)/shard_map/ppermute | solution.py:27
  40.9 54.4 %collective-permute-start.10 = (bf16[272,1536]{1,0:T(8,128)(2,1)S(1)}, bf16[272,1536]{1,0:T(8,128)(2,1)S(1)}, u32[]{:S(2)}, u32[]{:S(2)}) collective-permute-start(bf16[272,1536]{1,0:T(8,128)(2,1)S(1)} %collective-permute-done.8.refs_12_.refs_13_), channel_id=1, source_target_pairs={{0,4},{4,0},{8,12},{12,8},{1,5},{5,1},{9,13},{13,9},{2,6},{6,2},{1... | collective-permute-start | bytes 2506760 | tf_op jit(solution)/shard_map/ppermute | solution.py:27
  40.9 54.4 %collective-permute-start.6 = (bf16[2,128,1536]{2,1,0:T(8,128)(2,1)}, bf16[2,128,1536]{2,1,0:T(8,128)(2,1)}, u32[]{:S(2)}, u32[]{:S(2)}) collective-permute-start(bf16[2,128,1536]{2,1,0:T(8,128)(2,1)} %get-tuple-element.35.refs_7_.refs_8_), channel_id=1, source_target_pairs={{0,4},{4,0},{8,12},{12,8},{1,5},{5,1},{9,13},{13,9},{2,6},{6,2},{1... | collective-permute-start | bytes 2359304 | tf_op jit(solution)/shard_map/ppermute | solution.py:27
  56.7 38.6 %collective-permute-start.7 = (bf16[2,128,1536]{2,1,0:T(8,128)(2,1)}, bf16[2,128,1536]{2,1,0:T(8,128)(2,1)}, u32[]{:S(2)}, u32[]{:S(2)}) collective-permute-start(bf16[2,128,1536]{2,1,0:T(8,128)(2,1)} %collective-permute-done.5.refs_8_.refs_9_), channel_id=1, source_target_pairs={{0,4},{4,0},{8,12},{12,8},{1,5},{5,1},{9,13},{13,9},{2,6},{6,2},{1... | collective-permute-start | bytes 2359304 | tf_op jit(solution)/shard_map/ppermute | solution.py:27
  56.7 8.2 %collective-permute-start.19 = (bf16[96,768]{1,0:T(8,128)(2,1)S(1)}, bf16[96,768]{1,0:T(8,128)(2,1)}, u32[]{:S(2)}, u32[]{:S(2)}) collective-permute-start(bf16[96,768]{1,0:T(8,128)(2,1)S(1)} %collective-permute-done.18.refs_28_.refs_29_), channel_id=1, source_target_pairs={{0,1},{1,2},{2,3},{3,0},{4,5},{5,6},{6,7},{7,4},{8,9},{9,10},{10,1... | collective-permute-start | bytes 442376 | tf_op jit(solution)/shard_map/ppermute | solution.py:32
  64.9 7.3 %collective-permute-start.12 = (bf16[96,768]{1,0:T(8,128)(2,1)S(1)}, bf16[96,768]{1,0:T(8,128)(2,1)S(1)}, u32[]{:S(2)}, u32[]{:S(2)}) collective-permute-start(bf16[96,768]{1,0:T(8,128)(2,1)S(1)} %collective-permute-done.11.refs_17_.refs_18_), channel_id=1, source_target_pairs={{0,1},{1,2},{2,3},{3,0},{4,5},{5,6},{6,7},{7,4},{8,9},{9,10},{10,1... | collective-permute-start | bytes 442376 | tf_op jit(solution)/shard_map/ppermute | solution.py:32
  72.8 6.9 %collective-permute-start.14 = (bf16[96,768]{1,0:T(8,128)(2,1)S(1)}, bf16[96,768]{1,0:T(8,128)(2,1)S(1)}, u32[]{:S(2)}, u32[]{:S(2)}) collective-permute-start(bf16[96,768]{1,0:T(8,128)(2,1)S(1)} %collective-permute-done.13.refs_21_.refs_22_), channel_id=1, source_target_pairs={{0,1},{1,2},{2,3},{3,0},{4,5},{5,6},{6,7},{7,4},{8,9},{9,10},{10,1... | collective-permute-start | bytes 442376 | tf_op jit(solution)/shard_map/ppermute | solution.py:32
  80.4 6.9 %collective-permute-start.17 = (bf16[96,768]{1,0:T(8,128)(2,1)S(1)}, bf16[96,768]{1,0:T(8,128)(2,1)S(1)}, u32[]{:S(2)}, u32[]{:S(2)}) collective-permute-start(bf16[96,768]{1,0:T(8,128)(2,1)S(1)} %collective-permute-done.16.refs_25_.refs_26_), channel_id=1, source_target_pairs={{0,1},{1,2},{2,3},{3,0},{4,5},{5,6},{6,7},{7,4},{8,9},{9,10},{10,1... | collective-permute-start | bytes 442376 | tf_op jit(solution)/shard_map/ppermute | solution.py:32
  88.0 7.3 %collective-permute-start.20 = (bf16[96,768]{1,0:T(8,128)(2,1)}, bf16[96,768]{1,0:T(8,128)(2,1)}, u32[]{:S(2)}, u32[]{:S(2)}) collective-permute-start(bf16[96,768]{1,0:T(8,128)(2,1)} %collective-permute-done.19.refs_29_.refs_30_), channel_id=1, source_target_pairs={{0,1},{1,2},{2,3},{3,0},{4,5},{5,6},{6,7},{7,4},{8,9},{9,10},{10,1... | collective-permute-start | bytes 442376 | tf_op jit(solution)/shard_map/ppermute | solution.py:32
  119.8 17.6 %collective-permute-start.21 = (bf16[2,128,384]{2,1,0:T(8,128)(2,1)S(1)}, bf16[2,128,384]{2,1,0:T(8,128)(2,1)S(1)}, u32[]{:S(2)}, u32[]{:S(2)}) collective-permute-start(bf16[2,128,384]{2,1,0:T(8,128)(2,1)S(1)} %get-tuple-element.37.refs_0_), channel_id=1, source_target_pairs={{0,16},{1,17},{2,18},{3,19},{4,20},{5,21},{6,22},{7,23},{8,24},{9,... | collective-permute-start | bytes 589832 | tf_op jit(solution)/shard_map/ppermute | solution.py:17
  123.3 15.7 %collective-permute-start.25 = (bf16[2,128,384]{2,1,0:T(8,128)(2,1)S(1)}, bf16[2,128,384]{2,1,0:T(8,128)(2,1)S(1)}, u32[]{:S(2)}, u32[]{:S(2)}) collective-permute-start(bf16[2,128,384]{2,1,0:T(8,128)(2,1)S(1)} %get-tuple-element.38.refs_1_), channel_id=1, source_target_pairs={{0,16},{1,17},{2,18},{3,19},{4,20},{5,21},{6,22},{7,23},{8,24},{9,... | collective-permute-start | bytes 589832 | tf_op jit(solution)/shard_map/ppermute | solution.py:17
  134.8 4.7 %collective-permute-start.32 = (bf16[2,128,384]{2,1,0:T(8,128)(2,1)S(1)}, bf16[2,128,384]{2,1,0:T(8,128)(2,1)S(1)}, u32[]{:S(2)}, u32[]{:S(2)}) collective-permute-start(bf16[2,128,384]{2,1,0:T(8,128)(2,1)S(1)} %get-tuple-element.40.refs_2_), channel_id=1, source_target_pairs={{0,16},{1,17},{2,18},{3,19},{4,20},{5,21},{6,22},{7,23},{8,24},{9,... | collective-permute-start | bytes 589832 | tf_op jit(solution)/shard_map/ppermute | solution.py:17
  136.1 5.3 %collective-permute-start.36 = (bf16[2,128,384]{2,1,0:T(8,128)(2,1)S(1)}, bf16[2,128,384]{2,1,0:T(8,128)(2,1)S(1)}, u32[]{:S(2)}, u32[]{:S(2)}) collective-permute-start(bf16[2,128,384]{2,1,0:T(8,128)(2,1)S(1)} %get-tuple-element.41.refs_3_), channel_id=1, source_target_pairs={{0,16},{1,17},{2,18},{3,19},{4,20},{5,21},{6,22},{7,23},{8,24},{9,... | collective-permute-start | bytes 589832 | tf_op jit(solution)/shard_map/ppermute | solution.py:17
  137.4 6.1 %collective-permute-start.22 = (bf16[2,128,384]{2,1,0:T(8,128)(2,1)S(1)}, bf16[2,128,384]{2,1,0:T(8,128)(2,1)S(1)}, u32[]{:S(2)}, u32[]{:S(2)}) collective-permute-start(bf16[2,128,384]{2,1,0:T(8,128)(2,1)S(1)} %collective-permute-done.21.refs_32_), channel_id=1, source_target_pairs={{0,8},{4,12},{8,0},{12,4},{1,9},{5,13},{9,1},{13,5},{2,10},{6,14},... | collective-permute-start | bytes 589832 | tf_op jit(solution)/shard_map/ppermute | solution.py:27
  139.0 8.8 %collective-permute-start.26 = (bf16[2,128,384]{2,1,0:T(8,128)(2,1)S(1)}, bf16[2,128,384]{2,1,0:T(8,128)(2,1)S(1)}, u32[]{:S(2)}, u32[]{:S(2)}) collective-permute-start(bf16[2,128,384]{2,1,0:T(8,128)(2,1)S(1)} %collective-permute-done.25.refs_36_), channel_id=1, source_target_pairs={{0,8},{4,12},{8,0},{12,4},{1,9},{5,13},{9,1},{13,5},{2,10},{6,14},... | collective-permute-start | bytes 589832 | tf_op jit(solution)/shard_map/ppermute | solution.py:27
  139.5 8.2 %collective-permute-start.23 = (bf16[2,128,384]{2,1,0:T(8,128)(2,1)S(1)}, bf16[2,128,384]{2,1,0:T(8,128)(2,1)S(1)}, u32[]{:S(2)}, u32[]{:S(2)}) collective-permute-start(bf16[2,128,384]{2,1,0:T(8,128)(2,1)S(1)} %collective-permute-done.21.refs_32_), channel_id=1, source_target_pairs={{0,4},{4,0},{8,12},{12,8},{1,5},{5,1},{9,13},{13,9},{2,6},{6,2},{1... | collective-permute-start | bytes 589832 | tf_op jit(solution)/shard_map/ppermute | solution.py:27
  139.5 8.8 %collective-permute-start.27 = (bf16[2,128,384]{2,1,0:T(8,128)(2,1)S(1)}, bf16[2,128,384]{2,1,0:T(8,128)(2,1)S(1)}, u32[]{:S(2)}, u32[]{:S(2)}) collective-permute-start(bf16[2,128,384]{2,1,0:T(8,128)(2,1)S(1)} %collective-permute-done.25.refs_36_), channel_id=1, source_target_pairs={{0,4},{4,0},{8,12},{12,8},{1,5},{5,1},{9,13},{13,9},{2,6},{6,2},{1... | collective-permute-start | bytes 589832 | tf_op jit(solution)/shard_map/ppermute | solution.py:27
  141.4 10.2 %collective-permute-start.33 = (bf16[2,128,384]{2,1,0:T(8,128)(2,1)S(1)}, bf16[2,128,384]{2,1,0:T(8,128)(2,1)S(1)}, u32[]{:S(2)}, u32[]{:S(2)}) collective-permute-start(bf16[2,128,384]{2,1,0:T(8,128)(2,1)S(1)} %collective-permute-done.32.refs_32_), channel_id=1, source_target_pairs={{0,8},{4,12},{8,0},{12,4},{1,9},{5,13},{9,1},{13,5},{2,10},{6,14},... | collective-permute-start | bytes 589832 | tf_op jit(solution)/shard_map/ppermute | solution.py:27
  143.5 10.1 %collective-permute-start.37 = (bf16[2,128,384]{2,1,0:T(8,128)(2,1)S(1)}, bf16[2,128,384]{2,1,0:T(8,128)(2,1)S(1)}, u32[]{:S(2)}, u32[]{:S(2)}) collective-permute-start(bf16[2,128,384]{2,1,0:T(8,128)(2,1)S(1)} %collective-permute-done.36.refs_36_), channel_id=1, source_target_pairs={{0,8},{4,12},{8,0},{12,4},{1,9},{5,13},{9,1},{13,5},{2,10},{6,14},... | collective-permute-start | bytes 589832 | tf_op jit(solution)/shard_map/ppermute | solution.py:27
  147.8 5.9 %collective-permute-start.24 = (bf16[2,128,384]{2,1,0:T(8,128)(2,1)S(1)}, bf16[2,128,384]{2,1,0:T(8,128)(2,1)S(1)}, u32[]{:S(2)}, u32[]{:S(2)}) collective-permute-start(bf16[2,128,384]{2,1,0:T(8,128)(2,1)S(1)} %collective-permute-done.22.refs_33_), channel_id=1, source_target_pairs={{0,4},{4,0},{8,12},{12,8},{1,5},{5,1},{9,13},{13,9},{2,6},{6,2},{1... | collective-permute-start | bytes 589832 | tf_op jit(solution)/shard_map/ppermute | solution.py:27
  147.8 6.4 %collective-permute-start.28 = (bf16[2,128,384]{2,1,0:T(8,128)(2,1)S(1)}, bf16[2,128,384]{2,1,0:T(8,128)(2,1)S(1)}, u32[]{:S(2)}, u32[]{:S(2)}) collective-permute-start(bf16[2,128,384]{2,1,0:T(8,128)(2,1)S(1)} %collective-permute-done.26.refs_37_), channel_id=1, source_target_pairs={{0,4},{4,0},{8,12},{12,8},{1,5},{5,1},{9,13},{13,9},{2,6},{6,2},{1... | collective-permute-start | bytes 589832 | tf_op jit(solution)/shard_map/ppermute | solution.py:27
  148.3 17.8 %collective-permute-start.34 = (bf16[2,128,384]{2,1,0:T(8,128)(2,1)S(1)}, bf16[2,128,384]{2,1,0:T(8,128)(2,1)S(1)}, u32[]{:S(2)}, u32[]{:S(2)}) collective-permute-start(bf16[2,128,384]{2,1,0:T(8,128)(2,1)S(1)} %collective-permute-done.32.refs_32_), channel_id=1, source_target_pairs={{0,4},{4,0},{8,12},{12,8},{1,5},{5,1},{9,13},{13,9},{2,6},{6,2},{1... | collective-permute-start | bytes 589832 | tf_op jit(solution)/shard_map/ppermute | solution.py:27
  151.6 14.5 %collective-permute-start.38 = (bf16[2,128,384]{2,1,0:T(8,128)(2,1)S(1)}, bf16[2,128,384]{2,1,0:T(8,128)(2,1)S(1)}, u32[]{:S(2)}, u32[]{:S(2)}) collective-permute-start(bf16[2,128,384]{2,1,0:T(8,128)(2,1)S(1)} %collective-permute-done.36.refs_36_), channel_id=1, source_target_pairs={{0,4},{4,0},{8,12},{12,8},{1,5},{5,1},{9,13},{13,9},{2,6},{6,2},{1... | collective-permute-start | bytes 589832 | tf_op jit(solution)/shard_map/ppermute | solution.py:27
  153.7 12.5 %collective-permute-start.35 = (bf16[2,128,384]{2,1,0:T(8,128)(2,1)S(1)}, bf16[2,128,384]{2,1,0:T(8,128)(2,1)S(1)}, u32[]{:S(2)}, u32[]{:S(2)}) collective-permute-start(bf16[2,128,384]{2,1,0:T(8,128)(2,1)S(1)} %collective-permute-done.33.refs_33_), channel_id=1, source_target_pairs={{0,4},{4,0},{8,12},{12,8},{1,5},{5,1},{9,13},{13,9},{2,6},{6,2},{1... | collective-permute-start | bytes 589832 | tf_op jit(solution)/shard_map/ppermute | solution.py:27
  153.7 12.5 %collective-permute-start.39 = (bf16[2,128,384]{2,1,0:T(8,128)(2,1)S(1)}, bf16[2,128,384]{2,1,0:T(8,128)(2,1)S(1)}, u32[]{:S(2)}, u32[]{:S(2)}) collective-permute-start(bf16[2,128,384]{2,1,0:T(8,128)(2,1)S(1)} %collective-permute-done.37.refs_37_), channel_id=1, source_target_pairs={{0,4},{4,0},{8,12},{12,8},{1,5},{5,1},{9,13},{13,9},{2,6},{6,2},{1... | collective-permute-start | bytes 589832 | tf_op jit(solution)/shard_map/ppermute | solution.py:27
  154.2 12.0 %copy-start.29 = (bf16[96,768]{1,0:T(8,128)(2,1)S(1)}, bf16[96,768]{1,0:T(8,128)(2,1)}, u32[]{:S(2)}) copy-start(bf16[96,768]{1,0:T(8,128)(2,1)} %copy-done.27) | copy-start | bytes 442372
  164.9 1.3 copy-start.2
  164.9 1.3 copy-start.5
  164.9 1.3 copy-start.8
  164.9 1.3 copy-start.10
  164.9 1.3 copy-start.13
  164.9 1.3 copy-start.16
  164.9 1.3 copy-start.19
  165.0 1.3 copy-start.22
  177.9 6.2 %collective-permute-start.43 = (bf16[96,256]{1,0:T(8,128)(2,1)S(1)}, bf16[96,256]{1,0:T(8,128)(2,1)S(1)}, u32[]{:S(2)}, u32[]{:S(2)}) collective-permute-start(bf16[96,256]{1,0:T(8,128)(2,1)S(1)} %get-tuple-element.55), channel_id=1, source_target_pairs={{0,1},{1,2},{2,3},{3,0},{4,5},{5,6},{6,7},{7,4},{8,9},{9,10},{10,1... | collective-permute-start | bytes 147464 | tf_op jit(solution)/shard_map/ppermute | solution.py:32
  177.9 7.1 %collective-permute-start.44 = (bf16[96,256]{1,0:T(8,128)(2,1)S(1)}, bf16[96,256]{1,0:T(8,128)(2,1)S(1)}, u32[]{:S(2)}, u32[]{:S(2)}) collective-permute-start(bf16[96,256]{1,0:T(8,128)(2,1)S(1)} %get-tuple-element.56), channel_id=1, source_target_pairs={{0,2},{1,3},{2,0},{3,1},{4,6},{5,7},{6,4},{7,5},{8,10},{9,11},{10,... | collective-permute-start | bytes 147464 | tf_op jit(solution)/shard_map/ppermute | solution.py:32
  178.0 12.6 %collective-permute-start.40 = (bf16[128,384]{1,0:T(8,128)(2,1)S(1)}, bf16[128,384]{1,0:T(8,128)(2,1)S(1)}, u32[]{:S(2)}, u32[]{:S(2)}) collective-permute-start(bf16[128,384]{1,0:T(8,128)(2,1)S(1)} %get-tuple-element.51), channel_id=1, source_target_pairs={{0,4},{4,0},{8,12},{12,8},{1,5},{5,1},{9,13},{13,9},{2,6},{6,2},{1... | collective-permute-start | bytes 294920 | tf_op jit(solution)/shard_map/ppermute | solution.py:27
  178.2 17.5 %collective-permute-start.29 = (bf16[2,128,384]{2,1,0:T(8,128)(2,1)S(1)}, bf16[2,128,384]{2,1,0:T(8,128)(2,1)S(1)}, u32[]{:S(2)}, u32[]{:S(2)}) collective-permute-start(bf16[2,128,384]{2,1,0:T(8,128)(2,1)S(1)} %get-tuple-element.46.refs_43_), channel_id=1, source_target_pairs={{0,4},{4,0},{8,12},{12,8},{1,5},{5,1},{9,13},{13,9},{2,6},{6,2},{1... | collective-permute-start | bytes 589832 | tf_op jit(solution)/shard_map/ppermute | solution.py:27
  178.6 17.1 %collective-permute-start.30 = (bf16[2,128,384]{2,1,0:T(8,128)(2,1)S(1)}, bf16[2,128,384]{2,1,0:T(8,128)(2,1)S(1)}, u32[]{:S(2)}, u32[]{:S(2)}) collective-permute-start(bf16[2,128,384]{2,1,0:T(8,128)(2,1)S(1)} %get-tuple-element.47.refs_44_), channel_id=1, source_target_pairs={{0,8},{4,12},{8,0},{12,4},{1,9},{5,13},{9,1},{13,5},{2,10},{6,14},... | collective-permute-start | bytes 589832 | tf_op jit(solution)/shard_map/ppermute | solution.py:27
  184.1 11.6 %collective-permute-start.31 = (bf16[2,128,384]{2,1,0:T(8,128)(2,1)S(1)}, bf16[2,128,384]{2,1,0:T(8,128)(2,1)S(1)}, u32[]{:S(2)}, u32[]{:S(2)}) collective-permute-start(bf16[2,128,384]{2,1,0:T(8,128)(2,1)S(1)} %get-tuple-element.48.refs_45_), channel_id=1, source_target_pairs={{0,12},{4,8},{8,4},{12,0},{1,13},{5,9},{9,5},{13,1},{2,14},{6,10},... | collective-permute-start | bytes 589832 | tf_op jit(solution)/shard_map/ppermute | solution.py:27
  185.0 4.3 %collective-permute-start.45 = (bf16[96,256]{1,0:T(8,128)(2,1)S(1)}, bf16[96,256]{1,0:T(8,128)(2,1)S(1)}, u32[]{:S(2)}, u32[]{:S(2)}) collective-permute-start(bf16[96,256]{1,0:T(8,128)(2,1)S(1)} %get-tuple-element.57), channel_id=1, source_target_pairs={{0,3},{1,0},{2,1},{3,2},{4,7},{5,4},{6,5},{7,6},{8,11},{9,8},{10,9... | collective-permute-start | bytes 147464 | tf_op jit(solution)/shard_map/ppermute | solution.py:32
  189.4 5.0 %collective-permute-start.41 = (bf16[128,384]{1,0:T(8,128)(2,1)S(1)}, bf16[128,384]{1,0:T(8,128)(2,1)S(1)}, u32[]{:S(2)}, u32[]{:S(2)}) collective-permute-start(bf16[128,384]{1,0:T(8,128)(2,1)S(1)} %get-tuple-element.52), channel_id=1, source_target_pairs={{0,8},{4,12},{8,0},{12,4},{1,9},{5,13},{9,1},{13,5},{2,10},{6,14},... | collective-permute-start | bytes 294920 | tf_op jit(solution)/shard_map/ppermute | solution.py:27
  190.7 5.1 %collective-permute-start.42 = (bf16[128,384]{1,0:T(8,128)(2,1)S(1)}, bf16[128,384]{1,0:T(8,128)(2,1)S(1)}, u32[]{:S(2)}, u32[]{:S(2)}) collective-permute-start(bf16[128,384]{1,0:T(8,128)(2,1)S(1)} %get-tuple-element.53), channel_id=1, source_target_pairs={{0,12},{4,8},{8,4},{12,0},{1,13},{5,9},{9,5},{13,1},{2,14},{6,10},... | collective-permute-start | bytes 294920 | tf_op jit(solution)/shard_map/ppermute | solution.py:27
  (26 other events, 20.5 us)

commit v4 on v1

--- a/solution.py
+++ b/solution.py
@@ -1,6 +1,11 @@
+import functools
+import math
+
 import jax
 import jax.numpy as jnp
 from jax import lax
+from jax.experimental import pallas as pl
+from jax.experimental.pallas import tpu as pltpu
 from jax.sharding import PartitionSpec as P
 
 epsilon = 1e-06
@@ -17,7 +22,533 @@
     return lax.ppermute(value, axis, [(source, (source + 1) % count) for source in range(count)])
 
 
-def body(
+def swap(value, bit):
+    count = lax.axis_size("seq")
+    return lax.ppermute(value, "seq", [(source, source ^ bit) for source in range(count)])
+
+
+def shifted(value, axis, shift):
+    count = lax.axis_size(axis)
+    return lax.ppermute(value, axis, [(source, (source + shift) % count) for source in range(count)])
+
+
+def offsets_of(count):
+    offsets = [0]
+    bit = count // 2
+    while bit:
+        offsets = offsets + [offset ^ bit for offset in offsets]
+        bit //= 2
+    return offsets
+
+
+def turn_and_batch(step, turns):
+    section = lax.axis_index("pipe")
+    turn = jnp.clip(step - section, 0, turns - 1)
+    return turn, turn - section + 1
+
+
+def pack_kernel(wq, wkv, own, *outs):
+    cols = outs[0].shape[1] // 2
+    seq = lax.axis_index("seq")
+    targets = (own.at[0],) + outs
+    for m, out in enumerate(targets):
+        start = pl.multiple_of((seq ^ m) * cols, 128)
+        out[:, :cols] = wq[0, :, pl.ds(start, cols)]
+        out[:, cols:] = wkv[0, :, pl.ds(start, cols)]
+
+
+def pair_kernel(own, other, out):
+    out[0] = own[0]
+    out[1] = other[...]
+
+
+def stack_kernel(dep, a, b, out):
+    out[0] = a[...]
+    out[1] = b[...]
+
+
+def first_kernel(turns, dep, incoming, contacts, out, states):
+    rows = incoming.shape[3]
+    for turn in range(2):
+        out[turn * rows : (turn + 1) * rows] = incoming[0, turn, 0]
+    states[...] = jnp.zeros_like(states)
+    for step in range(turns + 1):
+        _, batch = turn_and_batch(step, turns)
+        states[step : step + 1] = contacts[batch].astype(jnp.float32)
+    out[2 * rows :, : states.shape[1]] = states[...].astype(jnp.bfloat16)
+
+
+def second_kernel(dep, incoming, cotangent, out):
+    turns, rows, feats = cotangent.shape[1], cotangent.shape[3], cotangent.shape[4]
+    out[:rows] = incoming[0, 2, 0]
+    for turn in range(turns):
+        out[rows:, turn * feats : (turn + 1) * feats] = cotangent[0, turn, 0]
+
+
+def step_kernel(cfg, *refs):
+    step, has_relay, first_step = cfg["step"], cfg["has_relay"], cfg["first_step"]
+    pieces, hops, head, turns = cfg["pieces"], cfg["hops"], cfg["head"], cfg["turns"]
+    heads, group, halves = cfg["heads"], cfg["group"], cfg["halves"]
+    refs = list(refs)
+
+    def take(count):
+        taken, refs[:count] = refs[:count], []
+        return taken
+
+    bias, times, table, gain, freq, gate, flags = take(7)
+    first = take(pieces)
+    second = take(pieces) if step >= 2 else None
+    chunks = take(2 * hops) if first_step else None
+    weights = None if first_step else take(1)[0]
+    relay = take(pieces * halves) if has_relay else None
+    outs = take(halves)
+    if first_step:
+        weights = take(1)[0]
+    scaled, mod, square, own_hidden, proj, att, sem_w = take(7)
+    offsets = offsets_of(pieces)
+    frames, width = scaled.shape
+    rows, cols = frames // pieces, att.shape[1]
+    part = pieces // halves
+    seq, rep, section = lax.axis_index("seq"), lax.axis_index("dp"), lax.axis_index("pipe")
+    turn, batch = turn_and_batch(step, turns)
+
+    w_copies = []
+    if first_step:
+        w_rows = chunks[0].shape[1]
+        for ring in range(2):
+            for hop in range(hops):
+                for j in range(2):
+                    block = (seq ^ (2 * ring + j)) * hops + lax.rem(rep + hops - hop, hops)
+                    w_copies.append(
+                        pltpu.make_async_copy(
+                            chunks[ring * hops + hop].at[j],
+                            weights.at[pl.ds(pl.multiple_of(block * w_rows, 16), w_rows)],
+                            sem_w.at[len(w_copies)],
+                        )
+                    )
+        for copy in w_copies:
+            copy.start()
+
+    labels = lax.broadcasted_iota(jnp.int32, (32, rows), 0)
+    columns = []
+    for i in range(pieces):
+        state = first[i][2 * rows : 2 * rows + 16, :rows][step : step + 1]
+        state = state.astype(jnp.float32).astype(jnp.int32)
+        flag = flags[batch, :, pl.ds(pl.multiple_of((seq ^ offsets[i]) * rows, 128), rows)]
+        one = jnp.where(labels == state, 1.0, 0.0)
+        columns.append(jnp.where(labels == 16, flag.astype(jnp.float32), one).T)
+    columns = jnp.concatenate(columns, axis=0)
+    onehot = columns[:, : table.shape[1]].astype(jnp.bfloat16)
+    flag_column = columns[:, 16:17]
+
+    time = times[batch, 0].astype(jnp.float32)
+    mod[...] = gain[...] * (1.0 + 0.5 * jnp.sin(time * freq[...]))
+
+    def normalize(relayed):
+        total = jnp.zeros((frames, 128), jnp.float32)
+        for i in range(pieces):
+            lanes = pl.ds(pl.multiple_of((seq ^ offsets[i]) * cols, 128), cols)
+            blocks = []
+            for p in range(pieces):
+                if relayed:
+                    j = offsets.index(offsets[i] ^ offsets[p])
+                    blocks.append(relay[(j // part) * pieces + i][j % part])
+                elif step < 2:
+                    at = pl.multiple_of(jnp.minimum(turn, 1) * rows, 128)
+                    blocks.append(first[p][pl.ds(at, rows), lanes])
+                else:
+                    blocks.append(second[p][:rows, lanes])
+            hidden = jnp.concatenate(blocks, axis=0).astype(jnp.float32) + jnp.dot(
+                onehot, table[0, :, lanes], preferred_element_type=jnp.float32
+            )
+            for lane in range(0, cols, 128):
+                piece = hidden[:, lane : lane + 128]
+                total = total + piece * piece
+            scaled[:, lanes] = (hidden * mod[:, lanes]).astype(jnp.bfloat16)
+            if i == 0:
+                own_hidden[...] = hidden
+        square[...] = total
+
+    if has_relay:
+
+        @pl.when(section == 0)
+        def _():
+            normalize(False)
+
+        @pl.when(section != 0)
+        def _():
+            normalize(True)
+    else:
+        normalize(False)
+    mean = jnp.sum(square[...], axis=1, keepdims=True) * (1.0 / width)
+    scale = lax.rsqrt(mean + epsilon)
+    for copy in w_copies:
+        copy.wait()
+    projected = jnp.dot(scaled[...], weights[...], preferred_element_type=jnp.float32) * scale
+    score_scale = head ** (-0.5) * math.log2(math.e)
+    proj[:, :cols] = (projected[:, :cols] * score_scale).astype(jnp.bfloat16)
+    proj[:, cols : 2 * cols] = projected[:, cols:].astype(jnp.bfloat16)
+    proj[:, 2 * cols :] = jnp.zeros((frames, 128), jnp.bfloat16)
+    lanes = lax.broadcasted_iota(jnp.int32, (frames, 128), 1)
+    row_lanes = lax.broadcasted_iota(jnp.int32, (1, 128), 1)
+    flag_lanes = jnp.logical_or(lanes == head, lanes == head + 1)
+
+    def part_of(at):
+        return proj[:, at : at + 128].astype(jnp.float32)
+
+    keys, values = [], []
+    for kv in range(heads // group):
+        base = cols + kv * 2 * head
+        key = jnp.where(flag_lanes, flag_column, jnp.where(lanes < head, part_of(base), 0.0))
+        value = jnp.where(lanes < head, part_of(base + head), jnp.where(lanes == head, 1.0, 0.0))
+        keys.append(key.astype(jnp.bfloat16))
+        values.append(value.astype(jnp.bfloat16))
+
+    def scores_of(h):
+        strength = jnp.zeros((1, 128), jnp.float32) + bias[0, seq * heads + h] * math.log2(math.e)
+        coarse = strength.astype(jnp.bfloat16).astype(jnp.float32)
+        tail = jnp.where(
+            row_lanes == head, coarse, jnp.where(row_lanes == head + 1, strength - coarse, 0.0)
+        )
+        query = jnp.where(lanes < head, part_of(h * head), tail).astype(jnp.bfloat16)
+        return lax.dot_general(
+            query, keys[h // group], (((1,), (1,)), ((), ())), preferred_element_type=jnp.float32
+        )
+
+    scores = scores_of(0)
+    for h in range(heads):
+        ahead = scores_of(h + 1) if h + 1 < heads else None
+        top = jnp.max(scores, axis=1, keepdims=True)
+        weight = jnp.exp2(scores - top).astype(jnp.bfloat16)
+        mixed = jnp.dot(weight, values[h // group], preferred_element_type=jnp.float32)
+        att[:, h * head : (h + 1) * head] = mixed[:, :head] * (1.0 / mixed[:, head : head + 1])
+        scores = ahead
+    own = pl.ds(pl.multiple_of(seq * cols, 128), cols)
+    attended = att[...].astype(jnp.bfloat16).astype(jnp.float32)
+    output = (own_hidden[...] + gate[:, own] * attended).astype(jnp.bfloat16)
+    blocks = output.reshape(pieces, rows, cols)
+    for k in range(halves):
+        outs[k][...] = blocks[k * part : (k + 1) * part]
+
+
+def tie_kernel(count, *refs):
+    pass
+
+
+def grad_of(output, second, turn, rows, feats):
+    cot = jnp.concatenate(
+        [piece[rows : 2 * rows, turn * feats : (turn + 1) * feats] for piece in second], axis=0
+    )
+    return lax.dot_general(
+        output, cot, (((0,), (0,)), ((), ())), preferred_element_type=jnp.float32
+    )
+
+
+def early_kernel(turns, pieces, halves, feats, *refs):
+    outs, second = refs[: turns * halves], refs[turns * halves : turns * halves + pieces]
+    sends, grad = refs[turns * halves + pieces : -1], refs[-1]
+    section = lax.axis_index("pipe")
+    offsets = offsets_of(pieces)
+    part = pieces // halves
+    rows = outs[0].shape[1]
+    total = None
+    for turn in range(turns - 1):
+        blocks = []
+        for p in range(pieces):
+            k, j = p // part, p % part
+            block = jnp.where(
+                section == 0, outs[turn * halves + k][j], outs[(turn + 1) * halves + k][j]
+            )
+            sends[offsets[p]][turn] = block
+            blocks.append(block)
+        share = grad_of(jnp.concatenate(blocks, axis=0), second, turn, rows, feats)
+        total = share if total is None else total + share
+    grad[...] = total
+
+
+def settle_kernel(turns, pieces, halves, hops, feats, *refs):
+    refs = list(refs)
+
+    def take(count):
+        taken, refs[:count] = refs[:count], []
+        return taken
+
+    before, now, second, early = take(halves), take(halves), take(pieces), take(pieces)
+    early_grad = take(1)[0]
+    late, own_grad, grads = take(pieces), take(1)[0], take(hops - 1)
+    section_out = take(1)[0]
+    rows_out, total, sem = take(3)
+    section, seq, rep = lax.axis_index("pipe"), lax.axis_index("seq"), lax.axis_index("dp")
+    offsets = offsets_of(pieces)
+    part = pieces // halves
+    rows, cols = early[0].shape[1:]
+    for m in range(pieces):
+        lanes = pl.ds(pl.multiple_of((seq ^ m) * cols, 128), cols)
+        for turn in range(turns - 1):
+            rows_out[turn, :, lanes] = early[m][turn]
+    copy = pltpu.make_async_copy(rows_out, section_out.at[pl.ds(0, turns - 1)], sem)
+    copy.start()
+    blocks = []
+    for p in range(pieces):
+        block = jnp.where(section == 0, before[p // part][p % part], now[p // part][p % part])
+        late[offsets[p]][...] = block
+        blocks.append(block)
+    share = grad_of(jnp.concatenate(blocks, axis=0), second, turns - 1, rows, feats)
+    factor = float(turns * hops * rows * pieces) ** (-0.5)
+    total[...] = (share + early_grad[...]) * factor
+    g_rows = cols // hops
+    own_grad[...] = total[pl.ds(pl.multiple_of(rep * g_rows, 8), g_rows)]
+    for shift in range(1, hops):
+        at = pl.multiple_of(lax.rem(rep + shift, hops) * g_rows, 8)
+        grads[shift - 1][...] = total[pl.ds(at, g_rows)].astype(jnp.bfloat16)
+    copy.wait()
+
+
+def finish_kernel(pieces, hops, *refs):
+    held, late, refs = refs[0], refs[1 : pieces + 1], refs[pieces + 1 :]
+    own_grad, parts, (section_out, grad, row_out, sem) = refs[0], refs[1:hops], refs[hops:]
+    seq = lax.axis_index("seq")
+    cols = late[0].shape[1]
+    for m in range(pieces):
+        lanes = pl.ds(pl.multiple_of((seq ^ m) * cols, 128), cols)
+        row_out[:, lanes] = late[m][...]
+    copy = pltpu.make_async_copy(row_out, section_out.at[section_out.shape[0] - 1], sem)
+    copy.start()
+    total = own_grad[...]
+    for part in parts:
+        total = total + part[...].astype(jnp.float32)
+    grad[...] = total
+    copy.wait()
+
+
+HALVES = 2
+MIB = 1024 * 1024
+
+
+def paired_body(
+    incoming,
+    contacts,
+    keyframes,
+    timesteps,
+    w_query,
+    w_keyval,
+    norm_gain,
+    time_freq,
+    contact_table,
+    key_bias,
+    attn_gate,
+    head_cotangent,
+):
+    seq_count = lax.axis_size("seq")
+    hops = lax.axis_size("dp")
+    rows, width, turns = incoming.shape[3], incoming.shape[4], incoming.shape[1]
+    frames = rows * seq_count
+    heads_all = key_bias.shape[1]
+    head = width // heads_all
+    heads = heads_all // seq_count
+    kv_heads = w_keyval.shape[2] // (2 * head * seq_count)
+    feats = head_cotangent.shape[4]
+    cols = width // seq_count
+    w_rows = w_query.shape[1]
+    steps = turns + 1
+    part = seq_count // HALVES
+    kind = jnp.bfloat16
+    smem = pl.BlockSpec(memory_space=pltpu.SMEM)
+    vmem = pl.BlockSpec(memory_space=pltpu.VMEM)
+    anywhere = pl.BlockSpec(memory_space=pl.ANY)
+    shape = jax.ShapeDtypeStruct
+
+    def call(kernel, name, out_shape, in_specs, operands, scratch=(), limit=4, flops=0, **options):
+        return pl.pallas_call(
+            kernel,
+            out_shape=out_shape,
+            in_specs=in_specs,
+            scratch_shapes=list(scratch),
+            compiler_params=pltpu.CompilerParams(vmem_limit_bytes=limit * MIB),
+            cost_estimate=pl.CostEstimate(
+                flops=flops, bytes_accessed=flops // 512, transcendentals=0
+            ),
+            name=name,
+            **options,
+        )(*operands)
+
+    block = shape((w_rows, 2 * cols), kind)
+    pair = shape((2, w_rows, 2 * cols), kind)
+    packed = call(
+        pack_kernel,
+        "pack",
+        [pair] + [block] * (seq_count - 1),
+        [vmem, vmem],
+        [w_query, w_keyval],
+        out_specs=[vmem] * seq_count,
+    )
+    blocks = [swap(packed[m], m) for m in range(1, seq_count)]
+    near = call(
+        pair_kernel, "near", pair, [vmem, vmem], [packed[0], blocks[0]], out_specs=vmem
+    )
+    far = call(
+        stack_kernel, "far", pair, [anywhere, vmem, vmem], [near] + blocks[1:], out_specs=vmem
+    )
+    rings = [[near], [far]]
+    for hop in range(1, hops):
+        for ring in rings:
+            ring.append(shifted(ring[-1], "dp", 1))
+
+    mine = call(
+        functools.partial(first_kernel, turns),
+        "first",
+        shape((2 * rows + 16, width), kind),
+        [anywhere, vmem, vmem],
+        [far, incoming, contacts],
+        [pltpu.VMEM((16, 128), jnp.float32)],
+        out_specs=vmem,
+    )
+    across = swap(mine, 2)
+    first = [mine, across, swap(mine, 1), swap(across, 1)]
+    mine = call(
+        second_kernel,
+        "second",
+        shape((2 * rows, width), kind),
+        [anywhere, vmem, vmem],
+        [across, incoming, head_cotangent],
+        out_specs=vmem,
+    )
+    across = swap(mine, 2)
+    second = [mine, across, swap(mine, 1), swap(across, 1)]
+
+    outputs = []
+    relayed = {}
+    weights = None
+    for step in range(steps):
+        cfg = {
+            "step": step,
+            "has_relay": step in relayed,
+            "first_step": step == 0,
+            "pieces": seq_count,
+            "hops": hops,
+            "head": head,
+            "heads": heads,
+            "group": heads // kv_heads,
+            "turns": turns,
+            "halves": HALVES,
+        }
+        operands = [key_bias, timesteps, contact_table, norm_gain, time_freq, attn_gate, keyframes]
+        operands += first
+        if step >= 2:
+            operands += second
+        operands += rings[0] + rings[1] if step == 0 else [weights]
+        operands += relayed.get(step, [])
+        out_shape = [shape((part, rows, cols), kind)] * HALVES
+        if step == 0:
+            out_shape += [shape((width, 2 * cols), kind)]
+        results = call(
+            functools.partial(step_kernel, cfg),
+            "step%d" % step,
+            out_shape,
+            [smem, smem] + [vmem] * (len(operands) - 2),
+            operands,
+            [
+                pltpu.VMEM((frames, width), kind),
+                pltpu.VMEM((1, width), jnp.float32),
+                pltpu.VMEM((frames, 128), jnp.float32),
+                pltpu.VMEM((frames, cols), jnp.float32),
+                pltpu.VMEM((frames, 2 * cols + 128), kind),
+                pltpu.VMEM((frames, cols), jnp.float32),
+                pltpu.SemaphoreType.DMA((4 * hops,)),
+            ],
+            20,
+            2 * frames * width * 2 * cols + 4 * heads * frames * frames * head,
+            out_specs=[vmem] * len(out_shape),
+        )
+        outputs.append(list(results[:HALVES]))
+        if step == 0:
+            weights = results[HALVES]
+        if step == 2:
+            pending = [piece for k in range(HALVES) for piece in (crossing[k][0], crossing[k][1])]
+            tied = call(
+                functools.partial(tie_kernel, len(pending)),
+                "tie",
+                [shape(piece.shape, kind) for piece in pending],
+                [anywhere] * (len(pending) + 1),
+                pending + [outputs[-1][0]],
+                out_specs=[anywhere] * len(pending),
+                input_output_aliases={i: i for i in range(len(pending))},
+            )
+            relayed[3] = []
+            for k in range(HALVES):
+                mine, across = tied[2 * k], tied[2 * k + 1]
+                relayed[3] += [mine, across, swap(mine, 1), swap(across, 1)]
+            early = call(
+                functools.partial(early_kernel, turns, seq_count, HALVES, feats),
+                "early",
+                [shape((turns - 1, rows, cols), kind)] * seq_count
+                + [shape((cols, feats), jnp.float32)],
+                [vmem] * (turns * HALVES + seq_count),
+                [half for output in outputs for half in output] + second,
+                limit=8,
+                out_specs=[vmem] * (seq_count + 1),
+            )
+            early, early_grad = list(early[:-1]), early[-1]
+            early = [early[0]] + [swap(early[m], m) for m in range(1, seq_count)]
+        if step + 2 < steps:
+            pieces = [passed_along(half, "pipe", 1) for half in outputs[-1]]
+            crossing = [(piece, swap(piece, 2)) for piece in pieces]
+            if step == 0:
+                relayed[2] = []
+                for mine, across in crossing:
+                    relayed[2] += [mine, across, swap(mine, 1), swap(across, 1)]
+
+    g_shape = (cols // hops, feats)
+    operands = outputs[-2] + outputs[-1] + second + early + [early_grad]
+    settled = call(
+        functools.partial(settle_kernel, turns, seq_count, HALVES, hops, feats),
+        "settle",
+        [shape((rows, cols), kind)] * seq_count
+        + [shape(g_shape, jnp.float32)]
+        + [shape(g_shape, kind)] * (hops - 1)
+        + [shape((turns, rows, width), kind)],
+        [vmem] * len(operands),
+        operands,
+        [
+            pltpu.VMEM((turns - 1, rows, width), kind),
+            pltpu.VMEM((cols, feats), jnp.float32),
+            pltpu.SemaphoreType.DMA,
+        ],
+        8,
+        out_specs=[vmem] * (seq_count + hops) + [anywhere],
+    )
+    late, grads, held = settled[:seq_count], settled[seq_count:-1], settled[-1]
+    late = [late[0]] + [swap(late[m], m) for m in range(1, seq_count)]
+    grads = [grads[0]] + [shifted(grads[k], "dp", k) for k in range(1, hops)]
+    section_out, grad_rows = call(
+        functools.partial(finish_kernel, seq_count, hops),
+        "finish",
+        [shape((turns, rows, width), kind), shape(g_shape, jnp.float32)],
+        [anywhere] + [vmem] * (seq_count + hops),
+        [held] + late + grads,
+        [pltpu.VMEM((rows, width), kind), pltpu.SemaphoreType.DMA],
+        out_specs=[anywhere, vmem],
+        input_output_aliases={0: 0},
+    )
+    return (section_out[None, :, None], grad_rows[None])
+
+
+def body(incoming, contacts, keyframes, timesteps, w_query, *others):
+    count = lax.axis_size("seq")
+    cols = w_query.shape[2] // count
+    paired = (
+        lax.axis_size("pipe") == 2
+        and count == 4
+        and cols % 128 == 0
+        and w_query.shape[1] % 16 == 0
+        and incoming.shape[3] == 128
+        and incoming.shape[1] == 3
+    )
+    chosen = paired_body if paired else general_body
+    return chosen(incoming, contacts, keyframes, timesteps, w_query, *others)
+
+
+def general_body(
     incoming,
     contacts,
     keyframes,

time: 238 us -> 148 us (0.62)
  matrix products: 38.9 us -> 0 us
  Pallas kernels: 0 us -> 35.2 us
  blocking collectives: 34.1 us -> 0 us
  between operations: 17.4 us -> 1.2 us
  other arithmetic: 15.3 us -> 0 us
  local copies, waits for them, and re-layouts: 24.2 us -> 9.69 us
  waiting for transfers between devices: 80.5 us -> 70 us
  starting transfers between devices: 25.8 us -> 30.9 us
    dot_general x47 -> x0, matrix products: 38.9 us -> none  [the longest x4 8.13 us: body(): jnp.dot(onehot, table, preferred_element_type=jnp.float32)]
    ppermute x3 -> x36, waiting for transfers between devices: 31.1 us -> 66.4 us  [the longest x9 35.1 us: shifted(): lax.ppermute(value, axis, [(source, (source + shift) % count) for source...]
    pallas_call x0 -> x13, Pallas kernels: none -> 35.2 us  [call(): pl.pallas_call(kernel, out_shape=out_shape, in_specs=in_specs, scratch_sh...]
    all_gather x6 -> x0, waiting for transfers between devices: 25.1 us -> none  [the longest x2 21.1 us: body(): handed[step + lag] = lax.all_gather(piece, 'seq', axis=1, tiled=True)]
    ppermute x3 -> x36, starting transfers between devices: 1.67 us -> 23.6 us  [the longest x27 15.6 us: swap(): lax.ppermute(value, 'seq', [(source, source ^ bit) for source in range(co...]
    all_gather x2 -> x0, blocking collectives: 17.6 us -> none  [the longest x1 12.5 us: body(): cot_all = lax.all_gather(head_cotangent[0, :, 0], 'seq', axis=1, tiled=True)]
    all_to_all x1 -> x0, blocking collectives: 16.5 us -> none  [body(): lax.all_to_all(w_parts, 'seq', split_axis=0, concat_axis=0, tiled=True)]
    all_to_all x4 -> x0, waiting for transfers between devices: 16.2 us -> none  [the longest x3 10.6 us: body(): lax.all_to_all(own, 'seq', split_axis=0, concat_axis=1, tiled=True)]
  transfers between devices with their start and end apart: 15 -> 40, of which waited for: 10 -> 16; matrix products, arithmetic and copies ran while one was open for 25% -> 0% of each run, Pallas kernels for 0% -> 22%
where the time goes in v4:
time: 148 us; the launch traced here: 147 us
  waiting for transfers between devices  70 us (47%)
  Pallas kernels  35.2 us (24%)
  starting transfers between devices  30.9 us (21%)
  local copies, waits for them, and re-layouts  9.69 us (7%)
    pallas_call x13, Pallas kernels, call(): pl.pallas_call(kernel, out_shape=out_shape, in_specs=in_specs, scratch_sh...  35.2 us
    ppermute x9, waiting for transfers between devices, shifted(): lax.ppermute(value, axis, [(source, (source + shift) % count) for source...  35.1 us
    ppermute x27, waiting for transfers between devices, swap(): lax.ppermute(value, 'seq', [(source, source ^ bit) for source in range(co...  31.3 us
    ppermute x27, starting transfers between devices, swap(): lax.ppermute(value, 'seq', [(source, source ^ bit) for source in range(co...  15.6 us
    unnamed x49, local copies, waits for them, and re-layouts  9.69 us
    ppermute x9, starting transfers between devices, shifted(): lax.ppermute(value, axis, [(source, (source + shift) % count) for source...  7.97 us
    ppermute x4, starting transfers between devices, passed_along(): lax.ppermute(value, axis, [(source, source + steps) for source in range(f...  7.34 us
    ppermute x4, waiting for transfers between devices, passed_along(): lax.ppermute(value, axis, [(source, source + steps) for source in range(f...  3.61 us
  transfers between devices with their start and end apart: 40, of which 16 were waited for; matrix products, arithmetic and copies ran while one was open for 0% of the time, Pallas kernels for 22%

profile of v4, /device:TPU:0, one launch (start us, length us, event | category | flops | bytes accessed | tf_op | source)
XLA Modules:
  0.0 147.0 jit_solution(5709402097174159993)
XLA Ops:
  0.7 1.0 copy-done.9
  1.7 1.0 copy-done.10
  2.7 0.1 pack.1
  2.7 0.5 collective-permute-start
  3.2 2.6 %collective-permute-start.1 = (bf16[96,768]{1,0:T(8,128)(2,1)S(1)}, bf16[96,768]{1,0:T(8,128)(2,1)S(1)}, u32[]{:S(2)}, u32[]{:S(2)}) collective-permute-start(bf16[96,768]{1,0:T(8,128)(2,1)S(1)} %get-tuple-element.37), channel_id=1, source_target_pairs={{0,8},{4,12},{8,0},{12,4},{1,9},{5,13},{9,1},{13,5},{2,10},{6,14},... | collective-permute-start | bytes 442376 | tf_op jit(solution)/shard_map/ppermute | solution.py:27
  5.8 0.1 collective-permute-start.2
  5.9 4.6 %collective-permute-done.1.a = bf16[96,768]{1,0:T(8,128)(2,1)S(1)} collective-permute-done((bf16[96,768]{1,0:T(8,128)(2,1)S(1)}, bf16[96,768]{1,0:T(8,128)(2,1)S(1)}, u32[]{:S(2)}, u32[]{:S(2)}) %collective-permute-start.1) | collective-permute-done | bytes 147488 | tf_op jit(solution)/shard_map/ppermute | solution.py:27
  10.5 2.6 %collective-permute-done.2.b = bf16[96,768]{1,0:T(8,128)(2,1)S(1)} collective-permute-done((bf16[96,768]{1,0:T(8,128)(2,1)S(1)}, bf16[96,768]{1,0:T(8,128)(2,1)S(1)}, u32[]{:S(2)}, u32[]{:S(2)}) %collective-permute-start.2) | collective-permute-done | bytes 147488 | tf_op jit(solution)/shard_map/ppermute | solution.py:27
  13.2 0.1 first.1.refs_7_
  13.4 1.6 %collective-permute-start.3 = (bf16[272,1536]{1,0:T(8,128)(2,1)S(1)}, bf16[272,1536]{1,0:T(8,128)(2,1)}, u32[]{:S(2)}, u32[]{:S(2)}) collective-permute-start(bf16[272,1536]{1,0:T(8,128)(2,1)S(1)} %first.1.refs_7_), channel_id=1, source_target_pairs={{0,8},{4,12},{8,0},{12,4},{1,9},{5,13},{9,1},{13,5},{2,10},{6,14},... | collective-permute-start | bytes 2506760 | tf_op jit(solution)/shard_map/ppermute | solution.py:27
  15.0 1.6 %collective-permute-start.12 = (bf16[2,96,768]{2,1,0:T(8,128)(2,1)S(1)}, bf16[2,96,768]{2,1,0:T(8,128)(2,1)S(1)}, u32[]{:S(2)}, u32[]{:S(2)}) collective-permute-start(bf16[2,96,768]{2,1,0:T(8,128)(2,1)S(1)} %far.1.dep.refs_15_), channel_id=1, source_target_pairs={{0,1},{1,2},{2,3},{3,0},{4,5},{5,6},{6,7},{7,4},{8,9},{9,10},{10,1... | collective-permute-start | bytes 884744 | tf_op jit(solution)/shard_map/ppermute | solution.py:32
  16.6 1.6 %collective-permute-start.9 = (bf16[2,96,768]{2,1,0:T(8,128)(2,1)S(1)}, bf16[2,96,768]{2,1,0:T(8,128)(2,1)S(1)}, u32[]{:S(2)}, u32[]{:S(2)}) collective-permute-start(bf16[2,96,768]{2,1,0:T(8,128)(2,1)S(1)} %near.1.dep.refs_11_), channel_id=1, source_target_pairs={{0,1},{1,2},{2,3},{3,0},{4,5},{5,6},{6,7},{7,4},{8,9},{9,10},{10,1... | collective-permute-start | bytes 884744 | tf_op jit(solution)/shard_map/ppermute | solution.py:32
  18.2 16.0 %collective-permute-done.3.dep.refs_8_ = bf16[272,1536]{1,0:T(8,128)(2,1)} collective-permute-done((bf16[272,1536]{1,0:T(8,128)(2,1)S(1)}, bf16[272,1536]{1,0:T(8,128)(2,1)}, u32[]{:S(2)}, u32[]{:S(2)}) %collective-permute-start.3) | collective-permute-done | bytes 835616 | tf_op jit(solution)/shard_map/ppermute | solution.py:27
  34.2 1.8 %collective-permute-start.6 = (bf16[256,1536]{1,0:T(8,128)(2,1)S(1)}, bf16[256,1536]{1,0:T(8,128)(2,1)S(1)}, u32[]{:S(2)}, u32[]{:S(2)}) collective-permute-start(bf16[256,1536]{1,0:T(8,128)(2,1)S(1)} %second.1.refs_11_.refs_6_.refs_4_), channel_id=1, source_target_pairs={{0,8},{4,12},{8,0},{12,4},{1,9},{5,13},{9,1},{13,5},{2,10},{6,14},... | collective-permute-start | bytes 2359304 | tf_op jit(solution)/shard_map/ppermute | solution.py:27
  36.0 1.6 %collective-permute-start.13 = (bf16[2,96,768]{2,1,0:T(8,128)(2,1)S(1)}, bf16[2,96,768]{2,1,0:T(8,128)(2,1)}, u32[]{:S(2)}, u32[]{:S(2)}) collective-permute-start(bf16[2,96,768]{2,1,0:T(8,128)(2,1)S(1)} %collective-permute-done.12.refs_16_), channel_id=1, source_target_pairs={{0,1},{1,2},{2,3},{3,0},{4,5},{5,6},{6,7},{7,4},{8,9},{9,10},{10,1... | collective-permute-start | bytes 884744 | tf_op jit(solution)/shard_map/ppermute | solution.py:32
  37.6 0.7 copy-done.19
  38.3 1.6 %collective-permute-start.10 = (bf16[2,96,768]{2,1,0:T(8,128)(2,1)S(1)}, bf16[2,96,768]{2,1,0:T(8,128)(2,1)}, u32[]{:S(2)}, u32[]{:S(2)}) collective-permute-start(bf16[2,96,768]{2,1,0:T(8,128)(2,1)S(1)} %collective-permute-done.9.refs_12_), channel_id=1, source_target_pairs={{0,1},{1,2},{2,3},{3,0},{4,5},{5,6},{6,7},{7,4},{8,9},{9,10},{10,1... | collective-permute-start | bytes 884744 | tf_op jit(solution)/shard_map/ppermute | solution.py:32
  39.9 0.7 copy-done.21
  40.6 7.1 %collective-permute-done.13.refs_17_ = bf16[2,96,768]{2,1,0:T(8,128)(2,1)} collective-permute-done((bf16[2,96,768]{2,1,0:T(8,128)(2,1)S(1)}, bf16[2,96,768]{2,1,0:T(8,128)(2,1)}, u32[]{:S(2)}, u32[]{:S(2)}) %collective-permute-start.13) | collective-permute-done | bytes 294944 | tf_op jit(solution)/shard_map/ppermute | solution.py:32
  47.8 5.7 %collective-permute-done.10.refs_13_ = bf16[2,96,768]{2,1,0:T(8,128)(2,1)} collective-permute-done((bf16[2,96,768]{2,1,0:T(8,128)(2,1)S(1)}, bf16[2,96,768]{2,1,0:T(8,128)(2,1)}, u32[]{:S(2)}, u32[]{:S(2)}) %collective-permute-start.10) | collective-permute-done | bytes 294944 | tf_op jit(solution)/shard_map/ppermute | solution.py:32
  53.5 0.9 copy-done.4
  54.3 1.3 collective-permute-start.11
  55.6 0.1 copy.20.refs_1_
  55.7 9.8 %collective-permute-done.14.refs_18_ = bf16[2,96,768]{2,1,0:T(8,128)(2,1)} collective-permute-done((bf16[2,96,768]{2,1,0:T(8,128)(2,1)}, bf16[2,96,768]{2,1,0:T(8,128)(2,1)}, u32[]{:S(2)}, u32[]{:S(2)}) %collective-permute-start.14) | collective-permute-done | bytes 294944 | tf_op jit(solution)/shard_map/ppermute | solution.py:32
  65.5 4.7 %collective-permute-done.11.refs_14_ = bf16[2,96,768]{2,1,0:T(8,128)(2,1)} collective-permute-done((bf16[2,96,768]{2,1,0:T(8,128)(2,1)}, bf16[2,96,768]{2,1,0:T(8,128)(2,1)}, u32[]{:S(2)}, u32[]{:S(2)}) %collective-permute-start.11) | collective-permute-done | bytes 294944 | tf_op jit(solution)/shard_map/ppermute | solution.py:32
  70.3 1.1 copy-done.1
  71.5 1.1 copy-done.5
  72.6 1.0 copy-done.8
  73.6 1.0 copy-done.20
  74.5 1.0 copy-done.22
  75.5 10.7 %step0.1 = (bf16[2,128,384]{2,1,0:T(8,128)(2,1)S(1)}, bf16[2,128,384]{2,1,0:T(8,128)(2,1)S(1)}, bf16[1536,768]{1,0:T(8,128)(2,1)S(1)}) custom-call(f32[1,16]{1,0:T(1,128)S(1)} %copy-done.17, s32[4,1]{1,0:T(4,128)S(1)} %copy.20.refs_1_, bf16[1,16,1536]{2,1,0:T(8,128)(2,1)S(1)} %copy-done.11, f32[1,1536]{1,0:T(1,128)S(1)} %copy-done.14, ...), custom_call_target="tpu_custom_call" | custom-call | flops 1610612736 | bytes 3145728 | tf_op jit(solution)/shard_map/step0/pallas_call | solution.py:362
  86.2 3.4 %collective-permute-start.15 = (bf16[2,128,384]{2,1,0:T(8,128)(2,1)S(1)}, bf16[2,128,384]{2,1,0:T(8,128)(2,1)S(1)}, u32[]{:S(2)}, u32[]{:S(2)}) collective-permute-start(bf16[2,128,384]{2,1,0:T(8,128)(2,1)S(1)} %get-tuple-element.40.refs_0_), channel_id=1, source_target_pairs={{0,16},{1,17},{2,18},{3,19},{4,20},{5,21},{6,22},{7,23},{8,24},{9,... | collective-permute-start | bytes 589832 | tf_op jit(solution)/shard_map/ppermute | solution.py:17
  89.7 1.3 collective-permute-start.19
  91.0 6.9 %step1.1 = (bf16[2,128,384]{2,1,0:T(8,128)(2,1)S(1)}, bf16[2,128,384]{2,1,0:T(8,128)(2,1)S(1)}) custom-call(f32[1,16]{1,0:T(1,128)S(1)} %copy-done.17, s32[4,1]{1,0:T(4,128)S(1)} %copy.20.refs_1_, bf16[1,16,1536]{2,1,0:T(8,128)(2,1)S(1)} %copy-done.11, f32[1,1536]{1,0:T(1,128)S(1)} %copy-done.14, f32[1,1536]{1,0:T(1,128)S(1)} %copy-done.15, ...), custom_call_target="tpu_custom_call" | custom-call | flops 1610612736 | bytes 3145728 | tf_op jit(solution)/shard_map/step1/pallas_call | solution.py:362
  97.9 1.3 collective-permute-start.23
  99.3 1.3 collective-permute-start.25
  100.6 0.6 collective-permute-start.16
  101.2 1.5 %collective-permute-start.20 = (bf16[2,128,384]{2,1,0:T(8,128)(2,1)S(1)}, bf16[2,128,384]{2,1,0:T(8,128)(2,1)S(1)}, u32[]{:S(2)}, u32[]{:S(2)}) collective-permute-start(bf16[2,128,384]{2,1,0:T(8,128)(2,1)S(1)} %collective-permute-done.19.refs_20_), channel_id=1, source_target_pairs={{0,8},{4,12},{8,0},{12,4},{1,9},{5,13},{9,1},{13,5},{2,10},{6,14},... | collective-permute-start | bytes 589832 | tf_op jit(solution)/shard_map/ppermute | solution.py:27
  102.7 1.5 %collective-permute-done.23.refs_0_ = bf16[2,128,384]{2,1,0:T(8,128)(2,1)S(1)} collective-permute-done((bf16[2,128,384]{2,1,0:T(8,128)(2,1)S(1)}, bf16[2,128,384]{2,1,0:T(8,128)(2,1)S(1)}, u32[]{:S(2)}, u32[]{:S(2)}) %collective-permute-start.23) | collective-permute-done | bytes 196640 | tf_op jit(solution)/shard_map/ppermute | solution.py:17
  104.2 2.1 %collective-permute-done.25.refs_2_ = bf16[2,128,384]{2,1,0:T(8,128)(2,1)S(1)} collective-permute-done((bf16[2,128,384]{2,1,0:T(8,128)(2,1)S(1)}, bf16[2,128,384]{2,1,0:T(8,128)(2,1)S(1)}, u32[]{:S(2)}, u32[]{:S(2)}) %collective-permute-start.25) | collective-permute-done | bytes 196640 | tf_op jit(solution)/shard_map/ppermute | solution.py:17
  106.3 1.5 %collective-permute-done.16.refs_17_ = bf16[2,128,384]{2,1,0:T(8,128)(2,1)S(1)} collective-permute-done((bf16[2,128,384]{2,1,0:T(8,128)(2,1)S(1)}, bf16[2,128,384]{2,1,0:T(8,128)(2,1)S(1)}, u32[]{:S(2)}, u32[]{:S(2)}) %collective-permute-start.16) | collective-permute-done | bytes 196640 | tf_op jit(solution)/shard_map/ppermute | solution.py:27
  107.8 2.1 %collective-permute-done.20.refs_21_ = bf16[2,128,384]{2,1,0:T(8,128)(2,1)S(1)} collective-permute-done((bf16[2,128,384]{2,1,0:T(8,128)(2,1)S(1)}, bf16[2,128,384]{2,1,0:T(8,128)(2,1)S(1)}, u32[]{:S(2)}, u32[]{:S(2)}) %collective-permute-start.20) | collective-permute-done | bytes 196640 | tf_op jit(solution)/shard_map/ppermute | solution.py:27
  109.9 0.5 collective-permute-start.24
  110.5 1.5 %collective-permute-start.26 = (bf16[2,128,384]{2,1,0:T(8,128)(2,1)S(1)}, bf16[2,128,384]{2,1,0:T(8,128)(2,1)S(1)}, u32[]{:S(2)}, u32[]{:S(2)}) collective-permute-start(bf16[2,128,384]{2,1,0:T(8,128)(2,1)S(1)} %collective-permute-done.25.refs_2_), channel_id=1, source_target_pairs={{0,8},{4,12},{8,0},{12,4},{1,9},{5,13},{9,1},{13,5},{2,10},{6,14},... | collective-permute-start | bytes 589832 | tf_op jit(solution)/shard_map/ppermute | solution.py:27
  112.0 7.2 %step2.1 = (bf16[2,128,384]{2,1,0:T(8,128)(2,1)S(1)}, bf16[2,128,384]{2,1,0:T(8,128)(2,1)S(1)}) custom-call(f32[1,16]{1,0:T(1,128)S(1)} %copy-done.17, s32[4,1]{1,0:T(4,128)S(1)} %copy.20.refs_1_, bf16[1,16,1536]{2,1,0:T(8,128)(2,1)S(1)} %copy-done.11, f32[1,1536]{1,0:T(1,128)S(1)} %copy-done.14, f32[1,1536]{1,0:T(1,128)S(1)} %copy-done.15, ...), custom_call_target="tpu_custom_call" | custom-call | flops 1610612736 | bytes 3145728 | tf_op jit(solution)/shard_map/step2/pallas_call | solution.py:362
  119.2 2.3 %collective-permute-done.26.refs_3_ = bf16[2,128,384]{2,1,0:T(8,128)(2,1)S(1)} collective-permute-done((bf16[2,128,384]{2,1,0:T(8,128)(2,1)S(1)}, bf16[2,128,384]{2,1,0:T(8,128)(2,1)S(1)}, u32[]{:S(2)}, u32[]{:S(2)}) %collective-permute-start.26) | collective-permute-done | bytes 196640 | tf_op jit(solution)/shard_map/ppermute | solution.py:27
  121.4 0.5 collective-permute-start.28
  122.0 0.5 collective-permute-start.30
  122.5 0.5 early.1
  123.0 0.1 collective-permute-start.31
  123.0 0.6 collective-permute-start.32
  123.7 1.2 collective-permute-start.33
  124.9 7.0 %step3.1 = (bf16[2,128,384]{2,1,0:T(8,128)(2,1)S(1)}, bf16[2,128,384]{2,1,0:T(8,128)(2,1)S(1)}) custom-call(f32[1,16]{1,0:T(1,128)S(1)} %copy-done.17, s32[4,1]{1,0:T(4,128)S(1)} %copy.20.refs_1_, bf16[1,16,1536]{2,1,0:T(8,128)(2,1)S(1)} %copy-done.11, f32[1,1536]{1,0:T(1,128)S(1)} %copy-done.14, f32[1,1536]{1,0:T(1,128)S(1)} %copy-done.15, ...), custom_call_target="tpu_custom_call" | custom-call | flops 1610612736 | bytes 3145728 | tf_op jit(solution)/shard_map/step3/pallas_call | solution.py:362
  131.9 2.2 %collective-permute-done.33.refs_11_ = bf16[2,128,384]{2,1,0:T(8,128)(2,1)S(1)} collective-permute-done((bf16[2,128,384]{2,1,0:T(8,128)(2,1)S(1)}, bf16[2,128,384]{2,1,0:T(8,128)(2,1)S(1)}, u32[]{:S(2)}, u32[]{:S(2)}) %collective-permute-start.33) | collective-permute-done | bytes 196640 | tf_op jit(solution)/shard_map/ppermute | solution.py:27
  134.1 1.3 settle.1
  135.4 0.1 collective-permute-start.37
  135.4 0.4 collective-permute-start.34
  135.8 0.5 collective-permute-start.35
  136.3 1.0 collective-permute-start.36
  137.4 0.3 collective-permute-start.38
  137.7 3.6 %collective-permute-done.37.refs_6_ = bf16[96,256]{1,0:T(8,128)(2,1)S(1)} collective-permute-done((bf16[96,256]{1,0:T(8,128)(2,1)S(1)}, bf16[96,256]{1,0:T(8,128)(2,1)S(1)}, u32[]{:S(2)}, u32[]{:S(2)}) %collective-permute-start.37) | collective-permute-done | bytes 49184 | tf_op jit(solution)/shard_map/ppermute | solution.py:32
  141.3 2.1 %collective-permute-done.38.refs_7_ = bf16[96,256]{1,0:T(8,128)(2,1)S(1)} collective-permute-done((bf16[96,256]{1,0:T(8,128)(2,1)S(1)}, bf16[96,256]{1,0:T(8,128)(2,1)S(1)}, u32[]{:S(2)}, u32[]{:S(2)}) %collective-permute-start.38) | collective-permute-done | bytes 49184 | tf_op jit(solution)/shard_map/ppermute | solution.py:32
  143.4 2.0 %collective-permute-done.39.refs_8_ = bf16[96,256]{1,0:T(8,128)(2,1)S(1)} collective-permute-done((bf16[96,256]{1,0:T(8,128)(2,1)S(1)}, bf16[96,256]{1,0:T(8,128)(2,1)S(1)}, u32[]{:S(2)}, u32[]{:S(2)}) %collective-permute-start.39) | collective-permute-done | bytes 49184 | tf_op jit(solution)/shard_map/ppermute | solution.py:32
  145.4 1.5 finish.1
  (78 shorter events, 0.3 us)
Async XLA Ops:
  0.6 12.5 %copy-start.3 = (bf16[1,3,1,128,1536]{4,3,2,1,0:T(8,128)(2,1)S(1)}, bf16[1,3,1,128,1536]{4,3,2,1,0:T(8,128)(2,1)}, u32[]{:S(2)}) copy-start(bf16[1,3,1,128,1536]{4,3,2,1,0:T(8,128)(2,1)} %incoming.3) | copy-start | bytes 3538948
  0.6 1.1 copy-start.9
  1.7 1.0 copy-start.10
  2.7 10.5 %copy-start.18 = (s32[4,1,128]{2,1,0:T(1,128)S(1)}, s32[4,1,128]{2,1,0:T(1,128)}, u32[]{:S(2)}) copy-start(s32[4,1,128]{2,1,0:T(1,128)} %contacts.1) | copy-start | bytes 6148
  2.7 3.2 %collective-permute-start = (bf16[96,768]{1,0:T(8,128)(2,1)S(1)}, bf16[96,768]{1,0:T(8,128)(2,1)S(1)}, u32[]{:S(2)}, u32[]{:S(2)}) collective-permute-start(bf16[96,768]{1,0:T(8,128)(2,1)S(1)} %get-tuple-element.36), channel_id=1, source_target_pairs={{0,4},{4,0},{8,12},{12,8},{1,5},{5,1},{9,13},{13,9},{2,6},{6,2},{1... | collective-permute-start | bytes 442376 | tf_op jit(solution)/shard_map/ppermute | solution.py:27
  3.2 7.3 %collective-permute-start.1 = (bf16[96,768]{1,0:T(8,128)(2,1)S(1)}, bf16[96,768]{1,0:T(8,128)(2,1)S(1)}, u32[]{:S(2)}, u32[]{:S(2)}) collective-permute-start(bf16[96,768]{1,0:T(8,128)(2,1)S(1)} %get-tuple-element.37), channel_id=1, source_target_pairs={{0,8},{4,12},{8,0},{12,4},{1,9},{5,13},{9,1},{13,5},{2,10},{6,14},... | collective-permute-start | bytes 442376 | tf_op jit(solution)/shard_map/ppermute | solution.py:27
  5.8 7.3 %collective-permute-start.2 = (bf16[96,768]{1,0:T(8,128)(2,1)S(1)}, bf16[96,768]{1,0:T(8,128)(2,1)S(1)}, u32[]{:S(2)}, u32[]{:S(2)}) collective-permute-start(bf16[96,768]{1,0:T(8,128)(2,1)S(1)} %get-tuple-element.38), channel_id=1, source_target_pairs={{0,12},{4,8},{8,4},{12,0},{1,13},{5,9},{9,5},{13,1},{2,14},{6,10},... | collective-permute-start | bytes 442376 | tf_op jit(solution)/shard_map/ppermute | solution.py:27
  13.2 21.0 %copy-start.7 = (bf16[2,96,768]{2,1,0:T(8,128)(2,1)}, bf16[2,96,768]{2,1,0:T(8,128)(2,1)S(1)}, u32[]{:S(2)}) copy-start(bf16[2,96,768]{2,1,0:T(8,128)(2,1)S(1)} %far.1.dep.refs_15_) | copy-start | bytes 884740
  13.2 21.0 %copy-start.12 = (bf16[1,3,1,128,256]{4,3,2,1,0:T(8,128)(2,1)S(1)}, bf16[1,3,1,128,256]{4,3,2,1,0:T(8,128)(2,1)}, u32[]{:S(2)}) copy-start(bf16[1,3,1,128,256]{4,3,2,1,0:T(8,128)(2,1)} %cotangent.1) | copy-start | bytes 589828
  13.3 20.9 %copy-start = (bf16[272,1536]{1,0:T(8,128)(2,1)}, bf16[272,1536]{1,0:T(8,128)(2,1)S(1)}, u32[]{:S(2)}) copy-start(bf16[272,1536]{1,0:T(8,128)(2,1)S(1)} %first.1.refs_7_) | copy-start | bytes 2506756
  13.3 42.4 %copy-start.23 = (s32[4,1]{0,1:T(1,128)S(1)}, s32[4,1]{0,1:T(1,128)}, u32[]{:S(2)}) copy-start(s32[4,1]{0,1:T(1,128)} %param.15) | copy-start | bytes 52
  13.3 57.0 %copy-start.11 = (bf16[1,16,1536]{2,1,0:T(8,128)(2,1)S(1)}, bf16[1,16,1536]{2,1,0:T(8,128)(2,1)}, u32[]{:S(2)}) copy-start(bf16[1,16,1536]{2,1,0:T(8,128)(2,1)} %refs_2_.7) | copy-start | bytes 147460
  13.3 57.0 %copy-start.13 = (s32[4,1,512]{2,1,0:T(1,128)S(1)}, s32[4,1,512]{2,1,0:T(1,128)}, u32[]{:S(2)}) copy-start(s32[4,1,512]{2,1,0:T(1,128)} %refs_6_.7) | copy-start | bytes 24580
  13.3 57.0 %copy-start.14 = (f32[1,1536]{1,0:T(1,128)S(1)}, f32[1,1536]{1,0:T(1,128)}, u32[]{:S(2)}) copy-start(f32[1,1536]{1,0:T(1,128)} %refs_3_.7) | copy-start | bytes 18436
  13.3 57.0 %copy-start.15 = (f32[1,1536]{1,0:T(1,128)S(1)}, f32[1,1536]{1,0:T(1,128)}, u32[]{:S(2)}) copy-start(f32[1,1536]{1,0:T(1,128)} %refs_4_.7) | copy-start | bytes 18436
  13.3 57.0 %copy-start.16 = (f32[1,1536]{1,0:T(1,128)S(1)}, f32[1,1536]{1,0:T(1,128)}, u32[]{:S(2)}) copy-start(f32[1,1536]{1,0:T(1,128)} %refs_5_.7) | copy-start | bytes 18436
  13.4 57.0 %copy-start.17 = (f32[1,16]{1,0:T(1,128)S(1)}, f32[1,16]{1,0:T(1,128)}, u32[]{:S(2)}) copy-start(f32[1,16]{1,0:T(1,128)} %refs_0_.7) | copy-start | bytes 196
  13.4 20.8 %collective-permute-start.3 = (bf16[272,1536]{1,0:T(8,128)(2,1)S(1)}, bf16[272,1536]{1,0:T(8,128)(2,1)}, u32[]{:S(2)}, u32[]{:S(2)}) collective-permute-start(bf16[272,1536]{1,0:T(8,128)(2,1)S(1)} %first.1.refs_7_), channel_id=1, source_target_pairs={{0,8},{4,12},{8,0},{12,4},{1,9},{5,13},{9,1},{13,5},{2,10},{6,14},... | collective-permute-start | bytes 2506760 | tf_op jit(solution)/shard_map/ppermute | solution.py:27
  15.0 38.5 %collective-permute-start.4 = (bf16[272,1536]{1,0:T(8,128)(2,1)S(1)}, bf16[272,1536]{1,0:T(8,128)(2,1)S(1)}, u32[]{:S(2)}, u32[]{:S(2)}) collective-permute-start(bf16[272,1536]{1,0:T(8,128)(2,1)S(1)} %first.1.refs_7_), channel_id=1, source_target_pairs={{0,4},{4,0},{8,12},{12,8},{1,5},{5,1},{9,13},{13,9},{2,6},{6,2},{1... | collective-permute-start | bytes 2506760 | tf_op jit(solution)/shard_map/ppermute | solution.py:27
  15.0 21.0 %collective-permute-start.12 = (bf16[2,96,768]{2,1,0:T(8,128)(2,1)S(1)}, bf16[2,96,768]{2,1,0:T(8,128)(2,1)S(1)}, u32[]{:S(2)}, u32[]{:S(2)}) collective-permute-start(bf16[2,96,768]{2,1,0:T(8,128)(2,1)S(1)} %far.1.dep.refs_15_), channel_id=1, source_target_pairs={{0,1},{1,2},{2,3},{3,0},{4,5},{5,6},{6,7},{7,4},{8,9},{9,10},{10,1... | collective-permute-start | bytes 884744 | tf_op jit(solution)/shard_map/ppermute | solution.py:32
  16.6 21.7 %collective-permute-start.9 = (bf16[2,96,768]{2,1,0:T(8,128)(2,1)S(1)}, bf16[2,96,768]{2,1,0:T(8,128)(2,1)S(1)}, u32[]{:S(2)}, u32[]{:S(2)}) collective-permute-start(bf16[2,96,768]{2,1,0:T(8,128)(2,1)S(1)} %near.1.dep.refs_11_), channel_id=1, source_target_pairs={{0,1},{1,2},{2,3},{3,0},{4,5},{5,6},{6,7},{7,4},{8,9},{9,10},{10,1... | collective-permute-start | bytes 884744 | tf_op jit(solution)/shard_map/ppermute | solution.py:32
  34.2 36.1 %collective-permute-start.5 = (bf16[272,1536]{1,0:T(8,128)(2,1)}, bf16[272,1536]{1,0:T(8,128)(2,1)}, u32[]{:S(2)}, u32[]{:S(2)}) collective-permute-start(bf16[272,1536]{1,0:T(8,128)(2,1)} %collective-permute-done.3.dep.refs_8_), channel_id=1, source_target_pairs={{0,4},{4,0},{8,12},{12,8},{1,5},{5,1},{9,13},{13,9},{2,6},{6,2},{1... | collective-permute-start | bytes 2506760 | tf_op jit(solution)/shard_map/ppermute | solution.py:27
  34.2 21.4 %collective-permute-start.6 = (bf16[256,1536]{1,0:T(8,128)(2,1)S(1)}, bf16[256,1536]{1,0:T(8,128)(2,1)S(1)}, u32[]{:S(2)}, u32[]{:S(2)}) collective-permute-start(bf16[256,1536]{1,0:T(8,128)(2,1)S(1)} %second.1.refs_11_.refs_6_.refs_4_), channel_id=1, source_target_pairs={{0,8},{4,12},{8,0},{12,4},{1,9},{5,13},{9,1},{13,5},{2,10},{6,14},... | collective-permute-start | bytes 2359304 | tf_op jit(solution)/shard_map/ppermute | solution.py:27
  36.0 11.7 %collective-permute-start.13 = (bf16[2,96,768]{2,1,0:T(8,128)(2,1)S(1)}, bf16[2,96,768]{2,1,0:T(8,128)(2,1)}, u32[]{:S(2)}, u32[]{:S(2)}) collective-permute-start(bf16[2,96,768]{2,1,0:T(8,128)(2,1)S(1)} %collective-permute-done.12.refs_16_), channel_id=1, source_target_pairs={{0,1},{1,2},{2,3},{3,0},{4,5},{5,6},{6,7},{7,4},{8,9},{9,10},{10,1... | collective-permute-start | bytes 884744 | tf_op jit(solution)/shard_map/ppermute | solution.py:32
  37.6 0.7 copy-start.19
  38.3 15.1 %collective-permute-start.10 = (bf16[2,96,768]{2,1,0:T(8,128)(2,1)S(1)}, bf16[2,96,768]{2,1,0:T(8,128)(2,1)}, u32[]{:S(2)}, u32[]{:S(2)}) collective-permute-start(bf16[2,96,768]{2,1,0:T(8,128)(2,1)S(1)} %collective-permute-done.9.refs_12_), channel_id=1, source_target_pairs={{0,1},{1,2},{2,3},{3,0},{4,5},{5,6},{6,7},{7,4},{8,9},{9,10},{10,1... | collective-permute-start | bytes 884744 | tf_op jit(solution)/shard_map/ppermute | solution.py:32
  39.9 0.7 copy-start.21
  47.8 51.5 %collective-permute-start.7 = (bf16[256,1536]{1,0:T(8,128)(2,1)S(1)}, bf16[256,1536]{1,0:T(8,128)(2,1)S(1)}, u32[]{:S(2)}, u32[]{:S(2)}) collective-permute-start(bf16[256,1536]{1,0:T(8,128)(2,1)S(1)} %second.1.refs_11_.refs_6_.refs_4_), channel_id=1, source_target_pairs={{0,4},{4,0},{8,12},{12,8},{1,5},{5,1},{9,13},{13,9},{2,6},{6,2},{1... | collective-permute-start | bytes 2359304 | tf_op jit(solution)/shard_map/ppermute | solution.py:27
  53.4 12.1 %collective-permute-start.14 = (bf16[2,96,768]{2,1,0:T(8,128)(2,1)}, bf16[2,96,768]{2,1,0:T(8,128)(2,1)}, u32[]{:S(2)}, u32[]{:S(2)}) collective-permute-start(bf16[2,96,768]{2,1,0:T(8,128)(2,1)} %collective-permute-done.13.refs_17_), channel_id=1, source_target_pairs={{0,1},{1,2},{2,3},{3,0},{4,5},{5,6},{6,7},{7,4},{8,9},{9,10},{10,1... | collective-permute-start | bytes 884744 | tf_op jit(solution)/shard_map/ppermute | solution.py:32
  53.4 0.9 copy-start.4
  54.3 15.9 %collective-permute-start.11 = (bf16[2,96,768]{2,1,0:T(8,128)(2,1)}, bf16[2,96,768]{2,1,0:T(8,128)(2,1)}, u32[]{:S(2)}, u32[]{:S(2)}) collective-permute-start(bf16[2,96,768]{2,1,0:T(8,128)(2,1)} %collective-permute-done.10.refs_13_), channel_id=1, source_target_pairs={{0,1},{1,2},{2,3},{3,0},{4,5},{5,6},{6,7},{7,4},{8,9},{9,10},{10,1... | collective-permute-start | bytes 884744 | tf_op jit(solution)/shard_map/ppermute | solution.py:32
  55.6 56.3 %collective-permute-start.8 = (bf16[256,1536]{1,0:T(8,128)(2,1)S(1)}, bf16[256,1536]{1,0:T(8,128)(2,1)S(1)}, u32[]{:S(2)}, u32[]{:S(2)}) collective-permute-start(bf16[256,1536]{1,0:T(8,128)(2,1)S(1)} %collective-permute-done.6.refs_12_.refs_7_.refs_5_), channel_id=1, source_target_pairs={{0,4},{4,0},{8,12},{12,8},{1,5},{5,1},{9,13},{13,9},{2,6},{6,2},{1... | collective-permute-start | bytes 2359304 | tf_op jit(solution)/shard_map/ppermute | solution.py:27
  70.3 1.2 copy-start.1
  71.5 1.1 copy-start.5
  72.6 1.0 copy-start.8
  73.6 1.0 copy-start.20
  74.5 1.0 copy-start.22
  75.5 15.5 %copy-start.2 = (bf16[272,1536]{1,0:T(8,128)(2,1)S(1)}, bf16[272,1536]{1,0:T(8,128)(2,1)}, u32[]{:S(2)}) copy-start(bf16[272,1536]{1,0:T(8,128)(2,1)} %copy-done) | copy-start | bytes 2506756
  75.5 15.5 %copy-start.6 = (bf16[272,1536]{1,0:T(8,128)(2,1)S(1)}, bf16[272,1536]{1,0:T(8,128)(2,1)}, u32[]{:S(2)}) copy-start(bf16[272,1536]{1,0:T(8,128)(2,1)} %copy-done.4) | copy-start | bytes 2506756
  86.2 14.3 %collective-permute-start.15 = (bf16[2,128,384]{2,1,0:T(8,128)(2,1)S(1)}, bf16[2,128,384]{2,1,0:T(8,128)(2,1)S(1)}, u32[]{:S(2)}, u32[]{:S(2)}) collective-permute-start(bf16[2,128,384]{2,1,0:T(8,128)(2,1)S(1)} %get-tuple-element.40.refs_0_), channel_id=1, source_target_pairs={{0,16},{1,17},{2,18},{3,19},{4,20},{5,21},{6,22},{7,23},{8,24},{9,... | collective-permute-start | bytes 589832 | tf_op jit(solution)/shard_map/ppermute | solution.py:17
  89.7 11.5 %collective-permute-start.19 = (bf16[2,128,384]{2,1,0:T(8,128)(2,1)S(1)}, bf16[2,128,384]{2,1,0:T(8,128)(2,1)S(1)}, u32[]{:S(2)}, u32[]{:S(2)}) collective-permute-start(bf16[2,128,384]{2,1,0:T(8,128)(2,1)S(1)} %get-tuple-element.41.refs_1_), channel_id=1, source_target_pairs={{0,16},{1,17},{2,18},{3,19},{4,20},{5,21},{6,22},{7,23},{8,24},{9,... | collective-permute-start | bytes 589832 | tf_op jit(solution)/shard_map/ppermute | solution.py:17
  97.9 6.2 %collective-permute-start.23 = (bf16[2,128,384]{2,1,0:T(8,128)(2,1)S(1)}, bf16[2,128,384]{2,1,0:T(8,128)(2,1)S(1)}, u32[]{:S(2)}, u32[]{:S(2)}) collective-permute-start(bf16[2,128,384]{2,1,0:T(8,128)(2,1)S(1)} %get-tuple-element.44.refs_2_), channel_id=1, source_target_pairs={{0,16},{1,17},{2,18},{3,19},{4,20},{5,21},{6,22},{7,23},{8,24},{9,... | collective-permute-start | bytes 589832 | tf_op jit(solution)/shard_map/ppermute | solution.py:17
  99.3 7.0 %collective-permute-start.25 = (bf16[2,128,384]{2,1,0:T(8,128)(2,1)S(1)}, bf16[2,128,384]{2,1,0:T(8,128)(2,1)S(1)}, u32[]{:S(2)}, u32[]{:S(2)}) collective-permute-start(bf16[2,128,384]{2,1,0:T(8,128)(2,1)S(1)} %get-tuple-element.45.refs_3_), channel_id=1, source_target_pairs={{0,16},{1,17},{2,18},{3,19},{4,20},{5,21},{6,22},{7,23},{8,24},{9,... | collective-permute-start | bytes 589832 | tf_op jit(solution)/shard_map/ppermute | solution.py:17
  100.6 7.2 %collective-permute-start.16 = (bf16[2,128,384]{2,1,0:T(8,128)(2,1)S(1)}, bf16[2,128,384]{2,1,0:T(8,128)(2,1)S(1)}, u32[]{:S(2)}, u32[]{:S(2)}) collective-permute-start(bf16[2,128,384]{2,1,0:T(8,128)(2,1)S(1)} %collective-permute-done.15.refs_16_), channel_id=1, source_target_pairs={{0,8},{4,12},{8,0},{12,4},{1,9},{5,13},{9,1},{13,5},{2,10},{6,14},... | collective-permute-start | bytes 589832 | tf_op jit(solution)/shard_map/ppermute | solution.py:27
  101.2 8.7 %collective-permute-start.20 = (bf16[2,128,384]{2,1,0:T(8,128)(2,1)S(1)}, bf16[2,128,384]{2,1,0:T(8,128)(2,1)S(1)}, u32[]{:S(2)}, u32[]{:S(2)}) collective-permute-start(bf16[2,128,384]{2,1,0:T(8,128)(2,1)S(1)} %collective-permute-done.19.refs_20_), channel_id=1, source_target_pairs={{0,8},{4,12},{8,0},{12,4},{1,9},{5,13},{9,1},{13,5},{2,10},{6,14},... | collective-permute-start | bytes 589832 | tf_op jit(solution)/shard_map/ppermute | solution.py:27
  104.2 5.7 %collective-permute-start.17 = (bf16[2,128,384]{2,1,0:T(8,128)(2,1)S(1)}, bf16[2,128,384]{2,1,0:T(8,128)(2,1)S(1)}, u32[]{:S(2)}, u32[]{:S(2)}) collective-permute-start(bf16[2,128,384]{2,1,0:T(8,128)(2,1)S(1)} %collective-permute-done.15.refs_16_), channel_id=1, source_target_pairs={{0,4},{4,0},{8,12},{12,8},{1,5},{5,1},{9,13},{13,9},{2,6},{6,2},{1... | collective-permute-start | bytes 589832 | tf_op jit(solution)/shard_map/ppermute | solution.py:27
  106.3 4.2 %collective-permute-start.21 = (bf16[2,128,384]{2,1,0:T(8,128)(2,1)S(1)}, bf16[2,128,384]{2,1,0:T(8,128)(2,1)S(1)}, u32[]{:S(2)}, u32[]{:S(2)}) collective-permute-start(bf16[2,128,384]{2,1,0:T(8,128)(2,1)S(1)} %collective-permute-done.19.refs_20_), channel_id=1, source_target_pairs={{0,4},{4,0},{8,12},{12,8},{1,5},{5,1},{9,13},{13,9},{2,6},{6,2},{1... | collective-permute-start | bytes 589832 | tf_op jit(solution)/shard_map/ppermute | solution.py:27
  107.8 4.1 %collective-permute-start.18 = (bf16[2,128,384]{2,1,0:T(8,128)(2,1)S(1)}, bf16[2,128,384]{2,1,0:T(8,128)(2,1)S(1)}, u32[]{:S(2)}, u32[]{:S(2)}) collective-permute-start(bf16[2,128,384]{2,1,0:T(8,128)(2,1)S(1)} %collective-permute-done.16.refs_17_), channel_id=1, source_target_pairs={{0,4},{4,0},{8,12},{12,8},{1,5},{5,1},{9,13},{13,9},{2,6},{6,2},{1... | collective-permute-start | bytes 589832 | tf_op jit(solution)/shard_map/ppermute | solution.py:27
  109.9 2.0 %collective-permute-start.22 = (bf16[2,128,384]{2,1,0:T(8,128)(2,1)S(1)}, bf16[2,128,384]{2,1,0:T(8,128)(2,1)S(1)}, u32[]{:S(2)}, u32[]{:S(2)}) collective-permute-start(bf16[2,128,384]{2,1,0:T(8,128)(2,1)S(1)} %collective-permute-done.20.refs_21_), channel_id=1, source_target_pairs={{0,4},{4,0},{8,12},{12,8},{1,5},{5,1},{9,13},{13,9},{2,6},{6,2},{1... | collective-permute-start | bytes 589832 | tf_op jit(solution)/shard_map/ppermute | solution.py:27
  109.9 9.3 %collective-permute-start.24 = (bf16[2,128,384]{2,1,0:T(8,128)(2,1)S(1)}, bf16[2,128,384]{2,1,0:T(8,128)(2,1)S(1)}, u32[]{:S(2)}, u32[]{:S(2)}) collective-permute-start(bf16[2,128,384]{2,1,0:T(8,128)(2,1)S(1)} %collective-permute-done.23.refs_0_), channel_id=1, source_target_pairs={{0,8},{4,12},{8,0},{12,4},{1,9},{5,13},{9,1},{13,5},{2,10},{6,14},... | collective-permute-start | bytes 589832 | tf_op jit(solution)/shard_map/ppermute | solution.py:27
  110.5 11.0 %collective-permute-start.26 = (bf16[2,128,384]{2,1,0:T(8,128)(2,1)S(1)}, bf16[2,128,384]{2,1,0:T(8,128)(2,1)S(1)}, u32[]{:S(2)}, u32[]{:S(2)}) collective-permute-start(bf16[2,128,384]{2,1,0:T(8,128)(2,1)S(1)} %collective-permute-done.25.refs_2_), channel_id=1, source_target_pairs={{0,8},{4,12},{8,0},{12,4},{1,9},{5,13},{9,1},{13,5},{2,10},{6,14},... | collective-permute-start | bytes 589832 | tf_op jit(solution)/shard_map/ppermute | solution.py:27
  121.4 1.6 %collective-permute-start.27 = (bf16[2,128,384]{2,1,0:T(8,128)(2,1)S(1)}, bf16[2,128,384]{2,1,0:T(8,128)(2,1)S(1)}, u32[]{:S(2)}, u32[]{:S(2)}) collective-permute-start(bf16[2,128,384]{2,1,0:T(8,128)(2,1)S(1)} %get-tuple-element.46.refs_16_), channel_id=1, source_target_pairs={{0,4},{4,0},{8,12},{12,8},{1,5},{5,1},{9,13},{13,9},{2,6},{6,2},{1... | collective-permute-start | bytes 589832 | tf_op jit(solution)/shard_map/ppermute | solution.py:27
  121.4 2.2 %collective-permute-start.28 = (bf16[2,128,384]{2,1,0:T(8,128)(2,1)S(1)}, bf16[2,128,384]{2,1,0:T(8,128)(2,1)S(1)}, u32[]{:S(2)}, u32[]{:S(2)}) collective-permute-start(bf16[2,128,384]{2,1,0:T(8,128)(2,1)S(1)} %get-tuple-element.47.refs_17_), channel_id=1, source_target_pairs={{0,4},{4,0},{8,12},{12,8},{1,5},{5,1},{9,13},{13,9},{2,6},{6,2},{1... | collective-permute-start | bytes 589832 | tf_op jit(solution)/shard_map/ppermute | solution.py:27
  122.0 3.0 %collective-permute-start.29 = (bf16[2,128,384]{2,1,0:T(8,128)(2,1)S(1)}, bf16[2,128,384]{2,1,0:T(8,128)(2,1)S(1)}, u32[]{:S(2)}, u32[]{:S(2)}) collective-permute-start(bf16[2,128,384]{2,1,0:T(8,128)(2,1)S(1)} %get-tuple-element.48.refs_20_), channel_id=1, source_target_pairs={{0,4},{4,0},{8,12},{12,8},{1,5},{5,1},{9,13},{13,9},{2,6},{6,2},{1... | collective-permute-start | bytes 589832 | tf_op jit(solution)/shard_map/ppermute | solution.py:27
  122.0 3.0 %collective-permute-start.30 = (bf16[2,128,384]{2,1,0:T(8,128)(2,1)S(1)}, bf16[2,128,384]{2,1,0:T(8,128)(2,1)S(1)}, u32[]{:S(2)}, u32[]{:S(2)}) collective-permute-start(bf16[2,128,384]{2,1,0:T(8,128)(2,1)S(1)} %get-tuple-element.49.refs_21_), channel_id=1, source_target_pairs={{0,4},{4,0},{8,12},{12,8},{1,5},{5,1},{9,13},{13,9},{2,6},{6,2},{1... | collective-permute-start | bytes 589832 | tf_op jit(solution)/shard_map/ppermute | solution.py:27
  123.0 9.0 %collective-permute-start.31 = (bf16[2,128,384]{2,1,0:T(8,128)(2,1)S(1)}, bf16[2,128,384]{2,1,0:T(8,128)(2,1)S(1)}, u32[]{:S(2)}, u32[]{:S(2)}) collective-permute-start(bf16[2,128,384]{2,1,0:T(8,128)(2,1)S(1)} %get-tuple-element.53), channel_id=1, source_target_pairs={{0,4},{4,0},{8,12},{12,8},{1,5},{5,1},{9,13},{13,9},{2,6},{6,2},{1... | collective-permute-start | bytes 589832 | tf_op jit(solution)/shard_map/ppermute | solution.py:27
  123.0 8.9 %collective-permute-start.32 = (bf16[2,128,384]{2,1,0:T(8,128)(2,1)S(1)}, bf16[2,128,384]{2,1,0:T(8,128)(2,1)S(1)}, u32[]{:S(2)}, u32[]{:S(2)}) collective-permute-start(bf16[2,128,384]{2,1,0:T(8,128)(2,1)S(1)} %get-tuple-element.54), channel_id=1, source_target_pairs={{0,8},{4,12},{8,0},{12,4},{1,9},{5,13},{9,1},{13,5},{2,10},{6,14},... | collective-permute-start | bytes 589832 | tf_op jit(solution)/shard_map/ppermute | solution.py:27
  123.7 10.4 %collective-permute-start.33 = (bf16[2,128,384]{2,1,0:T(8,128)(2,1)S(1)}, bf16[2,128,384]{2,1,0:T(8,128)(2,1)S(1)}, u32[]{:S(2)}, u32[]{:S(2)}) collective-permute-start(bf16[2,128,384]{2,1,0:T(8,128)(2,1)S(1)} %get-tuple-element.55), channel_id=1, source_target_pairs={{0,12},{4,8},{8,4},{12,0},{1,13},{5,9},{9,5},{13,1},{2,14},{6,10},... | collective-permute-start | bytes 589832 | tf_op jit(solution)/shard_map/ppermute | solution.py:27
  135.4 5.9 %collective-permute-start.37 = (bf16[96,256]{1,0:T(8,128)(2,1)S(1)}, bf16[96,256]{1,0:T(8,128)(2,1)S(1)}, u32[]{:S(2)}, u32[]{:S(2)}) collective-permute-start(bf16[96,256]{1,0:T(8,128)(2,1)S(1)} %get-tuple-element.63), channel_id=1, source_target_pairs={{0,1},{1,2},{2,3},{3,0},{4,5},{5,6},{6,7},{7,4},{8,9},{9,10},{10,1... | collective-permute-start | bytes 147464 | tf_op jit(solution)/shard_map/ppermute | solution.py:32
  135.4 10.0 %collective-permute-start.34 = (bf16[128,384]{1,0:T(8,128)(2,1)S(1)}, bf16[128,384]{1,0:T(8,128)(2,1)S(1)}, u32[]{:S(2)}, u32[]{:S(2)}) collective-permute-start(bf16[128,384]{1,0:T(8,128)(2,1)S(1)} %get-tuple-element.59), channel_id=1, source_target_pairs={{0,4},{4,0},{8,12},{12,8},{1,5},{5,1},{9,13},{13,9},{2,6},{6,2},{1... | collective-permute-start | bytes 294920 | tf_op jit(solution)/shard_map/ppermute | solution.py:27
  135.8 9.6 %collective-permute-start.35 = (bf16[128,384]{1,0:T(8,128)(2,1)S(1)}, bf16[128,384]{1,0:T(8,128)(2,1)S(1)}, u32[]{:S(2)}, u32[]{:S(2)}) collective-permute-start(bf16[128,384]{1,0:T(8,128)(2,1)S(1)} %get-tuple-element.60), channel_id=1, source_target_pairs={{0,8},{4,12},{8,0},{12,4},{1,9},{5,13},{9,1},{13,5},{2,10},{6,14},... | collective-permute-start | bytes 294920 | tf_op jit(solution)/shard_map/ppermute | solution.py:27
  136.3 9.1 %collective-permute-start.36 = (bf16[128,384]{1,0:T(8,128)(2,1)S(1)}, bf16[128,384]{1,0:T(8,128)(2,1)S(1)}, u32[]{:S(2)}, u32[]{:S(2)}) collective-permute-start(bf16[128,384]{1,0:T(8,128)(2,1)S(1)} %get-tuple-element.61), channel_id=1, source_target_pairs={{0,12},{4,8},{8,4},{12,0},{1,13},{5,9},{9,5},{13,1},{2,14},{6,10},... | collective-permute-start | bytes 294920 | tf_op jit(solution)/shard_map/ppermute | solution.py:27
  137.4 6.1 %collective-permute-start.38 = (bf16[96,256]{1,0:T(8,128)(2,1)S(1)}, bf16[96,256]{1,0:T(8,128)(2,1)S(1)}, u32[]{:S(2)}, u32[]{:S(2)}) collective-permute-start(bf16[96,256]{1,0:T(8,128)(2,1)S(1)} %get-tuple-element.64), channel_id=1, source_target_pairs={{0,2},{1,3},{2,0},{3,1},{4,6},{5,7},{6,4},{7,5},{8,10},{9,11},{10,... | collective-permute-start | bytes 147464 | tf_op jit(solution)/shard_map/ppermute | solution.py:32
  141.3 4.1 %collective-permute-start.39 = (bf16[96,256]{1,0:T(8,128)(2,1)S(1)}, bf16[96,256]{1,0:T(8,128)(2,1)S(1)}, u32[]{:S(2)}, u32[]{:S(2)}) collective-permute-start(bf16[96,256]{1,0:T(8,128)(2,1)S(1)} %get-tuple-element.65), channel_id=1, source_target_pairs={{0,3},{1,0},{2,1},{3,2},{4,7},{5,4},{6,5},{7,6},{8,11},{9,8},{10,9... | collective-permute-start | bytes 147464 | tf_op jit(solution)/shard_map/ppermute | solution.py:32

commit v5 on v4

--- a/solution.py
+++ b/solution.py
@@ -47,27 +47,33 @@
     return turn, turn - section + 1
 
 
-def pack_kernel(wq, wkv, own, *outs):
+def pack_kernel(wq, wkv, *refs):
+    outs, sems = refs[:-1], refs[-1]
     cols = outs[0].shape[1] // 2
     seq = lax.axis_index("seq")
-    targets = (own.at[0],) + outs
-    for m, out in enumerate(targets):
+    copies = []
+    for m, out in enumerate(outs):
         start = pl.multiple_of((seq ^ m) * cols, 128)
-        out[:, :cols] = wq[0, :, pl.ds(start, cols)]
-        out[:, cols:] = wkv[0, :, pl.ds(start, cols)]
-
-
-def pair_kernel(own, other, out):
-    out[0] = own[0]
-    out[1] = other[...]
-
-
-def stack_kernel(dep, a, b, out):
+        for k, source in enumerate((wq, wkv)):
+            copies.append(
+                pltpu.make_async_copy(
+                    source.at[0, :, pl.ds(start, cols)],
+                    out.at[:, pl.ds(k * cols, cols)],
+                    sems.at[2 * m + k],
+                )
+            )
+    for copy in copies:
+        copy.start()
+    for copy in copies:
+        copy.wait()
+
+
+def stack_kernel(a, b, out):
     out[0] = a[...]
     out[1] = b[...]
 
 
-def first_kernel(turns, dep, incoming, contacts, out, states):
+def first_kernel(turns, near, beside, far, incoming, contacts, out, states):
     rows = incoming.shape[3]
     for turn in range(2):
         out[turn * rows : (turn + 1) * rows] = incoming[0, turn, 0]
@@ -85,8 +91,67 @@
         out[rows:, turn * feats : (turn + 1) * feats] = cotangent[0, turn, 0]
 
 
+def columns_of(rows_of, pieces, rows):
+    labels = lax.broadcasted_iota(jnp.int32, (32, rows), 0)
+    columns = []
+    for i in range(pieces):
+        state, flag = rows_of(i)
+        one = jnp.zeros((32, rows), jnp.float32)
+        if state is not None:
+            one = jnp.where(labels == state, 1.0, 0.0)
+        if flag is not None:
+            one = jnp.where(labels == 16, flag, one)
+        columns.append(one.T)
+    return jnp.concatenate(columns, axis=0)
+
+
+def modulation(step, turns, times, gain, freq):
+    _, batch = turn_and_batch(step, turns)
+    return gain[...] * (1.0 + 0.5 * jnp.sin(times[batch, 0].astype(jnp.float32) * freq[...]))
+
+
+def norm_kernel(turns, pieces, times, table, gain, freq, *refs):
+    first, refs = refs[:pieces], refs[pieces + 1 :]
+    scaled, scales, owns, embeds, mod = refs[0:2], refs[2:4], refs[4:6], refs[6:8], refs[8]
+    frames, width = scaled[0].shape
+    rows, cols = frames // pieces, owns[0].shape[1]
+    seq = lax.axis_index("seq")
+    offsets = offsets_of(pieces)
+    for step in range(turns + 1):
+
+        def state_of(i):
+            state = first[i][2 * rows : 2 * rows + 16, :rows][step : step + 1]
+            return state.astype(jnp.float32).astype(jnp.int32), None
+
+        onehot = columns_of(state_of, pieces, rows)[:, : table.shape[1]].astype(jnp.bfloat16)
+        if step >= 2:
+            for at in range(0, width, 256):
+                embeds[step - 2][:, at : at + 256] = jnp.dot(
+                    onehot, table[0, :, at : at + 256], preferred_element_type=jnp.float32
+                ).astype(jnp.bfloat16)
+            continue
+        turn, _ = turn_and_batch(step, turns)
+        at = pl.multiple_of(jnp.minimum(turn, 1) * rows, 128)
+        mod[...] = modulation(step, turns, times, gain, freq)
+        total = jnp.zeros((frames, 128), jnp.float32)
+        for i in range(pieces):
+            lanes = pl.ds(pl.multiple_of((seq ^ offsets[i]) * cols, 128), cols)
+            current = jnp.concatenate([first[p][pl.ds(at, rows), lanes] for p in range(pieces)])
+            hidden = current.astype(jnp.float32) + jnp.dot(
+                onehot, table[0, :, lanes], preferred_element_type=jnp.float32
+            )
+            for lane in range(0, cols, 128):
+                piece = hidden[:, lane : lane + 128]
+                total = total + piece * piece
+            scaled[step][:, lanes] = (hidden * mod[:, lanes]).astype(jnp.bfloat16)
+            if i == 0:
+                owns[step][...] = hidden
+        mean = jnp.sum(total, axis=1, keepdims=True) * (1.0 / width)
+        scales[step][...] = jnp.broadcast_to(lax.rsqrt(mean + epsilon), (frames, 128))
+
+
 def step_kernel(cfg, *refs):
-    step, has_relay, first_step = cfg["step"], cfg["has_relay"], cfg["first_step"]
+    step, has_relay = cfg["step"], cfg["has_relay"]
     pieces, hops, head, turns = cfg["pieces"], cfg["hops"], cfg["head"], cfg["turns"]
     heads, group, halves = cfg["heads"], cfg["group"], cfg["halves"]
     refs = list(refs)
@@ -95,54 +160,33 @@
         taken, refs[:count] = refs[:count], []
         return taken
 
-    bias, times, table, gain, freq, gate, flags = take(7)
-    first = take(pieces)
-    second = take(pieces) if step >= 2 else None
-    chunks = take(2 * hops) if first_step else None
-    weights = None if first_step else take(1)[0]
-    relay = take(pieces * halves) if has_relay else None
+    bias, times, gain, freq, gate, flags = take(6)
+    if has_relay:
+        second, embed, relay = take(pieces), take(1)[0], take(pieces * halves)
+    else:
+        scaled, scales, own_hidden = take(3)
+    chunks = take(3 * hops) if step == 0 else None
+    weights = None if step == 0 else take(1)[0]
     outs = take(halves)
-    if first_step:
+    if step == 0:
         weights = take(1)[0]
-    scaled, mod, square, own_hidden, proj, att, sem_w = take(7)
+    proj, att = take(2)
+    if has_relay:
+        scaled, scales, own_hidden, mod = take(4)
     offsets = offsets_of(pieces)
     frames, width = scaled.shape
     rows, cols = frames // pieces, att.shape[1]
     part = pieces // halves
     seq, rep, section = lax.axis_index("seq"), lax.axis_index("dp"), lax.axis_index("pipe")
-    turn, batch = turn_and_batch(step, turns)
-
-    w_copies = []
-    if first_step:
-        w_rows = chunks[0].shape[1]
-        for ring in range(2):
+    _, batch = turn_and_batch(step, turns)
+
+    if step == 0:
+        w_rows = width // (pieces * hops)
+        for m in range(pieces):
             for hop in range(hops):
-                for j in range(2):
-                    block = (seq ^ (2 * ring + j)) * hops + lax.rem(rep + hops - hop, hops)
-                    w_copies.append(
-                        pltpu.make_async_copy(
-                            chunks[ring * hops + hop].at[j],
-                            weights.at[pl.ds(pl.multiple_of(block * w_rows, 16), w_rows)],
-                            sem_w.at[len(w_copies)],
-                        )
-                    )
-        for copy in w_copies:
-            copy.start()
-
-    labels = lax.broadcasted_iota(jnp.int32, (32, rows), 0)
-    columns = []
-    for i in range(pieces):
-        state = first[i][2 * rows : 2 * rows + 16, :rows][step : step + 1]
-        state = state.astype(jnp.float32).astype(jnp.int32)
-        flag = flags[batch, :, pl.ds(pl.multiple_of((seq ^ offsets[i]) * rows, 128), rows)]
-        one = jnp.where(labels == state, 1.0, 0.0)
-        columns.append(jnp.where(labels == 16, flag.astype(jnp.float32), one).T)
-    columns = jnp.concatenate(columns, axis=0)
-    onehot = columns[:, : table.shape[1]].astype(jnp.bfloat16)
-    flag_column = columns[:, 16:17]
-
-    time = times[batch, 0].astype(jnp.float32)
-    mod[...] = gain[...] * (1.0 + 0.5 * jnp.sin(time * freq[...]))
+                block = (seq ^ m) * hops + lax.rem(rep + hops - hop, hops)
+                chunk = chunks[m * hops + hop] if m < 2 else chunks[2 * hops + hop].at[m - 2]
+                weights[pl.ds(pl.multiple_of(block * w_rows, 16), w_rows)] = chunk[...]
 
     def normalize(relayed):
         total = jnp.zeros((frames, 128), jnp.float32)
@@ -153,23 +197,20 @@
                 if relayed:
                     j = offsets.index(offsets[i] ^ offsets[p])
                     blocks.append(relay[(j // part) * pieces + i][j % part])
-                elif step < 2:
-                    at = pl.multiple_of(jnp.minimum(turn, 1) * rows, 128)
-                    blocks.append(first[p][pl.ds(at, rows), lanes])
                 else:
                     blocks.append(second[p][:rows, lanes])
-            hidden = jnp.concatenate(blocks, axis=0).astype(jnp.float32) + jnp.dot(
-                onehot, table[0, :, lanes], preferred_element_type=jnp.float32
-            )
+            hidden = jnp.concatenate(blocks, axis=0).astype(jnp.float32)
+            hidden = hidden + embed[:, lanes].astype(jnp.float32)
             for lane in range(0, cols, 128):
                 piece = hidden[:, lane : lane + 128]
                 total = total + piece * piece
             scaled[:, lanes] = (hidden * mod[:, lanes]).astype(jnp.bfloat16)
             if i == 0:
                 own_hidden[...] = hidden
-        square[...] = total
+        scales[...] = total
 
     if has_relay:
+        mod[...] = modulation(step, turns, times, gain, freq)
 
         @pl.when(section == 0)
         def _():
@@ -178,12 +219,17 @@
         @pl.when(section != 0)
         def _():
             normalize(True)
+
+        mean = jnp.sum(scales[...], axis=1, keepdims=True) * (1.0 / width)
+        scale = lax.rsqrt(mean + epsilon)
     else:
-        normalize(False)
-    mean = jnp.sum(square[...], axis=1, keepdims=True) * (1.0 / width)
-    scale = lax.rsqrt(mean + epsilon)
-    for copy in w_copies:
-        copy.wait()
+        scale = scales[:, :1]
+
+    def flag_of(i):
+        lanes = pl.ds(pl.multiple_of((seq ^ offsets[i]) * rows, 128), rows)
+        return None, flags[batch, :, lanes].astype(jnp.float32)
+
+    flag_column = columns_of(flag_of, pieces, rows)[:, 16:17]
     projected = jnp.dot(scaled[...], weights[...], preferred_element_type=jnp.float32) * scale
     score_scale = head ** (-0.5) * math.log2(math.e)
     proj[:, :cols] = (projected[:, :cols] * score_scale).astype(jnp.bfloat16)
@@ -231,7 +277,7 @@
         outs[k][...] = blocks[k * part : (k + 1) * part]
 
 
-def tie_kernel(count, *refs):
+def tie_kernel(*refs):
     pass
 
 
@@ -372,49 +418,82 @@
             **options,
         )(*operands)
 
-    block = shape((w_rows, 2 * cols), kind)
-    pair = shape((2, w_rows, 2 * cols), kind)
+    def pin(value, space=pltpu.VMEM):
+        return pltpu.with_memory_space_constraint(value, space)
+
     packed = call(
         pack_kernel,
         "pack",
-        [pair] + [block] * (seq_count - 1),
+        [pltpu.VMEM((w_rows, 2 * cols), kind)] * seq_count,
+        [anywhere, anywhere],
+        [pin(w_query, pltpu.HBM), pin(w_keyval, pltpu.HBM)],
+        [pltpu.SemaphoreType.DMA((2 * seq_count,))],
+        out_specs=[vmem] * seq_count,
+    )
+    blocks = [packed[0]] + [swap(packed[m], m) for m in range(1, seq_count)]
+    far = call(
+        stack_kernel,
+        "far",
+        pltpu.VMEM((2, w_rows, 2 * cols), kind),
         [vmem, vmem],
-        [w_query, w_keyval],
-        out_specs=[vmem] * seq_count,
-    )
-    blocks = [swap(packed[m], m) for m in range(1, seq_count)]
-    near = call(
-        pair_kernel, "near", pair, [vmem, vmem], [packed[0], blocks[0]], out_specs=vmem
-    )
-    far = call(
-        stack_kernel, "far", pair, [anywhere, vmem, vmem], [near] + blocks[1:], out_specs=vmem
-    )
-    rings = [[near], [far]]
+        blocks[2:],
+        out_specs=vmem,
+    )
+    rings = [[blocks[0]], [blocks[1]], [far]]
     for hop in range(1, hops):
         for ring in rings:
             ring.append(shifted(ring[-1], "dp", 1))
 
+    def tie(values, deps):
+        return call(
+            tie_kernel,
+            "tie",
+            [shape(value.shape, kind) for value in values],
+            [anywhere] * (len(values) + len(deps)),
+            list(values) + list(deps),
+            out_specs=[anywhere] * len(values),
+            input_output_aliases={i: i for i in range(len(values))},
+        )
+
     mine = call(
         functools.partial(first_kernel, turns),
         "first",
-        shape((2 * rows + 16, width), kind),
-        [anywhere, vmem, vmem],
-        [far, incoming, contacts],
+        pltpu.VMEM((2 * rows + 16, width), kind),
+        [anywhere] * 3 + [vmem, vmem],
+        [rings[0][1], rings[1][1], far, incoming, contacts],
         [pltpu.VMEM((16, 128), jnp.float32)],
         out_specs=vmem,
     )
     across = swap(mine, 2)
-    first = [mine, across, swap(mine, 1), swap(across, 1)]
+    beside = swap(mine, 1)
+    (across,) = tie([across], [ring[-2] for ring in rings])
+    first = [mine, across, beside, swap(across, 1)]
     mine = call(
         second_kernel,
         "second",
-        shape((2 * rows, width), kind),
+        pltpu.VMEM((2 * rows, width), kind),
         [anywhere, vmem, vmem],
         [across, incoming, head_cotangent],
         out_specs=vmem,
     )
     across = swap(mine, 2)
     second = [mine, across, swap(mine, 1), swap(across, 1)]
+
+    prepared = call(
+        functools.partial(norm_kernel, turns, seq_count),
+        "norm",
+        [pltpu.VMEM((frames, width), kind)] * 2
+        + [pltpu.VMEM((frames, 128), jnp.float32)] * 2
+        + [pltpu.VMEM((frames, cols), jnp.float32)] * 2
+        + [pltpu.VMEM((frames, width), kind)] * 2,
+        [smem] + [vmem] * (3 + seq_count) + [anywhere],
+        [timesteps, contact_table, norm_gain, time_freq]
+        + [pin(piece) for piece in first]
+        + [rings[0][-1]],
+        [pltpu.VMEM((1, width), jnp.float32)],
+        8,
+        out_specs=[vmem] * 8,
+    )
 
     outputs = []
     relayed = {}
@@ -423,7 +502,6 @@
         cfg = {
             "step": step,
             "has_relay": step in relayed,
-            "first_step": step == 0,
             "pieces": seq_count,
             "hops": hops,
             "head": head,
@@ -432,31 +510,34 @@
             "turns": turns,
             "halves": HALVES,
         }
-        operands = [key_bias, timesteps, contact_table, norm_gain, time_freq, attn_gate, keyframes]
-        operands += first
-        if step >= 2:
-            operands += second
-        operands += rings[0] + rings[1] if step == 0 else [weights]
-        operands += relayed.get(step, [])
-        out_shape = [shape((part, rows, cols), kind)] * HALVES
+        operands = [key_bias, timesteps, norm_gain, time_freq, attn_gate, keyframes]
+        scratch = [
+            pltpu.VMEM((frames, 2 * cols + 128), kind),
+            pltpu.VMEM((frames, cols), jnp.float32),
+        ]
+        if step in relayed:
+            large = second + [prepared[4 + step]] + relayed[step]
+            scratch += [
+                pltpu.VMEM((frames, width), kind),
+                pltpu.VMEM((frames, 128), jnp.float32),
+                pltpu.VMEM((frames, cols), jnp.float32),
+                pltpu.VMEM((1, width), jnp.float32),
+            ]
+        else:
+            large = [prepared[step], prepared[2 + step], prepared[4 + step]]
+        large += rings[0] + rings[1] + rings[2] if step == 0 else [weights]
+        operands += [pin(value) for value in large]
+        out_shape = [pltpu.VMEM((part, rows, cols), kind)] * HALVES
         if step == 0:
-            out_shape += [shape((width, 2 * cols), kind)]
+            out_shape += [pltpu.VMEM((width, 2 * cols), kind)]
         results = call(
             functools.partial(step_kernel, cfg),
             "step%d" % step,
             out_shape,
             [smem, smem] + [vmem] * (len(operands) - 2),
             operands,
-            [
-                pltpu.VMEM((frames, width), kind),
-                pltpu.VMEM((1, width), jnp.float32),
-                pltpu.VMEM((frames, 128), jnp.float32),
-                pltpu.VMEM((frames, cols), jnp.float32),
-                pltpu.VMEM((frames, 2 * cols + 128), kind),
-                pltpu.VMEM((frames, cols), jnp.float32),
-                pltpu.SemaphoreType.DMA((4 * hops,)),
-            ],
-            20,
+            scratch,
+            16,
             2 * frames * width * 2 * cols + 4 * heads * frames * frames * head,
             out_specs=[vmem] * len(out_shape),
         )
@@ -465,15 +546,7 @@
             weights = results[HALVES]
         if step == 2:
             pending = [piece for k in range(HALVES) for piece in (crossing[k][0], crossing[k][1])]
-            tied = call(
-                functools.partial(tie_kernel, len(pending)),
-                "tie",
-                [shape(piece.shape, kind) for piece in pending],
-                [anywhere] * (len(pending) + 1),
-                pending + [outputs[-1][0]],
-                out_specs=[anywhere] * len(pending),
-                input_output_aliases={i: i for i in range(len(pending))},
-            )
+            tied = tie(pending, [outputs[-1][0]])
             relayed[3] = []
             for k in range(HALVES):
                 mine, across = tied[2 * k], tied[2 * k + 1]

time: 148 us -> 139 us (0.939)
  Pallas kernels: 35.2 us -> 30.9 us
  starting transfers between devices: 30.9 us -> 27.4 us
  local copies, waits for them, and re-layouts: 9.69 us -> 6.36 us
  waiting for transfers between devices: 70 us -> 73 us
    ppermute x9 -> x12, waiting for transfers between devices: 35.1 us -> 43.8 us  [shifted(): lax.ppermute(value, axis, [(source, (source + shift) % count) for source...]
    ppermute x27, waiting for transfers between devices: 31.3 us -> 23 us  [swap(): lax.ppermute(value, 'seq', [(source, source ^ bit) for source in range(co...]
    pallas_call x13 -> x14, Pallas kernels: 35.2 us -> 30.9 us  [call(): pl.pallas_call(kernel, out_shape=out_shape, in_specs=in_specs, scratch_sh...]
    ppermute x9 -> x12, starting transfers between devices: 7.97 us -> 4.46 us  [shifted(): lax.ppermute(value, axis, [(source, (source + shift) % count) for source...]
    unnamed x49 -> x59, local copies, waits for them, and re-layouts: 9.69 us -> 6.36 us
    ppermute x4, waiting for transfers between devices: 3.61 us -> 6.16 us  [passed_along(): lax.ppermute(value, axis, [(source, source + steps) for source in range(f...]
  transfers between devices with their start and end apart: 40 -> 43, of which waited for: 16 -> 18; matrix products, arithmetic and copies ran while one was open for 0% -> 0% of each run, Pallas kernels for 22% -> 19%
where the time goes in v5:
time: 139 us
  waiting for transfers between devices  73 us (53%)
  Pallas kernels  30.9 us (22%)
  starting transfers between devices  27.4 us (20%)
  local copies, waits for them, and re-layouts  6.36 us (5%)
    ppermute x12, waiting for transfers between devices, shifted(): lax.ppermute(value, axis, [(source, (source + shift) % count) for source...  43.8 us
    pallas_call x14, Pallas kernels, call(): pl.pallas_call(kernel, out_shape=out_shape, in_specs=in_specs, scratch_sh...  30.9 us
    ppermute x27, waiting for transfers between devices, swap(): lax.ppermute(value, 'seq', [(source, source ^ bit) for source in range(co...  23 us
    ppermute x27, starting transfers between devices, swap(): lax.ppermute(value, 'seq', [(source, source ^ bit) for source in range(co...  15.4 us
    ppermute x4, starting transfers between devices, passed_along(): lax.ppermute(value, axis, [(source, source + steps) for source in range(f...  7.52 us
    unnamed x59, local copies, waits for them, and re-layouts  6.36 us
    ppermute x4, waiting for transfers between devices, passed_along(): lax.ppermute(value, axis, [(source, source + steps) for source in range(f...  6.16 us
    ppermute x12, starting transfers between devices, shifted(): lax.ppermute(value, axis, [(source, (source + shift) % count) for source...  4.46 us
  transfers between devices with their start and end apart: 43, of which 18 were waited for; matrix products, arithmetic and copies ran while one was open for 0% of the time, Pallas kernels for 19%

profile of v5, /device:TPU:0, one launch (start us, length us, event | category | flops | bytes accessed | tf_op | source)
XLA Modules:
  0.0 138.9 jit_solution(14665497730940316165)
XLA Ops:
  0.6 1.3 pack.1
  2.0 0.5 collective-permute-start.1
  2.5 2.6 %collective-permute-start.3 = (bf16[96,768]{1,0:T(8,128)(2,1)S(1)}, bf16[96,768]{1,0:T(8,128)(2,1)S(1)}, u32[]{:S(2)}, u32[]{:S(2)}) collective-permute-start(bf16[96,768]{1,0:T(8,128)(2,1)S(1)} %get-tuple-element.45), channel_id=1, source_target_pairs={{0,8},{4,12},{8,0},{12,4},{1,9},{5,13},{9,1},{13,5},{2,10},{6,14},... | collective-permute-start | bytes 442376 | tf_op jit(solution)/shard_map/ppermute | solution.py:27
  5.1 0.1 collective-permute-start.4
  5.1 1.8 %collective-permute-start = (bf16[96,768]{1,0:T(8,128)(2,1)S(1)}, bf16[96,768]{1,0:T(8,128)(2,1)S(1)}, u32[]{:S(2)}, u32[]{:S(2)}) collective-permute-start(bf16[96,768]{1,0:T(8,128)(2,1)S(1)} %get-tuple-element.43.refs_9_), channel_id=1, source_target_pairs={{0,1},{1,2},{2,3},{3,0},{4,5},{5,6},{6,7},{7,4},{8,9},{9,10},{10,1... | collective-permute-start | bytes 442376 | tf_op jit(solution)/shard_map/ppermute | solution.py:32
  6.9 1.6 %collective-permute-start.2 = (bf16[96,768]{1,0:T(8,128)(2,1)S(1)}, bf16[96,768]{1,0:T(8,128)(2,1)S(1)}, u32[]{:S(2)}, u32[]{:S(2)}) collective-permute-start(bf16[96,768]{1,0:T(8,128)(2,1)S(1)} %collective-permute-done.1.refs_13_), channel_id=1, source_target_pairs={{0,1},{1,2},{2,3},{3,0},{4,5},{5,6},{6,7},{7,4},{8,9},{9,10},{10,1... | collective-permute-start | bytes 442376 | tf_op jit(solution)/shard_map/ppermute | solution.py:32
  8.5 1.2 collective-permute-done.3.a
  9.8 2.6 %collective-permute-done.4.b = bf16[96,768]{1,0:T(8,128)(2,1)S(1)} collective-permute-done((bf16[96,768]{1,0:T(8,128)(2,1)S(1)}, bf16[96,768]{1,0:T(8,128)(2,1)S(1)}, u32[]{:S(2)}, u32[]{:S(2)}) %collective-permute-start.4) | collective-permute-done | bytes 147488 | tf_op jit(solution)/shard_map/ppermute | solution.py:27
  12.4 1.2 collective-permute-done.near.refs_10_
  13.7 2.8 %collective-permute-done.2.beside.refs_14_ = bf16[96,768]{1,0:T(8,128)(2,1)S(1)} collective-permute-done((bf16[96,768]{1,0:T(8,128)(2,1)S(1)}, bf16[96,768]{1,0:T(8,128)(2,1)S(1)}, u32[]{:S(2)}, u32[]{:S(2)}) %collective-permute-start.2) | collective-permute-done | bytes 147488 | tf_op jit(solution)/shard_map/ppermute | solution.py:32
  16.5 0.7 copy-done.21
  17.2 0.1 first.1.refs_0_
  17.3 1.6 %collective-permute-start.5 = (bf16[272,1536]{1,0:T(8,128)(2,1)S(1)}, bf16[272,1536]{1,0:T(8,128)(2,1)}, u32[]{:S(2)}, u32[]{:S(2)}) collective-permute-start(bf16[272,1536]{1,0:T(8,128)(2,1)S(1)} %first.1.refs_0_), channel_id=1, source_target_pairs={{0,8},{4,12},{8,0},{12,4},{1,9},{5,13},{9,1},{13,5},{2,10},{6,14},... | collective-permute-start | bytes 2506760 | tf_op jit(solution)/shard_map/ppermute | solution.py:27
  18.8 10.0 %collective-permute-done.8.refs_18_ = bf16[2,96,768]{2,1,0:T(8,128)(2,1)S(1)} collective-permute-done((bf16[2,96,768]{2,1,0:T(8,128)(2,1)S(1)}, bf16[2,96,768]{2,1,0:T(8,128)(2,1)S(1)}, u32[]{:S(2)}, u32[]{:S(2)}) %collective-permute-start.8) | collective-permute-done | bytes 294944 | tf_op jit(solution)/shard_map/ppermute | solution.py:32
  28.9 0.7 copy-done.22
  29.6 1.0 collective-permute-start.7
  30.6 12.2 %collective-permute-done.6.refs_1_.refs_11_ = bf16[96,768]{1,0:T(8,128)(2,1)S(1)} collective-permute-done((bf16[96,768]{1,0:T(8,128)(2,1)S(1)}, bf16[96,768]{1,0:T(8,128)(2,1)S(1)}, u32[]{:S(2)}, u32[]{:S(2)}) %collective-permute-start.6) | collective-permute-done | bytes 147488 | tf_op jit(solution)/shard_map/ppermute | solution.py:32
  42.7 1.7 %collective-permute-done.7.refs_2_.refs_15_ = bf16[96,768]{1,0:T(8,128)(2,1)} collective-permute-done((bf16[96,768]{1,0:T(8,128)(2,1)S(1)}, bf16[96,768]{1,0:T(8,128)(2,1)}, u32[]{:S(2)}, u32[]{:S(2)}) %collective-permute-start.7) | collective-permute-done | bytes 147488 | tf_op jit(solution)/shard_map/ppermute | solution.py:32
  44.5 0.1 collective-permute-start.14
  44.6 0.9 collective-permute-start.10
  45.5 0.2 collective-permute-start.11
  45.7 7.9 %collective-permute-done.15.refs_4_.refs_12_ = bf16[96,768]{1,0:T(8,128)(2,1)S(1)} collective-permute-done((bf16[96,768]{1,0:T(8,128)(2,1)S(1)}, bf16[96,768]{1,0:T(8,128)(2,1)S(1)}, u32[]{:S(2)}, u32[]{:S(2)}) %collective-permute-start.15) | collective-permute-done | bytes 147488 | tf_op jit(solution)/shard_map/ppermute | solution.py:32
  53.6 0.7 copy-done.12
  54.3 0.9 copy-done.3
  55.2 9.4 %collective-permute-done.10.refs_7_.refs_5_ = bf16[256,1536]{1,0:T(8,128)(2,1)S(1)} collective-permute-done((bf16[256,1536]{1,0:T(8,128)(2,1)S(1)}, bf16[256,1536]{1,0:T(8,128)(2,1)S(1)}, u32[]{:S(2)}, u32[]{:S(2)}) %collective-permute-start.10) | collective-permute-done | bytes 786464 | tf_op jit(solution)/shard_map/ppermute | solution.py:27
  64.6 0.1 copy.22.times.refs_1_
  64.8 1.1 copy-done.2
  65.9 1.1 copy-done.4
  67.0 0.9 copy-done.13
  68.0 3.8 %norm.1 = (bf16[512,1536]{1,0:T(8,128)(2,1)S(1)}, bf16[512,1536]{1,0:T(8,128)(2,1)S(1)}, f32[512,128]{1,0:T(8,128)S(1)}, f32[512,128]{1,0:T(8,128)S(1)}, f32[512...) custom-call(s32[4,1]{1,0:T(4,128)S(1)} %copy.22.times.refs_1_, ...), custom_call_target="tpu_custom_call" | custom-call | tf_op jit(solution)/shard_map/norm/pallas_call | solution.py:408
  72.0 5.9 %step0.1 = (bf16[2,128,384]{2,1,0:T(8,128)(2,1)S(1)}, bf16[2,128,384]{2,1,0:T(8,128)(2,1)S(1)}, bf16[1536,768]{1,0:T(8,128)(2,1)S(1)}) custom-call(f32[1,16]{1,0:T(1,128)S(1)} %copy-done.20, s32[4,1]{1,0:T(4,128)S(1)} %copy.22.times.refs_1_, f32[1,1536]{1,0:T(1,128)S(1)} %copy-done.15, f32[1,1536]{1,0:T(1,128)S(1)} %copy-done.16, f32[1,1536]{1,0:T(1,128)S(1)} %copy-done.19, ...), custom_call_target="tpu_custom_call" | custom-call | flops 1610612736 | bytes 3145728 | tf_op jit(solution)/shard_map/step0/pallas_call | solution.py:408
  77.9 3.4 %collective-permute-start.18 = (bf16[2,128,384]{2,1,0:T(8,128)(2,1)S(1)}, bf16[2,128,384]{2,1,0:T(8,128)(2,1)S(1)}, u32[]{:S(2)}, u32[]{:S(2)}) collective-permute-start(bf16[2,128,384]{2,1,0:T(8,128)(2,1)S(1)} %get-tuple-element.51.refs_0_), channel_id=1, source_target_pairs={{0,16},{1,17},{2,18},{3,19},{4,20},{5,21},{6,22},{7,23},{8,24},{9,... | collective-permute-start | bytes 589832 | tf_op jit(solution)/shard_map/ppermute | solution.py:17
  81.3 1.3 collective-permute-start.22
  82.6 5.0 %step1.1 = (bf16[2,128,384]{2,1,0:T(8,128)(2,1)S(1)}, bf16[2,128,384]{2,1,0:T(8,128)(2,1)S(1)}) custom-call(f32[1,16]{1,0:T(1,128)S(1)} %copy-done.20, s32[4,1]{1,0:T(4,128)S(1)} %copy.22.times.refs_1_, f32[1,1536]{1,0:T(1,128)S(1)} %copy-done.15, f32[1,1536]{1,0:T(1,128)S(1)} %copy-done.16, f32[1,1536]{1,0:T(1,128)S(1)} %copy-done.19, ...), custom_call_target="tpu_custom_call" | custom-call | flops 1610612736 | bytes 3145728 | tf_op jit(solution)/shard_map/step1/pallas_call | solution.py:408
  87.7 1.3 collective-permute-start.26
  89.0 1.5 %collective-permute-start.28 = (bf16[2,128,384]{2,1,0:T(8,128)(2,1)S(1)}, bf16[2,128,384]{2,1,0:T(8,128)(2,1)S(1)}, u32[]{:S(2)}, u32[]{:S(2)}) collective-permute-start(bf16[2,128,384]{2,1,0:T(8,128)(2,1)S(1)} %get-tuple-element.61.refs_3_), channel_id=1, source_target_pairs={{0,16},{1,17},{2,18},{3,19},{4,20},{5,21},{6,22},{7,23},{8,24},{9,... | collective-permute-start | bytes 589832 | tf_op jit(solution)/shard_map/ppermute | solution.py:17
  90.5 0.6 collective-permute-start.19
  91.1 1.5 %collective-permute-start.23 = (bf16[2,128,384]{2,1,0:T(8,128)(2,1)S(1)}, bf16[2,128,384]{2,1,0:T(8,128)(2,1)S(1)}, u32[]{:S(2)}, u32[]{:S(2)}) collective-permute-start(bf16[2,128,384]{2,1,0:T(8,128)(2,1)S(1)} %collective-permute-done.22.refs_15_), channel_id=1, source_target_pairs={{0,8},{4,12},{8,0},{12,4},{1,9},{5,13},{9,1},{13,5},{2,10},{6,14},... | collective-permute-start | bytes 589832 | tf_op jit(solution)/shard_map/ppermute | solution.py:27
  92.6 2.3 %collective-permute-done.26.refs_0_ = bf16[2,128,384]{2,1,0:T(8,128)(2,1)S(1)} collective-permute-done((bf16[2,128,384]{2,1,0:T(8,128)(2,1)S(1)}, bf16[2,128,384]{2,1,0:T(8,128)(2,1)S(1)}, u32[]{:S(2)}, u32[]{:S(2)}) %collective-permute-start.26) | collective-permute-done | bytes 196640 | tf_op jit(solution)/shard_map/ppermute | solution.py:17
  94.9 3.8 %collective-permute-done.28.refs_2_ = bf16[2,128,384]{2,1,0:T(8,128)(2,1)S(1)} collective-permute-done((bf16[2,128,384]{2,1,0:T(8,128)(2,1)S(1)}, bf16[2,128,384]{2,1,0:T(8,128)(2,1)S(1)}, u32[]{:S(2)}, u32[]{:S(2)}) %collective-permute-start.28) | collective-permute-done | bytes 196640 | tf_op jit(solution)/shard_map/ppermute | solution.py:17
  98.8 0.5 collective-permute-start.21
  99.3 2.5 %collective-permute-done.23.refs_16_ = bf16[2,128,384]{2,1,0:T(8,128)(2,1)S(1)} collective-permute-done((bf16[2,128,384]{2,1,0:T(8,128)(2,1)S(1)}, bf16[2,128,384]{2,1,0:T(8,128)(2,1)S(1)}, u32[]{:S(2)}, u32[]{:S(2)}) %collective-permute-start.23) | collective-permute-done | bytes 196640 | tf_op jit(solution)/shard_map/ppermute | solution.py:27
  101.8 0.5 collective-permute-start.27
  102.3 1.5 %collective-permute-start.29 = (bf16[2,128,384]{2,1,0:T(8,128)(2,1)S(1)}, bf16[2,128,384]{2,1,0:T(8,128)(2,1)S(1)}, u32[]{:S(2)}, u32[]{:S(2)}) collective-permute-start(bf16[2,128,384]{2,1,0:T(8,128)(2,1)S(1)} %collective-permute-done.28.refs_2_), channel_id=1, source_target_pairs={{0,8},{4,12},{8,0},{12,4},{1,9},{5,13},{9,1},{13,5},{2,10},{6,14},... | collective-permute-start | bytes 589832 | tf_op jit(solution)/shard_map/ppermute | solution.py:27
  103.9 5.8 %step2.1 = (bf16[2,128,384]{2,1,0:T(8,128)(2,1)S(1)}, bf16[2,128,384]{2,1,0:T(8,128)(2,1)S(1)}) custom-call(f32[1,16]{1,0:T(1,128)S(1)} %copy-done.20, s32[4,1]{1,0:T(4,128)S(1)} %copy.22.times.refs_1_, f32[1,1536]{1,0:T(1,128)S(1)} %copy-done.15, f32[1,1536]{1,0:T(1,128)S(1)} %copy-done.16, f32[1,1536]{1,0:T(1,128)S(1)} %copy-done.19, ...), custom_call_target="tpu_custom_call" | custom-call | flops 1610612736 | bytes 3145728 | tf_op jit(solution)/shard_map/step2/pallas_call | solution.py:408
  109.7 3.7 %collective-permute-done.29.refs_3_ = bf16[2,128,384]{2,1,0:T(8,128)(2,1)S(1)} collective-permute-done((bf16[2,128,384]{2,1,0:T(8,128)(2,1)S(1)}, bf16[2,128,384]{2,1,0:T(8,128)(2,1)S(1)}, u32[]{:S(2)}, u32[]{:S(2)}) %collective-permute-start.29) | collective-permute-done | bytes 196640 | tf_op jit(solution)/shard_map/ppermute | solution.py:27
  113.3 0.5 collective-permute-start.31
  113.9 0.5 collective-permute-start.33
  114.4 0.5 early.1
  114.8 0.1 collective-permute-start.34
  114.9 0.6 collective-permute-start.35
  115.5 1.3 collective-permute-start.36
  116.8 5.8 %step3.1 = (bf16[2,128,384]{2,1,0:T(8,128)(2,1)S(1)}, bf16[2,128,384]{2,1,0:T(8,128)(2,1)S(1)}) custom-call(f32[1,16]{1,0:T(1,128)S(1)} %copy-done.20, s32[4,1]{1,0:T(4,128)S(1)} %copy.22.times.refs_1_, f32[1,1536]{1,0:T(1,128)S(1)} %copy-done.15, f32[1,1536]{1,0:T(1,128)S(1)} %copy-done.16, f32[1,1536]{1,0:T(1,128)S(1)} %copy-done.19, ...), custom_call_target="tpu_custom_call" | custom-call | flops 1610612736 | bytes 3145728 | tf_op jit(solution)/shard_map/step3/pallas_call | solution.py:408
  122.6 0.1 collective-permute-done.35.refs_10_
  122.7 3.3 %collective-permute-done.36.refs_11_ = bf16[2,128,384]{2,1,0:T(8,128)(2,1)S(1)} collective-permute-done((bf16[2,128,384]{2,1,0:T(8,128)(2,1)S(1)}, bf16[2,128,384]{2,1,0:T(8,128)(2,1)S(1)}, u32[]{:S(2)}, u32[]{:S(2)}) %collective-permute-start.36) | collective-permute-done | bytes 196640 | tf_op jit(solution)/shard_map/ppermute | solution.py:27
  126.0 1.2 settle.1
  127.2 0.1 collective-permute-start.40
  127.3 0.4 collective-permute-start.37
  127.7 0.5 collective-permute-start.38
  128.2 1.0 collective-permute-start.39
  129.2 3.9 %collective-permute-done.40.refs_6_ = bf16[96,256]{1,0:T(8,128)(2,1)S(1)} collective-permute-done((bf16[96,256]{1,0:T(8,128)(2,1)S(1)}, bf16[96,256]{1,0:T(8,128)(2,1)S(1)}, u32[]{:S(2)}, u32[]{:S(2)}) %collective-permute-start.40) | collective-permute-done | bytes 49184 | tf_op jit(solution)/shard_map/ppermute | solution.py:32
  133.2 2.1 %collective-permute-done.41.refs_7_ = bf16[96,256]{1,0:T(8,128)(2,1)S(1)} collective-permute-done((bf16[96,256]{1,0:T(8,128)(2,1)S(1)}, bf16[96,256]{1,0:T(8,128)(2,1)S(1)}, u32[]{:S(2)}, u32[]{:S(2)}) %collective-permute-start.41) | collective-permute-done | bytes 49184 | tf_op jit(solution)/shard_map/ppermute | solution.py:32
  135.3 2.0 %collective-permute-done.42.refs_8_ = bf16[96,256]{1,0:T(8,128)(2,1)S(1)} collective-permute-done((bf16[96,256]{1,0:T(8,128)(2,1)S(1)}, bf16[96,256]{1,0:T(8,128)(2,1)S(1)}, u32[]{:S(2)}, u32[]{:S(2)}) %collective-permute-start.42) | collective-permute-done | bytes 49184 | tf_op jit(solution)/shard_map/ppermute | solution.py:32
  137.3 1.4 %finish.1 = (bf16[3,128,1536]{2,1,0:T(8,128)(2,1)}, f32[96,256]{1,0:T(8,128)}) custom-call(bf16[3,128,1536]{2,1,0:T(8,128)(2,1)} %get-tuple-element.73.refs_0_, bf16[128,384]{1,0:T(8,128)(2,1)S(1)} %get-tuple-element.74.refs_1_, bf16[128,384]{1,0:T(8,128)(2,1)S(1)} %collective-permute-done.37.refs_2_, ...), custom_call_target="tpu_custom_call", output_to_operand_aliasing={{0}: (0, {})} | custom-call | tf_op jit(solution)/shard_map/finish/pallas_call | solution.py:408
  (95 shorter events, 0.3 us)
Async XLA Ops:
  0.6 15.9 %copy-start = (bf16[1,3,1,128,1536]{4,3,2,1,0:T(8,128)(2,1)S(1)}, bf16[1,3,1,128,1536]{4,3,2,1,0:T(8,128)(2,1)}, u32[]{:S(2)}) copy-start(bf16[1,3,1,128,1536]{4,3,2,1,0:T(8,128)(2,1)} %incoming.3) | copy-start | bytes 3538948
  2.0 14.5 %copy-start.24 = (bf16[96,768]{1,0:T(8,128)(2,1)}, bf16[96,768]{1,0:T(8,128)(2,1)S(1)}, u32[]{:S(2)}) copy-start(bf16[96,768]{1,0:T(8,128)(2,1)S(1)} %get-tuple-element.43.refs_9_) | copy-start | bytes 442372
  2.0 5.0 %collective-permute-start.1 = (bf16[96,768]{1,0:T(8,128)(2,1)S(1)}, bf16[96,768]{1,0:T(8,128)(2,1)S(1)}, u32[]{:S(2)}, u32[]{:S(2)}) collective-permute-start(bf16[96,768]{1,0:T(8,128)(2,1)S(1)} %get-tuple-element.44), channel_id=1, source_target_pairs={{0,4},{4,0},{8,12},{12,8},{1,5},{5,1},{9,13},{13,9},{2,6},{6,2},{1... | collective-permute-start | bytes 442376 | tf_op jit(solution)/shard_map/ppermute | solution.py:27
  2.5 7.3 %collective-permute-start.3 = (bf16[96,768]{1,0:T(8,128)(2,1)S(1)}, bf16[96,768]{1,0:T(8,128)(2,1)S(1)}, u32[]{:S(2)}, u32[]{:S(2)}) collective-permute-start(bf16[96,768]{1,0:T(8,128)(2,1)S(1)} %get-tuple-element.45), channel_id=1, source_target_pairs={{0,8},{4,12},{8,0},{12,4},{1,9},{5,13},{9,1},{13,5},{2,10},{6,14},... | collective-permute-start | bytes 442376 | tf_op jit(solution)/shard_map/ppermute | solution.py:27
  5.1 7.3 %collective-permute-start.4 = (bf16[96,768]{1,0:T(8,128)(2,1)S(1)}, bf16[96,768]{1,0:T(8,128)(2,1)S(1)}, u32[]{:S(2)}, u32[]{:S(2)}) collective-permute-start(bf16[96,768]{1,0:T(8,128)(2,1)S(1)} %get-tuple-element.46), channel_id=1, source_target_pairs={{0,12},{4,8},{8,4},{12,0},{1,13},{5,9},{9,5},{13,1},{2,14},{6,10},... | collective-permute-start | bytes 442376 | tf_op jit(solution)/shard_map/ppermute | solution.py:27
  5.1 8.5 %collective-permute-start = (bf16[96,768]{1,0:T(8,128)(2,1)S(1)}, bf16[96,768]{1,0:T(8,128)(2,1)S(1)}, u32[]{:S(2)}, u32[]{:S(2)}) collective-permute-start(bf16[96,768]{1,0:T(8,128)(2,1)S(1)} %get-tuple-element.43.refs_9_), channel_id=1, source_target_pairs={{0,1},{1,2},{2,3},{3,0},{4,5},{5,6},{6,7},{7,4},{8,9},{9,10},{10,1... | collective-permute-start | bytes 442376 | tf_op jit(solution)/shard_map/ppermute | solution.py:32
  6.9 10.3 %copy-start.26 = (bf16[96,768]{1,0:T(8,128)(2,1)}, bf16[96,768]{1,0:T(8,128)(2,1)S(1)}, u32[]{:S(2)}) copy-start(bf16[96,768]{1,0:T(8,128)(2,1)S(1)} %collective-permute-done.1.refs_13_) | copy-start | bytes 442372
  6.9 9.5 %collective-permute-start.2 = (bf16[96,768]{1,0:T(8,128)(2,1)S(1)}, bf16[96,768]{1,0:T(8,128)(2,1)S(1)}, u32[]{:S(2)}, u32[]{:S(2)}) collective-permute-start(bf16[96,768]{1,0:T(8,128)(2,1)S(1)} %collective-permute-done.1.refs_13_), channel_id=1, source_target_pairs={{0,1},{1,2},{2,3},{3,0},{4,5},{5,6},{6,7},{7,4},{8,9},{9,10},{10,1... | collective-permute-start | bytes 442376 | tf_op jit(solution)/shard_map/ppermute | solution.py:32
  13.7 30.8 %copy-start.6 = (bf16[96,768]{1,0:T(8,128)(2,1)}, bf16[96,768]{1,0:T(8,128)(2,1)S(1)}, u32[]{:S(2)}) copy-start(bf16[96,768]{1,0:T(8,128)(2,1)S(1)} %collective-permute-done.near.refs_10_) | copy-start | bytes 442372
  17.2 25.6 %copy-start.8 = (bf16[96,768]{1,0:T(8,128)(2,1)}, bf16[96,768]{1,0:T(8,128)(2,1)S(1)}, u32[]{:S(2)}) copy-start(bf16[96,768]{1,0:T(8,128)(2,1)S(1)} %collective-permute-done.2.beside.refs_14_) | copy-start | bytes 442372
  17.2 27.4 %copy-start.1 = (bf16[272,1536]{1,0:T(8,128)(2,1)}, bf16[272,1536]{1,0:T(8,128)(2,1)S(1)}, u32[]{:S(2)}) copy-start(bf16[272,1536]{1,0:T(8,128)(2,1)S(1)} %first.1.refs_0_) | copy-start | bytes 2506756
  17.3 27.3 %copy-start.5 = (bf16[1,3,1,128,256]{4,3,2,1,0:T(8,128)(2,1)S(1)}, bf16[1,3,1,128,256]{4,3,2,1,0:T(8,128)(2,1)}, u32[]{:S(2)}) copy-start(bf16[1,3,1,128,256]{4,3,2,1,0:T(8,128)(2,1)} %cotangent.1) | copy-start | bytes 589828
  17.3 27.2 %collective-permute-start.5 = (bf16[272,1536]{1,0:T(8,128)(2,1)S(1)}, bf16[272,1536]{1,0:T(8,128)(2,1)}, u32[]{:S(2)}, u32[]{:S(2)}) collective-permute-start(bf16[272,1536]{1,0:T(8,128)(2,1)S(1)} %first.1.refs_0_), channel_id=1, source_target_pairs={{0,8},{4,12},{8,0},{12,4},{1,9},{5,13},{9,1},{13,5},{2,10},{6,14},... | collective-permute-start | bytes 2506760 | tf_op jit(solution)/shard_map/ppermute | solution.py:27
  18.8 10.0 %collective-permute-start.8 = (bf16[2,96,768]{2,1,0:T(8,128)(2,1)S(1)}, bf16[2,96,768]{2,1,0:T(8,128)(2,1)S(1)}, u32[]{:S(2)}, u32[]{:S(2)}) collective-permute-start(bf16[2,96,768]{2,1,0:T(8,128)(2,1)S(1)} %far.1.refs_17_), channel_id=1, source_target_pairs={{0,1},{1,2},{2,3},{3,0},{4,5},{5,6},{6,7},{7,4},{8,9},{9,10},{10,1... | collective-permute-start | bytes 884744 | tf_op jit(solution)/shard_map/ppermute | solution.py:32
  28.9 15.6 %collective-permute-start.9 = (bf16[2,96,768]{2,1,0:T(8,128)(2,1)S(1)}, bf16[2,96,768]{2,1,0:T(8,128)(2,1)}, u32[]{:S(2)}, u32[]{:S(2)}) collective-permute-start(bf16[2,96,768]{2,1,0:T(8,128)(2,1)S(1)} %collective-permute-done.8.refs_18_), channel_id=1, source_target_pairs={{0,1},{1,2},{2,3},{3,0},{4,5},{5,6},{6,7},{7,4},{8,9},{9,10},{10,1... | collective-permute-start | bytes 884744 | tf_op jit(solution)/shard_map/ppermute | solution.py:32
  29.6 13.2 %collective-permute-start.6 = (bf16[96,768]{1,0:T(8,128)(2,1)S(1)}, bf16[96,768]{1,0:T(8,128)(2,1)S(1)}, u32[]{:S(2)}, u32[]{:S(2)}) collective-permute-start(bf16[96,768]{1,0:T(8,128)(2,1)S(1)} %collective-permute-done.near.refs_10_), channel_id=1, source_target_pairs={{0,1},{1,2},{2,3},{3,0},{4,5},{5,6},{6,7},{7,4},{8,9},{9,10},{10,1... | collective-permute-start | bytes 442376 | tf_op jit(solution)/shard_map/ppermute | solution.py:32
  29.6 14.8 %collective-permute-start.7 = (bf16[96,768]{1,0:T(8,128)(2,1)S(1)}, bf16[96,768]{1,0:T(8,128)(2,1)}, u32[]{:S(2)}, u32[]{:S(2)}) collective-permute-start(bf16[96,768]{1,0:T(8,128)(2,1)S(1)} %collective-permute-done.2.beside.refs_14_), channel_id=1, source_target_pairs={{0,1},{1,2},{2,3},{3,0},{4,5},{5,6},{6,7},{7,4},{8,9},{9,10},{10,1... | collective-permute-start | bytes 442376 | tf_op jit(solution)/shard_map/ppermute | solution.py:32
  30.6 23.7 %collective-permute-start.13 = (bf16[272,1536]{1,0:T(8,128)(2,1)S(1)}, bf16[272,1536]{1,0:T(8,128)(2,1)S(1)}, u32[]{:S(2)}, u32[]{:S(2)}) collective-permute-start(bf16[272,1536]{1,0:T(8,128)(2,1)S(1)} %first.1.refs_0_), channel_id=1, source_target_pairs={{0,4},{4,0},{8,12},{12,8},{1,5},{5,1},{9,13},{13,9},{2,6},{6,2},{1... | collective-permute-start | bytes 2506760 | tf_op jit(solution)/shard_map/ppermute | solution.py:27
  44.4 20.2 %copy-start.28 = (s32[4,1]{0,1:T(1,128)S(1)}, s32[4,1]{0,1:T(1,128)}, u32[]{:S(2)}) copy-start(s32[4,1]{0,1:T(1,128)} %param.15) | copy-start | bytes 52
  44.4 20.3 %copy-start.15 = (f32[1,1536]{1,0:T(1,128)S(1)}, f32[1,1536]{1,0:T(1,128)}, u32[]{:S(2)}) copy-start(f32[1,1536]{1,0:T(1,128)} %refs_2_.7) | copy-start | bytes 18436
  44.5 20.3 %copy-start.16 = (f32[1,1536]{1,0:T(1,128)S(1)}, f32[1,1536]{1,0:T(1,128)}, u32[]{:S(2)}) copy-start(f32[1,1536]{1,0:T(1,128)} %refs_3_.7) | copy-start | bytes 18436
  44.5 20.3 %copy-start.17 = (bf16[1,16,1536]{2,1,0:T(8,128)(2,1)S(1)}, bf16[1,16,1536]{2,1,0:T(8,128)(2,1)}, u32[]{:S(2)}) copy-start(bf16[1,16,1536]{2,1,0:T(8,128)(2,1)} %table.1) | copy-start | bytes 147460
  44.5 20.2 %collective-permute-start.14 = (bf16[272,1536]{1,0:T(8,128)(2,1)}, bf16[272,1536]{1,0:T(8,128)(2,1)}, u32[]{:S(2)}, u32[]{:S(2)}) collective-permute-start(bf16[272,1536]{1,0:T(8,128)(2,1)} %tie.2.dep.refs_1_), channel_id=1, source_target_pairs={{0,4},{4,0},{8,12},{12,8},{1,5},{5,1},{9,13},{13,9},{2,6},{6,2},{1... | collective-permute-start | bytes 2506760 | tf_op jit(solution)/shard_map/ppermute | solution.py:27
  44.6 20.0 %collective-permute-start.10 = (bf16[256,1536]{1,0:T(8,128)(2,1)S(1)}, bf16[256,1536]{1,0:T(8,128)(2,1)S(1)}, u32[]{:S(2)}, u32[]{:S(2)}) collective-permute-start(bf16[256,1536]{1,0:T(8,128)(2,1)S(1)} %second.1.refs_6_.refs_4_), channel_id=1, source_target_pairs={{0,8},{4,12},{8,0},{12,4},{1,9},{5,13},{9,1},{13,5},{2,10},{6,14},... | collective-permute-start | bytes 2359304 | tf_op jit(solution)/shard_map/ppermute | solution.py:27
  45.5 43.5 %collective-permute-start.11 = (bf16[256,1536]{1,0:T(8,128)(2,1)S(1)}, bf16[256,1536]{1,0:T(8,128)(2,1)S(1)}, u32[]{:S(2)}, u32[]{:S(2)}) collective-permute-start(bf16[256,1536]{1,0:T(8,128)(2,1)S(1)} %second.1.refs_6_.refs_4_), channel_id=1, source_target_pairs={{0,4},{4,0},{8,12},{12,8},{1,5},{5,1},{9,13},{13,9},{2,6},{6,2},{1... | collective-permute-start | bytes 2359304 | tf_op jit(solution)/shard_map/ppermute | solution.py:27
  45.7 7.9 %collective-permute-start.15 = (bf16[96,768]{1,0:T(8,128)(2,1)S(1)}, bf16[96,768]{1,0:T(8,128)(2,1)S(1)}, u32[]{:S(2)}, u32[]{:S(2)}) collective-permute-start(bf16[96,768]{1,0:T(8,128)(2,1)S(1)} %collective-permute-done.6.refs_1_.refs_11_), channel_id=1, source_target_pairs={{0,1},{1,2},{2,3},{3,0},{4,5},{5,6},{6,7},{7,4},{8,9},{9,10},{10,1... | collective-permute-start | bytes 442376 | tf_op jit(solution)/shard_map/ppermute | solution.py:32
  54.3 17.6 %collective-permute-start.17 = (bf16[2,96,768]{2,1,0:T(8,128)(2,1)}, bf16[2,96,768]{2,1,0:T(8,128)(2,1)}, u32[]{:S(2)}, u32[]{:S(2)}) collective-permute-start(bf16[2,96,768]{2,1,0:T(8,128)(2,1)} %collective-permute-done.9.refs_3_.refs_19_), channel_id=1, source_target_pairs={{0,1},{1,2},{2,3},{3,0},{4,5},{5,6},{6,7},{7,4},{8,9},{9,10},{10,1... | collective-permute-start | bytes 884744 | tf_op jit(solution)/shard_map/ppermute | solution.py:32
  55.2 16.7 %collective-permute-start.16 = (bf16[96,768]{1,0:T(8,128)(2,1)}, bf16[96,768]{1,0:T(8,128)(2,1)}, u32[]{:S(2)}, u32[]{:S(2)}) collective-permute-start(bf16[96,768]{1,0:T(8,128)(2,1)} %collective-permute-done.7.refs_2_.refs_15_), channel_id=1, source_target_pairs={{0,1},{1,2},{2,3},{3,0},{4,5},{5,6},{6,7},{7,4},{8,9},{9,10},{10,1... | collective-permute-start | bytes 442376 | tf_op jit(solution)/shard_map/ppermute | solution.py:32
  64.6 39.2 %collective-permute-start.12 = (bf16[256,1536]{1,0:T(8,128)(2,1)S(1)}, bf16[256,1536]{1,0:T(8,128)(2,1)S(1)}, u32[]{:S(2)}, u32[]{:S(2)}) collective-permute-start(bf16[256,1536]{1,0:T(8,128)(2,1)S(1)} %collective-permute-done.10.refs_7_.refs_5_), channel_id=1, source_target_pairs={{0,4},{4,0},{8,12},{12,8},{1,5},{5,1},{9,13},{13,9},{2,6},{6,2},{1... | collective-permute-start | bytes 2359304 | tf_op jit(solution)/shard_map/ppermute | solution.py:27
  68.0 3.9 %copy-start.7 = (bf16[96,768]{1,0:T(8,128)(2,1)S(1)}, bf16[96,768]{1,0:T(8,128)(2,1)}, u32[]{:S(2)}) copy-start(bf16[96,768]{1,0:T(8,128)(2,1)} %copy-done.6) | copy-start | bytes 442372
  68.0 3.9 %copy-start.9 = (bf16[96,768]{1,0:T(8,128)(2,1)S(1)}, bf16[96,768]{1,0:T(8,128)(2,1)}, u32[]{:S(2)}) copy-start(bf16[96,768]{1,0:T(8,128)(2,1)} %copy-done.8) | copy-start | bytes 442372
  68.0 4.0 %copy-start.11 = (bf16[96,768]{1,0:T(8,128)(2,1)S(1)}, bf16[96,768]{1,0:T(8,128)(2,1)}, u32[]{:S(2)}) copy-start(bf16[96,768]{1,0:T(8,128)(2,1)} %copy-done.10) | copy-start | bytes 442372
  68.0 4.0 %copy-start.14 = (bf16[96,768]{1,0:T(8,128)(2,1)S(1)}, bf16[96,768]{1,0:T(8,128)(2,1)}, u32[]{:S(2)}) copy-start(bf16[96,768]{1,0:T(8,128)(2,1)} %copy-done.12) | copy-start | bytes 442372
  68.0 4.0 %copy-start.18 = (s32[4,1,512]{2,1,0:T(1,128)S(1)}, s32[4,1,512]{2,1,0:T(1,128)}, u32[]{:S(2)}) copy-start(s32[4,1,512]{2,1,0:T(1,128)} %refs_5_.7) | copy-start | bytes 24580
  68.0 4.0 %copy-start.19 = (f32[1,1536]{1,0:T(1,128)S(1)}, f32[1,1536]{1,0:T(1,128)}, u32[]{:S(2)}) copy-start(f32[1,1536]{1,0:T(1,128)} %refs_4_.7) | copy-start | bytes 18436
  68.0 4.0 %copy-start.20 = (f32[1,16]{1,0:T(1,128)S(1)}, f32[1,16]{1,0:T(1,128)}, u32[]{:S(2)}) copy-start(f32[1,16]{1,0:T(1,128)} %refs_0_.7) | copy-start | bytes 196
  68.0 4.0 %copy-start.23 = (bf16[2,96,768]{2,1,0:T(8,128)(2,1)S(1)}, bf16[2,96,768]{2,1,0:T(8,128)(2,1)}, u32[]{:S(2)}) copy-start(bf16[2,96,768]{2,1,0:T(8,128)(2,1)} %copy-done.22) | copy-start | bytes 884740
  68.0 4.0 %copy-start.25 = (bf16[96,768]{1,0:T(8,128)(2,1)S(1)}, bf16[96,768]{1,0:T(8,128)(2,1)}, u32[]{:S(2)}) copy-start(bf16[96,768]{1,0:T(8,128)(2,1)} %copy-done.24) | copy-start | bytes 442372
  68.0 4.0 %copy-start.27 = (bf16[96,768]{1,0:T(8,128)(2,1)S(1)}, bf16[96,768]{1,0:T(8,128)(2,1)}, u32[]{:S(2)}) copy-start(bf16[96,768]{1,0:T(8,128)(2,1)} %copy-done.26) | copy-start | bytes 442372
  77.9 12.6 %collective-permute-start.18 = (bf16[2,128,384]{2,1,0:T(8,128)(2,1)S(1)}, bf16[2,128,384]{2,1,0:T(8,128)(2,1)S(1)}, u32[]{:S(2)}, u32[]{:S(2)}) collective-permute-start(bf16[2,128,384]{2,1,0:T(8,128)(2,1)S(1)} %get-tuple-element.51.refs_0_), channel_id=1, source_target_pairs={{0,16},{1,17},{2,18},{3,19},{4,20},{5,21},{6,22},{7,23},{8,24},{9,... | collective-permute-start | bytes 589832 | tf_op jit(solution)/shard_map/ppermute | solution.py:17
  81.3 9.8 %collective-permute-start.22 = (bf16[2,128,384]{2,1,0:T(8,128)(2,1)S(1)}, bf16[2,128,384]{2,1,0:T(8,128)(2,1)S(1)}, u32[]{:S(2)}, u32[]{:S(2)}) collective-permute-start(bf16[2,128,384]{2,1,0:T(8,128)(2,1)S(1)} %get-tuple-element.52.refs_1_), channel_id=1, source_target_pairs={{0,16},{1,17},{2,18},{3,19},{4,20},{5,21},{6,22},{7,23},{8,24},{9,... | collective-permute-start | bytes 589832 | tf_op jit(solution)/shard_map/ppermute | solution.py:17
  87.7 7.3 %collective-permute-start.26 = (bf16[2,128,384]{2,1,0:T(8,128)(2,1)S(1)}, bf16[2,128,384]{2,1,0:T(8,128)(2,1)S(1)}, u32[]{:S(2)}, u32[]{:S(2)}) collective-permute-start(bf16[2,128,384]{2,1,0:T(8,128)(2,1)S(1)} %get-tuple-element.60.refs_2_), channel_id=1, source_target_pairs={{0,16},{1,17},{2,18},{3,19},{4,20},{5,21},{6,22},{7,23},{8,24},{9,... | collective-permute-start | bytes 589832 | tf_op jit(solution)/shard_map/ppermute | solution.py:17
  89.0 9.8 %collective-permute-start.28 = (bf16[2,128,384]{2,1,0:T(8,128)(2,1)S(1)}, bf16[2,128,384]{2,1,0:T(8,128)(2,1)S(1)}, u32[]{:S(2)}, u32[]{:S(2)}) collective-permute-start(bf16[2,128,384]{2,1,0:T(8,128)(2,1)S(1)} %get-tuple-element.61.refs_3_), channel_id=1, source_target_pairs={{0,16},{1,17},{2,18},{3,19},{4,20},{5,21},{6,22},{7,23},{8,24},{9,... | collective-permute-start | bytes 589832 | tf_op jit(solution)/shard_map/ppermute | solution.py:17
  90.5 8.3 %collective-permute-start.19 = (bf16[2,128,384]{2,1,0:T(8,128)(2,1)S(1)}, bf16[2,128,384]{2,1,0:T(8,128)(2,1)S(1)}, u32[]{:S(2)}, u32[]{:S(2)}) collective-permute-start(bf16[2,128,384]{2,1,0:T(8,128)(2,1)S(1)} %collective-permute-done.18.refs_11_), channel_id=1, source_target_pairs={{0,8},{4,12},{8,0},{12,4},{1,9},{5,13},{9,1},{13,5},{2,10},{6,14},... | collective-permute-start | bytes 589832 | tf_op jit(solution)/shard_map/ppermute | solution.py:27
  91.1 10.7 %collective-permute-start.23 = (bf16[2,128,384]{2,1,0:T(8,128)(2,1)S(1)}, bf16[2,128,384]{2,1,0:T(8,128)(2,1)S(1)}, u32[]{:S(2)}, u32[]{:S(2)}) collective-permute-start(bf16[2,128,384]{2,1,0:T(8,128)(2,1)S(1)} %collective-permute-done.22.refs_15_), channel_id=1, source_target_pairs={{0,8},{4,12},{8,0},{12,4},{1,9},{5,13},{9,1},{13,5},{2,10},{6,14},... | collective-permute-start | bytes 589832 | tf_op jit(solution)/shard_map/ppermute | solution.py:27
  94.9 6.9 %collective-permute-start.20 = (bf16[2,128,384]{2,1,0:T(8,128)(2,1)S(1)}, bf16[2,128,384]{2,1,0:T(8,128)(2,1)S(1)}, u32[]{:S(2)}, u32[]{:S(2)}) collective-permute-start(bf16[2,128,384]{2,1,0:T(8,128)(2,1)S(1)} %collective-permute-done.18.refs_11_), channel_id=1, source_target_pairs={{0,4},{4,0},{8,12},{12,8},{1,5},{5,1},{9,13},{13,9},{2,6},{6,2},{1... | collective-permute-start | bytes 589832 | tf_op jit(solution)/shard_map/ppermute | solution.py:27
  98.8 3.6 %collective-permute-start.24 = (bf16[2,128,384]{2,1,0:T(8,128)(2,1)S(1)}, bf16[2,128,384]{2,1,0:T(8,128)(2,1)S(1)}, u32[]{:S(2)}, u32[]{:S(2)}) collective-permute-start(bf16[2,128,384]{2,1,0:T(8,128)(2,1)S(1)} %collective-permute-done.22.refs_15_), channel_id=1, source_target_pairs={{0,4},{4,0},{8,12},{12,8},{1,5},{5,1},{9,13},{13,9},{2,6},{6,2},{1... | collective-permute-start | bytes 589832 | tf_op jit(solution)/shard_map/ppermute | solution.py:27
  98.8 5.1 %collective-permute-start.21 = (bf16[2,128,384]{2,1,0:T(8,128)(2,1)S(1)}, bf16[2,128,384]{2,1,0:T(8,128)(2,1)S(1)}, u32[]{:S(2)}, u32[]{:S(2)}) collective-permute-start(bf16[2,128,384]{2,1,0:T(8,128)(2,1)S(1)} %collective-permute-done.19.refs_12_), channel_id=1, source_target_pairs={{0,4},{4,0},{8,12},{12,8},{1,5},{5,1},{9,13},{13,9},{2,6},{6,2},{1... | collective-permute-start | bytes 589832 | tf_op jit(solution)/shard_map/ppermute | solution.py:27
  101.8 2.0 %collective-permute-start.25 = (bf16[2,128,384]{2,1,0:T(8,128)(2,1)S(1)}, bf16[2,128,384]{2,1,0:T(8,128)(2,1)S(1)}, u32[]{:S(2)}, u32[]{:S(2)}) collective-permute-start(bf16[2,128,384]{2,1,0:T(8,128)(2,1)S(1)} %collective-permute-done.23.refs_16_), channel_id=1, source_target_pairs={{0,4},{4,0},{8,12},{12,8},{1,5},{5,1},{9,13},{13,9},{2,6},{6,2},{1... | collective-permute-start | bytes 589832 | tf_op jit(solution)/shard_map/ppermute | solution.py:27
  101.8 7.8 %collective-permute-start.27 = (bf16[2,128,384]{2,1,0:T(8,128)(2,1)S(1)}, bf16[2,128,384]{2,1,0:T(8,128)(2,1)S(1)}, u32[]{:S(2)}, u32[]{:S(2)}) collective-permute-start(bf16[2,128,384]{2,1,0:T(8,128)(2,1)S(1)} %collective-permute-done.26.refs_0_), channel_id=1, source_target_pairs={{0,8},{4,12},{8,0},{12,4},{1,9},{5,13},{9,1},{13,5},{2,10},{6,14},... | collective-permute-start | bytes 589832 | tf_op jit(solution)/shard_map/ppermute | solution.py:27
  102.3 11.0 %collective-permute-start.29 = (bf16[2,128,384]{2,1,0:T(8,128)(2,1)S(1)}, bf16[2,128,384]{2,1,0:T(8,128)(2,1)S(1)}, u32[]{:S(2)}, u32[]{:S(2)}) collective-permute-start(bf16[2,128,384]{2,1,0:T(8,128)(2,1)S(1)} %collective-permute-done.28.refs_2_), channel_id=1, source_target_pairs={{0,8},{4,12},{8,0},{12,4},{1,9},{5,13},{9,1},{13,5},{2,10},{6,14},... | collective-permute-start | bytes 589832 | tf_op jit(solution)/shard_map/ppermute | solution.py:27
  113.3 1.6 %collective-permute-start.30 = (bf16[2,128,384]{2,1,0:T(8,128)(2,1)S(1)}, bf16[2,128,384]{2,1,0:T(8,128)(2,1)S(1)}, u32[]{:S(2)}, u32[]{:S(2)}) collective-permute-start(bf16[2,128,384]{2,1,0:T(8,128)(2,1)S(1)} %get-tuple-element.62.refs_11_), channel_id=1, source_target_pairs={{0,4},{4,0},{8,12},{12,8},{1,5},{5,1},{9,13},{13,9},{2,6},{6,2},{1... | collective-permute-start | bytes 589832 | tf_op jit(solution)/shard_map/ppermute | solution.py:27
  113.3 2.2 %collective-permute-start.31 = (bf16[2,128,384]{2,1,0:T(8,128)(2,1)S(1)}, bf16[2,128,384]{2,1,0:T(8,128)(2,1)S(1)}, u32[]{:S(2)}, u32[]{:S(2)}) collective-permute-start(bf16[2,128,384]{2,1,0:T(8,128)(2,1)S(1)} %get-tuple-element.63.refs_12_), channel_id=1, source_target_pairs={{0,4},{4,0},{8,12},{12,8},{1,5},{5,1},{9,13},{13,9},{2,6},{6,2},{1... | collective-permute-start | bytes 589832 | tf_op jit(solution)/shard_map/ppermute | solution.py:27
  113.8 3.0 %collective-permute-start.32 = (bf16[2,128,384]{2,1,0:T(8,128)(2,1)S(1)}, bf16[2,128,384]{2,1,0:T(8,128)(2,1)S(1)}, u32[]{:S(2)}, u32[]{:S(2)}) collective-permute-start(bf16[2,128,384]{2,1,0:T(8,128)(2,1)S(1)} %get-tuple-element.64.refs_15_), channel_id=1, source_target_pairs={{0,4},{4,0},{8,12},{12,8},{1,5},{5,1},{9,13},{13,9},{2,6},{6,2},{1... | collective-permute-start | bytes 589832 | tf_op jit(solution)/shard_map/ppermute | solution.py:27
  113.9 3.0 %collective-permute-start.33 = (bf16[2,128,384]{2,1,0:T(8,128)(2,1)S(1)}, bf16[2,128,384]{2,1,0:T(8,128)(2,1)S(1)}, u32[]{:S(2)}, u32[]{:S(2)}) collective-permute-start(bf16[2,128,384]{2,1,0:T(8,128)(2,1)S(1)} %get-tuple-element.65.refs_16_), channel_id=1, source_target_pairs={{0,4},{4,0},{8,12},{12,8},{1,5},{5,1},{9,13},{13,9},{2,6},{6,2},{1... | collective-permute-start | bytes 589832 | tf_op jit(solution)/shard_map/ppermute | solution.py:27
  114.8 7.7 %collective-permute-start.34 = (bf16[2,128,384]{2,1,0:T(8,128)(2,1)S(1)}, bf16[2,128,384]{2,1,0:T(8,128)(2,1)S(1)}, u32[]{:S(2)}, u32[]{:S(2)}) collective-permute-start(bf16[2,128,384]{2,1,0:T(8,128)(2,1)S(1)} %get-tuple-element.69), channel_id=1, source_target_pairs={{0,4},{4,0},{8,12},{12,8},{1,5},{5,1},{9,13},{13,9},{2,6},{6,2},{1... | collective-permute-start | bytes 589832 | tf_op jit(solution)/shard_map/ppermute | solution.py:27
  114.9 7.8 %collective-permute-start.35 = (bf16[2,128,384]{2,1,0:T(8,128)(2,1)S(1)}, bf16[2,128,384]{2,1,0:T(8,128)(2,1)S(1)}, u32[]{:S(2)}, u32[]{:S(2)}) collective-permute-start(bf16[2,128,384]{2,1,0:T(8,128)(2,1)S(1)} %get-tuple-element.70), channel_id=1, source_target_pairs={{0,8},{4,12},{8,0},{12,4},{1,9},{5,13},{9,1},{13,5},{2,10},{6,14},... | collective-permute-start | bytes 589832 | tf_op jit(solution)/shard_map/ppermute | solution.py:27
  115.5 10.5 %collective-permute-start.36 = (bf16[2,128,384]{2,1,0:T(8,128)(2,1)S(1)}, bf16[2,128,384]{2,1,0:T(8,128)(2,1)S(1)}, u32[]{:S(2)}, u32[]{:S(2)}) collective-permute-start(bf16[2,128,384]{2,1,0:T(8,128)(2,1)S(1)} %get-tuple-element.71), channel_id=1, source_target_pairs={{0,12},{4,8},{8,4},{12,0},{1,13},{5,9},{9,5},{13,1},{2,14},{6,10},... | collective-permute-start | bytes 589832 | tf_op jit(solution)/shard_map/ppermute | solution.py:27
  127.2 5.9 %collective-permute-start.40 = (bf16[96,256]{1,0:T(8,128)(2,1)S(1)}, bf16[96,256]{1,0:T(8,128)(2,1)S(1)}, u32[]{:S(2)}, u32[]{:S(2)}) collective-permute-start(bf16[96,256]{1,0:T(8,128)(2,1)S(1)} %get-tuple-element.79), channel_id=1, source_target_pairs={{0,1},{1,2},{2,3},{3,0},{4,5},{5,6},{6,7},{7,4},{8,9},{9,10},{10,1... | collective-permute-start | bytes 147464 | tf_op jit(solution)/shard_map/ppermute | solution.py:32
  127.3 10.0 %collective-permute-start.37 = (bf16[128,384]{1,0:T(8,128)(2,1)S(1)}, bf16[128,384]{1,0:T(8,128)(2,1)S(1)}, u32[]{:S(2)}, u32[]{:S(2)}) collective-permute-start(bf16[128,384]{1,0:T(8,128)(2,1)S(1)} %get-tuple-element.75), channel_id=1, source_target_pairs={{0,4},{4,0},{8,12},{12,8},{1,5},{5,1},{9,13},{13,9},{2,6},{6,2},{1... | collective-permute-start | bytes 294920 | tf_op jit(solution)/shard_map/ppermute | solution.py:27
  127.7 9.6 %collective-permute-start.38 = (bf16[128,384]{1,0:T(8,128)(2,1)S(1)}, bf16[128,384]{1,0:T(8,128)(2,1)S(1)}, u32[]{:S(2)}, u32[]{:S(2)}) collective-permute-start(bf16[128,384]{1,0:T(8,128)(2,1)S(1)} %get-tuple-element.76), channel_id=1, source_target_pairs={{0,8},{4,12},{8,0},{12,4},{1,9},{5,13},{9,1},{13,5},{2,10},{6,14},... | collective-permute-start | bytes 294920 | tf_op jit(solution)/shard_map/ppermute | solution.py:27
  128.2 9.1 %collective-permute-start.39 = (bf16[128,384]{1,0:T(8,128)(2,1)S(1)}, bf16[128,384]{1,0:T(8,128)(2,1)S(1)}, u32[]{:S(2)}, u32[]{:S(2)}) collective-permute-start(bf16[128,384]{1,0:T(8,128)(2,1)S(1)} %get-tuple-element.77), channel_id=1, source_target_pairs={{0,12},{4,8},{8,4},{12,0},{1,13},{5,9},{9,5},{13,1},{2,14},{6,10},... | collective-permute-start | bytes 294920 | tf_op jit(solution)/shard_map/ppermute | solution.py:27
  129.2 6.1 %collective-permute-start.41 = (bf16[96,256]{1,0:T(8,128)(2,1)S(1)}, bf16[96,256]{1,0:T(8,128)(2,1)S(1)}, u32[]{:S(2)}, u32[]{:S(2)}) collective-permute-start(bf16[96,256]{1,0:T(8,128)(2,1)S(1)} %get-tuple-element.80), channel_id=1, source_target_pairs={{0,2},{1,3},{2,0},{3,1},{4,6},{5,7},{6,4},{7,5},{8,10},{9,11},{10,... | collective-permute-start | bytes 147464 | tf_op jit(solution)/shard_map/ppermute | solution.py:32
  133.2 4.1 %collective-permute-start.42 = (bf16[96,256]{1,0:T(8,128)(2,1)S(1)}, bf16[96,256]{1,0:T(8,128)(2,1)S(1)}, u32[]{:S(2)}, u32[]{:S(2)}) collective-permute-start(bf16[96,256]{1,0:T(8,128)(2,1)S(1)} %get-tuple-element.81), channel_id=1, source_target_pairs={{0,3},{1,0},{2,1},{3,2},{4,7},{5,4},{6,5},{7,6},{8,11},{9,8},{10,9... | collective-permute-start | bytes 147464 | tf_op jit(solution)/shard_map/ppermute | solution.py:32
  (8 other events, 9.2 us)

commit v6 on v5

--- a/solution.py
+++ b/solution.py
@@ -68,12 +68,37 @@
         copy.wait()
 
 
-def stack_kernel(a, b, out):
-    out[0] = a[...]
-    out[1] = b[...]
-
-
-def first_kernel(turns, near, beside, far, incoming, contacts, out, states):
+def stack_kernel(deps, *refs):
+    out = refs[-1]
+    at = 0
+    for ref in refs[deps:-1]:
+        if len(ref.shape) == 2:
+            out[at] = ref[...]
+            at += 1
+        else:
+            out[at : at + ref.shape[0]] = ref[...]
+            at += ref.shape[0]
+
+
+def place_kernel(hop, hops, *refs):
+    weights, parts = refs[-1], refs[:-1]
+    if hop > 0:
+        parts = parts[:-1]
+    place(hop, hops, parts, weights)
+
+
+def place(hop, hops, parts, weights):
+    seq, rep = lax.axis_index("seq"), lax.axis_index("dp")
+    m = 0
+    for part in parts:
+        count, rows = part.shape[:2]
+        for j in range(count):
+            block = (seq ^ m) * hops + lax.rem(rep + hops - hop, hops)
+            weights[pl.ds(pl.multiple_of(block * rows, 16), rows)] = part[j]
+            m += 1
+
+
+def first_kernel(turns, far, incoming, contacts, out, states):
     rows = incoming.shape[3]
     for turn in range(2):
         out[turn * rows : (turn + 1) * rows] = incoming[0, turn, 0]
@@ -111,8 +136,16 @@
 
 
 def norm_kernel(turns, pieces, times, table, gain, freq, *refs):
-    first, refs = refs[:pieces], refs[pieces + 1 :]
+    sources, refs = refs[:pieces], refs[pieces:]
     scaled, scales, owns, embeds, mod = refs[0:2], refs[2:4], refs[4:6], refs[6:8], refs[8]
+    first, sems = refs[9 : 9 + pieces], refs[9 + pieces]
+    copies = [
+        pltpu.make_async_copy(sources[i], first[i], sems.at[i]) for i in range(pieces)
+    ]
+    for copy in copies:
+        copy.start()
+    for copy in copies:
+        copy.wait()
     frames, width = scaled[0].shape
     rows, cols = frames // pieces, owns[0].shape[1]
     seq = lax.axis_index("seq")
@@ -165,8 +198,8 @@
         second, embed, relay = take(pieces), take(1)[0], take(pieces * halves)
     else:
         scaled, scales, own_hidden = take(3)
-    chunks = take(3 * hops) if step == 0 else None
-    weights = None if step == 0 else take(1)[0]
+    chunk = take(1) if step == 0 else None
+    weights = take(1)[0]
     outs = take(halves)
     if step == 0:
         weights = take(1)[0]
@@ -181,12 +214,7 @@
     _, batch = turn_and_batch(step, turns)
 
     if step == 0:
-        w_rows = width // (pieces * hops)
-        for m in range(pieces):
-            for hop in range(hops):
-                block = (seq ^ m) * hops + lax.rem(rep + hops - hop, hops)
-                chunk = chunks[m * hops + hop] if m < 2 else chunks[2 * hops + hop].at[m - 2]
-                weights[pl.ds(pl.multiple_of(block * w_rows, 16), w_rows)] = chunk[...]
+        place(hops - 1, hops, chunk, weights)
 
     def normalize(relayed):
         total = jnp.zeros((frames, 128), jnp.float32)
@@ -367,7 +395,7 @@
     copy.wait()
 
 
-HALVES = 2
+HALVES = 1
 MIB = 1024 * 1024
 
 
@@ -431,18 +459,43 @@
         out_specs=[vmem] * seq_count,
     )
     blocks = [packed[0]] + [swap(packed[m], m) for m in range(1, seq_count)]
-    far = call(
-        stack_kernel,
-        "far",
-        pltpu.VMEM((2, w_rows, 2 * cols), kind),
-        [vmem, vmem],
-        blocks[2:],
-        out_specs=vmem,
-    )
-    rings = [[blocks[0]], [blocks[1]], [far]]
-    for hop in range(1, hops):
-        for ring in rings:
-            ring.append(shifted(ring[-1], "dp", 1))
+
+    def stacked(name, count, deps, values):
+        return call(
+            functools.partial(stack_kernel, len(deps)),
+            name,
+            pltpu.VMEM((count, w_rows, 2 * cols), kind),
+            [anywhere] * len(deps) + [vmem] * len(values),
+            deps + values,
+            out_specs=vmem,
+        )
+
+    weights = None
+
+    def placed(hop, parts):
+        operands = [pin(part) for part in parts] + ([pin(weights)] if hop else [])
+        return call(
+            functools.partial(place_kernel, hop, hops),
+            "place%d" % hop,
+            pltpu.VMEM((width, 2 * cols), kind),
+            [vmem] * len(operands),
+            operands,
+            out_specs=vmem,
+            input_output_aliases={len(parts): 0} if hop else {},
+        )
+
+    near = stacked("near", 2, [], blocks[:2])
+    near_next = shifted(near, "dp", 1)
+    far = stacked("far", 2, [near_next], blocks[2:])
+    far_next = shifted(far, "dp", 1)
+    weights = placed(0, [near, far])
+    chunk = stacked("whole", seq_count, [], [near_next, far_next])
+    weights = placed(1, [chunk])
+    for hop in range(2, hops):
+        chunk = shifted(chunk, "dp", 1)
+        if hop + 1 < hops:
+            weights = placed(hop, [chunk])
+            late_chunk = chunk
 
     def tie(values, deps):
         return call(
@@ -459,26 +512,15 @@
         functools.partial(first_kernel, turns),
         "first",
         pltpu.VMEM((2 * rows + 16, width), kind),
-        [anywhere] * 3 + [vmem, vmem],
-        [rings[0][1], rings[1][1], far, incoming, contacts],
+        [anywhere, vmem, vmem],
+        [far, incoming, contacts],
         [pltpu.VMEM((16, 128), jnp.float32)],
         out_specs=vmem,
     )
     across = swap(mine, 2)
     beside = swap(mine, 1)
-    (across,) = tie([across], [ring[-2] for ring in rings])
+    (across,) = tie([across], [late_chunk])
     first = [mine, across, beside, swap(across, 1)]
-    mine = call(
-        second_kernel,
-        "second",
-        pltpu.VMEM((2 * rows, width), kind),
-        [anywhere, vmem, vmem],
-        [across, incoming, head_cotangent],
-        out_specs=vmem,
-    )
-    across = swap(mine, 2)
-    second = [mine, across, swap(mine, 1), swap(across, 1)]
-
     prepared = call(
         functools.partial(norm_kernel, turns, seq_count),
         "norm",
@@ -486,18 +528,30 @@
         + [pltpu.VMEM((frames, 128), jnp.float32)] * 2
         + [pltpu.VMEM((frames, cols), jnp.float32)] * 2
         + [pltpu.VMEM((frames, width), kind)] * 2,
-        [smem] + [vmem] * (3 + seq_count) + [anywhere],
+        [smem] + [vmem] * 3 + [anywhere] * seq_count,
         [timesteps, contact_table, norm_gain, time_freq]
-        + [pin(piece) for piece in first]
-        + [rings[0][-1]],
-        [pltpu.VMEM((1, width), jnp.float32)],
-        8,
+        + [pin(piece, pltpu.HBM) for piece in first],
+        [pltpu.VMEM((1, width), jnp.float32)]
+        + [pltpu.VMEM((2 * rows + 16, width), kind)] * seq_count
+        + [pltpu.SemaphoreType.DMA((seq_count,))],
+        12,
         out_specs=[vmem] * 8,
     )
+
+    mine = call(
+        second_kernel,
+        "second",
+        pltpu.VMEM((2 * rows, width), kind),
+        [anywhere, vmem, vmem],
+        [prepared[2], incoming, head_cotangent],
+        out_specs=vmem,
+    )
+    across = swap(mine, 2)
+    second = [mine, across, swap(mine, 1), swap(across, 1)]
 
     outputs = []
     relayed = {}
-    weights = None
+    handed = []
     for step in range(steps):
         cfg = {
             "step": step,
@@ -525,7 +579,7 @@
             ]
         else:
             large = [prepared[step], prepared[2 + step], prepared[4 + step]]
-        large += rings[0] + rings[1] + rings[2] if step == 0 else [weights]
+        large += [chunk, weights] if step == 0 else [weights]
         operands += [pin(value) for value in large]
         out_shape = [pltpu.VMEM((part, rows, cols), kind)] * HALVES
         if step == 0:
@@ -540,6 +594,7 @@
             16,
             2 * frames * width * 2 * cols + 4 * heads * frames * frames * head,
             out_specs=[vmem] * len(out_shape),
+            input_output_aliases={len(operands) - 1: HALVES} if step == 0 else {},
         )
         outputs.append(list(results[:HALVES]))
         if step == 0:
@@ -564,12 +619,13 @@
             early, early_grad = list(early[:-1]), early[-1]
             early = [early[0]] + [swap(early[m], m) for m in range(1, seq_count)]
         if step + 2 < steps:
-            pieces = [passed_along(half, "pipe", 1) for half in outputs[-1]]
-            crossing = [(piece, swap(piece, 2)) for piece in pieces]
-            if step == 0:
-                relayed[2] = []
-                for mine, across in crossing:
-                    relayed[2] += [mine, across, swap(mine, 1), swap(across, 1)]
+            handed.append([passed_along(half, "pipe", 1) for half in outputs[-1]])
+        if step == 1:
+            relayed[2] = []
+            for piece in tie(handed[0], [outputs[-1][0]]):
+                across = swap(piece, 2)
+                relayed[2] += [piece, across, swap(piece, 1), swap(across, 1)]
+            crossing = [(piece, swap(piece, 2)) for piece in handed[1]]
 
     g_shape = (cols // hops, feats)
     operands = outputs[-2] + outputs[-1] + second + early + [early_grad]

time: 139 us -> 128 us (0.921)
  local copies, waits for them, and re-layouts: 6.36 us -> 0.97 us
  starting transfers between devices: 27.4 us -> 22.7 us
  waiting for transfers between devices: 73 us -> 70 us
  Pallas kernels: 30.9 us -> 33.1 us
    ppermute x12 -> x7, waiting for transfers between devices: 43.8 us -> 31 us  [shifted(): lax.ppermute(value, axis, [(source, (source + shift) % count) for source...]
    ppermute x27 -> x21, waiting for transfers between devices: 23 us -> 30.8 us  [swap(): lax.ppermute(value, 'seq', [(source, source ^ bit) for source in range(co...]
    unnamed x59 -> x29, local copies, waits for them, and re-layouts: 6.36 us -> 0.97 us
    ppermute x27 -> x21, starting transfers between devices: 15.4 us -> 11.7 us  [swap(): lax.ppermute(value, 'seq', [(source, source ^ bit) for source in range(co...]
    pallas_call x14 -> x20, Pallas kernels: 30.9 us -> 33.1 us  [call(): pl.pallas_call(kernel, out_shape=out_shape, in_specs=in_specs, scratch_sh...]
    ppermute x4 -> x2, waiting for transfers between devices: 6.16 us -> 8.16 us  [passed_along(): lax.ppermute(value, axis, [(source, source + steps) for source in range(f...]
    ppermute x12 -> x7, starting transfers between devices: 4.46 us -> 3.27 us  [shifted(): lax.ppermute(value, axis, [(source, (source + shift) % count) for source...]
    ppermute x4 -> x2, starting transfers between devices: 7.52 us -> 7.68 us  [passed_along(): lax.ppermute(value, axis, [(source, source + steps) for source in range(f...]
  transfers between devices with their start and end apart: 43 -> 30, of which waited for: 18 -> 18; matrix products, arithmetic and copies ran while one was open for 0% -> 0% of each run, Pallas kernels for 19% -> 23%
where the time goes in v6:
time: 128 us
  waiting for transfers between devices  70 us (55%)
  Pallas kernels  33.1 us (26%)
  starting transfers between devices  22.7 us (18%)
    pallas_call x20, Pallas kernels, call(): pl.pallas_call(kernel, out_shape=out_shape, in_specs=in_specs, scratch_sh...  33.1 us
    ppermute x7, waiting for transfers between devices, shifted(): lax.ppermute(value, axis, [(source, (source + shift) % count) for source...  31 us
    ppermute x21, waiting for transfers between devices, swap(): lax.ppermute(value, 'seq', [(source, source ^ bit) for source in range(co...  30.8 us
    ppermute x21, starting transfers between devices, swap(): lax.ppermute(value, 'seq', [(source, source ^ bit) for source in range(co...  11.7 us
    ppermute x2, waiting for transfers between devices, passed_along(): lax.ppermute(value, axis, [(source, source + steps) for source in range(f...  8.16 us
    ppermute x2, starting transfers between devices, passed_along(): lax.ppermute(value, axis, [(source, source + steps) for source in range(f...  7.68 us
    ppermute x7, starting transfers between devices, shifted(): lax.ppermute(value, axis, [(source, (source + shift) % count) for source...  3.27 us
  transfers between devices with their start and end apart: 30, of which 18 were waited for; matrix products, arithmetic and copies ran while one was open for 0% of the time, Pallas kernels for 23%

profile of v6, /device:TPU:0, one launch (start us, length us, event | category | flops | bytes accessed | tf_op | source)
XLA Modules:
  0.0 127.9 jit_solution(1047695532680448327)
XLA Ops:
  0.7 1.3 %pack.1 = (bf16[96,768]{1,0:T(8,128)(2,1)S(1)}, bf16[96,768]{1,0:T(8,128)(2,1)S(1)}, bf16[96,768]{1,0:T(8,128)(2,1)S(1)}, bf16[96,768]{1,0:T(8,128)(2,1)S(1)}) custom-call(bf16[1,96,1536]{2,1,0:T(8,128)(2,1)} %wq.1, bf16[1,96,1536]{2,1,0:T(8,128)(2,1)} %wkv.1), custom_call_target="tpu_custom_call" | custom-call | tf_op jit(solution)/shard_map/pack/pallas_call | solution.py:436
  2.0 0.5 collective-permute-start
  2.5 1.0 collective-permute-done.refs_1_
  3.5 3.0 %collective-permute-start.1 = (bf16[2,96,768]{2,1,0:T(8,128)(2,1)S(1)}, bf16[2,96,768]{2,1,0:T(8,128)(2,1)S(1)}, u32[]{:S(2)}, u32[]{:S(2)}) collective-permute-start(bf16[2,96,768]{2,1,0:T(8,128)(2,1)S(1)} %near.1.refs_0_), channel_id=1, source_target_pairs={{0,1},{1,2},{2,3},{3,0},{4,5},{5,6},{6,7},{7,4},{8,9},{9,10},{10,1... | collective-permute-start | bytes 884744 | tf_op jit(solution)/shard_map/ppermute | solution.py:32
  6.5 1.5 %collective-permute-start.2 = (bf16[96,768]{1,0:T(8,128)(2,1)S(1)}, bf16[96,768]{1,0:T(8,128)(2,1)S(1)}, u32[]{:S(2)}, u32[]{:S(2)}) collective-permute-start(bf16[96,768]{1,0:T(8,128)(2,1)S(1)} %get-tuple-element.36), channel_id=1, source_target_pairs={{0,8},{4,12},{8,0},{12,4},{1,9},{5,13},{9,1},{13,5},{2,10},{6,14},... | collective-permute-start | bytes 442376 | tf_op jit(solution)/shard_map/ppermute | solution.py:27
  8.0 5.2 %collective-permute-done.2.refs_1_ = bf16[96,768]{1,0:T(8,128)(2,1)S(1)} collective-permute-done((bf16[96,768]{1,0:T(8,128)(2,1)S(1)}, bf16[96,768]{1,0:T(8,128)(2,1)S(1)}, u32[]{:S(2)}, u32[]{:S(2)}) %collective-permute-start.2) | collective-permute-done | bytes 147488 | tf_op jit(solution)/shard_map/ppermute | solution.py:27
  13.2 1.1 collective-permute-done.3.refs_2_
  14.3 1.6 %collective-permute-done.1.refs_0_ = bf16[2,96,768]{2,1,0:T(8,128)(2,1)S(1)} collective-permute-done((bf16[2,96,768]{2,1,0:T(8,128)(2,1)S(1)}, bf16[2,96,768]{2,1,0:T(8,128)(2,1)S(1)}, u32[]{:S(2)}, u32[]{:S(2)}) %collective-permute-start.1) | collective-permute-done | bytes 294944 | tf_op jit(solution)/shard_map/ppermute | solution.py:32
  15.9 0.1 collective-permute-start.5
  16.0 0.1 first.1.refs_0_
  16.0 0.0 copy-start.2
  16.0 0.0 copy-start.13
  16.1 0.0 copy-start.6
  16.1 0.0 copy-start.7
  16.1 0.0 copy-start.8
  16.1 1.6 %collective-permute-start.4 = (bf16[272,1536]{1,0:T(8,128)(2,1)S(1)}, bf16[272,1536]{1,0:T(8,128)(2,1)S(1)}, u32[]{:S(2)}, u32[]{:S(2)}) collective-permute-start(bf16[272,1536]{1,0:T(8,128)(2,1)S(1)} %first.1.refs_0_), channel_id=1, source_target_pairs={{0,8},{4,12},{8,0},{12,4},{1,9},{5,13},{9,1},{13,5},{2,10},{6,14},... | collective-permute-start | bytes 2506760 | tf_op jit(solution)/shard_map/ppermute | solution.py:27
  17.6 8.6 %collective-permute-done.5.refs_1_ = bf16[2,96,768]{2,1,0:T(8,128)(2,1)S(1)} collective-permute-done((bf16[2,96,768]{2,1,0:T(8,128)(2,1)S(1)}, bf16[2,96,768]{2,1,0:T(8,128)(2,1)S(1)}, u32[]{:S(2)}, u32[]{:S(2)}) %collective-permute-start.5) | collective-permute-done | bytes 294944 | tf_op jit(solution)/shard_map/ppermute | solution.py:32
  26.3 0.1 collective-permute-start.6
  26.4 0.8 copy-done.3
  27.2 10.0 %collective-permute-done.4.refs_0_ = bf16[272,1536]{1,0:T(8,128)(2,1)S(1)} collective-permute-done((bf16[272,1536]{1,0:T(8,128)(2,1)S(1)}, bf16[272,1536]{1,0:T(8,128)(2,1)S(1)}, u32[]{:S(2)}, u32[]{:S(2)}) %collective-permute-start.4) | collective-permute-done | bytes 835616 | tf_op jit(solution)/shard_map/ppermute | solution.py:27
  37.2 5.1 %collective-permute-done.6.refs_1_.refs_0_ = bf16[4,96,768]{2,1,0:T(8,128)(2,1)} collective-permute-done((bf16[4,96,768]{2,1,0:T(8,128)(2,1)S(1)}, bf16[4,96,768]{2,1,0:T(8,128)(2,1)}, u32[]{:S(2)}, u32[]{:S(2)}) %collective-permute-start.6) | collective-permute-done | bytes 589856 | tf_op jit(solution)/shard_map/ppermute | solution.py:32
  42.3 0.1 collective-permute-start.12
  42.3 0.1 copy.25.times.refs_1_
  42.4 2.3 %collective-permute-done.8.refs_3_ = bf16[272,1536]{1,0:T(8,128)(2,1)} collective-permute-done((bf16[272,1536]{1,0:T(8,128)(2,1)S(1)}, bf16[272,1536]{1,0:T(8,128)(2,1)}, u32[]{:S(2)}, u32[]{:S(2)}) %collective-permute-start.8) | collective-permute-done | bytes 835616 | tf_op jit(solution)/shard_map/ppermute | solution.py:27
  44.8 4.8 %norm.1 = (bf16[512,1536]{1,0:T(8,128)(2,1)S(1)}, bf16[512,1536]{1,0:T(8,128)(2,1)S(1)}, f32[512,128]{1,0:T(8,128)S(1)}, f32[512,128]{1,0:T(8,128)S(1)}, f32[512...) custom-call(s32[4,1]{1,0:T(4,128)S(1)} %copy.25.times.refs_1_, ...), custom_call_target="tpu_custom_call" | custom-call | tf_op jit(solution)/shard_map/norm/pallas_call | solution.py:436
  49.6 1.4 %collective-permute-start.9 = (bf16[256,1536]{1,0:T(8,128)(2,1)S(1)}, bf16[256,1536]{1,0:T(8,128)(2,1)S(1)}, u32[]{:S(2)}, u32[]{:S(2)}) collective-permute-start(bf16[256,1536]{1,0:T(8,128)(2,1)S(1)} %second.1.refs_6_.refs_3_.refs_2_), channel_id=1, source_target_pairs={{0,8},{4,12},{8,0},{12,4},{1,9},{5,13},{9,1},{13,5},{2,10},{6,14},... | collective-permute-start | bytes 2359304 | tf_op jit(solution)/shard_map/ppermute | solution.py:27
  51.0 0.1 place0.1.refs_1_
  51.1 0.1 place1.1.refs_1_
  51.1 0.0 copy-start.9
  51.1 0.0 copy-start.10
  51.2 0.0 copy-start.11
  51.2 1.1 place2.1.refs_10_
  52.3 7.8 %collective-permute-done.12.refs_9_ = bf16[4,96,768]{2,1,0:T(8,128)(2,1)} collective-permute-done((bf16[4,96,768]{2,1,0:T(8,128)(2,1)}, bf16[4,96,768]{2,1,0:T(8,128)(2,1)}, u32[]{:S(2)}, u32[]{:S(2)}) %collective-permute-start.12) | collective-permute-done | bytes 589856 | tf_op jit(solution)/shard_map/ppermute | solution.py:32
  60.1 5.6 %step0.1 = (bf16[4,128,384]{2,1,0:T(8,128)(2,1)S(1)}, bf16[1536,768]{1,0:T(8,128)(2,1)S(1)}) custom-call(f32[1,16]{1,0:T(1,128)S(1)} %copy-done.11, s32[4,1]{1,0:T(4,128)S(1)} %copy.25.times.refs_1_, f32[1,1536]{1,0:T(1,128)S(1)} %copy-done.6, f32[1,1536]{1,0:T(1,128)S(1)} %copy-done.7, f32[1,1536]{1,0:T(1,128)S(1)} %copy-done.10, ...), custom_call_target="tpu_custom_call", output_to_operand_aliasing={{1}: (10, {})} | custom-call | flops 1610612736 | bytes 3145728 | tf_op jit(solution)/shard_map/step0/pallas_call | solution.py:436
  65.7 3.3 %collective-permute-start.13 = (bf16[4,128,384]{2,1,0:T(8,128)(2,1)S(1)}, bf16[4,128,384]{2,1,0:T(8,128)(2,1)S(1)}, u32[]{:S(2)}, u32[]{:S(2)}) collective-permute-start(bf16[4,128,384]{2,1,0:T(8,128)(2,1)S(1)} %get-tuple-element.42.refs_0_), channel_id=1, source_target_pairs={{0,16},{1,17},{2,18},{3,19},{4,20},{5,21},{6,22},{7,23},{8,24},{9,... | collective-permute-start | bytes 1179656 | tf_op jit(solution)/shard_map/ppermute | solution.py:17
  69.0 0.1 collective-permute-start.10
  69.1 5.0 %step1.1.refs_1_ = bf16[4,128,384]{2,1,0:T(8,128)(2,1)S(1)} custom-call(f32[1,16]{1,0:T(1,128)S(1)} %copy-done.11, s32[4,1]{1,0:T(4,128)S(1)} %copy.25.times.refs_1_, f32[1,1536]{1,0:T(1,128)S(1)} %copy-done.6, f32[1,1536]{1,0:T(1,128)S(1)} %copy-done.7, f32[1,1536]{1,0:T(1,128)S(1)} %copy-done.10, s32[4,1,512]{2,1,0:T(1,128)S(1)} %copy-done.9, ...), custom_call_target="tpu_custom_call" | custom-call | flops 1610612736 | bytes 3145728 | tf_op jit(solution)/shard_map/step1/pallas_call | solution.py:436
  74.2 3.0 %collective-permute-done.13.refs_0_ = bf16[4,128,384]{2,1,0:T(8,128)(2,1)S(1)} collective-permute-done((bf16[4,128,384]{2,1,0:T(8,128)(2,1)S(1)}, bf16[4,128,384]{2,1,0:T(8,128)(2,1)S(1)}, u32[]{:S(2)}, u32[]{:S(2)}) %collective-permute-start.13) | collective-permute-done | bytes 393248 | tf_op jit(solution)/shard_map/ppermute | solution.py:17
  77.2 1.5 %collective-permute-start.14 = (bf16[4,128,384]{2,1,0:T(8,128)(2,1)S(1)}, bf16[4,128,384]{2,1,0:T(8,128)(2,1)S(1)}, u32[]{:S(2)}, u32[]{:S(2)}) collective-permute-start(bf16[4,128,384]{2,1,0:T(8,128)(2,1)S(1)} %tie.4.refs_11_), channel_id=1, source_target_pairs={{0,8},{4,12},{8,0},{12,4},{1,9},{5,13},{9,1},{13,5},{2,10},{6,14},... | collective-permute-start | bytes 1179656 | tf_op jit(solution)/shard_map/ppermute | solution.py:27
  78.7 4.4 %collective-permute-start.17 = (bf16[4,128,384]{2,1,0:T(8,128)(2,1)S(1)}, bf16[4,128,384]{2,1,0:T(8,128)(2,1)S(1)}, u32[]{:S(2)}, u32[]{:S(2)}) collective-permute-start(bf16[4,128,384]{2,1,0:T(8,128)(2,1)S(1)} %step1.1.refs_1_), channel_id=1, source_target_pairs={{0,16},{1,17},{2,18},{3,19},{4,20},{5,21},{6,22},{7,23},{8,24},{9,... | collective-permute-start | bytes 1179656 | tf_op jit(solution)/shard_map/ppermute | solution.py:17
  83.1 0.3 collective-permute-start.15
  83.4 3.6 %collective-permute-done.14.refs_12_ = bf16[4,128,384]{2,1,0:T(8,128)(2,1)S(1)} collective-permute-done((bf16[4,128,384]{2,1,0:T(8,128)(2,1)S(1)}, bf16[4,128,384]{2,1,0:T(8,128)(2,1)S(1)}, u32[]{:S(2)}, u32[]{:S(2)}) %collective-permute-start.14) | collective-permute-done | bytes 393248 | tf_op jit(solution)/shard_map/ppermute | solution.py:27
  87.0 5.1 %collective-permute-done.17.refs_0_ = bf16[4,128,384]{2,1,0:T(8,128)(2,1)S(1)} collective-permute-done((bf16[4,128,384]{2,1,0:T(8,128)(2,1)S(1)}, bf16[4,128,384]{2,1,0:T(8,128)(2,1)S(1)}, u32[]{:S(2)}, u32[]{:S(2)}) %collective-permute-start.17) | collective-permute-done | bytes 393248 | tf_op jit(solution)/shard_map/ppermute | solution.py:17
  92.1 0.5 collective-permute-start.18
  92.6 6.0 %step2.1.refs_2_.refs_0_ = bf16[4,128,384]{2,1,0:T(8,128)(2,1)S(1)} custom-call(f32[1,16]{1,0:T(1,128)S(1)} %copy-done.11, s32[4,1]{1,0:T(4,128)S(1)} %copy.25.times.refs_1_, f32[1,1536]{1,0:T(1,128)S(1)} %copy-done.6, f32[1,1536]{1,0:T(1,128)S(1)} %copy-done.7, f32[1,1536]{1,0:T(1,128)S(1)} %copy-done.10, s32[4,1,512]{2,1,0:T(1,128)S(1)} %copy-done.9, ...), custom_call_target="tpu_custom_call" | custom-call | flops 1610612736 | bytes 3145728 | tf_op jit(solution)/shard_map/step2/pallas_call | solution.py:436
  98.6 4.2 %collective-permute-done.18.refs_1_ = bf16[4,128,384]{2,1,0:T(8,128)(2,1)S(1)} collective-permute-done((bf16[4,128,384]{2,1,0:T(8,128)(2,1)S(1)}, bf16[4,128,384]{2,1,0:T(8,128)(2,1)S(1)}, u32[]{:S(2)}, u32[]{:S(2)}) %collective-permute-start.18) | collective-permute-done | bytes 393248 | tf_op jit(solution)/shard_map/ppermute | solution.py:27
  102.8 0.5 collective-permute-start.20
  103.3 0.5 early.1
  103.9 0.1 collective-permute-start.21
  103.9 0.6 collective-permute-start.22
  104.5 1.3 collective-permute-start.23
  105.8 5.8 %step3.1.refs_1_ = bf16[4,128,384]{2,1,0:T(8,128)(2,1)S(1)} custom-call(f32[1,16]{1,0:T(1,128)S(1)} %copy-done.11, s32[4,1]{1,0:T(4,128)S(1)} %copy.25.times.refs_1_, f32[1,1536]{1,0:T(1,128)S(1)} %copy-done.6, f32[1,1536]{1,0:T(1,128)S(1)} %copy-done.7, f32[1,1536]{1,0:T(1,128)S(1)} %copy-done.10, s32[4,1,512]{2,1,0:T(1,128)S(1)} %copy-done.9, ...), custom_call_target="tpu_custom_call" | custom-call | flops 1610612736 | bytes 3145728 | tf_op jit(solution)/shard_map/step3/pallas_call | solution.py:436
  111.6 0.1 collective-permute-done.22.refs_8_
  111.7 3.3 %collective-permute-done.23.refs_9_ = bf16[2,128,384]{2,1,0:T(8,128)(2,1)S(1)} collective-permute-done((bf16[2,128,384]{2,1,0:T(8,128)(2,1)S(1)}, bf16[2,128,384]{2,1,0:T(8,128)(2,1)S(1)}, u32[]{:S(2)}, u32[]{:S(2)}) %collective-permute-start.23) | collective-permute-done | bytes 196640 | tf_op jit(solution)/shard_map/ppermute | solution.py:27
  115.0 1.2 settle.1
  116.3 0.1 collective-permute-start.27
  116.3 0.3 collective-permute-start.24
  116.7 0.5 collective-permute-start.25
  117.2 1.1 collective-permute-start.26
  118.3 0.0 collective-permute-start.28
  118.3 3.9 %collective-permute-done.27.refs_6_ = bf16[96,256]{1,0:T(8,128)(2,1)S(1)} collective-permute-done((bf16[96,256]{1,0:T(8,128)(2,1)S(1)}, bf16[96,256]{1,0:T(8,128)(2,1)S(1)}, u32[]{:S(2)}, u32[]{:S(2)}) %collective-permute-start.27) | collective-permute-done | bytes 49184 | tf_op jit(solution)/shard_map/ppermute | solution.py:32
  122.2 2.1 %collective-permute-done.28.refs_7_ = bf16[96,256]{1,0:T(8,128)(2,1)S(1)} collective-permute-done((bf16[96,256]{1,0:T(8,128)(2,1)S(1)}, bf16[96,256]{1,0:T(8,128)(2,1)S(1)}, u32[]{:S(2)}, u32[]{:S(2)}) %collective-permute-start.28) | collective-permute-done | bytes 49184 | tf_op jit(solution)/shard_map/ppermute | solution.py:32
  124.3 2.0 %collective-permute-done.29.refs_8_ = bf16[96,256]{1,0:T(8,128)(2,1)S(1)} collective-permute-done((bf16[96,256]{1,0:T(8,128)(2,1)S(1)}, bf16[96,256]{1,0:T(8,128)(2,1)S(1)}, u32[]{:S(2)}, u32[]{:S(2)}) %collective-permute-start.29) | collective-permute-done | bytes 49184 | tf_op jit(solution)/shard_map/ppermute | solution.py:32
  126.3 1.5 %finish.1 = (bf16[3,128,1536]{2,1,0:T(8,128)(2,1)}, f32[96,256]{1,0:T(8,128)}) custom-call(bf16[3,128,1536]{2,1,0:T(8,128)(2,1)} %get-tuple-element.55.refs_0_, bf16[128,384]{1,0:T(8,128)(2,1)S(1)} %get-tuple-element.56.refs_1_, bf16[128,384]{1,0:T(8,128)(2,1)S(1)} %collective-permute-done.24.refs_2_, ...), custom_call_target="tpu_custom_call", output_to_operand_aliasing={{0}: (0, {})} | custom-call | tf_op jit(solution)/shard_map/finish/pallas_call | solution.py:436
  (45 shorter events, 0.2 us)
Async XLA Ops:
  0.6 15.3 %copy-start = (bf16[1,3,1,128,1536]{4,3,2,1,0:T(8,128)(2,1)S(1)}, bf16[1,3,1,128,1536]{4,3,2,1,0:T(8,128)(2,1)}, u32[]{:S(2)}) copy-start(bf16[1,3,1,128,1536]{4,3,2,1,0:T(8,128)(2,1)} %incoming.3) | copy-start | bytes 3538948
  0.6 15.3 %copy-start.12 = (s32[4,1,128]{2,1,0:T(1,128)S(1)}, s32[4,1,128]{2,1,0:T(1,128)}, u32[]{:S(2)}) copy-start(s32[4,1,128]{2,1,0:T(1,128)} %contacts.1) | copy-start | bytes 6148
  2.0 1.5 %collective-permute-start = (bf16[96,768]{1,0:T(8,128)(2,1)S(1)}, bf16[96,768]{1,0:T(8,128)(2,1)S(1)}, u32[]{:S(2)}, u32[]{:S(2)}) collective-permute-start(bf16[96,768]{1,0:T(8,128)(2,1)S(1)} %get-tuple-element.35), channel_id=1, source_target_pairs={{0,4},{4,0},{8,12},{12,8},{1,5},{5,1},{9,13},{13,9},{2,6},{6,2},{1... | collective-permute-start | bytes 442376 | tf_op jit(solution)/shard_map/ppermute | solution.py:27
  3.5 12.3 %collective-permute-start.1 = (bf16[2,96,768]{2,1,0:T(8,128)(2,1)S(1)}, bf16[2,96,768]{2,1,0:T(8,128)(2,1)S(1)}, u32[]{:S(2)}, u32[]{:S(2)}) collective-permute-start(bf16[2,96,768]{2,1,0:T(8,128)(2,1)S(1)} %near.1.refs_0_), channel_id=1, source_target_pairs={{0,1},{1,2},{2,3},{3,0},{4,5},{5,6},{6,7},{7,4},{8,9},{9,10},{10,1... | collective-permute-start | bytes 884744 | tf_op jit(solution)/shard_map/ppermute | solution.py:32
  6.5 6.7 %collective-permute-start.2 = (bf16[96,768]{1,0:T(8,128)(2,1)S(1)}, bf16[96,768]{1,0:T(8,128)(2,1)S(1)}, u32[]{:S(2)}, u32[]{:S(2)}) collective-permute-start(bf16[96,768]{1,0:T(8,128)(2,1)S(1)} %get-tuple-element.36), channel_id=1, source_target_pairs={{0,8},{4,12},{8,0},{12,4},{1,9},{5,13},{9,1},{13,5},{2,10},{6,14},... | collective-permute-start | bytes 442376 | tf_op jit(solution)/shard_map/ppermute | solution.py:27
  8.0 6.3 %collective-permute-start.3 = (bf16[96,768]{1,0:T(8,128)(2,1)S(1)}, bf16[96,768]{1,0:T(8,128)(2,1)S(1)}, u32[]{:S(2)}, u32[]{:S(2)}) collective-permute-start(bf16[96,768]{1,0:T(8,128)(2,1)S(1)} %get-tuple-element.37), channel_id=1, source_target_pairs={{0,12},{4,8},{8,4},{12,0},{1,13},{5,9},{9,5},{13,1},{2,14},{6,10},... | collective-permute-start | bytes 442376 | tf_op jit(solution)/shard_map/ppermute | solution.py:27
  15.9 10.4 %collective-permute-start.5 = (bf16[2,96,768]{2,1,0:T(8,128)(2,1)S(1)}, bf16[2,96,768]{2,1,0:T(8,128)(2,1)S(1)}, u32[]{:S(2)}, u32[]{:S(2)}) collective-permute-start(bf16[2,96,768]{2,1,0:T(8,128)(2,1)S(1)} %far.1.refs_1_), channel_id=1, source_target_pairs={{0,1},{1,2},{2,3},{3,0},{4,5},{5,6},{6,7},{7,4},{8,9},{9,10},{10,1... | collective-permute-start | bytes 884744 | tf_op jit(solution)/shard_map/ppermute | solution.py:32
  16.0 26.2 %copy-start.2 = (bf16[272,1536]{1,0:T(8,128)(2,1)}, bf16[272,1536]{1,0:T(8,128)(2,1)S(1)}, u32[]{:S(2)}) copy-start(bf16[272,1536]{1,0:T(8,128)(2,1)S(1)} %first.1.refs_0_) | copy-start | bytes 2506756
  16.0 26.3 %copy-start.13 = (s32[4,1]{0,1:T(1,128)S(1)}, s32[4,1]{0,1:T(1,128)}, u32[]{:S(2)}) copy-start(s32[4,1]{0,1:T(1,128)} %param.15) | copy-start | bytes 52
  16.1 28.7 %copy-start.6 = (f32[1,1536]{1,0:T(1,128)S(1)}, f32[1,1536]{1,0:T(1,128)}, u32[]{:S(2)}) copy-start(f32[1,1536]{1,0:T(1,128)} %refs_2_.7) | copy-start | bytes 18436
  16.1 28.7 %copy-start.7 = (f32[1,1536]{1,0:T(1,128)S(1)}, f32[1,1536]{1,0:T(1,128)}, u32[]{:S(2)}) copy-start(f32[1,1536]{1,0:T(1,128)} %refs_3_.7) | copy-start | bytes 18436
  16.1 28.7 %copy-start.8 = (bf16[1,16,1536]{2,1,0:T(8,128)(2,1)S(1)}, bf16[1,16,1536]{2,1,0:T(8,128)(2,1)}, u32[]{:S(2)}) copy-start(bf16[1,16,1536]{2,1,0:T(8,128)(2,1)} %table.1) | copy-start | bytes 147460
  16.1 21.1 %collective-permute-start.4 = (bf16[272,1536]{1,0:T(8,128)(2,1)S(1)}, bf16[272,1536]{1,0:T(8,128)(2,1)S(1)}, u32[]{:S(2)}, u32[]{:S(2)}) collective-permute-start(bf16[272,1536]{1,0:T(8,128)(2,1)S(1)} %first.1.refs_0_), channel_id=1, source_target_pairs={{0,8},{4,12},{8,0},{12,4},{1,9},{5,13},{9,1},{13,5},{2,10},{6,14},... | collective-permute-start | bytes 2506760 | tf_op jit(solution)/shard_map/ppermute | solution.py:27
  26.3 15.9 %collective-permute-start.6 = (bf16[4,96,768]{2,1,0:T(8,128)(2,1)S(1)}, bf16[4,96,768]{2,1,0:T(8,128)(2,1)}, u32[]{:S(2)}, u32[]{:S(2)}) collective-permute-start(bf16[4,96,768]{2,1,0:T(8,128)(2,1)S(1)} %whole.1.refs_0_), channel_id=1, source_target_pairs={{0,1},{1,2},{2,3},{3,0},{4,5},{5,6},{6,7},{7,4},{8,9},{9,10},{10,1... | collective-permute-start | bytes 1769480 | tf_op jit(solution)/shard_map/ppermute | solution.py:32
  26.4 0.8 copy-start.3
  27.2 15.2 %collective-permute-start.7 = (bf16[272,1536]{1,0:T(8,128)(2,1)S(1)}, bf16[272,1536]{1,0:T(8,128)(2,1)}, u32[]{:S(2)}, u32[]{:S(2)}) collective-permute-start(bf16[272,1536]{1,0:T(8,128)(2,1)S(1)} %first.1.refs_0_), channel_id=1, source_target_pairs={{0,4},{4,0},{8,12},{12,8},{1,5},{5,1},{9,13},{13,9},{2,6},{6,2},{1... | collective-permute-start | bytes 2506760 | tf_op jit(solution)/shard_map/ppermute | solution.py:27
  42.2 2.5 %copy-start.1 = (bf16[272,1536]{1,0:T(8,128)(2,1)}, bf16[272,1536]{1,0:T(8,128)(2,1)S(1)}, u32[]{:S(2)}) copy-start(bf16[272,1536]{1,0:T(8,128)(2,1)S(1)} %tie.3.refs_1_) | copy-start | bytes 2506756
  42.2 2.5 %collective-permute-start.8 = (bf16[272,1536]{1,0:T(8,128)(2,1)S(1)}, bf16[272,1536]{1,0:T(8,128)(2,1)}, u32[]{:S(2)}, u32[]{:S(2)}) collective-permute-start(bf16[272,1536]{1,0:T(8,128)(2,1)S(1)} %tie.3.refs_1_), channel_id=1, source_target_pairs={{0,4},{4,0},{8,12},{12,8},{1,5},{5,1},{9,13},{13,9},{2,6},{6,2},{1... | collective-permute-start | bytes 2506760 | tf_op jit(solution)/shard_map/ppermute | solution.py:27
  42.3 17.8 %collective-permute-start.12 = (bf16[4,96,768]{2,1,0:T(8,128)(2,1)}, bf16[4,96,768]{2,1,0:T(8,128)(2,1)}, u32[]{:S(2)}, u32[]{:S(2)}) collective-permute-start(bf16[4,96,768]{2,1,0:T(8,128)(2,1)} %collective-permute-done.6.refs_1_.refs_0_), channel_id=1, source_target_pairs={{0,1},{1,2},{2,3},{3,0},{4,5},{5,6},{6,7},{7,4},{8,9},{9,10},{10,1... | collective-permute-start | bytes 1769480 | tf_op jit(solution)/shard_map/ppermute | solution.py:32
  42.4 7.1 %copy-start.5 = (bf16[1,3,1,128,256]{4,3,2,1,0:T(8,128)(2,1)S(1)}, bf16[1,3,1,128,256]{4,3,2,1,0:T(8,128)(2,1)}, u32[]{:S(2)}) copy-start(bf16[1,3,1,128,256]{4,3,2,1,0:T(8,128)(2,1)} %cotangent.1) | copy-start | bytes 589828
  49.6 1.5 %copy-start.4 = (bf16[4,96,768]{2,1,0:T(8,128)(2,1)S(1)}, bf16[4,96,768]{2,1,0:T(8,128)(2,1)}, u32[]{:S(2)}) copy-start(bf16[4,96,768]{2,1,0:T(8,128)(2,1)} %copy-done.3) | copy-start | bytes 1769476
  49.6 29.1 %collective-permute-start.9 = (bf16[256,1536]{1,0:T(8,128)(2,1)S(1)}, bf16[256,1536]{1,0:T(8,128)(2,1)S(1)}, u32[]{:S(2)}, u32[]{:S(2)}) collective-permute-start(bf16[256,1536]{1,0:T(8,128)(2,1)S(1)} %second.1.refs_6_.refs_3_.refs_2_), channel_id=1, source_target_pairs={{0,8},{4,12},{8,0},{12,4},{1,9},{5,13},{9,1},{13,5},{2,10},{6,14},... | collective-permute-start | bytes 2359304 | tf_op jit(solution)/shard_map/ppermute | solution.py:27
  51.1 9.0 %copy-start.9 = (s32[4,1,512]{2,1,0:T(1,128)S(1)}, s32[4,1,512]{2,1,0:T(1,128)}, u32[]{:S(2)}) copy-start(s32[4,1,512]{2,1,0:T(1,128)} %refs_5_.7) | copy-start | bytes 24580
  51.1 9.0 %copy-start.10 = (f32[1,1536]{1,0:T(1,128)S(1)}, f32[1,1536]{1,0:T(1,128)}, u32[]{:S(2)}) copy-start(f32[1,1536]{1,0:T(1,128)} %refs_4_.7) | copy-start | bytes 18436
  51.2 9.0 %copy-start.11 = (f32[1,16]{1,0:T(1,128)S(1)}, f32[1,16]{1,0:T(1,128)}, u32[]{:S(2)}) copy-start(f32[1,16]{1,0:T(1,128)} %refs_0_.7) | copy-start | bytes 196
  65.7 11.4 %collective-permute-start.13 = (bf16[4,128,384]{2,1,0:T(8,128)(2,1)S(1)}, bf16[4,128,384]{2,1,0:T(8,128)(2,1)S(1)}, u32[]{:S(2)}, u32[]{:S(2)}) collective-permute-start(bf16[4,128,384]{2,1,0:T(8,128)(2,1)S(1)} %get-tuple-element.42.refs_0_), channel_id=1, source_target_pairs={{0,16},{1,17},{2,18},{3,19},{4,20},{5,21},{6,22},{7,23},{8,24},{9,... | collective-permute-start | bytes 1179656 | tf_op jit(solution)/shard_map/ppermute | solution.py:17
  69.0 23.6 %collective-permute-start.10 = (bf16[256,1536]{1,0:T(8,128)(2,1)S(1)}, bf16[256,1536]{1,0:T(8,128)(2,1)S(1)}, u32[]{:S(2)}, u32[]{:S(2)}) collective-permute-start(bf16[256,1536]{1,0:T(8,128)(2,1)S(1)} %second.1.refs_6_.refs_3_.refs_2_), channel_id=1, source_target_pairs={{0,4},{4,0},{8,12},{12,8},{1,5},{5,1},{9,13},{13,9},{2,6},{6,2},{1... | collective-permute-start | bytes 2359304 | tf_op jit(solution)/shard_map/ppermute | solution.py:27
  77.2 9.8 %collective-permute-start.14 = (bf16[4,128,384]{2,1,0:T(8,128)(2,1)S(1)}, bf16[4,128,384]{2,1,0:T(8,128)(2,1)S(1)}, u32[]{:S(2)}, u32[]{:S(2)}) collective-permute-start(bf16[4,128,384]{2,1,0:T(8,128)(2,1)S(1)} %tie.4.refs_11_), channel_id=1, source_target_pairs={{0,8},{4,12},{8,0},{12,4},{1,9},{5,13},{9,1},{13,5},{2,10},{6,14},... | collective-permute-start | bytes 1179656 | tf_op jit(solution)/shard_map/ppermute | solution.py:27
  78.7 14.0 %collective-permute-start.11 = (bf16[256,1536]{1,0:T(8,128)(2,1)S(1)}, bf16[256,1536]{1,0:T(8,128)(2,1)S(1)}, u32[]{:S(2)}, u32[]{:S(2)}) collective-permute-start(bf16[256,1536]{1,0:T(8,128)(2,1)S(1)} %collective-permute-done.9.refs_7_.refs_4_.refs_3_), channel_id=1, source_target_pairs={{0,4},{4,0},{8,12},{12,8},{1,5},{5,1},{9,13},{13,9},{2,6},{6,2},{1... | collective-permute-start | bytes 2359304 | tf_op jit(solution)/shard_map/ppermute | solution.py:27
  78.7 13.4 %collective-permute-start.17 = (bf16[4,128,384]{2,1,0:T(8,128)(2,1)S(1)}, bf16[4,128,384]{2,1,0:T(8,128)(2,1)S(1)}, u32[]{:S(2)}, u32[]{:S(2)}) collective-permute-start(bf16[4,128,384]{2,1,0:T(8,128)(2,1)S(1)} %step1.1.refs_1_), channel_id=1, source_target_pairs={{0,16},{1,17},{2,18},{3,19},{4,20},{5,21},{6,22},{7,23},{8,24},{9,... | collective-permute-start | bytes 1179656 | tf_op jit(solution)/shard_map/ppermute | solution.py:17
  83.1 9.5 %collective-permute-start.15 = (bf16[4,128,384]{2,1,0:T(8,128)(2,1)S(1)}, bf16[4,128,384]{2,1,0:T(8,128)(2,1)S(1)}, u32[]{:S(2)}, u32[]{:S(2)}) collective-permute-start(bf16[4,128,384]{2,1,0:T(8,128)(2,1)S(1)} %tie.4.refs_11_), channel_id=1, source_target_pairs={{0,4},{4,0},{8,12},{12,8},{1,5},{5,1},{9,13},{13,9},{2,6},{6,2},{1... | collective-permute-start | bytes 1179656 | tf_op jit(solution)/shard_map/ppermute | solution.py:27
  87.0 5.7 %collective-permute-start.16 = (bf16[4,128,384]{2,1,0:T(8,128)(2,1)S(1)}, bf16[4,128,384]{2,1,0:T(8,128)(2,1)S(1)}, u32[]{:S(2)}, u32[]{:S(2)}) collective-permute-start(bf16[4,128,384]{2,1,0:T(8,128)(2,1)S(1)} %collective-permute-done.14.refs_12_), channel_id=1, source_target_pairs={{0,4},{4,0},{8,12},{12,8},{1,5},{5,1},{9,13},{13,9},{2,6},{6,2},{1... | collective-permute-start | bytes 1179656 | tf_op jit(solution)/shard_map/ppermute | solution.py:27
  92.1 10.7 %collective-permute-start.18 = (bf16[4,128,384]{2,1,0:T(8,128)(2,1)S(1)}, bf16[4,128,384]{2,1,0:T(8,128)(2,1)S(1)}, u32[]{:S(2)}, u32[]{:S(2)}) collective-permute-start(bf16[4,128,384]{2,1,0:T(8,128)(2,1)S(1)} %collective-permute-done.17.refs_0_), channel_id=1, source_target_pairs={{0,8},{4,12},{8,0},{12,4},{1,9},{5,13},{9,1},{13,5},{2,10},{6,14},... | collective-permute-start | bytes 1179656 | tf_op jit(solution)/shard_map/ppermute | solution.py:27
  102.8 3.0 %collective-permute-start.19 = (bf16[4,128,384]{2,1,0:T(8,128)(2,1)S(1)}, bf16[4,128,384]{2,1,0:T(8,128)(2,1)S(1)}, u32[]{:S(2)}, u32[]{:S(2)}) collective-permute-start(bf16[4,128,384]{2,1,0:T(8,128)(2,1)S(1)} %get-tuple-element.48.refs_11_), channel_id=1, source_target_pairs={{0,4},{4,0},{8,12},{12,8},{1,5},{5,1},{9,13},{13,9},{2,6},{6,2},{1... | collective-permute-start | bytes 1179656 | tf_op jit(solution)/shard_map/ppermute | solution.py:27
  102.8 3.0 %collective-permute-start.20 = (bf16[4,128,384]{2,1,0:T(8,128)(2,1)S(1)}, bf16[4,128,384]{2,1,0:T(8,128)(2,1)S(1)}, u32[]{:S(2)}, u32[]{:S(2)}) collective-permute-start(bf16[4,128,384]{2,1,0:T(8,128)(2,1)S(1)} %get-tuple-element.49.refs_12_), channel_id=1, source_target_pairs={{0,4},{4,0},{8,12},{12,8},{1,5},{5,1},{9,13},{13,9},{2,6},{6,2},{1... | collective-permute-start | bytes 1179656 | tf_op jit(solution)/shard_map/ppermute | solution.py:27
  103.9 7.7 %collective-permute-start.21 = (bf16[2,128,384]{2,1,0:T(8,128)(2,1)S(1)}, bf16[2,128,384]{2,1,0:T(8,128)(2,1)S(1)}, u32[]{:S(2)}, u32[]{:S(2)}) collective-permute-start(bf16[2,128,384]{2,1,0:T(8,128)(2,1)S(1)} %get-tuple-element.51), channel_id=1, source_target_pairs={{0,4},{4,0},{8,12},{12,8},{1,5},{5,1},{9,13},{13,9},{2,6},{6,2},{1... | collective-permute-start | bytes 589832 | tf_op jit(solution)/shard_map/ppermute | solution.py:27
  103.9 7.8 %collective-permute-start.22 = (bf16[2,128,384]{2,1,0:T(8,128)(2,1)S(1)}, bf16[2,128,384]{2,1,0:T(8,128)(2,1)S(1)}, u32[]{:S(2)}, u32[]{:S(2)}) collective-permute-start(bf16[2,128,384]{2,1,0:T(8,128)(2,1)S(1)} %get-tuple-element.52), channel_id=1, source_target_pairs={{0,8},{4,12},{8,0},{12,4},{1,9},{5,13},{9,1},{13,5},{2,10},{6,14},... | collective-permute-start | bytes 589832 | tf_op jit(solution)/shard_map/ppermute | solution.py:27
  104.5 10.5 %collective-permute-start.23 = (bf16[2,128,384]{2,1,0:T(8,128)(2,1)S(1)}, bf16[2,128,384]{2,1,0:T(8,128)(2,1)S(1)}, u32[]{:S(2)}, u32[]{:S(2)}) collective-permute-start(bf16[2,128,384]{2,1,0:T(8,128)(2,1)S(1)} %get-tuple-element.53), channel_id=1, source_target_pairs={{0,12},{4,8},{8,4},{12,0},{1,13},{5,9},{9,5},{13,1},{2,14},{6,10},... | collective-permute-start | bytes 589832 | tf_op jit(solution)/shard_map/ppermute | solution.py:27
  116.3 5.9 %collective-permute-start.27 = (bf16[96,256]{1,0:T(8,128)(2,1)S(1)}, bf16[96,256]{1,0:T(8,128)(2,1)S(1)}, u32[]{:S(2)}, u32[]{:S(2)}) collective-permute-start(bf16[96,256]{1,0:T(8,128)(2,1)S(1)} %get-tuple-element.61), channel_id=1, source_target_pairs={{0,1},{1,2},{2,3},{3,0},{4,5},{5,6},{6,7},{7,4},{8,9},{9,10},{10,1... | collective-permute-start | bytes 147464 | tf_op jit(solution)/shard_map/ppermute | solution.py:32
  116.3 10.0 %collective-permute-start.24 = (bf16[128,384]{1,0:T(8,128)(2,1)S(1)}, bf16[128,384]{1,0:T(8,128)(2,1)S(1)}, u32[]{:S(2)}, u32[]{:S(2)}) collective-permute-start(bf16[128,384]{1,0:T(8,128)(2,1)S(1)} %get-tuple-element.57), channel_id=1, source_target_pairs={{0,4},{4,0},{8,12},{12,8},{1,5},{5,1},{9,13},{13,9},{2,6},{6,2},{1... | collective-permute-start | bytes 294920 | tf_op jit(solution)/shard_map/ppermute | solution.py:27
  116.7 9.6 %collective-permute-start.25 = (bf16[128,384]{1,0:T(8,128)(2,1)S(1)}, bf16[128,384]{1,0:T(8,128)(2,1)S(1)}, u32[]{:S(2)}, u32[]{:S(2)}) collective-permute-start(bf16[128,384]{1,0:T(8,128)(2,1)S(1)} %get-tuple-element.58), channel_id=1, source_target_pairs={{0,8},{4,12},{8,0},{12,4},{1,9},{5,13},{9,1},{13,5},{2,10},{6,14},... | collective-permute-start | bytes 294920 | tf_op jit(solution)/shard_map/ppermute | solution.py:27
  117.2 9.1 %collective-permute-start.26 = (bf16[128,384]{1,0:T(8,128)(2,1)S(1)}, bf16[128,384]{1,0:T(8,128)(2,1)S(1)}, u32[]{:S(2)}, u32[]{:S(2)}) collective-permute-start(bf16[128,384]{1,0:T(8,128)(2,1)S(1)} %get-tuple-element.59), channel_id=1, source_target_pairs={{0,12},{4,8},{8,4},{12,0},{1,13},{5,9},{9,5},{13,1},{2,14},{6,10},... | collective-permute-start | bytes 294920 | tf_op jit(solution)/shard_map/ppermute | solution.py:27
  118.3 6.1 %collective-permute-start.28 = (bf16[96,256]{1,0:T(8,128)(2,1)S(1)}, bf16[96,256]{1,0:T(8,128)(2,1)S(1)}, u32[]{:S(2)}, u32[]{:S(2)}) collective-permute-start(bf16[96,256]{1,0:T(8,128)(2,1)S(1)} %get-tuple-element.62), channel_id=1, source_target_pairs={{0,2},{1,3},{2,0},{3,1},{4,6},{5,7},{6,4},{7,5},{8,10},{9,11},{10,... | collective-permute-start | bytes 147464 | tf_op jit(solution)/shard_map/ppermute | solution.py:32
  122.2 4.1 %collective-permute-start.29 = (bf16[96,256]{1,0:T(8,128)(2,1)S(1)}, bf16[96,256]{1,0:T(8,128)(2,1)S(1)}, u32[]{:S(2)}, u32[]{:S(2)}) collective-permute-start(bf16[96,256]{1,0:T(8,128)(2,1)S(1)} %get-tuple-element.63), channel_id=1, source_target_pairs={{0,3},{1,0},{2,1},{3,2},{4,7},{5,4},{6,5},{7,6},{8,11},{9,8},{10,9... | collective-permute-start | bytes 147464 | tf_op jit(solution)/shard_map/ppermute | solution.py:32

commit v7 on v6

--- a/solution.py
+++ b/solution.py
@@ -25,6 +25,12 @@
 def swap(value, bit):
     count = lax.axis_size("seq")
     return lax.ppermute(value, "seq", [(source, source ^ bit) for source in range(count)])
+
+
+def swap_within(section, value, bit):
+    count = lax.axis_size("seq")
+    pairs = [(section * count + i, section * count + (i ^ bit)) for i in range(count)]
+    return lax.ppermute(value, ("pipe", "seq"), pairs)
 
 
 def shifted(value, axis, shift):
@@ -136,7 +142,7 @@
 
 
 def norm_kernel(turns, pieces, times, table, gain, freq, *refs):
-    sources, refs = refs[:pieces], refs[pieces:]
+    sources, refs = refs[:pieces], refs[pieces + 1 :]
     scaled, scales, owns, embeds, mod = refs[0:2], refs[2:4], refs[4:6], refs[6:8], refs[8]
     first, sems = refs[9 : 9 + pieces], refs[9 + pieces]
     copies = [
@@ -198,7 +204,7 @@
         second, embed, relay = take(pieces), take(1)[0], take(pieces * halves)
     else:
         scaled, scales, own_hidden = take(3)
-    chunk = take(1) if step == 0 else None
+    chunk = take(2) if step == 0 else None
     weights = take(1)[0]
     outs = take(halves)
     if step == 0:
@@ -395,7 +401,7 @@
     copy.wait()
 
 
-HALVES = 1
+HALVES = 2
 MIB = 1024 * 1024
 
 
@@ -488,14 +494,13 @@
     near_next = shifted(near, "dp", 1)
     far = stacked("far", 2, [near_next], blocks[2:])
     far_next = shifted(far, "dp", 1)
-    weights = placed(0, [near, far])
-    chunk = stacked("whole", seq_count, [], [near_next, far_next])
-    weights = placed(1, [chunk])
-    for hop in range(2, hops):
-        chunk = shifted(chunk, "dp", 1)
-        if hop + 1 < hops:
-            weights = placed(hop, [chunk])
-            late_chunk = chunk
+    rings = [[near, near_next], [far, far_next]]
+    for hop in range(2, hops - 1):
+        for chunks in rings:
+            chunks.append(shifted(chunks[-1], "dp", 1))
+    last_chunk = [shifted(chunks[-1], "dp", 1) for chunks in rings]
+    for hop in range(hops - 1):
+        weights = placed(hop, [chunks[hop] for chunks in rings])
 
     def tie(values, deps):
         return call(
@@ -519,7 +524,7 @@
     )
     across = swap(mine, 2)
     beside = swap(mine, 1)
-    (across,) = tie([across], [late_chunk])
+    (across,) = tie([across], [chunks[-1] for chunks in rings])
     first = [mine, across, beside, swap(across, 1)]
     prepared = call(
         functools.partial(norm_kernel, turns, seq_count),
@@ -528,9 +533,10 @@
         + [pltpu.VMEM((frames, 128), jnp.float32)] * 2
         + [pltpu.VMEM((frames, cols), jnp.float32)] * 2
         + [pltpu.VMEM((frames, width), kind)] * 2,
-        [smem] + [vmem] * 3 + [anywhere] * seq_count,
+        [smem] + [vmem] * 3 + [anywhere] * (seq_count + 1),
         [timesteps, contact_table, norm_gain, time_freq]
-        + [pin(piece, pltpu.HBM) for piece in first],
+        + [pin(piece, pltpu.HBM) for piece in first]
+        + [weights],
         [pltpu.VMEM((1, width), jnp.float32)]
         + [pltpu.VMEM((2 * rows + 16, width), kind)] * seq_count
         + [pltpu.SemaphoreType.DMA((seq_count,))],
@@ -543,15 +549,13 @@
         "second",
         pltpu.VMEM((2 * rows, width), kind),
         [anywhere, vmem, vmem],
-        [prepared[2], incoming, head_cotangent],
+        [across, incoming, head_cotangent],
         out_specs=vmem,
     )
-    across = swap(mine, 2)
-    second = [mine, across, swap(mine, 1), swap(across, 1)]
+    second = [mine, swap(mine, 2), swap(mine, 1)]
 
     outputs = []
     relayed = {}
-    handed = []
     for step in range(steps):
         cfg = {
             "step": step,
@@ -579,7 +583,7 @@
             ]
         else:
             large = [prepared[step], prepared[2 + step], prepared[4 + step]]
-        large += [chunk, weights] if step == 0 else [weights]
+        large += last_chunk + [weights] if step == 0 else [weights]
         operands += [pin(value) for value in large]
         out_shape = [pltpu.VMEM((part, rows, cols), kind)] * HALVES
         if step == 0:
@@ -599,13 +603,15 @@
         outputs.append(list(results[:HALVES]))
         if step == 0:
             weights = results[HALVES]
+            (second[1],) = tie([second[1]], [outputs[-1][0]])
+            second.append(swap(second[1], 1))
         if step == 2:
             pending = [piece for k in range(HALVES) for piece in (crossing[k][0], crossing[k][1])]
             tied = tie(pending, [outputs[-1][0]])
             relayed[3] = []
             for k in range(HALVES):
                 mine, across = tied[2 * k], tied[2 * k + 1]
-                relayed[3] += [mine, across, swap(mine, 1), swap(across, 1)]
+                relayed[3] += [mine, across, swap_within(1, mine, 1), swap_within(1, across, 1)]
             early = call(
                 functools.partial(early_kernel, turns, seq_count, HALVES, feats),
                 "early",
@@ -619,13 +625,23 @@
             early, early_grad = list(early[:-1]), early[-1]
             early = [early[0]] + [swap(early[m], m) for m in range(1, seq_count)]
         if step + 2 < steps:
-            handed.append([passed_along(half, "pipe", 1) for half in outputs[-1]])
-        if step == 1:
-            relayed[2] = []
-            for piece in tie(handed[0], [outputs[-1][0]]):
-                across = swap(piece, 2)
-                relayed[2] += [piece, across, swap(piece, 1), swap(across, 1)]
-            crossing = [(piece, swap(piece, 2)) for piece in handed[1]]
+            crossing = []
+            for k, half in enumerate(outputs[-1]):
+                piece = passed_along(half, "pipe", 1)
+                if step == 1 and k == 1:
+                    across = passed_along(swap_within(0, half, 2), "pipe", 1)
+                else:
+                    across = swap_within(1, piece, 2)
+                crossing.append((piece, across))
+            if step == 0:
+                relayed[2] = []
+                for mine, across in crossing:
+                    relayed[2] += [
+                        mine,
+                        across,
+                        swap_within(1, mine, 1),
+                        swap_within(1, across, 1),
+                    ]
 
     g_shape = (cols // hops, feats)
     operands = outputs[-2] + outputs[-1] + second + early + [early_grad]

time: 128 us -> 137 us (1.070)
  the two profiles are of different devices: /device:TPU:0 before, /device:TPU:4 now
where the time goes in v7:
time: 137 us; the launch traced here: 136 us
  waiting for transfers between devices  50.7 us (37%)
  starting transfers between devices  47.6 us (35%)
  Pallas kernels  32.9 us (24%)
  local copies, waits for them, and re-layouts  3.73 us (3%)
    ppermute x9, waiting for transfers between devices, shifted(): lax.ppermute(value, axis, [(source, (source + shift) % count) for source...  37.1 us
    pallas_call x19, Pallas kernels, call(): pl.pallas_call(kernel, out_shape=out_shape, in_specs=in_specs, scratch_sh...  32.9 us
    ppermute x12, starting transfers between devices, swap_within(): return lax.ppermute(value, ('pipe', 'seq'), pairs)  28.1 us
    ppermute x15, waiting for transfers between devices, swap(): lax.ppermute(value, 'seq', [(source, source ^ bit) for source in range(co...  11.1 us
    ppermute x15, starting transfers between devices, swap(): lax.ppermute(value, 'seq', [(source, source ^ bit) for source in range(co...  7.73 us
    ppermute x5, starting transfers between devices, passed_along(): lax.ppermute(value, axis, [(source, source + steps) for source in range(f...  6.64 us
    ppermute x9, starting transfers between devices, shifted(): lax.ppermute(value, axis, [(source, (source + shift) % count) for source...  5.13 us
    unnamed x39, local copies, waits for them, and re-layouts  3.73 us
  transfers between devices with their start and end apart: 41, of which 17 were waited for; matrix products, arithmetic and copies ran while one was open for 0% of the time, Pallas kernels for 21%

profile of v7, /device:TPU:4, one launch (start us, length us, event | category | flops | bytes accessed | tf_op | source)
XLA Modules:
  0.0 136.3 jit_solution(14751555812358087320)
XLA Ops:
  0.7 1.3 pack.1
  2.0 1.4 collective-permute-done.refs_1_
  3.4 1.6 %collective-permute-start.1 = (bf16[2,96,768]{2,1,0:T(8,128)(2,1)S(1)}, bf16[2,96,768]{2,1,0:T(8,128)(2,1)S(1)}, u32[]{:S(2)}, u32[]{:S(2)}) collective-permute-start(bf16[2,96,768]{2,1,0:T(8,128)(2,1)S(1)} %near.1.refs_0_), channel_id=1, source_target_pairs={{0,1},{1,2},{2,3},{3,0},{4,5},{5,6},{6,7},{7,4},{8,9},{9,10},{10,1... | collective-permute-start | bytes 884744 | tf_op jit(solution)/shard_map/ppermute | solution.py:38
  5.1 0.7 copy-done.3
  5.8 1.5 %collective-permute-start.2 = (bf16[96,768]{1,0:T(8,128)(2,1)S(1)}, bf16[96,768]{1,0:T(8,128)(2,1)S(1)}, u32[]{:S(2)}, u32[]{:S(2)}) collective-permute-start(bf16[96,768]{1,0:T(8,128)(2,1)S(1)} %get-tuple-element.45), channel_id=1, source_target_pairs={{0,8},{4,12},{8,0},{12,4},{1,9},{5,13},{9,1},{13,5},{2,10},{6,14},... | collective-permute-start | bytes 442376 | tf_op jit(solution)/shard_map/ppermute | solution.py:27
  7.3 5.2 %collective-permute-done.2.refs_1_ = bf16[96,768]{1,0:T(8,128)(2,1)S(1)} collective-permute-done((bf16[96,768]{1,0:T(8,128)(2,1)S(1)}, bf16[96,768]{1,0:T(8,128)(2,1)S(1)}, u32[]{:S(2)}, u32[]{:S(2)}) %collective-permute-start.2) | collective-permute-done | bytes 147488 | tf_op jit(solution)/shard_map/ppermute | solution.py:27
  12.5 1.1 collective-permute-done.3.refs_2_
  13.6 0.8 collective-permute-done.1.refs_0_
  14.5 1.6 %collective-permute-start.4 = (bf16[272,1536]{1,0:T(8,128)(2,1)S(1)}, bf16[272,1536]{1,0:T(8,128)(2,1)S(1)}, u32[]{:S(2)}, u32[]{:S(2)}) collective-permute-start(bf16[272,1536]{1,0:T(8,128)(2,1)S(1)} %first.1.refs_0_), channel_id=1, source_target_pairs={{0,8},{4,12},{8,0},{12,4},{1,9},{5,13},{9,1},{13,5},{2,10},{6,14},... | collective-permute-start | bytes 2506760 | tf_op jit(solution)/shard_map/ppermute | solution.py:27
  16.1 0.6 collective-permute-start.6
  16.7 1.6 %collective-permute-start.5 = (bf16[2,96,768]{2,1,0:T(8,128)(2,1)S(1)}, bf16[2,96,768]{2,1,0:T(8,128)(2,1)}, u32[]{:S(2)}, u32[]{:S(2)}) collective-permute-start(bf16[2,96,768]{2,1,0:T(8,128)(2,1)S(1)} %collective-permute-done.1.refs_0_), channel_id=1, source_target_pairs={{0,1},{1,2},{2,3},{3,0},{4,5},{5,6},{6,7},{7,4},{8,9},{9,10},{10,1... | collective-permute-start | bytes 884744 | tf_op jit(solution)/shard_map/ppermute | solution.py:38
  18.3 9.5 %collective-permute-done.6.refs_1_ = bf16[2,96,768]{2,1,0:T(8,128)(2,1)S(1)} collective-permute-done((bf16[2,96,768]{2,1,0:T(8,128)(2,1)S(1)}, bf16[2,96,768]{2,1,0:T(8,128)(2,1)S(1)}, u32[]{:S(2)}, u32[]{:S(2)}) %collective-permute-start.6) | collective-permute-done | bytes 294944 | tf_op jit(solution)/shard_map/ppermute | solution.py:38
  27.8 6.4 %collective-permute-done.5.refs_1_.refs_0_ = bf16[2,96,768]{2,1,0:T(8,128)(2,1)} collective-permute-done((bf16[2,96,768]{2,1,0:T(8,128)(2,1)S(1)}, bf16[2,96,768]{2,1,0:T(8,128)(2,1)}, u32[]{:S(2)}, u32[]{:S(2)}) %collective-permute-start.5) | collective-permute-done | bytes 294944 | tf_op jit(solution)/shard_map/ppermute | solution.py:38
  34.2 5.2 %collective-permute-done.7.refs_2_.refs_1_ = bf16[2,96,768]{2,1,0:T(8,128)(2,1)} collective-permute-done((bf16[2,96,768]{2,1,0:T(8,128)(2,1)S(1)}, bf16[2,96,768]{2,1,0:T(8,128)(2,1)}, u32[]{:S(2)}, u32[]{:S(2)}) %collective-permute-start.7) | collective-permute-done | bytes 294944 | tf_op jit(solution)/shard_map/ppermute | solution.py:38
  39.4 0.1 collective-permute-start.10
  39.6 0.6 collective-permute-start.8
  40.2 1.2 collective-permute-start.12
  41.4 0.9 copy-done.17
  42.3 0.1 copy.26.times.refs_1_
  42.4 1.0 copy-done.4
  43.4 0.9 copy-done.6
  44.3 0.1 copy-done.8
  44.5 1.1 place2.1.refs_4_.refs_11_
  45.7 4.8 %norm.1 = (bf16[512,1536]{1,0:T(8,128)(2,1)S(1)}, bf16[512,1536]{1,0:T(8,128)(2,1)S(1)}, f32[512,128]{1,0:T(8,128)S(1)}, f32[512,128]{1,0:T(8,128)S(1)}, f32[512...) custom-call(s32[4,1]{1,0:T(4,128)S(1)} %copy.26.times.refs_1_, ...), custom_call_target="tpu_custom_call" | custom-call | tf_op jit(solution)/shard_map/norm/pallas_call | solution.py:442
  50.5 1.6 %collective-permute-done.11.refs_9_ = bf16[2,96,768]{2,1,0:T(8,128)(2,1)} collective-permute-done((bf16[2,96,768]{2,1,0:T(8,128)(2,1)}, bf16[2,96,768]{2,1,0:T(8,128)(2,1)}, u32[]{:S(2)}, u32[]{:S(2)}) %collective-permute-start.11) | collective-permute-done | bytes 294944 | tf_op jit(solution)/shard_map/ppermute | solution.py:38
  52.1 5.6 %collective-permute-done.12.refs_10_ = bf16[2,96,768]{2,1,0:T(8,128)(2,1)} collective-permute-done((bf16[2,96,768]{2,1,0:T(8,128)(2,1)}, bf16[2,96,768]{2,1,0:T(8,128)(2,1)}, u32[]{:S(2)}, u32[]{:S(2)}) %collective-permute-start.12) | collective-permute-done | bytes 294944 | tf_op jit(solution)/shard_map/ppermute | solution.py:38
  57.7 5.6 %step0.1 = (bf16[2,128,384]{2,1,0:T(8,128)(2,1)S(1)}, bf16[2,128,384]{2,1,0:T(8,128)(2,1)S(1)}, bf16[1536,768]{1,0:T(8,128)(2,1)S(1)}) custom-call(f32[1,16]{1,0:T(1,128)S(1)} %copy-done.15, s32[4,1]{1,0:T(4,128)S(1)} %copy.26.times.refs_1_, f32[1,1536]{1,0:T(1,128)S(1)} %copy-done.10, f32[1,1536]{1,0:T(1,128)S(1)} %copy-done.11, ...), custom_call_target="tpu_custom_call", output_to_operand_aliasing={{2}: (11, {})} | custom-call | flops 1610612736 | bytes 3145728 | tf_op jit(solution)/shard_map/step0/pallas_call | solution.py:442
  63.4 1.3 collective-permute-start.15
  64.7 1.3 collective-permute-start.19
  66.0 5.0 %step1.1 = (bf16[2,128,384]{2,1,0:T(8,128)(2,1)S(1)}, bf16[2,128,384]{2,1,0:T(8,128)(2,1)S(1)}) custom-call(f32[1,16]{1,0:T(1,128)S(1)} %copy-done.15, s32[4,1]{1,0:T(4,128)S(1)} %copy.26.times.refs_1_, f32[1,1536]{1,0:T(1,128)S(1)} %copy-done.10, f32[1,1536]{1,0:T(1,128)S(1)} %copy-done.11, f32[1,1536]{1,0:T(1,128)S(1)} %copy-done.14, ...), custom_call_target="tpu_custom_call" | custom-call | flops 1610612736 | bytes 3145728 | tf_op jit(solution)/shard_map/step1/pallas_call | solution.py:442
  71.1 1.3 collective-permute-start.23
  72.4 0.7 collective-permute-start.26
  73.1 3.4 %collective-permute-start.16 = (bf16[2,128,384]{2,1,0:T(8,128)(2,1)S(1)}, bf16[2,128,384]{2,1,0:T(8,128)(2,1)S(1)}, u32[]{:S(2)}, u32[]{:S(2)}) collective-permute-start(bf16[2,128,384]{2,1,0:T(8,128)(2,1)S(1)} %collective-permute-done.15.refs_11_), channel_id=1, source_target_pairs={{16,24},{20,28},{24,16},{28,20},{17,25},{21,29},{25,17},{29,21},{1... | collective-permute-start | bytes 589832 | tf_op jit(solution)/shard_map/ppermute | solution.py:33
  76.5 0.7 collective-permute-done.19.refs_15_
  77.2 3.4 %collective-permute-start.20 = (bf16[2,128,384]{2,1,0:T(8,128)(2,1)S(1)}, bf16[2,128,384]{2,1,0:T(8,128)(2,1)S(1)}, u32[]{:S(2)}, u32[]{:S(2)}) collective-permute-start(bf16[2,128,384]{2,1,0:T(8,128)(2,1)S(1)} %collective-permute-done.19.refs_15_), channel_id=1, source_target_pairs={{16,24},{20,28},{24,16},{28,20},{17,25},{21,29},{25,17},{29,21},{1... | collective-permute-start | bytes 589832 | tf_op jit(solution)/shard_map/ppermute | solution.py:33
  80.6 0.4 collective-permute-done.23.refs_0_
  81.0 1.9 %collective-permute-start.17 = (bf16[2,128,384]{2,1,0:T(8,128)(2,1)S(1)}, bf16[2,128,384]{2,1,0:T(8,128)(2,1)S(1)}, u32[]{:S(2)}, u32[]{:S(2)}) collective-permute-start(bf16[2,128,384]{2,1,0:T(8,128)(2,1)S(1)} %collective-permute-done.15.refs_11_), channel_id=1, source_target_pairs={{16,20},{20,16},{24,28},{28,24},{17,21},{21,17},{25,29},{29,25},{1... | collective-permute-start | bytes 589832 | tf_op jit(solution)/shard_map/ppermute | solution.py:33
  83.0 2.4 %collective-permute-start.21 = (bf16[2,128,384]{2,1,0:T(8,128)(2,1)S(1)}, bf16[2,128,384]{2,1,0:T(8,128)(2,1)S(1)}, u32[]{:S(2)}, u32[]{:S(2)}) collective-permute-start(bf16[2,128,384]{2,1,0:T(8,128)(2,1)S(1)} %collective-permute-done.19.refs_15_), channel_id=1, source_target_pairs={{16,20},{20,16},{24,28},{28,24},{17,21},{21,17},{25,29},{29,25},{1... | collective-permute-start | bytes 589832 | tf_op jit(solution)/shard_map/ppermute | solution.py:33
  85.4 1.9 %collective-permute-start.18 = (bf16[2,128,384]{2,1,0:T(8,128)(2,1)S(1)}, bf16[2,128,384]{2,1,0:T(8,128)(2,1)S(1)}, u32[]{:S(2)}, u32[]{:S(2)}) collective-permute-start(bf16[2,128,384]{2,1,0:T(8,128)(2,1)S(1)} %collective-permute-done.16.refs_12_), channel_id=1, source_target_pairs={{16,20},{20,16},{24,28},{28,24},{17,21},{21,17},{25,29},{29,25},{1... | collective-permute-start | bytes 589832 | tf_op jit(solution)/shard_map/ppermute | solution.py:33
  87.3 2.4 %collective-permute-start.22 = (bf16[2,128,384]{2,1,0:T(8,128)(2,1)S(1)}, bf16[2,128,384]{2,1,0:T(8,128)(2,1)S(1)}, u32[]{:S(2)}, u32[]{:S(2)}) collective-permute-start(bf16[2,128,384]{2,1,0:T(8,128)(2,1)S(1)} %collective-permute-done.20.refs_16_), channel_id=1, source_target_pairs={{16,20},{20,16},{24,28},{28,24},{17,21},{21,17},{25,29},{29,25},{1... | collective-permute-start | bytes 589832 | tf_op jit(solution)/shard_map/ppermute | solution.py:33
  89.8 1.5 %collective-permute-start.25 = (bf16[2,128,384]{2,1,0:T(8,128)(2,1)S(1)}, bf16[2,128,384]{2,1,0:T(8,128)(2,1)S(1)}, u32[]{:S(2)}, u32[]{:S(2)}) collective-permute-start(bf16[2,128,384]{2,1,0:T(8,128)(2,1)S(1)} %get-tuple-element.61.refs_3_), channel_id=1, source_target_pairs={{0,16},{1,17},{2,18},{3,19},{4,20},{5,21},{6,22},{7,23},{8,24},{9,... | collective-permute-start | bytes 589832 | tf_op jit(solution)/shard_map/ppermute | solution.py:17
  91.3 3.4 %collective-permute-start.24 = (bf16[2,128,384]{2,1,0:T(8,128)(2,1)S(1)}, bf16[2,128,384]{2,1,0:T(8,128)(2,1)S(1)}, u32[]{:S(2)}, u32[]{:S(2)}) collective-permute-start(bf16[2,128,384]{2,1,0:T(8,128)(2,1)S(1)} %collective-permute-done.23.refs_0_), channel_id=1, source_target_pairs={{16,24},{20,28},{24,16},{28,20},{17,25},{21,29},{25,17},{29,21},{1... | collective-permute-start | bytes 589832 | tf_op jit(solution)/shard_map/ppermute | solution.py:33
  94.7 1.3 collective-permute-start.27
  96.0 5.8 %step2.1 = (bf16[2,128,384]{2,1,0:T(8,128)(2,1)S(1)}, bf16[2,128,384]{2,1,0:T(8,128)(2,1)S(1)}) custom-call(f32[1,16]{1,0:T(1,128)S(1)} %copy-done.15, s32[4,1]{1,0:T(4,128)S(1)} %copy.26.times.refs_1_, f32[1,1536]{1,0:T(1,128)S(1)} %copy-done.10, f32[1,1536]{1,0:T(1,128)S(1)} %copy-done.11, f32[1,1536]{1,0:T(1,128)S(1)} %copy-done.14, ...), custom_call_target="tpu_custom_call" | custom-call | flops 1610612736 | bytes 3145728 | tf_op jit(solution)/shard_map/step2/pallas_call | solution.py:442
  101.8 1.3 collective-permute-done.27.refs_3_
  103.1 1.9 %collective-permute-start.28 = (bf16[2,128,384]{2,1,0:T(8,128)(2,1)S(1)}, bf16[2,128,384]{2,1,0:T(8,128)(2,1)S(1)}, u32[]{:S(2)}, u32[]{:S(2)}) collective-permute-start(bf16[2,128,384]{2,1,0:T(8,128)(2,1)S(1)} %get-tuple-element.62.refs_11_), channel_id=1, source_target_pairs={{16,20},{20,16},{24,28},{28,24},{17,21},{21,17},{25,29},{29,25},{1... | collective-permute-start | bytes 589832 | tf_op jit(solution)/shard_map/ppermute | solution.py:33
  105.0 2.4 %collective-permute-start.29 = (bf16[2,128,384]{2,1,0:T(8,128)(2,1)S(1)}, bf16[2,128,384]{2,1,0:T(8,128)(2,1)S(1)}, u32[]{:S(2)}, u32[]{:S(2)}) collective-permute-start(bf16[2,128,384]{2,1,0:T(8,128)(2,1)S(1)} %get-tuple-element.63.refs_12_), channel_id=1, source_target_pairs={{16,20},{20,16},{24,28},{28,24},{17,21},{21,17},{25,29},{29,25},{1... | collective-permute-start | bytes 589832 | tf_op jit(solution)/shard_map/ppermute | solution.py:33
  107.4 1.9 %collective-permute-start.30 = (bf16[2,128,384]{2,1,0:T(8,128)(2,1)S(1)}, bf16[2,128,384]{2,1,0:T(8,128)(2,1)S(1)}, u32[]{:S(2)}, u32[]{:S(2)}) collective-permute-start(bf16[2,128,384]{2,1,0:T(8,128)(2,1)S(1)} %get-tuple-element.64.refs_15_), channel_id=1, source_target_pairs={{16,20},{20,16},{24,28},{28,24},{17,21},{21,17},{25,29},{29,25},{1... | collective-permute-start | bytes 589832 | tf_op jit(solution)/shard_map/ppermute | solution.py:33
  109.4 2.4 %collective-permute-start.31 = (bf16[2,128,384]{2,1,0:T(8,128)(2,1)S(1)}, bf16[2,128,384]{2,1,0:T(8,128)(2,1)S(1)}, u32[]{:S(2)}, u32[]{:S(2)}) collective-permute-start(bf16[2,128,384]{2,1,0:T(8,128)(2,1)S(1)} %get-tuple-element.65.refs_16_), channel_id=1, source_target_pairs={{16,20},{20,16},{24,28},{28,24},{17,21},{21,17},{25,29},{29,25},{1... | collective-permute-start | bytes 589832 | tf_op jit(solution)/shard_map/ppermute | solution.py:33
  111.8 0.5 early.1
  112.3 0.1 collective-permute-start.32
  112.4 1.3 collective-permute-start.33
  113.7 0.5 collective-permute-start.34
  114.2 5.8 %step3.1 = (bf16[2,128,384]{2,1,0:T(8,128)(2,1)S(1)}, bf16[2,128,384]{2,1,0:T(8,128)(2,1)S(1)}) custom-call(f32[1,16]{1,0:T(1,128)S(1)} %copy-done.15, s32[4,1]{1,0:T(4,128)S(1)} %copy.26.times.refs_1_, f32[1,1536]{1,0:T(1,128)S(1)} %copy-done.10, f32[1,1536]{1,0:T(1,128)S(1)} %copy-done.11, f32[1,1536]{1,0:T(1,128)S(1)} %copy-done.14, ...), custom_call_target="tpu_custom_call" | custom-call | flops 1610612736 | bytes 3145728 | tf_op jit(solution)/shard_map/step3/pallas_call | solution.py:442
  120.0 0.1 collective-permute-done.33.refs_10_
  120.1 3.3 %collective-permute-done.34.refs_11_ = bf16[2,128,384]{2,1,0:T(8,128)(2,1)S(1)} collective-permute-done((bf16[2,128,384]{2,1,0:T(8,128)(2,1)S(1)}, bf16[2,128,384]{2,1,0:T(8,128)(2,1)S(1)}, u32[]{:S(2)}, u32[]{:S(2)}) %collective-permute-start.34) | collective-permute-done | bytes 196640 | tf_op jit(solution)/shard_map/ppermute | solution.py:27
  123.4 1.2 settle.1
  124.7 0.4 collective-permute-start.35
  125.1 1.3 collective-permute-start.36
  126.3 0.3 collective-permute-start.37
  126.7 3.9 %collective-permute-done.38.refs_6_ = bf16[96,256]{1,0:T(8,128)(2,1)S(1)} collective-permute-done((bf16[96,256]{1,0:T(8,128)(2,1)S(1)}, bf16[96,256]{1,0:T(8,128)(2,1)S(1)}, u32[]{:S(2)}, u32[]{:S(2)}) %collective-permute-start.38) | collective-permute-done | bytes 49184 | tf_op jit(solution)/shard_map/ppermute | solution.py:38
  130.6 2.1 %collective-permute-done.39.refs_7_ = bf16[96,256]{1,0:T(8,128)(2,1)S(1)} collective-permute-done((bf16[96,256]{1,0:T(8,128)(2,1)S(1)}, bf16[96,256]{1,0:T(8,128)(2,1)S(1)}, u32[]{:S(2)}, u32[]{:S(2)}) %collective-permute-start.39) | collective-permute-done | bytes 49184 | tf_op jit(solution)/shard_map/ppermute | solution.py:38
  132.7 2.0 %collective-permute-done.40.refs_8_ = bf16[96,256]{1,0:T(8,128)(2,1)S(1)} collective-permute-done((bf16[96,256]{1,0:T(8,128)(2,1)S(1)}, bf16[96,256]{1,0:T(8,128)(2,1)S(1)}, u32[]{:S(2)}, u32[]{:S(2)}) %collective-permute-start.40) | collective-permute-done | bytes 49184 | tf_op jit(solution)/shard_map/ppermute | solution.py:38
  134.7 1.5 %finish.1 = (bf16[3,128,1536]{2,1,0:T(8,128)(2,1)}, f32[96,256]{1,0:T(8,128)}) custom-call(bf16[3,128,1536]{2,1,0:T(8,128)(2,1)} %get-tuple-element.73.refs_0_, bf16[128,384]{1,0:T(8,128)(2,1)S(1)} %get-tuple-element.74.refs_1_, bf16[128,384]{1,0:T(8,128)(2,1)S(1)} %collective-permute-done.35.refs_2_, ...), custom_call_target="tpu_custom_call", output_to_operand_aliasing={{0}: (0, {})} | custom-call | tf_op jit(solution)/shard_map/finish/pallas_call | solution.py:442
  (76 shorter events, 0.6 us)
Async XLA Ops:
  0.6 13.8 %copy-start.1 = (bf16[1,3,1,128,1536]{4,3,2,1,0:T(8,128)(2,1)S(1)}, bf16[1,3,1,128,1536]{4,3,2,1,0:T(8,128)(2,1)}, u32[]{:S(2)}) copy-start(bf16[1,3,1,128,1536]{4,3,2,1,0:T(8,128)(2,1)} %incoming.3) | copy-start | bytes 3538948
  0.6 13.8 %copy-start.16 = (s32[4,1,128]{2,1,0:T(1,128)S(1)}, s32[4,1,128]{2,1,0:T(1,128)}, u32[]{:S(2)}) copy-start(s32[4,1,128]{2,1,0:T(1,128)} %contacts.1) | copy-start | bytes 6148
  2.0 1.4 %collective-permute-start = (bf16[96,768]{1,0:T(8,128)(2,1)S(1)}, bf16[96,768]{1,0:T(8,128)(2,1)S(1)}, u32[]{:S(2)}, u32[]{:S(2)}) collective-permute-start(bf16[96,768]{1,0:T(8,128)(2,1)S(1)} %get-tuple-element.44), channel_id=1, source_target_pairs={{0,4},{4,0},{8,12},{12,8},{1,5},{5,1},{9,13},{13,9},{2,6},{6,2},{1... | collective-permute-start | bytes 442376 | tf_op jit(solution)/shard_map/ppermute | solution.py:27
  3.4 11.0 %collective-permute-start.1 = (bf16[2,96,768]{2,1,0:T(8,128)(2,1)S(1)}, bf16[2,96,768]{2,1,0:T(8,128)(2,1)S(1)}, u32[]{:S(2)}, u32[]{:S(2)}) collective-permute-start(bf16[2,96,768]{2,1,0:T(8,128)(2,1)S(1)} %near.1.refs_0_), channel_id=1, source_target_pairs={{0,1},{1,2},{2,3},{3,0},{4,5},{5,6},{6,7},{7,4},{8,9},{9,10},{10,1... | collective-permute-start | bytes 884744 | tf_op jit(solution)/shard_map/ppermute | solution.py:38
  5.1 0.7 copy-start.3
  5.8 6.7 %collective-permute-start.2 = (bf16[96,768]{1,0:T(8,128)(2,1)S(1)}, bf16[96,768]{1,0:T(8,128)(2,1)S(1)}, u32[]{:S(2)}, u32[]{:S(2)}) collective-permute-start(bf16[96,768]{1,0:T(8,128)(2,1)S(1)} %get-tuple-element.45), channel_id=1, source_target_pairs={{0,8},{4,12},{8,0},{12,4},{1,9},{5,13},{9,1},{13,5},{2,10},{6,14},... | collective-permute-start | bytes 442376 | tf_op jit(solution)/shard_map/ppermute | solution.py:27
  7.3 6.3 %collective-permute-start.3 = (bf16[96,768]{1,0:T(8,128)(2,1)S(1)}, bf16[96,768]{1,0:T(8,128)(2,1)S(1)}, u32[]{:S(2)}, u32[]{:S(2)}) collective-permute-start(bf16[96,768]{1,0:T(8,128)(2,1)S(1)} %get-tuple-element.46), channel_id=1, source_target_pairs={{0,12},{4,8},{8,4},{12,0},{1,13},{5,9},{9,5},{13,1},{2,14},{6,10},... | collective-permute-start | bytes 442376 | tf_op jit(solution)/shard_map/ppermute | solution.py:27
  14.4 2.3 %copy-start.5 = (bf16[2,96,768]{2,1,0:T(8,128)(2,1)}, bf16[2,96,768]{2,1,0:T(8,128)(2,1)S(1)}, u32[]{:S(2)}) copy-start(bf16[2,96,768]{2,1,0:T(8,128)(2,1)S(1)} %collective-permute-done.1.refs_0_) | copy-start | bytes 884740
  14.5 25.0 %copy-start.2 = (bf16[272,1536]{1,0:T(8,128)(2,1)}, bf16[272,1536]{1,0:T(8,128)(2,1)S(1)}, u32[]{:S(2)}) copy-start(bf16[272,1536]{1,0:T(8,128)(2,1)S(1)} %first.1.refs_0_) | copy-start | bytes 2506756
  14.5 25.0 %copy-start.9 = (bf16[1,3,1,128,256]{4,3,2,1,0:T(8,128)(2,1)S(1)}, bf16[1,3,1,128,256]{4,3,2,1,0:T(8,128)(2,1)}, u32[]{:S(2)}) copy-start(bf16[1,3,1,128,256]{4,3,2,1,0:T(8,128)(2,1)} %cotangent.1) | copy-start | bytes 589828
  14.5 24.9 %collective-permute-start.4 = (bf16[272,1536]{1,0:T(8,128)(2,1)S(1)}, bf16[272,1536]{1,0:T(8,128)(2,1)S(1)}, u32[]{:S(2)}, u32[]{:S(2)}) collective-permute-start(bf16[272,1536]{1,0:T(8,128)(2,1)S(1)} %first.1.refs_0_), channel_id=1, source_target_pairs={{0,8},{4,12},{8,0},{12,4},{1,9},{5,13},{9,1},{13,5},{2,10},{6,14},... | collective-permute-start | bytes 2506760 | tf_op jit(solution)/shard_map/ppermute | solution.py:27
  16.1 11.7 %collective-permute-start.6 = (bf16[2,96,768]{2,1,0:T(8,128)(2,1)S(1)}, bf16[2,96,768]{2,1,0:T(8,128)(2,1)S(1)}, u32[]{:S(2)}, u32[]{:S(2)}) collective-permute-start(bf16[2,96,768]{2,1,0:T(8,128)(2,1)S(1)} %far.1.refs_1_), channel_id=1, source_target_pairs={{0,1},{1,2},{2,3},{3,0},{4,5},{5,6},{6,7},{7,4},{8,9},{9,10},{10,1... | collective-permute-start | bytes 884744 | tf_op jit(solution)/shard_map/ppermute | solution.py:38
  16.7 17.5 %collective-permute-start.5 = (bf16[2,96,768]{2,1,0:T(8,128)(2,1)S(1)}, bf16[2,96,768]{2,1,0:T(8,128)(2,1)}, u32[]{:S(2)}, u32[]{:S(2)}) collective-permute-start(bf16[2,96,768]{2,1,0:T(8,128)(2,1)S(1)} %collective-permute-done.1.refs_0_), channel_id=1, source_target_pairs={{0,1},{1,2},{2,3},{3,0},{4,5},{5,6},{6,7},{7,4},{8,9},{9,10},{10,1... | collective-permute-start | bytes 884744 | tf_op jit(solution)/shard_map/ppermute | solution.py:38
  27.8 11.6 %copy-start.7 = (bf16[2,96,768]{2,1,0:T(8,128)(2,1)}, bf16[2,96,768]{2,1,0:T(8,128)(2,1)S(1)}, u32[]{:S(2)}) copy-start(bf16[2,96,768]{2,1,0:T(8,128)(2,1)S(1)} %collective-permute-done.6.refs_1_) | copy-start | bytes 884740
  27.8 11.6 %collective-permute-start.7 = (bf16[2,96,768]{2,1,0:T(8,128)(2,1)S(1)}, bf16[2,96,768]{2,1,0:T(8,128)(2,1)}, u32[]{:S(2)}, u32[]{:S(2)}) collective-permute-start(bf16[2,96,768]{2,1,0:T(8,128)(2,1)S(1)} %collective-permute-done.6.refs_1_), channel_id=1, source_target_pairs={{0,1},{1,2},{2,3},{3,0},{4,5},{5,6},{6,7},{7,4},{8,9},{9,10},{10,1... | collective-permute-start | bytes 884744 | tf_op jit(solution)/shard_map/ppermute | solution.py:38
  27.8 13.6 %collective-permute-start.9 = (bf16[272,1536]{1,0:T(8,128)(2,1)S(1)}, bf16[272,1536]{1,0:T(8,128)(2,1)S(1)}, u32[]{:S(2)}, u32[]{:S(2)}) collective-permute-start(bf16[272,1536]{1,0:T(8,128)(2,1)S(1)} %first.1.refs_0_), channel_id=1, source_target_pairs={{0,4},{4,0},{8,12},{12,8},{1,5},{5,1},{9,13},{13,9},{2,6},{6,2},{1... | collective-permute-start | bytes 2506760 | tf_op jit(solution)/shard_map/ppermute | solution.py:27
  39.4 4.0 %copy-start = (bf16[272,1536]{1,0:T(8,128)(2,1)}, bf16[272,1536]{1,0:T(8,128)(2,1)S(1)}, u32[]{:S(2)}) copy-start(bf16[272,1536]{1,0:T(8,128)(2,1)S(1)} %tie.3.dep.refs_1_) | copy-start | bytes 2506756
  39.4 2.9 %copy-start.18 = (s32[4,1]{0,1:T(1,128)S(1)}, s32[4,1]{0,1:T(1,128)}, u32[]{:S(2)}) copy-start(s32[4,1]{0,1:T(1,128)} %param.15) | copy-start | bytes 52
  39.4 6.2 %collective-permute-start.10 = (bf16[272,1536]{1,0:T(8,128)(2,1)S(1)}, bf16[272,1536]{1,0:T(8,128)(2,1)}, u32[]{:S(2)}, u32[]{:S(2)}) collective-permute-start(bf16[272,1536]{1,0:T(8,128)(2,1)S(1)} %tie.3.dep.refs_1_), channel_id=1, source_target_pairs={{0,4},{4,0},{8,12},{12,8},{1,5},{5,1},{9,13},{13,9},{2,6},{6,2},{1... | collective-permute-start | bytes 2506760 | tf_op jit(solution)/shard_map/ppermute | solution.py:27
  39.6 23.8 %collective-permute-start.8 = (bf16[256,1536]{1,0:T(8,128)(2,1)S(1)}, bf16[256,1536]{1,0:T(8,128)(2,1)S(1)}, u32[]{:S(2)}, u32[]{:S(2)}) collective-permute-start(bf16[256,1536]{1,0:T(8,128)(2,1)S(1)} %second.1.refs_6_.refs_4_), channel_id=1, source_target_pairs={{0,8},{4,12},{8,0},{12,4},{1,9},{5,13},{9,1},{13,5},{2,10},{6,14},... | collective-permute-start | bytes 2359304 | tf_op jit(solution)/shard_map/ppermute | solution.py:27
  40.2 12.0 %collective-permute-start.11 = (bf16[2,96,768]{2,1,0:T(8,128)(2,1)}, bf16[2,96,768]{2,1,0:T(8,128)(2,1)}, u32[]{:S(2)}, u32[]{:S(2)}) collective-permute-start(bf16[2,96,768]{2,1,0:T(8,128)(2,1)} %collective-permute-done.5.refs_1_.refs_0_), channel_id=1, source_target_pairs={{0,1},{1,2},{2,3},{3,0},{4,5},{5,6},{6,7},{7,4},{8,9},{9,10},{10,1... | collective-permute-start | bytes 884744 | tf_op jit(solution)/shard_map/ppermute | solution.py:38
  40.2 17.5 %collective-permute-start.12 = (bf16[2,96,768]{2,1,0:T(8,128)(2,1)}, bf16[2,96,768]{2,1,0:T(8,128)(2,1)}, u32[]{:S(2)}, u32[]{:S(2)}) collective-permute-start(bf16[2,96,768]{2,1,0:T(8,128)(2,1)} %collective-permute-done.7.refs_2_.refs_1_), channel_id=1, source_target_pairs={{0,1},{1,2},{2,3},{3,0},{4,5},{5,6},{6,7},{7,4},{8,9},{9,10},{10,1... | collective-permute-start | bytes 884744 | tf_op jit(solution)/shard_map/ppermute | solution.py:38
  41.4 0.9 copy-start.17
  42.3 30.1 %collective-permute-start.13 = (bf16[256,1536]{1,0:T(8,128)(2,1)S(1)}, bf16[256,1536]{1,0:T(8,128)(2,1)S(1)}, u32[]{:S(2)}, u32[]{:S(2)}) collective-permute-start(bf16[256,1536]{1,0:T(8,128)(2,1)S(1)} %second.1.refs_6_.refs_4_), channel_id=1, source_target_pairs={{0,4},{4,0},{8,12},{12,8},{1,5},{5,1},{9,13},{13,9},{2,6},{6,2},{1... | collective-permute-start | bytes 2359304 | tf_op jit(solution)/shard_map/ppermute | solution.py:27
  42.4 1.0 copy-start.4
  43.4 1.0 copy-start.6
  43.4 1.0 copy-start.8
  44.5 1.2 copy-start.10
  44.5 1.2 copy-start.11
  44.5 1.2 copy-start.12
  45.6 12.1 %copy-start.13 = (s32[4,1,512]{2,1,0:T(1,128)S(1)}, s32[4,1,512]{2,1,0:T(1,128)}, u32[]{:S(2)}) copy-start(s32[4,1,512]{2,1,0:T(1,128)} %refs_5_.7) | copy-start | bytes 24580
  45.6 12.1 %copy-start.14 = (f32[1,1536]{1,0:T(1,128)S(1)}, f32[1,1536]{1,0:T(1,128)}, u32[]{:S(2)}) copy-start(f32[1,1536]{1,0:T(1,128)} %refs_4_.7) | copy-start | bytes 18436
  45.6 12.1 %copy-start.15 = (f32[1,16]{1,0:T(1,128)S(1)}, f32[1,16]{1,0:T(1,128)}, u32[]{:S(2)}) copy-start(f32[1,16]{1,0:T(1,128)} %refs_0_.7) | copy-start | bytes 196
  63.4 32.6 %collective-permute-start.14 = (bf16[256,1536]{1,0:T(8,128)(2,1)S(1)}, bf16[256,1536]{1,0:T(8,128)(2,1)S(1)}, u32[]{:S(2)}, u32[]{:S(2)}) collective-permute-start(bf16[256,1536]{1,0:T(8,128)(2,1)S(1)} %tie.4.refs_7_.refs_5_), channel_id=1, source_target_pairs={{0,4},{4,0},{8,12},{12,8},{1,5},{5,1},{9,13},{13,9},{2,6},{6,2},{1... | collective-permute-start | bytes 2359304 | tf_op jit(solution)/shard_map/ppermute | solution.py:27
  63.4 9.6 %collective-permute-start.15 = (bf16[2,128,384]{2,1,0:T(8,128)(2,1)S(1)}, bf16[2,128,384]{2,1,0:T(8,128)(2,1)S(1)}, u32[]{:S(2)}, u32[]{:S(2)}) collective-permute-start(bf16[2,128,384]{2,1,0:T(8,128)(2,1)S(1)} %get-tuple-element.50.refs_1_.refs_0_), channel_id=1, source_target_pairs={{0,16},{1,17},{2,18},{3,19},{4,20},{5,21},{6,22},{7,23},{8,24},{9,... | collective-permute-start | bytes 589832 | tf_op jit(solution)/shard_map/ppermute | solution.py:17
  64.7 12.5 %collective-permute-start.19 = (bf16[2,128,384]{2,1,0:T(8,128)(2,1)S(1)}, bf16[2,128,384]{2,1,0:T(8,128)(2,1)S(1)}, u32[]{:S(2)}, u32[]{:S(2)}) collective-permute-start(bf16[2,128,384]{2,1,0:T(8,128)(2,1)S(1)} %get-tuple-element.52.refs_1_), channel_id=1, source_target_pairs={{0,16},{1,17},{2,18},{3,19},{4,20},{5,21},{6,22},{7,23},{8,24},{9,... | collective-permute-start | bytes 589832 | tf_op jit(solution)/shard_map/ppermute | solution.py:17
  71.1 10.0 %collective-permute-start.23 = (bf16[2,128,384]{2,1,0:T(8,128)(2,1)S(1)}, bf16[2,128,384]{2,1,0:T(8,128)(2,1)S(1)}, u32[]{:S(2)}, u32[]{:S(2)}) collective-permute-start(bf16[2,128,384]{2,1,0:T(8,128)(2,1)S(1)} %get-tuple-element.60.refs_2_), channel_id=1, source_target_pairs={{0,16},{1,17},{2,18},{3,19},{4,20},{5,21},{6,22},{7,23},{8,24},{9,... | collective-permute-start | bytes 589832 | tf_op jit(solution)/shard_map/ppermute | solution.py:17
  72.4 10.6 %collective-permute-start.26 = (bf16[2,128,384]{2,1,0:T(8,128)(2,1)S(1)}, bf16[2,128,384]{2,1,0:T(8,128)(2,1)S(1)}, u32[]{:S(2)}, u32[]{:S(2)}) collective-permute-start(bf16[2,128,384]{2,1,0:T(8,128)(2,1)S(1)} %get-tuple-element.61.refs_3_), channel_id=1, source_target_pairs={{0,8},{4,12},{8,0},{12,4},{1,9},{5,13},{9,1},{13,5},{2,10},{6,14},... | collective-permute-start | bytes 589832 | tf_op jit(solution)/shard_map/ppermute | solution.py:33
  73.1 12.3 %collective-permute-start.16 = (bf16[2,128,384]{2,1,0:T(8,128)(2,1)S(1)}, bf16[2,128,384]{2,1,0:T(8,128)(2,1)S(1)}, u32[]{:S(2)}, u32[]{:S(2)}) collective-permute-start(bf16[2,128,384]{2,1,0:T(8,128)(2,1)S(1)} %collective-permute-done.15.refs_11_), channel_id=1, source_target_pairs={{16,24},{20,28},{24,16},{28,20},{17,25},{21,29},{25,17},{29,21},{1... | collective-permute-start | bytes 589832 | tf_op jit(solution)/shard_map/ppermute | solution.py:33
  77.2 10.1 %collective-permute-start.20 = (bf16[2,128,384]{2,1,0:T(8,128)(2,1)S(1)}, bf16[2,128,384]{2,1,0:T(8,128)(2,1)S(1)}, u32[]{:S(2)}, u32[]{:S(2)}) collective-permute-start(bf16[2,128,384]{2,1,0:T(8,128)(2,1)S(1)} %collective-permute-done.19.refs_15_), channel_id=1, source_target_pairs={{16,24},{20,28},{24,16},{28,20},{17,25},{21,29},{25,17},{29,21},{1... | collective-permute-start | bytes 589832 | tf_op jit(solution)/shard_map/ppermute | solution.py:33
  81.0 8.7 %collective-permute-start.17 = (bf16[2,128,384]{2,1,0:T(8,128)(2,1)S(1)}, bf16[2,128,384]{2,1,0:T(8,128)(2,1)S(1)}, u32[]{:S(2)}, u32[]{:S(2)}) collective-permute-start(bf16[2,128,384]{2,1,0:T(8,128)(2,1)S(1)} %collective-permute-done.15.refs_11_), channel_id=1, source_target_pairs={{16,20},{20,16},{24,28},{28,24},{17,21},{21,17},{25,29},{29,25},{1... | collective-permute-start | bytes 589832 | tf_op jit(solution)/shard_map/ppermute | solution.py:33
  83.0 8.3 %collective-permute-start.21 = (bf16[2,128,384]{2,1,0:T(8,128)(2,1)S(1)}, bf16[2,128,384]{2,1,0:T(8,128)(2,1)S(1)}, u32[]{:S(2)}, u32[]{:S(2)}) collective-permute-start(bf16[2,128,384]{2,1,0:T(8,128)(2,1)S(1)} %collective-permute-done.19.refs_15_), channel_id=1, source_target_pairs={{16,20},{20,16},{24,28},{28,24},{17,21},{21,17},{25,29},{29,25},{1... | collective-permute-start | bytes 589832 | tf_op jit(solution)/shard_map/ppermute | solution.py:33
  85.4 9.3 %collective-permute-start.18 = (bf16[2,128,384]{2,1,0:T(8,128)(2,1)S(1)}, bf16[2,128,384]{2,1,0:T(8,128)(2,1)S(1)}, u32[]{:S(2)}, u32[]{:S(2)}) collective-permute-start(bf16[2,128,384]{2,1,0:T(8,128)(2,1)S(1)} %collective-permute-done.16.refs_12_), channel_id=1, source_target_pairs={{16,20},{20,16},{24,28},{28,24},{17,21},{21,17},{25,29},{29,25},{1... | collective-permute-start | bytes 589832 | tf_op jit(solution)/shard_map/ppermute | solution.py:33
  87.3 8.6 %collective-permute-start.22 = (bf16[2,128,384]{2,1,0:T(8,128)(2,1)S(1)}, bf16[2,128,384]{2,1,0:T(8,128)(2,1)S(1)}, u32[]{:S(2)}, u32[]{:S(2)}) collective-permute-start(bf16[2,128,384]{2,1,0:T(8,128)(2,1)S(1)} %collective-permute-done.20.refs_16_), channel_id=1, source_target_pairs={{16,20},{20,16},{24,28},{28,24},{17,21},{21,17},{25,29},{29,25},{1... | collective-permute-start | bytes 589832 | tf_op jit(solution)/shard_map/ppermute | solution.py:33
  89.8 12.0 %collective-permute-start.25 = (bf16[2,128,384]{2,1,0:T(8,128)(2,1)S(1)}, bf16[2,128,384]{2,1,0:T(8,128)(2,1)S(1)}, u32[]{:S(2)}, u32[]{:S(2)}) collective-permute-start(bf16[2,128,384]{2,1,0:T(8,128)(2,1)S(1)} %get-tuple-element.61.refs_3_), channel_id=1, source_target_pairs={{0,16},{1,17},{2,18},{3,19},{4,20},{5,21},{6,22},{7,23},{8,24},{9,... | collective-permute-start | bytes 589832 | tf_op jit(solution)/shard_map/ppermute | solution.py:17
  91.3 10.6 %collective-permute-start.24 = (bf16[2,128,384]{2,1,0:T(8,128)(2,1)S(1)}, bf16[2,128,384]{2,1,0:T(8,128)(2,1)S(1)}, u32[]{:S(2)}, u32[]{:S(2)}) collective-permute-start(bf16[2,128,384]{2,1,0:T(8,128)(2,1)S(1)} %collective-permute-done.23.refs_0_), channel_id=1, source_target_pairs={{16,24},{20,28},{24,16},{28,20},{17,25},{21,29},{25,17},{29,21},{1... | collective-permute-start | bytes 589832 | tf_op jit(solution)/shard_map/ppermute | solution.py:33
  94.7 8.4 %collective-permute-start.27 = (bf16[2,128,384]{2,1,0:T(8,128)(2,1)S(1)}, bf16[2,128,384]{2,1,0:T(8,128)(2,1)S(1)}, u32[]{:S(2)}, u32[]{:S(2)}) collective-permute-start(bf16[2,128,384]{2,1,0:T(8,128)(2,1)S(1)} %collective-permute-done.26), channel_id=1, source_target_pairs={{0,16},{1,17},{2,18},{3,19},{4,20},{5,21},{6,22},{7,23},{8,24},{9,... | collective-permute-start | bytes 589832 | tf_op jit(solution)/shard_map/ppermute | solution.py:17
  103.1 9.3 %collective-permute-start.28 = (bf16[2,128,384]{2,1,0:T(8,128)(2,1)S(1)}, bf16[2,128,384]{2,1,0:T(8,128)(2,1)S(1)}, u32[]{:S(2)}, u32[]{:S(2)}) collective-permute-start(bf16[2,128,384]{2,1,0:T(8,128)(2,1)S(1)} %get-tuple-element.62.refs_11_), channel_id=1, source_target_pairs={{16,20},{20,16},{24,28},{28,24},{17,21},{21,17},{25,29},{29,25},{1... | collective-permute-start | bytes 589832 | tf_op jit(solution)/shard_map/ppermute | solution.py:33
  105.0 8.7 %collective-permute-start.29 = (bf16[2,128,384]{2,1,0:T(8,128)(2,1)S(1)}, bf16[2,128,384]{2,1,0:T(8,128)(2,1)S(1)}, u32[]{:S(2)}, u32[]{:S(2)}) collective-permute-start(bf16[2,128,384]{2,1,0:T(8,128)(2,1)S(1)} %get-tuple-element.63.refs_12_), channel_id=1, source_target_pairs={{16,20},{20,16},{24,28},{28,24},{17,21},{21,17},{25,29},{29,25},{1... | collective-permute-start | bytes 589832 | tf_op jit(solution)/shard_map/ppermute | solution.py:33
  107.4 6.8 %collective-permute-start.30 = (bf16[2,128,384]{2,1,0:T(8,128)(2,1)S(1)}, bf16[2,128,384]{2,1,0:T(8,128)(2,1)S(1)}, u32[]{:S(2)}, u32[]{:S(2)}) collective-permute-start(bf16[2,128,384]{2,1,0:T(8,128)(2,1)S(1)} %get-tuple-element.64.refs_15_), channel_id=1, source_target_pairs={{16,20},{20,16},{24,28},{28,24},{17,21},{21,17},{25,29},{29,25},{1... | collective-permute-start | bytes 589832 | tf_op jit(solution)/shard_map/ppermute | solution.py:33
  109.4 4.9 %collective-permute-start.31 = (bf16[2,128,384]{2,1,0:T(8,128)(2,1)S(1)}, bf16[2,128,384]{2,1,0:T(8,128)(2,1)S(1)}, u32[]{:S(2)}, u32[]{:S(2)}) collective-permute-start(bf16[2,128,384]{2,1,0:T(8,128)(2,1)S(1)} %get-tuple-element.65.refs_16_), channel_id=1, source_target_pairs={{16,20},{20,16},{24,28},{28,24},{17,21},{21,17},{25,29},{29,25},{1... | collective-permute-start | bytes 589832 | tf_op jit(solution)/shard_map/ppermute | solution.py:33
  112.3 7.7 %collective-permute-start.32 = (bf16[2,128,384]{2,1,0:T(8,128)(2,1)S(1)}, bf16[2,128,384]{2,1,0:T(8,128)(2,1)S(1)}, u32[]{:S(2)}, u32[]{:S(2)}) collective-permute-start(bf16[2,128,384]{2,1,0:T(8,128)(2,1)S(1)} %get-tuple-element.69), channel_id=1, source_target_pairs={{0,4},{4,0},{8,12},{12,8},{1,5},{5,1},{9,13},{13,9},{2,6},{6,2},{1... | collective-permute-start | bytes 589832 | tf_op jit(solution)/shard_map/ppermute | solution.py:27
  112.4 7.8 %collective-permute-start.33 = (bf16[2,128,384]{2,1,0:T(8,128)(2,1)S(1)}, bf16[2,128,384]{2,1,0:T(8,128)(2,1)S(1)}, u32[]{:S(2)}, u32[]{:S(2)}) collective-permute-start(bf16[2,128,384]{2,1,0:T(8,128)(2,1)S(1)} %get-tuple-element.70), channel_id=1, source_target_pairs={{0,8},{4,12},{8,0},{12,4},{1,9},{5,13},{9,1},{13,5},{2,10},{6,14},... | collective-permute-start | bytes 589832 | tf_op jit(solution)/shard_map/ppermute | solution.py:27
  113.7 9.7 %collective-permute-start.34 = (bf16[2,128,384]{2,1,0:T(8,128)(2,1)S(1)}, bf16[2,128,384]{2,1,0:T(8,128)(2,1)S(1)}, u32[]{:S(2)}, u32[]{:S(2)}) collective-permute-start(bf16[2,128,384]{2,1,0:T(8,128)(2,1)S(1)} %get-tuple-element.71), channel_id=1, source_target_pairs={{0,12},{4,8},{8,4},{12,0},{1,13},{5,9},{9,5},{13,1},{2,14},{6,10},... | collective-permute-start | bytes 589832 | tf_op jit(solution)/shard_map/ppermute | solution.py:27
  124.7 5.9 %collective-permute-start.38 = (bf16[96,256]{1,0:T(8,128)(2,1)S(1)}, bf16[96,256]{1,0:T(8,128)(2,1)S(1)}, u32[]{:S(2)}, u32[]{:S(2)}) collective-permute-start(bf16[96,256]{1,0:T(8,128)(2,1)S(1)} %get-tuple-element.79), channel_id=1, source_target_pairs={{0,1},{1,2},{2,3},{3,0},{4,5},{5,6},{6,7},{7,4},{8,9},{9,10},{10,1... | collective-permute-start | bytes 147464 | tf_op jit(solution)/shard_map/ppermute | solution.py:38
  124.7 10.0 %collective-permute-start.35 = (bf16[128,384]{1,0:T(8,128)(2,1)S(1)}, bf16[128,384]{1,0:T(8,128)(2,1)S(1)}, u32[]{:S(2)}, u32[]{:S(2)}) collective-permute-start(bf16[128,384]{1,0:T(8,128)(2,1)S(1)} %get-tuple-element.75), channel_id=1, source_target_pairs={{0,4},{4,0},{8,12},{12,8},{1,5},{5,1},{9,13},{13,9},{2,6},{6,2},{1... | collective-permute-start | bytes 294920 | tf_op jit(solution)/shard_map/ppermute | solution.py:27
  125.1 9.6 %collective-permute-start.36 = (bf16[128,384]{1,0:T(8,128)(2,1)S(1)}, bf16[128,384]{1,0:T(8,128)(2,1)S(1)}, u32[]{:S(2)}, u32[]{:S(2)}) collective-permute-start(bf16[128,384]{1,0:T(8,128)(2,1)S(1)} %get-tuple-element.76), channel_id=1, source_target_pairs={{0,8},{4,12},{8,0},{12,4},{1,9},{5,13},{9,1},{13,5},{2,10},{6,14},... | collective-permute-start | bytes 294920 | tf_op jit(solution)/shard_map/ppermute | solution.py:27
  126.3 8.4 %collective-permute-start.37 = (bf16[128,384]{1,0:T(8,128)(2,1)S(1)}, bf16[128,384]{1,0:T(8,128)(2,1)S(1)}, u32[]{:S(2)}, u32[]{:S(2)}) collective-permute-start(bf16[128,384]{1,0:T(8,128)(2,1)S(1)} %get-tuple-element.77), channel_id=1, source_target_pairs={{0,12},{4,8},{8,4},{12,0},{1,13},{5,9},{9,5},{13,1},{2,14},{6,10},... | collective-permute-start | bytes 294920 | tf_op jit(solution)/shard_map/ppermute | solution.py:27
  126.7 6.1 %collective-permute-start.39 = (bf16[96,256]{1,0:T(8,128)(2,1)S(1)}, bf16[96,256]{1,0:T(8,128)(2,1)S(1)}, u32[]{:S(2)}, u32[]{:S(2)}) collective-permute-start(bf16[96,256]{1,0:T(8,128)(2,1)S(1)} %get-tuple-element.80), channel_id=1, source_target_pairs={{0,2},{1,3},{2,0},{3,1},{4,6},{5,7},{6,4},{7,5},{8,10},{9,11},{10,... | collective-permute-start | bytes 147464 | tf_op jit(solution)/shard_map/ppermute | solution.py:38
  130.6 4.1 %collective-permute-start.40 = (bf16[96,256]{1,0:T(8,128)(2,1)S(1)}, bf16[96,256]{1,0:T(8,128)(2,1)S(1)}, u32[]{:S(2)}, u32[]{:S(2)}) collective-permute-start(bf16[96,256]{1,0:T(8,128)(2,1)S(1)} %get-tuple-element.81), channel_id=1, source_target_pairs={{0,3},{1,0},{2,1},{3,2},{4,7},{5,4},{6,5},{7,6},{8,11},{9,8},{10,9... | collective-permute-start | bytes 147464 | tf_op jit(solution)/shard_map/ppermute | solution.py:38

commit v8 on v7

--- a/solution.py
+++ b/solution.py
@@ -31,6 +31,10 @@
     count = lax.axis_size("seq")
     pairs = [(section * count + i, section * count + (i ^ bit)) for i in range(count)]
     return lax.ppermute(value, ("pipe", "seq"), pairs)
+
+
+def handed_over(value):
+    return lax.ppermute(value, "pipe", [(0, 1), (1, 0)])
 
 
 def shifted(value, axis, shift):
@@ -611,7 +615,7 @@
             relayed[3] = []
             for k in range(HALVES):
                 mine, across = tied[2 * k], tied[2 * k + 1]
-                relayed[3] += [mine, across, swap_within(1, mine, 1), swap_within(1, across, 1)]
+                relayed[3] += [mine, across, swap(mine, 1), swap(across, 1)]
             early = call(
                 functools.partial(early_kernel, turns, seq_count, HALVES, feats),
                 "early",
@@ -627,21 +631,16 @@
         if step + 2 < steps:
             crossing = []
             for k, half in enumerate(outputs[-1]):
-                piece = passed_along(half, "pipe", 1)
+                piece = handed_over(half)
                 if step == 1 and k == 1:
-                    across = passed_along(swap_within(0, half, 2), "pipe", 1)
+                    across = handed_over(swap_within(0, half, 2))
                 else:
-                    across = swap_within(1, piece, 2)
+                    across = swap(piece, 2)
                 crossing.append((piece, across))
             if step == 0:
                 relayed[2] = []
                 for mine, across in crossing:
-                    relayed[2] += [
-                        mine,
-                        across,
-                        swap_within(1, mine, 1),
-                        swap_within(1, across, 1),
-                    ]
+                    relayed[2] += [mine, across, swap(mine, 1), swap(across, 1)]
 
     g_shape = (cols // hops, feats)
     operands = outputs[-2] + outputs[-1] + second + early + [early_grad]

time: 137 us -> 128 us (0.934)
  the two profiles are of different devices: /device:TPU:4 before, /device:TPU:0 now
where the time goes in v8:
time: 128 us; the launch traced here: 127 us
  waiting for transfers between devices  61.1 us (48%)
  Pallas kernels  32.8 us (26%)
  starting transfers between devices  28.5 us (22%)
  local copies, waits for them, and re-layouts  3.73 us (3%)
    ppermute x9, waiting for transfers between devices, shifted(): lax.ppermute(value, axis, [(source, (source + shift) % count) for source...  37.1 us
    pallas_call x19, Pallas kernels, call(): pl.pallas_call(kernel, out_shape=out_shape, in_specs=in_specs, scratch_sh...  32.8 us
    ppermute x26, waiting for transfers between devices, swap(): lax.ppermute(value, 'seq', [(source, source ^ bit) for source in range(co...  17.8 us
    ppermute x26, starting transfers between devices, swap(): lax.ppermute(value, 'seq', [(source, source ^ bit) for source in range(co...  12.9 us
    ppermute x9, starting transfers between devices, shifted(): lax.ppermute(value, axis, [(source, (source + shift) % count) for source...  6.49 us
    ppermute x5, starting transfers between devices, handed_over(): return lax.ppermute(value, 'pipe', [(0, 1), (1, 0)])  5.63 us
    unnamed x39, local copies, waits for them, and re-layouts  3.73 us
    ppermute x1, starting transfers between devices, swap_within(): return lax.ppermute(value, ('pipe', 'seq'), pairs)  3.57 us
  transfers between devices with their start and end apart: 41, of which 19 were waited for; matrix products, arithmetic and copies ran while one was open for 0% of the time, Pallas kernels for 23%

profile of v8, /device:TPU:0, one launch (start us, length us, event | category | flops | bytes accessed | tf_op | source)
XLA Modules:
  0.0 127.4 jit_solution(11099974653176628921)
XLA Ops:
  0.7 1.3 %pack.1 = (bf16[96,768]{1,0:T(8,128)(2,1)S(1)}, bf16[96,768]{1,0:T(8,128)(2,1)S(1)}, bf16[96,768]{1,0:T(8,128)(2,1)S(1)}, bf16[96,768]{1,0:T(8,128)(2,1)S(1)}) custom-call(bf16[1,96,1536]{2,1,0:T(8,128)(2,1)} %wq.1, bf16[1,96,1536]{2,1,0:T(8,128)(2,1)} %wkv.1), custom_call_target="tpu_custom_call" | custom-call | tf_op jit(solution)/shard_map/pack/pallas_call | solution.py:446
  2.0 0.5 collective-permute-start
  2.5 1.0 collective-permute-done.refs_1_
  3.5 3.0 %collective-permute-start.1 = (bf16[2,96,768]{2,1,0:T(8,128)(2,1)S(1)}, bf16[2,96,768]{2,1,0:T(8,128)(2,1)S(1)}, u32[]{:S(2)}, u32[]{:S(2)}) collective-permute-start(bf16[2,96,768]{2,1,0:T(8,128)(2,1)S(1)} %near.1.refs_0_), channel_id=1, source_target_pairs={{0,1},{1,2},{2,3},{3,0},{4,5},{5,6},{6,7},{7,4},{8,9},{9,10},{10,1... | collective-permute-start | bytes 884744 | tf_op jit(solution)/shard_map/ppermute | solution.py:42
  6.5 0.7 copy-done.3
  7.2 1.5 %collective-permute-start.2 = (bf16[96,768]{1,0:T(8,128)(2,1)S(1)}, bf16[96,768]{1,0:T(8,128)(2,1)S(1)}, u32[]{:S(2)}, u32[]{:S(2)}) collective-permute-start(bf16[96,768]{1,0:T(8,128)(2,1)S(1)} %get-tuple-element.45), channel_id=1, source_target_pairs={{0,8},{4,12},{8,0},{12,4},{1,9},{5,13},{9,1},{13,5},{2,10},{6,14},... | collective-permute-start | bytes 442376 | tf_op jit(solution)/shard_map/ppermute | solution.py:27
  8.7 5.2 %collective-permute-done.2.refs_1_ = bf16[96,768]{1,0:T(8,128)(2,1)S(1)} collective-permute-done((bf16[96,768]{1,0:T(8,128)(2,1)S(1)}, bf16[96,768]{1,0:T(8,128)(2,1)S(1)}, u32[]{:S(2)}, u32[]{:S(2)}) %collective-permute-start.2) | collective-permute-done | bytes 147488 | tf_op jit(solution)/shard_map/ppermute | solution.py:27
  14.0 1.1 collective-permute-done.3.refs_2_
  15.0 0.8 collective-permute-done.1.refs_0_
  15.9 0.1 first.1.refs_0_
  16.0 1.6 %collective-permute-start.4 = (bf16[272,1536]{1,0:T(8,128)(2,1)S(1)}, bf16[272,1536]{1,0:T(8,128)(2,1)S(1)}, u32[]{:S(2)}, u32[]{:S(2)}) collective-permute-start(bf16[272,1536]{1,0:T(8,128)(2,1)S(1)} %first.1.refs_0_), channel_id=1, source_target_pairs={{0,8},{4,12},{8,0},{12,4},{1,9},{5,13},{9,1},{13,5},{2,10},{6,14},... | collective-permute-start | bytes 2506760 | tf_op jit(solution)/shard_map/ppermute | solution.py:27
  17.5 0.6 collective-permute-start.6
  18.2 1.6 %collective-permute-start.5 = (bf16[2,96,768]{2,1,0:T(8,128)(2,1)S(1)}, bf16[2,96,768]{2,1,0:T(8,128)(2,1)}, u32[]{:S(2)}, u32[]{:S(2)}) collective-permute-start(bf16[2,96,768]{2,1,0:T(8,128)(2,1)S(1)} %collective-permute-done.1.refs_0_), channel_id=1, source_target_pairs={{0,1},{1,2},{2,3},{3,0},{4,5},{5,6},{6,7},{7,4},{8,9},{9,10},{10,1... | collective-permute-start | bytes 884744 | tf_op jit(solution)/shard_map/ppermute | solution.py:42
  19.8 9.5 %collective-permute-done.6.refs_1_ = bf16[2,96,768]{2,1,0:T(8,128)(2,1)S(1)} collective-permute-done((bf16[2,96,768]{2,1,0:T(8,128)(2,1)S(1)}, bf16[2,96,768]{2,1,0:T(8,128)(2,1)S(1)}, u32[]{:S(2)}, u32[]{:S(2)}) %collective-permute-start.6) | collective-permute-done | bytes 294944 | tf_op jit(solution)/shard_map/ppermute | solution.py:42
  29.3 6.4 %collective-permute-done.5.refs_1_.refs_0_ = bf16[2,96,768]{2,1,0:T(8,128)(2,1)} collective-permute-done((bf16[2,96,768]{2,1,0:T(8,128)(2,1)S(1)}, bf16[2,96,768]{2,1,0:T(8,128)(2,1)}, u32[]{:S(2)}, u32[]{:S(2)}) %collective-permute-start.5) | collective-permute-done | bytes 294944 | tf_op jit(solution)/shard_map/ppermute | solution.py:42
  35.7 5.2 %collective-permute-done.7.refs_2_.refs_1_ = bf16[2,96,768]{2,1,0:T(8,128)(2,1)} collective-permute-done((bf16[2,96,768]{2,1,0:T(8,128)(2,1)S(1)}, bf16[2,96,768]{2,1,0:T(8,128)(2,1)}, u32[]{:S(2)}, u32[]{:S(2)}) %collective-permute-start.7) | collective-permute-done | bytes 294944 | tf_op jit(solution)/shard_map/ppermute | solution.py:42
  40.9 0.1 collective-permute-start.10
  41.0 0.6 collective-permute-start.8
  41.6 1.2 collective-permute-start.12
  42.8 0.9 copy-done.17
  43.7 0.1 copy.26.times.refs_1_
  43.8 1.0 copy-done.4
  44.8 0.1 place0.1.refs_2_
  44.9 0.9 copy-done.6
  45.8 0.1 copy-done.8
  45.9 1.1 place2.1.refs_4_.refs_11_
  47.1 4.8 %norm.1 = (bf16[512,1536]{1,0:T(8,128)(2,1)S(1)}, bf16[512,1536]{1,0:T(8,128)(2,1)S(1)}, f32[512,128]{1,0:T(8,128)S(1)}, f32[512,128]{1,0:T(8,128)S(1)}, f32[512...) custom-call(s32[4,1]{1,0:T(4,128)S(1)} %copy.26.times.refs_1_, ...), custom_call_target="tpu_custom_call" | custom-call | tf_op jit(solution)/shard_map/norm/pallas_call | solution.py:446
  52.0 1.6 %collective-permute-done.11.refs_9_ = bf16[2,96,768]{2,1,0:T(8,128)(2,1)} collective-permute-done((bf16[2,96,768]{2,1,0:T(8,128)(2,1)}, bf16[2,96,768]{2,1,0:T(8,128)(2,1)}, u32[]{:S(2)}, u32[]{:S(2)}) %collective-permute-start.11) | collective-permute-done | bytes 294944 | tf_op jit(solution)/shard_map/ppermute | solution.py:42
  53.6 5.6 %collective-permute-done.12.refs_10_ = bf16[2,96,768]{2,1,0:T(8,128)(2,1)} collective-permute-done((bf16[2,96,768]{2,1,0:T(8,128)(2,1)}, bf16[2,96,768]{2,1,0:T(8,128)(2,1)}, u32[]{:S(2)}, u32[]{:S(2)}) %collective-permute-start.12) | collective-permute-done | bytes 294944 | tf_op jit(solution)/shard_map/ppermute | solution.py:42
  59.2 5.6 %step0.1 = (bf16[2,128,384]{2,1,0:T(8,128)(2,1)S(1)}, bf16[2,128,384]{2,1,0:T(8,128)(2,1)S(1)}, bf16[1536,768]{1,0:T(8,128)(2,1)S(1)}) custom-call(f32[1,16]{1,0:T(1,128)S(1)} %copy-done.15, s32[4,1]{1,0:T(4,128)S(1)} %copy.26.times.refs_1_, f32[1,1536]{1,0:T(1,128)S(1)} %copy-done.10, f32[1,1536]{1,0:T(1,128)S(1)} %copy-done.11, ...), custom_call_target="tpu_custom_call", output_to_operand_aliasing={{2}: (11, {})} | custom-call | flops 1610612736 | bytes 3145728 | tf_op jit(solution)/shard_map/step0/pallas_call | solution.py:446
  64.8 0.1 collective-permute-start.14
  64.9 1.6 %collective-permute-start.15 = (bf16[2,128,384]{2,1,0:T(8,128)(2,1)S(1)}, bf16[2,128,384]{2,1,0:T(8,128)(2,1)S(1)}, u32[]{:S(2)}, u32[]{:S(2)}) collective-permute-start(bf16[2,128,384]{2,1,0:T(8,128)(2,1)S(1)} %get-tuple-element.50.refs_1_.refs_0_), channel_id=1, source_target_pairs={{0,16},{16,0},{1,17},{17,1},{2,18},{18,2},{3,19},{19,3},{4,20},{20... | collective-permute-start | bytes 589832 | tf_op jit(solution)/shard_map/ppermute | solution.py:37
  66.5 0.5 collective-permute-start.19
  67.0 5.0 %step1.1 = (bf16[2,128,384]{2,1,0:T(8,128)(2,1)S(1)}, bf16[2,128,384]{2,1,0:T(8,128)(2,1)S(1)}) custom-call(f32[1,16]{1,0:T(1,128)S(1)} %copy-done.15, s32[4,1]{1,0:T(4,128)S(1)} %copy.26.times.refs_1_, f32[1,1536]{1,0:T(1,128)S(1)} %copy-done.10, f32[1,1536]{1,0:T(1,128)S(1)} %copy-done.11, f32[1,1536]{1,0:T(1,128)S(1)} %copy-done.14, ...), custom_call_target="tpu_custom_call" | custom-call | flops 1610612736 | bytes 3145728 | tf_op jit(solution)/shard_map/step1/pallas_call | solution.py:446
  72.0 1.6 %collective-permute-start.23 = (bf16[2,128,384]{2,1,0:T(8,128)(2,1)S(1)}, bf16[2,128,384]{2,1,0:T(8,128)(2,1)S(1)}, u32[]{:S(2)}, u32[]{:S(2)}) collective-permute-start(bf16[2,128,384]{2,1,0:T(8,128)(2,1)S(1)} %get-tuple-element.60.refs_2_), channel_id=1, source_target_pairs={{0,16},{16,0},{1,17},{17,1},{2,18},{18,2},{3,19},{19,3},{4,20},{20... | collective-permute-start | bytes 589832 | tf_op jit(solution)/shard_map/ppermute | solution.py:37
  73.6 3.6 %collective-permute-start.26 = (bf16[2,128,384]{2,1,0:T(8,128)(2,1)S(1)}, bf16[2,128,384]{2,1,0:T(8,128)(2,1)S(1)}, u32[]{:S(2)}, u32[]{:S(2)}) collective-permute-start(bf16[2,128,384]{2,1,0:T(8,128)(2,1)S(1)} %get-tuple-element.61.refs_3_), channel_id=1, source_target_pairs={{0,8},{4,12},{8,0},{12,4},{1,9},{5,13},{9,1},{13,5},{2,10},{6,14},... | collective-permute-start | bytes 589832 | tf_op jit(solution)/shard_map/ppermute | solution.py:33
  77.2 0.6 collective-permute-start.16
  77.8 1.5 %collective-permute-start.20 = (bf16[2,128,384]{2,1,0:T(8,128)(2,1)S(1)}, bf16[2,128,384]{2,1,0:T(8,128)(2,1)S(1)}, u32[]{:S(2)}, u32[]{:S(2)}) collective-permute-start(bf16[2,128,384]{2,1,0:T(8,128)(2,1)S(1)} %collective-permute-done.19.refs_15_), channel_id=1, source_target_pairs={{0,8},{4,12},{8,0},{12,4},{1,9},{5,13},{9,1},{13,5},{2,10},{6,14},... | collective-permute-start | bytes 589832 | tf_op jit(solution)/shard_map/ppermute | solution.py:27
  79.3 1.3 %collective-permute-done.23.refs_0_ = bf16[2,128,384]{2,1,0:T(8,128)(2,1)S(1)} collective-permute-done((bf16[2,128,384]{2,1,0:T(8,128)(2,1)S(1)}, bf16[2,128,384]{2,1,0:T(8,128)(2,1)S(1)}, u32[]{:S(2)}, u32[]{:S(2)}) %collective-permute-start.23) | collective-permute-done | bytes 196640 | tf_op jit(solution)/shard_map/ppermute | solution.py:37
  80.6 2.7 %collective-permute-done.26 = bf16[2,128,384]{2,1,0:T(8,128)(2,1)S(1)} collective-permute-done((bf16[2,128,384]{2,1,0:T(8,128)(2,1)S(1)}, bf16[2,128,384]{2,1,0:T(8,128)(2,1)S(1)}, u32[]{:S(2)}, u32[]{:S(2)}) %collective-permute-start.26) | collective-permute-done | bytes 196640 | tf_op jit(solution)/shard_map/ppermute | solution.py:33
  83.3 4.2 %collective-permute-done.16.refs_12_ = bf16[2,128,384]{2,1,0:T(8,128)(2,1)S(1)} collective-permute-done((bf16[2,128,384]{2,1,0:T(8,128)(2,1)S(1)}, bf16[2,128,384]{2,1,0:T(8,128)(2,1)S(1)}, u32[]{:S(2)}, u32[]{:S(2)}) %collective-permute-start.16) | collective-permute-done | bytes 196640 | tf_op jit(solution)/shard_map/ppermute | solution.py:27
  87.5 2.8 %collective-permute-done.20.refs_16_ = bf16[2,128,384]{2,1,0:T(8,128)(2,1)S(1)} collective-permute-done((bf16[2,128,384]{2,1,0:T(8,128)(2,1)S(1)}, bf16[2,128,384]{2,1,0:T(8,128)(2,1)S(1)}, u32[]{:S(2)}, u32[]{:S(2)}) %collective-permute-start.20) | collective-permute-done | bytes 196640 | tf_op jit(solution)/shard_map/ppermute | solution.py:27
  90.4 1.6 %collective-permute-start.24 = (bf16[2,128,384]{2,1,0:T(8,128)(2,1)S(1)}, bf16[2,128,384]{2,1,0:T(8,128)(2,1)S(1)}, u32[]{:S(2)}, u32[]{:S(2)}) collective-permute-start(bf16[2,128,384]{2,1,0:T(8,128)(2,1)S(1)} %collective-permute-done.23.refs_0_), channel_id=1, source_target_pairs={{0,8},{4,12},{8,0},{12,4},{1,9},{5,13},{9,1},{13,5},{2,10},{6,14},... | collective-permute-start | bytes 589832 | tf_op jit(solution)/shard_map/ppermute | solution.py:27
  91.9 1.9 %collective-permute-start.27 = (bf16[2,128,384]{2,1,0:T(8,128)(2,1)S(1)}, bf16[2,128,384]{2,1,0:T(8,128)(2,1)S(1)}, u32[]{:S(2)}, u32[]{:S(2)}) collective-permute-start(bf16[2,128,384]{2,1,0:T(8,128)(2,1)S(1)} %collective-permute-done.26), channel_id=1, source_target_pairs={{0,16},{16,0},{1,17},{17,1},{2,18},{18,2},{3,19},{19,3},{4,20},{20... | collective-permute-start | bytes 589832 | tf_op jit(solution)/shard_map/ppermute | solution.py:37
  93.9 5.8 %step2.1 = (bf16[2,128,384]{2,1,0:T(8,128)(2,1)S(1)}, bf16[2,128,384]{2,1,0:T(8,128)(2,1)S(1)}) custom-call(f32[1,16]{1,0:T(1,128)S(1)} %copy-done.15, s32[4,1]{1,0:T(4,128)S(1)} %copy.26.times.refs_1_, f32[1,1536]{1,0:T(1,128)S(1)} %copy-done.10, f32[1,1536]{1,0:T(1,128)S(1)} %copy-done.11, f32[1,1536]{1,0:T(1,128)S(1)} %copy-done.14, ...), custom_call_target="tpu_custom_call" | custom-call | flops 1610612736 | bytes 3145728 | tf_op jit(solution)/shard_map/step2/pallas_call | solution.py:446
  99.7 2.2 %collective-permute-done.27.refs_3_ = bf16[2,128,384]{2,1,0:T(8,128)(2,1)S(1)} collective-permute-done((bf16[2,128,384]{2,1,0:T(8,128)(2,1)S(1)}, bf16[2,128,384]{2,1,0:T(8,128)(2,1)S(1)}, u32[]{:S(2)}, u32[]{:S(2)}) %collective-permute-start.27) | collective-permute-done | bytes 196640 | tf_op jit(solution)/shard_map/ppermute | solution.py:37
  101.9 0.5 collective-permute-start.29
  102.4 0.5 collective-permute-start.31
  102.9 0.5 early.1
  103.4 0.1 collective-permute-start.32
  103.5 1.6 %collective-permute-start.33 = (bf16[2,128,384]{2,1,0:T(8,128)(2,1)S(1)}, bf16[2,128,384]{2,1,0:T(8,128)(2,1)S(1)}, u32[]{:S(2)}, u32[]{:S(2)}) collective-permute-start(bf16[2,128,384]{2,1,0:T(8,128)(2,1)S(1)} %get-tuple-element.70), channel_id=1, source_target_pairs={{0,8},{4,12},{8,0},{12,4},{1,9},{5,13},{9,1},{13,5},{2,10},{6,14},... | collective-permute-start | bytes 589832 | tf_op jit(solution)/shard_map/ppermute | solution.py:27
  105.0 0.3 collective-permute-start.34
  105.3 5.8 %step3.1 = (bf16[2,128,384]{2,1,0:T(8,128)(2,1)S(1)}, bf16[2,128,384]{2,1,0:T(8,128)(2,1)S(1)}) custom-call(f32[1,16]{1,0:T(1,128)S(1)} %copy-done.15, s32[4,1]{1,0:T(4,128)S(1)} %copy.26.times.refs_1_, f32[1,1536]{1,0:T(1,128)S(1)} %copy-done.10, f32[1,1536]{1,0:T(1,128)S(1)} %copy-done.11, f32[1,1536]{1,0:T(1,128)S(1)} %copy-done.14, ...), custom_call_target="tpu_custom_call" | custom-call | flops 1610612736 | bytes 3145728 | tf_op jit(solution)/shard_map/step3/pallas_call | solution.py:446
  111.1 0.1 collective-permute-done.33.refs_10_
  111.2 3.3 %collective-permute-done.34.refs_11_ = bf16[2,128,384]{2,1,0:T(8,128)(2,1)S(1)} collective-permute-done((bf16[2,128,384]{2,1,0:T(8,128)(2,1)S(1)}, bf16[2,128,384]{2,1,0:T(8,128)(2,1)S(1)}, u32[]{:S(2)}, u32[]{:S(2)}) %collective-permute-start.34) | collective-permute-done | bytes 196640 | tf_op jit(solution)/shard_map/ppermute | solution.py:27
  114.5 1.2 settle.1
  115.8 0.1 collective-permute-start.38
  115.8 0.4 collective-permute-start.35
  116.2 1.5 %collective-permute-start.36 = (bf16[128,384]{1,0:T(8,128)(2,1)S(1)}, bf16[128,384]{1,0:T(8,128)(2,1)S(1)}, u32[]{:S(2)}, u32[]{:S(2)}) collective-permute-start(bf16[128,384]{1,0:T(8,128)(2,1)S(1)} %get-tuple-element.76), channel_id=1, source_target_pairs={{0,8},{4,12},{8,0},{12,4},{1,9},{5,13},{9,1},{13,5},{2,10},{6,14},... | collective-permute-start | bytes 294920 | tf_op jit(solution)/shard_map/ppermute | solution.py:27
  117.7 0.1 collective-permute-start.37
  117.8 3.9 %collective-permute-done.38.refs_6_ = bf16[96,256]{1,0:T(8,128)(2,1)S(1)} collective-permute-done((bf16[96,256]{1,0:T(8,128)(2,1)S(1)}, bf16[96,256]{1,0:T(8,128)(2,1)S(1)}, u32[]{:S(2)}, u32[]{:S(2)}) %collective-permute-start.38) | collective-permute-done | bytes 49184 | tf_op jit(solution)/shard_map/ppermute | solution.py:42
  121.7 2.1 %collective-permute-done.39.refs_7_ = bf16[96,256]{1,0:T(8,128)(2,1)S(1)} collective-permute-done((bf16[96,256]{1,0:T(8,128)(2,1)S(1)}, bf16[96,256]{1,0:T(8,128)(2,1)S(1)}, u32[]{:S(2)}, u32[]{:S(2)}) %collective-permute-start.39) | collective-permute-done | bytes 49184 | tf_op jit(solution)/shard_map/ppermute | solution.py:42
  123.8 2.0 %collective-permute-done.40.refs_8_ = bf16[96,256]{1,0:T(8,128)(2,1)S(1)} collective-permute-done((bf16[96,256]{1,0:T(8,128)(2,1)S(1)}, bf16[96,256]{1,0:T(8,128)(2,1)S(1)}, u32[]{:S(2)}, u32[]{:S(2)}) %collective-permute-start.40) | collective-permute-done | bytes 49184 | tf_op jit(solution)/shard_map/ppermute | solution.py:42
  125.8 1.5 %finish.1 = (bf16[3,128,1536]{2,1,0:T(8,128)(2,1)}, f32[96,256]{1,0:T(8,128)}) custom-call(bf16[3,128,1536]{2,1,0:T(8,128)(2,1)} %get-tuple-element.73.refs_0_, bf16[128,384]{1,0:T(8,128)(2,1)S(1)} %get-tuple-element.74.refs_1_, bf16[128,384]{1,0:T(8,128)(2,1)S(1)} %collective-permute-done.35.refs_2_, ...), custom_call_target="tpu_custom_call", output_to_operand_aliasing={{0}: (0, {})} | custom-call | tf_op jit(solution)/shard_map/finish/pallas_call | solution.py:446
  (76 shorter events, 0.3 us)
Async XLA Ops:
  0.6 15.3 %copy-start.1 = (bf16[1,3,1,128,1536]{4,3,2,1,0:T(8,128)(2,1)S(1)}, bf16[1,3,1,128,1536]{4,3,2,1,0:T(8,128)(2,1)}, u32[]{:S(2)}) copy-start(bf16[1,3,1,128,1536]{4,3,2,1,0:T(8,128)(2,1)} %incoming.3) | copy-start | bytes 3538948
  0.6 15.3 %copy-start.16 = (s32[4,1,128]{2,1,0:T(1,128)S(1)}, s32[4,1,128]{2,1,0:T(1,128)}, u32[]{:S(2)}) copy-start(s32[4,1,128]{2,1,0:T(1,128)} %contacts.1) | copy-start | bytes 6148
  2.0 1.5 %collective-permute-start = (bf16[96,768]{1,0:T(8,128)(2,1)S(1)}, bf16[96,768]{1,0:T(8,128)(2,1)S(1)}, u32[]{:S(2)}, u32[]{:S(2)}) collective-permute-start(bf16[96,768]{1,0:T(8,128)(2,1)S(1)} %get-tuple-element.44), channel_id=1, source_target_pairs={{0,4},{4,0},{8,12},{12,8},{1,5},{5,1},{9,13},{13,9},{2,6},{6,2},{1... | collective-permute-start | bytes 442376 | tf_op jit(solution)/shard_map/ppermute | solution.py:27
  3.5 12.3 %collective-permute-start.1 = (bf16[2,96,768]{2,1,0:T(8,128)(2,1)S(1)}, bf16[2,96,768]{2,1,0:T(8,128)(2,1)S(1)}, u32[]{:S(2)}, u32[]{:S(2)}) collective-permute-start(bf16[2,96,768]{2,1,0:T(8,128)(2,1)S(1)} %near.1.refs_0_), channel_id=1, source_target_pairs={{0,1},{1,2},{2,3},{3,0},{4,5},{5,6},{6,7},{7,4},{8,9},{9,10},{10,1... | collective-permute-start | bytes 884744 | tf_op jit(solution)/shard_map/ppermute | solution.py:42
  6.5 0.7 copy-start.3
  7.2 6.7 %collective-permute-start.2 = (bf16[96,768]{1,0:T(8,128)(2,1)S(1)}, bf16[96,768]{1,0:T(8,128)(2,1)S(1)}, u32[]{:S(2)}, u32[]{:S(2)}) collective-permute-start(bf16[96,768]{1,0:T(8,128)(2,1)S(1)} %get-tuple-element.45), channel_id=1, source_target_pairs={{0,8},{4,12},{8,0},{12,4},{1,9},{5,13},{9,1},{13,5},{2,10},{6,14},... | collective-permute-start | bytes 442376 | tf_op jit(solution)/shard_map/ppermute | solution.py:27
  8.7 6.3 %collective-permute-start.3 = (bf16[96,768]{1,0:T(8,128)(2,1)S(1)}, bf16[96,768]{1,0:T(8,128)(2,1)S(1)}, u32[]{:S(2)}, u32[]{:S(2)}) collective-permute-start(bf16[96,768]{1,0:T(8,128)(2,1)S(1)} %get-tuple-element.46), channel_id=1, source_target_pairs={{0,12},{4,8},{8,4},{12,0},{1,13},{5,9},{9,5},{13,1},{2,14},{6,10},... | collective-permute-start | bytes 442376 | tf_op jit(solution)/shard_map/ppermute | solution.py:27
  15.9 2.3 %copy-start.5 = (bf16[2,96,768]{2,1,0:T(8,128)(2,1)}, bf16[2,96,768]{2,1,0:T(8,128)(2,1)S(1)}, u32[]{:S(2)}) copy-start(bf16[2,96,768]{2,1,0:T(8,128)(2,1)S(1)} %collective-permute-done.1.refs_0_) | copy-start | bytes 884740
  16.0 25.0 %copy-start.2 = (bf16[272,1536]{1,0:T(8,128)(2,1)}, bf16[272,1536]{1,0:T(8,128)(2,1)S(1)}, u32[]{:S(2)}) copy-start(bf16[272,1536]{1,0:T(8,128)(2,1)S(1)} %first.1.refs_0_) | copy-start | bytes 2506756
  16.0 25.0 %copy-start.9 = (bf16[1,3,1,128,256]{4,3,2,1,0:T(8,128)(2,1)S(1)}, bf16[1,3,1,128,256]{4,3,2,1,0:T(8,128)(2,1)}, u32[]{:S(2)}) copy-start(bf16[1,3,1,128,256]{4,3,2,1,0:T(8,128)(2,1)} %cotangent.1) | copy-start | bytes 589828
  16.0 24.9 %collective-permute-start.4 = (bf16[272,1536]{1,0:T(8,128)(2,1)S(1)}, bf16[272,1536]{1,0:T(8,128)(2,1)S(1)}, u32[]{:S(2)}, u32[]{:S(2)}) collective-permute-start(bf16[272,1536]{1,0:T(8,128)(2,1)S(1)} %first.1.refs_0_), channel_id=1, source_target_pairs={{0,8},{4,12},{8,0},{12,4},{1,9},{5,13},{9,1},{13,5},{2,10},{6,14},... | collective-permute-start | bytes 2506760 | tf_op jit(solution)/shard_map/ppermute | solution.py:27
  17.5 11.7 %collective-permute-start.6 = (bf16[2,96,768]{2,1,0:T(8,128)(2,1)S(1)}, bf16[2,96,768]{2,1,0:T(8,128)(2,1)S(1)}, u32[]{:S(2)}, u32[]{:S(2)}) collective-permute-start(bf16[2,96,768]{2,1,0:T(8,128)(2,1)S(1)} %far.1.refs_1_), channel_id=1, source_target_pairs={{0,1},{1,2},{2,3},{3,0},{4,5},{5,6},{6,7},{7,4},{8,9},{9,10},{10,1... | collective-permute-start | bytes 884744 | tf_op jit(solution)/shard_map/ppermute | solution.py:42
  18.2 17.5 %collective-permute-start.5 = (bf16[2,96,768]{2,1,0:T(8,128)(2,1)S(1)}, bf16[2,96,768]{2,1,0:T(8,128)(2,1)}, u32[]{:S(2)}, u32[]{:S(2)}) collective-permute-start(bf16[2,96,768]{2,1,0:T(8,128)(2,1)S(1)} %collective-permute-done.1.refs_0_), channel_id=1, source_target_pairs={{0,1},{1,2},{2,3},{3,0},{4,5},{5,6},{6,7},{7,4},{8,9},{9,10},{10,1... | collective-permute-start | bytes 884744 | tf_op jit(solution)/shard_map/ppermute | solution.py:42
  29.2 11.6 %copy-start.7 = (bf16[2,96,768]{2,1,0:T(8,128)(2,1)}, bf16[2,96,768]{2,1,0:T(8,128)(2,1)S(1)}, u32[]{:S(2)}) copy-start(bf16[2,96,768]{2,1,0:T(8,128)(2,1)S(1)} %collective-permute-done.6.refs_1_) | copy-start | bytes 884740
  29.2 11.6 %collective-permute-start.7 = (bf16[2,96,768]{2,1,0:T(8,128)(2,1)S(1)}, bf16[2,96,768]{2,1,0:T(8,128)(2,1)}, u32[]{:S(2)}, u32[]{:S(2)}) collective-permute-start(bf16[2,96,768]{2,1,0:T(8,128)(2,1)S(1)} %collective-permute-done.6.refs_1_), channel_id=1, source_target_pairs={{0,1},{1,2},{2,3},{3,0},{4,5},{5,6},{6,7},{7,4},{8,9},{9,10},{10,1... | collective-permute-start | bytes 884744 | tf_op jit(solution)/shard_map/ppermute | solution.py:42
  29.2 13.6 %collective-permute-start.9 = (bf16[272,1536]{1,0:T(8,128)(2,1)S(1)}, bf16[272,1536]{1,0:T(8,128)(2,1)S(1)}, u32[]{:S(2)}, u32[]{:S(2)}) collective-permute-start(bf16[272,1536]{1,0:T(8,128)(2,1)S(1)} %first.1.refs_0_), channel_id=1, source_target_pairs={{0,4},{4,0},{8,12},{12,8},{1,5},{5,1},{9,13},{13,9},{2,6},{6,2},{1... | collective-permute-start | bytes 2506760 | tf_op jit(solution)/shard_map/ppermute | solution.py:27
  40.8 4.0 %copy-start = (bf16[272,1536]{1,0:T(8,128)(2,1)}, bf16[272,1536]{1,0:T(8,128)(2,1)S(1)}, u32[]{:S(2)}) copy-start(bf16[272,1536]{1,0:T(8,128)(2,1)S(1)} %tie.3.dep.refs_1_) | copy-start | bytes 2506756
  40.9 2.9 %copy-start.18 = (s32[4,1]{0,1:T(1,128)S(1)}, s32[4,1]{0,1:T(1,128)}, u32[]{:S(2)}) copy-start(s32[4,1]{0,1:T(1,128)} %param.15) | copy-start | bytes 52
  40.9 6.2 %collective-permute-start.10 = (bf16[272,1536]{1,0:T(8,128)(2,1)S(1)}, bf16[272,1536]{1,0:T(8,128)(2,1)}, u32[]{:S(2)}, u32[]{:S(2)}) collective-permute-start(bf16[272,1536]{1,0:T(8,128)(2,1)S(1)} %tie.3.dep.refs_1_), channel_id=1, source_target_pairs={{0,4},{4,0},{8,12},{12,8},{1,5},{5,1},{9,13},{13,9},{2,6},{6,2},{1... | collective-permute-start | bytes 2506760 | tf_op jit(solution)/shard_map/ppermute | solution.py:27
  41.0 23.8 %collective-permute-start.8 = (bf16[256,1536]{1,0:T(8,128)(2,1)S(1)}, bf16[256,1536]{1,0:T(8,128)(2,1)S(1)}, u32[]{:S(2)}, u32[]{:S(2)}) collective-permute-start(bf16[256,1536]{1,0:T(8,128)(2,1)S(1)} %second.1.refs_6_.refs_4_), channel_id=1, source_target_pairs={{0,8},{4,12},{8,0},{12,4},{1,9},{5,13},{9,1},{13,5},{2,10},{6,14},... | collective-permute-start | bytes 2359304 | tf_op jit(solution)/shard_map/ppermute | solution.py:27
  41.6 12.0 %collective-permute-start.11 = (bf16[2,96,768]{2,1,0:T(8,128)(2,1)}, bf16[2,96,768]{2,1,0:T(8,128)(2,1)}, u32[]{:S(2)}, u32[]{:S(2)}) collective-permute-start(bf16[2,96,768]{2,1,0:T(8,128)(2,1)} %collective-permute-done.5.refs_1_.refs_0_), channel_id=1, source_target_pairs={{0,1},{1,2},{2,3},{3,0},{4,5},{5,6},{6,7},{7,4},{8,9},{9,10},{10,1... | collective-permute-start | bytes 884744 | tf_op jit(solution)/shard_map/ppermute | solution.py:42
  41.6 17.5 %collective-permute-start.12 = (bf16[2,96,768]{2,1,0:T(8,128)(2,1)}, bf16[2,96,768]{2,1,0:T(8,128)(2,1)}, u32[]{:S(2)}, u32[]{:S(2)}) collective-permute-start(bf16[2,96,768]{2,1,0:T(8,128)(2,1)} %collective-permute-done.7.refs_2_.refs_1_), channel_id=1, source_target_pairs={{0,1},{1,2},{2,3},{3,0},{4,5},{5,6},{6,7},{7,4},{8,9},{9,10},{10,1... | collective-permute-start | bytes 884744 | tf_op jit(solution)/shard_map/ppermute | solution.py:42
  42.8 0.9 copy-start.17
  43.7 29.9 %collective-permute-start.13 = (bf16[256,1536]{1,0:T(8,128)(2,1)S(1)}, bf16[256,1536]{1,0:T(8,128)(2,1)S(1)}, u32[]{:S(2)}, u32[]{:S(2)}) collective-permute-start(bf16[256,1536]{1,0:T(8,128)(2,1)S(1)} %second.1.refs_6_.refs_4_), channel_id=1, source_target_pairs={{0,4},{4,0},{8,12},{12,8},{1,5},{5,1},{9,13},{13,9},{2,6},{6,2},{1... | collective-permute-start | bytes 2359304 | tf_op jit(solution)/shard_map/ppermute | solution.py:27
  43.8 1.0 copy-start.4
  44.8 1.0 copy-start.6
  44.8 1.0 copy-start.8
  45.9 1.2 copy-start.10
  45.9 1.2 copy-start.11
  45.9 1.2 copy-start.12
  47.1 12.1 %copy-start.13 = (s32[4,1,512]{2,1,0:T(1,128)S(1)}, s32[4,1,512]{2,1,0:T(1,128)}, u32[]{:S(2)}) copy-start(s32[4,1,512]{2,1,0:T(1,128)} %refs_5_.7) | copy-start | bytes 24580
  47.1 12.1 %copy-start.14 = (f32[1,1536]{1,0:T(1,128)S(1)}, f32[1,1536]{1,0:T(1,128)}, u32[]{:S(2)}) copy-start(f32[1,1536]{1,0:T(1,128)} %refs_4_.7) | copy-start | bytes 18436
  47.1 12.1 %copy-start.15 = (f32[1,16]{1,0:T(1,128)S(1)}, f32[1,16]{1,0:T(1,128)}, u32[]{:S(2)}) copy-start(f32[1,16]{1,0:T(1,128)} %refs_0_.7) | copy-start | bytes 196
  64.8 29.1 %collective-permute-start.14 = (bf16[256,1536]{1,0:T(8,128)(2,1)S(1)}, bf16[256,1536]{1,0:T(8,128)(2,1)S(1)}, u32[]{:S(2)}, u32[]{:S(2)}) collective-permute-start(bf16[256,1536]{1,0:T(8,128)(2,1)S(1)} %tie.4.refs_7_.refs_5_), channel_id=1, source_target_pairs={{0,4},{4,0},{8,12},{12,8},{1,5},{5,1},{9,13},{13,9},{2,6},{6,2},{1... | collective-permute-start | bytes 2359304 | tf_op jit(solution)/shard_map/ppermute | solution.py:27
  64.9 12.3 %collective-permute-start.15 = (bf16[2,128,384]{2,1,0:T(8,128)(2,1)S(1)}, bf16[2,128,384]{2,1,0:T(8,128)(2,1)S(1)}, u32[]{:S(2)}, u32[]{:S(2)}) collective-permute-start(bf16[2,128,384]{2,1,0:T(8,128)(2,1)S(1)} %get-tuple-element.50.refs_1_.refs_0_), channel_id=1, source_target_pairs={{0,16},{16,0},{1,17},{17,1},{2,18},{18,2},{3,19},{19,3},{4,20},{20... | collective-permute-start | bytes 589832 | tf_op jit(solution)/shard_map/ppermute | solution.py:37
  66.5 11.3 %collective-permute-start.19 = (bf16[2,128,384]{2,1,0:T(8,128)(2,1)S(1)}, bf16[2,128,384]{2,1,0:T(8,128)(2,1)S(1)}, u32[]{:S(2)}, u32[]{:S(2)}) collective-permute-start(bf16[2,128,384]{2,1,0:T(8,128)(2,1)S(1)} %get-tuple-element.52.refs_1_), channel_id=1, source_target_pairs={{0,16},{16,0},{1,17},{17,1},{2,18},{18,2},{3,19},{19,3},{4,20},{20... | collective-permute-start | bytes 589832 | tf_op jit(solution)/shard_map/ppermute | solution.py:37
  72.0 8.6 %collective-permute-start.23 = (bf16[2,128,384]{2,1,0:T(8,128)(2,1)S(1)}, bf16[2,128,384]{2,1,0:T(8,128)(2,1)S(1)}, u32[]{:S(2)}, u32[]{:S(2)}) collective-permute-start(bf16[2,128,384]{2,1,0:T(8,128)(2,1)S(1)} %get-tuple-element.60.refs_2_), channel_id=1, source_target_pairs={{0,16},{16,0},{1,17},{17,1},{2,18},{18,2},{3,19},{19,3},{4,20},{20... | collective-permute-start | bytes 589832 | tf_op jit(solution)/shard_map/ppermute | solution.py:37
  73.6 9.7 %collective-permute-start.26 = (bf16[2,128,384]{2,1,0:T(8,128)(2,1)S(1)}, bf16[2,128,384]{2,1,0:T(8,128)(2,1)S(1)}, u32[]{:S(2)}, u32[]{:S(2)}) collective-permute-start(bf16[2,128,384]{2,1,0:T(8,128)(2,1)S(1)} %get-tuple-element.61.refs_3_), channel_id=1, source_target_pairs={{0,8},{4,12},{8,0},{12,4},{1,9},{5,13},{9,1},{13,5},{2,10},{6,14},... | collective-permute-start | bytes 589832 | tf_op jit(solution)/shard_map/ppermute | solution.py:33
  77.2 10.3 %collective-permute-start.16 = (bf16[2,128,384]{2,1,0:T(8,128)(2,1)S(1)}, bf16[2,128,384]{2,1,0:T(8,128)(2,1)S(1)}, u32[]{:S(2)}, u32[]{:S(2)}) collective-permute-start(bf16[2,128,384]{2,1,0:T(8,128)(2,1)S(1)} %collective-permute-done.15.refs_11_), channel_id=1, source_target_pairs={{0,8},{4,12},{8,0},{12,4},{1,9},{5,13},{9,1},{13,5},{2,10},{6,14},... | collective-permute-start | bytes 589832 | tf_op jit(solution)/shard_map/ppermute | solution.py:27
  77.8 12.5 %collective-permute-start.20 = (bf16[2,128,384]{2,1,0:T(8,128)(2,1)S(1)}, bf16[2,128,384]{2,1,0:T(8,128)(2,1)S(1)}, u32[]{:S(2)}, u32[]{:S(2)}) collective-permute-start(bf16[2,128,384]{2,1,0:T(8,128)(2,1)S(1)} %collective-permute-done.19.refs_15_), channel_id=1, source_target_pairs={{0,8},{4,12},{8,0},{12,4},{1,9},{5,13},{9,1},{13,5},{2,10},{6,14},... | collective-permute-start | bytes 589832 | tf_op jit(solution)/shard_map/ppermute | solution.py:27
  80.6 9.7 %collective-permute-start.17 = (bf16[2,128,384]{2,1,0:T(8,128)(2,1)S(1)}, bf16[2,128,384]{2,1,0:T(8,128)(2,1)S(1)}, u32[]{:S(2)}, u32[]{:S(2)}) collective-permute-start(bf16[2,128,384]{2,1,0:T(8,128)(2,1)S(1)} %collective-permute-done.15.refs_11_), channel_id=1, source_target_pairs={{0,4},{4,0},{8,12},{12,8},{1,5},{5,1},{9,13},{13,9},{2,6},{6,2},{1... | collective-permute-start | bytes 589832 | tf_op jit(solution)/shard_map/ppermute | solution.py:27
  83.3 7.0 %collective-permute-start.21 = (bf16[2,128,384]{2,1,0:T(8,128)(2,1)S(1)}, bf16[2,128,384]{2,1,0:T(8,128)(2,1)S(1)}, u32[]{:S(2)}, u32[]{:S(2)}) collective-permute-start(bf16[2,128,384]{2,1,0:T(8,128)(2,1)S(1)} %collective-permute-done.19.refs_15_), channel_id=1, source_target_pairs={{0,4},{4,0},{8,12},{12,8},{1,5},{5,1},{9,13},{13,9},{2,6},{6,2},{1... | collective-permute-start | bytes 589832 | tf_op jit(solution)/shard_map/ppermute | solution.py:27
  87.5 4.4 %collective-permute-start.18 = (bf16[2,128,384]{2,1,0:T(8,128)(2,1)S(1)}, bf16[2,128,384]{2,1,0:T(8,128)(2,1)S(1)}, u32[]{:S(2)}, u32[]{:S(2)}) collective-permute-start(bf16[2,128,384]{2,1,0:T(8,128)(2,1)S(1)} %collective-permute-done.16.refs_12_), channel_id=1, source_target_pairs={{0,4},{4,0},{8,12},{12,8},{1,5},{5,1},{9,13},{13,9},{2,6},{6,2},{1... | collective-permute-start | bytes 589832 | tf_op jit(solution)/shard_map/ppermute | solution.py:27
  90.3 3.5 %collective-permute-start.22 = (bf16[2,128,384]{2,1,0:T(8,128)(2,1)S(1)}, bf16[2,128,384]{2,1,0:T(8,128)(2,1)S(1)}, u32[]{:S(2)}, u32[]{:S(2)}) collective-permute-start(bf16[2,128,384]{2,1,0:T(8,128)(2,1)S(1)} %collective-permute-done.20.refs_16_), channel_id=1, source_target_pairs={{0,4},{4,0},{8,12},{12,8},{1,5},{5,1},{9,13},{13,9},{2,6},{6,2},{1... | collective-permute-start | bytes 589832 | tf_op jit(solution)/shard_map/ppermute | solution.py:27
  90.3 9.3 %collective-permute-start.25 = (bf16[2,128,384]{2,1,0:T(8,128)(2,1)S(1)}, bf16[2,128,384]{2,1,0:T(8,128)(2,1)S(1)}, u32[]{:S(2)}, u32[]{:S(2)}) collective-permute-start(bf16[2,128,384]{2,1,0:T(8,128)(2,1)S(1)} %get-tuple-element.61.refs_3_), channel_id=1, source_target_pairs={{0,16},{16,0},{1,17},{17,1},{2,18},{18,2},{3,19},{19,3},{4,20},{20... | collective-permute-start | bytes 589832 | tf_op jit(solution)/shard_map/ppermute | solution.py:37
  90.4 9.3 %collective-permute-start.24 = (bf16[2,128,384]{2,1,0:T(8,128)(2,1)S(1)}, bf16[2,128,384]{2,1,0:T(8,128)(2,1)S(1)}, u32[]{:S(2)}, u32[]{:S(2)}) collective-permute-start(bf16[2,128,384]{2,1,0:T(8,128)(2,1)S(1)} %collective-permute-done.23.refs_0_), channel_id=1, source_target_pairs={{0,8},{4,12},{8,0},{12,4},{1,9},{5,13},{9,1},{13,5},{2,10},{6,14},... | collective-permute-start | bytes 589832 | tf_op jit(solution)/shard_map/ppermute | solution.py:27
  91.9 9.9 %collective-permute-start.27 = (bf16[2,128,384]{2,1,0:T(8,128)(2,1)S(1)}, bf16[2,128,384]{2,1,0:T(8,128)(2,1)S(1)}, u32[]{:S(2)}, u32[]{:S(2)}) collective-permute-start(bf16[2,128,384]{2,1,0:T(8,128)(2,1)S(1)} %collective-permute-done.26), channel_id=1, source_target_pairs={{0,16},{16,0},{1,17},{17,1},{2,18},{18,2},{3,19},{19,3},{4,20},{20... | collective-permute-start | bytes 589832 | tf_op jit(solution)/shard_map/ppermute | solution.py:37
  101.9 1.6 %collective-permute-start.28 = (bf16[2,128,384]{2,1,0:T(8,128)(2,1)S(1)}, bf16[2,128,384]{2,1,0:T(8,128)(2,1)S(1)}, u32[]{:S(2)}, u32[]{:S(2)}) collective-permute-start(bf16[2,128,384]{2,1,0:T(8,128)(2,1)S(1)} %get-tuple-element.62.refs_11_), channel_id=1, source_target_pairs={{0,4},{4,0},{8,12},{12,8},{1,5},{5,1},{9,13},{13,9},{2,6},{6,2},{1... | collective-permute-start | bytes 589832 | tf_op jit(solution)/shard_map/ppermute | solution.py:27
  101.9 3.2 %collective-permute-start.29 = (bf16[2,128,384]{2,1,0:T(8,128)(2,1)S(1)}, bf16[2,128,384]{2,1,0:T(8,128)(2,1)S(1)}, u32[]{:S(2)}, u32[]{:S(2)}) collective-permute-start(bf16[2,128,384]{2,1,0:T(8,128)(2,1)S(1)} %get-tuple-element.63.refs_12_), channel_id=1, source_target_pairs={{0,4},{4,0},{8,12},{12,8},{1,5},{5,1},{9,13},{13,9},{2,6},{6,2},{1... | collective-permute-start | bytes 589832 | tf_op jit(solution)/shard_map/ppermute | solution.py:27
  102.4 3.0 %collective-permute-start.30 = (bf16[2,128,384]{2,1,0:T(8,128)(2,1)S(1)}, bf16[2,128,384]{2,1,0:T(8,128)(2,1)S(1)}, u32[]{:S(2)}, u32[]{:S(2)}) collective-permute-start(bf16[2,128,384]{2,1,0:T(8,128)(2,1)S(1)} %get-tuple-element.64.refs_15_), channel_id=1, source_target_pairs={{0,4},{4,0},{8,12},{12,8},{1,5},{5,1},{9,13},{13,9},{2,6},{6,2},{1... | collective-permute-start | bytes 589832 | tf_op jit(solution)/shard_map/ppermute | solution.py:27
  102.4 3.0 %collective-permute-start.31 = (bf16[2,128,384]{2,1,0:T(8,128)(2,1)S(1)}, bf16[2,128,384]{2,1,0:T(8,128)(2,1)S(1)}, u32[]{:S(2)}, u32[]{:S(2)}) collective-permute-start(bf16[2,128,384]{2,1,0:T(8,128)(2,1)S(1)} %get-tuple-element.65.refs_16_), channel_id=1, source_target_pairs={{0,4},{4,0},{8,12},{12,8},{1,5},{5,1},{9,13},{13,9},{2,6},{6,2},{1... | collective-permute-start | bytes 589832 | tf_op jit(solution)/shard_map/ppermute | solution.py:27
  103.4 7.7 %collective-permute-start.32 = (bf16[2,128,384]{2,1,0:T(8,128)(2,1)S(1)}, bf16[2,128,384]{2,1,0:T(8,128)(2,1)S(1)}, u32[]{:S(2)}, u32[]{:S(2)}) collective-permute-start(bf16[2,128,384]{2,1,0:T(8,128)(2,1)S(1)} %get-tuple-element.69), channel_id=1, source_target_pairs={{0,4},{4,0},{8,12},{12,8},{1,5},{5,1},{9,13},{13,9},{2,6},{6,2},{1... | collective-permute-start | bytes 589832 | tf_op jit(solution)/shard_map/ppermute | solution.py:27
  103.5 7.8 %collective-permute-start.33 = (bf16[2,128,384]{2,1,0:T(8,128)(2,1)S(1)}, bf16[2,128,384]{2,1,0:T(8,128)(2,1)S(1)}, u32[]{:S(2)}, u32[]{:S(2)}) collective-permute-start(bf16[2,128,384]{2,1,0:T(8,128)(2,1)S(1)} %get-tuple-element.70), channel_id=1, source_target_pairs={{0,8},{4,12},{8,0},{12,4},{1,9},{5,13},{9,1},{13,5},{2,10},{6,14},... | collective-permute-start | bytes 589832 | tf_op jit(solution)/shard_map/ppermute | solution.py:27
  105.0 9.5 %collective-permute-start.34 = (bf16[2,128,384]{2,1,0:T(8,128)(2,1)S(1)}, bf16[2,128,384]{2,1,0:T(8,128)(2,1)S(1)}, u32[]{:S(2)}, u32[]{:S(2)}) collective-permute-start(bf16[2,128,384]{2,1,0:T(8,128)(2,1)S(1)} %get-tuple-element.71), channel_id=1, source_target_pairs={{0,12},{4,8},{8,4},{12,0},{1,13},{5,9},{9,5},{13,1},{2,14},{6,10},... | collective-permute-start | bytes 589832 | tf_op jit(solution)/shard_map/ppermute | solution.py:27
  115.8 5.9 %collective-permute-start.38 = (bf16[96,256]{1,0:T(8,128)(2,1)S(1)}, bf16[96,256]{1,0:T(8,128)(2,1)S(1)}, u32[]{:S(2)}, u32[]{:S(2)}) collective-permute-start(bf16[96,256]{1,0:T(8,128)(2,1)S(1)} %get-tuple-element.79), channel_id=1, source_target_pairs={{0,1},{1,2},{2,3},{3,0},{4,5},{5,6},{6,7},{7,4},{8,9},{9,10},{10,1... | collective-permute-start | bytes 147464 | tf_op jit(solution)/shard_map/ppermute | solution.py:42
  115.8 10.0 %collective-permute-start.35 = (bf16[128,384]{1,0:T(8,128)(2,1)S(1)}, bf16[128,384]{1,0:T(8,128)(2,1)S(1)}, u32[]{:S(2)}, u32[]{:S(2)}) collective-permute-start(bf16[128,384]{1,0:T(8,128)(2,1)S(1)} %get-tuple-element.75), channel_id=1, source_target_pairs={{0,4},{4,0},{8,12},{12,8},{1,5},{5,1},{9,13},{13,9},{2,6},{6,2},{1... | collective-permute-start | bytes 294920 | tf_op jit(solution)/shard_map/ppermute | solution.py:27
  116.2 9.6 %collective-permute-start.36 = (bf16[128,384]{1,0:T(8,128)(2,1)S(1)}, bf16[128,384]{1,0:T(8,128)(2,1)S(1)}, u32[]{:S(2)}, u32[]{:S(2)}) collective-permute-start(bf16[128,384]{1,0:T(8,128)(2,1)S(1)} %get-tuple-element.76), channel_id=1, source_target_pairs={{0,8},{4,12},{8,0},{12,4},{1,9},{5,13},{9,1},{13,5},{2,10},{6,14},... | collective-permute-start | bytes 294920 | tf_op jit(solution)/shard_map/ppermute | solution.py:27
  117.7 8.1 %collective-permute-start.37 = (bf16[128,384]{1,0:T(8,128)(2,1)S(1)}, bf16[128,384]{1,0:T(8,128)(2,1)S(1)}, u32[]{:S(2)}, u32[]{:S(2)}) collective-permute-start(bf16[128,384]{1,0:T(8,128)(2,1)S(1)} %get-tuple-element.77), channel_id=1, source_target_pairs={{0,12},{4,8},{8,4},{12,0},{1,13},{5,9},{9,5},{13,1},{2,14},{6,10},... | collective-permute-start | bytes 294920 | tf_op jit(solution)/shard_map/ppermute | solution.py:27
  117.8 6.1 %collective-permute-start.39 = (bf16[96,256]{1,0:T(8,128)(2,1)S(1)}, bf16[96,256]{1,0:T(8,128)(2,1)S(1)}, u32[]{:S(2)}, u32[]{:S(2)}) collective-permute-start(bf16[96,256]{1,0:T(8,128)(2,1)S(1)} %get-tuple-element.80), channel_id=1, source_target_pairs={{0,2},{1,3},{2,0},{3,1},{4,6},{5,7},{6,4},{7,5},{8,10},{9,11},{10,... | collective-permute-start | bytes 147464 | tf_op jit(solution)/shard_map/ppermute | solution.py:42
  121.7 4.1 %collective-permute-start.40 = (bf16[96,256]{1,0:T(8,128)(2,1)S(1)}, bf16[96,256]{1,0:T(8,128)(2,1)S(1)}, u32[]{:S(2)}, u32[]{:S(2)}) collective-permute-start(bf16[96,256]{1,0:T(8,128)(2,1)S(1)} %get-tuple-element.81), channel_id=1, source_target_pairs={{0,3},{1,0},{2,1},{3,2},{4,7},{5,4},{6,5},{7,6},{8,11},{9,8},{10,9... | collective-permute-start | bytes 147464 | tf_op jit(solution)/shard_map/ppermute | solution.py:42

commit v9 on v8

--- a/solution.py
+++ b/solution.py
@@ -25,12 +25,6 @@
 def swap(value, bit):
     count = lax.axis_size("seq")
     return lax.ppermute(value, "seq", [(source, source ^ bit) for source in range(count)])
-
-
-def swap_within(section, value, bit):
-    count = lax.axis_size("seq")
-    pairs = [(section * count + i, section * count + (i ^ bit)) for i in range(count)]
-    return lax.ppermute(value, ("pipe", "seq"), pairs)
 
 
 def handed_over(value):
@@ -146,7 +140,7 @@
 
 
 def norm_kernel(turns, pieces, times, table, gain, freq, *refs):
-    sources, refs = refs[:pieces], refs[pieces + 1 :]
+    sources, refs = refs[:pieces], refs[pieces + 2 :]
     scaled, scales, owns, embeds, mod = refs[0:2], refs[2:4], refs[4:6], refs[6:8], refs[8]
     first, sems = refs[9 : 9 + pieces], refs[9 + pieces]
     copies = [
@@ -288,24 +282,33 @@
         keys.append(key.astype(jnp.bfloat16))
         values.append(value.astype(jnp.bfloat16))
 
-    def scores_of(h):
+    queries = []
+    for h in range(heads):
         strength = jnp.zeros((1, 128), jnp.float32) + bias[0, seq * heads + h] * math.log2(math.e)
         coarse = strength.astype(jnp.bfloat16).astype(jnp.float32)
         tail = jnp.where(
             row_lanes == head, coarse, jnp.where(row_lanes == head + 1, strength - coarse, 0.0)
         )
-        query = jnp.where(lanes < head, part_of(h * head), tail).astype(jnp.bfloat16)
+        queries.append(jnp.where(lanes < head, part_of(h * head), tail).astype(jnp.bfloat16))
+
+    def scores_of(h, at):
         return lax.dot_general(
-            query, keys[h // group], (((1,), (1,)), ((), ())), preferred_element_type=jnp.float32
-        )
-
-    scores = scores_of(0)
-    for h in range(heads):
-        ahead = scores_of(h + 1) if h + 1 < heads else None
+            queries[h][at : at + rows],
+            keys[h // group],
+            (((1,), (1,)), ((), ())),
+            preferred_element_type=jnp.float32,
+        )
+
+    tasks = [(h, at) for h in range(heads) for at in range(0, frames, rows)]
+    scores = scores_of(*tasks[0])
+    for index, (h, at) in enumerate(tasks):
+        ahead = scores_of(*tasks[index + 1]) if index + 1 < len(tasks) else None
         top = jnp.max(scores, axis=1, keepdims=True)
         weight = jnp.exp2(scores - top).astype(jnp.bfloat16)
         mixed = jnp.dot(weight, values[h // group], preferred_element_type=jnp.float32)
-        att[:, h * head : (h + 1) * head] = mixed[:, :head] * (1.0 / mixed[:, head : head + 1])
+        att[at : at + rows, h * head : (h + 1) * head] = mixed[:, :head] * (
+            1.0 / mixed[:, head : head + 1]
+        )
         scores = ahead
     own = pl.ds(pl.multiple_of(seq * cols, 128), cols)
     attended = att[...].astype(jnp.bfloat16).astype(jnp.float32)
@@ -528,7 +531,7 @@
     )
     across = swap(mine, 2)
     beside = swap(mine, 1)
-    (across,) = tie([across], [chunks[-1] for chunks in rings])
+    (across,) = tie([across], [last_chunk[0], rings[1][-1]])
     first = [mine, across, beside, swap(across, 1)]
     prepared = call(
         functools.partial(norm_kernel, turns, seq_count),
@@ -537,10 +540,10 @@
         + [pltpu.VMEM((frames, 128), jnp.float32)] * 2
         + [pltpu.VMEM((frames, cols), jnp.float32)] * 2
         + [pltpu.VMEM((frames, width), kind)] * 2,
-        [smem] + [vmem] * 3 + [anywhere] * (seq_count + 1),
+        [smem] + [vmem] * 3 + [anywhere] * (seq_count + 2),
         [timesteps, contact_table, norm_gain, time_freq]
         + [pin(piece, pltpu.HBM) for piece in first]
-        + [weights],
+        + [weights, last_chunk[0]],
         [pltpu.VMEM((1, width), jnp.float32)]
         + [pltpu.VMEM((2 * rows + 16, width), kind)] * seq_count
         + [pltpu.SemaphoreType.DMA((seq_count,))],
@@ -630,13 +633,9 @@
             early = [early[0]] + [swap(early[m], m) for m in range(1, seq_count)]
         if step + 2 < steps:
             crossing = []
-            for k, half in enumerate(outputs[-1]):
+            for half in outputs[-1]:
                 piece = handed_over(half)
-                if step == 1 and k == 1:
-                    across = handed_over(swap_within(0, half, 2))
-                else:
-                    across = swap(piece, 2)
-                crossing.append((piece, across))
+                crossing.append((piece, swap(piece, 2)))
             if step == 0:
                 relayed[2] = []
                 for mine, across in crossing:

time: 128 us -> 126 us (0.984)
  starting transfers between devices: 28.5 us -> 22.9 us
  Pallas kernels: 32.8 us -> 37.8 us
  waiting for transfers between devices: 61.1 us -> 58.9 us
    ppermute x5 -> x4, waiting for transfers between devices: 3.54 us -> 8.75 us  [handed_over(): return lax.ppermute(value, 'pipe', [(0, 1), (1, 0)])]
    pallas_call x19, Pallas kernels: 32.8 us -> 37.8 us  [call(): pl.pallas_call(kernel, out_shape=out_shape, in_specs=in_specs, scratch_sh...]
    ppermute x26 -> x27, waiting for transfers between devices: 17.8 us -> 14.2 us  [swap(): lax.ppermute(value, 'seq', [(source, source ^ bit) for source in range(co...]
    ppermute x1 -> x0, starting transfers between devices: 3.57 us -> none  [swap_within(): return lax.ppermute(value, ('pipe', 'seq'), pairs)]
    ppermute x1 -> x0, waiting for transfers between devices: 2.68 us -> none  [swap_within(): return lax.ppermute(value, ('pipe', 'seq'), pairs)]
    ppermute x5 -> x4, starting transfers between devices: 5.63 us -> 4.12 us  [handed_over(): return lax.ppermute(value, 'pipe', [(0, 1), (1, 0)])]
    unnamed x39 -> x43, local copies, waits for them, and re-layouts: 3.73 us -> 4.99 us
    ppermute x26 -> x27, starting transfers between devices: 12.9 us -> 12.4 us  [swap(): lax.ppermute(value, 'seq', [(source, source ^ bit) for source in range(co...]
  transfers between devices with their start and end apart: 41 -> 40, of which waited for: 19 -> 20; matrix products, arithmetic and copies ran while one was open for 0% -> 0% of each run, Pallas kernels for 23% -> 26%
where the time goes in v9:
time: 126 us
  waiting for transfers between devices  58.9 us (47%)
  Pallas kernels  37.8 us (30%)
  starting transfers between devices  22.9 us (18%)
  local copies, waits for them, and re-layouts  4.99 us (4%)
    pallas_call x19, Pallas kernels, call(): pl.pallas_call(kernel, out_shape=out_shape, in_specs=in_specs, scratch_sh...  37.8 us
    ppermute x9, waiting for transfers between devices, shifted(): lax.ppermute(value, axis, [(source, (source + shift) % count) for source...  36 us
    ppermute x27, waiting for transfers between devices, swap(): lax.ppermute(value, 'seq', [(source, source ^ bit) for source in range(co...  14.2 us
    ppermute x27, starting transfers between devices, swap(): lax.ppermute(value, 'seq', [(source, source ^ bit) for source in range(co...  12.4 us
    ppermute x4, waiting for transfers between devices, handed_over(): return lax.ppermute(value, 'pipe', [(0, 1), (1, 0)])  8.75 us
    ppermute x9, starting transfers between devices, shifted(): lax.ppermute(value, axis, [(source, (source + shift) % count) for source...  6.37 us
    unnamed x43, local copies, waits for them, and re-layouts  4.99 us
    ppermute x4, starting transfers between devices, handed_over(): return lax.ppermute(value, 'pipe', [(0, 1), (1, 0)])  4.12 us
  transfers between devices with their start and end apart: 40, of which 20 were waited for; matrix products, arithmetic and copies ran while one was open for 0% of the time, Pallas kernels for 26%

profile of v9, /device:TPU:0, one launch (start us, length us, event | category | flops | bytes accessed | tf_op | source)
XLA Modules:
  0.0 125.7 jit_solution(10941488336494548756)
XLA Ops:
  0.7 1.3 %pack.1 = (bf16[96,768]{1,0:T(8,128)(2,1)S(1)}, bf16[96,768]{1,0:T(8,128)(2,1)S(1)}, bf16[96,768]{1,0:T(8,128)(2,1)S(1)}, bf16[96,768]{1,0:T(8,128)(2,1)S(1)}) custom-call(bf16[1,96,1536]{2,1,0:T(8,128)(2,1)} %wq.1, bf16[1,96,1536]{2,1,0:T(8,128)(2,1)} %wkv.1), custom_call_target="tpu_custom_call" | custom-call | tf_op jit(solution)/shard_map/pack/pallas_call | solution.py:449
  2.0 0.5 collective-permute-start
  2.5 1.0 collective-permute-done.refs_1_
  3.5 3.0 %collective-permute-start.1 = (bf16[2,96,768]{2,1,0:T(8,128)(2,1)S(1)}, bf16[2,96,768]{2,1,0:T(8,128)(2,1)S(1)}, u32[]{:S(2)}, u32[]{:S(2)}) collective-permute-start(bf16[2,96,768]{2,1,0:T(8,128)(2,1)S(1)} %near.1.refs_0_), channel_id=1, source_target_pairs={{0,1},{1,2},{2,3},{3,0},{4,5},{5,6},{6,7},{7,4},{8,9},{9,10},{10,1... | collective-permute-start | bytes 884744 | tf_op jit(solution)/shard_map/ppermute | solution.py:36
  6.5 0.7 copy-done.4
  7.2 1.5 %collective-permute-start.2 = (bf16[96,768]{1,0:T(8,128)(2,1)S(1)}, bf16[96,768]{1,0:T(8,128)(2,1)S(1)}, u32[]{:S(2)}, u32[]{:S(2)}) collective-permute-start(bf16[96,768]{1,0:T(8,128)(2,1)S(1)} %get-tuple-element.45), channel_id=1, source_target_pairs={{0,8},{4,12},{8,0},{12,4},{1,9},{5,13},{9,1},{13,5},{2,10},{6,14},... | collective-permute-start | bytes 442376 | tf_op jit(solution)/shard_map/ppermute | solution.py:27
  8.7 5.2 %collective-permute-done.2.refs_1_ = bf16[96,768]{1,0:T(8,128)(2,1)S(1)} collective-permute-done((bf16[96,768]{1,0:T(8,128)(2,1)S(1)}, bf16[96,768]{1,0:T(8,128)(2,1)S(1)}, u32[]{:S(2)}, u32[]{:S(2)}) %collective-permute-start.2) | collective-permute-done | bytes 147488 | tf_op jit(solution)/shard_map/ppermute | solution.py:27
  14.0 1.1 collective-permute-done.3.refs_2_
  15.0 0.8 collective-permute-done.1.refs_0_
  15.9 1.0 first.1.refs_0_
  16.9 1.5 %collective-permute-start.4 = (bf16[272,1536]{1,0:T(8,128)(2,1)}, bf16[272,1536]{1,0:T(8,128)(2,1)S(1)}, u32[]{:S(2)}, u32[]{:S(2)}) collective-permute-start(bf16[272,1536]{1,0:T(8,128)(2,1)} %first.1.refs_0_), channel_id=1, source_target_pairs={{0,8},{4,12},{8,0},{12,4},{1,9},{5,13},{9,1},{13,5},{2,10},{6,14},... | collective-permute-start | bytes 2506760 | tf_op jit(solution)/shard_map/ppermute | solution.py:27
  18.4 0.6 collective-permute-start.7
  19.0 1.6 %collective-permute-start.5 = (bf16[2,96,768]{2,1,0:T(8,128)(2,1)S(1)}, bf16[2,96,768]{2,1,0:T(8,128)(2,1)S(1)}, u32[]{:S(2)}, u32[]{:S(2)}) collective-permute-start(bf16[2,96,768]{2,1,0:T(8,128)(2,1)S(1)} %collective-permute-done.1.refs_0_), channel_id=1, source_target_pairs={{0,1},{1,2},{2,3},{3,0},{4,5},{5,6},{6,7},{7,4},{8,9},{9,10},{10,1... | collective-permute-start | bytes 884744 | tf_op jit(solution)/shard_map/ppermute | solution.py:36
  20.6 9.5 %collective-permute-done.7.refs_1_ = bf16[2,96,768]{2,1,0:T(8,128)(2,1)S(1)} collective-permute-done((bf16[2,96,768]{2,1,0:T(8,128)(2,1)S(1)}, bf16[2,96,768]{2,1,0:T(8,128)(2,1)S(1)}, u32[]{:S(2)}, u32[]{:S(2)}) %collective-permute-start.7) | collective-permute-done | bytes 294944 | tf_op jit(solution)/shard_map/ppermute | solution.py:36
  30.1 6.3 %collective-permute-done.5.refs_0_ = bf16[2,96,768]{2,1,0:T(8,128)(2,1)S(1)} collective-permute-done((bf16[2,96,768]{2,1,0:T(8,128)(2,1)S(1)}, bf16[2,96,768]{2,1,0:T(8,128)(2,1)S(1)}, u32[]{:S(2)}, u32[]{:S(2)}) %collective-permute-start.5) | collective-permute-done | bytes 294944 | tf_op jit(solution)/shard_map/ppermute | solution.py:36
  36.4 0.7 copy-done.10
  37.1 5.7 %collective-permute-done.8.refs_2_.refs_1_ = bf16[2,96,768]{2,1,0:T(8,128)(2,1)} collective-permute-done((bf16[2,96,768]{2,1,0:T(8,128)(2,1)S(1)}, bf16[2,96,768]{2,1,0:T(8,128)(2,1)}, u32[]{:S(2)}, u32[]{:S(2)}) %collective-permute-start.8) | collective-permute-done | bytes 294944 | tf_op jit(solution)/shard_map/ppermute | solution.py:36
  42.8 5.1 %collective-permute-done.6.refs_1_.refs_5_.refs_9_ = bf16[2,96,768]{2,1,0:T(8,128)(2,1)S(1)} collective-permute-done((bf16[2,96,768]{2,1,0:T(8,128)(2,1)S(1)}, bf16[2,96,768]{2,1,0:T(8,128)(2,1)S(1)}, u32[]{:S(2)}, u32[]{:S(2)}) %collective-permute-start.6) | collective-permute-done | bytes 294944 | tf_op jit(solution)/shard_map/ppermute | solution.py:36
  47.9 0.1 collective-permute-start.11
  48.0 0.6 copy-done.2
  48.6 0.5 collective-permute-start.9
  49.1 0.1 copy.26.times.refs_1_
  49.2 1.0 copy-done.5
  50.3 0.9 copy-done.7
  51.2 0.1 copy-done.9
  51.3 0.9 copy-done.11
  52.2 1.1 place2.1.refs_4_.refs_11_
  53.4 4.8 %norm.1 = (bf16[512,1536]{1,0:T(8,128)(2,1)S(1)}, bf16[512,1536]{1,0:T(8,128)(2,1)S(1)}, f32[512,128]{1,0:T(8,128)S(1)}, f32[512,128]{1,0:T(8,128)S(1)}, f32[512...) custom-call(s32[4,1]{1,0:T(4,128)S(1)} %copy.26.times.refs_1_, ...), custom_call_target="tpu_custom_call" | custom-call | tf_op jit(solution)/shard_map/norm/pallas_call | solution.py:449
  58.2 1.7 %collective-permute-done.12.refs_10_ = bf16[2,96,768]{2,1,0:T(8,128)(2,1)} collective-permute-done((bf16[2,96,768]{2,1,0:T(8,128)(2,1)}, bf16[2,96,768]{2,1,0:T(8,128)(2,1)}, u32[]{:S(2)}, u32[]{:S(2)}) %collective-permute-start.12) | collective-permute-done | bytes 294944 | tf_op jit(solution)/shard_map/ppermute | solution.py:36
  59.9 6.5 %step0.1 = (bf16[2,128,384]{2,1,0:T(8,128)(2,1)S(1)}, bf16[2,128,384]{2,1,0:T(8,128)(2,1)S(1)}, bf16[1536,768]{1,0:T(8,128)(2,1)S(1)}) custom-call(f32[1,16]{1,0:T(1,128)S(1)} %copy-done.18, s32[4,1]{1,0:T(4,128)S(1)} %copy.26.times.refs_1_, f32[1,1536]{1,0:T(1,128)S(1)} %copy-done.13, f32[1,1536]{1,0:T(1,128)S(1)} %copy-done.14, ...), custom_call_target="tpu_custom_call", output_to_operand_aliasing={{2}: (11, {})} | custom-call | flops 1610612736 | bytes 3145728 | tf_op jit(solution)/shard_map/step0/pallas_call | solution.py:449
  66.4 1.7 %collective-permute-done.9.refs_0_ = bf16[256,1536]{1,0:T(8,128)(2,1)S(1)} collective-permute-done((bf16[256,1536]{1,0:T(8,128)(2,1)S(1)}, bf16[256,1536]{1,0:T(8,128)(2,1)S(1)}, u32[]{:S(2)}, u32[]{:S(2)}) %collective-permute-start.9) | collective-permute-done | bytes 786464 | tf_op jit(solution)/shard_map/ppermute | solution.py:27
  68.1 1.5 %collective-permute-start.15 = (bf16[2,128,384]{2,1,0:T(8,128)(2,1)S(1)}, bf16[2,128,384]{2,1,0:T(8,128)(2,1)S(1)}, u32[]{:S(2)}, u32[]{:S(2)}) collective-permute-start(bf16[2,128,384]{2,1,0:T(8,128)(2,1)S(1)} %get-tuple-element.50.refs_1_.refs_0_), channel_id=1, source_target_pairs={{0,16},{16,0},{1,17},{17,1},{2,18},{18,2},{3,19},{19,3},{4,20},{20... | collective-permute-start | bytes 589832 | tf_op jit(solution)/shard_map/ppermute | solution.py:31
  69.6 0.5 collective-permute-start.19
  70.1 6.0 %step1.1 = (bf16[2,128,384]{2,1,0:T(8,128)(2,1)S(1)}, bf16[2,128,384]{2,1,0:T(8,128)(2,1)S(1)}) custom-call(f32[1,16]{1,0:T(1,128)S(1)} %copy-done.18, s32[4,1]{1,0:T(4,128)S(1)} %copy.26.times.refs_1_, f32[1,1536]{1,0:T(1,128)S(1)} %copy-done.13, f32[1,1536]{1,0:T(1,128)S(1)} %copy-done.14, f32[1,1536]{1,0:T(1,128)S(1)} %copy-done.17, ...), custom_call_target="tpu_custom_call" | custom-call | flops 1610612736 | bytes 3145728 | tf_op jit(solution)/shard_map/step1/pallas_call | solution.py:449
  76.1 1.6 %collective-permute-start.23 = (bf16[2,128,384]{2,1,0:T(8,128)(2,1)S(1)}, bf16[2,128,384]{2,1,0:T(8,128)(2,1)S(1)}, u32[]{:S(2)}, u32[]{:S(2)}) collective-permute-start(bf16[2,128,384]{2,1,0:T(8,128)(2,1)S(1)} %get-tuple-element.60.refs_2_), channel_id=1, source_target_pairs={{0,16},{16,0},{1,17},{17,1},{2,18},{18,2},{3,19},{19,3},{4,20},{20... | collective-permute-start | bytes 589832 | tf_op jit(solution)/shard_map/ppermute | solution.py:31
  77.7 0.5 collective-permute-start.25
  78.2 0.6 collective-permute-start.16
  78.7 1.2 collective-permute-done.19.refs_15_
  80.0 0.5 collective-permute-start.20
  80.5 3.7 %collective-permute-done.23.refs_0_ = bf16[2,128,384]{2,1,0:T(8,128)(2,1)S(1)} collective-permute-done((bf16[2,128,384]{2,1,0:T(8,128)(2,1)S(1)}, bf16[2,128,384]{2,1,0:T(8,128)(2,1)S(1)}, u32[]{:S(2)}, u32[]{:S(2)}) %collective-permute-start.23) | collective-permute-done | bytes 196640 | tf_op jit(solution)/shard_map/ppermute | solution.py:31
  84.2 3.8 %collective-permute-done.25.refs_2_ = bf16[2,128,384]{2,1,0:T(8,128)(2,1)S(1)} collective-permute-done((bf16[2,128,384]{2,1,0:T(8,128)(2,1)S(1)}, bf16[2,128,384]{2,1,0:T(8,128)(2,1)S(1)}, u32[]{:S(2)}, u32[]{:S(2)}) %collective-permute-start.25) | collective-permute-done | bytes 196640 | tf_op jit(solution)/shard_map/ppermute | solution.py:31
  88.0 0.5 collective-permute-start.18
  88.6 0.6 collective-permute-start.24
  89.2 0.3 collective-permute-done.21.refs_17_
  89.5 1.2 collective-permute-start.26
  90.7 6.9 %step2.1 = (bf16[2,128,384]{2,1,0:T(8,128)(2,1)S(1)}, bf16[2,128,384]{2,1,0:T(8,128)(2,1)S(1)}) custom-call(f32[1,16]{1,0:T(1,128)S(1)} %copy-done.18, s32[4,1]{1,0:T(4,128)S(1)} %copy.26.times.refs_1_, f32[1,1536]{1,0:T(1,128)S(1)} %copy-done.13, f32[1,1536]{1,0:T(1,128)S(1)} %copy-done.14, f32[1,1536]{1,0:T(1,128)S(1)} %copy-done.17, ...), custom_call_target="tpu_custom_call" | custom-call | flops 1610612736 | bytes 3145728 | tf_op jit(solution)/shard_map/step2/pallas_call | solution.py:449
  97.6 2.5 %collective-permute-done.26.refs_3_ = bf16[2,128,384]{2,1,0:T(8,128)(2,1)S(1)} collective-permute-done((bf16[2,128,384]{2,1,0:T(8,128)(2,1)S(1)}, bf16[2,128,384]{2,1,0:T(8,128)(2,1)S(1)}, u32[]{:S(2)}, u32[]{:S(2)}) %collective-permute-start.26) | collective-permute-done | bytes 196640 | tf_op jit(solution)/shard_map/ppermute | solution.py:27
  100.1 0.5 collective-permute-start.28
  100.6 0.5 collective-permute-start.30
  101.1 0.5 early.1
  101.6 0.1 collective-permute-start.31
  101.7 0.6 collective-permute-start.32
  102.3 1.2 collective-permute-start.33
  103.6 6.9 %step3.1 = (bf16[2,128,384]{2,1,0:T(8,128)(2,1)S(1)}, bf16[2,128,384]{2,1,0:T(8,128)(2,1)S(1)}) custom-call(f32[1,16]{1,0:T(1,128)S(1)} %copy-done.18, s32[4,1]{1,0:T(4,128)S(1)} %copy.26.times.refs_1_, f32[1,1536]{1,0:T(1,128)S(1)} %copy-done.13, f32[1,1536]{1,0:T(1,128)S(1)} %copy-done.14, f32[1,1536]{1,0:T(1,128)S(1)} %copy-done.17, ...), custom_call_target="tpu_custom_call" | custom-call | flops 1610612736 | bytes 3145728 | tf_op jit(solution)/shard_map/step3/pallas_call | solution.py:449
  110.5 2.3 %collective-permute-done.33.refs_11_ = bf16[2,128,384]{2,1,0:T(8,128)(2,1)S(1)} collective-permute-done((bf16[2,128,384]{2,1,0:T(8,128)(2,1)S(1)}, bf16[2,128,384]{2,1,0:T(8,128)(2,1)S(1)}, u32[]{:S(2)}, u32[]{:S(2)}) %collective-permute-start.33) | collective-permute-done | bytes 196640 | tf_op jit(solution)/shard_map/ppermute | solution.py:27
  112.8 1.2 settle.1
  114.1 0.4 collective-permute-start.34
  114.4 0.5 collective-permute-start.35
  115.0 1.0 collective-permute-start.36
  116.0 1.1 collective-permute-start.38
  117.1 2.8 %collective-permute-done.37.refs_6_ = bf16[96,256]{1,0:T(8,128)(2,1)S(1)} collective-permute-done((bf16[96,256]{1,0:T(8,128)(2,1)S(1)}, bf16[96,256]{1,0:T(8,128)(2,1)S(1)}, u32[]{:S(2)}, u32[]{:S(2)}) %collective-permute-start.37) | collective-permute-done | bytes 49184 | tf_op jit(solution)/shard_map/ppermute | solution.py:36
  120.0 2.1 %collective-permute-done.38.refs_7_ = bf16[96,256]{1,0:T(8,128)(2,1)S(1)} collective-permute-done((bf16[96,256]{1,0:T(8,128)(2,1)S(1)}, bf16[96,256]{1,0:T(8,128)(2,1)S(1)}, u32[]{:S(2)}, u32[]{:S(2)}) %collective-permute-start.38) | collective-permute-done | bytes 49184 | tf_op jit(solution)/shard_map/ppermute | solution.py:36
  122.1 2.0 %collective-permute-done.39.refs_8_ = bf16[96,256]{1,0:T(8,128)(2,1)S(1)} collective-permute-done((bf16[96,256]{1,0:T(8,128)(2,1)S(1)}, bf16[96,256]{1,0:T(8,128)(2,1)S(1)}, u32[]{:S(2)}, u32[]{:S(2)}) %collective-permute-start.39) | collective-permute-done | bytes 49184 | tf_op jit(solution)/shard_map/ppermute | solution.py:36
  124.1 1.5 %finish.1 = (bf16[3,128,1536]{2,1,0:T(8,128)(2,1)}, f32[96,256]{1,0:T(8,128)}) custom-call(bf16[3,128,1536]{2,1,0:T(8,128)(2,1)} %get-tuple-element.73.refs_0_, bf16[128,384]{1,0:T(8,128)(2,1)S(1)} %get-tuple-element.74.refs_1_, bf16[128,384]{1,0:T(8,128)(2,1)S(1)} %collective-permute-done.34.refs_2_, ...), custom_call_target="tpu_custom_call", output_to_operand_aliasing={{0}: (0, {})} | custom-call | tf_op jit(solution)/shard_map/finish/pallas_call | solution.py:449
  (78 shorter events, 0.5 us)
Async XLA Ops:
  0.6 15.3 %copy-start.1 = (bf16[1,3,1,128,1536]{4,3,2,1,0:T(8,128)(2,1)S(1)}, bf16[1,3,1,128,1536]{4,3,2,1,0:T(8,128)(2,1)}, u32[]{:S(2)}) copy-start(bf16[1,3,1,128,1536]{4,3,2,1,0:T(8,128)(2,1)} %incoming.3) | copy-start | bytes 3538948
  0.6 15.3 %copy-start.19 = (s32[4,1,128]{2,1,0:T(1,128)S(1)}, s32[4,1,128]{2,1,0:T(1,128)}, u32[]{:S(2)}) copy-start(s32[4,1,128]{2,1,0:T(1,128)} %contacts.1) | copy-start | bytes 6148
  2.0 1.5 %collective-permute-start = (bf16[96,768]{1,0:T(8,128)(2,1)S(1)}, bf16[96,768]{1,0:T(8,128)(2,1)S(1)}, u32[]{:S(2)}, u32[]{:S(2)}) collective-permute-start(bf16[96,768]{1,0:T(8,128)(2,1)S(1)} %get-tuple-element.44), channel_id=1, source_target_pairs={{0,4},{4,0},{8,12},{12,8},{1,5},{5,1},{9,13},{13,9},{2,6},{6,2},{1... | collective-permute-start | bytes 442376 | tf_op jit(solution)/shard_map/ppermute | solution.py:27
  3.5 12.3 %collective-permute-start.1 = (bf16[2,96,768]{2,1,0:T(8,128)(2,1)S(1)}, bf16[2,96,768]{2,1,0:T(8,128)(2,1)S(1)}, u32[]{:S(2)}, u32[]{:S(2)}) collective-permute-start(bf16[2,96,768]{2,1,0:T(8,128)(2,1)S(1)} %near.1.refs_0_), channel_id=1, source_target_pairs={{0,1},{1,2},{2,3},{3,0},{4,5},{5,6},{6,7},{7,4},{8,9},{9,10},{10,1... | collective-permute-start | bytes 884744 | tf_op jit(solution)/shard_map/ppermute | solution.py:36
  6.5 0.7 copy-start.4
  7.2 6.7 %collective-permute-start.2 = (bf16[96,768]{1,0:T(8,128)(2,1)S(1)}, bf16[96,768]{1,0:T(8,128)(2,1)S(1)}, u32[]{:S(2)}, u32[]{:S(2)}) collective-permute-start(bf16[96,768]{1,0:T(8,128)(2,1)S(1)} %get-tuple-element.45), channel_id=1, source_target_pairs={{0,8},{4,12},{8,0},{12,4},{1,9},{5,13},{9,1},{13,5},{2,10},{6,14},... | collective-permute-start | bytes 442376 | tf_op jit(solution)/shard_map/ppermute | solution.py:27
  8.7 6.3 %collective-permute-start.3 = (bf16[96,768]{1,0:T(8,128)(2,1)S(1)}, bf16[96,768]{1,0:T(8,128)(2,1)S(1)}, u32[]{:S(2)}, u32[]{:S(2)}) collective-permute-start(bf16[96,768]{1,0:T(8,128)(2,1)S(1)} %get-tuple-element.46), channel_id=1, source_target_pairs={{0,12},{4,8},{8,4},{12,0},{1,13},{5,9},{9,5},{13,1},{2,14},{6,10},... | collective-permute-start | bytes 442376 | tf_op jit(solution)/shard_map/ppermute | solution.py:27
  15.9 3.1 %copy-start.6 = (bf16[2,96,768]{2,1,0:T(8,128)(2,1)}, bf16[2,96,768]{2,1,0:T(8,128)(2,1)S(1)}, u32[]{:S(2)}) copy-start(bf16[2,96,768]{2,1,0:T(8,128)(2,1)S(1)} %collective-permute-done.1.refs_0_) | copy-start | bytes 884740
  16.9 31.1 %copy-start.12 = (bf16[1,3,1,128,256]{4,3,2,1,0:T(8,128)(2,1)S(1)}, bf16[1,3,1,128,256]{4,3,2,1,0:T(8,128)(2,1)}, u32[]{:S(2)}) copy-start(bf16[1,3,1,128,256]{4,3,2,1,0:T(8,128)(2,1)} %cotangent.1) | copy-start | bytes 589828
  16.9 31.0 %collective-permute-start.4 = (bf16[272,1536]{1,0:T(8,128)(2,1)}, bf16[272,1536]{1,0:T(8,128)(2,1)S(1)}, u32[]{:S(2)}, u32[]{:S(2)}) collective-permute-start(bf16[272,1536]{1,0:T(8,128)(2,1)} %first.1.refs_0_), channel_id=1, source_target_pairs={{0,8},{4,12},{8,0},{12,4},{1,9},{5,13},{9,1},{13,5},{2,10},{6,14},... | collective-permute-start | bytes 2506760 | tf_op jit(solution)/shard_map/ppermute | solution.py:27
  18.4 11.7 %collective-permute-start.7 = (bf16[2,96,768]{2,1,0:T(8,128)(2,1)S(1)}, bf16[2,96,768]{2,1,0:T(8,128)(2,1)S(1)}, u32[]{:S(2)}, u32[]{:S(2)}) collective-permute-start(bf16[2,96,768]{2,1,0:T(8,128)(2,1)S(1)} %far.1.refs_1_), channel_id=1, source_target_pairs={{0,1},{1,2},{2,3},{3,0},{4,5},{5,6},{6,7},{7,4},{8,9},{9,10},{10,1... | collective-permute-start | bytes 884744 | tf_op jit(solution)/shard_map/ppermute | solution.py:36
  19.0 17.4 %collective-permute-start.5 = (bf16[2,96,768]{2,1,0:T(8,128)(2,1)S(1)}, bf16[2,96,768]{2,1,0:T(8,128)(2,1)S(1)}, u32[]{:S(2)}, u32[]{:S(2)}) collective-permute-start(bf16[2,96,768]{2,1,0:T(8,128)(2,1)S(1)} %collective-permute-done.1.refs_0_), channel_id=1, source_target_pairs={{0,1},{1,2},{2,3},{3,0},{4,5},{5,6},{6,7},{7,4},{8,9},{9,10},{10,1... | collective-permute-start | bytes 884744 | tf_op jit(solution)/shard_map/ppermute | solution.py:36
  30.1 18.0 %copy-start.8 = (bf16[2,96,768]{2,1,0:T(8,128)(2,1)}, bf16[2,96,768]{2,1,0:T(8,128)(2,1)S(1)}, u32[]{:S(2)}) copy-start(bf16[2,96,768]{2,1,0:T(8,128)(2,1)S(1)} %collective-permute-done.7.refs_1_) | copy-start | bytes 884740
  30.1 12.7 %collective-permute-start.8 = (bf16[2,96,768]{2,1,0:T(8,128)(2,1)S(1)}, bf16[2,96,768]{2,1,0:T(8,128)(2,1)}, u32[]{:S(2)}, u32[]{:S(2)}) collective-permute-start(bf16[2,96,768]{2,1,0:T(8,128)(2,1)S(1)} %collective-permute-done.7.refs_1_), channel_id=1, source_target_pairs={{0,1},{1,2},{2,3},{3,0},{4,5},{5,6},{6,7},{7,4},{8,9},{9,10},{10,1... | collective-permute-start | bytes 884744 | tf_op jit(solution)/shard_map/ppermute | solution.py:36
  36.4 11.5 %collective-permute-start.6 = (bf16[2,96,768]{2,1,0:T(8,128)(2,1)S(1)}, bf16[2,96,768]{2,1,0:T(8,128)(2,1)S(1)}, u32[]{:S(2)}, u32[]{:S(2)}) collective-permute-start(bf16[2,96,768]{2,1,0:T(8,128)(2,1)S(1)} %collective-permute-done.5.refs_0_), channel_id=1, source_target_pairs={{0,1},{1,2},{2,3},{3,0},{4,5},{5,6},{6,7},{7,4},{8,9},{9,10},{10,1... | collective-permute-start | bytes 884744 | tf_op jit(solution)/shard_map/ppermute | solution.py:36
  36.4 0.7 copy-start.10
  37.1 16.2 %collective-permute-start.10 = (bf16[272,1536]{1,0:T(8,128)(2,1)}, bf16[272,1536]{1,0:T(8,128)(2,1)}, u32[]{:S(2)}, u32[]{:S(2)}) collective-permute-start(bf16[272,1536]{1,0:T(8,128)(2,1)} %first.1.refs_0_), channel_id=1, source_target_pairs={{0,4},{4,0},{8,12},{12,8},{1,5},{5,1},{9,13},{13,9},{2,6},{6,2},{1... | collective-permute-start | bytes 2506760 | tf_op jit(solution)/shard_map/ppermute | solution.py:27
  47.9 0.7 copy-start.2
  47.9 2.4 %copy-start = (bf16[272,1536]{1,0:T(8,128)(2,1)}, bf16[272,1536]{1,0:T(8,128)(2,1)S(1)}, u32[]{:S(2)}) copy-start(bf16[272,1536]{1,0:T(8,128)(2,1)S(1)} %tie.3.dep.refs_1_) | copy-start | bytes 2506756
  47.9 1.3 copy-start.20
  47.9 5.4 %collective-permute-start.11 = (bf16[272,1536]{1,0:T(8,128)(2,1)S(1)}, bf16[272,1536]{1,0:T(8,128)(2,1)}, u32[]{:S(2)}, u32[]{:S(2)}) collective-permute-start(bf16[272,1536]{1,0:T(8,128)(2,1)S(1)} %tie.3.dep.refs_1_), channel_id=1, source_target_pairs={{0,4},{4,0},{8,12},{12,8},{1,5},{5,1},{9,13},{13,9},{2,6},{6,2},{1... | collective-permute-start | bytes 2506760 | tf_op jit(solution)/shard_map/ppermute | solution.py:27
  48.6 19.5 %collective-permute-start.9 = (bf16[256,1536]{1,0:T(8,128)(2,1)S(1)}, bf16[256,1536]{1,0:T(8,128)(2,1)S(1)}, u32[]{:S(2)}, u32[]{:S(2)}) collective-permute-start(bf16[256,1536]{1,0:T(8,128)(2,1)S(1)} %second.1.refs_6_.refs_4_), channel_id=1, source_target_pairs={{0,8},{4,12},{8,0},{12,4},{1,9},{5,13},{9,1},{13,5},{2,10},{6,14},... | collective-permute-start | bytes 2359304 | tf_op jit(solution)/shard_map/ppermute | solution.py:27
  49.1 10.8 %collective-permute-start.12 = (bf16[2,96,768]{2,1,0:T(8,128)(2,1)}, bf16[2,96,768]{2,1,0:T(8,128)(2,1)}, u32[]{:S(2)}, u32[]{:S(2)}) collective-permute-start(bf16[2,96,768]{2,1,0:T(8,128)(2,1)} %collective-permute-done.8.refs_2_.refs_1_), channel_id=1, source_target_pairs={{0,1},{1,2},{2,3},{3,0},{4,5},{5,6},{6,7},{7,4},{8,9},{9,10},{10,1... | collective-permute-start | bytes 884744 | tf_op jit(solution)/shard_map/ppermute | solution.py:36
  49.1 28.5 %collective-permute-start.13 = (bf16[256,1536]{1,0:T(8,128)(2,1)S(1)}, bf16[256,1536]{1,0:T(8,128)(2,1)S(1)}, u32[]{:S(2)}, u32[]{:S(2)}) collective-permute-start(bf16[256,1536]{1,0:T(8,128)(2,1)S(1)} %second.1.refs_6_.refs_4_), channel_id=1, source_target_pairs={{0,4},{4,0},{8,12},{12,8},{1,5},{5,1},{9,13},{13,9},{2,6},{6,2},{1... | collective-permute-start | bytes 2359304 | tf_op jit(solution)/shard_map/ppermute | solution.py:27
  49.2 1.0 copy-start.5
  50.2 1.0 copy-start.7
  50.2 1.0 copy-start.9
  51.3 1.0 copy-start.11
  52.2 1.1 copy-start.3
  52.2 1.1 copy-start.13
  52.2 1.1 copy-start.14
  52.2 1.2 copy-start.15
  53.3 6.6 %copy-start.16 = (s32[4,1,512]{2,1,0:T(1,128)S(1)}, s32[4,1,512]{2,1,0:T(1,128)}, u32[]{:S(2)}) copy-start(s32[4,1,512]{2,1,0:T(1,128)} %refs_5_.7) | copy-start | bytes 24580
  53.3 6.6 %copy-start.17 = (f32[1,1536]{1,0:T(1,128)S(1)}, f32[1,1536]{1,0:T(1,128)}, u32[]{:S(2)}) copy-start(f32[1,1536]{1,0:T(1,128)} %refs_4_.7) | copy-start | bytes 18436
  53.3 6.6 %copy-start.18 = (f32[1,16]{1,0:T(1,128)S(1)}, f32[1,16]{1,0:T(1,128)}, u32[]{:S(2)}) copy-start(f32[1,16]{1,0:T(1,128)} %refs_0_.7) | copy-start | bytes 196
  68.1 22.6 %collective-permute-start.14 = (bf16[256,1536]{1,0:T(8,128)(2,1)S(1)}, bf16[256,1536]{1,0:T(8,128)(2,1)S(1)}, u32[]{:S(2)}, u32[]{:S(2)}) collective-permute-start(bf16[256,1536]{1,0:T(8,128)(2,1)S(1)} %tie.4.refs_7_.refs_5_), channel_id=1, source_target_pairs={{0,4},{4,0},{8,12},{12,8},{1,5},{5,1},{9,13},{13,9},{2,6},{6,2},{1... | collective-permute-start | bytes 2359304 | tf_op jit(solution)/shard_map/ppermute | solution.py:27
  68.1 10.1 %collective-permute-start.15 = (bf16[2,128,384]{2,1,0:T(8,128)(2,1)S(1)}, bf16[2,128,384]{2,1,0:T(8,128)(2,1)S(1)}, u32[]{:S(2)}, u32[]{:S(2)}) collective-permute-start(bf16[2,128,384]{2,1,0:T(8,128)(2,1)S(1)} %get-tuple-element.50.refs_1_.refs_0_), channel_id=1, source_target_pairs={{0,16},{16,0},{1,17},{17,1},{2,18},{18,2},{3,19},{19,3},{4,20},{20... | collective-permute-start | bytes 589832 | tf_op jit(solution)/shard_map/ppermute | solution.py:31
  69.6 10.4 %collective-permute-start.19 = (bf16[2,128,384]{2,1,0:T(8,128)(2,1)S(1)}, bf16[2,128,384]{2,1,0:T(8,128)(2,1)S(1)}, u32[]{:S(2)}, u32[]{:S(2)}) collective-permute-start(bf16[2,128,384]{2,1,0:T(8,128)(2,1)S(1)} %get-tuple-element.52.refs_1_), channel_id=1, source_target_pairs={{0,16},{16,0},{1,17},{17,1},{2,18},{18,2},{3,19},{19,3},{4,20},{20... | collective-permute-start | bytes 589832 | tf_op jit(solution)/shard_map/ppermute | solution.py:31
  76.1 8.1 %collective-permute-start.23 = (bf16[2,128,384]{2,1,0:T(8,128)(2,1)S(1)}, bf16[2,128,384]{2,1,0:T(8,128)(2,1)S(1)}, u32[]{:S(2)}, u32[]{:S(2)}) collective-permute-start(bf16[2,128,384]{2,1,0:T(8,128)(2,1)S(1)} %get-tuple-element.60.refs_2_), channel_id=1, source_target_pairs={{0,16},{16,0},{1,17},{17,1},{2,18},{18,2},{3,19},{19,3},{4,20},{20... | collective-permute-start | bytes 589832 | tf_op jit(solution)/shard_map/ppermute | solution.py:31
  77.7 10.3 %collective-permute-start.25 = (bf16[2,128,384]{2,1,0:T(8,128)(2,1)S(1)}, bf16[2,128,384]{2,1,0:T(8,128)(2,1)S(1)}, u32[]{:S(2)}, u32[]{:S(2)}) collective-permute-start(bf16[2,128,384]{2,1,0:T(8,128)(2,1)S(1)} %get-tuple-element.61.refs_3_), channel_id=1, source_target_pairs={{0,16},{16,0},{1,17},{17,1},{2,18},{18,2},{3,19},{19,3},{4,20},{20... | collective-permute-start | bytes 589832 | tf_op jit(solution)/shard_map/ppermute | solution.py:31
  78.2 9.8 %collective-permute-start.16 = (bf16[2,128,384]{2,1,0:T(8,128)(2,1)S(1)}, bf16[2,128,384]{2,1,0:T(8,128)(2,1)S(1)}, u32[]{:S(2)}, u32[]{:S(2)}) collective-permute-start(bf16[2,128,384]{2,1,0:T(8,128)(2,1)S(1)} %collective-permute-done.15.refs_11_), channel_id=1, source_target_pairs={{0,8},{4,12},{8,0},{12,4},{1,9},{5,13},{9,1},{13,5},{2,10},{6,14},... | collective-permute-start | bytes 589832 | tf_op jit(solution)/shard_map/ppermute | solution.py:27
  80.0 8.6 %collective-permute-start.20 = (bf16[2,128,384]{2,1,0:T(8,128)(2,1)S(1)}, bf16[2,128,384]{2,1,0:T(8,128)(2,1)S(1)}, u32[]{:S(2)}, u32[]{:S(2)}) collective-permute-start(bf16[2,128,384]{2,1,0:T(8,128)(2,1)S(1)} %collective-permute-done.19.refs_15_), channel_id=1, source_target_pairs={{0,8},{4,12},{8,0},{12,4},{1,9},{5,13},{9,1},{13,5},{2,10},{6,14},... | collective-permute-start | bytes 589832 | tf_op jit(solution)/shard_map/ppermute | solution.py:27
  84.2 4.4 %collective-permute-start.17 = (bf16[2,128,384]{2,1,0:T(8,128)(2,1)S(1)}, bf16[2,128,384]{2,1,0:T(8,128)(2,1)S(1)}, u32[]{:S(2)}, u32[]{:S(2)}) collective-permute-start(bf16[2,128,384]{2,1,0:T(8,128)(2,1)S(1)} %collective-permute-done.15.refs_11_), channel_id=1, source_target_pairs={{0,4},{4,0},{8,12},{12,8},{1,5},{5,1},{9,13},{13,9},{2,6},{6,2},{1... | collective-permute-start | bytes 589832 | tf_op jit(solution)/shard_map/ppermute | solution.py:27
  88.0 1.4 %collective-permute-start.21 = (bf16[2,128,384]{2,1,0:T(8,128)(2,1)S(1)}, bf16[2,128,384]{2,1,0:T(8,128)(2,1)S(1)}, u32[]{:S(2)}, u32[]{:S(2)}) collective-permute-start(bf16[2,128,384]{2,1,0:T(8,128)(2,1)S(1)} %collective-permute-done.19.refs_15_), channel_id=1, source_target_pairs={{0,4},{4,0},{8,12},{12,8},{1,5},{5,1},{9,13},{13,9},{2,6},{6,2},{1... | collective-permute-start | bytes 589832 | tf_op jit(solution)/shard_map/ppermute | solution.py:27
  88.0 2.6 %collective-permute-start.18 = (bf16[2,128,384]{2,1,0:T(8,128)(2,1)S(1)}, bf16[2,128,384]{2,1,0:T(8,128)(2,1)S(1)}, u32[]{:S(2)}, u32[]{:S(2)}) collective-permute-start(bf16[2,128,384]{2,1,0:T(8,128)(2,1)S(1)} %collective-permute-done.16.refs_12_), channel_id=1, source_target_pairs={{0,4},{4,0},{8,12},{12,8},{1,5},{5,1},{9,13},{13,9},{2,6},{6,2},{1... | collective-permute-start | bytes 589832 | tf_op jit(solution)/shard_map/ppermute | solution.py:27
  88.6 2.1 %collective-permute-start.22 = (bf16[2,128,384]{2,1,0:T(8,128)(2,1)S(1)}, bf16[2,128,384]{2,1,0:T(8,128)(2,1)S(1)}, u32[]{:S(2)}, u32[]{:S(2)}) collective-permute-start(bf16[2,128,384]{2,1,0:T(8,128)(2,1)S(1)} %collective-permute-done.20.refs_16_), channel_id=1, source_target_pairs={{0,4},{4,0},{8,12},{12,8},{1,5},{5,1},{9,13},{13,9},{2,6},{6,2},{1... | collective-permute-start | bytes 589832 | tf_op jit(solution)/shard_map/ppermute | solution.py:27
  88.6 9.0 %collective-permute-start.24 = (bf16[2,128,384]{2,1,0:T(8,128)(2,1)S(1)}, bf16[2,128,384]{2,1,0:T(8,128)(2,1)S(1)}, u32[]{:S(2)}, u32[]{:S(2)}) collective-permute-start(bf16[2,128,384]{2,1,0:T(8,128)(2,1)S(1)} %collective-permute-done.23.refs_0_), channel_id=1, source_target_pairs={{0,8},{4,12},{8,0},{12,4},{1,9},{5,13},{9,1},{13,5},{2,10},{6,14},... | collective-permute-start | bytes 589832 | tf_op jit(solution)/shard_map/ppermute | solution.py:27
  89.5 10.7 %collective-permute-start.26 = (bf16[2,128,384]{2,1,0:T(8,128)(2,1)S(1)}, bf16[2,128,384]{2,1,0:T(8,128)(2,1)S(1)}, u32[]{:S(2)}, u32[]{:S(2)}) collective-permute-start(bf16[2,128,384]{2,1,0:T(8,128)(2,1)S(1)} %collective-permute-done.25.refs_2_), channel_id=1, source_target_pairs={{0,8},{4,12},{8,0},{12,4},{1,9},{5,13},{9,1},{13,5},{2,10},{6,14},... | collective-permute-start | bytes 589832 | tf_op jit(solution)/shard_map/ppermute | solution.py:27
  100.1 1.6 %collective-permute-start.27 = (bf16[2,128,384]{2,1,0:T(8,128)(2,1)S(1)}, bf16[2,128,384]{2,1,0:T(8,128)(2,1)S(1)}, u32[]{:S(2)}, u32[]{:S(2)}) collective-permute-start(bf16[2,128,384]{2,1,0:T(8,128)(2,1)S(1)} %get-tuple-element.62.refs_11_), channel_id=1, source_target_pairs={{0,4},{4,0},{8,12},{12,8},{1,5},{5,1},{9,13},{13,9},{2,6},{6,2},{1... | collective-permute-start | bytes 589832 | tf_op jit(solution)/shard_map/ppermute | solution.py:27
  100.1 2.2 %collective-permute-start.28 = (bf16[2,128,384]{2,1,0:T(8,128)(2,1)S(1)}, bf16[2,128,384]{2,1,0:T(8,128)(2,1)S(1)}, u32[]{:S(2)}, u32[]{:S(2)}) collective-permute-start(bf16[2,128,384]{2,1,0:T(8,128)(2,1)S(1)} %get-tuple-element.63.refs_12_), channel_id=1, source_target_pairs={{0,4},{4,0},{8,12},{12,8},{1,5},{5,1},{9,13},{13,9},{2,6},{6,2},{1... | collective-permute-start | bytes 589832 | tf_op jit(solution)/shard_map/ppermute | solution.py:27
  100.6 3.0 %collective-permute-start.29 = (bf16[2,128,384]{2,1,0:T(8,128)(2,1)S(1)}, bf16[2,128,384]{2,1,0:T(8,128)(2,1)S(1)}, u32[]{:S(2)}, u32[]{:S(2)}) collective-permute-start(bf16[2,128,384]{2,1,0:T(8,128)(2,1)S(1)} %get-tuple-element.64.refs_15_), channel_id=1, source_target_pairs={{0,4},{4,0},{8,12},{12,8},{1,5},{5,1},{9,13},{13,9},{2,6},{6,2},{1... | collective-permute-start | bytes 589832 | tf_op jit(solution)/shard_map/ppermute | solution.py:27
  100.6 3.0 %collective-permute-start.30 = (bf16[2,128,384]{2,1,0:T(8,128)(2,1)S(1)}, bf16[2,128,384]{2,1,0:T(8,128)(2,1)S(1)}, u32[]{:S(2)}, u32[]{:S(2)}) collective-permute-start(bf16[2,128,384]{2,1,0:T(8,128)(2,1)S(1)} %get-tuple-element.65.refs_16_), channel_id=1, source_target_pairs={{0,4},{4,0},{8,12},{12,8},{1,5},{5,1},{9,13},{13,9},{2,6},{6,2},{1... | collective-permute-start | bytes 589832 | tf_op jit(solution)/shard_map/ppermute | solution.py:27
  101.6 8.9 %collective-permute-start.31 = (bf16[2,128,384]{2,1,0:T(8,128)(2,1)S(1)}, bf16[2,128,384]{2,1,0:T(8,128)(2,1)S(1)}, u32[]{:S(2)}, u32[]{:S(2)}) collective-permute-start(bf16[2,128,384]{2,1,0:T(8,128)(2,1)S(1)} %get-tuple-element.69), channel_id=1, source_target_pairs={{0,4},{4,0},{8,12},{12,8},{1,5},{5,1},{9,13},{13,9},{2,6},{6,2},{1... | collective-permute-start | bytes 589832 | tf_op jit(solution)/shard_map/ppermute | solution.py:27
  101.7 8.8 %collective-permute-start.32 = (bf16[2,128,384]{2,1,0:T(8,128)(2,1)S(1)}, bf16[2,128,384]{2,1,0:T(8,128)(2,1)S(1)}, u32[]{:S(2)}, u32[]{:S(2)}) collective-permute-start(bf16[2,128,384]{2,1,0:T(8,128)(2,1)S(1)} %get-tuple-element.70), channel_id=1, source_target_pairs={{0,8},{4,12},{8,0},{12,4},{1,9},{5,13},{9,1},{13,5},{2,10},{6,14},... | collective-permute-start | bytes 589832 | tf_op jit(solution)/shard_map/ppermute | solution.py:27
  102.3 10.4 %collective-permute-start.33 = (bf16[2,128,384]{2,1,0:T(8,128)(2,1)S(1)}, bf16[2,128,384]{2,1,0:T(8,128)(2,1)S(1)}, u32[]{:S(2)}, u32[]{:S(2)}) collective-permute-start(bf16[2,128,384]{2,1,0:T(8,128)(2,1)S(1)} %get-tuple-element.71), channel_id=1, source_target_pairs={{0,12},{4,8},{8,4},{12,0},{1,13},{5,9},{9,5},{13,1},{2,14},{6,10},... | collective-permute-start | bytes 589832 | tf_op jit(solution)/shard_map/ppermute | solution.py:27
  114.0 5.9 %collective-permute-start.37 = (bf16[96,256]{1,0:T(8,128)(2,1)S(1)}, bf16[96,256]{1,0:T(8,128)(2,1)S(1)}, u32[]{:S(2)}, u32[]{:S(2)}) collective-permute-start(bf16[96,256]{1,0:T(8,128)(2,1)S(1)} %get-tuple-element.79), channel_id=1, source_target_pairs={{0,1},{1,2},{2,3},{3,0},{4,5},{5,6},{6,7},{7,4},{8,9},{9,10},{10,1... | collective-permute-start | bytes 147464 | tf_op jit(solution)/shard_map/ppermute | solution.py:36
  114.1 10.0 %collective-permute-start.34 = (bf16[128,384]{1,0:T(8,128)(2,1)S(1)}, bf16[128,384]{1,0:T(8,128)(2,1)S(1)}, u32[]{:S(2)}, u32[]{:S(2)}) collective-permute-start(bf16[128,384]{1,0:T(8,128)(2,1)S(1)} %get-tuple-element.75), channel_id=1, source_target_pairs={{0,4},{4,0},{8,12},{12,8},{1,5},{5,1},{9,13},{13,9},{2,6},{6,2},{1... | collective-permute-start | bytes 294920 | tf_op jit(solution)/shard_map/ppermute | solution.py:27
  114.4 9.6 %collective-permute-start.35 = (bf16[128,384]{1,0:T(8,128)(2,1)S(1)}, bf16[128,384]{1,0:T(8,128)(2,1)S(1)}, u32[]{:S(2)}, u32[]{:S(2)}) collective-permute-start(bf16[128,384]{1,0:T(8,128)(2,1)S(1)} %get-tuple-element.76), channel_id=1, source_target_pairs={{0,8},{4,12},{8,0},{12,4},{1,9},{5,13},{9,1},{13,5},{2,10},{6,14},... | collective-permute-start | bytes 294920 | tf_op jit(solution)/shard_map/ppermute | solution.py:27
  115.0 9.1 %collective-permute-start.36 = (bf16[128,384]{1,0:T(8,128)(2,1)S(1)}, bf16[128,384]{1,0:T(8,128)(2,1)S(1)}, u32[]{:S(2)}, u32[]{:S(2)}) collective-permute-start(bf16[128,384]{1,0:T(8,128)(2,1)S(1)} %get-tuple-element.77), channel_id=1, source_target_pairs={{0,12},{4,8},{8,4},{12,0},{1,13},{5,9},{9,5},{13,1},{2,14},{6,10},... | collective-permute-start | bytes 294920 | tf_op jit(solution)/shard_map/ppermute | solution.py:27
  116.0 6.1 %collective-permute-start.38 = (bf16[96,256]{1,0:T(8,128)(2,1)S(1)}, bf16[96,256]{1,0:T(8,128)(2,1)S(1)}, u32[]{:S(2)}, u32[]{:S(2)}) collective-permute-start(bf16[96,256]{1,0:T(8,128)(2,1)S(1)} %get-tuple-element.80), channel_id=1, source_target_pairs={{0,2},{1,3},{2,0},{3,1},{4,6},{5,7},{6,4},{7,5},{8,10},{9,11},{10,... | collective-permute-start | bytes 147464 | tf_op jit(solution)/shard_map/ppermute | solution.py:36
  120.0 4.1 %collective-permute-start.39 = (bf16[96,256]{1,0:T(8,128)(2,1)S(1)}, bf16[96,256]{1,0:T(8,128)(2,1)S(1)}, u32[]{:S(2)}, u32[]{:S(2)}) collective-permute-start(bf16[96,256]{1,0:T(8,128)(2,1)S(1)} %get-tuple-element.81), channel_id=1, source_target_pairs={{0,3},{1,0},{2,1},{3,2},{4,7},{5,4},{6,5},{7,6},{8,11},{9,8},{10,9... | collective-permute-start | bytes 147464 | tf_op jit(solution)/shard_map/ppermute | solution.py:36

commit v10 on v8

--- a/solution.py
+++ b/solution.py
@@ -27,12 +27,6 @@
     return lax.ppermute(value, "seq", [(source, source ^ bit) for source in range(count)])
 
 
-def swap_within(section, value, bit):
-    count = lax.axis_size("seq")
-    pairs = [(section * count + i, section * count + (i ^ bit)) for i in range(count)]
-    return lax.ppermute(value, ("pipe", "seq"), pairs)
-
-
 def handed_over(value):
     return lax.ppermute(value, "pipe", [(0, 1), (1, 0)])
 
@@ -40,6 +34,16 @@
 def shifted(value, axis, shift):
     count = lax.axis_size(axis)
     return lax.ppermute(value, axis, [(source, (source + shift) % count) for source in range(count)])
+
+
+def fold(index):
+    return index ^ (index >> 1)
+
+
+def ring_step(value):
+    count = lax.axis_size("dp")
+    pairs = [(fold(place), fold((place + 1) % count)) for place in range(count)]
+    return lax.ppermute(value, "dp", pairs)
 
 
 def offsets_of(count):
@@ -103,7 +107,7 @@
     for part in parts:
         count, rows = part.shape[:2]
         for j in range(count):
-            block = (seq ^ m) * hops + lax.rem(rep + hops - hop, hops)
+            block = (seq ^ m) * hops + fold(lax.rem(fold(rep) + hops - hop, hops))
             weights[pl.ds(pl.multiple_of(block * rows, 16), rows)] = part[j]
             m += 1
 
@@ -303,7 +307,7 @@
     for h in range(heads):
         ahead = scores_of(h + 1) if h + 1 < heads else None
         top = jnp.max(scores, axis=1, keepdims=True)
-        weight = jnp.exp2(scores - top).astype(jnp.bfloat16)
+        weight = jnp.exp2((scores - top).astype(jnp.bfloat16))
         mixed = jnp.dot(weight, values[h // group], preferred_element_type=jnp.float32)
         att[:, h * head : (h + 1) * head] = mixed[:, :head] * (1.0 / mixed[:, head : head + 1])
         scores = ahead
@@ -495,14 +499,14 @@
         )
 
     near = stacked("near", 2, [], blocks[:2])
-    near_next = shifted(near, "dp", 1)
+    near_next = ring_step(near)
     far = stacked("far", 2, [near_next], blocks[2:])
-    far_next = shifted(far, "dp", 1)
+    far_next = ring_step(far)
     rings = [[near, near_next], [far, far_next]]
     for hop in range(2, hops - 1):
         for chunks in rings:
-            chunks.append(shifted(chunks[-1], "dp", 1))
-    last_chunk = [shifted(chunks[-1], "dp", 1) for chunks in rings]
+            chunks.append(ring_step(chunks[-1]))
+    last_chunk = [ring_step(chunks[-1]) for chunks in rings]
     for hop in range(hops - 1):
         weights = placed(hop, [chunks[hop] for chunks in rings])
 
@@ -607,6 +611,7 @@
         outputs.append(list(results[:HALVES]))
         if step == 0:
             weights = results[HALVES]
+        if step == 0:
             (second[1],) = tie([second[1]], [outputs[-1][0]])
             second.append(swap(second[1], 1))
         if step == 2:
@@ -630,13 +635,9 @@
             early = [early[0]] + [swap(early[m], m) for m in range(1, seq_count)]
         if step + 2 < steps:
             crossing = []
-            for k, half in enumerate(outputs[-1]):
+            for half in outputs[-1]:
                 piece = handed_over(half)
-                if step == 1 and k == 1:
-                    across = handed_over(swap_within(0, half, 2))
-                else:
-                    across = swap(piece, 2)
-                crossing.append((piece, across))
+                crossing.append((piece, swap(piece, 2)))
             if step == 0:
                 relayed[2] = []
                 for mine, across in crossing:
@@ -682,6 +683,7 @@
     cols = w_query.shape[2] // count
     paired = (
         lax.axis_size("pipe") == 2
+        and lax.axis_size("dp") == 4
         and count == 4
         and cols % 128 == 0
         and w_query.shape[1] % 16 == 0

time: 128 us -> 121 us (0.945)
  waiting for transfers between devices: 61.1 us -> 46.9 us
  starting transfers between devices: 28.5 us -> 35.6 us
    ppermute x9 -> x3, waiting for transfers between devices: 37.1 us -> 3.79 us  [shifted(): lax.ppermute(value, axis, [(source, (source + shift) % count) for source...]
    ppermute x1 -> x6, waiting for transfers between devices: 2.68 us -> 21.5 us  [ring_step(): return lax.ppermute(value, 'dp', pairs)]
    ppermute x1 -> x6, starting transfers between devices: 3.57 us -> 12.2 us  [ring_step(): return lax.ppermute(value, 'dp', pairs)]
    ppermute x5 -> x4, waiting for transfers between devices: 3.54 us -> 7.71 us  [handed_over(): return lax.ppermute(value, 'pipe', [(0, 1), (1, 0)])]
    ppermute x26 -> x27, waiting for transfers between devices: 17.8 us -> 13.8 us  [swap(): lax.ppermute(value, 'seq', [(source, source ^ bit) for source in range(co...]
    ppermute x9 -> x3, starting transfers between devices: 6.49 us -> 4.38 us  [shifted(): lax.ppermute(value, axis, [(source, (source + shift) % count) for source...]
    ppermute x26 -> x27, starting transfers between devices: 12.9 us -> 14.9 us  [swap(): lax.ppermute(value, 'seq', [(source, source ^ bit) for source in range(co...]
    ppermute x5 -> x4, starting transfers between devices: 5.63 us -> 4.18 us  [handed_over(): return lax.ppermute(value, 'pipe', [(0, 1), (1, 0)])]
  transfers between devices with their start and end apart: 41 -> 40, of which waited for: 19 -> 16; matrix products, arithmetic and copies ran while one was open for 0% -> 0% of each run, Pallas kernels for 23% -> 24%
where the time goes in v10:
time: 121 us; the launch traced here: 120 us
  waiting for transfers between devices  46.9 us (39%)
  starting transfers between devices  35.6 us (29%)
  Pallas kernels  33.1 us (27%)
  local copies, waits for them, and re-layouts  3.72 us (3%)
    pallas_call x19, Pallas kernels, call(): pl.pallas_call(kernel, out_shape=out_shape, in_specs=in_specs, scratch_sh...  33.1 us
    ppermute x6, waiting for transfers between devices, ring_step(): return lax.ppermute(value, 'dp', pairs)  21.5 us
    ppermute x27, starting transfers between devices, swap(): lax.ppermute(value, 'seq', [(source, source ^ bit) for source in range(co...  14.9 us
    ppermute x27, waiting for transfers between devices, swap(): lax.ppermute(value, 'seq', [(source, source ^ bit) for source in range(co...  13.8 us
    ppermute x6, starting transfers between devices, ring_step(): return lax.ppermute(value, 'dp', pairs)  12.2 us
    ppermute x4, waiting for transfers between devices, handed_over(): return lax.ppermute(value, 'pipe', [(0, 1), (1, 0)])  7.71 us
    ppermute x3, starting transfers between devices, shifted(): lax.ppermute(value, axis, [(source, (source + shift) % count) for source...  4.38 us
    ppermute x4, starting transfers between devices, handed_over(): return lax.ppermute(value, 'pipe', [(0, 1), (1, 0)])  4.18 us
  transfers between devices with their start and end apart: 40, of which 16 were waited for; matrix products, arithmetic and copies ran while one was open for 0% of the time, Pallas kernels for 24%

profile of v10, /device:TPU:0, one launch (start us, length us, event | category | flops | bytes accessed | tf_op | source)
XLA Modules:
  0.0 120.5 jit_solution(17853685564892320082)
XLA Ops:
  0.7 1.3 %pack.1 = (bf16[96,768]{1,0:T(8,128)(2,1)S(1)}, bf16[96,768]{1,0:T(8,128)(2,1)S(1)}, bf16[96,768]{1,0:T(8,128)(2,1)S(1)}, bf16[96,768]{1,0:T(8,128)(2,1)S(1)}) custom-call(bf16[1,96,1536]{2,1,0:T(8,128)(2,1)} %wq.1, bf16[1,96,1536]{2,1,0:T(8,128)(2,1)} %wkv.1), custom_call_target="tpu_custom_call" | custom-call | tf_op jit(solution)/shard_map/pack/pallas_call | solution.py:450
  2.0 0.5 collective-permute-start
  2.5 1.0 collective-permute-done.refs_1_
  3.5 3.0 %collective-permute-start.1 = (bf16[2,96,768]{2,1,0:T(8,128)(2,1)S(1)}, bf16[2,96,768]{2,1,0:T(8,128)(2,1)S(1)}, u32[]{:S(2)}, u32[]{:S(2)}) collective-permute-start(bf16[2,96,768]{2,1,0:T(8,128)(2,1)S(1)} %near.1.refs_0_), channel_id=1, source_target_pairs={{0,1},{1,3},{3,2},{2,0},{4,5},{5,7},{7,6},{6,4},{8,9},{9,11},{11,1... | collective-permute-start | bytes 884744 | tf_op jit(solution)/shard_map/ppermute | solution.py:46
  6.5 0.7 copy-done.3
  7.2 1.5 %collective-permute-start.2 = (bf16[96,768]{1,0:T(8,128)(2,1)S(1)}, bf16[96,768]{1,0:T(8,128)(2,1)S(1)}, u32[]{:S(2)}, u32[]{:S(2)}) collective-permute-start(bf16[96,768]{1,0:T(8,128)(2,1)S(1)} %get-tuple-element.45), channel_id=1, source_target_pairs={{0,8},{4,12},{8,0},{12,4},{1,9},{5,13},{9,1},{13,5},{2,10},{6,14},... | collective-permute-start | bytes 442376 | tf_op jit(solution)/shard_map/ppermute | solution.py:27
  8.7 5.2 %collective-permute-done.2.refs_1_ = bf16[96,768]{1,0:T(8,128)(2,1)S(1)} collective-permute-done((bf16[96,768]{1,0:T(8,128)(2,1)S(1)}, bf16[96,768]{1,0:T(8,128)(2,1)S(1)}, u32[]{:S(2)}, u32[]{:S(2)}) %collective-permute-start.2) | collective-permute-done | bytes 147488 | tf_op jit(solution)/shard_map/ppermute | solution.py:27
  13.9 1.1 collective-permute-done.3.refs_2_
  15.1 1.4 %collective-permute-start.4 = (bf16[272,1536]{1,0:T(8,128)(2,1)S(1)}, bf16[272,1536]{1,0:T(8,128)(2,1)S(1)}, u32[]{:S(2)}, u32[]{:S(2)}) collective-permute-start(bf16[272,1536]{1,0:T(8,128)(2,1)S(1)} %first.1.refs_0_), channel_id=1, source_target_pairs={{0,8},{4,12},{8,0},{12,4},{1,9},{5,13},{9,1},{13,5},{2,10},{6,14},... | collective-permute-start | bytes 2506760 | tf_op jit(solution)/shard_map/ppermute | solution.py:27
  16.6 2.6 %collective-permute-start.6 = (bf16[2,96,768]{2,1,0:T(8,128)(2,1)S(1)}, bf16[2,96,768]{2,1,0:T(8,128)(2,1)S(1)}, u32[]{:S(2)}, u32[]{:S(2)}) collective-permute-start(bf16[2,96,768]{2,1,0:T(8,128)(2,1)S(1)} %far.1.refs_1_), channel_id=1, source_target_pairs={{0,1},{1,3},{3,2},{2,0},{4,5},{5,7},{7,6},{6,4},{8,9},{9,11},{11,1... | collective-permute-start | bytes 884744 | tf_op jit(solution)/shard_map/ppermute | solution.py:46
  19.2 1.6 %collective-permute-start.5 = (bf16[2,96,768]{2,1,0:T(8,128)(2,1)S(1)}, bf16[2,96,768]{2,1,0:T(8,128)(2,1)}, u32[]{:S(2)}, u32[]{:S(2)}) collective-permute-start(bf16[2,96,768]{2,1,0:T(8,128)(2,1)S(1)} %collective-permute-done.1.refs_0_), channel_id=1, source_target_pairs={{0,1},{1,3},{3,2},{2,0},{4,5},{5,7},{7,6},{6,4},{8,9},{9,11},{11,1... | collective-permute-start | bytes 884744 | tf_op jit(solution)/shard_map/ppermute | solution.py:46
  20.8 6.6 %collective-permute-done.6.refs_1_ = bf16[2,96,768]{2,1,0:T(8,128)(2,1)S(1)} collective-permute-done((bf16[2,96,768]{2,1,0:T(8,128)(2,1)S(1)}, bf16[2,96,768]{2,1,0:T(8,128)(2,1)S(1)}, u32[]{:S(2)}, u32[]{:S(2)}) %collective-permute-start.6) | collective-permute-done | bytes 294944 | tf_op jit(solution)/shard_map/ppermute | solution.py:46
  27.4 1.7 %collective-permute-start.7 = (bf16[2,96,768]{2,1,0:T(8,128)(2,1)S(1)}, bf16[2,96,768]{2,1,0:T(8,128)(2,1)}, u32[]{:S(2)}, u32[]{:S(2)}) collective-permute-start(bf16[2,96,768]{2,1,0:T(8,128)(2,1)S(1)} %collective-permute-done.6.refs_1_), channel_id=1, source_target_pairs={{0,1},{1,3},{3,2},{2,0},{4,5},{5,7},{7,6},{6,4},{8,9},{9,11},{11,1... | collective-permute-start | bytes 884744 | tf_op jit(solution)/shard_map/ppermute | solution.py:46
  29.0 4.7 %collective-permute-done.5.refs_1_.refs_0_ = bf16[2,96,768]{2,1,0:T(8,128)(2,1)} collective-permute-done((bf16[2,96,768]{2,1,0:T(8,128)(2,1)S(1)}, bf16[2,96,768]{2,1,0:T(8,128)(2,1)}, u32[]{:S(2)}, u32[]{:S(2)}) %collective-permute-start.5) | collective-permute-done | bytes 294944 | tf_op jit(solution)/shard_map/ppermute | solution.py:46
  33.8 6.0 %collective-permute-done.7.refs_2_.refs_1_ = bf16[2,96,768]{2,1,0:T(8,128)(2,1)} collective-permute-done((bf16[2,96,768]{2,1,0:T(8,128)(2,1)S(1)}, bf16[2,96,768]{2,1,0:T(8,128)(2,1)}, u32[]{:S(2)}, u32[]{:S(2)}) %collective-permute-start.7) | collective-permute-done | bytes 294944 | tf_op jit(solution)/shard_map/ppermute | solution.py:46
  39.8 0.1 collective-permute-start.10
  40.0 0.6 collective-permute-start.8
  40.6 1.7 %collective-permute-start.11 = (bf16[2,96,768]{2,1,0:T(8,128)(2,1)}, bf16[2,96,768]{2,1,0:T(8,128)(2,1)}, u32[]{:S(2)}, u32[]{:S(2)}) collective-permute-start(bf16[2,96,768]{2,1,0:T(8,128)(2,1)} %collective-permute-done.5.refs_1_.refs_0_), channel_id=1, source_target_pairs={{0,1},{1,3},{3,2},{2,0},{4,5},{5,7},{7,6},{6,4},{8,9},{9,11},{11,1... | collective-permute-start | bytes 884744 | tf_op jit(solution)/shard_map/ppermute | solution.py:46
  42.2 1.6 %collective-permute-start.12 = (bf16[2,96,768]{2,1,0:T(8,128)(2,1)}, bf16[2,96,768]{2,1,0:T(8,128)(2,1)}, u32[]{:S(2)}, u32[]{:S(2)}) collective-permute-start(bf16[2,96,768]{2,1,0:T(8,128)(2,1)} %collective-permute-done.7.refs_2_.refs_1_), channel_id=1, source_target_pairs={{0,1},{1,3},{3,2},{2,0},{4,5},{5,7},{7,6},{6,4},{8,9},{9,11},{11,1... | collective-permute-start | bytes 884744 | tf_op jit(solution)/shard_map/ppermute | solution.py:46
  43.9 0.9 copy-done.17
  44.8 0.1 copy.26.times.refs_1_
  44.9 1.0 copy-done.4
  45.9 0.9 copy-done.6
  46.8 0.1 copy-done.8
  47.0 1.1 place2.1.refs_4_.refs_11_
  48.2 4.8 %norm.1 = (bf16[512,1536]{1,0:T(8,128)(2,1)S(1)}, bf16[512,1536]{1,0:T(8,128)(2,1)S(1)}, f32[512,128]{1,0:T(8,128)S(1)}, f32[512,128]{1,0:T(8,128)S(1)}, f32[512...) custom-call(s32[4,1]{1,0:T(4,128)S(1)} %copy.26.times.refs_1_, ...), custom_call_target="tpu_custom_call" | custom-call | tf_op jit(solution)/shard_map/norm/pallas_call | solution.py:450
  53.0 4.2 %collective-permute-done.12.refs_10_ = bf16[2,96,768]{2,1,0:T(8,128)(2,1)} collective-permute-done((bf16[2,96,768]{2,1,0:T(8,128)(2,1)}, bf16[2,96,768]{2,1,0:T(8,128)(2,1)}, u32[]{:S(2)}, u32[]{:S(2)}) %collective-permute-start.12) | collective-permute-done | bytes 294944 | tf_op jit(solution)/shard_map/ppermute | solution.py:46
  57.2 5.6 %step0.1 = (bf16[2,128,384]{2,1,0:T(8,128)(2,1)S(1)}, bf16[2,128,384]{2,1,0:T(8,128)(2,1)S(1)}, bf16[1536,768]{1,0:T(8,128)(2,1)S(1)}) custom-call(f32[1,16]{1,0:T(1,128)S(1)} %copy-done.15, s32[4,1]{1,0:T(4,128)S(1)} %copy.26.times.refs_1_, f32[1,1536]{1,0:T(1,128)S(1)} %copy-done.10, f32[1,1536]{1,0:T(1,128)S(1)} %copy-done.11, ...), custom_call_target="tpu_custom_call", output_to_operand_aliasing={{2}: (11, {})} | custom-call | flops 1610612736 | bytes 3145728 | tf_op jit(solution)/shard_map/step0/pallas_call | solution.py:450
  62.9 0.1 collective-permute-start.14
  62.9 1.6 %collective-permute-start.15 = (bf16[2,128,384]{2,1,0:T(8,128)(2,1)S(1)}, bf16[2,128,384]{2,1,0:T(8,128)(2,1)S(1)}, u32[]{:S(2)}, u32[]{:S(2)}) collective-permute-start(bf16[2,128,384]{2,1,0:T(8,128)(2,1)S(1)} %get-tuple-element.50.refs_1_.refs_0_), channel_id=1, source_target_pairs={{0,16},{16,0},{1,17},{17,1},{2,18},{18,2},{3,19},{19,3},{4,20},{20... | collective-permute-start | bytes 589832 | tf_op jit(solution)/shard_map/ppermute | solution.py:31
  64.5 0.5 collective-permute-start.19
  65.0 5.1 %step1.1 = (bf16[2,128,384]{2,1,0:T(8,128)(2,1)S(1)}, bf16[2,128,384]{2,1,0:T(8,128)(2,1)S(1)}) custom-call(f32[1,16]{1,0:T(1,128)S(1)} %copy-done.15, s32[4,1]{1,0:T(4,128)S(1)} %copy.26.times.refs_1_, f32[1,1536]{1,0:T(1,128)S(1)} %copy-done.10, f32[1,1536]{1,0:T(1,128)S(1)} %copy-done.11, f32[1,1536]{1,0:T(1,128)S(1)} %copy-done.14, ...), custom_call_target="tpu_custom_call" | custom-call | flops 1610612736 | bytes 3145728 | tf_op jit(solution)/shard_map/step1/pallas_call | solution.py:450
  70.1 1.6 %collective-permute-start.23 = (bf16[2,128,384]{2,1,0:T(8,128)(2,1)S(1)}, bf16[2,128,384]{2,1,0:T(8,128)(2,1)S(1)}, u32[]{:S(2)}, u32[]{:S(2)}) collective-permute-start(bf16[2,128,384]{2,1,0:T(8,128)(2,1)S(1)} %get-tuple-element.60.refs_2_), channel_id=1, source_target_pairs={{0,16},{16,0},{1,17},{17,1},{2,18},{18,2},{3,19},{19,3},{4,20},{20... | collective-permute-start | bytes 589832 | tf_op jit(solution)/shard_map/ppermute | solution.py:31
  71.7 0.5 collective-permute-start.25
  72.2 1.5 %collective-permute-start.16 = (bf16[2,128,384]{2,1,0:T(8,128)(2,1)S(1)}, bf16[2,128,384]{2,1,0:T(8,128)(2,1)S(1)}, u32[]{:S(2)}, u32[]{:S(2)}) collective-permute-start(bf16[2,128,384]{2,1,0:T(8,128)(2,1)S(1)} %collective-permute-done.15.refs_11_), channel_id=1, source_target_pairs={{0,8},{4,12},{8,0},{12,4},{1,9},{5,13},{9,1},{13,5},{2,10},{6,14},... | collective-permute-start | bytes 589832 | tf_op jit(solution)/shard_map/ppermute | solution.py:27
  73.7 1.2 %collective-permute-done.19.refs_15_ = bf16[2,128,384]{2,1,0:T(8,128)(2,1)S(1)} collective-permute-done((bf16[2,128,384]{2,1,0:T(8,128)(2,1)S(1)}, bf16[2,128,384]{2,1,0:T(8,128)(2,1)S(1)}, u32[]{:S(2)}, u32[]{:S(2)}) %collective-permute-start.19) | collective-permute-done | bytes 196640 | tf_op jit(solution)/shard_map/ppermute | solution.py:31
  74.9 1.5 %collective-permute-start.20 = (bf16[2,128,384]{2,1,0:T(8,128)(2,1)S(1)}, bf16[2,128,384]{2,1,0:T(8,128)(2,1)S(1)}, u32[]{:S(2)}, u32[]{:S(2)}) collective-permute-start(bf16[2,128,384]{2,1,0:T(8,128)(2,1)S(1)} %collective-permute-done.19.refs_15_), channel_id=1, source_target_pairs={{0,8},{4,12},{8,0},{12,4},{1,9},{5,13},{9,1},{13,5},{2,10},{6,14},... | collective-permute-start | bytes 589832 | tf_op jit(solution)/shard_map/ppermute | solution.py:27
  76.4 2.7 %collective-permute-done.23.refs_0_ = bf16[2,128,384]{2,1,0:T(8,128)(2,1)S(1)} collective-permute-done((bf16[2,128,384]{2,1,0:T(8,128)(2,1)S(1)}, bf16[2,128,384]{2,1,0:T(8,128)(2,1)S(1)}, u32[]{:S(2)}, u32[]{:S(2)}) %collective-permute-start.23) | collective-permute-done | bytes 196640 | tf_op jit(solution)/shard_map/ppermute | solution.py:31
  79.1 3.8 %collective-permute-done.25.refs_2_ = bf16[2,128,384]{2,1,0:T(8,128)(2,1)S(1)} collective-permute-done((bf16[2,128,384]{2,1,0:T(8,128)(2,1)S(1)}, bf16[2,128,384]{2,1,0:T(8,128)(2,1)S(1)}, u32[]{:S(2)}, u32[]{:S(2)}) %collective-permute-start.25) | collective-permute-done | bytes 196640 | tf_op jit(solution)/shard_map/ppermute | solution.py:31
  82.9 0.5 collective-permute-start.18
  83.4 0.1 collective-permute-start.22
  83.5 1.5 %collective-permute-start.24 = (bf16[2,128,384]{2,1,0:T(8,128)(2,1)S(1)}, bf16[2,128,384]{2,1,0:T(8,128)(2,1)S(1)}, u32[]{:S(2)}, u32[]{:S(2)}) collective-permute-start(bf16[2,128,384]{2,1,0:T(8,128)(2,1)S(1)} %collective-permute-done.23.refs_0_), channel_id=1, source_target_pairs={{0,8},{4,12},{8,0},{12,4},{1,9},{5,13},{9,1},{13,5},{2,10},{6,14},... | collective-permute-start | bytes 589832 | tf_op jit(solution)/shard_map/ppermute | solution.py:27
  85.0 0.8 collective-permute-start.26
  85.8 6.0 %step2.1 = (bf16[2,128,384]{2,1,0:T(8,128)(2,1)S(1)}, bf16[2,128,384]{2,1,0:T(8,128)(2,1)S(1)}) custom-call(f32[1,16]{1,0:T(1,128)S(1)} %copy-done.15, s32[4,1]{1,0:T(4,128)S(1)} %copy.26.times.refs_1_, f32[1,1536]{1,0:T(1,128)S(1)} %copy-done.10, f32[1,1536]{1,0:T(1,128)S(1)} %copy-done.11, f32[1,1536]{1,0:T(1,128)S(1)} %copy-done.14, ...), custom_call_target="tpu_custom_call" | custom-call | flops 1610612736 | bytes 3145728 | tf_op jit(solution)/shard_map/step2/pallas_call | solution.py:450
  91.9 3.1 %collective-permute-done.26.refs_3_ = bf16[2,128,384]{2,1,0:T(8,128)(2,1)S(1)} collective-permute-done((bf16[2,128,384]{2,1,0:T(8,128)(2,1)S(1)}, bf16[2,128,384]{2,1,0:T(8,128)(2,1)S(1)}, u32[]{:S(2)}, u32[]{:S(2)}) %collective-permute-start.26) | collective-permute-done | bytes 196640 | tf_op jit(solution)/shard_map/ppermute | solution.py:27
  94.9 0.5 collective-permute-start.28
  95.5 0.5 collective-permute-start.30
  96.0 0.5 early.1
  96.5 0.1 collective-permute-start.31
  96.5 1.6 %collective-permute-start.32 = (bf16[2,128,384]{2,1,0:T(8,128)(2,1)S(1)}, bf16[2,128,384]{2,1,0:T(8,128)(2,1)S(1)}, u32[]{:S(2)}, u32[]{:S(2)}) collective-permute-start(bf16[2,128,384]{2,1,0:T(8,128)(2,1)S(1)} %get-tuple-element.70), channel_id=1, source_target_pairs={{0,8},{4,12},{8,0},{12,4},{1,9},{5,13},{9,1},{13,5},{2,10},{6,14},... | collective-permute-start | bytes 589832 | tf_op jit(solution)/shard_map/ppermute | solution.py:27
  98.1 0.3 collective-permute-start.33
  98.4 5.8 %step3.1 = (bf16[2,128,384]{2,1,0:T(8,128)(2,1)S(1)}, bf16[2,128,384]{2,1,0:T(8,128)(2,1)S(1)}) custom-call(f32[1,16]{1,0:T(1,128)S(1)} %copy-done.15, s32[4,1]{1,0:T(4,128)S(1)} %copy.26.times.refs_1_, f32[1,1536]{1,0:T(1,128)S(1)} %copy-done.10, f32[1,1536]{1,0:T(1,128)S(1)} %copy-done.11, f32[1,1536]{1,0:T(1,128)S(1)} %copy-done.14, ...), custom_call_target="tpu_custom_call" | custom-call | flops 1610612736 | bytes 3145728 | tf_op jit(solution)/shard_map/step3/pallas_call | solution.py:450
  104.2 0.1 collective-permute-done.32.refs_10_
  104.3 3.3 %collective-permute-done.33.refs_11_ = bf16[2,128,384]{2,1,0:T(8,128)(2,1)S(1)} collective-permute-done((bf16[2,128,384]{2,1,0:T(8,128)(2,1)S(1)}, bf16[2,128,384]{2,1,0:T(8,128)(2,1)S(1)}, u32[]{:S(2)}, u32[]{:S(2)}) %collective-permute-start.33) | collective-permute-done | bytes 196640 | tf_op jit(solution)/shard_map/ppermute | solution.py:27
  107.6 1.2 %settle.1 = (bf16[128,384]{1,0:T(8,128)(2,1)S(1)}, bf16[128,384]{1,0:T(8,128)(2,1)S(1)}, bf16[128,384]{1,0:T(8,128)(2,1)S(1)}, bf16[128,384]{1,0:T(8,128)(2,1)S(...) custom-call(bf16[2,128,384]{2,1,0:T(8,128)(2,1)S(1)} %get-tuple-elem, ...), custom_call_target="tpu_custom_call" | custom-call | tf_op jit(solution)/shard_map/settle/pallas_call | solution.py:450
  108.8 0.8 collective-permute-start.37
  109.7 1.5 %collective-permute-start.35 = (bf16[128,384]{1,0:T(8,128)(2,1)S(1)}, bf16[128,384]{1,0:T(8,128)(2,1)S(1)}, u32[]{:S(2)}, u32[]{:S(2)}) collective-permute-start(bf16[128,384]{1,0:T(8,128)(2,1)S(1)} %get-tuple-element.76), channel_id=1, source_target_pairs={{0,8},{4,12},{8,0},{12,4},{1,9},{5,13},{9,1},{13,5},{2,10},{6,14},... | collective-permute-start | bytes 294920 | tf_op jit(solution)/shard_map/ppermute | solution.py:27
  111.2 0.4 collective-permute-start.36
  111.6 2.5 %collective-permute-start.38 = (bf16[96,256]{1,0:T(8,128)(2,1)S(1)}, bf16[96,256]{1,0:T(8,128)(2,1)S(1)}, u32[]{:S(2)}, u32[]{:S(2)}) collective-permute-start(bf16[96,256]{1,0:T(8,128)(2,1)S(1)} %get-tuple-element.80), channel_id=1, source_target_pairs={{0,2},{1,3},{2,0},{3,1},{4,6},{5,7},{6,4},{7,5},{8,10},{9,11},{10,... | collective-permute-start | bytes 147464 | tf_op jit(solution)/shard_map/ppermute | solution.py:36
  114.1 0.7 collective-permute-done.37.refs_6_
  114.8 1.0 collective-permute-start.39
  115.8 1.9 %collective-permute-done.38.refs_7_ = bf16[96,256]{1,0:T(8,128)(2,1)S(1)} collective-permute-done((bf16[96,256]{1,0:T(8,128)(2,1)S(1)}, bf16[96,256]{1,0:T(8,128)(2,1)S(1)}, u32[]{:S(2)}, u32[]{:S(2)}) %collective-permute-start.38) | collective-permute-done | bytes 49184 | tf_op jit(solution)/shard_map/ppermute | solution.py:36
  117.7 1.2 collective-permute-done.39.refs_8_
  118.9 1.5 %finish.1 = (bf16[3,128,1536]{2,1,0:T(8,128)(2,1)}, f32[96,256]{1,0:T(8,128)}) custom-call(bf16[3,128,1536]{2,1,0:T(8,128)(2,1)} %get-tuple-element.73.refs_0_, bf16[128,384]{1,0:T(8,128)(2,1)S(1)} %get-tuple-element.74.refs_1_, bf16[128,384]{1,0:T(8,128)(2,1)S(1)} %collective-permute-done.34.refs_2_, ...), custom_call_target="tpu_custom_call", output_to_operand_aliasing={{0}: (0, {})} | custom-call | tf_op jit(solution)/shard_map/finish/pallas_call | solution.py:450
  (74 shorter events, 0.4 us)
Async XLA Ops:
  0.6 14.4 %copy-start.1 = (bf16[1,3,1,128,1536]{4,3,2,1,0:T(8,128)(2,1)S(1)}, bf16[1,3,1,128,1536]{4,3,2,1,0:T(8,128)(2,1)}, u32[]{:S(2)}) copy-start(bf16[1,3,1,128,1536]{4,3,2,1,0:T(8,128)(2,1)} %incoming.3) | copy-start | bytes 3538948
  0.6 14.4 %copy-start.16 = (s32[4,1,128]{2,1,0:T(1,128)S(1)}, s32[4,1,128]{2,1,0:T(1,128)}, u32[]{:S(2)}) copy-start(s32[4,1,128]{2,1,0:T(1,128)} %contacts.1) | copy-start | bytes 6148
  2.0 1.5 %collective-permute-start = (bf16[96,768]{1,0:T(8,128)(2,1)S(1)}, bf16[96,768]{1,0:T(8,128)(2,1)S(1)}, u32[]{:S(2)}, u32[]{:S(2)}) collective-permute-start(bf16[96,768]{1,0:T(8,128)(2,1)S(1)} %get-tuple-element.44), channel_id=1, source_target_pairs={{0,4},{4,0},{8,12},{12,8},{1,5},{5,1},{9,13},{13,9},{2,6},{6,2},{1... | collective-permute-start | bytes 442376 | tf_op jit(solution)/shard_map/ppermute | solution.py:27
  3.5 11.5 %collective-permute-start.1 = (bf16[2,96,768]{2,1,0:T(8,128)(2,1)S(1)}, bf16[2,96,768]{2,1,0:T(8,128)(2,1)S(1)}, u32[]{:S(2)}, u32[]{:S(2)}) collective-permute-start(bf16[2,96,768]{2,1,0:T(8,128)(2,1)S(1)} %near.1.refs_0_), channel_id=1, source_target_pairs={{0,1},{1,3},{3,2},{2,0},{4,5},{5,7},{7,6},{6,4},{8,9},{9,11},{11,1... | collective-permute-start | bytes 884744 | tf_op jit(solution)/shard_map/ppermute | solution.py:46
  6.5 0.7 copy-start.3
  7.2 6.7 %collective-permute-start.2 = (bf16[96,768]{1,0:T(8,128)(2,1)S(1)}, bf16[96,768]{1,0:T(8,128)(2,1)S(1)}, u32[]{:S(2)}, u32[]{:S(2)}) collective-permute-start(bf16[96,768]{1,0:T(8,128)(2,1)S(1)} %get-tuple-element.45), channel_id=1, source_target_pairs={{0,8},{4,12},{8,0},{12,4},{1,9},{5,13},{9,1},{13,5},{2,10},{6,14},... | collective-permute-start | bytes 442376 | tf_op jit(solution)/shard_map/ppermute | solution.py:27
  8.7 6.3 %collective-permute-start.3 = (bf16[96,768]{1,0:T(8,128)(2,1)S(1)}, bf16[96,768]{1,0:T(8,128)(2,1)S(1)}, u32[]{:S(2)}, u32[]{:S(2)}) collective-permute-start(bf16[96,768]{1,0:T(8,128)(2,1)S(1)} %get-tuple-element.46), channel_id=1, source_target_pairs={{0,12},{4,8},{8,4},{12,0},{1,13},{5,9},{9,5},{13,1},{2,14},{6,10},... | collective-permute-start | bytes 442376 | tf_op jit(solution)/shard_map/ppermute | solution.py:27
  15.0 4.2 %copy-start.5 = (bf16[2,96,768]{2,1,0:T(8,128)(2,1)}, bf16[2,96,768]{2,1,0:T(8,128)(2,1)S(1)}, u32[]{:S(2)}) copy-start(bf16[2,96,768]{2,1,0:T(8,128)(2,1)S(1)} %collective-permute-done.1.refs_0_) | copy-start | bytes 884740
  15.1 24.8 %copy-start.2 = (bf16[272,1536]{1,0:T(8,128)(2,1)}, bf16[272,1536]{1,0:T(8,128)(2,1)S(1)}, u32[]{:S(2)}) copy-start(bf16[272,1536]{1,0:T(8,128)(2,1)S(1)} %first.1.refs_0_) | copy-start | bytes 2506756
  15.1 24.8 %copy-start.9 = (bf16[1,3,1,128,256]{4,3,2,1,0:T(8,128)(2,1)S(1)}, bf16[1,3,1,128,256]{4,3,2,1,0:T(8,128)(2,1)}, u32[]{:S(2)}) copy-start(bf16[1,3,1,128,256]{4,3,2,1,0:T(8,128)(2,1)} %cotangent.1) | copy-start | bytes 589828
  15.1 24.6 %collective-permute-start.4 = (bf16[272,1536]{1,0:T(8,128)(2,1)S(1)}, bf16[272,1536]{1,0:T(8,128)(2,1)S(1)}, u32[]{:S(2)}, u32[]{:S(2)}) collective-permute-start(bf16[272,1536]{1,0:T(8,128)(2,1)S(1)} %first.1.refs_0_), channel_id=1, source_target_pairs={{0,8},{4,12},{8,0},{12,4},{1,9},{5,13},{9,1},{13,5},{2,10},{6,14},... | collective-permute-start | bytes 2506760 | tf_op jit(solution)/shard_map/ppermute | solution.py:27
  16.6 10.8 %collective-permute-start.6 = (bf16[2,96,768]{2,1,0:T(8,128)(2,1)S(1)}, bf16[2,96,768]{2,1,0:T(8,128)(2,1)S(1)}, u32[]{:S(2)}, u32[]{:S(2)}) collective-permute-start(bf16[2,96,768]{2,1,0:T(8,128)(2,1)S(1)} %far.1.refs_1_), channel_id=1, source_target_pairs={{0,1},{1,3},{3,2},{2,0},{4,5},{5,7},{7,6},{6,4},{8,9},{9,11},{11,1... | collective-permute-start | bytes 884744 | tf_op jit(solution)/shard_map/ppermute | solution.py:46
  19.2 14.6 %collective-permute-start.5 = (bf16[2,96,768]{2,1,0:T(8,128)(2,1)S(1)}, bf16[2,96,768]{2,1,0:T(8,128)(2,1)}, u32[]{:S(2)}, u32[]{:S(2)}) collective-permute-start(bf16[2,96,768]{2,1,0:T(8,128)(2,1)S(1)} %collective-permute-done.1.refs_0_), channel_id=1, source_target_pairs={{0,1},{1,3},{3,2},{2,0},{4,5},{5,7},{7,6},{6,4},{8,9},{9,11},{11,1... | collective-permute-start | bytes 884744 | tf_op jit(solution)/shard_map/ppermute | solution.py:46
  27.4 12.4 %copy-start.7 = (bf16[2,96,768]{2,1,0:T(8,128)(2,1)}, bf16[2,96,768]{2,1,0:T(8,128)(2,1)S(1)}, u32[]{:S(2)}) copy-start(bf16[2,96,768]{2,1,0:T(8,128)(2,1)S(1)} %collective-permute-done.6.refs_1_) | copy-start | bytes 884740
  27.4 12.4 %collective-permute-start.7 = (bf16[2,96,768]{2,1,0:T(8,128)(2,1)S(1)}, bf16[2,96,768]{2,1,0:T(8,128)(2,1)}, u32[]{:S(2)}, u32[]{:S(2)}) collective-permute-start(bf16[2,96,768]{2,1,0:T(8,128)(2,1)S(1)} %collective-permute-done.6.refs_1_), channel_id=1, source_target_pairs={{0,1},{1,3},{3,2},{2,0},{4,5},{5,7},{7,6},{6,4},{8,9},{9,11},{11,1... | collective-permute-start | bytes 884744 | tf_op jit(solution)/shard_map/ppermute | solution.py:46
  29.0 14.9 %collective-permute-start.9 = (bf16[272,1536]{1,0:T(8,128)(2,1)S(1)}, bf16[272,1536]{1,0:T(8,128)(2,1)S(1)}, u32[]{:S(2)}, u32[]{:S(2)}) collective-permute-start(bf16[272,1536]{1,0:T(8,128)(2,1)S(1)} %first.1.refs_0_), channel_id=1, source_target_pairs={{0,4},{4,0},{8,12},{12,8},{1,5},{5,1},{9,13},{13,9},{2,6},{6,2},{1... | collective-permute-start | bytes 2506760 | tf_op jit(solution)/shard_map/ppermute | solution.py:27
  39.8 6.1 %copy-start = (bf16[272,1536]{1,0:T(8,128)(2,1)}, bf16[272,1536]{1,0:T(8,128)(2,1)S(1)}, u32[]{:S(2)}) copy-start(bf16[272,1536]{1,0:T(8,128)(2,1)S(1)} %tie.3.dep.refs_1_) | copy-start | bytes 2506756
  39.8 5.0 %copy-start.18 = (s32[4,1]{0,1:T(1,128)S(1)}, s32[4,1]{0,1:T(1,128)}, u32[]{:S(2)}) copy-start(s32[4,1]{0,1:T(1,128)} %param.15) | copy-start | bytes 52
  39.8 8.4 %collective-permute-start.10 = (bf16[272,1536]{1,0:T(8,128)(2,1)S(1)}, bf16[272,1536]{1,0:T(8,128)(2,1)}, u32[]{:S(2)}, u32[]{:S(2)}) collective-permute-start(bf16[272,1536]{1,0:T(8,128)(2,1)S(1)} %tie.3.dep.refs_1_), channel_id=1, source_target_pairs={{0,4},{4,0},{8,12},{12,8},{1,5},{5,1},{9,13},{13,9},{2,6},{6,2},{1... | collective-permute-start | bytes 2506760 | tf_op jit(solution)/shard_map/ppermute | solution.py:27
  40.0 22.9 %collective-permute-start.8 = (bf16[256,1536]{1,0:T(8,128)(2,1)S(1)}, bf16[256,1536]{1,0:T(8,128)(2,1)S(1)}, u32[]{:S(2)}, u32[]{:S(2)}) collective-permute-start(bf16[256,1536]{1,0:T(8,128)(2,1)S(1)} %second.1.refs_6_.refs_4_), channel_id=1, source_target_pairs={{0,8},{4,12},{8,0},{12,4},{1,9},{5,13},{9,1},{13,5},{2,10},{6,14},... | collective-permute-start | bytes 2359304 | tf_op jit(solution)/shard_map/ppermute | solution.py:27
  40.6 12.5 %collective-permute-start.11 = (bf16[2,96,768]{2,1,0:T(8,128)(2,1)}, bf16[2,96,768]{2,1,0:T(8,128)(2,1)}, u32[]{:S(2)}, u32[]{:S(2)}) collective-permute-start(bf16[2,96,768]{2,1,0:T(8,128)(2,1)} %collective-permute-done.5.refs_1_.refs_0_), channel_id=1, source_target_pairs={{0,1},{1,3},{3,2},{2,0},{4,5},{5,7},{7,6},{6,4},{8,9},{9,11},{11,1... | collective-permute-start | bytes 884744 | tf_op jit(solution)/shard_map/ppermute | solution.py:46
  42.2 15.0 %collective-permute-start.12 = (bf16[2,96,768]{2,1,0:T(8,128)(2,1)}, bf16[2,96,768]{2,1,0:T(8,128)(2,1)}, u32[]{:S(2)}, u32[]{:S(2)}) collective-permute-start(bf16[2,96,768]{2,1,0:T(8,128)(2,1)} %collective-permute-done.7.refs_2_.refs_1_), channel_id=1, source_target_pairs={{0,1},{1,3},{3,2},{2,0},{4,5},{5,7},{7,6},{6,4},{8,9},{9,11},{11,1... | collective-permute-start | bytes 884744 | tf_op jit(solution)/shard_map/ppermute | solution.py:46
  43.9 0.9 copy-start.17
  44.8 26.9 %collective-permute-start.13 = (bf16[256,1536]{1,0:T(8,128)(2,1)S(1)}, bf16[256,1536]{1,0:T(8,128)(2,1)S(1)}, u32[]{:S(2)}, u32[]{:S(2)}) collective-permute-start(bf16[256,1536]{1,0:T(8,128)(2,1)S(1)} %second.1.refs_6_.refs_4_), channel_id=1, source_target_pairs={{0,4},{4,0},{8,12},{12,8},{1,5},{5,1},{9,13},{13,9},{2,6},{6,2},{1... | collective-permute-start | bytes 2359304 | tf_op jit(solution)/shard_map/ppermute | solution.py:27
  44.9 1.0 copy-start.4
  45.9 1.0 copy-start.6
  45.9 1.0 copy-start.8
  47.0 1.2 %copy-start.10 = (f32[1,1536]{1,0:T(1,128)S(1)}, f32[1,1536]{1,0:T(1,128)}, u32[]{:S(2)}) copy-start(f32[1,1536]{1,0:T(1,128)} %refs_2_.7) | copy-start | bytes 18436
  47.0 1.2 %copy-start.11 = (f32[1,1536]{1,0:T(1,128)S(1)}, f32[1,1536]{1,0:T(1,128)}, u32[]{:S(2)}) copy-start(f32[1,1536]{1,0:T(1,128)} %refs_3_.7) | copy-start | bytes 18436
  47.0 1.2 %copy-start.12 = (bf16[1,16,1536]{2,1,0:T(8,128)(2,1)S(1)}, bf16[1,16,1536]{2,1,0:T(8,128)(2,1)}, u32[]{:S(2)}) copy-start(bf16[1,16,1536]{2,1,0:T(8,128)(2,1)} %table.1) | copy-start | bytes 147460
  48.1 9.1 %copy-start.13 = (s32[4,1,512]{2,1,0:T(1,128)S(1)}, s32[4,1,512]{2,1,0:T(1,128)}, u32[]{:S(2)}) copy-start(s32[4,1,512]{2,1,0:T(1,128)} %refs_5_.7) | copy-start | bytes 24580
  48.2 9.1 %copy-start.14 = (f32[1,1536]{1,0:T(1,128)S(1)}, f32[1,1536]{1,0:T(1,128)}, u32[]{:S(2)}) copy-start(f32[1,1536]{1,0:T(1,128)} %refs_4_.7) | copy-start | bytes 18436
  48.2 9.0 %copy-start.15 = (f32[1,16]{1,0:T(1,128)S(1)}, f32[1,16]{1,0:T(1,128)}, u32[]{:S(2)}) copy-start(f32[1,16]{1,0:T(1,128)} %refs_0_.7) | copy-start | bytes 196
  62.9 23.0 %collective-permute-start.14 = (bf16[256,1536]{1,0:T(8,128)(2,1)S(1)}, bf16[256,1536]{1,0:T(8,128)(2,1)S(1)}, u32[]{:S(2)}, u32[]{:S(2)}) collective-permute-start(bf16[256,1536]{1,0:T(8,128)(2,1)S(1)} %tie.4.refs_7_.refs_5_), channel_id=1, source_target_pairs={{0,4},{4,0},{8,12},{12,8},{1,5},{5,1},{9,13},{13,9},{2,6},{6,2},{1... | collective-permute-start | bytes 2359304 | tf_op jit(solution)/shard_map/ppermute | solution.py:27
  62.9 9.2 %collective-permute-start.15 = (bf16[2,128,384]{2,1,0:T(8,128)(2,1)S(1)}, bf16[2,128,384]{2,1,0:T(8,128)(2,1)S(1)}, u32[]{:S(2)}, u32[]{:S(2)}) collective-permute-start(bf16[2,128,384]{2,1,0:T(8,128)(2,1)S(1)} %get-tuple-element.50.refs_1_.refs_0_), channel_id=1, source_target_pairs={{0,16},{16,0},{1,17},{17,1},{2,18},{18,2},{3,19},{19,3},{4,20},{20... | collective-permute-start | bytes 589832 | tf_op jit(solution)/shard_map/ppermute | solution.py:31
  64.5 10.4 %collective-permute-start.19 = (bf16[2,128,384]{2,1,0:T(8,128)(2,1)S(1)}, bf16[2,128,384]{2,1,0:T(8,128)(2,1)S(1)}, u32[]{:S(2)}, u32[]{:S(2)}) collective-permute-start(bf16[2,128,384]{2,1,0:T(8,128)(2,1)S(1)} %get-tuple-element.52.refs_1_), channel_id=1, source_target_pairs={{0,16},{16,0},{1,17},{17,1},{2,18},{18,2},{3,19},{19,3},{4,20},{20... | collective-permute-start | bytes 589832 | tf_op jit(solution)/shard_map/ppermute | solution.py:31
  70.1 9.0 %collective-permute-start.23 = (bf16[2,128,384]{2,1,0:T(8,128)(2,1)S(1)}, bf16[2,128,384]{2,1,0:T(8,128)(2,1)S(1)}, u32[]{:S(2)}, u32[]{:S(2)}) collective-permute-start(bf16[2,128,384]{2,1,0:T(8,128)(2,1)S(1)} %get-tuple-element.60.refs_2_), channel_id=1, source_target_pairs={{0,16},{16,0},{1,17},{17,1},{2,18},{18,2},{3,19},{19,3},{4,20},{20... | collective-permute-start | bytes 589832 | tf_op jit(solution)/shard_map/ppermute | solution.py:31
  71.7 11.2 %collective-permute-start.25 = (bf16[2,128,384]{2,1,0:T(8,128)(2,1)S(1)}, bf16[2,128,384]{2,1,0:T(8,128)(2,1)S(1)}, u32[]{:S(2)}, u32[]{:S(2)}) collective-permute-start(bf16[2,128,384]{2,1,0:T(8,128)(2,1)S(1)} %get-tuple-element.61.refs_3_), channel_id=1, source_target_pairs={{0,16},{16,0},{1,17},{17,1},{2,18},{18,2},{3,19},{19,3},{4,20},{20... | collective-permute-start | bytes 589832 | tf_op jit(solution)/shard_map/ppermute | solution.py:31
  72.2 10.7 %collective-permute-start.16 = (bf16[2,128,384]{2,1,0:T(8,128)(2,1)S(1)}, bf16[2,128,384]{2,1,0:T(8,128)(2,1)S(1)}, u32[]{:S(2)}, u32[]{:S(2)}) collective-permute-start(bf16[2,128,384]{2,1,0:T(8,128)(2,1)S(1)} %collective-permute-done.15.refs_11_), channel_id=1, source_target_pairs={{0,8},{4,12},{8,0},{12,4},{1,9},{5,13},{9,1},{13,5},{2,10},{6,14},... | collective-permute-start | bytes 589832 | tf_op jit(solution)/shard_map/ppermute | solution.py:27
  74.9 8.5 %collective-permute-start.20 = (bf16[2,128,384]{2,1,0:T(8,128)(2,1)S(1)}, bf16[2,128,384]{2,1,0:T(8,128)(2,1)S(1)}, u32[]{:S(2)}, u32[]{:S(2)}) collective-permute-start(bf16[2,128,384]{2,1,0:T(8,128)(2,1)S(1)} %collective-permute-done.19.refs_15_), channel_id=1, source_target_pairs={{0,8},{4,12},{8,0},{12,4},{1,9},{5,13},{9,1},{13,5},{2,10},{6,14},... | collective-permute-start | bytes 589832 | tf_op jit(solution)/shard_map/ppermute | solution.py:27
  79.1 4.4 %collective-permute-start.17 = (bf16[2,128,384]{2,1,0:T(8,128)(2,1)S(1)}, bf16[2,128,384]{2,1,0:T(8,128)(2,1)S(1)}, u32[]{:S(2)}, u32[]{:S(2)}) collective-permute-start(bf16[2,128,384]{2,1,0:T(8,128)(2,1)S(1)} %collective-permute-done.15.refs_11_), channel_id=1, source_target_pairs={{0,4},{4,0},{8,12},{12,8},{1,5},{5,1},{9,13},{13,9},{2,6},{6,2},{1... | collective-permute-start | bytes 589832 | tf_op jit(solution)/shard_map/ppermute | solution.py:27
  82.9 2.1 %collective-permute-start.21 = (bf16[2,128,384]{2,1,0:T(8,128)(2,1)S(1)}, bf16[2,128,384]{2,1,0:T(8,128)(2,1)S(1)}, u32[]{:S(2)}, u32[]{:S(2)}) collective-permute-start(bf16[2,128,384]{2,1,0:T(8,128)(2,1)S(1)} %collective-permute-done.19.refs_15_), channel_id=1, source_target_pairs={{0,4},{4,0},{8,12},{12,8},{1,5},{5,1},{9,13},{13,9},{2,6},{6,2},{1... | collective-permute-start | bytes 589832 | tf_op jit(solution)/shard_map/ppermute | solution.py:27
  82.9 2.9 %collective-permute-start.18 = (bf16[2,128,384]{2,1,0:T(8,128)(2,1)S(1)}, bf16[2,128,384]{2,1,0:T(8,128)(2,1)S(1)}, u32[]{:S(2)}, u32[]{:S(2)}) collective-permute-start(bf16[2,128,384]{2,1,0:T(8,128)(2,1)S(1)} %collective-permute-done.16.refs_12_), channel_id=1, source_target_pairs={{0,4},{4,0},{8,12},{12,8},{1,5},{5,1},{9,13},{13,9},{2,6},{6,2},{1... | collective-permute-start | bytes 589832 | tf_op jit(solution)/shard_map/ppermute | solution.py:27
  83.4 2.4 %collective-permute-start.22 = (bf16[2,128,384]{2,1,0:T(8,128)(2,1)S(1)}, bf16[2,128,384]{2,1,0:T(8,128)(2,1)S(1)}, u32[]{:S(2)}, u32[]{:S(2)}) collective-permute-start(bf16[2,128,384]{2,1,0:T(8,128)(2,1)S(1)} %collective-permute-done.20.refs_16_), channel_id=1, source_target_pairs={{0,4},{4,0},{8,12},{12,8},{1,5},{5,1},{9,13},{13,9},{2,6},{6,2},{1... | collective-permute-start | bytes 589832 | tf_op jit(solution)/shard_map/ppermute | solution.py:27
  83.5 8.4 %collective-permute-start.24 = (bf16[2,128,384]{2,1,0:T(8,128)(2,1)S(1)}, bf16[2,128,384]{2,1,0:T(8,128)(2,1)S(1)}, u32[]{:S(2)}, u32[]{:S(2)}) collective-permute-start(bf16[2,128,384]{2,1,0:T(8,128)(2,1)S(1)} %collective-permute-done.23.refs_0_), channel_id=1, source_target_pairs={{0,8},{4,12},{8,0},{12,4},{1,9},{5,13},{9,1},{13,5},{2,10},{6,14},... | collective-permute-start | bytes 589832 | tf_op jit(solution)/shard_map/ppermute | solution.py:27
  85.0 10.0 %collective-permute-start.26 = (bf16[2,128,384]{2,1,0:T(8,128)(2,1)S(1)}, bf16[2,128,384]{2,1,0:T(8,128)(2,1)S(1)}, u32[]{:S(2)}, u32[]{:S(2)}) collective-permute-start(bf16[2,128,384]{2,1,0:T(8,128)(2,1)S(1)} %collective-permute-done.25.refs_2_), channel_id=1, source_target_pairs={{0,8},{4,12},{8,0},{12,4},{1,9},{5,13},{9,1},{13,5},{2,10},{6,14},... | collective-permute-start | bytes 589832 | tf_op jit(solution)/shard_map/ppermute | solution.py:27
  94.9 1.6 %collective-permute-start.27 = (bf16[2,128,384]{2,1,0:T(8,128)(2,1)S(1)}, bf16[2,128,384]{2,1,0:T(8,128)(2,1)S(1)}, u32[]{:S(2)}, u32[]{:S(2)}) collective-permute-start(bf16[2,128,384]{2,1,0:T(8,128)(2,1)S(1)} %get-tuple-element.62.refs_11_), channel_id=1, source_target_pairs={{0,4},{4,0},{8,12},{12,8},{1,5},{5,1},{9,13},{13,9},{2,6},{6,2},{1... | collective-permute-start | bytes 589832 | tf_op jit(solution)/shard_map/ppermute | solution.py:27
  94.9 3.2 %collective-permute-start.28 = (bf16[2,128,384]{2,1,0:T(8,128)(2,1)S(1)}, bf16[2,128,384]{2,1,0:T(8,128)(2,1)S(1)}, u32[]{:S(2)}, u32[]{:S(2)}) collective-permute-start(bf16[2,128,384]{2,1,0:T(8,128)(2,1)S(1)} %get-tuple-element.63.refs_12_), channel_id=1, source_target_pairs={{0,4},{4,0},{8,12},{12,8},{1,5},{5,1},{9,13},{13,9},{2,6},{6,2},{1... | collective-permute-start | bytes 589832 | tf_op jit(solution)/shard_map/ppermute | solution.py:27
  95.5 2.9 %collective-permute-start.29 = (bf16[2,128,384]{2,1,0:T(8,128)(2,1)S(1)}, bf16[2,128,384]{2,1,0:T(8,128)(2,1)S(1)}, u32[]{:S(2)}, u32[]{:S(2)}) collective-permute-start(bf16[2,128,384]{2,1,0:T(8,128)(2,1)S(1)} %get-tuple-element.64.refs_15_), channel_id=1, source_target_pairs={{0,4},{4,0},{8,12},{12,8},{1,5},{5,1},{9,13},{13,9},{2,6},{6,2},{1... | collective-permute-start | bytes 589832 | tf_op jit(solution)/shard_map/ppermute | solution.py:27
  95.5 2.9 %collective-permute-start.30 = (bf16[2,128,384]{2,1,0:T(8,128)(2,1)S(1)}, bf16[2,128,384]{2,1,0:T(8,128)(2,1)S(1)}, u32[]{:S(2)}, u32[]{:S(2)}) collective-permute-start(bf16[2,128,384]{2,1,0:T(8,128)(2,1)S(1)} %get-tuple-element.65.refs_16_), channel_id=1, source_target_pairs={{0,4},{4,0},{8,12},{12,8},{1,5},{5,1},{9,13},{13,9},{2,6},{6,2},{1... | collective-permute-start | bytes 589832 | tf_op jit(solution)/shard_map/ppermute | solution.py:27
  96.5 7.8 %collective-permute-start.31 = (bf16[2,128,384]{2,1,0:T(8,128)(2,1)S(1)}, bf16[2,128,384]{2,1,0:T(8,128)(2,1)S(1)}, u32[]{:S(2)}, u32[]{:S(2)}) collective-permute-start(bf16[2,128,384]{2,1,0:T(8,128)(2,1)S(1)} %get-tuple-element.69), channel_id=1, source_target_pairs={{0,4},{4,0},{8,12},{12,8},{1,5},{5,1},{9,13},{13,9},{2,6},{6,2},{1... | collective-permute-start | bytes 589832 | tf_op jit(solution)/shard_map/ppermute | solution.py:27
  96.5 7.8 %collective-permute-start.32 = (bf16[2,128,384]{2,1,0:T(8,128)(2,1)S(1)}, bf16[2,128,384]{2,1,0:T(8,128)(2,1)S(1)}, u32[]{:S(2)}, u32[]{:S(2)}) collective-permute-start(bf16[2,128,384]{2,1,0:T(8,128)(2,1)S(1)} %get-tuple-element.70), channel_id=1, source_target_pairs={{0,8},{4,12},{8,0},{12,4},{1,9},{5,13},{9,1},{13,5},{2,10},{6,14},... | collective-permute-start | bytes 589832 | tf_op jit(solution)/shard_map/ppermute | solution.py:27
  98.1 9.5 %collective-permute-start.33 = (bf16[2,128,384]{2,1,0:T(8,128)(2,1)S(1)}, bf16[2,128,384]{2,1,0:T(8,128)(2,1)S(1)}, u32[]{:S(2)}, u32[]{:S(2)}) collective-permute-start(bf16[2,128,384]{2,1,0:T(8,128)(2,1)S(1)} %get-tuple-element.71), channel_id=1, source_target_pairs={{0,12},{4,8},{8,4},{12,0},{1,13},{5,9},{9,5},{13,1},{2,14},{6,10},... | collective-permute-start | bytes 589832 | tf_op jit(solution)/shard_map/ppermute | solution.py:27
  108.8 5.9 %collective-permute-start.37 = (bf16[96,256]{1,0:T(8,128)(2,1)S(1)}, bf16[96,256]{1,0:T(8,128)(2,1)S(1)}, u32[]{:S(2)}, u32[]{:S(2)}) collective-permute-start(bf16[96,256]{1,0:T(8,128)(2,1)S(1)} %get-tuple-element.79), channel_id=1, source_target_pairs={{0,1},{1,2},{2,3},{3,0},{4,5},{5,6},{6,7},{7,4},{8,9},{9,10},{10,1... | collective-permute-start | bytes 147464 | tf_op jit(solution)/shard_map/ppermute | solution.py:36
  109.7 9.2 %collective-permute-start.34 = (bf16[128,384]{1,0:T(8,128)(2,1)S(1)}, bf16[128,384]{1,0:T(8,128)(2,1)S(1)}, u32[]{:S(2)}, u32[]{:S(2)}) collective-permute-start(bf16[128,384]{1,0:T(8,128)(2,1)S(1)} %get-tuple-element.75), channel_id=1, source_target_pairs={{0,4},{4,0},{8,12},{12,8},{1,5},{5,1},{9,13},{13,9},{2,6},{6,2},{1... | collective-permute-start | bytes 294920 | tf_op jit(solution)/shard_map/ppermute | solution.py:27
  109.7 9.2 %collective-permute-start.35 = (bf16[128,384]{1,0:T(8,128)(2,1)S(1)}, bf16[128,384]{1,0:T(8,128)(2,1)S(1)}, u32[]{:S(2)}, u32[]{:S(2)}) collective-permute-start(bf16[128,384]{1,0:T(8,128)(2,1)S(1)} %get-tuple-element.76), channel_id=1, source_target_pairs={{0,8},{4,12},{8,0},{12,4},{1,9},{5,13},{9,1},{13,5},{2,10},{6,14},... | collective-permute-start | bytes 294920 | tf_op jit(solution)/shard_map/ppermute | solution.py:27
  111.2 7.7 %collective-permute-start.36 = (bf16[128,384]{1,0:T(8,128)(2,1)S(1)}, bf16[128,384]{1,0:T(8,128)(2,1)S(1)}, u32[]{:S(2)}, u32[]{:S(2)}) collective-permute-start(bf16[128,384]{1,0:T(8,128)(2,1)S(1)} %get-tuple-element.77), channel_id=1, source_target_pairs={{0,12},{4,8},{8,4},{12,0},{1,13},{5,9},{9,5},{13,1},{2,14},{6,10},... | collective-permute-start | bytes 294920 | tf_op jit(solution)/shard_map/ppermute | solution.py:27
  111.6 6.1 %collective-permute-start.38 = (bf16[96,256]{1,0:T(8,128)(2,1)S(1)}, bf16[96,256]{1,0:T(8,128)(2,1)S(1)}, u32[]{:S(2)}, u32[]{:S(2)}) collective-permute-start(bf16[96,256]{1,0:T(8,128)(2,1)S(1)} %get-tuple-element.80), channel_id=1, source_target_pairs={{0,2},{1,3},{2,0},{3,1},{4,6},{5,7},{6,4},{7,5},{8,10},{9,11},{10,... | collective-permute-start | bytes 147464 | tf_op jit(solution)/shard_map/ppermute | solution.py:36
  114.8 4.1 %collective-permute-start.39 = (bf16[96,256]{1,0:T(8,128)(2,1)S(1)}, bf16[96,256]{1,0:T(8,128)(2,1)S(1)}, u32[]{:S(2)}, u32[]{:S(2)}) collective-permute-start(bf16[96,256]{1,0:T(8,128)(2,1)S(1)} %get-tuple-element.81), channel_id=1, source_target_pairs={{0,3},{1,0},{2,1},{3,2},{4,7},{5,4},{6,5},{7,6},{8,11},{9,8},{10,9... | collective-permute-start | bytes 147464 | tf_op jit(solution)/shard_map/ppermute | solution.py:36

commit v11 on v10

--- a/solution.py
+++ b/solution.py
@@ -222,7 +222,7 @@
         scaled, scales, own_hidden, mod = take(4)
     offsets = offsets_of(pieces)
     frames, width = scaled.shape
-    rows, cols = frames // pieces, att.shape[1]
+    rows, cols = frames // pieces, att.shape[0]
     part = pieces // halves
     seq, rep, section = lax.axis_index("seq"), lax.axis_index("dp"), lax.axis_index("pipe")
     _, batch = turn_and_batch(step, turns)
@@ -290,7 +290,7 @@
         key = jnp.where(flag_lanes, flag_column, jnp.where(lanes < head, part_of(base), 0.0))
         value = jnp.where(lanes < head, part_of(base + head), jnp.where(lanes == head, 1.0, 0.0))
         keys.append(key.astype(jnp.bfloat16))
-        values.append(value.astype(jnp.bfloat16))
+        values.append(value.T.astype(jnp.bfloat16))
 
     def scores_of(h):
         strength = jnp.zeros((1, 128), jnp.float32) + bias[0, seq * heads + h] * math.log2(math.e)
@@ -300,19 +300,19 @@
         )
         query = jnp.where(lanes < head, part_of(h * head), tail).astype(jnp.bfloat16)
         return lax.dot_general(
-            query, keys[h // group], (((1,), (1,)), ((), ())), preferred_element_type=jnp.float32
+            keys[h // group], query, (((1,), (1,)), ((), ())), preferred_element_type=jnp.float32
         )
 
     scores = scores_of(0)
     for h in range(heads):
         ahead = scores_of(h + 1) if h + 1 < heads else None
-        top = jnp.max(scores, axis=1, keepdims=True)
-        weight = jnp.exp2((scores - top).astype(jnp.bfloat16))
-        mixed = jnp.dot(weight, values[h // group], preferred_element_type=jnp.float32)
-        att[:, h * head : (h + 1) * head] = mixed[:, :head] * (1.0 / mixed[:, head : head + 1])
+        top = jnp.max(scores, axis=0, keepdims=True)
+        weight = jnp.exp2(scores - top).astype(jnp.bfloat16)
+        mixed = jnp.dot(values[h // group], weight, preferred_element_type=jnp.float32)
+        att[h * head : (h + 1) * head, :] = mixed[:head] * (1.0 / mixed[head : head + 1])
         scores = ahead
     own = pl.ds(pl.multiple_of(seq * cols, 128), cols)
-    attended = att[...].astype(jnp.bfloat16).astype(jnp.float32)
+    attended = att[...].T.astype(jnp.bfloat16).astype(jnp.float32)
     output = (own_hidden[...] + gate[:, own] * attended).astype(jnp.bfloat16)
     blocks = output.reshape(pieces, rows, cols)
     for k in range(halves):
@@ -361,7 +361,7 @@
         taken, refs[:count] = refs[:count], []
         return taken
 
-    before, now, second, early = take(halves), take(halves), take(pieces), take(pieces)
+    before, now, second, early = take(halves), take(halves), take(pieces), take(pieces - 1)
     early_grad = take(1)[0]
     late, own_grad, grads = take(pieces), take(1)[0], take(hops - 1)
     section_out = take(1)[0]
@@ -370,7 +370,7 @@
     offsets = offsets_of(pieces)
     part = pieces // halves
     rows, cols = early[0].shape[1:]
-    for m in range(pieces):
+    for m in range(pieces - 1):
         lanes = pl.ds(pl.multiple_of((seq ^ m) * cols, 128), cols)
         for turn in range(turns - 1):
             rows_out[turn, :, lanes] = early[m][turn]
@@ -393,19 +393,25 @@
 
 
 def finish_kernel(pieces, hops, *refs):
-    held, late, refs = refs[0], refs[1 : pieces + 1], refs[pieces + 1 :]
-    own_grad, parts, (section_out, grad, row_out, sem) = refs[0], refs[1:hops], refs[hops:]
+    held, early, late, refs = refs[0], refs[1], refs[2 : pieces + 2], refs[pieces + 2 :]
+    own_grad, parts, (section_out, grad, row_out, sems) = refs[0], refs[1:hops], refs[hops:]
     seq = lax.axis_index("seq")
     cols = late[0].shape[1]
+    last_lanes = pl.ds(pl.multiple_of((seq ^ (pieces - 1)) * cols, 128), cols)
+    early_copy = pltpu.make_async_copy(
+        early, section_out.at[pl.ds(0, early.shape[0]), :, last_lanes], sems.at[0]
+    )
+    early_copy.start()
     for m in range(pieces):
         lanes = pl.ds(pl.multiple_of((seq ^ m) * cols, 128), cols)
         row_out[:, lanes] = late[m][...]
-    copy = pltpu.make_async_copy(row_out, section_out.at[section_out.shape[0] - 1], sem)
+    copy = pltpu.make_async_copy(row_out, section_out.at[section_out.shape[0] - 1], sems.at[1])
     copy.start()
     total = own_grad[...]
     for part in parts:
         total = total + part[...].astype(jnp.float32)
     grad[...] = total
+    early_copy.wait()
     copy.wait()
 
 
@@ -579,7 +585,7 @@
         operands = [key_bias, timesteps, norm_gain, time_freq, attn_gate, keyframes]
         scratch = [
             pltpu.VMEM((frames, 2 * cols + 128), kind),
-            pltpu.VMEM((frames, cols), jnp.float32),
+            pltpu.VMEM((cols, frames), jnp.float32),
         ]
         if step in relayed:
             large = second + [prepared[4 + step]] + relayed[step]
@@ -644,7 +650,7 @@
                     relayed[2] += [mine, across, swap(mine, 1), swap(across, 1)]
 
     g_shape = (cols // hops, feats)
-    operands = outputs[-2] + outputs[-1] + second + early + [early_grad]
+    operands = outputs[-2] + outputs[-1] + second + early[:-1] + [early_grad]
     settled = call(
         functools.partial(settle_kernel, turns, seq_count, HALVES, hops, feats),
         "settle",
@@ -669,9 +675,9 @@
         functools.partial(finish_kernel, seq_count, hops),
         "finish",
         [shape((turns, rows, width), kind), shape(g_shape, jnp.float32)],
-        [anywhere] + [vmem] * (seq_count + hops),
-        [held] + late + grads,
-        [pltpu.VMEM((rows, width), kind), pltpu.SemaphoreType.DMA],
+        [anywhere] + [vmem] * (seq_count + hops + 1),
+        [held, early[-1]] + late + grads,
+        [pltpu.VMEM((rows, width), kind), pltpu.SemaphoreType.DMA((2,))],
         out_specs=[anywhere, vmem],
         input_output_aliases={0: 0},
     )

time: 121 us -> 117 us (0.967)
  Pallas kernels: 33.1 us -> 29.4 us
    pallas_call x19, Pallas kernels: 33.1 us -> 29.4 us  [call(): pl.pallas_call(kernel, out_shape=out_shape, in_specs=in_specs, scratch_sh...]
    ppermute x27, waiting for transfers between devices: 13.8 us -> 12.3 us  [swap(): lax.ppermute(value, 'seq', [(source, source ^ bit) for source in range(co...]
  transfers between devices with their start and end apart: 40 -> 40, of which waited for: 16 -> 16; matrix products, arithmetic and copies ran while one was open for 0% -> 0% of each run, Pallas kernels for 24% -> 23%
where the time goes in v11:
time: 117 us; the launch traced here: 116 us
  waiting for transfers between devices  46.4 us (40%)
  starting transfers between devices  35.6 us (30%)
  Pallas kernels  29.4 us (25%)
  local copies, waits for them, and re-layouts  3.72 us (3%)
    pallas_call x19, Pallas kernels, call(): pl.pallas_call(kernel, out_shape=out_shape, in_specs=in_specs, scratch_sh...  29.4 us
    ppermute x6, waiting for transfers between devices, ring_step(): return lax.ppermute(value, 'dp', pairs)  21.5 us
    ppermute x27, starting transfers between devices, swap(): lax.ppermute(value, 'seq', [(source, source ^ bit) for source in range(co...  14.9 us
    ppermute x27, waiting for transfers between devices, swap(): lax.ppermute(value, 'seq', [(source, source ^ bit) for source in range(co...  12.3 us
    ppermute x6, starting transfers between devices, ring_step(): return lax.ppermute(value, 'dp', pairs)  12.2 us
    ppermute x4, waiting for transfers between devices, handed_over(): return lax.ppermute(value, 'pipe', [(0, 1), (1, 0)])  8.69 us
    ppermute x3, starting transfers between devices, shifted(): lax.ppermute(value, axis, [(source, (source + shift) % count) for source...  4.36 us
    ppermute x4, starting transfers between devices, handed_over(): return lax.ppermute(value, 'pipe', [(0, 1), (1, 0)])  4.18 us
  transfers between devices with their start and end apart: 40, of which 16 were waited for; matrix products, arithmetic and copies ran while one was open for 0% of the time, Pallas kernels for 23%

profile of v11, /device:TPU:0, one launch (start us, length us, event | category | flops | bytes accessed | tf_op | source)
XLA Modules:
  0.0 116.3 jit_solution(12445356166786704848)
XLA Ops:
  0.7 1.3 %pack.1 = (bf16[96,768]{1,0:T(8,128)(2,1)S(1)}, bf16[96,768]{1,0:T(8,128)(2,1)S(1)}, bf16[96,768]{1,0:T(8,128)(2,1)S(1)}, bf16[96,768]{1,0:T(8,128)(2,1)S(1)}) custom-call(bf16[1,96,1536]{2,1,0:T(8,128)(2,1)} %wq.1, bf16[1,96,1536]{2,1,0:T(8,128)(2,1)} %wkv.1), custom_call_target="tpu_custom_call" | custom-call | tf_op jit(solution)/shard_map/pack/pallas_call | solution.py:456
  2.0 0.5 collective-permute-start
  2.5 1.0 collective-permute-done.refs_1_
  3.5 3.0 %collective-permute-start.1 = (bf16[2,96,768]{2,1,0:T(8,128)(2,1)S(1)}, bf16[2,96,768]{2,1,0:T(8,128)(2,1)S(1)}, u32[]{:S(2)}, u32[]{:S(2)}) collective-permute-start(bf16[2,96,768]{2,1,0:T(8,128)(2,1)S(1)} %near.1.refs_0_), channel_id=1, source_target_pairs={{0,1},{1,3},{3,2},{2,0},{4,5},{5,7},{7,6},{6,4},{8,9},{9,11},{11,1... | collective-permute-start | bytes 884744 | tf_op jit(solution)/shard_map/ppermute | solution.py:46
  6.5 0.7 copy-done.3
  7.2 1.5 %collective-permute-start.2 = (bf16[96,768]{1,0:T(8,128)(2,1)S(1)}, bf16[96,768]{1,0:T(8,128)(2,1)S(1)}, u32[]{:S(2)}, u32[]{:S(2)}) collective-permute-start(bf16[96,768]{1,0:T(8,128)(2,1)S(1)} %get-tuple-element.45), channel_id=1, source_target_pairs={{0,8},{4,12},{8,0},{12,4},{1,9},{5,13},{9,1},{13,5},{2,10},{6,14},... | collective-permute-start | bytes 442376 | tf_op jit(solution)/shard_map/ppermute | solution.py:27
  8.7 5.2 %collective-permute-done.2.refs_1_ = bf16[96,768]{1,0:T(8,128)(2,1)S(1)} collective-permute-done((bf16[96,768]{1,0:T(8,128)(2,1)S(1)}, bf16[96,768]{1,0:T(8,128)(2,1)S(1)}, u32[]{:S(2)}, u32[]{:S(2)}) %collective-permute-start.2) | collective-permute-done | bytes 147488 | tf_op jit(solution)/shard_map/ppermute | solution.py:27
  13.9 1.1 collective-permute-done.3.refs_2_
  15.1 1.4 %collective-permute-start.4 = (bf16[272,1536]{1,0:T(8,128)(2,1)S(1)}, bf16[272,1536]{1,0:T(8,128)(2,1)S(1)}, u32[]{:S(2)}, u32[]{:S(2)}) collective-permute-start(bf16[272,1536]{1,0:T(8,128)(2,1)S(1)} %first.1.refs_0_), channel_id=1, source_target_pairs={{0,8},{4,12},{8,0},{12,4},{1,9},{5,13},{9,1},{13,5},{2,10},{6,14},... | collective-permute-start | bytes 2506760 | tf_op jit(solution)/shard_map/ppermute | solution.py:27
  16.6 2.6 %collective-permute-start.6 = (bf16[2,96,768]{2,1,0:T(8,128)(2,1)S(1)}, bf16[2,96,768]{2,1,0:T(8,128)(2,1)S(1)}, u32[]{:S(2)}, u32[]{:S(2)}) collective-permute-start(bf16[2,96,768]{2,1,0:T(8,128)(2,1)S(1)} %far.1.refs_1_), channel_id=1, source_target_pairs={{0,1},{1,3},{3,2},{2,0},{4,5},{5,7},{7,6},{6,4},{8,9},{9,11},{11,1... | collective-permute-start | bytes 884744 | tf_op jit(solution)/shard_map/ppermute | solution.py:46
  19.2 1.6 %collective-permute-start.5 = (bf16[2,96,768]{2,1,0:T(8,128)(2,1)S(1)}, bf16[2,96,768]{2,1,0:T(8,128)(2,1)}, u32[]{:S(2)}, u32[]{:S(2)}) collective-permute-start(bf16[2,96,768]{2,1,0:T(8,128)(2,1)S(1)} %collective-permute-done.1.refs_0_), channel_id=1, source_target_pairs={{0,1},{1,3},{3,2},{2,0},{4,5},{5,7},{7,6},{6,4},{8,9},{9,11},{11,1... | collective-permute-start | bytes 884744 | tf_op jit(solution)/shard_map/ppermute | solution.py:46
  20.8 6.6 %collective-permute-done.6.refs_1_ = bf16[2,96,768]{2,1,0:T(8,128)(2,1)S(1)} collective-permute-done((bf16[2,96,768]{2,1,0:T(8,128)(2,1)S(1)}, bf16[2,96,768]{2,1,0:T(8,128)(2,1)S(1)}, u32[]{:S(2)}, u32[]{:S(2)}) %collective-permute-start.6) | collective-permute-done | bytes 294944 | tf_op jit(solution)/shard_map/ppermute | solution.py:46
  27.4 1.7 %collective-permute-start.7 = (bf16[2,96,768]{2,1,0:T(8,128)(2,1)S(1)}, bf16[2,96,768]{2,1,0:T(8,128)(2,1)}, u32[]{:S(2)}, u32[]{:S(2)}) collective-permute-start(bf16[2,96,768]{2,1,0:T(8,128)(2,1)S(1)} %collective-permute-done.6.refs_1_), channel_id=1, source_target_pairs={{0,1},{1,3},{3,2},{2,0},{4,5},{5,7},{7,6},{6,4},{8,9},{9,11},{11,1... | collective-permute-start | bytes 884744 | tf_op jit(solution)/shard_map/ppermute | solution.py:46
  29.0 4.7 %collective-permute-done.5.refs_1_.refs_0_ = bf16[2,96,768]{2,1,0:T(8,128)(2,1)} collective-permute-done((bf16[2,96,768]{2,1,0:T(8,128)(2,1)S(1)}, bf16[2,96,768]{2,1,0:T(8,128)(2,1)}, u32[]{:S(2)}, u32[]{:S(2)}) %collective-permute-start.5) | collective-permute-done | bytes 294944 | tf_op jit(solution)/shard_map/ppermute | solution.py:46
  33.8 6.0 %collective-permute-done.7.refs_2_.refs_1_ = bf16[2,96,768]{2,1,0:T(8,128)(2,1)} collective-permute-done((bf16[2,96,768]{2,1,0:T(8,128)(2,1)S(1)}, bf16[2,96,768]{2,1,0:T(8,128)(2,1)}, u32[]{:S(2)}, u32[]{:S(2)}) %collective-permute-start.7) | collective-permute-done | bytes 294944 | tf_op jit(solution)/shard_map/ppermute | solution.py:46
  39.8 0.1 collective-permute-start.10
  40.0 0.6 collective-permute-start.8
  40.6 1.7 %collective-permute-start.11 = (bf16[2,96,768]{2,1,0:T(8,128)(2,1)}, bf16[2,96,768]{2,1,0:T(8,128)(2,1)}, u32[]{:S(2)}, u32[]{:S(2)}) collective-permute-start(bf16[2,96,768]{2,1,0:T(8,128)(2,1)} %collective-permute-done.5.refs_1_.refs_0_), channel_id=1, source_target_pairs={{0,1},{1,3},{3,2},{2,0},{4,5},{5,7},{7,6},{6,4},{8,9},{9,11},{11,1... | collective-permute-start | bytes 884744 | tf_op jit(solution)/shard_map/ppermute | solution.py:46
  42.2 1.6 %collective-permute-start.12 = (bf16[2,96,768]{2,1,0:T(8,128)(2,1)}, bf16[2,96,768]{2,1,0:T(8,128)(2,1)}, u32[]{:S(2)}, u32[]{:S(2)}) collective-permute-start(bf16[2,96,768]{2,1,0:T(8,128)(2,1)} %collective-permute-done.7.refs_2_.refs_1_), channel_id=1, source_target_pairs={{0,1},{1,3},{3,2},{2,0},{4,5},{5,7},{7,6},{6,4},{8,9},{9,11},{11,1... | collective-permute-start | bytes 884744 | tf_op jit(solution)/shard_map/ppermute | solution.py:46
  43.9 0.9 copy-done.17
  44.8 0.1 copy.26.times.refs_1_
  44.9 1.0 copy-done.4
  45.9 0.9 copy-done.6
  46.8 0.1 copy-done.8
  47.0 1.1 place2.1.refs_4_.refs_11_
  48.2 4.8 %norm.1 = (bf16[512,1536]{1,0:T(8,128)(2,1)S(1)}, bf16[512,1536]{1,0:T(8,128)(2,1)S(1)}, f32[512,128]{1,0:T(8,128)S(1)}, f32[512,128]{1,0:T(8,128)S(1)}, f32[512...) custom-call(s32[4,1]{1,0:T(4,128)S(1)} %copy.26.times.refs_1_, ...), custom_call_target="tpu_custom_call" | custom-call | tf_op jit(solution)/shard_map/norm/pallas_call | solution.py:456
  53.0 4.2 %collective-permute-done.12.refs_10_ = bf16[2,96,768]{2,1,0:T(8,128)(2,1)} collective-permute-done((bf16[2,96,768]{2,1,0:T(8,128)(2,1)}, bf16[2,96,768]{2,1,0:T(8,128)(2,1)}, u32[]{:S(2)}, u32[]{:S(2)}) %collective-permute-start.12) | collective-permute-done | bytes 294944 | tf_op jit(solution)/shard_map/ppermute | solution.py:46
  57.2 4.6 %step0.1 = (bf16[2,128,384]{2,1,0:T(8,128)(2,1)S(1)}, bf16[2,128,384]{2,1,0:T(8,128)(2,1)S(1)}, bf16[1536,768]{1,0:T(8,128)(2,1)S(1)}) custom-call(f32[1,16]{1,0:T(1,128)S(1)} %copy-done.15, s32[4,1]{1,0:T(4,128)S(1)} %copy.26.times.refs_1_, f32[1,1536]{1,0:T(1,128)S(1)} %copy-done.10, f32[1,1536]{1,0:T(1,128)S(1)} %copy-done.11, ...), custom_call_target="tpu_custom_call", output_to_operand_aliasing={{2}: (11, {})} | custom-call | flops 1610612736 | bytes 3145728 | tf_op jit(solution)/shard_map/step0/pallas_call | solution.py:456
  61.9 0.1 collective-permute-start.14
  62.0 1.6 %collective-permute-start.15 = (bf16[2,128,384]{2,1,0:T(8,128)(2,1)S(1)}, bf16[2,128,384]{2,1,0:T(8,128)(2,1)S(1)}, u32[]{:S(2)}, u32[]{:S(2)}) collective-permute-start(bf16[2,128,384]{2,1,0:T(8,128)(2,1)S(1)} %get-tuple-element.50.refs_1_.refs_0_), channel_id=1, source_target_pairs={{0,16},{16,0},{1,17},{17,1},{2,18},{18,2},{3,19},{19,3},{4,20},{20... | collective-permute-start | bytes 589832 | tf_op jit(solution)/shard_map/ppermute | solution.py:31
  63.6 0.5 collective-permute-start.19
  64.1 4.1 %step1.1 = (bf16[2,128,384]{2,1,0:T(8,128)(2,1)S(1)}, bf16[2,128,384]{2,1,0:T(8,128)(2,1)S(1)}) custom-call(f32[1,16]{1,0:T(1,128)S(1)} %copy-done.15, s32[4,1]{1,0:T(4,128)S(1)} %copy.26.times.refs_1_, f32[1,1536]{1,0:T(1,128)S(1)} %copy-done.10, f32[1,1536]{1,0:T(1,128)S(1)} %copy-done.11, f32[1,1536]{1,0:T(1,128)S(1)} %copy-done.14, ...), custom_call_target="tpu_custom_call" | custom-call | flops 1610612736 | bytes 3145728 | tf_op jit(solution)/shard_map/step1/pallas_call | solution.py:456
  68.1 1.6 %collective-permute-start.23 = (bf16[2,128,384]{2,1,0:T(8,128)(2,1)S(1)}, bf16[2,128,384]{2,1,0:T(8,128)(2,1)S(1)}, u32[]{:S(2)}, u32[]{:S(2)}) collective-permute-start(bf16[2,128,384]{2,1,0:T(8,128)(2,1)S(1)} %get-tuple-element.60.refs_2_), channel_id=1, source_target_pairs={{0,16},{16,0},{1,17},{17,1},{2,18},{18,2},{3,19},{19,3},{4,20},{20... | collective-permute-start | bytes 589832 | tf_op jit(solution)/shard_map/ppermute | solution.py:31
  69.7 0.5 collective-permute-start.25
  70.2 1.5 %collective-permute-start.16 = (bf16[2,128,384]{2,1,0:T(8,128)(2,1)S(1)}, bf16[2,128,384]{2,1,0:T(8,128)(2,1)S(1)}, u32[]{:S(2)}, u32[]{:S(2)}) collective-permute-start(bf16[2,128,384]{2,1,0:T(8,128)(2,1)S(1)} %collective-permute-done.15.refs_11_), channel_id=1, source_target_pairs={{0,8},{4,12},{8,0},{12,4},{1,9},{5,13},{9,1},{13,5},{2,10},{6,14},... | collective-permute-start | bytes 589832 | tf_op jit(solution)/shard_map/ppermute | solution.py:27
  71.7 2.2 %collective-permute-done.19.refs_15_ = bf16[2,128,384]{2,1,0:T(8,128)(2,1)S(1)} collective-permute-done((bf16[2,128,384]{2,1,0:T(8,128)(2,1)S(1)}, bf16[2,128,384]{2,1,0:T(8,128)(2,1)S(1)}, u32[]{:S(2)}, u32[]{:S(2)}) %collective-permute-start.19) | collective-permute-done | bytes 196640 | tf_op jit(solution)/shard_map/ppermute | solution.py:31
  73.9 1.5 %collective-permute-start.20 = (bf16[2,128,384]{2,1,0:T(8,128)(2,1)S(1)}, bf16[2,128,384]{2,1,0:T(8,128)(2,1)S(1)}, u32[]{:S(2)}, u32[]{:S(2)}) collective-permute-start(bf16[2,128,384]{2,1,0:T(8,128)(2,1)S(1)} %collective-permute-done.19.refs_15_), channel_id=1, source_target_pairs={{0,8},{4,12},{8,0},{12,4},{1,9},{5,13},{9,1},{13,5},{2,10},{6,14},... | collective-permute-start | bytes 589832 | tf_op jit(solution)/shard_map/ppermute | solution.py:27
  75.4 2.7 %collective-permute-done.23.refs_0_ = bf16[2,128,384]{2,1,0:T(8,128)(2,1)S(1)} collective-permute-done((bf16[2,128,384]{2,1,0:T(8,128)(2,1)S(1)}, bf16[2,128,384]{2,1,0:T(8,128)(2,1)S(1)}, u32[]{:S(2)}, u32[]{:S(2)}) %collective-permute-start.23) | collective-permute-done | bytes 196640 | tf_op jit(solution)/shard_map/ppermute | solution.py:31
  78.2 3.8 %collective-permute-done.25.refs_2_ = bf16[2,128,384]{2,1,0:T(8,128)(2,1)S(1)} collective-permute-done((bf16[2,128,384]{2,1,0:T(8,128)(2,1)S(1)}, bf16[2,128,384]{2,1,0:T(8,128)(2,1)S(1)}, u32[]{:S(2)}, u32[]{:S(2)}) %collective-permute-start.25) | collective-permute-done | bytes 196640 | tf_op jit(solution)/shard_map/ppermute | solution.py:31
  81.9 0.5 collective-permute-start.18
  82.4 0.1 collective-permute-start.22
  82.5 1.5 %collective-permute-start.24 = (bf16[2,128,384]{2,1,0:T(8,128)(2,1)S(1)}, bf16[2,128,384]{2,1,0:T(8,128)(2,1)S(1)}, u32[]{:S(2)}, u32[]{:S(2)}) collective-permute-start(bf16[2,128,384]{2,1,0:T(8,128)(2,1)S(1)} %collective-permute-done.23.refs_0_), channel_id=1, source_target_pairs={{0,8},{4,12},{8,0},{12,4},{1,9},{5,13},{9,1},{13,5},{2,10},{6,14},... | collective-permute-start | bytes 589832 | tf_op jit(solution)/shard_map/ppermute | solution.py:27
  84.0 0.8 collective-permute-start.26
  84.9 5.1 %step2.1 = (bf16[2,128,384]{2,1,0:T(8,128)(2,1)S(1)}, bf16[2,128,384]{2,1,0:T(8,128)(2,1)S(1)}) custom-call(f32[1,16]{1,0:T(1,128)S(1)} %copy-done.15, s32[4,1]{1,0:T(4,128)S(1)} %copy.26.times.refs_1_, f32[1,1536]{1,0:T(1,128)S(1)} %copy-done.10, f32[1,1536]{1,0:T(1,128)S(1)} %copy-done.11, f32[1,1536]{1,0:T(1,128)S(1)} %copy-done.14, ...), custom_call_target="tpu_custom_call" | custom-call | flops 1610612736 | bytes 3145728 | tf_op jit(solution)/shard_map/step2/pallas_call | solution.py:456
  90.0 0.2 collective-permute-done.24.refs_1_
  90.2 3.8 %collective-permute-done.26.refs_3_ = bf16[2,128,384]{2,1,0:T(8,128)(2,1)S(1)} collective-permute-done((bf16[2,128,384]{2,1,0:T(8,128)(2,1)S(1)}, bf16[2,128,384]{2,1,0:T(8,128)(2,1)S(1)}, u32[]{:S(2)}, u32[]{:S(2)}) %collective-permute-start.26) | collective-permute-done | bytes 196640 | tf_op jit(solution)/shard_map/ppermute | solution.py:27
  94.0 0.5 collective-permute-start.28
  94.5 0.5 collective-permute-start.30
  95.0 0.5 early.1
  95.5 0.1 collective-permute-start.31
  95.6 1.6 %collective-permute-start.32 = (bf16[2,128,384]{2,1,0:T(8,128)(2,1)S(1)}, bf16[2,128,384]{2,1,0:T(8,128)(2,1)S(1)}, u32[]{:S(2)}, u32[]{:S(2)}) collective-permute-start(bf16[2,128,384]{2,1,0:T(8,128)(2,1)S(1)} %get-tuple-element.70), channel_id=1, source_target_pairs={{0,8},{4,12},{8,0},{12,4},{1,9},{5,13},{9,1},{13,5},{2,10},{6,14},... | collective-permute-start | bytes 589832 | tf_op jit(solution)/shard_map/ppermute | solution.py:27
  97.1 0.3 collective-permute-start.33
  97.4 4.9 %step3.1 = (bf16[2,128,384]{2,1,0:T(8,128)(2,1)S(1)}, bf16[2,128,384]{2,1,0:T(8,128)(2,1)S(1)}) custom-call(f32[1,16]{1,0:T(1,128)S(1)} %copy-done.15, s32[4,1]{1,0:T(4,128)S(1)} %copy.26.times.refs_1_, f32[1,1536]{1,0:T(1,128)S(1)} %copy-done.10, f32[1,1536]{1,0:T(1,128)S(1)} %copy-done.11, f32[1,1536]{1,0:T(1,128)S(1)} %copy-done.14, ...), custom_call_target="tpu_custom_call" | custom-call | flops 1610612736 | bytes 3145728 | tf_op jit(solution)/shard_map/step3/pallas_call | solution.py:456
  102.4 1.0 collective-permute-done.32.refs_10_
  103.3 1.2 %settle.1 = (bf16[128,384]{1,0:T(8,128)(2,1)S(1)}, bf16[128,384]{1,0:T(8,128)(2,1)S(1)}, bf16[128,384]{1,0:T(8,128)(2,1)S(1)}, bf16[128,384]{1,0:T(8,128)(2,1)S(...) custom-call(bf16[2,128,384]{2,1,0:T(8,128)(2,1)S(1)} %get-tuple-elem, ...), custom_call_target="tpu_custom_call" | custom-call | tf_op jit(solution)/shard_map/settle/pallas_call | solution.py:456
  104.6 0.8 collective-permute-start.37
  105.4 1.5 %collective-permute-start.35 = (bf16[128,384]{1,0:T(8,128)(2,1)S(1)}, bf16[128,384]{1,0:T(8,128)(2,1)S(1)}, u32[]{:S(2)}, u32[]{:S(2)}) collective-permute-start(bf16[128,384]{1,0:T(8,128)(2,1)S(1)} %get-tuple-element.76), channel_id=1, source_target_pairs={{0,8},{4,12},{8,0},{12,4},{1,9},{5,13},{9,1},{13,5},{2,10},{6,14},... | collective-permute-start | bytes 294920 | tf_op jit(solution)/shard_map/ppermute | solution.py:27
  106.9 0.4 collective-permute-start.36
  107.3 2.5 %collective-permute-start.38 = (bf16[96,256]{1,0:T(8,128)(2,1)S(1)}, bf16[96,256]{1,0:T(8,128)(2,1)S(1)}, u32[]{:S(2)}, u32[]{:S(2)}) collective-permute-start(bf16[96,256]{1,0:T(8,128)(2,1)S(1)} %get-tuple-element.80), channel_id=1, source_target_pairs={{0,2},{1,3},{2,0},{3,1},{4,6},{5,7},{6,4},{7,5},{8,10},{9,11},{10,... | collective-permute-start | bytes 147464 | tf_op jit(solution)/shard_map/ppermute | solution.py:36
  109.8 0.7 collective-permute-done.37.refs_7_
  110.5 1.0 collective-permute-start.39
  111.5 1.9 %collective-permute-done.38.refs_8_ = bf16[96,256]{1,0:T(8,128)(2,1)S(1)} collective-permute-done((bf16[96,256]{1,0:T(8,128)(2,1)S(1)}, bf16[96,256]{1,0:T(8,128)(2,1)S(1)}, u32[]{:S(2)}, u32[]{:S(2)}) %collective-permute-start.38) | collective-permute-done | bytes 49184 | tf_op jit(solution)/shard_map/ppermute | solution.py:36
  113.4 1.2 %collective-permute-done.39.refs_9_ = bf16[96,256]{1,0:T(8,128)(2,1)S(1)} collective-permute-done((bf16[96,256]{1,0:T(8,128)(2,1)S(1)}, bf16[96,256]{1,0:T(8,128)(2,1)S(1)}, u32[]{:S(2)}, u32[]{:S(2)}) %collective-permute-start.39) | collective-permute-done | bytes 49184 | tf_op jit(solution)/shard_map/ppermute | solution.py:36
  114.6 1.5 %finish.1 = (bf16[3,128,1536]{2,1,0:T(8,128)(2,1)}, f32[96,256]{1,0:T(8,128)}) custom-call(bf16[3,128,1536]{2,1,0:T(8,128)(2,1)} %get-tuple-element.72.refs_0_, bf16[2,128,384]{2,1,0:T(8,128)(2,1)S(1)} %collective-permute-done.33.refs_1_, bf16[128,384]{1,0:T(8,128)(2,1)S(1)} %get-tuple-element.74.refs_2_, ...), custom_call_target="tpu_custom_call", output_to_operand_aliasing={{0}: (0, {})} | custom-call | tf_op jit(solution)/shard_map/finish/pallas_call | solution.py:456
  (74 shorter events, 0.4 us)
Async XLA Ops:
  0.6 14.4 %copy-start.1 = (bf16[1,3,1,128,1536]{4,3,2,1,0:T(8,128)(2,1)S(1)}, bf16[1,3,1,128,1536]{4,3,2,1,0:T(8,128)(2,1)}, u32[]{:S(2)}) copy-start(bf16[1,3,1,128,1536]{4,3,2,1,0:T(8,128)(2,1)} %incoming.3) | copy-start | bytes 3538948
  0.6 14.4 %copy-start.16 = (s32[4,1,128]{2,1,0:T(1,128)S(1)}, s32[4,1,128]{2,1,0:T(1,128)}, u32[]{:S(2)}) copy-start(s32[4,1,128]{2,1,0:T(1,128)} %contacts.1) | copy-start | bytes 6148
  2.0 1.5 %collective-permute-start = (bf16[96,768]{1,0:T(8,128)(2,1)S(1)}, bf16[96,768]{1,0:T(8,128)(2,1)S(1)}, u32[]{:S(2)}, u32[]{:S(2)}) collective-permute-start(bf16[96,768]{1,0:T(8,128)(2,1)S(1)} %get-tuple-element.44), channel_id=1, source_target_pairs={{0,4},{4,0},{8,12},{12,8},{1,5},{5,1},{9,13},{13,9},{2,6},{6,2},{1... | collective-permute-start | bytes 442376 | tf_op jit(solution)/shard_map/ppermute | solution.py:27
  3.5 11.5 %collective-permute-start.1 = (bf16[2,96,768]{2,1,0:T(8,128)(2,1)S(1)}, bf16[2,96,768]{2,1,0:T(8,128)(2,1)S(1)}, u32[]{:S(2)}, u32[]{:S(2)}) collective-permute-start(bf16[2,96,768]{2,1,0:T(8,128)(2,1)S(1)} %near.1.refs_0_), channel_id=1, source_target_pairs={{0,1},{1,3},{3,2},{2,0},{4,5},{5,7},{7,6},{6,4},{8,9},{9,11},{11,1... | collective-permute-start | bytes 884744 | tf_op jit(solution)/shard_map/ppermute | solution.py:46
  6.5 0.7 copy-start.3
  7.2 6.7 %collective-permute-start.2 = (bf16[96,768]{1,0:T(8,128)(2,1)S(1)}, bf16[96,768]{1,0:T(8,128)(2,1)S(1)}, u32[]{:S(2)}, u32[]{:S(2)}) collective-permute-start(bf16[96,768]{1,0:T(8,128)(2,1)S(1)} %get-tuple-element.45), channel_id=1, source_target_pairs={{0,8},{4,12},{8,0},{12,4},{1,9},{5,13},{9,1},{13,5},{2,10},{6,14},... | collective-permute-start | bytes 442376 | tf_op jit(solution)/shard_map/ppermute | solution.py:27
  8.7 6.3 %collective-permute-start.3 = (bf16[96,768]{1,0:T(8,128)(2,1)S(1)}, bf16[96,768]{1,0:T(8,128)(2,1)S(1)}, u32[]{:S(2)}, u32[]{:S(2)}) collective-permute-start(bf16[96,768]{1,0:T(8,128)(2,1)S(1)} %get-tuple-element.46), channel_id=1, source_target_pairs={{0,12},{4,8},{8,4},{12,0},{1,13},{5,9},{9,5},{13,1},{2,14},{6,10},... | collective-permute-start | bytes 442376 | tf_op jit(solution)/shard_map/ppermute | solution.py:27
  15.0 4.2 %copy-start.5 = (bf16[2,96,768]{2,1,0:T(8,128)(2,1)}, bf16[2,96,768]{2,1,0:T(8,128)(2,1)S(1)}, u32[]{:S(2)}) copy-start(bf16[2,96,768]{2,1,0:T(8,128)(2,1)S(1)} %collective-permute-done.1.refs_0_) | copy-start | bytes 884740
  15.1 24.8 %copy-start.2 = (bf16[272,1536]{1,0:T(8,128)(2,1)}, bf16[272,1536]{1,0:T(8,128)(2,1)S(1)}, u32[]{:S(2)}) copy-start(bf16[272,1536]{1,0:T(8,128)(2,1)S(1)} %first.1.refs_0_) | copy-start | bytes 2506756
  15.1 24.8 %copy-start.9 = (bf16[1,3,1,128,256]{4,3,2,1,0:T(8,128)(2,1)S(1)}, bf16[1,3,1,128,256]{4,3,2,1,0:T(8,128)(2,1)}, u32[]{:S(2)}) copy-start(bf16[1,3,1,128,256]{4,3,2,1,0:T(8,128)(2,1)} %cotangent.1) | copy-start | bytes 589828
  15.1 24.6 %collective-permute-start.4 = (bf16[272,1536]{1,0:T(8,128)(2,1)S(1)}, bf16[272,1536]{1,0:T(8,128)(2,1)S(1)}, u32[]{:S(2)}, u32[]{:S(2)}) collective-permute-start(bf16[272,1536]{1,0:T(8,128)(2,1)S(1)} %first.1.refs_0_), channel_id=1, source_target_pairs={{0,8},{4,12},{8,0},{12,4},{1,9},{5,13},{9,1},{13,5},{2,10},{6,14},... | collective-permute-start | bytes 2506760 | tf_op jit(solution)/shard_map/ppermute | solution.py:27
  16.6 10.8 %collective-permute-start.6 = (bf16[2,96,768]{2,1,0:T(8,128)(2,1)S(1)}, bf16[2,96,768]{2,1,0:T(8,128)(2,1)S(1)}, u32[]{:S(2)}, u32[]{:S(2)}) collective-permute-start(bf16[2,96,768]{2,1,0:T(8,128)(2,1)S(1)} %far.1.refs_1_), channel_id=1, source_target_pairs={{0,1},{1,3},{3,2},{2,0},{4,5},{5,7},{7,6},{6,4},{8,9},{9,11},{11,1... | collective-permute-start | bytes 884744 | tf_op jit(solution)/shard_map/ppermute | solution.py:46
  19.2 14.6 %collective-permute-start.5 = (bf16[2,96,768]{2,1,0:T(8,128)(2,1)S(1)}, bf16[2,96,768]{2,1,0:T(8,128)(2,1)}, u32[]{:S(2)}, u32[]{:S(2)}) collective-permute-start(bf16[2,96,768]{2,1,0:T(8,128)(2,1)S(1)} %collective-permute-done.1.refs_0_), channel_id=1, source_target_pairs={{0,1},{1,3},{3,2},{2,0},{4,5},{5,7},{7,6},{6,4},{8,9},{9,11},{11,1... | collective-permute-start | bytes 884744 | tf_op jit(solution)/shard_map/ppermute | solution.py:46
  27.4 12.4 %copy-start.7 = (bf16[2,96,768]{2,1,0:T(8,128)(2,1)}, bf16[2,96,768]{2,1,0:T(8,128)(2,1)S(1)}, u32[]{:S(2)}) copy-start(bf16[2,96,768]{2,1,0:T(8,128)(2,1)S(1)} %collective-permute-done.6.refs_1_) | copy-start | bytes 884740
  27.4 12.4 %collective-permute-start.7 = (bf16[2,96,768]{2,1,0:T(8,128)(2,1)S(1)}, bf16[2,96,768]{2,1,0:T(8,128)(2,1)}, u32[]{:S(2)}, u32[]{:S(2)}) collective-permute-start(bf16[2,96,768]{2,1,0:T(8,128)(2,1)S(1)} %collective-permute-done.6.refs_1_), channel_id=1, source_target_pairs={{0,1},{1,3},{3,2},{2,0},{4,5},{5,7},{7,6},{6,4},{8,9},{9,11},{11,1... | collective-permute-start | bytes 884744 | tf_op jit(solution)/shard_map/ppermute | solution.py:46
  29.0 14.9 %collective-permute-start.9 = (bf16[272,1536]{1,0:T(8,128)(2,1)S(1)}, bf16[272,1536]{1,0:T(8,128)(2,1)S(1)}, u32[]{:S(2)}, u32[]{:S(2)}) collective-permute-start(bf16[272,1536]{1,0:T(8,128)(2,1)S(1)} %first.1.refs_0_), channel_id=1, source_target_pairs={{0,4},{4,0},{8,12},{12,8},{1,5},{5,1},{9,13},{13,9},{2,6},{6,2},{1... | collective-permute-start | bytes 2506760 | tf_op jit(solution)/shard_map/ppermute | solution.py:27
  39.8 6.1 %copy-start = (bf16[272,1536]{1,0:T(8,128)(2,1)}, bf16[272,1536]{1,0:T(8,128)(2,1)S(1)}, u32[]{:S(2)}) copy-start(bf16[272,1536]{1,0:T(8,128)(2,1)S(1)} %tie.3.dep.refs_1_) | copy-start | bytes 2506756
  39.8 5.0 %copy-start.18 = (s32[4,1]{0,1:T(1,128)S(1)}, s32[4,1]{0,1:T(1,128)}, u32[]{:S(2)}) copy-start(s32[4,1]{0,1:T(1,128)} %param.15) | copy-start | bytes 52
  39.8 8.4 %collective-permute-start.10 = (bf16[272,1536]{1,0:T(8,128)(2,1)S(1)}, bf16[272,1536]{1,0:T(8,128)(2,1)}, u32[]{:S(2)}, u32[]{:S(2)}) collective-permute-start(bf16[272,1536]{1,0:T(8,128)(2,1)S(1)} %tie.3.dep.refs_1_), channel_id=1, source_target_pairs={{0,4},{4,0},{8,12},{12,8},{1,5},{5,1},{9,13},{13,9},{2,6},{6,2},{1... | collective-permute-start | bytes 2506760 | tf_op jit(solution)/shard_map/ppermute | solution.py:27
  40.0 21.9 %collective-permute-start.8 = (bf16[256,1536]{1,0:T(8,128)(2,1)S(1)}, bf16[256,1536]{1,0:T(8,128)(2,1)S(1)}, u32[]{:S(2)}, u32[]{:S(2)}) collective-permute-start(bf16[256,1536]{1,0:T(8,128)(2,1)S(1)} %second.1.refs_6_.refs_4_), channel_id=1, source_target_pairs={{0,8},{4,12},{8,0},{12,4},{1,9},{5,13},{9,1},{13,5},{2,10},{6,14},... | collective-permute-start | bytes 2359304 | tf_op jit(solution)/shard_map/ppermute | solution.py:27
  40.6 12.5 %collective-permute-start.11 = (bf16[2,96,768]{2,1,0:T(8,128)(2,1)}, bf16[2,96,768]{2,1,0:T(8,128)(2,1)}, u32[]{:S(2)}, u32[]{:S(2)}) collective-permute-start(bf16[2,96,768]{2,1,0:T(8,128)(2,1)} %collective-permute-done.5.refs_1_.refs_0_), channel_id=1, source_target_pairs={{0,1},{1,3},{3,2},{2,0},{4,5},{5,7},{7,6},{6,4},{8,9},{9,11},{11,1... | collective-permute-start | bytes 884744 | tf_op jit(solution)/shard_map/ppermute | solution.py:46
  42.2 15.0 %collective-permute-start.12 = (bf16[2,96,768]{2,1,0:T(8,128)(2,1)}, bf16[2,96,768]{2,1,0:T(8,128)(2,1)}, u32[]{:S(2)}, u32[]{:S(2)}) collective-permute-start(bf16[2,96,768]{2,1,0:T(8,128)(2,1)} %collective-permute-done.7.refs_2_.refs_1_), channel_id=1, source_target_pairs={{0,1},{1,3},{3,2},{2,0},{4,5},{5,7},{7,6},{6,4},{8,9},{9,11},{11,1... | collective-permute-start | bytes 884744 | tf_op jit(solution)/shard_map/ppermute | solution.py:46
  43.9 0.9 copy-start.17
  44.8 24.9 %collective-permute-start.13 = (bf16[256,1536]{1,0:T(8,128)(2,1)S(1)}, bf16[256,1536]{1,0:T(8,128)(2,1)S(1)}, u32[]{:S(2)}, u32[]{:S(2)}) collective-permute-start(bf16[256,1536]{1,0:T(8,128)(2,1)S(1)} %second.1.refs_6_.refs_4_), channel_id=1, source_target_pairs={{0,4},{4,0},{8,12},{12,8},{1,5},{5,1},{9,13},{13,9},{2,6},{6,2},{1... | collective-permute-start | bytes 2359304 | tf_op jit(solution)/shard_map/ppermute | solution.py:27
  44.9 1.0 copy-start.4
  45.9 1.0 copy-start.6
  45.9 1.0 copy-start.8
  47.0 1.2 %copy-start.10 = (f32[1,1536]{1,0:T(1,128)S(1)}, f32[1,1536]{1,0:T(1,128)}, u32[]{:S(2)}) copy-start(f32[1,1536]{1,0:T(1,128)} %refs_2_.7) | copy-start | bytes 18436
  47.0 1.2 %copy-start.11 = (f32[1,1536]{1,0:T(1,128)S(1)}, f32[1,1536]{1,0:T(1,128)}, u32[]{:S(2)}) copy-start(f32[1,1536]{1,0:T(1,128)} %refs_3_.7) | copy-start | bytes 18436
  47.0 1.2 %copy-start.12 = (bf16[1,16,1536]{2,1,0:T(8,128)(2,1)S(1)}, bf16[1,16,1536]{2,1,0:T(8,128)(2,1)}, u32[]{:S(2)}) copy-start(bf16[1,16,1536]{2,1,0:T(8,128)(2,1)} %table.1) | copy-start | bytes 147460
  48.1 9.1 %copy-start.13 = (s32[4,1,512]{2,1,0:T(1,128)S(1)}, s32[4,1,512]{2,1,0:T(1,128)}, u32[]{:S(2)}) copy-start(s32[4,1,512]{2,1,0:T(1,128)} %refs_5_.7) | copy-start | bytes 24580
  48.2 9.1 %copy-start.14 = (f32[1,1536]{1,0:T(1,128)S(1)}, f32[1,1536]{1,0:T(1,128)}, u32[]{:S(2)}) copy-start(f32[1,1536]{1,0:T(1,128)} %refs_4_.7) | copy-start | bytes 18436
  48.2 9.0 %copy-start.15 = (f32[1,16]{1,0:T(1,128)S(1)}, f32[1,16]{1,0:T(1,128)}, u32[]{:S(2)}) copy-start(f32[1,16]{1,0:T(1,128)} %refs_0_.7) | copy-start | bytes 196
  61.9 23.0 %collective-permute-start.14 = (bf16[256,1536]{1,0:T(8,128)(2,1)S(1)}, bf16[256,1536]{1,0:T(8,128)(2,1)S(1)}, u32[]{:S(2)}, u32[]{:S(2)}) collective-permute-start(bf16[256,1536]{1,0:T(8,128)(2,1)S(1)} %tie.4.refs_7_.refs_5_), channel_id=1, source_target_pairs={{0,4},{4,0},{8,12},{12,8},{1,5},{5,1},{9,13},{13,9},{2,6},{6,2},{1... | collective-permute-start | bytes 2359304 | tf_op jit(solution)/shard_map/ppermute | solution.py:27
  62.0 8.3 %collective-permute-start.15 = (bf16[2,128,384]{2,1,0:T(8,128)(2,1)S(1)}, bf16[2,128,384]{2,1,0:T(8,128)(2,1)S(1)}, u32[]{:S(2)}, u32[]{:S(2)}) collective-permute-start(bf16[2,128,384]{2,1,0:T(8,128)(2,1)S(1)} %get-tuple-element.50.refs_1_.refs_0_), channel_id=1, source_target_pairs={{0,16},{16,0},{1,17},{17,1},{2,18},{18,2},{3,19},{19,3},{4,20},{20... | collective-permute-start | bytes 589832 | tf_op jit(solution)/shard_map/ppermute | solution.py:31
  63.6 10.4 %collective-permute-start.19 = (bf16[2,128,384]{2,1,0:T(8,128)(2,1)S(1)}, bf16[2,128,384]{2,1,0:T(8,128)(2,1)S(1)}, u32[]{:S(2)}, u32[]{:S(2)}) collective-permute-start(bf16[2,128,384]{2,1,0:T(8,128)(2,1)S(1)} %get-tuple-element.52.refs_1_), channel_id=1, source_target_pairs={{0,16},{16,0},{1,17},{17,1},{2,18},{18,2},{3,19},{19,3},{4,20},{20... | collective-permute-start | bytes 589832 | tf_op jit(solution)/shard_map/ppermute | solution.py:31
  68.1 10.0 %collective-permute-start.23 = (bf16[2,128,384]{2,1,0:T(8,128)(2,1)S(1)}, bf16[2,128,384]{2,1,0:T(8,128)(2,1)S(1)}, u32[]{:S(2)}, u32[]{:S(2)}) collective-permute-start(bf16[2,128,384]{2,1,0:T(8,128)(2,1)S(1)} %get-tuple-element.60.refs_2_), channel_id=1, source_target_pairs={{0,16},{16,0},{1,17},{17,1},{2,18},{18,2},{3,19},{19,3},{4,20},{20... | collective-permute-start | bytes 589832 | tf_op jit(solution)/shard_map/ppermute | solution.py:31
  69.7 12.2 %collective-permute-start.25 = (bf16[2,128,384]{2,1,0:T(8,128)(2,1)S(1)}, bf16[2,128,384]{2,1,0:T(8,128)(2,1)S(1)}, u32[]{:S(2)}, u32[]{:S(2)}) collective-permute-start(bf16[2,128,384]{2,1,0:T(8,128)(2,1)S(1)} %get-tuple-element.61.refs_3_), channel_id=1, source_target_pairs={{0,16},{16,0},{1,17},{17,1},{2,18},{18,2},{3,19},{19,3},{4,20},{20... | collective-permute-start | bytes 589832 | tf_op jit(solution)/shard_map/ppermute | solution.py:31
  70.2 11.7 %collective-permute-start.16 = (bf16[2,128,384]{2,1,0:T(8,128)(2,1)S(1)}, bf16[2,128,384]{2,1,0:T(8,128)(2,1)S(1)}, u32[]{:S(2)}, u32[]{:S(2)}) collective-permute-start(bf16[2,128,384]{2,1,0:T(8,128)(2,1)S(1)} %collective-permute-done.15.refs_11_), channel_id=1, source_target_pairs={{0,8},{4,12},{8,0},{12,4},{1,9},{5,13},{9,1},{13,5},{2,10},{6,14},... | collective-permute-start | bytes 589832 | tf_op jit(solution)/shard_map/ppermute | solution.py:27
  73.9 8.5 %collective-permute-start.20 = (bf16[2,128,384]{2,1,0:T(8,128)(2,1)S(1)}, bf16[2,128,384]{2,1,0:T(8,128)(2,1)S(1)}, u32[]{:S(2)}, u32[]{:S(2)}) collective-permute-start(bf16[2,128,384]{2,1,0:T(8,128)(2,1)S(1)} %collective-permute-done.19.refs_15_), channel_id=1, source_target_pairs={{0,8},{4,12},{8,0},{12,4},{1,9},{5,13},{9,1},{13,5},{2,10},{6,14},... | collective-permute-start | bytes 589832 | tf_op jit(solution)/shard_map/ppermute | solution.py:27
  78.2 4.4 %collective-permute-start.17 = (bf16[2,128,384]{2,1,0:T(8,128)(2,1)S(1)}, bf16[2,128,384]{2,1,0:T(8,128)(2,1)S(1)}, u32[]{:S(2)}, u32[]{:S(2)}) collective-permute-start(bf16[2,128,384]{2,1,0:T(8,128)(2,1)S(1)} %collective-permute-done.15.refs_11_), channel_id=1, source_target_pairs={{0,4},{4,0},{8,12},{12,8},{1,5},{5,1},{9,13},{13,9},{2,6},{6,2},{1... | collective-permute-start | bytes 589832 | tf_op jit(solution)/shard_map/ppermute | solution.py:27
  81.9 2.1 %collective-permute-start.21 = (bf16[2,128,384]{2,1,0:T(8,128)(2,1)S(1)}, bf16[2,128,384]{2,1,0:T(8,128)(2,1)S(1)}, u32[]{:S(2)}, u32[]{:S(2)}) collective-permute-start(bf16[2,128,384]{2,1,0:T(8,128)(2,1)S(1)} %collective-permute-done.19.refs_15_), channel_id=1, source_target_pairs={{0,4},{4,0},{8,12},{12,8},{1,5},{5,1},{9,13},{13,9},{2,6},{6,2},{1... | collective-permute-start | bytes 589832 | tf_op jit(solution)/shard_map/ppermute | solution.py:27
  81.9 2.9 %collective-permute-start.18 = (bf16[2,128,384]{2,1,0:T(8,128)(2,1)S(1)}, bf16[2,128,384]{2,1,0:T(8,128)(2,1)S(1)}, u32[]{:S(2)}, u32[]{:S(2)}) collective-permute-start(bf16[2,128,384]{2,1,0:T(8,128)(2,1)S(1)} %collective-permute-done.16.refs_12_), channel_id=1, source_target_pairs={{0,4},{4,0},{8,12},{12,8},{1,5},{5,1},{9,13},{13,9},{2,6},{6,2},{1... | collective-permute-start | bytes 589832 | tf_op jit(solution)/shard_map/ppermute | solution.py:27
  82.4 2.4 %collective-permute-start.22 = (bf16[2,128,384]{2,1,0:T(8,128)(2,1)S(1)}, bf16[2,128,384]{2,1,0:T(8,128)(2,1)S(1)}, u32[]{:S(2)}, u32[]{:S(2)}) collective-permute-start(bf16[2,128,384]{2,1,0:T(8,128)(2,1)S(1)} %collective-permute-done.20.refs_16_), channel_id=1, source_target_pairs={{0,4},{4,0},{8,12},{12,8},{1,5},{5,1},{9,13},{13,9},{2,6},{6,2},{1... | collective-permute-start | bytes 589832 | tf_op jit(solution)/shard_map/ppermute | solution.py:27
  82.5 7.7 %collective-permute-start.24 = (bf16[2,128,384]{2,1,0:T(8,128)(2,1)S(1)}, bf16[2,128,384]{2,1,0:T(8,128)(2,1)S(1)}, u32[]{:S(2)}, u32[]{:S(2)}) collective-permute-start(bf16[2,128,384]{2,1,0:T(8,128)(2,1)S(1)} %collective-permute-done.23.refs_0_), channel_id=1, source_target_pairs={{0,8},{4,12},{8,0},{12,4},{1,9},{5,13},{9,1},{13,5},{2,10},{6,14},... | collective-permute-start | bytes 589832 | tf_op jit(solution)/shard_map/ppermute | solution.py:27
  84.0 10.0 %collective-permute-start.26 = (bf16[2,128,384]{2,1,0:T(8,128)(2,1)S(1)}, bf16[2,128,384]{2,1,0:T(8,128)(2,1)S(1)}, u32[]{:S(2)}, u32[]{:S(2)}) collective-permute-start(bf16[2,128,384]{2,1,0:T(8,128)(2,1)S(1)} %collective-permute-done.25.refs_2_), channel_id=1, source_target_pairs={{0,8},{4,12},{8,0},{12,4},{1,9},{5,13},{9,1},{13,5},{2,10},{6,14},... | collective-permute-start | bytes 589832 | tf_op jit(solution)/shard_map/ppermute | solution.py:27
  94.0 1.6 %collective-permute-start.27 = (bf16[2,128,384]{2,1,0:T(8,128)(2,1)S(1)}, bf16[2,128,384]{2,1,0:T(8,128)(2,1)S(1)}, u32[]{:S(2)}, u32[]{:S(2)}) collective-permute-start(bf16[2,128,384]{2,1,0:T(8,128)(2,1)S(1)} %get-tuple-element.62.refs_11_), channel_id=1, source_target_pairs={{0,4},{4,0},{8,12},{12,8},{1,5},{5,1},{9,13},{13,9},{2,6},{6,2},{1... | collective-permute-start | bytes 589832 | tf_op jit(solution)/shard_map/ppermute | solution.py:27
  94.0 3.2 %collective-permute-start.28 = (bf16[2,128,384]{2,1,0:T(8,128)(2,1)S(1)}, bf16[2,128,384]{2,1,0:T(8,128)(2,1)S(1)}, u32[]{:S(2)}, u32[]{:S(2)}) collective-permute-start(bf16[2,128,384]{2,1,0:T(8,128)(2,1)S(1)} %get-tuple-element.63.refs_12_), channel_id=1, source_target_pairs={{0,4},{4,0},{8,12},{12,8},{1,5},{5,1},{9,13},{13,9},{2,6},{6,2},{1... | collective-permute-start | bytes 589832 | tf_op jit(solution)/shard_map/ppermute | solution.py:27
  94.5 3.0 %collective-permute-start.29 = (bf16[2,128,384]{2,1,0:T(8,128)(2,1)S(1)}, bf16[2,128,384]{2,1,0:T(8,128)(2,1)S(1)}, u32[]{:S(2)}, u32[]{:S(2)}) collective-permute-start(bf16[2,128,384]{2,1,0:T(8,128)(2,1)S(1)} %get-tuple-element.64.refs_15_), channel_id=1, source_target_pairs={{0,4},{4,0},{8,12},{12,8},{1,5},{5,1},{9,13},{13,9},{2,6},{6,2},{1... | collective-permute-start | bytes 589832 | tf_op jit(solution)/shard_map/ppermute | solution.py:27
  94.5 3.0 %collective-permute-start.30 = (bf16[2,128,384]{2,1,0:T(8,128)(2,1)S(1)}, bf16[2,128,384]{2,1,0:T(8,128)(2,1)S(1)}, u32[]{:S(2)}, u32[]{:S(2)}) collective-permute-start(bf16[2,128,384]{2,1,0:T(8,128)(2,1)S(1)} %get-tuple-element.65.refs_16_), channel_id=1, source_target_pairs={{0,4},{4,0},{8,12},{12,8},{1,5},{5,1},{9,13},{13,9},{2,6},{6,2},{1... | collective-permute-start | bytes 589832 | tf_op jit(solution)/shard_map/ppermute | solution.py:27
  95.5 6.9 %collective-permute-start.31 = (bf16[2,128,384]{2,1,0:T(8,128)(2,1)S(1)}, bf16[2,128,384]{2,1,0:T(8,128)(2,1)S(1)}, u32[]{:S(2)}, u32[]{:S(2)}) collective-permute-start(bf16[2,128,384]{2,1,0:T(8,128)(2,1)S(1)} %get-tuple-element.69), channel_id=1, source_target_pairs={{0,4},{4,0},{8,12},{12,8},{1,5},{5,1},{9,13},{13,9},{2,6},{6,2},{1... | collective-permute-start | bytes 589832 | tf_op jit(solution)/shard_map/ppermute | solution.py:27
  95.6 7.8 %collective-permute-start.32 = (bf16[2,128,384]{2,1,0:T(8,128)(2,1)S(1)}, bf16[2,128,384]{2,1,0:T(8,128)(2,1)S(1)}, u32[]{:S(2)}, u32[]{:S(2)}) collective-permute-start(bf16[2,128,384]{2,1,0:T(8,128)(2,1)S(1)} %get-tuple-element.70), channel_id=1, source_target_pairs={{0,8},{4,12},{8,0},{12,4},{1,9},{5,13},{9,1},{13,5},{2,10},{6,14},... | collective-permute-start | bytes 589832 | tf_op jit(solution)/shard_map/ppermute | solution.py:27
  97.1 10.1 %collective-permute-start.33 = (bf16[2,128,384]{2,1,0:T(8,128)(2,1)S(1)}, bf16[2,128,384]{2,1,0:T(8,128)(2,1)S(1)}, u32[]{:S(2)}, u32[]{:S(2)}) collective-permute-start(bf16[2,128,384]{2,1,0:T(8,128)(2,1)S(1)} %get-tuple-element.73), channel_id=1, source_target_pairs={{0,12},{4,8},{8,4},{12,0},{1,13},{5,9},{9,5},{13,1},{2,14},{6,10},... | collective-permute-start | bytes 589832 | tf_op jit(solution)/shard_map/ppermute | solution.py:27
  104.6 5.9 %collective-permute-start.37 = (bf16[96,256]{1,0:T(8,128)(2,1)S(1)}, bf16[96,256]{1,0:T(8,128)(2,1)S(1)}, u32[]{:S(2)}, u32[]{:S(2)}) collective-permute-start(bf16[96,256]{1,0:T(8,128)(2,1)S(1)} %get-tuple-element.79), channel_id=1, source_target_pairs={{0,1},{1,2},{2,3},{3,0},{4,5},{5,6},{6,7},{7,4},{8,9},{9,10},{10,1... | collective-permute-start | bytes 147464 | tf_op jit(solution)/shard_map/ppermute | solution.py:36
  105.4 9.2 %collective-permute-start.34 = (bf16[128,384]{1,0:T(8,128)(2,1)S(1)}, bf16[128,384]{1,0:T(8,128)(2,1)S(1)}, u32[]{:S(2)}, u32[]{:S(2)}) collective-permute-start(bf16[128,384]{1,0:T(8,128)(2,1)S(1)} %get-tuple-element.75), channel_id=1, source_target_pairs={{0,4},{4,0},{8,12},{12,8},{1,5},{5,1},{9,13},{13,9},{2,6},{6,2},{1... | collective-permute-start | bytes 294920 | tf_op jit(solution)/shard_map/ppermute | solution.py:27
  105.4 9.2 %collective-permute-start.35 = (bf16[128,384]{1,0:T(8,128)(2,1)S(1)}, bf16[128,384]{1,0:T(8,128)(2,1)S(1)}, u32[]{:S(2)}, u32[]{:S(2)}) collective-permute-start(bf16[128,384]{1,0:T(8,128)(2,1)S(1)} %get-tuple-element.76), channel_id=1, source_target_pairs={{0,8},{4,12},{8,0},{12,4},{1,9},{5,13},{9,1},{13,5},{2,10},{6,14},... | collective-permute-start | bytes 294920 | tf_op jit(solution)/shard_map/ppermute | solution.py:27
  106.9 7.7 %collective-permute-start.36 = (bf16[128,384]{1,0:T(8,128)(2,1)S(1)}, bf16[128,384]{1,0:T(8,128)(2,1)S(1)}, u32[]{:S(2)}, u32[]{:S(2)}) collective-permute-start(bf16[128,384]{1,0:T(8,128)(2,1)S(1)} %get-tuple-element.77), channel_id=1, source_target_pairs={{0,12},{4,8},{8,4},{12,0},{1,13},{5,9},{9,5},{13,1},{2,14},{6,10},... | collective-permute-start | bytes 294920 | tf_op jit(solution)/shard_map/ppermute | solution.py:27
  107.3 6.1 %collective-permute-start.38 = (bf16[96,256]{1,0:T(8,128)(2,1)S(1)}, bf16[96,256]{1,0:T(8,128)(2,1)S(1)}, u32[]{:S(2)}, u32[]{:S(2)}) collective-permute-start(bf16[96,256]{1,0:T(8,128)(2,1)S(1)} %get-tuple-element.80), channel_id=1, source_target_pairs={{0,2},{1,3},{2,0},{3,1},{4,6},{5,7},{6,4},{7,5},{8,10},{9,11},{10,... | collective-permute-start | bytes 147464 | tf_op jit(solution)/shard_map/ppermute | solution.py:36
  110.5 4.1 %collective-permute-start.39 = (bf16[96,256]{1,0:T(8,128)(2,1)S(1)}, bf16[96,256]{1,0:T(8,128)(2,1)S(1)}, u32[]{:S(2)}, u32[]{:S(2)}) collective-permute-start(bf16[96,256]{1,0:T(8,128)(2,1)S(1)} %get-tuple-element.81), channel_id=1, source_target_pairs={{0,3},{1,0},{2,1},{3,2},{4,7},{5,4},{6,5},{7,6},{8,11},{9,8},{10,9... | collective-permute-start | bytes 147464 | tf_op jit(solution)/shard_map/ppermute | solution.py:36

commit v12 on v11

--- a/solution.py
+++ b/solution.py
@@ -150,7 +150,7 @@
 
 
 def norm_kernel(turns, pieces, times, table, gain, freq, *refs):
-    sources, refs = refs[:pieces], refs[pieces + 1 :]
+    sources, refs = refs[:pieces], refs[pieces:]
     scaled, scales, owns, embeds, mod = refs[0:2], refs[2:4], refs[4:6], refs[6:8], refs[8]
     first, sems = refs[9 : 9 + pieces], refs[9 + pieces]
     copies = [
@@ -272,10 +272,14 @@
         return None, flags[batch, :, lanes].astype(jnp.float32)
 
     flag_column = columns_of(flag_of, pieces, rows)[:, 16:17]
-    projected = jnp.dot(scaled[...], weights[...], preferred_element_type=jnp.float32) * scale
     score_scale = head ** (-0.5) * math.log2(math.e)
-    proj[:, :cols] = (projected[:, :cols] * score_scale).astype(jnp.bfloat16)
-    proj[:, cols : 2 * cols] = projected[:, cols:].astype(jnp.bfloat16)
+    for at in range(0, 2 * cols, 256):
+        lane = at + lax.broadcasted_iota(jnp.int32, (1, 256), 1)
+        factor = jnp.where(lane < cols, score_scale, 1.0)
+        projected = jnp.dot(
+            scaled[...], weights[:, at : at + 256], preferred_element_type=jnp.float32
+        )
+        proj[:, at : at + 256] = (projected * scale * factor).astype(jnp.bfloat16)
     proj[:, 2 * cols :] = jnp.zeros((frames, 128), jnp.bfloat16)
     lanes = lax.broadcasted_iota(jnp.int32, (frames, 128), 1)
     row_lanes = lax.broadcasted_iota(jnp.int32, (1, 128), 1)
@@ -547,10 +551,9 @@
         + [pltpu.VMEM((frames, 128), jnp.float32)] * 2
         + [pltpu.VMEM((frames, cols), jnp.float32)] * 2
         + [pltpu.VMEM((frames, width), kind)] * 2,
-        [smem] + [vmem] * 3 + [anywhere] * (seq_count + 1),
+        [smem] + [vmem] * 3 + [anywhere] * seq_count,
         [timesteps, contact_table, norm_gain, time_freq]
-        + [pin(piece, pltpu.HBM) for piece in first]
-        + [weights],
+        + first,
         [pltpu.VMEM((1, width), jnp.float32)]
         + [pltpu.VMEM((2 * rows + 16, width), kind)] * seq_count
         + [pltpu.SemaphoreType.DMA((seq_count,))],
@@ -621,12 +624,6 @@
             (second[1],) = tie([second[1]], [outputs[-1][0]])
             second.append(swap(second[1], 1))
         if step == 2:
-            pending = [piece for k in range(HALVES) for piece in (crossing[k][0], crossing[k][1])]
-            tied = tie(pending, [outputs[-1][0]])
-            relayed[3] = []
-            for k in range(HALVES):
-                mine, across = tied[2 * k], tied[2 * k + 1]
-                relayed[3] += [mine, across, swap(mine, 1), swap(across, 1)]
             early = call(
                 functools.partial(early_kernel, turns, seq_count, HALVES, feats),
                 "early",
@@ -639,6 +636,12 @@
             )
             early, early_grad = list(early[:-1]), early[-1]
             early = [early[0]] + [swap(early[m], m) for m in range(1, seq_count)]
+            pending = [piece for k in range(HALVES) for piece in (crossing[k][0], crossing[k][1])]
+            tied = tie(pending, [early_grad])
+            relayed[3] = []
+            for k in range(HALVES):
+                mine, across = tied[2 * k], tied[2 * k + 1]
+                relayed[3] += [mine, across, swap(mine, 1), swap(across, 1)]
         if step + 2 < steps:
             crossing = []
             for half in outputs[-1]:

time: 117 us -> 116 us (level)
  Pallas kernels: 29.4 us -> 27.6 us
  waiting for transfers between devices: 46.4 us -> 47.7 us
    pallas_call x19, Pallas kernels: 29.4 us -> 27.6 us  [call(): pl.pallas_call(kernel, out_shape=out_shape, in_specs=in_specs, scratch_sh...]
    unnamed x39 -> x41, local copies, waits for them, and re-layouts: 3.72 us -> 3.98 us
  transfers between devices with their start and end apart: 40 -> 40, of which waited for: 16 -> 17; matrix products, arithmetic and copies ran while one was open for 0% -> 0% of each run, Pallas kernels for 23% -> 21%
where the time goes in v12:
time: 116 us
  waiting for transfers between devices  47.7 us (41%)
  starting transfers between devices  35.3 us (30%)
  Pallas kernels  27.6 us (24%)
  local copies, waits for them, and re-layouts  3.98 us (3%)
    pallas_call x19, Pallas kernels, call(): pl.pallas_call(kernel, out_shape=out_shape, in_specs=in_specs, scratch_sh...  27.6 us
    ppermute x6, waiting for transfers between devices, ring_step(): return lax.ppermute(value, 'dp', pairs)  21.6 us
    ppermute x27, starting transfers between devices, swap(): lax.ppermute(value, 'seq', [(source, source ^ bit) for source in range(co...  14.6 us
    ppermute x27, waiting for transfers between devices, swap(): lax.ppermute(value, 'seq', [(source, source ^ bit) for source in range(co...  13.3 us
    ppermute x6, starting transfers between devices, ring_step(): return lax.ppermute(value, 'dp', pairs)  12.2 us
    ppermute x4, waiting for transfers between devices, handed_over(): return lax.ppermute(value, 'pipe', [(0, 1), (1, 0)])  9.04 us
    ppermute x3, starting transfers between devices, shifted(): lax.ppermute(value, axis, [(source, (source + shift) % count) for source...  4.35 us
    ppermute x4, starting transfers between devices, handed_over(): return lax.ppermute(value, 'pipe', [(0, 1), (1, 0)])  4.18 us
  transfers between devices with their start and end apart: 40, of which 17 were waited for; matrix products, arithmetic and copies ran while one was open for 0% of the time, Pallas kernels for 21%

profile of v12, /device:TPU:0, one launch (start us, length us, event | category | flops | bytes accessed | tf_op | source)
XLA Modules:
  0.0 115.7 jit_solution(5796656532832921801)
XLA Ops:
  0.7 1.3 %pack.1 = (bf16[96,768]{1,0:T(8,128)(2,1)S(1)}, bf16[96,768]{1,0:T(8,128)(2,1)S(1)}, bf16[96,768]{1,0:T(8,128)(2,1)S(1)}, bf16[96,768]{1,0:T(8,128)(2,1)S(1)}) custom-call(bf16[1,96,1536]{2,1,0:T(8,128)(2,1)} %wq.1, bf16[1,96,1536]{2,1,0:T(8,128)(2,1)} %wkv.1), custom_call_target="tpu_custom_call" | custom-call | tf_op jit(solution)/shard_map/pack/pallas_call | solution.py:460
  2.0 0.5 collective-permute-start
  2.5 1.0 collective-permute-done.refs_1_
  3.5 3.0 %collective-permute-start.1 = (bf16[2,96,768]{2,1,0:T(8,128)(2,1)S(1)}, bf16[2,96,768]{2,1,0:T(8,128)(2,1)S(1)}, u32[]{:S(2)}, u32[]{:S(2)}) collective-permute-start(bf16[2,96,768]{2,1,0:T(8,128)(2,1)S(1)} %near.1.refs_0_), channel_id=1, source_target_pairs={{0,1},{1,3},{3,2},{2,0},{4,5},{5,7},{7,6},{6,4},{8,9},{9,11},{11,1... | collective-permute-start | bytes 884744 | tf_op jit(solution)/shard_map/ppermute | solution.py:46
  6.5 0.7 copy-done.3
  7.2 1.5 %collective-permute-start.2 = (bf16[96,768]{1,0:T(8,128)(2,1)S(1)}, bf16[96,768]{1,0:T(8,128)(2,1)S(1)}, u32[]{:S(2)}, u32[]{:S(2)}) collective-permute-start(bf16[96,768]{1,0:T(8,128)(2,1)S(1)} %get-tuple-element.45), channel_id=1, source_target_pairs={{0,8},{4,12},{8,0},{12,4},{1,9},{5,13},{9,1},{13,5},{2,10},{6,14},... | collective-permute-start | bytes 442376 | tf_op jit(solution)/shard_map/ppermute | solution.py:27
  8.7 5.2 %collective-permute-done.2.refs_1_ = bf16[96,768]{1,0:T(8,128)(2,1)S(1)} collective-permute-done((bf16[96,768]{1,0:T(8,128)(2,1)S(1)}, bf16[96,768]{1,0:T(8,128)(2,1)S(1)}, u32[]{:S(2)}, u32[]{:S(2)}) %collective-permute-start.2) | collective-permute-done | bytes 147488 | tf_op jit(solution)/shard_map/ppermute | solution.py:27
  14.0 1.1 collective-permute-done.3.refs_2_
  15.1 1.4 %collective-permute-start.4 = (bf16[272,1536]{1,0:T(8,128)(2,1)S(1)}, bf16[272,1536]{1,0:T(8,128)(2,1)S(1)}, u32[]{:S(2)}, u32[]{:S(2)}) collective-permute-start(bf16[272,1536]{1,0:T(8,128)(2,1)S(1)} %first.1.refs_0_), channel_id=1, source_target_pairs={{0,8},{4,12},{8,0},{12,4},{1,9},{5,13},{9,1},{13,5},{2,10},{6,14},... | collective-permute-start | bytes 2506760 | tf_op jit(solution)/shard_map/ppermute | solution.py:27
  16.6 2.6 %collective-permute-start.6 = (bf16[2,96,768]{2,1,0:T(8,128)(2,1)S(1)}, bf16[2,96,768]{2,1,0:T(8,128)(2,1)S(1)}, u32[]{:S(2)}, u32[]{:S(2)}) collective-permute-start(bf16[2,96,768]{2,1,0:T(8,128)(2,1)S(1)} %far.1.refs_1_), channel_id=1, source_target_pairs={{0,1},{1,3},{3,2},{2,0},{4,5},{5,7},{7,6},{6,4},{8,9},{9,11},{11,1... | collective-permute-start | bytes 884744 | tf_op jit(solution)/shard_map/ppermute | solution.py:46
  19.2 1.6 %collective-permute-start.5 = (bf16[2,96,768]{2,1,0:T(8,128)(2,1)S(1)}, bf16[2,96,768]{2,1,0:T(8,128)(2,1)}, u32[]{:S(2)}, u32[]{:S(2)}) collective-permute-start(bf16[2,96,768]{2,1,0:T(8,128)(2,1)S(1)} %collective-permute-done.1.refs_0_), channel_id=1, source_target_pairs={{0,1},{1,3},{3,2},{2,0},{4,5},{5,7},{7,6},{6,4},{8,9},{9,11},{11,1... | collective-permute-start | bytes 884744 | tf_op jit(solution)/shard_map/ppermute | solution.py:46
  20.8 6.6 %collective-permute-done.6.refs_1_ = bf16[2,96,768]{2,1,0:T(8,128)(2,1)S(1)} collective-permute-done((bf16[2,96,768]{2,1,0:T(8,128)(2,1)S(1)}, bf16[2,96,768]{2,1,0:T(8,128)(2,1)S(1)}, u32[]{:S(2)}, u32[]{:S(2)}) %collective-permute-start.6) | collective-permute-done | bytes 294944 | tf_op jit(solution)/shard_map/ppermute | solution.py:46
  27.4 1.7 %collective-permute-start.7 = (bf16[2,96,768]{2,1,0:T(8,128)(2,1)S(1)}, bf16[2,96,768]{2,1,0:T(8,128)(2,1)}, u32[]{:S(2)}, u32[]{:S(2)}) collective-permute-start(bf16[2,96,768]{2,1,0:T(8,128)(2,1)S(1)} %collective-permute-done.6.refs_1_), channel_id=1, source_target_pairs={{0,1},{1,3},{3,2},{2,0},{4,5},{5,7},{7,6},{6,4},{8,9},{9,11},{11,1... | collective-permute-start | bytes 884744 | tf_op jit(solution)/shard_map/ppermute | solution.py:46
  29.1 4.7 %collective-permute-done.5.refs_1_.refs_0_ = bf16[2,96,768]{2,1,0:T(8,128)(2,1)} collective-permute-done((bf16[2,96,768]{2,1,0:T(8,128)(2,1)S(1)}, bf16[2,96,768]{2,1,0:T(8,128)(2,1)}, u32[]{:S(2)}, u32[]{:S(2)}) %collective-permute-start.5) | collective-permute-done | bytes 294944 | tf_op jit(solution)/shard_map/ppermute | solution.py:46
  33.8 6.0 %collective-permute-done.7.refs_2_.refs_1_ = bf16[2,96,768]{2,1,0:T(8,128)(2,1)} collective-permute-done((bf16[2,96,768]{2,1,0:T(8,128)(2,1)S(1)}, bf16[2,96,768]{2,1,0:T(8,128)(2,1)}, u32[]{:S(2)}, u32[]{:S(2)}) %collective-permute-start.7) | collective-permute-done | bytes 294944 | tf_op jit(solution)/shard_map/ppermute | solution.py:46
  39.8 0.1 collective-permute-start.10
  40.0 0.6 collective-permute-start.8
  40.6 1.7 %collective-permute-start.11 = (bf16[2,96,768]{2,1,0:T(8,128)(2,1)}, bf16[2,96,768]{2,1,0:T(8,128)(2,1)}, u32[]{:S(2)}, u32[]{:S(2)}) collective-permute-start(bf16[2,96,768]{2,1,0:T(8,128)(2,1)} %collective-permute-done.5.refs_1_.refs_0_), channel_id=1, source_target_pairs={{0,1},{1,3},{3,2},{2,0},{4,5},{5,7},{7,6},{6,4},{8,9},{9,11},{11,1... | collective-permute-start | bytes 884744 | tf_op jit(solution)/shard_map/ppermute | solution.py:46
  42.2 1.6 %collective-permute-start.12 = (bf16[2,96,768]{2,1,0:T(8,128)(2,1)}, bf16[2,96,768]{2,1,0:T(8,128)(2,1)}, u32[]{:S(2)}, u32[]{:S(2)}) collective-permute-start(bf16[2,96,768]{2,1,0:T(8,128)(2,1)} %collective-permute-done.7.refs_2_.refs_1_), channel_id=1, source_target_pairs={{0,1},{1,3},{3,2},{2,0},{4,5},{5,7},{7,6},{6,4},{8,9},{9,11},{11,1... | collective-permute-start | bytes 884744 | tf_op jit(solution)/shard_map/ppermute | solution.py:46
  43.9 0.9 copy-done.7
  44.8 0.1 copy.26.times.refs_1_
  44.9 1.0 copy-done.4
  45.9 0.9 copy-done.6
  46.8 0.1 copy-done.10
  47.0 1.2 %place2.1.refs_11_ = bf16[1536,768]{1,0:T(8,128)(2,1)S(1)} custom-call(bf16[2,96,768]{2,1,0:T(8,128)(2,1)} %collective-permute-done.5.refs_1_.refs_0_, bf16[2,96,768]{2,1,0:T(8,128)(2,1)} %collective-permute-done.7.refs_2_.refs_1_, bf16[1536,768]{1,0:T(8,128)(2,1)S(1)} %place1.1.refs_2_), custom_call_target="tpu_custom_call", output_to_operand_aliasing={{}: (2, {})} | custom-call | tf_op jit(solution)/shard_map/place2/pallas_call | solution.py:460
  48.3 0.2 copy-done.8
  48.6 4.4 %norm.1 = (bf16[512,1536]{1,0:T(8,128)(2,1)S(1)}, bf16[512,1536]{1,0:T(8,128)(2,1)S(1)}, f32[512,128]{1,0:T(8,128)S(1)}, f32[512,128]{1,0:T(8,128)S(1)}, f32[512...) custom-call(s32[4,1]{1,0:T(4,128)S(1)} %copy.26.times.refs_1_, ...), custom_call_target="tpu_custom_call" | custom-call | tf_op jit(solution)/shard_map/norm/pallas_call | solution.py:460
  53.0 4.2 %collective-permute-done.12.refs_10_ = bf16[2,96,768]{2,1,0:T(8,128)(2,1)} collective-permute-done((bf16[2,96,768]{2,1,0:T(8,128)(2,1)}, bf16[2,96,768]{2,1,0:T(8,128)(2,1)}, u32[]{:S(2)}, u32[]{:S(2)}) %collective-permute-start.12) | collective-permute-done | bytes 294944 | tf_op jit(solution)/shard_map/ppermute | solution.py:46
  57.2 4.3 %step0.1 = (bf16[2,128,384]{2,1,0:T(8,128)(2,1)S(1)}, bf16[2,128,384]{2,1,0:T(8,128)(2,1)S(1)}, bf16[1536,768]{1,0:T(8,128)(2,1)S(1)}) custom-call(f32[1,16]{1,0:T(1,128)S(1)} %copy-done.17, s32[4,1]{1,0:T(4,128)S(1)} %copy.26.times.refs_1_, f32[1,1536]{1,0:T(1,128)S(1)} %copy-done.12, f32[1,1536]{1,0:T(1,128)S(1)} %copy-done.13, ...), custom_call_target="tpu_custom_call", output_to_operand_aliasing={{2}: (11, {})} | custom-call | flops 1610612736 | bytes 3145728 | tf_op jit(solution)/shard_map/step0/pallas_call | solution.py:460
  61.5 0.1 collective-permute-start.14
  61.6 1.6 %collective-permute-start.15 = (bf16[2,128,384]{2,1,0:T(8,128)(2,1)S(1)}, bf16[2,128,384]{2,1,0:T(8,128)(2,1)S(1)}, u32[]{:S(2)}, u32[]{:S(2)}) collective-permute-start(bf16[2,128,384]{2,1,0:T(8,128)(2,1)S(1)} %get-tuple-element.50.refs_1_.refs_0_), channel_id=1, source_target_pairs={{0,16},{16,0},{1,17},{17,1},{2,18},{18,2},{3,19},{19,3},{4,20},{20... | collective-permute-start | bytes 589832 | tf_op jit(solution)/shard_map/ppermute | solution.py:31
  63.2 0.5 collective-permute-start.19
  63.7 3.7 %step1.1 = (bf16[2,128,384]{2,1,0:T(8,128)(2,1)S(1)}, bf16[2,128,384]{2,1,0:T(8,128)(2,1)S(1)}) custom-call(f32[1,16]{1,0:T(1,128)S(1)} %copy-done.17, s32[4,1]{1,0:T(4,128)S(1)} %copy.26.times.refs_1_, f32[1,1536]{1,0:T(1,128)S(1)} %copy-done.12, f32[1,1536]{1,0:T(1,128)S(1)} %copy-done.13, f32[1,1536]{1,0:T(1,128)S(1)} %copy-done.16, ...), custom_call_target="tpu_custom_call" | custom-call | flops 1610612736 | bytes 3145728 | tf_op jit(solution)/shard_map/step1/pallas_call | solution.py:460
  67.4 1.6 %collective-permute-start.23 = (bf16[2,128,384]{2,1,0:T(8,128)(2,1)S(1)}, bf16[2,128,384]{2,1,0:T(8,128)(2,1)S(1)}, u32[]{:S(2)}, u32[]{:S(2)}) collective-permute-start(bf16[2,128,384]{2,1,0:T(8,128)(2,1)S(1)} %get-tuple-element.60.refs_2_), channel_id=1, source_target_pairs={{0,16},{16,0},{1,17},{17,1},{2,18},{18,2},{3,19},{19,3},{4,20},{20... | collective-permute-start | bytes 589832 | tf_op jit(solution)/shard_map/ppermute | solution.py:31
  69.0 0.5 collective-permute-start.25
  69.5 1.5 %collective-permute-start.16 = (bf16[2,128,384]{2,1,0:T(8,128)(2,1)S(1)}, bf16[2,128,384]{2,1,0:T(8,128)(2,1)S(1)}, u32[]{:S(2)}, u32[]{:S(2)}) collective-permute-start(bf16[2,128,384]{2,1,0:T(8,128)(2,1)S(1)} %collective-permute-done.15.refs_11_), channel_id=1, source_target_pairs={{0,8},{4,12},{8,0},{12,4},{1,9},{5,13},{9,1},{13,5},{2,10},{6,14},... | collective-permute-start | bytes 589832 | tf_op jit(solution)/shard_map/ppermute | solution.py:27
  71.0 2.6 %collective-permute-done.19.refs_15_ = bf16[2,128,384]{2,1,0:T(8,128)(2,1)S(1)} collective-permute-done((bf16[2,128,384]{2,1,0:T(8,128)(2,1)S(1)}, bf16[2,128,384]{2,1,0:T(8,128)(2,1)S(1)}, u32[]{:S(2)}, u32[]{:S(2)}) %collective-permute-start.19) | collective-permute-done | bytes 196640 | tf_op jit(solution)/shard_map/ppermute | solution.py:31
  73.6 1.5 %collective-permute-start.20 = (bf16[2,128,384]{2,1,0:T(8,128)(2,1)S(1)}, bf16[2,128,384]{2,1,0:T(8,128)(2,1)S(1)}, u32[]{:S(2)}, u32[]{:S(2)}) collective-permute-start(bf16[2,128,384]{2,1,0:T(8,128)(2,1)S(1)} %collective-permute-done.19.refs_15_), channel_id=1, source_target_pairs={{0,8},{4,12},{8,0},{12,4},{1,9},{5,13},{9,1},{13,5},{2,10},{6,14},... | collective-permute-start | bytes 589832 | tf_op jit(solution)/shard_map/ppermute | solution.py:27
  75.1 2.7 %collective-permute-done.23.refs_0_ = bf16[2,128,384]{2,1,0:T(8,128)(2,1)S(1)} collective-permute-done((bf16[2,128,384]{2,1,0:T(8,128)(2,1)S(1)}, bf16[2,128,384]{2,1,0:T(8,128)(2,1)S(1)}, u32[]{:S(2)}, u32[]{:S(2)}) %collective-permute-start.23) | collective-permute-done | bytes 196640 | tf_op jit(solution)/shard_map/ppermute | solution.py:31
  77.8 3.8 %collective-permute-done.25.refs_2_ = bf16[2,128,384]{2,1,0:T(8,128)(2,1)S(1)} collective-permute-done((bf16[2,128,384]{2,1,0:T(8,128)(2,1)S(1)}, bf16[2,128,384]{2,1,0:T(8,128)(2,1)S(1)}, u32[]{:S(2)}, u32[]{:S(2)}) %collective-permute-start.25) | collective-permute-done | bytes 196640 | tf_op jit(solution)/shard_map/ppermute | solution.py:31
  81.6 0.5 collective-permute-start.18
  82.1 1.5 %collective-permute-start.24 = (bf16[2,128,384]{2,1,0:T(8,128)(2,1)S(1)}, bf16[2,128,384]{2,1,0:T(8,128)(2,1)S(1)}, u32[]{:S(2)}, u32[]{:S(2)}) collective-permute-start(bf16[2,128,384]{2,1,0:T(8,128)(2,1)S(1)} %collective-permute-done.23.refs_0_), channel_id=1, source_target_pairs={{0,8},{4,12},{8,0},{12,4},{1,9},{5,13},{9,1},{13,5},{2,10},{6,14},... | collective-permute-start | bytes 589832 | tf_op jit(solution)/shard_map/ppermute | solution.py:27
  83.6 0.8 collective-permute-start.26
  84.5 4.7 %step2.1 = (bf16[2,128,384]{2,1,0:T(8,128)(2,1)S(1)}, bf16[2,128,384]{2,1,0:T(8,128)(2,1)S(1)}) custom-call(f32[1,16]{1,0:T(1,128)S(1)} %copy-done.17, s32[4,1]{1,0:T(4,128)S(1)} %copy.26.times.refs_1_, f32[1,1536]{1,0:T(1,128)S(1)} %copy-done.12, f32[1,1536]{1,0:T(1,128)S(1)} %copy-done.13, f32[1,1536]{1,0:T(1,128)S(1)} %copy-done.16, ...), custom_call_target="tpu_custom_call" | custom-call | flops 1610612736 | bytes 3145728 | tf_op jit(solution)/shard_map/step2/pallas_call | solution.py:460
  89.2 0.5 early.1
  89.7 0.1 collective-permute-done.24.refs_1_
  89.8 3.8 %collective-permute-done.26.refs_3_ = bf16[2,128,384]{2,1,0:T(8,128)(2,1)S(1)} collective-permute-done((bf16[2,128,384]{2,1,0:T(8,128)(2,1)S(1)}, bf16[2,128,384]{2,1,0:T(8,128)(2,1)S(1)}, u32[]{:S(2)}, u32[]{:S(2)}) %collective-permute-start.26) | collective-permute-done | bytes 196640 | tf_op jit(solution)/shard_map/ppermute | solution.py:27
  93.6 0.5 collective-permute-start.28
  94.1 0.5 collective-permute-start.30
  94.6 0.4 collective-permute-done.27.refs_13_
  95.0 1.5 %collective-permute-start.32 = (bf16[2,128,384]{2,1,0:T(8,128)(2,1)S(1)}, bf16[2,128,384]{2,1,0:T(8,128)(2,1)S(1)}, u32[]{:S(2)}, u32[]{:S(2)}) collective-permute-start(bf16[2,128,384]{2,1,0:T(8,128)(2,1)S(1)} %get-tuple-element.71), channel_id=1, source_target_pairs={{0,8},{4,12},{8,0},{12,4},{1,9},{5,13},{9,1},{13,5},{2,10},{6,14},... | collective-permute-start | bytes 589832 | tf_op jit(solution)/shard_map/ppermute | solution.py:27
  96.5 0.1 collective-permute-start.33
  96.7 4.5 %step3.1 = (bf16[2,128,384]{2,1,0:T(8,128)(2,1)S(1)}, bf16[2,128,384]{2,1,0:T(8,128)(2,1)S(1)}) custom-call(f32[1,16]{1,0:T(1,128)S(1)} %copy-done.17, s32[4,1]{1,0:T(4,128)S(1)} %copy.26.times.refs_1_, f32[1,1536]{1,0:T(1,128)S(1)} %copy-done.12, f32[1,1536]{1,0:T(1,128)S(1)} %copy-done.13, f32[1,1536]{1,0:T(1,128)S(1)} %copy-done.16, ...), custom_call_target="tpu_custom_call" | custom-call | flops 1610612736 | bytes 3145728 | tf_op jit(solution)/shard_map/step3/pallas_call | solution.py:460
  101.2 1.6 %collective-permute-done.32.refs_10_ = bf16[2,128,384]{2,1,0:T(8,128)(2,1)S(1)} collective-permute-done((bf16[2,128,384]{2,1,0:T(8,128)(2,1)S(1)}, bf16[2,128,384]{2,1,0:T(8,128)(2,1)S(1)}, u32[]{:S(2)}, u32[]{:S(2)}) %collective-permute-start.32) | collective-permute-done | bytes 196640 | tf_op jit(solution)/shard_map/ppermute | solution.py:27
  102.8 1.2 %settle.1 = (bf16[128,384]{1,0:T(8,128)(2,1)S(1)}, bf16[128,384]{1,0:T(8,128)(2,1)S(1)}, bf16[128,384]{1,0:T(8,128)(2,1)S(1)}, bf16[128,384]{1,0:T(8,128)(2,1)S(...) custom-call(bf16[2,128,384]{2,1,0:T(8,128)(2,1)S(1)} %get-tuple-elem, ...), custom_call_target="tpu_custom_call" | custom-call | tf_op jit(solution)/shard_map/settle/pallas_call | solution.py:460
  104.0 0.8 collective-permute-start.37
  104.9 1.5 %collective-permute-start.35 = (bf16[128,384]{1,0:T(8,128)(2,1)S(1)}, bf16[128,384]{1,0:T(8,128)(2,1)S(1)}, u32[]{:S(2)}, u32[]{:S(2)}) collective-permute-start(bf16[128,384]{1,0:T(8,128)(2,1)S(1)} %get-tuple-element.76), channel_id=1, source_target_pairs={{0,8},{4,12},{8,0},{12,4},{1,9},{5,13},{9,1},{13,5},{2,10},{6,14},... | collective-permute-start | bytes 294920 | tf_op jit(solution)/shard_map/ppermute | solution.py:27
  106.4 0.4 collective-permute-start.36
  106.7 2.5 %collective-permute-start.38 = (bf16[96,256]{1,0:T(8,128)(2,1)S(1)}, bf16[96,256]{1,0:T(8,128)(2,1)S(1)}, u32[]{:S(2)}, u32[]{:S(2)}) collective-permute-start(bf16[96,256]{1,0:T(8,128)(2,1)S(1)} %get-tuple-element.80), channel_id=1, source_target_pairs={{0,2},{1,3},{2,0},{3,1},{4,6},{5,7},{6,4},{7,5},{8,10},{9,11},{10,... | collective-permute-start | bytes 147464 | tf_op jit(solution)/shard_map/ppermute | solution.py:36
  109.3 0.7 collective-permute-done.37.refs_7_
  110.0 1.0 collective-permute-start.39
  110.9 1.9 %collective-permute-done.38.refs_8_ = bf16[96,256]{1,0:T(8,128)(2,1)S(1)} collective-permute-done((bf16[96,256]{1,0:T(8,128)(2,1)S(1)}, bf16[96,256]{1,0:T(8,128)(2,1)S(1)}, u32[]{:S(2)}, u32[]{:S(2)}) %collective-permute-start.38) | collective-permute-done | bytes 49184 | tf_op jit(solution)/shard_map/ppermute | solution.py:36
  112.9 1.2 %collective-permute-done.39.refs_9_ = bf16[96,256]{1,0:T(8,128)(2,1)S(1)} collective-permute-done((bf16[96,256]{1,0:T(8,128)(2,1)S(1)}, bf16[96,256]{1,0:T(8,128)(2,1)S(1)}, u32[]{:S(2)}, u32[]{:S(2)}) %collective-permute-start.39) | collective-permute-done | bytes 49184 | tf_op jit(solution)/shard_map/ppermute | solution.py:36
  114.1 1.5 %finish.1 = (bf16[3,128,1536]{2,1,0:T(8,128)(2,1)}, f32[96,256]{1,0:T(8,128)}) custom-call(bf16[3,128,1536]{2,1,0:T(8,128)(2,1)} %get-tuple-element.72.refs_0_, bf16[2,128,384]{2,1,0:T(8,128)(2,1)S(1)} %collective-permute-done.33.refs_1_, bf16[128,384]{1,0:T(8,128)(2,1)S(1)} %get-tuple-element.74.refs_2_, ...), custom_call_target="tpu_custom_call", output_to_operand_aliasing={{0}: (0, {})} | custom-call | tf_op jit(solution)/shard_map/finish/pallas_call | solution.py:460
  (76 shorter events, 0.5 us)
Async XLA Ops:
  0.6 14.4 %copy-start = (bf16[1,3,1,128,1536]{4,3,2,1,0:T(8,128)(2,1)S(1)}, bf16[1,3,1,128,1536]{4,3,2,1,0:T(8,128)(2,1)}, u32[]{:S(2)}) copy-start(bf16[1,3,1,128,1536]{4,3,2,1,0:T(8,128)(2,1)} %incoming.3) | copy-start | bytes 3538948
  0.6 14.4 %copy-start.18 = (s32[4,1,128]{2,1,0:T(1,128)S(1)}, s32[4,1,128]{2,1,0:T(1,128)}, u32[]{:S(2)}) copy-start(s32[4,1,128]{2,1,0:T(1,128)} %contacts.1) | copy-start | bytes 6148
  2.0 1.5 %collective-permute-start = (bf16[96,768]{1,0:T(8,128)(2,1)S(1)}, bf16[96,768]{1,0:T(8,128)(2,1)S(1)}, u32[]{:S(2)}, u32[]{:S(2)}) collective-permute-start(bf16[96,768]{1,0:T(8,128)(2,1)S(1)} %get-tuple-element.44), channel_id=1, source_target_pairs={{0,4},{4,0},{8,12},{12,8},{1,5},{5,1},{9,13},{13,9},{2,6},{6,2},{1... | collective-permute-start | bytes 442376 | tf_op jit(solution)/shard_map/ppermute | solution.py:27
  3.5 11.5 %collective-permute-start.1 = (bf16[2,96,768]{2,1,0:T(8,128)(2,1)S(1)}, bf16[2,96,768]{2,1,0:T(8,128)(2,1)S(1)}, u32[]{:S(2)}, u32[]{:S(2)}) collective-permute-start(bf16[2,96,768]{2,1,0:T(8,128)(2,1)S(1)} %near.1.refs_0_), channel_id=1, source_target_pairs={{0,1},{1,3},{3,2},{2,0},{4,5},{5,7},{7,6},{6,4},{8,9},{9,11},{11,1... | collective-permute-start | bytes 884744 | tf_op jit(solution)/shard_map/ppermute | solution.py:46
  6.5 0.7 copy-start.3
  7.2 6.7 %collective-permute-start.2 = (bf16[96,768]{1,0:T(8,128)(2,1)S(1)}, bf16[96,768]{1,0:T(8,128)(2,1)S(1)}, u32[]{:S(2)}, u32[]{:S(2)}) collective-permute-start(bf16[96,768]{1,0:T(8,128)(2,1)S(1)} %get-tuple-element.45), channel_id=1, source_target_pairs={{0,8},{4,12},{8,0},{12,4},{1,9},{5,13},{9,1},{13,5},{2,10},{6,14},... | collective-permute-start | bytes 442376 | tf_op jit(solution)/shard_map/ppermute | solution.py:27
  8.7 6.3 %collective-permute-start.3 = (bf16[96,768]{1,0:T(8,128)(2,1)S(1)}, bf16[96,768]{1,0:T(8,128)(2,1)S(1)}, u32[]{:S(2)}, u32[]{:S(2)}) collective-permute-start(bf16[96,768]{1,0:T(8,128)(2,1)S(1)} %get-tuple-element.46), channel_id=1, source_target_pairs={{0,12},{4,8},{8,4},{12,0},{1,13},{5,9},{9,5},{13,1},{2,14},{6,10},... | collective-permute-start | bytes 442376 | tf_op jit(solution)/shard_map/ppermute | solution.py:27
  15.0 4.2 %copy-start.5 = (bf16[2,96,768]{2,1,0:T(8,128)(2,1)}, bf16[2,96,768]{2,1,0:T(8,128)(2,1)S(1)}, u32[]{:S(2)}) copy-start(bf16[2,96,768]{2,1,0:T(8,128)(2,1)S(1)} %collective-permute-done.1.refs_0_) | copy-start | bytes 884740
  15.1 24.8 %copy-start.1 = (bf16[272,1536]{1,0:T(8,128)(2,1)}, bf16[272,1536]{1,0:T(8,128)(2,1)S(1)}, u32[]{:S(2)}) copy-start(bf16[272,1536]{1,0:T(8,128)(2,1)S(1)} %first.1.refs_0_) | copy-start | bytes 2506756
  15.1 24.8 %copy-start.11 = (bf16[1,3,1,128,256]{4,3,2,1,0:T(8,128)(2,1)S(1)}, bf16[1,3,1,128,256]{4,3,2,1,0:T(8,128)(2,1)}, u32[]{:S(2)}) copy-start(bf16[1,3,1,128,256]{4,3,2,1,0:T(8,128)(2,1)} %cotangent.1) | copy-start | bytes 589828
  15.1 24.6 %collective-permute-start.4 = (bf16[272,1536]{1,0:T(8,128)(2,1)S(1)}, bf16[272,1536]{1,0:T(8,128)(2,1)S(1)}, u32[]{:S(2)}, u32[]{:S(2)}) collective-permute-start(bf16[272,1536]{1,0:T(8,128)(2,1)S(1)} %first.1.refs_0_), channel_id=1, source_target_pairs={{0,8},{4,12},{8,0},{12,4},{1,9},{5,13},{9,1},{13,5},{2,10},{6,14},... | collective-permute-start | bytes 2506760 | tf_op jit(solution)/shard_map/ppermute | solution.py:27
  16.6 10.8 %collective-permute-start.6 = (bf16[2,96,768]{2,1,0:T(8,128)(2,1)S(1)}, bf16[2,96,768]{2,1,0:T(8,128)(2,1)S(1)}, u32[]{:S(2)}, u32[]{:S(2)}) collective-permute-start(bf16[2,96,768]{2,1,0:T(8,128)(2,1)S(1)} %far.1.refs_1_), channel_id=1, source_target_pairs={{0,1},{1,3},{3,2},{2,0},{4,5},{5,7},{7,6},{6,4},{8,9},{9,11},{11,1... | collective-permute-start | bytes 884744 | tf_op jit(solution)/shard_map/ppermute | solution.py:46
  19.2 14.6 %collective-permute-start.5 = (bf16[2,96,768]{2,1,0:T(8,128)(2,1)S(1)}, bf16[2,96,768]{2,1,0:T(8,128)(2,1)}, u32[]{:S(2)}, u32[]{:S(2)}) collective-permute-start(bf16[2,96,768]{2,1,0:T(8,128)(2,1)S(1)} %collective-permute-done.1.refs_0_), channel_id=1, source_target_pairs={{0,1},{1,3},{3,2},{2,0},{4,5},{5,7},{7,6},{6,4},{8,9},{9,11},{11,1... | collective-permute-start | bytes 884744 | tf_op jit(solution)/shard_map/ppermute | solution.py:46
  27.4 12.4 %copy-start.9 = (bf16[2,96,768]{2,1,0:T(8,128)(2,1)}, bf16[2,96,768]{2,1,0:T(8,128)(2,1)S(1)}, u32[]{:S(2)}) copy-start(bf16[2,96,768]{2,1,0:T(8,128)(2,1)S(1)} %collective-permute-done.6.refs_1_) | copy-start | bytes 884740
  27.4 12.4 %collective-permute-start.7 = (bf16[2,96,768]{2,1,0:T(8,128)(2,1)S(1)}, bf16[2,96,768]{2,1,0:T(8,128)(2,1)}, u32[]{:S(2)}, u32[]{:S(2)}) collective-permute-start(bf16[2,96,768]{2,1,0:T(8,128)(2,1)S(1)} %collective-permute-done.6.refs_1_), channel_id=1, source_target_pairs={{0,1},{1,3},{3,2},{2,0},{4,5},{5,7},{7,6},{6,4},{8,9},{9,11},{11,1... | collective-permute-start | bytes 884744 | tf_op jit(solution)/shard_map/ppermute | solution.py:46
  29.1 14.8 %collective-permute-start.9 = (bf16[272,1536]{1,0:T(8,128)(2,1)S(1)}, bf16[272,1536]{1,0:T(8,128)(2,1)S(1)}, u32[]{:S(2)}, u32[]{:S(2)}) collective-permute-start(bf16[272,1536]{1,0:T(8,128)(2,1)S(1)} %first.1.refs_0_), channel_id=1, source_target_pairs={{0,4},{4,0},{8,12},{12,8},{1,5},{5,1},{9,13},{13,9},{2,6},{6,2},{1... | collective-permute-start | bytes 2506760 | tf_op jit(solution)/shard_map/ppermute | solution.py:27
  39.8 5.0 %copy-start.19 = (s32[4,1]{0,1:T(1,128)S(1)}, s32[4,1]{0,1:T(1,128)}, u32[]{:S(2)}) copy-start(s32[4,1]{0,1:T(1,128)} %param.15) | copy-start | bytes 52
  39.8 8.5 %collective-permute-start.10 = (bf16[272,1536]{1,0:T(8,128)(2,1)S(1)}, bf16[272,1536]{1,0:T(8,128)(2,1)}, u32[]{:S(2)}, u32[]{:S(2)}) collective-permute-start(bf16[272,1536]{1,0:T(8,128)(2,1)S(1)} %tie.3.dep.refs_1_), channel_id=1, source_target_pairs={{0,4},{4,0},{8,12},{12,8},{1,5},{5,1},{9,13},{13,9},{2,6},{6,2},{1... | collective-permute-start | bytes 2506760 | tf_op jit(solution)/shard_map/ppermute | solution.py:27
  40.0 21.5 %collective-permute-start.8 = (bf16[256,1536]{1,0:T(8,128)(2,1)S(1)}, bf16[256,1536]{1,0:T(8,128)(2,1)S(1)}, u32[]{:S(2)}, u32[]{:S(2)}) collective-permute-start(bf16[256,1536]{1,0:T(8,128)(2,1)S(1)} %second.1.refs_6_.refs_4_), channel_id=1, source_target_pairs={{0,8},{4,12},{8,0},{12,4},{1,9},{5,13},{9,1},{13,5},{2,10},{6,14},... | collective-permute-start | bytes 2359304 | tf_op jit(solution)/shard_map/ppermute | solution.py:27
  40.6 12.4 %collective-permute-start.11 = (bf16[2,96,768]{2,1,0:T(8,128)(2,1)}, bf16[2,96,768]{2,1,0:T(8,128)(2,1)}, u32[]{:S(2)}, u32[]{:S(2)}) collective-permute-start(bf16[2,96,768]{2,1,0:T(8,128)(2,1)} %collective-permute-done.5.refs_1_.refs_0_), channel_id=1, source_target_pairs={{0,1},{1,3},{3,2},{2,0},{4,5},{5,7},{7,6},{6,4},{8,9},{9,11},{11,1... | collective-permute-start | bytes 884744 | tf_op jit(solution)/shard_map/ppermute | solution.py:46
  42.2 15.0 %collective-permute-start.12 = (bf16[2,96,768]{2,1,0:T(8,128)(2,1)}, bf16[2,96,768]{2,1,0:T(8,128)(2,1)}, u32[]{:S(2)}, u32[]{:S(2)}) collective-permute-start(bf16[2,96,768]{2,1,0:T(8,128)(2,1)} %collective-permute-done.7.refs_2_.refs_1_), channel_id=1, source_target_pairs={{0,1},{1,3},{3,2},{2,0},{4,5},{5,7},{7,6},{6,4},{8,9},{9,11},{11,1... | collective-permute-start | bytes 884744 | tf_op jit(solution)/shard_map/ppermute | solution.py:46
  43.9 0.9 copy-start.7
  44.8 24.2 %collective-permute-start.13 = (bf16[256,1536]{1,0:T(8,128)(2,1)S(1)}, bf16[256,1536]{1,0:T(8,128)(2,1)S(1)}, u32[]{:S(2)}, u32[]{:S(2)}) collective-permute-start(bf16[256,1536]{1,0:T(8,128)(2,1)S(1)} %second.1.refs_6_.refs_4_), channel_id=1, source_target_pairs={{0,4},{4,0},{8,12},{12,8},{1,5},{5,1},{9,13},{13,9},{2,6},{6,2},{1... | collective-permute-start | bytes 2359304 | tf_op jit(solution)/shard_map/ppermute | solution.py:27
  44.9 1.0 copy-start.4
  45.9 1.0 copy-start.6
  45.9 1.0 copy-start.10
  47.0 1.3 %copy-start.2 = (bf16[272,1536]{1,0:T(8,128)(2,1)S(1)}, bf16[272,1536]{1,0:T(8,128)(2,1)}, u32[]{:S(2)}) copy-start(bf16[272,1536]{1,0:T(8,128)(2,1)} %copy-done.1) | copy-start | bytes 2506756
  47.0 1.6 %copy-start.8 = (bf16[272,1536]{1,0:T(8,128)(2,1)S(1)}, bf16[272,1536]{1,0:T(8,128)(2,1)}, u32[]{:S(2)}) copy-start(bf16[272,1536]{1,0:T(8,128)(2,1)} %copy-done.7) | copy-start | bytes 2506756
  47.0 1.6 %copy-start.12 = (f32[1,1536]{1,0:T(1,128)S(1)}, f32[1,1536]{1,0:T(1,128)}, u32[]{:S(2)}) copy-start(f32[1,1536]{1,0:T(1,128)} %refs_2_.7) | copy-start | bytes 18436
  47.0 1.6 %copy-start.13 = (f32[1,1536]{1,0:T(1,128)S(1)}, f32[1,1536]{1,0:T(1,128)}, u32[]{:S(2)}) copy-start(f32[1,1536]{1,0:T(1,128)} %refs_3_.7) | copy-start | bytes 18436
  47.0 1.5 %copy-start.14 = (bf16[1,16,1536]{2,1,0:T(8,128)(2,1)S(1)}, bf16[1,16,1536]{2,1,0:T(8,128)(2,1)}, u32[]{:S(2)}) copy-start(bf16[1,16,1536]{2,1,0:T(8,128)(2,1)} %table.1) | copy-start | bytes 147460
  48.3 8.9 %copy-start.15 = (s32[4,1,512]{2,1,0:T(1,128)S(1)}, s32[4,1,512]{2,1,0:T(1,128)}, u32[]{:S(2)}) copy-start(s32[4,1,512]{2,1,0:T(1,128)} %refs_5_.7) | copy-start | bytes 24580
  48.3 8.9 %copy-start.16 = (f32[1,1536]{1,0:T(1,128)S(1)}, f32[1,1536]{1,0:T(1,128)}, u32[]{:S(2)}) copy-start(f32[1,1536]{1,0:T(1,128)} %refs_4_.7) | copy-start | bytes 18436
  48.3 8.9 %copy-start.17 = (f32[1,16]{1,0:T(1,128)S(1)}, f32[1,16]{1,0:T(1,128)}, u32[]{:S(2)}) copy-start(f32[1,16]{1,0:T(1,128)} %refs_0_.7) | copy-start | bytes 196
  61.5 23.0 %collective-permute-start.14 = (bf16[256,1536]{1,0:T(8,128)(2,1)S(1)}, bf16[256,1536]{1,0:T(8,128)(2,1)S(1)}, u32[]{:S(2)}, u32[]{:S(2)}) collective-permute-start(bf16[256,1536]{1,0:T(8,128)(2,1)S(1)} %tie.4.refs_7_.refs_5_), channel_id=1, source_target_pairs={{0,4},{4,0},{8,12},{12,8},{1,5},{5,1},{9,13},{13,9},{2,6},{6,2},{1... | collective-permute-start | bytes 2359304 | tf_op jit(solution)/shard_map/ppermute | solution.py:27
  61.6 7.9 %collective-permute-start.15 = (bf16[2,128,384]{2,1,0:T(8,128)(2,1)S(1)}, bf16[2,128,384]{2,1,0:T(8,128)(2,1)S(1)}, u32[]{:S(2)}, u32[]{:S(2)}) collective-permute-start(bf16[2,128,384]{2,1,0:T(8,128)(2,1)S(1)} %get-tuple-element.50.refs_1_.refs_0_), channel_id=1, source_target_pairs={{0,16},{16,0},{1,17},{17,1},{2,18},{18,2},{3,19},{19,3},{4,20},{20... | collective-permute-start | bytes 589832 | tf_op jit(solution)/shard_map/ppermute | solution.py:31
  63.2 10.4 %collective-permute-start.19 = (bf16[2,128,384]{2,1,0:T(8,128)(2,1)S(1)}, bf16[2,128,384]{2,1,0:T(8,128)(2,1)S(1)}, u32[]{:S(2)}, u32[]{:S(2)}) collective-permute-start(bf16[2,128,384]{2,1,0:T(8,128)(2,1)S(1)} %get-tuple-element.52.refs_1_), channel_id=1, source_target_pairs={{0,16},{16,0},{1,17},{17,1},{2,18},{18,2},{3,19},{19,3},{4,20},{20... | collective-permute-start | bytes 589832 | tf_op jit(solution)/shard_map/ppermute | solution.py:31
  67.4 10.4 %collective-permute-start.23 = (bf16[2,128,384]{2,1,0:T(8,128)(2,1)S(1)}, bf16[2,128,384]{2,1,0:T(8,128)(2,1)S(1)}, u32[]{:S(2)}, u32[]{:S(2)}) collective-permute-start(bf16[2,128,384]{2,1,0:T(8,128)(2,1)S(1)} %get-tuple-element.60.refs_2_), channel_id=1, source_target_pairs={{0,16},{16,0},{1,17},{17,1},{2,18},{18,2},{3,19},{19,3},{4,20},{20... | collective-permute-start | bytes 589832 | tf_op jit(solution)/shard_map/ppermute | solution.py:31
  69.0 12.5 %collective-permute-start.25 = (bf16[2,128,384]{2,1,0:T(8,128)(2,1)S(1)}, bf16[2,128,384]{2,1,0:T(8,128)(2,1)S(1)}, u32[]{:S(2)}, u32[]{:S(2)}) collective-permute-start(bf16[2,128,384]{2,1,0:T(8,128)(2,1)S(1)} %get-tuple-element.61.refs_3_), channel_id=1, source_target_pairs={{0,16},{16,0},{1,17},{17,1},{2,18},{18,2},{3,19},{19,3},{4,20},{20... | collective-permute-start | bytes 589832 | tf_op jit(solution)/shard_map/ppermute | solution.py:31
  69.5 12.0 %collective-permute-start.16 = (bf16[2,128,384]{2,1,0:T(8,128)(2,1)S(1)}, bf16[2,128,384]{2,1,0:T(8,128)(2,1)S(1)}, u32[]{:S(2)}, u32[]{:S(2)}) collective-permute-start(bf16[2,128,384]{2,1,0:T(8,128)(2,1)S(1)} %collective-permute-done.15.refs_11_), channel_id=1, source_target_pairs={{0,8},{4,12},{8,0},{12,4},{1,9},{5,13},{9,1},{13,5},{2,10},{6,14},... | collective-permute-start | bytes 589832 | tf_op jit(solution)/shard_map/ppermute | solution.py:27
  73.6 8.5 %collective-permute-start.20 = (bf16[2,128,384]{2,1,0:T(8,128)(2,1)S(1)}, bf16[2,128,384]{2,1,0:T(8,128)(2,1)S(1)}, u32[]{:S(2)}, u32[]{:S(2)}) collective-permute-start(bf16[2,128,384]{2,1,0:T(8,128)(2,1)S(1)} %collective-permute-done.19.refs_15_), channel_id=1, source_target_pairs={{0,8},{4,12},{8,0},{12,4},{1,9},{5,13},{9,1},{13,5},{2,10},{6,14},... | collective-permute-start | bytes 589832 | tf_op jit(solution)/shard_map/ppermute | solution.py:27
  77.8 4.4 %collective-permute-start.17 = (bf16[2,128,384]{2,1,0:T(8,128)(2,1)S(1)}, bf16[2,128,384]{2,1,0:T(8,128)(2,1)S(1)}, u32[]{:S(2)}, u32[]{:S(2)}) collective-permute-start(bf16[2,128,384]{2,1,0:T(8,128)(2,1)S(1)} %collective-permute-done.15.refs_11_), channel_id=1, source_target_pairs={{0,4},{4,0},{8,12},{12,8},{1,5},{5,1},{9,13},{13,9},{2,6},{6,2},{1... | collective-permute-start | bytes 589832 | tf_op jit(solution)/shard_map/ppermute | solution.py:27
  81.5 2.1 %collective-permute-start.21 = (bf16[2,128,384]{2,1,0:T(8,128)(2,1)S(1)}, bf16[2,128,384]{2,1,0:T(8,128)(2,1)S(1)}, u32[]{:S(2)}, u32[]{:S(2)}) collective-permute-start(bf16[2,128,384]{2,1,0:T(8,128)(2,1)S(1)} %collective-permute-done.19.refs_15_), channel_id=1, source_target_pairs={{0,4},{4,0},{8,12},{12,8},{1,5},{5,1},{9,13},{13,9},{2,6},{6,2},{1... | collective-permute-start | bytes 589832 | tf_op jit(solution)/shard_map/ppermute | solution.py:27
  81.6 2.9 %collective-permute-start.18 = (bf16[2,128,384]{2,1,0:T(8,128)(2,1)S(1)}, bf16[2,128,384]{2,1,0:T(8,128)(2,1)S(1)}, u32[]{:S(2)}, u32[]{:S(2)}) collective-permute-start(bf16[2,128,384]{2,1,0:T(8,128)(2,1)S(1)} %collective-permute-done.16.refs_12_), channel_id=1, source_target_pairs={{0,4},{4,0},{8,12},{12,8},{1,5},{5,1},{9,13},{13,9},{2,6},{6,2},{1... | collective-permute-start | bytes 589832 | tf_op jit(solution)/shard_map/ppermute | solution.py:27
  82.1 2.4 %collective-permute-start.22 = (bf16[2,128,384]{2,1,0:T(8,128)(2,1)S(1)}, bf16[2,128,384]{2,1,0:T(8,128)(2,1)S(1)}, u32[]{:S(2)}, u32[]{:S(2)}) collective-permute-start(bf16[2,128,384]{2,1,0:T(8,128)(2,1)S(1)} %collective-permute-done.20.refs_16_), channel_id=1, source_target_pairs={{0,4},{4,0},{8,12},{12,8},{1,5},{5,1},{9,13},{13,9},{2,6},{6,2},{1... | collective-permute-start | bytes 589832 | tf_op jit(solution)/shard_map/ppermute | solution.py:27
  82.1 7.7 %collective-permute-start.24 = (bf16[2,128,384]{2,1,0:T(8,128)(2,1)S(1)}, bf16[2,128,384]{2,1,0:T(8,128)(2,1)S(1)}, u32[]{:S(2)}, u32[]{:S(2)}) collective-permute-start(bf16[2,128,384]{2,1,0:T(8,128)(2,1)S(1)} %collective-permute-done.23.refs_0_), channel_id=1, source_target_pairs={{0,8},{4,12},{8,0},{12,4},{1,9},{5,13},{9,1},{13,5},{2,10},{6,14},... | collective-permute-start | bytes 589832 | tf_op jit(solution)/shard_map/ppermute | solution.py:27
  83.6 10.0 %collective-permute-start.26 = (bf16[2,128,384]{2,1,0:T(8,128)(2,1)S(1)}, bf16[2,128,384]{2,1,0:T(8,128)(2,1)S(1)}, u32[]{:S(2)}, u32[]{:S(2)}) collective-permute-start(bf16[2,128,384]{2,1,0:T(8,128)(2,1)S(1)} %collective-permute-done.25.refs_2_), channel_id=1, source_target_pairs={{0,8},{4,12},{8,0},{12,4},{1,9},{5,13},{9,1},{13,5},{2,10},{6,14},... | collective-permute-start | bytes 589832 | tf_op jit(solution)/shard_map/ppermute | solution.py:27
  93.6 1.4 %collective-permute-start.27 = (bf16[2,128,384]{2,1,0:T(8,128)(2,1)S(1)}, bf16[2,128,384]{2,1,0:T(8,128)(2,1)S(1)}, u32[]{:S(2)}, u32[]{:S(2)}) collective-permute-start(bf16[2,128,384]{2,1,0:T(8,128)(2,1)S(1)} %get-tuple-element.63.refs_11_), channel_id=1, source_target_pairs={{0,4},{4,0},{8,12},{12,8},{1,5},{5,1},{9,13},{13,9},{2,6},{6,2},{1... | collective-permute-start | bytes 589832 | tf_op jit(solution)/shard_map/ppermute | solution.py:27
  93.6 2.9 %collective-permute-start.28 = (bf16[2,128,384]{2,1,0:T(8,128)(2,1)S(1)}, bf16[2,128,384]{2,1,0:T(8,128)(2,1)S(1)}, u32[]{:S(2)}, u32[]{:S(2)}) collective-permute-start(bf16[2,128,384]{2,1,0:T(8,128)(2,1)S(1)} %get-tuple-element.64.refs_12_), channel_id=1, source_target_pairs={{0,4},{4,0},{8,12},{12,8},{1,5},{5,1},{9,13},{13,9},{2,6},{6,2},{1... | collective-permute-start | bytes 589832 | tf_op jit(solution)/shard_map/ppermute | solution.py:27
  94.1 2.5 %collective-permute-start.29 = (bf16[2,128,384]{2,1,0:T(8,128)(2,1)S(1)}, bf16[2,128,384]{2,1,0:T(8,128)(2,1)S(1)}, u32[]{:S(2)}, u32[]{:S(2)}) collective-permute-start(bf16[2,128,384]{2,1,0:T(8,128)(2,1)S(1)} %get-tuple-element.65.refs_15_), channel_id=1, source_target_pairs={{0,4},{4,0},{8,12},{12,8},{1,5},{5,1},{9,13},{13,9},{2,6},{6,2},{1... | collective-permute-start | bytes 589832 | tf_op jit(solution)/shard_map/ppermute | solution.py:27
  94.1 2.5 %collective-permute-start.30 = (bf16[2,128,384]{2,1,0:T(8,128)(2,1)S(1)}, bf16[2,128,384]{2,1,0:T(8,128)(2,1)S(1)}, u32[]{:S(2)}, u32[]{:S(2)}) collective-permute-start(bf16[2,128,384]{2,1,0:T(8,128)(2,1)S(1)} %get-tuple-element.66.refs_16_), channel_id=1, source_target_pairs={{0,4},{4,0},{8,12},{12,8},{1,5},{5,1},{9,13},{13,9},{2,6},{6,2},{1... | collective-permute-start | bytes 589832 | tf_op jit(solution)/shard_map/ppermute | solution.py:27
  94.6 6.6 %collective-permute-start.31 = (bf16[2,128,384]{2,1,0:T(8,128)(2,1)S(1)}, bf16[2,128,384]{2,1,0:T(8,128)(2,1)S(1)}, u32[]{:S(2)}, u32[]{:S(2)}) collective-permute-start(bf16[2,128,384]{2,1,0:T(8,128)(2,1)S(1)} %get-tuple-element.70), channel_id=1, source_target_pairs={{0,4},{4,0},{8,12},{12,8},{1,5},{5,1},{9,13},{13,9},{2,6},{6,2},{1... | collective-permute-start | bytes 589832 | tf_op jit(solution)/shard_map/ppermute | solution.py:27
  95.0 7.7 %collective-permute-start.32 = (bf16[2,128,384]{2,1,0:T(8,128)(2,1)S(1)}, bf16[2,128,384]{2,1,0:T(8,128)(2,1)S(1)}, u32[]{:S(2)}, u32[]{:S(2)}) collective-permute-start(bf16[2,128,384]{2,1,0:T(8,128)(2,1)S(1)} %get-tuple-element.71), channel_id=1, source_target_pairs={{0,8},{4,12},{8,0},{12,4},{1,9},{5,13},{9,1},{13,5},{2,10},{6,14},... | collective-permute-start | bytes 589832 | tf_op jit(solution)/shard_map/ppermute | solution.py:27
  96.5 10.2 %collective-permute-start.33 = (bf16[2,128,384]{2,1,0:T(8,128)(2,1)S(1)}, bf16[2,128,384]{2,1,0:T(8,128)(2,1)S(1)}, u32[]{:S(2)}, u32[]{:S(2)}) collective-permute-start(bf16[2,128,384]{2,1,0:T(8,128)(2,1)S(1)} %get-tuple-element.73), channel_id=1, source_target_pairs={{0,12},{4,8},{8,4},{12,0},{1,13},{5,9},{9,5},{13,1},{2,14},{6,10},... | collective-permute-start | bytes 589832 | tf_op jit(solution)/shard_map/ppermute | solution.py:27
  104.0 5.9 %collective-permute-start.37 = (bf16[96,256]{1,0:T(8,128)(2,1)S(1)}, bf16[96,256]{1,0:T(8,128)(2,1)S(1)}, u32[]{:S(2)}, u32[]{:S(2)}) collective-permute-start(bf16[96,256]{1,0:T(8,128)(2,1)S(1)} %get-tuple-element.79), channel_id=1, source_target_pairs={{0,1},{1,2},{2,3},{3,0},{4,5},{5,6},{6,7},{7,4},{8,9},{9,10},{10,1... | collective-permute-start | bytes 147464 | tf_op jit(solution)/shard_map/ppermute | solution.py:36
  104.9 9.2 %collective-permute-start.34 = (bf16[128,384]{1,0:T(8,128)(2,1)S(1)}, bf16[128,384]{1,0:T(8,128)(2,1)S(1)}, u32[]{:S(2)}, u32[]{:S(2)}) collective-permute-start(bf16[128,384]{1,0:T(8,128)(2,1)S(1)} %get-tuple-element.75), channel_id=1, source_target_pairs={{0,4},{4,0},{8,12},{12,8},{1,5},{5,1},{9,13},{13,9},{2,6},{6,2},{1... | collective-permute-start | bytes 294920 | tf_op jit(solution)/shard_map/ppermute | solution.py:27
  104.9 9.2 %collective-permute-start.35 = (bf16[128,384]{1,0:T(8,128)(2,1)S(1)}, bf16[128,384]{1,0:T(8,128)(2,1)S(1)}, u32[]{:S(2)}, u32[]{:S(2)}) collective-permute-start(bf16[128,384]{1,0:T(8,128)(2,1)S(1)} %get-tuple-element.76), channel_id=1, source_target_pairs={{0,8},{4,12},{8,0},{12,4},{1,9},{5,13},{9,1},{13,5},{2,10},{6,14},... | collective-permute-start | bytes 294920 | tf_op jit(solution)/shard_map/ppermute | solution.py:27
  106.4 7.7 %collective-permute-start.36 = (bf16[128,384]{1,0:T(8,128)(2,1)S(1)}, bf16[128,384]{1,0:T(8,128)(2,1)S(1)}, u32[]{:S(2)}, u32[]{:S(2)}) collective-permute-start(bf16[128,384]{1,0:T(8,128)(2,1)S(1)} %get-tuple-element.77), channel_id=1, source_target_pairs={{0,12},{4,8},{8,4},{12,0},{1,13},{5,9},{9,5},{13,1},{2,14},{6,10},... | collective-permute-start | bytes 294920 | tf_op jit(solution)/shard_map/ppermute | solution.py:27
  106.7 6.1 %collective-permute-start.38 = (bf16[96,256]{1,0:T(8,128)(2,1)S(1)}, bf16[96,256]{1,0:T(8,128)(2,1)S(1)}, u32[]{:S(2)}, u32[]{:S(2)}) collective-permute-start(bf16[96,256]{1,0:T(8,128)(2,1)S(1)} %get-tuple-element.80), channel_id=1, source_target_pairs={{0,2},{1,3},{2,0},{3,1},{4,6},{5,7},{6,4},{7,5},{8,10},{9,11},{10,... | collective-permute-start | bytes 147464 | tf_op jit(solution)/shard_map/ppermute | solution.py:36
  110.0 4.1 %collective-permute-start.39 = (bf16[96,256]{1,0:T(8,128)(2,1)S(1)}, bf16[96,256]{1,0:T(8,128)(2,1)S(1)}, u32[]{:S(2)}, u32[]{:S(2)}) collective-permute-start(bf16[96,256]{1,0:T(8,128)(2,1)S(1)} %get-tuple-element.81), channel_id=1, source_target_pairs={{0,3},{1,0},{2,1},{3,2},{4,7},{5,4},{6,5},{7,6},{8,11},{9,8},{10,9... | collective-permute-start | bytes 147464 | tf_op jit(solution)/shard_map/ppermute | solution.py:36

commit v13 on v12

--- a/solution.py
+++ b/solution.py
@@ -62,54 +62,52 @@
 
 
 def pack_kernel(wq, wkv, *refs):
-    outs, sems = refs[:-1], refs[-1]
-    cols = outs[0].shape[1] // 2
+    outs, (queries, keyvals, sems) = refs[:-3], refs[-3:]
+    parts, _, cols = outs[0].shape
+    half = cols // 2
     seq = lax.axis_index("seq")
     copies = []
-    for m, out in enumerate(outs):
+    for m in range(len(outs)):
         start = pl.multiple_of((seq ^ m) * cols, 128)
-        for k, source in enumerate((wq, wkv)):
+        for k, (source, held) in enumerate(((wq, queries), (wkv, keyvals))):
             copies.append(
                 pltpu.make_async_copy(
-                    source.at[0, :, pl.ds(start, cols)],
-                    out.at[:, pl.ds(k * cols, cols)],
-                    sems.at[2 * m + k],
+                    source.at[0, :, pl.ds(start, cols)], held.at[m], sems.at[2 * m + k]
                 )
             )
     for copy in copies:
         copy.start()
-    for copy in copies:
-        copy.wait()
-
-
-def stack_kernel(deps, *refs):
+    for m, out in enumerate(outs):
+        copies[2 * m].wait()
+        copies[2 * m + 1].wait()
+        for part in range(parts):
+            lanes = slice(part * half, (part + 1) * half)
+            out[part] = jnp.concatenate([queries[m][:, lanes], keyvals[m][:, lanes]], axis=1)
+
+
+def pair_kernel(deps, *refs):
     out = refs[-1]
-    at = 0
-    for ref in refs[deps:-1]:
-        if len(ref.shape) == 2:
-            out[at] = ref[...]
-            at += 1
-        else:
-            out[at : at + ref.shape[0]] = ref[...]
-            at += ref.shape[0]
-
-
-def place_kernel(hop, hops, *refs):
-    weights, parts = refs[-1], refs[:-1]
-    if hop > 0:
-        parts = parts[:-1]
-    place(hop, hops, parts, weights)
-
-
-def place(hop, hops, parts, weights):
+    for at, ref in enumerate(refs[deps:-1]):
+        out[at] = ref[...]
+
+
+def part_kernel(part, near, far, out):
+    for at in range(2):
+        out[at] = near[at, part]
+        out[at + 2] = far[at, part]
+
+
+def place(hop, hops, blocks, weights):
     seq, rep = lax.axis_index("seq"), lax.axis_index("dp")
-    m = 0
-    for part in parts:
-        count, rows = part.shape[:2]
-        for j in range(count):
-            block = (seq ^ m) * hops + fold(lax.rem(fold(rep) + hops - hop, hops))
-            weights[pl.ds(pl.multiple_of(block * rows, 16), rows)] = part[j]
-            m += 1
+    for m, block in enumerate(blocks):
+        rows = block.shape[0]
+        at = (seq ^ m) * hops + fold(lax.rem(fold(rep) + hops - hop, hops))
+        weights[pl.ds(pl.multiple_of(at * rows, 16), rows)] = block[...]
+
+
+def place_kernel(part, hops, near, far, chunk, weights):
+    place(0, hops, [near.at[0, part], near.at[1, part], far.at[0, part], far.at[1, part]], weights)
+    place(1, hops, [chunk.at[m] for m in range(4)], weights)
 
 
 def first_kernel(turns, far, incoming, contacts, out, states):
@@ -197,10 +195,26 @@
         scales[step][...] = jnp.broadcast_to(lax.rsqrt(mean + epsilon), (frames, 128))
 
 
+def dense(value, lead):
+    frames = value.shape[0]
+    rest = value[:, :64] if lead else value[:, 128:]
+    full = value[:, 64:] if lead else value[:, :128]
+    rest = jnp.concatenate([rest[: frames // 2], rest[frames // 2 :]], axis=1)
+    return jnp.concatenate([full, rest], axis=0)
+
+
+def undense(left, right, frames):
+    middle = []
+    for ref in (left, right):
+        rest = ref[frames:]
+        middle.append(jnp.concatenate([rest[:, :64], rest[:, 64:]], axis=0))
+    return jnp.concatenate([left[:frames], jnp.concatenate(middle, axis=1), right[:frames]], axis=1)
+
+
 def step_kernel(cfg, *refs):
-    step, has_relay = cfg["step"], cfg["has_relay"]
+    step, has_relay, parts = cfg["step"], cfg["has_relay"], cfg["parts"]
     pieces, hops, head, turns = cfg["pieces"], cfg["hops"], cfg["head"], cfg["turns"]
-    heads, group, halves = cfg["heads"], cfg["group"], cfg["halves"]
+    heads, group = cfg["heads"], cfg["group"]
     refs = list(refs)
 
     def take(count):
@@ -209,38 +223,41 @@
 
     bias, times, gain, freq, gate, flags = take(6)
     if has_relay:
-        second, embed, relay = take(pieces), take(1)[0], take(pieces * halves)
+        second, embed, relay = take(pieces), take(1)[0], take(2 * pieces)
     else:
         scaled, scales, own_hidden = take(3)
-    chunk = take(2) if step == 0 else None
-    weights = take(1)[0]
-    outs = take(halves)
+    chunks = take(2) if step == 0 else None
+    weights = take(len(parts))
+    left = take(1)[0] if parts == (1,) else None
+    sends = take(1)[0] if len(parts) == 1 else None
+    out = take(1)[0]
     if step == 0:
-        weights = take(1)[0]
+        weights = take(1)
     proj, att = take(2)
     if has_relay:
         scaled, scales, own_hidden, mod = take(4)
     offsets = offsets_of(pieces)
     frames, width = scaled.shape
-    rows, cols = frames // pieces, att.shape[0]
-    part = pieces // halves
-    seq, rep, section = lax.axis_index("seq"), lax.axis_index("dp"), lax.axis_index("pipe")
+    cols = att.shape[0]
+    half = cols // 2
+    rows = frames // pieces
+    seq, section = lax.axis_index("seq"), lax.axis_index("pipe")
     _, batch = turn_and_batch(step, turns)
 
     if step == 0:
-        place(hops - 1, hops, chunk, weights)
+        for hop, chunk in zip((2, 3), chunks):
+            place(hop, hops, [chunk.at[m] for m in range(pieces)], weights[0])
 
     def normalize(relayed):
         total = jnp.zeros((frames, 128), jnp.float32)
         for i in range(pieces):
             lanes = pl.ds(pl.multiple_of((seq ^ offsets[i]) * cols, 128), cols)
-            blocks = []
-            for p in range(pieces):
-                if relayed:
-                    j = offsets.index(offsets[i] ^ offsets[p])
-                    blocks.append(relay[(j // part) * pieces + i][j % part])
-                else:
-                    blocks.append(second[p][:rows, lanes])
+            if relayed:
+                value = undense(relay[i], relay[pieces + i], frames)
+                order = [offsets.index(offsets[i] ^ offsets[p]) for p in range(pieces)]
+                blocks = [value[j * rows : (j + 1) * rows] for j in order]
+            else:
+                blocks = [second[p][:rows, lanes] for p in range(pieces)]
             hidden = jnp.concatenate(blocks, axis=0).astype(jnp.float32)
             hidden = hidden + embed[:, lanes].astype(jnp.float32)
             for lane in range(0, cols, 128):
@@ -273,54 +290,73 @@
 
     flag_column = columns_of(flag_of, pieces, rows)[:, 16:17]
     score_scale = head ** (-0.5) * math.log2(math.e)
-    for at in range(0, 2 * cols, 256):
-        lane = at + lax.broadcasted_iota(jnp.int32, (1, 256), 1)
-        factor = jnp.where(lane < cols, score_scale, 1.0)
-        projected = jnp.dot(
-            scaled[...], weights[:, at : at + 256], preferred_element_type=jnp.float32
-        )
-        proj[:, at : at + 256] = (projected * scale * factor).astype(jnp.bfloat16)
-    proj[:, 2 * cols :] = jnp.zeros((frames, 128), jnp.bfloat16)
     lanes = lax.broadcasted_iota(jnp.int32, (frames, 128), 1)
     row_lanes = lax.broadcasted_iota(jnp.int32, (1, 128), 1)
     flag_lanes = jnp.logical_or(lanes == head, lanes == head + 1)
-
-    def part_of(at):
+    pitch = cols + 128
+
+    for k, part in enumerate(parts):
+        base = k * pitch
+        for at in range(0, cols, 256):
+            size = min(256, cols - at)
+            lane = at + lax.broadcasted_iota(jnp.int32, (1, size), 1)
+            factor = jnp.where(lane < half, score_scale, 1.0)
+            projected = jnp.dot(
+                scaled[...], weights[k][:, at : at + size], preferred_element_type=jnp.float32
+            )
+            proj[:, base + at : base + at + size] = (projected * scale * factor).astype(
+                jnp.bfloat16
+            )
+        proj[:, base + cols : base + pitch] = jnp.zeros((frames, 128), jnp.bfloat16)
+
+    def slice_of(at):
         return proj[:, at : at + 128].astype(jnp.float32)
 
     keys, values = [], []
-    for kv in range(heads // group):
-        base = cols + kv * 2 * head
-        key = jnp.where(flag_lanes, flag_column, jnp.where(lanes < head, part_of(base), 0.0))
-        value = jnp.where(lanes < head, part_of(base + head), jnp.where(lanes == head, 1.0, 0.0))
+    for k in range(len(parts)):
+        at = k * pitch + half
+        key = jnp.where(flag_lanes, flag_column, jnp.where(lanes < head, slice_of(at), 0.0))
+        value = jnp.where(
+            lanes < head, slice_of(at + head), jnp.where(lanes == head, 1.0, 0.0)
+        )
         keys.append(key.astype(jnp.bfloat16))
         values.append(value.T.astype(jnp.bfloat16))
 
-    def scores_of(h):
-        strength = jnp.zeros((1, 128), jnp.float32) + bias[0, seq * heads + h] * math.log2(math.e)
+    def scores_of(k, h):
+        strength = bias[0, seq * heads + parts[k] * group + h] * math.log2(math.e)
+        strength = jnp.zeros((1, 128), jnp.float32) + strength
         coarse = strength.astype(jnp.bfloat16).astype(jnp.float32)
         tail = jnp.where(
             row_lanes == head, coarse, jnp.where(row_lanes == head + 1, strength - coarse, 0.0)
         )
-        query = jnp.where(lanes < head, part_of(h * head), tail).astype(jnp.bfloat16)
+        query = jnp.where(lanes < head, slice_of(k * pitch + h * head), tail).astype(jnp.bfloat16)
         return lax.dot_general(
-            keys[h // group], query, (((1,), (1,)), ((), ())), preferred_element_type=jnp.float32
-        )
-
-    scores = scores_of(0)
-    for h in range(heads):
-        ahead = scores_of(h + 1) if h + 1 < heads else None
+            keys[k], query, (((1,), (1,)), ((), ())), preferred_element_type=jnp.float32
+        )
+
+    tasks = [(k, h) for k in range(len(parts)) for h in range(group)]
+    scores = scores_of(*tasks[0])
+    for index, (k, h) in enumerate(tasks):
+        ahead = scores_of(*tasks[index + 1]) if index + 1 < len(tasks) else None
         top = jnp.max(scores, axis=0, keepdims=True)
         weight = jnp.exp2(scores - top).astype(jnp.bfloat16)
-        mixed = jnp.dot(values[h // group], weight, preferred_element_type=jnp.float32)
-        att[h * head : (h + 1) * head, :] = mixed[:head] * (1.0 / mixed[head : head + 1])
+        mixed = jnp.dot(values[k], weight, preferred_element_type=jnp.float32)
+        at = (parts[k] * group + h) * head
+        att[at : at + head, :] = mixed[:head] * (1.0 / mixed[head : head + 1])
         scores = ahead
-    own = pl.ds(pl.multiple_of(seq * cols, 128), cols)
-    attended = att[...].T.astype(jnp.bfloat16).astype(jnp.float32)
-    output = (own_hidden[...] + gate[:, own] * attended).astype(jnp.bfloat16)
-    blocks = output.reshape(pieces, rows, cols)
-    for k in range(halves):
-        outs[k][...] = blocks[k * part : (k + 1) * part]
+    gates = gate[:, pl.ds(pl.multiple_of(seq * cols, 128), cols)]
+    first, last = parts[0] * half, (parts[-1] + 1) * half
+    attended = att[first:last].T.astype(jnp.bfloat16).astype(jnp.float32)
+    output = own_hidden[...][:, first:last] + gates[:, first:last] * attended
+    if parts == (0,):
+        out[:, :half] = output.astype(jnp.bfloat16)
+    elif parts == (1,):
+        output_both = jnp.concatenate([left[:, :half].astype(jnp.float32), output], axis=1)
+        out[...] = output_both.astype(jnp.bfloat16).reshape(pieces, rows, cols)
+    else:
+        out[...] = output.astype(jnp.bfloat16).reshape(pieces, rows, cols)
+    if sends is not None:
+        sends[...] = dense(output, parts == (1,)).astype(jnp.bfloat16)
 
 
 def tie_kernel(*refs):
@@ -419,7 +455,6 @@
     copy.wait()
 
 
-HALVES = 2
 MIB = 1024 * 1024
 
 
@@ -448,8 +483,6 @@
     feats = head_cotangent.shape[4]
     cols = width // seq_count
     w_rows = w_query.shape[1]
-    steps = turns + 1
-    part = seq_count // HALVES
     kind = jnp.bfloat16
     smem = pl.BlockSpec(memory_space=pltpu.SMEM)
     vmem = pl.BlockSpec(memory_space=pltpu.VMEM)
@@ -476,49 +509,53 @@
     packed = call(
         pack_kernel,
         "pack",
-        [pltpu.VMEM((w_rows, 2 * cols), kind)] * seq_count,
+        [pltpu.VMEM((2, w_rows, cols), kind)] * seq_count,
         [anywhere, anywhere],
         [pin(w_query, pltpu.HBM), pin(w_keyval, pltpu.HBM)],
-        [pltpu.SemaphoreType.DMA((2 * seq_count,))],
+        [pltpu.VMEM((seq_count, w_rows, cols), kind)] * 2
+        + [pltpu.SemaphoreType.DMA((2 * seq_count,))],
         out_specs=[vmem] * seq_count,
     )
     blocks = [packed[0]] + [swap(packed[m], m) for m in range(1, seq_count)]
 
-    def stacked(name, count, deps, values):
+    def paired(name, deps, values):
         return call(
-            functools.partial(stack_kernel, len(deps)),
+            functools.partial(pair_kernel, len(deps)),
             name,
-            pltpu.VMEM((count, w_rows, 2 * cols), kind),
-            [anywhere] * len(deps) + [vmem] * len(values),
+            pltpu.VMEM((2, 2, w_rows, cols), kind),
+            [anywhere] * len(deps) + [vmem] * 2,
             deps + values,
             out_specs=vmem,
         )
 
-    weights = None
-
-    def placed(hop, parts):
-        operands = [pin(part) for part in parts] + ([pin(weights)] if hop else [])
-        return call(
-            functools.partial(place_kernel, hop, hops),
-            "place%d" % hop,
-            pltpu.VMEM((width, 2 * cols), kind),
-            [vmem] * len(operands),
-            operands,
+    near = paired("near", [], blocks[:2])
+    near_next = ring_step(near)
+    far = paired("far", [near_next], blocks[2:])
+    far_next = ring_step(far)
+    rings, partial = [], []
+    for part in range(2):
+        chunk = call(
+            functools.partial(part_kernel, part),
+            "part%d" % part,
+            pltpu.VMEM((seq_count, w_rows, cols), kind),
+            [vmem, vmem],
+            [near_next, far_next],
             out_specs=vmem,
-            input_output_aliases={len(parts): 0} if hop else {},
-        )
-
-    near = stacked("near", 2, [], blocks[:2])
-    near_next = ring_step(near)
-    far = stacked("far", 2, [near_next], blocks[2:])
-    far_next = ring_step(far)
-    rings = [[near, near_next], [far, far_next]]
-    for hop in range(2, hops - 1):
-        for chunks in rings:
-            chunks.append(ring_step(chunks[-1]))
-    last_chunk = [ring_step(chunks[-1]) for chunks in rings]
-    for hop in range(hops - 1):
-        weights = placed(hop, [chunks[hop] for chunks in rings])
+        )
+        rings.append([chunk])
+        partial.append(
+            call(
+                functools.partial(place_kernel, part, hops),
+                "place%d" % part,
+                pltpu.VMEM((width, cols), kind),
+                [vmem] * 3,
+                [pin(near), pin(far), pin(chunk)],
+                out_specs=vmem,
+            )
+        )
+    for hop in range(2):
+        for ring in rings:
+            ring.append(ring_step(ring[-1]))
 
     def tie(values, deps):
         return call(
@@ -542,7 +579,7 @@
     )
     across = swap(mine, 2)
     beside = swap(mine, 1)
-    (across,) = tie([across], [chunks[-1] for chunks in rings])
+    (across,) = tie([across], [ring[1] for ring in rings])
     first = [mine, across, beside, swap(across, 1)]
     prepared = call(
         functools.partial(norm_kernel, turns, seq_count),
@@ -571,91 +608,107 @@
     )
     second = [mine, swap(mine, 2), swap(mine, 1)]
 
-    outputs = []
-    relayed = {}
-    for step in range(steps):
+    common = [key_bias, timesteps, norm_gain, time_freq, attn_gate, keyframes]
+
+    def run_step(step, parts, large, out_shape, aliases):
         cfg = {
             "step": step,
-            "has_relay": step in relayed,
+            "has_relay": step >= 2,
+            "parts": parts,
             "pieces": seq_count,
             "hops": hops,
             "head": head,
             "heads": heads,
             "group": heads // kv_heads,
             "turns": turns,
-            "halves": HALVES,
         }
-        operands = [key_bias, timesteps, norm_gain, time_freq, attn_gate, keyframes]
         scratch = [
-            pltpu.VMEM((frames, 2 * cols + 128), kind),
+            pltpu.VMEM((frames, len(parts) * (cols + 128)), kind),
             pltpu.VMEM((cols, frames), jnp.float32),
         ]
-        if step in relayed:
-            large = second + [prepared[4 + step]] + relayed[step]
+        if step >= 2:
             scratch += [
                 pltpu.VMEM((frames, width), kind),
                 pltpu.VMEM((frames, 128), jnp.float32),
                 pltpu.VMEM((frames, cols), jnp.float32),
                 pltpu.VMEM((1, width), jnp.float32),
             ]
-        else:
-            large = [prepared[step], prepared[2 + step], prepared[4 + step]]
-        large += last_chunk + [weights] if step == 0 else [weights]
-        operands += [pin(value) for value in large]
-        out_shape = [pltpu.VMEM((part, rows, cols), kind)] * HALVES
-        if step == 0:
-            out_shape += [pltpu.VMEM((width, 2 * cols), kind)]
-        results = call(
+        operands = common + [pin(value) for value in large]
+        return call(
             functools.partial(step_kernel, cfg),
-            "step%d" % step,
+            "step%d%s" % (step, "".join("ab"[part] for part in parts)),
             out_shape,
             [smem, smem] + [vmem] * (len(operands) - 2),
             operands,
             scratch,
             16,
-            2 * frames * width * 2 * cols + 4 * heads * frames * frames * head,
+            len(parts) * frames * (2 * width * cols + 2 * heads * frames * head),
             out_specs=[vmem] * len(out_shape),
-            input_output_aliases={len(operands) - 1: HALVES} if step == 0 else {},
-        )
-        outputs.append(list(results[:HALVES]))
-        if step == 0:
-            weights = results[HALVES]
-        if step == 0:
-            (second[1],) = tie([second[1]], [outputs[-1][0]])
-            second.append(swap(second[1], 1))
-        if step == 2:
-            early = call(
-                functools.partial(early_kernel, turns, seq_count, HALVES, feats),
-                "early",
-                [shape((turns - 1, rows, cols), kind)] * seq_count
-                + [shape((cols, feats), jnp.float32)],
-                [vmem] * (turns * HALVES + seq_count),
-                [half for output in outputs for half in output] + second,
-                limit=8,
-                out_specs=[vmem] * (seq_count + 1),
-            )
-            early, early_grad = list(early[:-1]), early[-1]
-            early = [early[0]] + [swap(early[m], m) for m in range(1, seq_count)]
-            pending = [piece for k in range(HALVES) for piece in (crossing[k][0], crossing[k][1])]
-            tied = tie(pending, [early_grad])
-            relayed[3] = []
-            for k in range(HALVES):
-                mine, across = tied[2 * k], tied[2 * k + 1]
-                relayed[3] += [mine, across, swap(mine, 1), swap(across, 1)]
-        if step + 2 < steps:
-            crossing = []
-            for half in outputs[-1]:
-                piece = handed_over(half)
-                crossing.append((piece, swap(piece, 2)))
+            input_output_aliases=aliases,
+        )
+
+    whole = pltpu.VMEM((seq_count, rows, cols), kind)
+    sent = pltpu.VMEM((frames * 3 // 2, 128), kind)
+    weights = list(partial)
+    relays, lefts, outputs = ([], []), [], []
+    for part in range(2):
+        for step in range(2):
+            large = [prepared[step], prepared[2 + step], prepared[4 + step]]
             if step == 0:
-                relayed[2] = []
-                for mine, across in crossing:
-                    relayed[2] += [mine, across, swap(mine, 1), swap(across, 1)]
+                chunks = rings[part][1:]
+                if part:
+                    (last_chunk,) = tie(chunks[1:], [relays[0][0][0], lefts[1]])
+                    chunks = [chunks[0], last_chunk]
+                large += chunks
+            large += [weights[part]]
+            aliases = {len(common) + len(large) - 1: 2} if step == 0 else {}
+            out_shape = [sent, whole if part else pltpu.VMEM((frames, 256), kind)]
+            if step == 0:
+                out_shape += [pltpu.VMEM((width, cols), kind)]
+            if part:
+                left = lefts[step]
+                if step == 1:
+                    (left,) = tie([left], [relays[1][0][0], relays[0][0][1]])
+                large += [left]
+            results = run_step(step, (part,), large, out_shape, aliases)
+            if step == 0:
+                weights[part] = results[2]
+            (outputs if part else lefts).append(results[1])
+            piece = handed_over(results[0])
+            relays[step].append((piece, swap(piece, 2)))
+    (second[1],) = tie([second[1]], [outputs[0]])
+    second.append(swap(second[1], 1))
+
+    def complete(crossing):
+        return [
+            piece
+            for mine, across in crossing
+            for piece in (mine, across, swap(mine, 1), swap(across, 1))
+        ]
+
+    relay = complete(relays[0])
+    (output,) = run_step(2, (0, 1), second + [prepared[6]] + relay + weights, [whole], {})
+    outputs.append(output)
+    early = call(
+        functools.partial(early_kernel, turns, seq_count, 1, feats),
+        "early",
+        [shape((turns - 1, rows, cols), kind)] * seq_count + [shape((cols, feats), jnp.float32)],
+        [vmem] * (turns + seq_count),
+        outputs + second,
+        limit=8,
+        out_specs=[vmem] * (seq_count + 1),
+    )
+    early, early_grad = list(early[:-1]), early[-1]
+    early = [early[0]] + [swap(early[m], m) for m in range(1, seq_count)]
+    tied = tie([piece for pair in relays[1] for piece in pair], [early_grad])
+    relay = complete([(tied[0], tied[1]), (tied[2], tied[3])])
+    (output,) = run_step(3, (0, 1), second + [prepared[7]] + relay + weights, [whole], {})
+    outputs.append(output)
 
     g_shape = (cols // hops, feats)
-    operands = outputs[-2] + outputs[-1] + second + early[:-1] + [early_grad]
+    operands = outputs[-2:] + second + early[:-1] + [early_grad]
     settled = call(
-        functools.partial(settle_kernel, turns, seq_count, HALVES, hops, feats),
+        functools.partial(settle_kernel, turns, seq_count, 1, hops, feats),
         "settle",
         [shape((rows, cols), kind)] * seq_count
         + [shape(g_shape, jnp.float32)]

time: 116 us -> 121 us (1.043)
  Pallas kernels: 27.6 us -> 31.2 us
  waiting for transfers between devices: 47.7 us -> 49.9 us
  starting transfers between devices: 35.3 us -> 33.3 us
    ppermute x4, waiting for transfers between devices: 9.04 us -> 13.7 us  [handed_over(): return lax.ppermute(value, 'pipe', [(0, 1), (1, 0)])]
    pallas_call x19 -> x24, Pallas kernels: 27.6 us -> 31.2 us  [call(): pl.pallas_call(kernel, out_shape=out_shape, in_specs=in_specs, scratch_sh...]
    ppermute x27, waiting for transfers between devices: 13.3 us -> 10.3 us  [swap(): lax.ppermute(value, 'seq', [(source, source ^ bit) for source in range(co...]
    ppermute x3, waiting for transfers between devices: 3.81 us -> 5.48 us  [shifted(): lax.ppermute(value, axis, [(source, (source + shift) % count) for source...]
    ppermute x3, starting transfers between devices: 4.35 us -> 2.68 us  [shifted(): lax.ppermute(value, axis, [(source, (source + shift) % count) for source...]
    unnamed x41 -> x35, local copies, waits for them, and re-layouts: 3.98 us -> 4.68 us
  transfers between devices with their start and end apart: 40 -> 40, of which waited for: 17 -> 17; matrix products, arithmetic and copies ran while one was open for 0% -> 1% of each run, Pallas kernels for 21% -> 23%
where the time goes in v13:
time: 121 us; the launch traced here: 120 us
  waiting for transfers between devices  49.9 us (41%)
  starting transfers between devices  33.3 us (28%)
  Pallas kernels  31.2 us (26%)
  local copies, waits for them, and re-layouts  4.68 us (4%)
  between operations  1.21 us (1%)
    pallas_call x24, Pallas kernels, call(): pl.pallas_call(kernel, out_shape=out_shape, in_specs=in_specs, scratch_sh...  31.2 us
    ppermute x6, waiting for transfers between devices, ring_step(): return lax.ppermute(value, 'dp', pairs)  20.5 us
    ppermute x27, starting transfers between devices, swap(): lax.ppermute(value, 'seq', [(source, source ^ bit) for source in range(co...  13.8 us
    ppermute x4, waiting for transfers between devices, handed_over(): return lax.ppermute(value, 'pipe', [(0, 1), (1, 0)])  13.7 us
    ppermute x6, starting transfers between devices, ring_step(): return lax.ppermute(value, 'dp', pairs)  11.5 us
    ppermute x27, waiting for transfers between devices, swap(): lax.ppermute(value, 'seq', [(source, source ^ bit) for source in range(co...  10.3 us
    ppermute x3, waiting for transfers between devices, shifted(): lax.ppermute(value, axis, [(source, (source + shift) % count) for source...  5.48 us
    ppermute x4, starting transfers between devices, handed_over(): return lax.ppermute(value, 'pipe', [(0, 1), (1, 0)])  5.24 us
  transfers between devices with their start and end apart: 40, of which 17 were waited for; matrix products, arithmetic and copies ran while one was open for 1% of the time, Pallas kernels for 23%

profile of v13, /device:TPU:0, one launch (start us, length us, event | category | flops | bytes accessed | tf_op | source)
XLA Modules:
  0.0 120.2 jit_solution(5488366885673058046)
XLA Ops:
  0.7 1.5 %pack.1 = (bf16[2,96,384]{2,1,0:T(8,128)(2,1)S(1)}, bf16[2,96,384]{2,1,0:T(8,128)(2,1)S(1)}, bf16[2,96,384]{2,1,0:T(8,128)(2,1)S(1)}, bf16[2,96,384]{2,1,0:T(8,128)(2,1)S(1)}) custom-call(bf16[1,96,1536]{2,1,0:T(8,128)(2,1)} %wq.1, bf16[1,96,1536]{2,1,0:T(8,128)(2,1)} %wkv.1), custom_call_target="tpu_custom_call" | custom-call | tf_op jit(solution)/shard_map/pack/pallas_call | solution.py:493
  2.1 0.5 collective-permute-start
  2.7 1.0 collective-permute-done.refs_1_
  3.7 3.0 %collective-permute-start.1 = (bf16[2,2,96,384]{3,2,1,0:T(8,128)(2,1)S(1)}, bf16[2,2,96,384]{3,2,1,0:T(8,128)(2,1)S(1)}, u32[]{:S(2)}, u32[]{:S(2)}) collective-permute-start(bf16[2,2,96,384]{3,2,1,0:T(8,128)(2,1)S(1)} %near.1), channel_id=1, source_target_pairs={{0,1},{1,3},{3,2},{2,0},{4,5},{5,7},{7,6},{6,4},{8,9},{9,11},{11,1... | collective-permute-start | bytes 884744 | tf_op jit(solution)/shard_map/ppermute | solution.py:46
  6.7 0.7 copy-done.1
  7.4 1.5 %collective-permute-start.2 = (bf16[2,96,384]{2,1,0:T(8,128)(2,1)S(1)}, bf16[2,96,384]{2,1,0:T(8,128)(2,1)S(1)}, u32[]{:S(2)}, u32[]{:S(2)}) collective-permute-start(bf16[2,96,384]{2,1,0:T(8,128)(2,1)S(1)} %get-tuple-element.46), channel_id=1, source_target_pairs={{0,8},{4,12},{8,0},{12,4},{1,9},{5,13},{9,1},{13,5},{2,10},{6,14},... | collective-permute-start | bytes 442376 | tf_op jit(solution)/shard_map/ppermute | solution.py:27
  8.9 5.2 %collective-permute-done.2.refs_1_ = bf16[2,96,384]{2,1,0:T(8,128)(2,1)S(1)} collective-permute-done((bf16[2,96,384]{2,1,0:T(8,128)(2,1)S(1)}, bf16[2,96,384]{2,1,0:T(8,128)(2,1)S(1)}, u32[]{:S(2)}, u32[]{:S(2)}) %collective-permute-start.2) | collective-permute-done | bytes 147488 | tf_op jit(solution)/shard_map/ppermute | solution.py:27
  14.1 1.1 collective-permute-done.3.refs_2_
  15.3 1.4 %collective-permute-start.4 = (bf16[272,1536]{1,0:T(8,128)(2,1)S(1)}, bf16[272,1536]{1,0:T(8,128)(2,1)S(1)}, u32[]{:S(2)}, u32[]{:S(2)}) collective-permute-start(bf16[272,1536]{1,0:T(8,128)(2,1)S(1)} %first.1.refs_0_), channel_id=1, source_target_pairs={{0,8},{4,12},{8,0},{12,4},{1,9},{5,13},{9,1},{13,5},{2,10},{6,14},... | collective-permute-start | bytes 2506760 | tf_op jit(solution)/shard_map/ppermute | solution.py:27
  16.7 2.6 %collective-permute-start.5 = (bf16[2,2,96,384]{3,2,1,0:T(8,128)(2,1)S(1)}, bf16[2,2,96,384]{3,2,1,0:T(8,128)(2,1)S(1)}, u32[]{:S(2)}, u32[]{:S(2)}) collective-permute-start(bf16[2,2,96,384]{3,2,1,0:T(8,128)(2,1)S(1)} %far.1), channel_id=1, source_target_pairs={{0,1},{1,3},{3,2},{2,0},{4,5},{5,7},{7,6},{6,4},{8,9},{9,11},{11,1... | collective-permute-start | bytes 884744 | tf_op jit(solution)/shard_map/ppermute | solution.py:46
  19.3 7.9 %collective-permute-done.5.far = bf16[2,2,96,384]{3,2,1,0:T(8,128)(2,1)S(1)} collective-permute-done((bf16[2,2,96,384]{3,2,1,0:T(8,128)(2,1)S(1)}, bf16[2,2,96,384]{3,2,1,0:T(8,128)(2,1)S(1)}, u32[]{:S(2)}, u32[]{:S(2)}) %collective-permute-start.5) | collective-permute-done | bytes 294944 | tf_op jit(solution)/shard_map/ppermute | solution.py:46
  27.3 1.7 %collective-permute-start.6 = (bf16[4,96,384]{2,1,0:T(8,128)(2,1)S(1)}, bf16[4,96,384]{2,1,0:T(8,128)(2,1)}, u32[]{:S(2)}, u32[]{:S(2)}) collective-permute-start(bf16[4,96,384]{2,1,0:T(8,128)(2,1)S(1)} %part0.1.chunk), channel_id=1, source_target_pairs={{0,1},{1,3},{3,2},{2,0},{4,5},{5,7},{7,6},{6,4},{8,9},{9,11},{11,1... | collective-permute-start | bytes 884744 | tf_op jit(solution)/shard_map/ppermute | solution.py:46
  29.1 1.7 %collective-permute-start.7 = (bf16[4,96,384]{2,1,0:T(8,128)(2,1)S(1)}, bf16[4,96,384]{2,1,0:T(8,128)(2,1)}, u32[]{:S(2)}, u32[]{:S(2)}) collective-permute-start(bf16[4,96,384]{2,1,0:T(8,128)(2,1)S(1)} %part1.1.chunk), channel_id=1, source_target_pairs={{0,1},{1,3},{3,2},{2,0},{4,5},{5,7},{7,6},{6,4},{8,9},{9,11},{11,1... | collective-permute-start | bytes 884744 | tf_op jit(solution)/shard_map/ppermute | solution.py:46
  30.8 7.5 %collective-permute-done.6.refs_1_.refs_9_ = bf16[4,96,384]{2,1,0:T(8,128)(2,1)} collective-permute-done((bf16[4,96,384]{2,1,0:T(8,128)(2,1)S(1)}, bf16[4,96,384]{2,1,0:T(8,128)(2,1)}, u32[]{:S(2)}, u32[]{:S(2)}) %collective-permute-start.6) | collective-permute-done | bytes 294944 | tf_op jit(solution)/shard_map/ppermute | solution.py:46
  38.2 5.1 %collective-permute-done.7.refs_2_.refs_9_ = bf16[4,96,384]{2,1,0:T(8,128)(2,1)} collective-permute-done((bf16[4,96,384]{2,1,0:T(8,128)(2,1)S(1)}, bf16[4,96,384]{2,1,0:T(8,128)(2,1)}, u32[]{:S(2)}, u32[]{:S(2)}) %collective-permute-start.7) | collective-permute-done | bytes 294944 | tf_op jit(solution)/shard_map/ppermute | solution.py:46
  43.5 0.6 collective-permute-start.8
  44.0 0.8 collective-permute-start.12
  44.8 1.7 %collective-permute-start.11 = (bf16[4,96,384]{2,1,0:T(8,128)(2,1)}, bf16[4,96,384]{2,1,0:T(8,128)(2,1)}, u32[]{:S(2)}, u32[]{:S(2)}) collective-permute-start(bf16[4,96,384]{2,1,0:T(8,128)(2,1)} %collective-permute-done.7.refs_2_.refs_9_), channel_id=1, source_target_pairs={{0,1},{1,3},{3,2},{2,0},{4,5},{5,7},{7,6},{6,4},{8,9},{9,11},{11,1... | collective-permute-start | bytes 884744 | tf_op jit(solution)/shard_map/ppermute | solution.py:46
  46.5 1.3 %copy.29.times.refs_1_ = s32[4,1]{1,0:T(4,128)} copy(s32[4,1]{0,1:T(1,128)} %param.15) | data formatting | bytes 32 | tf_op args[3]
  47.9 1.0 copy-done.2
  48.8 1.0 copy-done.7
  49.9 0.5 copy-done.13
  50.5 0.1 copy-done.14
  50.6 4.5 %norm.1 = (bf16[512,1536]{1,0:T(8,128)(2,1)S(1)}, bf16[512,1536]{1,0:T(8,128)(2,1)S(1)}, f32[512,128]{1,0:T(8,128)S(1)}, f32[512,128]{1,0:T(8,128)S(1)}, f32[512...) custom-call(s32[4,1]{1,0:T(4,128)S(1)} %copy-done.13, ...), custom_call_target="tpu_custom_call" | custom-call | tf_op jit(solution)/shard_map/norm/pallas_call | solution.py:493
  55.2 3.3 %step0a.1 = (bf16[768,128]{1,0:T(8,128)(2,1)S(1)}, bf16[512,256]{1,0:T(8,128)(2,1)S(1)}, bf16[1536,384]{1,0:T(8,128)(2,1)S(1)}) custom-call(f32[1,16]{1,0:T(1,128)S(1)} %copy-done.15, s32[4,1]{1,0:T(4,128)S(1)} %copy-done.13, f32[1,1536]{1,0:T(1,128)S(1)} %copy-done.8, f32[1,1536]{1,0:T(1,128)S(1)} %copy-done.9, ...), custom_call_target="tpu_custom_call", output_to_operand_aliasing={{2}: (11, {})} | custom-call | flops 805306368 | bytes 1572864 | tf_op jit(solution)/shard_map/step0a/pallas_call | solution.py:493
  58.5 1.6 %collective-permute-start.13 = (bf16[768,128]{1,0:T(8,128)(2,1)S(1)}, bf16[768,128]{1,0:T(8,128)(2,1)S(1)}, u32[]{:S(2)}, u32[]{:S(2)}) collective-permute-start(bf16[768,128]{1,0:T(8,128)(2,1)S(1)} %get-tuple-element.51), channel_id=1, source_target_pairs={{0,16},{16,0},{1,17},{17,1},{2,18},{18,2},{3,19},{19,3},{4,20},{20... | collective-permute-start | bytes 589832 | tf_op jit(solution)/shard_map/ppermute | solution.py:31
  60.1 0.1 place1.1.refs_11_
  60.2 2.7 %step1a.1 = (bf16[768,128]{1,0:T(8,128)(2,1)S(1)}, bf16[512,256]{1,0:T(8,128)(2,1)S(1)}) custom-call(f32[1,16]{1,0:T(1,128)S(1)} %copy-done.15, s32[4,1]{1,0:T(4,128)S(1)} %copy-done.13, f32[1,1536]{1,0:T(1,128)S(1)} %copy-done.8, f32[1,1536]{1,0:T(1,128)S(1)} %copy-done.9, f32[1,1536]{1,0:T(1,128)S(1)} %copy-done.11, s32[4,1,512]{2,1,0:T(1,128)S(1)} %copy-done.10, ...), custom_call_target="tpu_custom_call" | custom-call | flops 805306368 | bytes 1572864 | tf_op jit(solution)/shard_map/step1a/pallas_call | solution.py:493
  62.9 2.1 %collective-permute-done.13.refs_1_.refs_11_ = bf16[768,128]{1,0:T(8,128)(2,1)S(1)} collective-permute-done((bf16[768,128]{1,0:T(8,128)(2,1)S(1)}, bf16[768,128]{1,0:T(8,128)(2,1)S(1)}, u32[]{:S(2)}, u32[]{:S(2)}) %collective-permute-start.13) | collective-permute-done | bytes 196640 | tf_op jit(solution)/shard_map/ppermute | solution.py:31
  65.0 3.3 %step0b.1 = (bf16[768,128]{1,0:T(8,128)(2,1)S(1)}, bf16[4,128,384]{2,1,0:T(8,128)(2,1)S(1)}, bf16[1536,384]{1,0:T(8,128)(2,1)S(1)}) custom-call(f32[1,16]{1,0:T(1,128)S(1)} %copy-done.15, s32[4,1]{1,0:T(4,128)S(1)} %copy-done.13, f32[1,1536]{1,0:T(1,128)S(1)} %copy-done.8, f32[1,1536]{1,0:T(1,128)S(1)} %copy-done.9, ...), custom_call_target="tpu_custom_call", output_to_operand_aliasing={{2}: (11, {})} | custom-call | flops 805306368 | bytes 1572864 | tf_op jit(solution)/shard_map/step0b/pallas_call | solution.py:493
  68.3 0.1 collective-permute-start.15
  68.4 1.6 %collective-permute-start.23 = (bf16[768,128]{1,0:T(8,128)(2,1)S(1)}, bf16[768,128]{1,0:T(8,128)(2,1)S(1)}, u32[]{:S(2)}, u32[]{:S(2)}) collective-permute-start(bf16[768,128]{1,0:T(8,128)(2,1)S(1)} %get-tuple-element.63), channel_id=1, source_target_pairs={{0,16},{16,0},{1,17},{17,1},{2,18},{18,2},{3,19},{19,3},{4,20},{20... | collective-permute-start | bytes 589832 | tf_op jit(solution)/shard_map/ppermute | solution.py:31
  70.0 0.5 collective-permute-start.19
  70.5 1.5 %collective-permute-start.16 = (bf16[768,128]{1,0:T(8,128)(2,1)S(1)}, bf16[768,128]{1,0:T(8,128)(2,1)S(1)}, u32[]{:S(2)}, u32[]{:S(2)}) collective-permute-start(bf16[768,128]{1,0:T(8,128)(2,1)S(1)} %collective-permute-done.13.refs_1_.refs_11_), channel_id=1, source_target_pairs={{0,8},{4,12},{8,0},{12,4},{1,9},{5,13},{9,1},{13,5},{2,10},{6,14},... | collective-permute-start | bytes 589832 | tf_op jit(solution)/shard_map/ppermute | solution.py:27
  72.0 4.1 %collective-permute-done.23.refs_1_.refs_0_ = bf16[768,128]{1,0:T(8,128)(2,1)S(1)} collective-permute-done((bf16[768,128]{1,0:T(8,128)(2,1)S(1)}, bf16[768,128]{1,0:T(8,128)(2,1)S(1)}, u32[]{:S(2)}, u32[]{:S(2)}) %collective-permute-start.23) | collective-permute-done | bytes 196640 | tf_op jit(solution)/shard_map/ppermute | solution.py:31
  76.2 3.8 %collective-permute-done.19.refs_15_ = bf16[768,128]{1,0:T(8,128)(2,1)S(1)} collective-permute-done((bf16[768,128]{1,0:T(8,128)(2,1)S(1)}, bf16[768,128]{1,0:T(8,128)(2,1)S(1)}, u32[]{:S(2)}, u32[]{:S(2)}) %collective-permute-start.19) | collective-permute-done | bytes 196640 | tf_op jit(solution)/shard_map/ppermute | solution.py:31
  79.9 1.5 %collective-permute-start.20 = (bf16[768,128]{1,0:T(8,128)(2,1)S(1)}, bf16[768,128]{1,0:T(8,128)(2,1)S(1)}, u32[]{:S(2)}, u32[]{:S(2)}) collective-permute-start(bf16[768,128]{1,0:T(8,128)(2,1)S(1)} %collective-permute-done.19.refs_15_), channel_id=1, source_target_pairs={{0,8},{4,12},{8,0},{12,4},{1,9},{5,13},{9,1},{13,5},{2,10},{6,14},... | collective-permute-start | bytes 589832 | tf_op jit(solution)/shard_map/ppermute | solution.py:27
  81.5 2.7 %step1b.1 = (bf16[768,128]{1,0:T(8,128)(2,1)S(1)}, bf16[4,128,384]{2,1,0:T(8,128)(2,1)S(1)}) custom-call(f32[1,16]{1,0:T(1,128)S(1)} %copy-done.15, s32[4,1]{1,0:T(4,128)S(1)} %copy-done.13, f32[1,1536]{1,0:T(1,128)S(1)} %copy-done.8, f32[1,1536]{1,0:T(1,128)S(1)} %copy-done.9, f32[1,1536]{1,0:T(1,128)S(1)} %copy-done.11, s32[4,1,512]{2,1,0:T(1,128)S(1)} %copy-done.10, ...), custom_call_target="tpu_custom_call" | custom-call | flops 805306368 | bytes 1572864 | tf_op jit(solution)/shard_map/step1b/pallas_call | solution.py:493
  84.2 1.6 %collective-permute-start.25 = (bf16[768,128]{1,0:T(8,128)(2,1)S(1)}, bf16[768,128]{1,0:T(8,128)(2,1)S(1)}, u32[]{:S(2)}, u32[]{:S(2)}) collective-permute-start(bf16[768,128]{1,0:T(8,128)(2,1)S(1)} %get-tuple-element.64), channel_id=1, source_target_pairs={{0,16},{16,0},{1,17},{17,1},{2,18},{18,2},{3,19},{19,3},{4,20},{20... | collective-permute-start | bytes 589832 | tf_op jit(solution)/shard_map/ppermute | solution.py:31
  85.8 0.2 collective-permute-start.18
  86.0 0.4 collective-permute-done.20.refs_16_
  86.4 1.5 %collective-permute-start.24 = (bf16[768,128]{1,0:T(8,128)(2,1)S(1)}, bf16[768,128]{1,0:T(8,128)(2,1)S(1)}, u32[]{:S(2)}, u32[]{:S(2)}) collective-permute-start(bf16[768,128]{1,0:T(8,128)(2,1)S(1)} %collective-permute-done.23.refs_1_.refs_0_), channel_id=1, source_target_pairs={{0,8},{4,12},{8,0},{12,4},{1,9},{5,13},{9,1},{13,5},{2,10},{6,14},... | collective-permute-start | bytes 589832 | tf_op jit(solution)/shard_map/ppermute | solution.py:27
  87.9 3.7 %collective-permute-done.25.refs_2_ = bf16[768,128]{1,0:T(8,128)(2,1)S(1)} collective-permute-done((bf16[768,128]{1,0:T(8,128)(2,1)S(1)}, bf16[768,128]{1,0:T(8,128)(2,1)S(1)}, u32[]{:S(2)}, u32[]{:S(2)}) %collective-permute-start.25) | collective-permute-done | bytes 196640 | tf_op jit(solution)/shard_map/ppermute | solution.py:31
  91.6 0.5 collective-permute-start.26
  92.1 4.9 %step2ab.1.refs_2_.refs_0_ = bf16[4,128,384]{2,1,0:T(8,128)(2,1)S(1)} custom-call(f32[1,16]{1,0:T(1,128)S(1)} %copy-done.15, s32[4,1]{1,0:T(4,128)S(1)} %copy-done.13, f32[1,1536]{1,0:T(1,128)S(1)} %copy-done.8, f32[1,1536]{1,0:T(1,128)S(1)} %copy-done.9, f32[1,1536]{1,0:T(1,128)S(1)} %copy-done.11, s32[4,1,512]{2,1,0:T(1,128)S(1)} %copy-done.10, ...), custom_call_target="tpu_custom_call" | custom-call | flops 1610612736 | bytes 3145728 | tf_op jit(solution)/shard_map/step2ab/pallas_call | solution.py:493
  97.0 0.5 early.1
  97.5 0.6 collective-permute-done.26.refs_3_
  98.1 0.5 collective-permute-start.28
  98.6 0.5 collective-permute-start.30
  99.1 0.4 collective-permute-done.27.refs_13_
  99.6 1.3 %collective-permute-start.32 = (bf16[2,128,384]{2,1,0:T(8,128)(2,1)S(1)}, bf16[2,128,384]{2,1,0:T(8,128)(2,1)S(1)}, u32[]{:S(2)}, u32[]{:S(2)}) collective-permute-start(bf16[2,128,384]{2,1,0:T(8,128)(2,1)S(1)} %get-tuple-element.73), channel_id=1, source_target_pairs={{0,8},{4,12},{8,0},{12,4},{1,9},{5,13},{9,1},{13,5},{2,10},{6,14},... | collective-permute-start | bytes 589832 | tf_op jit(solution)/shard_map/ppermute | solution.py:27
  100.9 0.1 collective-permute-start.33
  101.1 4.7 %step3ab.1.refs_1_ = bf16[4,128,384]{2,1,0:T(8,128)(2,1)S(1)} custom-call(f32[1,16]{1,0:T(1,128)S(1)} %copy-done.15, s32[4,1]{1,0:T(4,128)S(1)} %copy-done.13, f32[1,1536]{1,0:T(1,128)S(1)} %copy-done.8, f32[1,1536]{1,0:T(1,128)S(1)} %copy-done.9, f32[1,1536]{1,0:T(1,128)S(1)} %copy-done.11, s32[4,1,512]{2,1,0:T(1,128)S(1)} %copy-done.10, ...), custom_call_target="tpu_custom_call" | custom-call | flops 1610612736 | bytes 3145728 | tf_op jit(solution)/shard_map/step3ab/pallas_call | solution.py:493
  105.8 1.5 %collective-permute-done.32.refs_8_ = bf16[2,128,384]{2,1,0:T(8,128)(2,1)S(1)} collective-permute-done((bf16[2,128,384]{2,1,0:T(8,128)(2,1)S(1)}, bf16[2,128,384]{2,1,0:T(8,128)(2,1)S(1)}, u32[]{:S(2)}, u32[]{:S(2)}) %collective-permute-start.32) | collective-permute-done | bytes 196640 | tf_op jit(solution)/shard_map/ppermute | solution.py:27
  107.3 1.2 %settle.1 = (bf16[128,384]{1,0:T(8,128)(2,1)S(1)}, bf16[128,384]{1,0:T(8,128)(2,1)S(1)}, bf16[128,384]{1,0:T(8,128)(2,1)S(1)}, bf16[128,384]{1,0:T(8,128)(2,1)S(...) custom-call(bf16[4,128,384]{2,1,0:T(8,128)(2,1)S(1)} %step2ab.1.refs, ...), custom_call_target="tpu_custom_call" | custom-call | tf_op jit(solution)/shard_map/settle/pallas_call | solution.py:493
  108.5 0.4 collective-permute-start.37
  108.9 1.3 %collective-permute-start.35 = (bf16[128,384]{1,0:T(8,128)(2,1)S(1)}, bf16[128,384]{1,0:T(8,128)(2,1)S(1)}, u32[]{:S(2)}, u32[]{:S(2)}) collective-permute-start(bf16[128,384]{1,0:T(8,128)(2,1)S(1)} %get-tuple-element.78), channel_id=1, source_target_pairs={{0,8},{4,12},{8,0},{12,4},{1,9},{5,13},{9,1},{13,5},{2,10},{6,14},... | collective-permute-start | bytes 294920 | tf_op jit(solution)/shard_map/ppermute | solution.py:27
  110.2 0.5 collective-permute-start.36
  110.8 2.2 %collective-permute-start.38 = (bf16[96,256]{1,0:T(8,128)(2,1)S(1)}, bf16[96,256]{1,0:T(8,128)(2,1)S(1)}, u32[]{:S(2)}, u32[]{:S(2)}) collective-permute-start(bf16[96,256]{1,0:T(8,128)(2,1)S(1)} %get-tuple-element.82), channel_id=1, source_target_pairs={{0,2},{1,3},{2,0},{3,1},{4,6},{5,7},{6,4},{7,5},{8,10},{9,11},{10,... | collective-permute-start | bytes 147464 | tf_op jit(solution)/shard_map/ppermute | solution.py:36
  112.9 1.5 %collective-permute-done.37.refs_7_ = bf16[96,256]{1,0:T(8,128)(2,1)S(1)} collective-permute-done((bf16[96,256]{1,0:T(8,128)(2,1)S(1)}, bf16[96,256]{1,0:T(8,128)(2,1)S(1)}, u32[]{:S(2)}, u32[]{:S(2)}) %collective-permute-start.37) | collective-permute-done | bytes 49184 | tf_op jit(solution)/shard_map/ppermute | solution.py:36
  114.5 0.1 collective-permute-start.39
  114.6 1.8 %collective-permute-done.38.refs_8_ = bf16[96,256]{1,0:T(8,128)(2,1)S(1)} collective-permute-done((bf16[96,256]{1,0:T(8,128)(2,1)S(1)}, bf16[96,256]{1,0:T(8,128)(2,1)S(1)}, u32[]{:S(2)}, u32[]{:S(2)}) %collective-permute-start.38) | collective-permute-done | bytes 49184 | tf_op jit(solution)/shard_map/ppermute | solution.py:36
  116.4 2.1 %collective-permute-done.39.refs_9_ = bf16[96,256]{1,0:T(8,128)(2,1)S(1)} collective-permute-done((bf16[96,256]{1,0:T(8,128)(2,1)S(1)}, bf16[96,256]{1,0:T(8,128)(2,1)S(1)}, u32[]{:S(2)}, u32[]{:S(2)}) %collective-permute-start.39) | collective-permute-done | bytes 49184 | tf_op jit(solution)/shard_map/ppermute | solution.py:36
  118.6 1.5 %finish.1 = (bf16[3,128,1536]{2,1,0:T(8,128)(2,1)}, f32[96,256]{1,0:T(8,128)}) custom-call(bf16[3,128,1536]{2,1,0:T(8,128)(2,1)} %get-tuple-element.74.refs_0_, bf16[2,128,384]{2,1,0:T(8,128)(2,1)S(1)} %collective-permute-done.33.refs_1_, bf16[128,384]{1,0:T(8,128)(2,1)S(1)} %get-tuple-element.76.refs_2_, ...), custom_call_target="tpu_custom_call", output_to_operand_aliasing={{0}: (0, {})} | custom-call | tf_op jit(solution)/shard_map/finish/pallas_call | solution.py:493
  (75 shorter events, 0.4 us)
Async XLA Ops:
  0.6 14.6 %copy-start = (bf16[1,3,1,128,1536]{4,3,2,1,0:T(8,128)(2,1)S(1)}, bf16[1,3,1,128,1536]{4,3,2,1,0:T(8,128)(2,1)}, u32[]{:S(2)}) copy-start(bf16[1,3,1,128,1536]{4,3,2,1,0:T(8,128)(2,1)} %incoming.3) | copy-start | bytes 3538948
  0.6 14.6 %copy-start.16 = (s32[4,1,128]{2,1,0:T(1,128)S(1)}, s32[4,1,128]{2,1,0:T(1,128)}, u32[]{:S(2)}) copy-start(s32[4,1,128]{2,1,0:T(1,128)} %contacts.1) | copy-start | bytes 6148
  2.1 1.5 %collective-permute-start = (bf16[2,96,384]{2,1,0:T(8,128)(2,1)S(1)}, bf16[2,96,384]{2,1,0:T(8,128)(2,1)S(1)}, u32[]{:S(2)}, u32[]{:S(2)}) collective-permute-start(bf16[2,96,384]{2,1,0:T(8,128)(2,1)S(1)} %get-tuple-element.45), channel_id=1, source_target_pairs={{0,4},{4,0},{8,12},{12,8},{1,5},{5,1},{9,13},{13,9},{2,6},{6,2},{1... | collective-permute-start | bytes 442376 | tf_op jit(solution)/shard_map/ppermute | solution.py:27
  3.7 11.5 %collective-permute-start.1 = (bf16[2,2,96,384]{3,2,1,0:T(8,128)(2,1)S(1)}, bf16[2,2,96,384]{3,2,1,0:T(8,128)(2,1)S(1)}, u32[]{:S(2)}, u32[]{:S(2)}) collective-permute-start(bf16[2,2,96,384]{3,2,1,0:T(8,128)(2,1)S(1)} %near.1), channel_id=1, source_target_pairs={{0,1},{1,3},{3,2},{2,0},{4,5},{5,7},{7,6},{6,4},{8,9},{9,11},{11,1... | collective-permute-start | bytes 884744 | tf_op jit(solution)/shard_map/ppermute | solution.py:46
  6.7 0.7 copy-start.1
  7.4 6.7 %collective-permute-start.2 = (bf16[2,96,384]{2,1,0:T(8,128)(2,1)S(1)}, bf16[2,96,384]{2,1,0:T(8,128)(2,1)S(1)}, u32[]{:S(2)}, u32[]{:S(2)}) collective-permute-start(bf16[2,96,384]{2,1,0:T(8,128)(2,1)S(1)} %get-tuple-element.46), channel_id=1, source_target_pairs={{0,8},{4,12},{8,0},{12,4},{1,9},{5,13},{9,1},{13,5},{2,10},{6,14},... | collective-permute-start | bytes 442376 | tf_op jit(solution)/shard_map/ppermute | solution.py:27
  8.9 6.3 %collective-permute-start.3 = (bf16[2,96,384]{2,1,0:T(8,128)(2,1)S(1)}, bf16[2,96,384]{2,1,0:T(8,128)(2,1)S(1)}, u32[]{:S(2)}, u32[]{:S(2)}) collective-permute-start(bf16[2,96,384]{2,1,0:T(8,128)(2,1)S(1)} %get-tuple-element.47), channel_id=1, source_target_pairs={{0,12},{4,8},{8,4},{12,0},{1,13},{5,9},{9,5},{13,1},{2,14},{6,10},... | collective-permute-start | bytes 442376 | tf_op jit(solution)/shard_map/ppermute | solution.py:27
  15.3 28.0 %collective-permute-start.4 = (bf16[272,1536]{1,0:T(8,128)(2,1)S(1)}, bf16[272,1536]{1,0:T(8,128)(2,1)S(1)}, u32[]{:S(2)}, u32[]{:S(2)}) collective-permute-start(bf16[272,1536]{1,0:T(8,128)(2,1)S(1)} %first.1.refs_0_), channel_id=1, source_target_pairs={{0,8},{4,12},{8,0},{12,4},{1,9},{5,13},{9,1},{13,5},{2,10},{6,14},... | collective-permute-start | bytes 2506760 | tf_op jit(solution)/shard_map/ppermute | solution.py:27
  16.7 10.5 %collective-permute-start.5 = (bf16[2,2,96,384]{3,2,1,0:T(8,128)(2,1)S(1)}, bf16[2,2,96,384]{3,2,1,0:T(8,128)(2,1)S(1)}, u32[]{:S(2)}, u32[]{:S(2)}) collective-permute-start(bf16[2,2,96,384]{3,2,1,0:T(8,128)(2,1)S(1)} %far.1), channel_id=1, source_target_pairs={{0,1},{1,3},{3,2},{2,0},{4,5},{5,7},{7,6},{6,4},{8,9},{9,11},{11,1... | collective-permute-start | bytes 884744 | tf_op jit(solution)/shard_map/ppermute | solution.py:46
  27.2 16.1 %copy-start.6 = (bf16[4,96,384]{2,1,0:T(8,128)(2,1)}, bf16[4,96,384]{2,1,0:T(8,128)(2,1)S(1)}, u32[]{:S(2)}) copy-start(bf16[4,96,384]{2,1,0:T(8,128)(2,1)S(1)} %part0.1.chunk) | copy-start | bytes 884740
  27.3 11.0 %collective-permute-start.6 = (bf16[4,96,384]{2,1,0:T(8,128)(2,1)S(1)}, bf16[4,96,384]{2,1,0:T(8,128)(2,1)}, u32[]{:S(2)}, u32[]{:S(2)}) collective-permute-start(bf16[4,96,384]{2,1,0:T(8,128)(2,1)S(1)} %part0.1.chunk), channel_id=1, source_target_pairs={{0,1},{1,3},{3,2},{2,0},{4,5},{5,7},{7,6},{6,4},{8,9},{9,11},{11,1... | collective-permute-start | bytes 884744 | tf_op jit(solution)/shard_map/ppermute | solution.py:46
  29.0 14.4 %copy-start.4 = (bf16[4,96,384]{2,1,0:T(8,128)(2,1)}, bf16[4,96,384]{2,1,0:T(8,128)(2,1)S(1)}, u32[]{:S(2)}) copy-start(bf16[4,96,384]{2,1,0:T(8,128)(2,1)S(1)} %part1.1.chunk) | copy-start | bytes 884740
  29.0 14.3 %copy-start.12 = (bf16[1,3,1,128,256]{4,3,2,1,0:T(8,128)(2,1)S(1)}, bf16[1,3,1,128,256]{4,3,2,1,0:T(8,128)(2,1)}, u32[]{:S(2)}) copy-start(bf16[1,3,1,128,256]{4,3,2,1,0:T(8,128)(2,1)} %cotangent.1) | copy-start | bytes 589828
  29.1 14.3 %collective-permute-start.7 = (bf16[4,96,384]{2,1,0:T(8,128)(2,1)S(1)}, bf16[4,96,384]{2,1,0:T(8,128)(2,1)}, u32[]{:S(2)}, u32[]{:S(2)}) collective-permute-start(bf16[4,96,384]{2,1,0:T(8,128)(2,1)S(1)} %part1.1.chunk), channel_id=1, source_target_pairs={{0,1},{1,3},{3,2},{2,0},{4,5},{5,7},{7,6},{6,4},{8,9},{9,11},{11,1... | collective-permute-start | bytes 884744 | tf_op jit(solution)/shard_map/ppermute | solution.py:46
  30.7 19.1 %collective-permute-start.9 = (bf16[272,1536]{1,0:T(8,128)(2,1)S(1)}, bf16[272,1536]{1,0:T(8,128)(2,1)}, u32[]{:S(2)}, u32[]{:S(2)}) collective-permute-start(bf16[272,1536]{1,0:T(8,128)(2,1)S(1)} %first.1.refs_0_), channel_id=1, source_target_pairs={{0,4},{4,0},{8,12},{12,8},{1,5},{5,1},{9,13},{13,9},{2,6},{6,2},{1... | collective-permute-start | bytes 2506760 | tf_op jit(solution)/shard_map/ppermute | solution.py:27
  43.4 6.6 %collective-permute-start.10 = (bf16[272,1536]{1,0:T(8,128)(2,1)S(1)}, bf16[272,1536]{1,0:T(8,128)(2,1)}, u32[]{:S(2)}, u32[]{:S(2)}) collective-permute-start(bf16[272,1536]{1,0:T(8,128)(2,1)S(1)} %tie.5.dep.refs_1_), channel_id=1, source_target_pairs={{0,4},{4,0},{8,12},{12,8},{1,5},{5,1},{9,13},{13,9},{2,6},{6,2},{1... | collective-permute-start | bytes 2506760 | tf_op jit(solution)/shard_map/ppermute | solution.py:27
  43.4 6.5 %copy-start.8 = (f32[1,1536]{1,0:T(1,128)S(1)}, f32[1,1536]{1,0:T(1,128)}, u32[]{:S(2)}) copy-start(f32[1,1536]{1,0:T(1,128)} %refs_2_.11) | copy-start | bytes 18436
  43.4 6.5 %copy-start.9 = (f32[1,1536]{1,0:T(1,128)S(1)}, f32[1,1536]{1,0:T(1,128)}, u32[]{:S(2)}) copy-start(f32[1,1536]{1,0:T(1,128)} %refs_3_.11) | copy-start | bytes 18436
  43.5 24.8 %collective-permute-start.8 = (bf16[256,1536]{1,0:T(8,128)(2,1)S(1)}, bf16[256,1536]{1,0:T(8,128)(2,1)S(1)}, u32[]{:S(2)}, u32[]{:S(2)}) collective-permute-start(bf16[256,1536]{1,0:T(8,128)(2,1)S(1)} %second.1.refs_6_.refs_3_.refs_2_), channel_id=1, source_target_pairs={{0,8},{4,12},{8,0},{12,4},{1,9},{5,13},{9,1},{13,5},{2,10},{6,14},... | collective-permute-start | bytes 2359304 | tf_op jit(solution)/shard_map/ppermute | solution.py:27
  44.0 11.1 %collective-permute-start.12 = (bf16[4,96,384]{2,1,0:T(8,128)(2,1)}, bf16[4,96,384]{2,1,0:T(8,128)(2,1)}, u32[]{:S(2)}, u32[]{:S(2)}) collective-permute-start(bf16[4,96,384]{2,1,0:T(8,128)(2,1)} %collective-permute-done.6.refs_1_.refs_9_), channel_id=1, source_target_pairs={{0,1},{1,3},{3,2},{2,0},{4,5},{5,7},{7,6},{6,4},{8,9},{9,11},{11,1... | collective-permute-start | bytes 884744 | tf_op jit(solution)/shard_map/ppermute | solution.py:46
  44.8 18.1 %collective-permute-start.11 = (bf16[4,96,384]{2,1,0:T(8,128)(2,1)}, bf16[4,96,384]{2,1,0:T(8,128)(2,1)}, u32[]{:S(2)}, u32[]{:S(2)}) collective-permute-start(bf16[4,96,384]{2,1,0:T(8,128)(2,1)} %collective-permute-done.7.refs_2_.refs_9_), channel_id=1, source_target_pairs={{0,1},{1,3},{3,2},{2,0},{4,5},{5,7},{7,6},{6,4},{8,9},{9,11},{11,1... | collective-permute-start | bytes 884744 | tf_op jit(solution)/shard_map/ppermute | solution.py:46
  47.9 1.0 copy-start.2
  48.8 1.0 copy-start.7
  49.8 0.7 copy-start.13
  49.8 0.8 copy-start.14
  49.9 5.3 %copy-start.10 = (s32[4,1,512]{2,1,0:T(1,128)S(1)}, s32[4,1,512]{2,1,0:T(1,128)}, u32[]{:S(2)}) copy-start(s32[4,1,512]{2,1,0:T(1,128)} %refs_5_.11) | copy-start | bytes 24580
  49.9 5.3 %copy-start.11 = (f32[1,1536]{1,0:T(1,128)S(1)}, f32[1,1536]{1,0:T(1,128)}, u32[]{:S(2)}) copy-start(f32[1,1536]{1,0:T(1,128)} %refs_4_.11) | copy-start | bytes 18436
  49.9 5.3 %copy-start.15 = (f32[1,16]{1,0:T(1,128)S(1)}, f32[1,16]{1,0:T(1,128)}, u32[]{:S(2)}) copy-start(f32[1,16]{1,0:T(1,128)} %refs_0_.11) | copy-start | bytes 196
  55.2 4.9 %copy-start.3 = (bf16[2,2,96,384]{3,2,1,0:T(8,128)(2,1)S(1)}, bf16[2,2,96,384]{3,2,1,0:T(8,128)(2,1)}, u32[]{:S(2)}) copy-start(bf16[2,2,96,384]{3,2,1,0:T(8,128)(2,1)} %copy-done.1) | copy-start | bytes 884740
  55.2 4.9 %copy-start.5 = (bf16[4,96,384]{2,1,0:T(8,128)(2,1)S(1)}, bf16[4,96,384]{2,1,0:T(8,128)(2,1)}, u32[]{:S(2)}) copy-start(bf16[4,96,384]{2,1,0:T(8,128)(2,1)} %copy-done.4) | copy-start | bytes 884740
  58.5 6.5 %collective-permute-start.13 = (bf16[768,128]{1,0:T(8,128)(2,1)S(1)}, bf16[768,128]{1,0:T(8,128)(2,1)S(1)}, u32[]{:S(2)}, u32[]{:S(2)}) collective-permute-start(bf16[768,128]{1,0:T(8,128)(2,1)S(1)} %get-tuple-element.51), channel_id=1, source_target_pairs={{0,16},{16,0},{1,17},{17,1},{2,18},{18,2},{3,19},{19,3},{4,20},{20... | collective-permute-start | bytes 589832 | tf_op jit(solution)/shard_map/ppermute | solution.py:31
  60.1 24.1 %collective-permute-start.14 = (bf16[256,1536]{1,0:T(8,128)(2,1)S(1)}, bf16[256,1536]{1,0:T(8,128)(2,1)S(1)}, u32[]{:S(2)}, u32[]{:S(2)}) collective-permute-start(bf16[256,1536]{1,0:T(8,128)(2,1)S(1)} %second.1.refs_6_.refs_3_.refs_2_), channel_id=1, source_target_pairs={{0,4},{4,0},{8,12},{12,8},{1,5},{5,1},{9,13},{13,9},{2,6},{6,2},{1... | collective-permute-start | bytes 2359304 | tf_op jit(solution)/shard_map/ppermute | solution.py:27
  68.3 23.8 %collective-permute-start.15 = (bf16[256,1536]{1,0:T(8,128)(2,1)S(1)}, bf16[256,1536]{1,0:T(8,128)(2,1)S(1)}, u32[]{:S(2)}, u32[]{:S(2)}) collective-permute-start(bf16[256,1536]{1,0:T(8,128)(2,1)S(1)} %tie.7.refs_7_.refs_4_.refs_3_), channel_id=1, source_target_pairs={{0,4},{4,0},{8,12},{12,8},{1,5},{5,1},{9,13},{13,9},{2,6},{6,2},{1... | collective-permute-start | bytes 2359304 | tf_op jit(solution)/shard_map/ppermute | solution.py:27
  68.4 7.8 %collective-permute-start.23 = (bf16[768,128]{1,0:T(8,128)(2,1)S(1)}, bf16[768,128]{1,0:T(8,128)(2,1)S(1)}, u32[]{:S(2)}, u32[]{:S(2)}) collective-permute-start(bf16[768,128]{1,0:T(8,128)(2,1)S(1)} %get-tuple-element.63), channel_id=1, source_target_pairs={{0,16},{16,0},{1,17},{17,1},{2,18},{18,2},{3,19},{19,3},{4,20},{20... | collective-permute-start | bytes 589832 | tf_op jit(solution)/shard_map/ppermute | solution.py:31
  70.0 9.9 %collective-permute-start.19 = (bf16[768,128]{1,0:T(8,128)(2,1)S(1)}, bf16[768,128]{1,0:T(8,128)(2,1)S(1)}, u32[]{:S(2)}, u32[]{:S(2)}) collective-permute-start(bf16[768,128]{1,0:T(8,128)(2,1)S(1)} %get-tuple-element.60), channel_id=1, source_target_pairs={{0,16},{16,0},{1,17},{17,1},{2,18},{18,2},{3,19},{19,3},{4,20},{20... | collective-permute-start | bytes 589832 | tf_op jit(solution)/shard_map/ppermute | solution.py:31
  70.5 11.0 %collective-permute-start.16 = (bf16[768,128]{1,0:T(8,128)(2,1)S(1)}, bf16[768,128]{1,0:T(8,128)(2,1)S(1)}, u32[]{:S(2)}, u32[]{:S(2)}) collective-permute-start(bf16[768,128]{1,0:T(8,128)(2,1)S(1)} %collective-permute-done.13.refs_1_.refs_11_), channel_id=1, source_target_pairs={{0,8},{4,12},{8,0},{12,4},{1,9},{5,13},{9,1},{13,5},{2,10},{6,14},... | collective-permute-start | bytes 589832 | tf_op jit(solution)/shard_map/ppermute | solution.py:27
  76.2 9.6 %collective-permute-start.17 = (bf16[768,128]{1,0:T(8,128)(2,1)S(1)}, bf16[768,128]{1,0:T(8,128)(2,1)S(1)}, u32[]{:S(2)}, u32[]{:S(2)}) collective-permute-start(bf16[768,128]{1,0:T(8,128)(2,1)S(1)} %collective-permute-done.13.refs_1_.refs_11_), channel_id=1, source_target_pairs={{0,4},{4,0},{8,12},{12,8},{1,5},{5,1},{9,13},{13,9},{2,6},{6,2},{1... | collective-permute-start | bytes 589832 | tf_op jit(solution)/shard_map/ppermute | solution.py:27
  79.9 6.5 %collective-permute-start.20 = (bf16[768,128]{1,0:T(8,128)(2,1)S(1)}, bf16[768,128]{1,0:T(8,128)(2,1)S(1)}, u32[]{:S(2)}, u32[]{:S(2)}) collective-permute-start(bf16[768,128]{1,0:T(8,128)(2,1)S(1)} %collective-permute-done.19.refs_15_), channel_id=1, source_target_pairs={{0,8},{4,12},{8,0},{12,4},{1,9},{5,13},{9,1},{13,5},{2,10},{6,14},... | collective-permute-start | bytes 589832 | tf_op jit(solution)/shard_map/ppermute | solution.py:27
  81.5 4.9 %collective-permute-start.21 = (bf16[768,128]{1,0:T(8,128)(2,1)S(1)}, bf16[768,128]{1,0:T(8,128)(2,1)S(1)}, u32[]{:S(2)}, u32[]{:S(2)}) collective-permute-start(bf16[768,128]{1,0:T(8,128)(2,1)S(1)} %collective-permute-done.19.refs_15_), channel_id=1, source_target_pairs={{0,4},{4,0},{8,12},{12,8},{1,5},{5,1},{9,13},{13,9},{2,6},{6,2},{1... | collective-permute-start | bytes 589832 | tf_op jit(solution)/shard_map/ppermute | solution.py:27
  84.2 7.4 %collective-permute-start.25 = (bf16[768,128]{1,0:T(8,128)(2,1)S(1)}, bf16[768,128]{1,0:T(8,128)(2,1)S(1)}, u32[]{:S(2)}, u32[]{:S(2)}) collective-permute-start(bf16[768,128]{1,0:T(8,128)(2,1)S(1)} %get-tuple-element.64), channel_id=1, source_target_pairs={{0,16},{16,0},{1,17},{17,1},{2,18},{18,2},{3,19},{19,3},{4,20},{20... | collective-permute-start | bytes 589832 | tf_op jit(solution)/shard_map/ppermute | solution.py:31
  85.8 6.3 %collective-permute-start.18 = (bf16[768,128]{1,0:T(8,128)(2,1)S(1)}, bf16[768,128]{1,0:T(8,128)(2,1)S(1)}, u32[]{:S(2)}, u32[]{:S(2)}) collective-permute-start(bf16[768,128]{1,0:T(8,128)(2,1)S(1)} %collective-permute-done.16.refs_12_.refs_2_), channel_id=1, source_target_pairs={{0,4},{4,0},{8,12},{12,8},{1,5},{5,1},{9,13},{13,9},{2,6},{6,2},{1... | collective-permute-start | bytes 589832 | tf_op jit(solution)/shard_map/ppermute | solution.py:27
  86.4 5.7 %collective-permute-start.22 = (bf16[768,128]{1,0:T(8,128)(2,1)S(1)}, bf16[768,128]{1,0:T(8,128)(2,1)S(1)}, u32[]{:S(2)}, u32[]{:S(2)}) collective-permute-start(bf16[768,128]{1,0:T(8,128)(2,1)S(1)} %collective-permute-done.20.refs_16_), channel_id=1, source_target_pairs={{0,4},{4,0},{8,12},{12,8},{1,5},{5,1},{9,13},{13,9},{2,6},{6,2},{1... | collective-permute-start | bytes 589832 | tf_op jit(solution)/shard_map/ppermute | solution.py:27
  86.4 11.1 %collective-permute-start.24 = (bf16[768,128]{1,0:T(8,128)(2,1)S(1)}, bf16[768,128]{1,0:T(8,128)(2,1)S(1)}, u32[]{:S(2)}, u32[]{:S(2)}) collective-permute-start(bf16[768,128]{1,0:T(8,128)(2,1)S(1)} %collective-permute-done.23.refs_1_.refs_0_), channel_id=1, source_target_pairs={{0,8},{4,12},{8,0},{12,4},{1,9},{5,13},{9,1},{13,5},{2,10},{6,14},... | collective-permute-start | bytes 589832 | tf_op jit(solution)/shard_map/ppermute | solution.py:27
  91.6 6.5 %collective-permute-start.26 = (bf16[768,128]{1,0:T(8,128)(2,1)S(1)}, bf16[768,128]{1,0:T(8,128)(2,1)S(1)}, u32[]{:S(2)}, u32[]{:S(2)}) collective-permute-start(bf16[768,128]{1,0:T(8,128)(2,1)S(1)} %collective-permute-done.25.refs_2_), channel_id=1, source_target_pairs={{0,8},{4,12},{8,0},{12,4},{1,9},{5,13},{9,1},{13,5},{2,10},{6,14},... | collective-permute-start | bytes 589832 | tf_op jit(solution)/shard_map/ppermute | solution.py:27
  98.1 1.4 %collective-permute-start.27 = (bf16[768,128]{1,0:T(8,128)(2,1)S(1)}, bf16[768,128]{1,0:T(8,128)(2,1)S(1)}, u32[]{:S(2)}, u32[]{:S(2)}) collective-permute-start(bf16[768,128]{1,0:T(8,128)(2,1)S(1)} %get-tuple-element.67.refs_11_), channel_id=1, source_target_pairs={{0,4},{4,0},{8,12},{12,8},{1,5},{5,1},{9,13},{13,9},{2,6},{6,2},{1... | collective-permute-start | bytes 589832 | tf_op jit(solution)/shard_map/ppermute | solution.py:27
  98.1 2.8 %collective-permute-start.28 = (bf16[768,128]{1,0:T(8,128)(2,1)S(1)}, bf16[768,128]{1,0:T(8,128)(2,1)S(1)}, u32[]{:S(2)}, u32[]{:S(2)}) collective-permute-start(bf16[768,128]{1,0:T(8,128)(2,1)S(1)} %get-tuple-element.68.refs_12_), channel_id=1, source_target_pairs={{0,4},{4,0},{8,12},{12,8},{1,5},{5,1},{9,13},{13,9},{2,6},{6,2},{1... | collective-permute-start | bytes 589832 | tf_op jit(solution)/shard_map/ppermute | solution.py:27
  98.6 2.4 %collective-permute-start.29 = (bf16[768,128]{1,0:T(8,128)(2,1)S(1)}, bf16[768,128]{1,0:T(8,128)(2,1)S(1)}, u32[]{:S(2)}, u32[]{:S(2)}) collective-permute-start(bf16[768,128]{1,0:T(8,128)(2,1)S(1)} %get-tuple-element.69.refs_15_), channel_id=1, source_target_pairs={{0,4},{4,0},{8,12},{12,8},{1,5},{5,1},{9,13},{13,9},{2,6},{6,2},{1... | collective-permute-start | bytes 589832 | tf_op jit(solution)/shard_map/ppermute | solution.py:27
  98.6 2.4 %collective-permute-start.30 = (bf16[768,128]{1,0:T(8,128)(2,1)S(1)}, bf16[768,128]{1,0:T(8,128)(2,1)S(1)}, u32[]{:S(2)}, u32[]{:S(2)}) collective-permute-start(bf16[768,128]{1,0:T(8,128)(2,1)S(1)} %get-tuple-element.70.refs_16_), channel_id=1, source_target_pairs={{0,4},{4,0},{8,12},{12,8},{1,5},{5,1},{9,13},{13,9},{2,6},{6,2},{1... | collective-permute-start | bytes 589832 | tf_op jit(solution)/shard_map/ppermute | solution.py:27
  99.1 6.6 %collective-permute-start.31 = (bf16[2,128,384]{2,1,0:T(8,128)(2,1)S(1)}, bf16[2,128,384]{2,1,0:T(8,128)(2,1)S(1)}, u32[]{:S(2)}, u32[]{:S(2)}) collective-permute-start(bf16[2,128,384]{2,1,0:T(8,128)(2,1)S(1)} %get-tuple-element.72), channel_id=1, source_target_pairs={{0,4},{4,0},{8,12},{12,8},{1,5},{5,1},{9,13},{13,9},{2,6},{6,2},{1... | collective-permute-start | bytes 589832 | tf_op jit(solution)/shard_map/ppermute | solution.py:27
  99.6 7.7 %collective-permute-start.32 = (bf16[2,128,384]{2,1,0:T(8,128)(2,1)S(1)}, bf16[2,128,384]{2,1,0:T(8,128)(2,1)S(1)}, u32[]{:S(2)}, u32[]{:S(2)}) collective-permute-start(bf16[2,128,384]{2,1,0:T(8,128)(2,1)S(1)} %get-tuple-element.73), channel_id=1, source_target_pairs={{0,8},{4,12},{8,0},{12,4},{1,9},{5,13},{9,1},{13,5},{2,10},{6,14},... | collective-permute-start | bytes 589832 | tf_op jit(solution)/shard_map/ppermute | solution.py:27
  100.9 9.8 %collective-permute-start.33 = (bf16[2,128,384]{2,1,0:T(8,128)(2,1)S(1)}, bf16[2,128,384]{2,1,0:T(8,128)(2,1)S(1)}, u32[]{:S(2)}, u32[]{:S(2)}) collective-permute-start(bf16[2,128,384]{2,1,0:T(8,128)(2,1)S(1)} %get-tuple-element.75), channel_id=1, source_target_pairs={{0,12},{4,8},{8,4},{12,0},{1,13},{5,9},{9,5},{13,1},{2,14},{6,10},... | collective-permute-start | bytes 589832 | tf_op jit(solution)/shard_map/ppermute | solution.py:27
  108.5 5.9 %collective-permute-start.37 = (bf16[96,256]{1,0:T(8,128)(2,1)S(1)}, bf16[96,256]{1,0:T(8,128)(2,1)S(1)}, u32[]{:S(2)}, u32[]{:S(2)}) collective-permute-start(bf16[96,256]{1,0:T(8,128)(2,1)S(1)} %get-tuple-element.81), channel_id=1, source_target_pairs={{0,1},{1,2},{2,3},{3,0},{4,5},{5,6},{6,7},{7,4},{8,9},{9,10},{10,1... | collective-permute-start | bytes 147464 | tf_op jit(solution)/shard_map/ppermute | solution.py:36
  108.9 9.7 %collective-permute-start.34 = (bf16[128,384]{1,0:T(8,128)(2,1)S(1)}, bf16[128,384]{1,0:T(8,128)(2,1)S(1)}, u32[]{:S(2)}, u32[]{:S(2)}) collective-permute-start(bf16[128,384]{1,0:T(8,128)(2,1)S(1)} %get-tuple-element.77), channel_id=1, source_target_pairs={{0,4},{4,0},{8,12},{12,8},{1,5},{5,1},{9,13},{13,9},{2,6},{6,2},{1... | collective-permute-start | bytes 294920 | tf_op jit(solution)/shard_map/ppermute | solution.py:27
  108.9 9.7 %collective-permute-start.35 = (bf16[128,384]{1,0:T(8,128)(2,1)S(1)}, bf16[128,384]{1,0:T(8,128)(2,1)S(1)}, u32[]{:S(2)}, u32[]{:S(2)}) collective-permute-start(bf16[128,384]{1,0:T(8,128)(2,1)S(1)} %get-tuple-element.78), channel_id=1, source_target_pairs={{0,8},{4,12},{8,0},{12,4},{1,9},{5,13},{9,1},{13,5},{2,10},{6,14},... | collective-permute-start | bytes 294920 | tf_op jit(solution)/shard_map/ppermute | solution.py:27
  110.2 8.3 %collective-permute-start.36 = (bf16[128,384]{1,0:T(8,128)(2,1)S(1)}, bf16[128,384]{1,0:T(8,128)(2,1)S(1)}, u32[]{:S(2)}, u32[]{:S(2)}) collective-permute-start(bf16[128,384]{1,0:T(8,128)(2,1)S(1)} %get-tuple-element.79), channel_id=1, source_target_pairs={{0,12},{4,8},{8,4},{12,0},{1,13},{5,9},{9,5},{13,1},{2,14},{6,10},... | collective-permute-start | bytes 294920 | tf_op jit(solution)/shard_map/ppermute | solution.py:27
  110.8 5.7 %collective-permute-start.38 = (bf16[96,256]{1,0:T(8,128)(2,1)S(1)}, bf16[96,256]{1,0:T(8,128)(2,1)S(1)}, u32[]{:S(2)}, u32[]{:S(2)}) collective-permute-start(bf16[96,256]{1,0:T(8,128)(2,1)S(1)} %get-tuple-element.82), channel_id=1, source_target_pairs={{0,2},{1,3},{2,0},{3,1},{4,6},{5,7},{6,4},{7,5},{8,10},{9,11},{10,... | collective-permute-start | bytes 147464 | tf_op jit(solution)/shard_map/ppermute | solution.py:36
  114.5 4.1 %collective-permute-start.39 = (bf16[96,256]{1,0:T(8,128)(2,1)S(1)}, bf16[96,256]{1,0:T(8,128)(2,1)S(1)}, u32[]{:S(2)}, u32[]{:S(2)}) collective-permute-start(bf16[96,256]{1,0:T(8,128)(2,1)S(1)} %get-tuple-element.83), channel_id=1, source_target_pairs={{0,3},{1,0},{2,1},{3,2},{4,7},{5,4},{6,5},{7,6},{8,11},{9,8},{10,9... | collective-permute-start | bytes 147464 | tf_op jit(solution)/shard_map/ppermute | solution.py:36

commit v14 on v13

--- a/solution.py
+++ b/solution.py
@@ -144,7 +144,7 @@
 
 def modulation(step, turns, times, gain, freq):
     _, batch = turn_and_batch(step, turns)
-    return gain[...] * (1.0 + 0.5 * jnp.sin(times[batch, 0].astype(jnp.float32) * freq[...]))
+    return gain[...] * (1.0 + 0.5 * jnp.sin(times[0, batch].astype(jnp.float32) * freq[...]))
 
 
 def norm_kernel(turns, pieces, times, table, gain, freq, *refs):
@@ -211,6 +211,15 @@
     return jnp.concatenate([left[:frames], jnp.concatenate(middle, axis=1), right[:frames]], axis=1)
 
 
+def second_pair_kernel(dep, mine, across, out):
+    out[0] = mine[...]
+    out[1] = across[...]
+
+
+def opened(pieces):
+    return list(pieces[:2]) + [pieces[2].at[0], pieces[2].at[1]]
+
+
 def step_kernel(cfg, *refs):
     step, has_relay, parts = cfg["step"], cfg["has_relay"], cfg["parts"]
     pieces, hops, head, turns = cfg["pieces"], cfg["hops"], cfg["head"], cfg["turns"]
@@ -223,7 +232,7 @@
 
     bias, times, gain, freq, gate, flags = take(6)
     if has_relay:
-        second, embed, relay = take(pieces), take(1)[0], take(2 * pieces)
+        second, embed, relay = opened(take(3)), take(1)[0], take(2 * pieces)
     else:
         scaled, scales, own_hidden = take(3)
     chunks = take(2) if step == 0 else None
@@ -373,8 +382,8 @@
 
 
 def early_kernel(turns, pieces, halves, feats, *refs):
-    outs, second = refs[: turns * halves], refs[turns * halves : turns * halves + pieces]
-    sends, grad = refs[turns * halves + pieces : -1], refs[-1]
+    outs, second = refs[: turns * halves], opened(refs[turns * halves : turns * halves + 3])
+    sends, grad = refs[turns * halves + 3 : -1], refs[-1]
     section = lax.axis_index("pipe")
     offsets = offsets_of(pieces)
     part = pieces // halves
@@ -401,7 +410,7 @@
         taken, refs[:count] = refs[:count], []
         return taken
 
-    before, now, second, early = take(halves), take(halves), take(pieces), take(pieces - 1)
+    before, now, second, early = take(halves), take(halves), opened(take(3)), take(pieces - 1)
     early_grad = take(1)[0]
     late, own_grad, grads = take(pieces), take(1)[0], take(hops - 1)
     section_out = take(1)[0]
@@ -503,6 +512,8 @@
             **options,
         )(*operands)
 
+    timesteps = timesteps.reshape(1, timesteps.shape[0])
+
     def pin(value, space=pltpu.VMEM):
         return pltpu.with_memory_space_constraint(value, space)
 
@@ -606,7 +617,7 @@
         [across, incoming, head_cotangent],
         out_specs=vmem,
     )
-    second = [mine, swap(mine, 2), swap(mine, 1)]
+    second = [mine, swap(mine, 2)]
 
     common = [key_bias, timesteps, norm_gain, time_freq, attn_gate, keyframes]
 
@@ -666,18 +677,25 @@
             if step == 0:
                 out_shape += [pltpu.VMEM((width, cols), kind)]
             if part:
-                left = lefts[step]
-                if step == 1:
-                    (left,) = tie([left], [relays[1][0][0], relays[0][0][1]])
-                large += [left]
+                large += [lefts[step]]
             results = run_step(step, (part,), large, out_shape, aliases)
             if step == 0:
                 weights[part] = results[2]
             (outputs if part else lefts).append(results[1])
             piece = handed_over(results[0])
-            relays[step].append((piece, swap(piece, 2)))
-    (second[1],) = tie([second[1]], [outputs[0]])
-    second.append(swap(second[1], 1))
+            relays[step].append([piece, None if part and not step else swap(piece, 2)])
+    (piece,) = tie([relays[0][1][0]], [outputs[1]])
+    relays[0][1] = [piece, swap(piece, 2)]
+    beside = call(
+        second_pair_kernel,
+        "beside",
+        pltpu.VMEM((2,) + second[0].shape, kind),
+        [anywhere, vmem, vmem],
+        [outputs[0]] + second,
+        limit=8,
+        out_specs=vmem,
+    )
+    second = [second[0], second[1], swap(beside, 1)]
 
     def complete(crossing):
         return [
@@ -693,7 +711,7 @@
         functools.partial(early_kernel, turns, seq_count, 1, feats),
         "early",
         [shape((turns - 1, rows, cols), kind)] * seq_count + [shape((cols, feats), jnp.float32)],
-        [vmem] * (turns + seq_count),
+        [vmem] * (turns + len(second)),
         outputs + second,
         limit=8,
         out_specs=[vmem] * (seq_count + 1),

time: 121 us -> 115 us (0.950)
  local copies, waits for them, and re-layouts: 4.68 us -> 0.06 us
  Pallas kernels: 31.2 us -> 28.9 us
  waiting for transfers between devices: 49.9 us -> 51.6 us
    unnamed x35 -> x20, local copies, waits for them, and re-layouts: 4.68 us -> 0.06 us
    ppermute x6, waiting for transfers between devices: 20.5 us -> 24.8 us  [ring_step(): return lax.ppermute(value, 'dp', pairs)]
    ppermute x4, waiting for transfers between devices: 13.7 us -> 9.51 us  [handed_over(): return lax.ppermute(value, 'pipe', [(0, 1), (1, 0)])]
    pallas_call x24, Pallas kernels: 31.2 us -> 28.9 us  [call(): pl.pallas_call(kernel, out_shape=out_shape, in_specs=in_specs, scratch_sh...]
    ppermute x27 -> x26, waiting for transfers between devices: 10.3 us -> 11.9 us  [swap(): lax.ppermute(value, 'seq', [(source, source ^ bit) for source in range(co...]
    ppermute x27 -> x26, starting transfers between devices: 13.8 us -> 14.2 us  [swap(): lax.ppermute(value, 'seq', [(source, source ^ bit) for source in range(co...]
  transfers between devices with their start and end apart: 40 -> 39, of which waited for: 17 -> 20; matrix products, arithmetic and copies ran while one was open for 1% -> 0% of each run, Pallas kernels for 23% -> 22%
where the time goes in v14:
time: 115 us
  waiting for transfers between devices  51.6 us (45%)
  starting transfers between devices  33 us (29%)
  Pallas kernels  28.9 us (25%)
    pallas_call x24, Pallas kernels, call(): pl.pallas_call(kernel, out_shape=out_shape, in_specs=in_specs, scratch_sh...  28.9 us
    ppermute x6, waiting for transfers between devices, ring_step(): return lax.ppermute(value, 'dp', pairs)  24.8 us
    ppermute x26, starting transfers between devices, swap(): lax.ppermute(value, 'seq', [(source, source ^ bit) for source in range(co...  14.2 us
    ppermute x26, waiting for transfers between devices, swap(): lax.ppermute(value, 'seq', [(source, source ^ bit) for source in range(co...  11.9 us
    ppermute x6, starting transfers between devices, ring_step(): return lax.ppermute(value, 'dp', pairs)  10.9 us
    ppermute x4, waiting for transfers between devices, handed_over(): return lax.ppermute(value, 'pipe', [(0, 1), (1, 0)])  9.51 us
    ppermute x3, waiting for transfers between devices, shifted(): lax.ppermute(value, axis, [(source, (source + shift) % count) for source...  5.3 us
    ppermute x4, starting transfers between devices, handed_over(): return lax.ppermute(value, 'pipe', [(0, 1), (1, 0)])  5.08 us
  transfers between devices with their start and end apart: 39, of which 20 were waited for; matrix products, arithmetic and copies ran while one was open for 0% of the time, Pallas kernels for 22%

profile of v14, /device:TPU:0, one launch (start us, length us, event | category | flops | bytes accessed | tf_op | source)
XLA Modules:
  0.0 114.7 jit_solution(6665004736232401567)
XLA Ops:
  0.7 1.5 %pack.1 = (bf16[2,96,384]{2,1,0:T(8,128)(2,1)S(1)}, bf16[2,96,384]{2,1,0:T(8,128)(2,1)S(1)}, bf16[2,96,384]{2,1,0:T(8,128)(2,1)S(1)}, bf16[2,96,384]{2,1,0:T(8,128)(2,1)S(1)}) custom-call(bf16[1,96,1536]{2,1,0:T(8,128)(2,1)} %wq.1, bf16[1,96,1536]{2,1,0:T(8,128)(2,1)} %wkv.1), custom_call_target="tpu_custom_call" | custom-call | tf_op jit(solution)/shard_map/pack/pallas_call | solution.py:502
  2.1 0.5 collective-permute-start
  2.7 1.0 collective-permute-done.refs_1_
  3.7 3.0 %collective-permute-start.1 = (bf16[2,2,96,384]{3,2,1,0:T(8,128)(2,1)S(1)}, bf16[2,2,96,384]{3,2,1,0:T(8,128)(2,1)S(1)}, u32[]{:S(2)}, u32[]{:S(2)}) collective-permute-start(bf16[2,2,96,384]{3,2,1,0:T(8,128)(2,1)S(1)} %near.1), channel_id=1, source_target_pairs={{0,1},{1,3},{3,2},{2,0},{4,5},{5,7},{7,6},{6,4},{8,9},{9,11},{11,1... | collective-permute-start | bytes 884744 | tf_op jit(solution)/shard_map/ppermute | solution.py:46
  6.7 1.5 %collective-permute-start.2 = (bf16[2,96,384]{2,1,0:T(8,128)(2,1)S(1)}, bf16[2,96,384]{2,1,0:T(8,128)(2,1)S(1)}, u32[]{:S(2)}, u32[]{:S(2)}) collective-permute-start(bf16[2,96,384]{2,1,0:T(8,128)(2,1)S(1)} %get-tuple-element.46), channel_id=1, source_target_pairs={{0,8},{4,12},{8,0},{12,4},{1,9},{5,13},{9,1},{13,5},{2,10},{6,14},... | collective-permute-start | bytes 442376 | tf_op jit(solution)/shard_map/ppermute | solution.py:27
  8.2 5.2 %collective-permute-done.2.refs_1_ = bf16[2,96,384]{2,1,0:T(8,128)(2,1)S(1)} collective-permute-done((bf16[2,96,384]{2,1,0:T(8,128)(2,1)S(1)}, bf16[2,96,384]{2,1,0:T(8,128)(2,1)S(1)}, u32[]{:S(2)}, u32[]{:S(2)}) %collective-permute-start.2) | collective-permute-done | bytes 147488 | tf_op jit(solution)/shard_map/ppermute | solution.py:27
  13.4 1.1 collective-permute-done.3.refs_2_
  14.5 0.5 collective-permute-done.1.refs_0_.near
  15.1 0.1 first.1.refs_0_
  15.1 1.6 %collective-permute-start.4 = (bf16[272,1536]{1,0:T(8,128)(2,1)S(1)}, bf16[272,1536]{1,0:T(8,128)(2,1)S(1)}, u32[]{:S(2)}, u32[]{:S(2)}) collective-permute-start(bf16[272,1536]{1,0:T(8,128)(2,1)S(1)} %first.1.refs_0_), channel_id=1, source_target_pairs={{0,8},{4,12},{8,0},{12,4},{1,9},{5,13},{9,1},{13,5},{2,10},{6,14},... | collective-permute-start | bytes 2506760 | tf_op jit(solution)/shard_map/ppermute | solution.py:27
  16.7 1.9 %collective-permute-start.5 = (bf16[2,2,96,384]{3,2,1,0:T(8,128)(2,1)S(1)}, bf16[2,2,96,384]{3,2,1,0:T(8,128)(2,1)S(1)}, u32[]{:S(2)}, u32[]{:S(2)}) collective-permute-start(bf16[2,2,96,384]{3,2,1,0:T(8,128)(2,1)S(1)} %far.1), channel_id=1, source_target_pairs={{0,1},{1,3},{3,2},{2,0},{4,5},{5,7},{7,6},{6,4},{8,9},{9,11},{11,1... | collective-permute-start | bytes 884744 | tf_op jit(solution)/shard_map/ppermute | solution.py:46
  18.6 7.9 %collective-permute-done.5.far = bf16[2,2,96,384]{3,2,1,0:T(8,128)(2,1)S(1)} collective-permute-done((bf16[2,2,96,384]{3,2,1,0:T(8,128)(2,1)S(1)}, bf16[2,2,96,384]{3,2,1,0:T(8,128)(2,1)S(1)}, u32[]{:S(2)}, u32[]{:S(2)}) %collective-permute-start.5) | collective-permute-done | bytes 294944 | tf_op jit(solution)/shard_map/ppermute | solution.py:46
  26.5 1.7 %collective-permute-start.6 = (bf16[4,96,384]{2,1,0:T(8,128)(2,1)S(1)}, bf16[4,96,384]{2,1,0:T(8,128)(2,1)S(1)}, u32[]{:S(2)}, u32[]{:S(2)}) collective-permute-start(bf16[4,96,384]{2,1,0:T(8,128)(2,1)S(1)} %part0.1.chunk), channel_id=1, source_target_pairs={{0,1},{1,3},{3,2},{2,0},{4,5},{5,7},{7,6},{6,4},{8,9},{9,11},{11,1... | collective-permute-start | bytes 884744 | tf_op jit(solution)/shard_map/ppermute | solution.py:46
  28.3 1.7 %collective-permute-start.7 = (bf16[4,96,384]{2,1,0:T(8,128)(2,1)S(1)}, bf16[4,96,384]{2,1,0:T(8,128)(2,1)S(1)}, u32[]{:S(2)}, u32[]{:S(2)}) collective-permute-start(bf16[4,96,384]{2,1,0:T(8,128)(2,1)S(1)} %part1.1.chunk), channel_id=1, source_target_pairs={{0,1},{1,3},{3,2},{2,0},{4,5},{5,7},{7,6},{6,4},{8,9},{9,11},{11,1... | collective-permute-start | bytes 884744 | tf_op jit(solution)/shard_map/ppermute | solution.py:46
  30.0 7.4 %collective-permute-done.6.refs_1_.refs_9_ = bf16[4,96,384]{2,1,0:T(8,128)(2,1)S(1)} collective-permute-done((bf16[4,96,384]{2,1,0:T(8,128)(2,1)S(1)}, bf16[4,96,384]{2,1,0:T(8,128)(2,1)S(1)}, u32[]{:S(2)}, u32[]{:S(2)}) %collective-permute-start.6) | collective-permute-done | bytes 294944 | tf_op jit(solution)/shard_map/ppermute | solution.py:46
  37.4 4.4 %collective-permute-done.7.refs_2_.refs_9_ = bf16[4,96,384]{2,1,0:T(8,128)(2,1)S(1)} collective-permute-done((bf16[4,96,384]{2,1,0:T(8,128)(2,1)S(1)}, bf16[4,96,384]{2,1,0:T(8,128)(2,1)S(1)}, u32[]{:S(2)}, u32[]{:S(2)}) %collective-permute-start.7) | collective-permute-done | bytes 294944 | tf_op jit(solution)/shard_map/ppermute | solution.py:46
  41.9 0.7 collective-permute-start.8
  42.6 1.4 %collective-permute-start.12 = (bf16[4,96,384]{2,1,0:T(8,128)(2,1)S(1)}, bf16[4,96,384]{2,1,0:T(8,128)(2,1)S(1)}, u32[]{:S(2)}, u32[]{:S(2)}) collective-permute-start(bf16[4,96,384]{2,1,0:T(8,128)(2,1)S(1)} %collective-permute-done.6.refs_1_.refs_9_), channel_id=1, source_target_pairs={{0,1},{1,3},{3,2},{2,0},{4,5},{5,7},{7,6},{6,4},{8,9},{9,11},{11,1... | collective-permute-start | bytes 884744 | tf_op jit(solution)/shard_map/ppermute | solution.py:46
  44.0 1.2 %collective-permute-start.11 = (bf16[4,96,384]{2,1,0:T(8,128)(2,1)S(1)}, bf16[4,96,384]{2,1,0:T(8,128)(2,1)S(1)}, u32[]{:S(2)}, u32[]{:S(2)}) collective-permute-start(bf16[4,96,384]{2,1,0:T(8,128)(2,1)S(1)} %collective-permute-done.7.refs_2_.refs_9_), channel_id=1, source_target_pairs={{0,1},{1,3},{3,2},{2,0},{4,5},{5,7},{7,6},{6,4},{8,9},{9,11},{11,1... | collective-permute-start | bytes 884744 | tf_op jit(solution)/shard_map/ppermute | solution.py:46
  45.2 0.1 place0.1.refs_11_
  45.3 3.3 %norm.1 = (bf16[512,1536]{1,0:T(8,128)(2,1)S(1)}, bf16[512,1536]{1,0:T(8,128)(2,1)S(1)}, f32[512,128]{1,0:T(8,128)S(1)}, f32[512,128]{1,0:T(8,128)S(1)}, f32[512...) custom-call(s32[1,4]{1,0:T(1,128)S(1)} %bitcast.5, ...), custom_call_target="tpu_custom_call" | custom-call | tf_op jit(solution)/shard_map/norm/pallas_call | solution.py:502
  48.7 4.6 %collective-permute-done.12.refs_10_ = bf16[4,96,384]{2,1,0:T(8,128)(2,1)S(1)} collective-permute-done((bf16[4,96,384]{2,1,0:T(8,128)(2,1)S(1)}, bf16[4,96,384]{2,1,0:T(8,128)(2,1)S(1)}, u32[]{:S(2)}, u32[]{:S(2)}) %collective-permute-start.12) | collective-permute-done | bytes 294944 | tf_op jit(solution)/shard_map/ppermute | solution.py:46
  53.3 2.7 %step0a.1 = (bf16[768,128]{1,0:T(8,128)(2,1)S(1)}, bf16[512,256]{1,0:T(8,128)(2,1)S(1)}, bf16[1536,384]{1,0:T(8,128)(2,1)S(1)}) custom-call(f32[1,16]{1,0:T(1,128)S(1)} %copy-done.8, s32[1,4]{1,0:T(1,128)S(1)} %bitcast.6, f32[1,1536]{1,0:T(1,128)S(1)} %copy-done.1, f32[1,1536]{1,0:T(1,128)S(1)} %copy-done.2, ...), custom_call_target="tpu_custom_call", output_to_operand_aliasing={{2}: (11, {})} | custom-call | flops 805306368 | bytes 1572864 | tf_op jit(solution)/shard_map/step0a/pallas_call | solution.py:502
  56.1 1.5 %collective-permute-start.13 = (bf16[768,128]{1,0:T(8,128)(2,1)S(1)}, bf16[768,128]{1,0:T(8,128)(2,1)S(1)}, u32[]{:S(2)}, u32[]{:S(2)}) collective-permute-start(bf16[768,128]{1,0:T(8,128)(2,1)S(1)} %get-tuple-element.51), channel_id=1, source_target_pairs={{0,16},{16,0},{1,17},{17,1},{2,18},{18,2},{3,19},{19,3},{4,20},{20... | collective-permute-start | bytes 589832 | tf_op jit(solution)/shard_map/ppermute | solution.py:31
  57.6 0.1 place1.1.refs_11_
  57.7 2.7 %step1a.1 = (bf16[768,128]{1,0:T(8,128)(2,1)S(1)}, bf16[512,256]{1,0:T(8,128)(2,1)S(1)}) custom-call(f32[1,16]{1,0:T(1,128)S(1)} %copy-done.8, s32[1,4]{1,0:T(1,128)S(1)} %bitcast.7, f32[1,1536]{1,0:T(1,128)S(1)} %copy-done.1, f32[1,1536]{1,0:T(1,128)S(1)} %copy-done.2, f32[1,1536]{1,0:T(1,128)S(1)} %copy-done.4, s32[4,1,512]{2,1,0:T(1,128)S(1)} %copy-done.3, ...), custom_call_target="tpu_custom_call" | custom-call | flops 805306368 | bytes 1572864 | tf_op jit(solution)/shard_map/step1a/pallas_call | solution.py:502
  60.3 1.5 %collective-permute-done.13.refs_1_.refs_10_ = bf16[768,128]{1,0:T(8,128)(2,1)S(1)} collective-permute-done((bf16[768,128]{1,0:T(8,128)(2,1)S(1)}, bf16[768,128]{1,0:T(8,128)(2,1)S(1)}, u32[]{:S(2)}, u32[]{:S(2)}) %collective-permute-start.13) | collective-permute-done | bytes 196640 | tf_op jit(solution)/shard_map/ppermute | solution.py:31
  61.8 2.8 %step0b.1 = (bf16[768,128]{1,0:T(8,128)(2,1)S(1)}, bf16[4,128,384]{2,1,0:T(8,128)(2,1)S(1)}, bf16[1536,384]{1,0:T(8,128)(2,1)S(1)}) custom-call(f32[1,16]{1,0:T(1,128)S(1)} %copy-done.8, s32[1,4]{1,0:T(1,128)S(1)} %bitcast.8, f32[1,1536]{1,0:T(1,128)S(1)} %copy-done.1, f32[1,1536]{1,0:T(1,128)S(1)} %copy-done.2, ...), custom_call_target="tpu_custom_call", output_to_operand_aliasing={{2}: (11, {})} | custom-call | flops 805306368 | bytes 1572864 | tf_op jit(solution)/shard_map/step0b/pallas_call | solution.py:502
  64.6 0.1 beside.1
  64.7 0.1 collective-permute-start.14
  64.8 1.5 %collective-permute-start.18 = (bf16[768,128]{1,0:T(8,128)(2,1)S(1)}, bf16[768,128]{1,0:T(8,128)(2,1)S(1)}, u32[]{:S(2)}, u32[]{:S(2)}) collective-permute-start(bf16[768,128]{1,0:T(8,128)(2,1)S(1)} %get-tuple-element.60), channel_id=1, source_target_pairs={{0,16},{16,0},{1,17},{17,1},{2,18},{18,2},{3,19},{19,3},{4,20},{20... | collective-permute-start | bytes 589832 | tf_op jit(solution)/shard_map/ppermute | solution.py:31
  66.3 0.6 collective-permute-start.22
  66.9 1.4 %collective-permute-start.15 = (bf16[768,128]{1,0:T(8,128)(2,1)S(1)}, bf16[768,128]{1,0:T(8,128)(2,1)S(1)}, u32[]{:S(2)}, u32[]{:S(2)}) collective-permute-start(bf16[768,128]{1,0:T(8,128)(2,1)S(1)} %collective-permute-done.13.refs_1_.refs_10_), channel_id=1, source_target_pairs={{0,8},{4,12},{8,0},{12,4},{1,9},{5,13},{9,1},{13,5},{2,10},{6,14},... | collective-permute-start | bytes 589832 | tf_op jit(solution)/shard_map/ppermute | solution.py:27
  68.3 2.7 %step1b.1 = (bf16[768,128]{1,0:T(8,128)(2,1)S(1)}, bf16[4,128,384]{2,1,0:T(8,128)(2,1)S(1)}) custom-call(f32[1,16]{1,0:T(1,128)S(1)} %copy-done.8, s32[1,4]{1,0:T(1,128)S(1)} %bitcast.9, f32[1,1536]{1,0:T(1,128)S(1)} %copy-done.1, f32[1,1536]{1,0:T(1,128)S(1)} %copy-done.2, f32[1,1536]{1,0:T(1,128)S(1)} %copy-done.4, s32[4,1,512]{2,1,0:T(1,128)S(1)} %copy-done.3, ...), custom_call_target="tpu_custom_call" | custom-call | flops 805306368 | bytes 1572864 | tf_op jit(solution)/shard_map/step1b/pallas_call | solution.py:502
  71.1 1.5 %collective-permute-done.18.refs_0_ = bf16[768,128]{1,0:T(8,128)(2,1)S(1)} collective-permute-done((bf16[768,128]{1,0:T(8,128)(2,1)S(1)}, bf16[768,128]{1,0:T(8,128)(2,1)S(1)}, u32[]{:S(2)}, u32[]{:S(2)}) %collective-permute-start.18) | collective-permute-done | bytes 196640 | tf_op jit(solution)/shard_map/ppermute | solution.py:31
  72.6 1.4 %collective-permute-start.19 = (bf16[768,128]{1,0:T(8,128)(2,1)S(1)}, bf16[768,128]{1,0:T(8,128)(2,1)S(1)}, u32[]{:S(2)}, u32[]{:S(2)}) collective-permute-start(bf16[768,128]{1,0:T(8,128)(2,1)S(1)} %tie.6.refs_14_), channel_id=1, source_target_pairs={{0,8},{4,12},{8,0},{12,4},{1,9},{5,13},{9,1},{13,5},{2,10},{6,14},... | collective-permute-start | bytes 589832 | tf_op jit(solution)/shard_map/ppermute | solution.py:27
  74.0 2.3 %collective-permute-done.22.refs_0_ = bf16[768,128]{1,0:T(8,128)(2,1)S(1)} collective-permute-done((bf16[768,128]{1,0:T(8,128)(2,1)S(1)}, bf16[768,128]{1,0:T(8,128)(2,1)S(1)}, u32[]{:S(2)}, u32[]{:S(2)}) %collective-permute-start.22) | collective-permute-done | bytes 196640 | tf_op jit(solution)/shard_map/ppermute | solution.py:31
  76.3 1.5 %collective-permute-start.24 = (bf16[768,128]{1,0:T(8,128)(2,1)S(1)}, bf16[768,128]{1,0:T(8,128)(2,1)S(1)}, u32[]{:S(2)}, u32[]{:S(2)}) collective-permute-start(bf16[768,128]{1,0:T(8,128)(2,1)S(1)} %get-tuple-element.65), channel_id=1, source_target_pairs={{0,16},{16,0},{1,17},{17,1},{2,18},{18,2},{3,19},{19,3},{4,20},{20... | collective-permute-start | bytes 589832 | tf_op jit(solution)/shard_map/ppermute | solution.py:31
  77.8 0.5 collective-permute-start.17
  78.3 0.3 collective-permute-done.19.refs_15_
  78.6 4.2 %collective-permute-done.24.refs_2_ = bf16[768,128]{1,0:T(8,128)(2,1)S(1)} collective-permute-done((bf16[768,128]{1,0:T(8,128)(2,1)S(1)}, bf16[768,128]{1,0:T(8,128)(2,1)S(1)}, u32[]{:S(2)}, u32[]{:S(2)}) %collective-permute-start.24) | collective-permute-done | bytes 196640 | tf_op jit(solution)/shard_map/ppermute | solution.py:31
  82.8 1.4 %collective-permute-start.23 = (bf16[768,128]{1,0:T(8,128)(2,1)S(1)}, bf16[768,128]{1,0:T(8,128)(2,1)S(1)}, u32[]{:S(2)}, u32[]{:S(2)}) collective-permute-start(bf16[768,128]{1,0:T(8,128)(2,1)S(1)} %collective-permute-done.22.refs_0_), channel_id=1, source_target_pairs={{0,8},{4,12},{8,0},{12,4},{1,9},{5,13},{9,1},{13,5},{2,10},{6,14},... | collective-permute-start | bytes 589832 | tf_op jit(solution)/shard_map/ppermute | solution.py:27
  84.2 0.6 collective-permute-start.25
  84.8 4.9 %step2ab.1.refs_2_.refs_0_ = bf16[4,128,384]{2,1,0:T(8,128)(2,1)S(1)} custom-call(f32[1,16]{1,0:T(1,128)S(1)} %copy-done.8, s32[1,4]{1,0:T(1,128)S(1)} %bitcast.10, f32[1,1536]{1,0:T(1,128)S(1)} %copy-done.1, f32[1,1536]{1,0:T(1,128)S(1)} %copy-done.2, f32[1,1536]{1,0:T(1,128)S(1)} %copy-done.4, s32[4,1,512]{2,1,0:T(1,128)S(1)} %copy-done.3, ...), custom_call_target="tpu_custom_call" | custom-call | flops 1610612736 | bytes 3145728 | tf_op jit(solution)/shard_map/step2ab/pallas_call | solution.py:502
  89.7 0.5 early.1
  90.2 0.3 collective-permute-done.23.refs_1_
  90.5 2.1 %collective-permute-done.25.refs_3_ = bf16[768,128]{1,0:T(8,128)(2,1)S(1)} collective-permute-done((bf16[768,128]{1,0:T(8,128)(2,1)S(1)}, bf16[768,128]{1,0:T(8,128)(2,1)S(1)}, u32[]{:S(2)}, u32[]{:S(2)}) %collective-permute-start.25) | collective-permute-done | bytes 196640 | tf_op jit(solution)/shard_map/ppermute | solution.py:27
  92.6 0.5 collective-permute-start.27
  93.1 0.5 collective-permute-start.29
  93.6 0.4 collective-permute-done.26.refs_12_
  94.0 1.4 %collective-permute-start.31 = (bf16[2,128,384]{2,1,0:T(8,128)(2,1)S(1)}, bf16[2,128,384]{2,1,0:T(8,128)(2,1)S(1)}, u32[]{:S(2)}, u32[]{:S(2)}) collective-permute-start(bf16[2,128,384]{2,1,0:T(8,128)(2,1)S(1)} %get-tuple-element.73), channel_id=1, source_target_pairs={{0,8},{4,12},{8,0},{12,4},{1,9},{5,13},{9,1},{13,5},{2,10},{6,14},... | collective-permute-start | bytes 589832 | tf_op jit(solution)/shard_map/ppermute | solution.py:27
  95.5 0.1 collective-permute-start.32
  95.6 4.7 %step3ab.1.refs_1_ = bf16[4,128,384]{2,1,0:T(8,128)(2,1)S(1)} custom-call(f32[1,16]{1,0:T(1,128)S(1)} %copy-done.8, s32[1,4]{1,0:T(1,128)S(1)} %bitcast.11, f32[1,1536]{1,0:T(1,128)S(1)} %copy-done.1, f32[1,1536]{1,0:T(1,128)S(1)} %copy-done.2, f32[1,1536]{1,0:T(1,128)S(1)} %copy-done.4, s32[4,1,512]{2,1,0:T(1,128)S(1)} %copy-done.3, ...), custom_call_target="tpu_custom_call" | custom-call | flops 1610612736 | bytes 3145728 | tf_op jit(solution)/shard_map/step3ab/pallas_call | solution.py:502
  100.3 1.5 %collective-permute-done.31.refs_7_ = bf16[2,128,384]{2,1,0:T(8,128)(2,1)S(1)} collective-permute-done((bf16[2,128,384]{2,1,0:T(8,128)(2,1)S(1)}, bf16[2,128,384]{2,1,0:T(8,128)(2,1)S(1)}, u32[]{:S(2)}, u32[]{:S(2)}) %collective-permute-start.31) | collective-permute-done | bytes 196640 | tf_op jit(solution)/shard_map/ppermute | solution.py:27
  101.8 1.2 %settle.1 = (bf16[128,384]{1,0:T(8,128)(2,1)S(1)}, bf16[128,384]{1,0:T(8,128)(2,1)S(1)}, bf16[128,384]{1,0:T(8,128)(2,1)S(1)}, bf16[128,384]{1,0:T(8,128)(2,1)S(...) custom-call(bf16[4,128,384]{2,1,0:T(8,128)(2,1)S(1)} %step2ab.1.refs, ...), custom_call_target="tpu_custom_call" | custom-call | tf_op jit(solution)/shard_map/settle/pallas_call | solution.py:502
  103.0 0.6 collective-permute-start.36
  103.6 1.5 %collective-permute-start.34 = (bf16[128,384]{1,0:T(8,128)(2,1)S(1)}, bf16[128,384]{1,0:T(8,128)(2,1)S(1)}, u32[]{:S(2)}, u32[]{:S(2)}) collective-permute-start(bf16[128,384]{1,0:T(8,128)(2,1)S(1)} %get-tuple-element.78), channel_id=1, source_target_pairs={{0,8},{4,12},{8,0},{12,4},{1,9},{5,13},{9,1},{13,5},{2,10},{6,14},... | collective-permute-start | bytes 294920 | tf_op jit(solution)/shard_map/ppermute | solution.py:27
  105.1 0.3 collective-permute-start.35
  105.4 2.1 %collective-permute-start.37 = (bf16[96,256]{1,0:T(8,128)(2,1)S(1)}, bf16[96,256]{1,0:T(8,128)(2,1)S(1)}, u32[]{:S(2)}, u32[]{:S(2)}) collective-permute-start(bf16[96,256]{1,0:T(8,128)(2,1)S(1)} %get-tuple-element.82), channel_id=1, source_target_pairs={{0,2},{1,3},{2,0},{3,1},{4,6},{5,7},{6,4},{7,5},{8,10},{9,11},{10,... | collective-permute-start | bytes 147464 | tf_op jit(solution)/shard_map/ppermute | solution.py:36
  107.5 1.4 %collective-permute-done.36.refs_7_ = bf16[96,256]{1,0:T(8,128)(2,1)S(1)} collective-permute-done((bf16[96,256]{1,0:T(8,128)(2,1)S(1)}, bf16[96,256]{1,0:T(8,128)(2,1)S(1)}, u32[]{:S(2)}, u32[]{:S(2)}) %collective-permute-start.36) | collective-permute-done | bytes 49184 | tf_op jit(solution)/shard_map/ppermute | solution.py:36
  108.9 0.2 collective-permute-start.38
  109.2 2.3 %collective-permute-done.37.refs_8_ = bf16[96,256]{1,0:T(8,128)(2,1)S(1)} collective-permute-done((bf16[96,256]{1,0:T(8,128)(2,1)S(1)}, bf16[96,256]{1,0:T(8,128)(2,1)S(1)}, u32[]{:S(2)}, u32[]{:S(2)}) %collective-permute-start.37) | collective-permute-done | bytes 49184 | tf_op jit(solution)/shard_map/ppermute | solution.py:36
  111.5 1.5 %collective-permute-done.38.refs_9_ = bf16[96,256]{1,0:T(8,128)(2,1)S(1)} collective-permute-done((bf16[96,256]{1,0:T(8,128)(2,1)S(1)}, bf16[96,256]{1,0:T(8,128)(2,1)S(1)}, u32[]{:S(2)}, u32[]{:S(2)}) %collective-permute-start.38) | collective-permute-done | bytes 49184 | tf_op jit(solution)/shard_map/ppermute | solution.py:36
  113.0 1.5 %finish.1 = (bf16[3,128,1536]{2,1,0:T(8,128)(2,1)}, f32[96,256]{1,0:T(8,128)}) custom-call(bf16[3,128,1536]{2,1,0:T(8,128)(2,1)} %get-tuple-element.74.refs_0_, bf16[2,128,384]{2,1,0:T(8,128)(2,1)S(1)} %collective-permute-done.32.refs_1_, bf16[128,384]{1,0:T(8,128)(2,1)S(1)} %get-tuple-element.76.refs_2_, ...), custom_call_target="tpu_custom_call", output_to_operand_aliasing={{0}: (0, {})} | custom-call | tf_op jit(solution)/shard_map/finish/pallas_call | solution.py:502
  (58 shorter events, 0.3 us)
Async XLA Ops:
  0.6 14.4 %copy-start = (bf16[1,3,1,128,1536]{4,3,2,1,0:T(8,128)(2,1)S(1)}, bf16[1,3,1,128,1536]{4,3,2,1,0:T(8,128)(2,1)}, u32[]{:S(2)}) copy-start(bf16[1,3,1,128,1536]{4,3,2,1,0:T(8,128)(2,1)} %incoming.3) | copy-start | bytes 3538948
  0.6 14.4 %copy-start.9 = (s32[4,1,128]{2,1,0:T(1,128)S(1)}, s32[4,1,128]{2,1,0:T(1,128)}, u32[]{:S(2)}) copy-start(s32[4,1,128]{2,1,0:T(1,128)} %contacts.1) | copy-start | bytes 6148
  2.1 1.5 %collective-permute-start = (bf16[2,96,384]{2,1,0:T(8,128)(2,1)S(1)}, bf16[2,96,384]{2,1,0:T(8,128)(2,1)S(1)}, u32[]{:S(2)}, u32[]{:S(2)}) collective-permute-start(bf16[2,96,384]{2,1,0:T(8,128)(2,1)S(1)} %get-tuple-element.45), channel_id=1, source_target_pairs={{0,4},{4,0},{8,12},{12,8},{1,5},{5,1},{9,13},{13,9},{2,6},{6,2},{1... | collective-permute-start | bytes 442376 | tf_op jit(solution)/shard_map/ppermute | solution.py:27
  3.7 11.3 %collective-permute-start.1 = (bf16[2,2,96,384]{3,2,1,0:T(8,128)(2,1)S(1)}, bf16[2,2,96,384]{3,2,1,0:T(8,128)(2,1)S(1)}, u32[]{:S(2)}, u32[]{:S(2)}) collective-permute-start(bf16[2,2,96,384]{3,2,1,0:T(8,128)(2,1)S(1)} %near.1), channel_id=1, source_target_pairs={{0,1},{1,3},{3,2},{2,0},{4,5},{5,7},{7,6},{6,4},{8,9},{9,11},{11,1... | collective-permute-start | bytes 884744 | tf_op jit(solution)/shard_map/ppermute | solution.py:46
  6.7 6.7 %collective-permute-start.2 = (bf16[2,96,384]{2,1,0:T(8,128)(2,1)S(1)}, bf16[2,96,384]{2,1,0:T(8,128)(2,1)S(1)}, u32[]{:S(2)}, u32[]{:S(2)}) collective-permute-start(bf16[2,96,384]{2,1,0:T(8,128)(2,1)S(1)} %get-tuple-element.46), channel_id=1, source_target_pairs={{0,8},{4,12},{8,0},{12,4},{1,9},{5,13},{9,1},{13,5},{2,10},{6,14},... | collective-permute-start | bytes 442376 | tf_op jit(solution)/shard_map/ppermute | solution.py:27
  8.2 6.3 %collective-permute-start.3 = (bf16[2,96,384]{2,1,0:T(8,128)(2,1)S(1)}, bf16[2,96,384]{2,1,0:T(8,128)(2,1)S(1)}, u32[]{:S(2)}, u32[]{:S(2)}) collective-permute-start(bf16[2,96,384]{2,1,0:T(8,128)(2,1)S(1)} %get-tuple-element.47), channel_id=1, source_target_pairs={{0,12},{4,8},{8,4},{12,0},{1,13},{5,9},{9,5},{13,1},{2,14},{6,10},... | collective-permute-start | bytes 442376 | tf_op jit(solution)/shard_map/ppermute | solution.py:27
  15.1 26.7 %collective-permute-start.4 = (bf16[272,1536]{1,0:T(8,128)(2,1)S(1)}, bf16[272,1536]{1,0:T(8,128)(2,1)S(1)}, u32[]{:S(2)}, u32[]{:S(2)}) collective-permute-start(bf16[272,1536]{1,0:T(8,128)(2,1)S(1)} %first.1.refs_0_), channel_id=1, source_target_pairs={{0,8},{4,12},{8,0},{12,4},{1,9},{5,13},{9,1},{13,5},{2,10},{6,14},... | collective-permute-start | bytes 2506760 | tf_op jit(solution)/shard_map/ppermute | solution.py:27
  16.7 9.8 %collective-permute-start.5 = (bf16[2,2,96,384]{3,2,1,0:T(8,128)(2,1)S(1)}, bf16[2,2,96,384]{3,2,1,0:T(8,128)(2,1)S(1)}, u32[]{:S(2)}, u32[]{:S(2)}) collective-permute-start(bf16[2,2,96,384]{3,2,1,0:T(8,128)(2,1)S(1)} %far.1), channel_id=1, source_target_pairs={{0,1},{1,3},{3,2},{2,0},{4,5},{5,7},{7,6},{6,4},{8,9},{9,11},{11,1... | collective-permute-start | bytes 884744 | tf_op jit(solution)/shard_map/ppermute | solution.py:46
  26.5 10.9 %collective-permute-start.6 = (bf16[4,96,384]{2,1,0:T(8,128)(2,1)S(1)}, bf16[4,96,384]{2,1,0:T(8,128)(2,1)S(1)}, u32[]{:S(2)}, u32[]{:S(2)}) collective-permute-start(bf16[4,96,384]{2,1,0:T(8,128)(2,1)S(1)} %part0.1.chunk), channel_id=1, source_target_pairs={{0,1},{1,3},{3,2},{2,0},{4,5},{5,7},{7,6},{6,4},{8,9},{9,11},{11,1... | collective-permute-start | bytes 884744 | tf_op jit(solution)/shard_map/ppermute | solution.py:46
  28.3 13.5 %copy-start.5 = (bf16[1,3,1,128,256]{4,3,2,1,0:T(8,128)(2,1)S(1)}, bf16[1,3,1,128,256]{4,3,2,1,0:T(8,128)(2,1)}, u32[]{:S(2)}) copy-start(bf16[1,3,1,128,256]{4,3,2,1,0:T(8,128)(2,1)} %cotangent.1) | copy-start | bytes 589828
  28.3 13.5 %collective-permute-start.7 = (bf16[4,96,384]{2,1,0:T(8,128)(2,1)S(1)}, bf16[4,96,384]{2,1,0:T(8,128)(2,1)S(1)}, u32[]{:S(2)}, u32[]{:S(2)}) collective-permute-start(bf16[4,96,384]{2,1,0:T(8,128)(2,1)S(1)} %part1.1.chunk), channel_id=1, source_target_pairs={{0,1},{1,3},{3,2},{2,0},{4,5},{5,7},{7,6},{6,4},{8,9},{9,11},{11,1... | collective-permute-start | bytes 884744 | tf_op jit(solution)/shard_map/ppermute | solution.py:46
  30.0 15.2 %collective-permute-start.9 = (bf16[272,1536]{1,0:T(8,128)(2,1)S(1)}, bf16[272,1536]{1,0:T(8,128)(2,1)S(1)}, u32[]{:S(2)}, u32[]{:S(2)}) collective-permute-start(bf16[272,1536]{1,0:T(8,128)(2,1)S(1)} %first.1.refs_0_), channel_id=1, source_target_pairs={{0,4},{4,0},{8,12},{12,8},{1,5},{5,1},{9,13},{13,9},{2,6},{6,2},{1... | collective-permute-start | bytes 2506760 | tf_op jit(solution)/shard_map/ppermute | solution.py:27
  41.8 3.4 %collective-permute-start.10 = (bf16[272,1536]{1,0:T(8,128)(2,1)S(1)}, bf16[272,1536]{1,0:T(8,128)(2,1)S(1)}, u32[]{:S(2)}, u32[]{:S(2)}) collective-permute-start(bf16[272,1536]{1,0:T(8,128)(2,1)S(1)} %tie.4.dep.refs_1_), channel_id=1, source_target_pairs={{0,4},{4,0},{8,12},{12,8},{1,5},{5,1},{9,13},{13,9},{2,6},{6,2},{1... | collective-permute-start | bytes 2506760 | tf_op jit(solution)/shard_map/ppermute | solution.py:27
  41.9 3.4 %copy-start.1 = (f32[1,1536]{1,0:T(1,128)S(1)}, f32[1,1536]{1,0:T(1,128)}, u32[]{:S(2)}) copy-start(f32[1,1536]{1,0:T(1,128)} %refs_2_.11) | copy-start | bytes 18436
  41.9 3.4 %copy-start.2 = (f32[1,1536]{1,0:T(1,128)S(1)}, f32[1,1536]{1,0:T(1,128)}, u32[]{:S(2)}) copy-start(f32[1,1536]{1,0:T(1,128)} %refs_3_.11) | copy-start | bytes 18436
  41.9 3.4 %copy-start.6 = (bf16[1,16,1536]{2,1,0:T(8,128)(2,1)S(1)}, bf16[1,16,1536]{2,1,0:T(8,128)(2,1)}, u32[]{:S(2)}) copy-start(bf16[1,16,1536]{2,1,0:T(8,128)(2,1)} %table.1) | copy-start | bytes 147460
  41.9 3.4 %copy-start.7 = (s32[4,1]{0,1:T(1,128)S(1)}, s32[4,1]{0,1:T(1,128)}, u32[]{:S(2)}) copy-start(s32[4,1]{0,1:T(1,128)} %param.15) | copy-start | bytes 52
  41.9 22.7 %collective-permute-start.8 = (bf16[256,1536]{1,0:T(8,128)(2,1)S(1)}, bf16[256,1536]{1,0:T(8,128)(2,1)S(1)}, u32[]{:S(2)}, u32[]{:S(2)}) collective-permute-start(bf16[256,1536]{1,0:T(8,128)(2,1)S(1)} %second.1.mine.refs_6_.refs_3_.refs_2_), channel_id=1, source_target_pairs={{0,8},{4,12},{8,0},{12,4},{1,9},{5,13},{9,1},{13,5},{2,10},{6,14},... | collective-permute-start | bytes 2359304 | tf_op jit(solution)/shard_map/ppermute | solution.py:27
  42.6 10.7 %collective-permute-start.12 = (bf16[4,96,384]{2,1,0:T(8,128)(2,1)S(1)}, bf16[4,96,384]{2,1,0:T(8,128)(2,1)S(1)}, u32[]{:S(2)}, u32[]{:S(2)}) collective-permute-start(bf16[4,96,384]{2,1,0:T(8,128)(2,1)S(1)} %collective-permute-done.6.refs_1_.refs_9_), channel_id=1, source_target_pairs={{0,1},{1,3},{3,2},{2,0},{4,5},{5,7},{7,6},{6,4},{8,9},{9,11},{11,1... | collective-permute-start | bytes 884744 | tf_op jit(solution)/shard_map/ppermute | solution.py:46
  44.0 16.4 %collective-permute-start.11 = (bf16[4,96,384]{2,1,0:T(8,128)(2,1)S(1)}, bf16[4,96,384]{2,1,0:T(8,128)(2,1)S(1)}, u32[]{:S(2)}, u32[]{:S(2)}) collective-permute-start(bf16[4,96,384]{2,1,0:T(8,128)(2,1)S(1)} %collective-permute-done.7.refs_2_.refs_9_), channel_id=1, source_target_pairs={{0,1},{1,3},{3,2},{2,0},{4,5},{5,7},{7,6},{6,4},{8,9},{9,11},{11,1... | collective-permute-start | bytes 884744 | tf_op jit(solution)/shard_map/ppermute | solution.py:46
  45.3 8.0 %copy-start.3 = (s32[4,1,512]{2,1,0:T(1,128)S(1)}, s32[4,1,512]{2,1,0:T(1,128)}, u32[]{:S(2)}) copy-start(s32[4,1,512]{2,1,0:T(1,128)} %refs_5_.11) | copy-start | bytes 24580
  45.3 8.0 %copy-start.4 = (f32[1,1536]{1,0:T(1,128)S(1)}, f32[1,1536]{1,0:T(1,128)}, u32[]{:S(2)}) copy-start(f32[1,1536]{1,0:T(1,128)} %refs_4_.11) | copy-start | bytes 18436
  45.3 8.0 %copy-start.8 = (f32[1,16]{1,0:T(1,128)S(1)}, f32[1,16]{1,0:T(1,128)}, u32[]{:S(2)}) copy-start(f32[1,16]{1,0:T(1,128)} %refs_0_.11) | copy-start | bytes 196
  56.1 5.7 %collective-permute-start.13 = (bf16[768,128]{1,0:T(8,128)(2,1)S(1)}, bf16[768,128]{1,0:T(8,128)(2,1)S(1)}, u32[]{:S(2)}, u32[]{:S(2)}) collective-permute-start(bf16[768,128]{1,0:T(8,128)(2,1)S(1)} %get-tuple-element.51), channel_id=1, source_target_pairs={{0,16},{16,0},{1,17},{17,1},{2,18},{18,2},{3,19},{19,3},{4,20},{20... | collective-permute-start | bytes 589832 | tf_op jit(solution)/shard_map/ppermute | solution.py:31
  64.7 20.1 %collective-permute-start.14 = (bf16[2,256,1536]{2,1,0:T(8,128)(2,1)S(1)}, bf16[2,256,1536]{2,1,0:T(8,128)(2,1)S(1)}, u32[]{:S(2)}, u32[]{:S(2)}) collective-permute-start(bf16[2,256,1536]{2,1,0:T(8,128)(2,1)S(1)} %beside.1), channel_id=1, source_target_pairs={{0,4},{4,0},{8,12},{12,8},{1,5},{5,1},{9,13},{13,9},{2,6},{6,2},{1... | collective-permute-start | bytes 4718600 | tf_op jit(solution)/shard_map/ppermute | solution.py:27
  64.8 7.8 %collective-permute-start.18 = (bf16[768,128]{1,0:T(8,128)(2,1)S(1)}, bf16[768,128]{1,0:T(8,128)(2,1)S(1)}, u32[]{:S(2)}, u32[]{:S(2)}) collective-permute-start(bf16[768,128]{1,0:T(8,128)(2,1)S(1)} %get-tuple-element.60), channel_id=1, source_target_pairs={{0,16},{16,0},{1,17},{17,1},{2,18},{18,2},{3,19},{19,3},{4,20},{20... | collective-permute-start | bytes 589832 | tf_op jit(solution)/shard_map/ppermute | solution.py:31
  66.3 10.0 %collective-permute-start.22 = (bf16[768,128]{1,0:T(8,128)(2,1)S(1)}, bf16[768,128]{1,0:T(8,128)(2,1)S(1)}, u32[]{:S(2)}, u32[]{:S(2)}) collective-permute-start(bf16[768,128]{1,0:T(8,128)(2,1)S(1)} %get-tuple-element.64), channel_id=1, source_target_pairs={{0,16},{16,0},{1,17},{17,1},{2,18},{18,2},{3,19},{19,3},{4,20},{20... | collective-permute-start | bytes 589832 | tf_op jit(solution)/shard_map/ppermute | solution.py:31
  66.9 10.9 %collective-permute-start.15 = (bf16[768,128]{1,0:T(8,128)(2,1)S(1)}, bf16[768,128]{1,0:T(8,128)(2,1)S(1)}, u32[]{:S(2)}, u32[]{:S(2)}) collective-permute-start(bf16[768,128]{1,0:T(8,128)(2,1)S(1)} %collective-permute-done.13.refs_1_.refs_10_), channel_id=1, source_target_pairs={{0,8},{4,12},{8,0},{12,4},{1,9},{5,13},{9,1},{13,5},{2,10},{6,14},... | collective-permute-start | bytes 589832 | tf_op jit(solution)/shard_map/ppermute | solution.py:27
  68.3 9.5 %collective-permute-start.16 = (bf16[768,128]{1,0:T(8,128)(2,1)S(1)}, bf16[768,128]{1,0:T(8,128)(2,1)S(1)}, u32[]{:S(2)}, u32[]{:S(2)}) collective-permute-start(bf16[768,128]{1,0:T(8,128)(2,1)S(1)} %collective-permute-done.13.refs_1_.refs_10_), channel_id=1, source_target_pairs={{0,4},{4,0},{8,12},{12,8},{1,5},{5,1},{9,13},{13,9},{2,6},{6,2},{1... | collective-permute-start | bytes 589832 | tf_op jit(solution)/shard_map/ppermute | solution.py:27
  72.6 6.0 %collective-permute-start.19 = (bf16[768,128]{1,0:T(8,128)(2,1)S(1)}, bf16[768,128]{1,0:T(8,128)(2,1)S(1)}, u32[]{:S(2)}, u32[]{:S(2)}) collective-permute-start(bf16[768,128]{1,0:T(8,128)(2,1)S(1)} %tie.6.refs_14_), channel_id=1, source_target_pairs={{0,8},{4,12},{8,0},{12,4},{1,9},{5,13},{9,1},{13,5},{2,10},{6,14},... | collective-permute-start | bytes 589832 | tf_op jit(solution)/shard_map/ppermute | solution.py:27
  76.3 6.5 %collective-permute-start.24 = (bf16[768,128]{1,0:T(8,128)(2,1)S(1)}, bf16[768,128]{1,0:T(8,128)(2,1)S(1)}, u32[]{:S(2)}, u32[]{:S(2)}) collective-permute-start(bf16[768,128]{1,0:T(8,128)(2,1)S(1)} %get-tuple-element.65), channel_id=1, source_target_pairs={{0,16},{16,0},{1,17},{17,1},{2,18},{18,2},{3,19},{19,3},{4,20},{20... | collective-permute-start | bytes 589832 | tf_op jit(solution)/shard_map/ppermute | solution.py:31
  77.8 6.4 %collective-permute-start.20 = (bf16[768,128]{1,0:T(8,128)(2,1)S(1)}, bf16[768,128]{1,0:T(8,128)(2,1)S(1)}, u32[]{:S(2)}, u32[]{:S(2)}) collective-permute-start(bf16[768,128]{1,0:T(8,128)(2,1)S(1)} %tie.6.refs_14_), channel_id=1, source_target_pairs={{0,4},{4,0},{8,12},{12,8},{1,5},{5,1},{9,13},{13,9},{2,6},{6,2},{1... | collective-permute-start | bytes 589832 | tf_op jit(solution)/shard_map/ppermute | solution.py:27
  77.8 7.0 %collective-permute-start.17 = (bf16[768,128]{1,0:T(8,128)(2,1)S(1)}, bf16[768,128]{1,0:T(8,128)(2,1)S(1)}, u32[]{:S(2)}, u32[]{:S(2)}) collective-permute-start(bf16[768,128]{1,0:T(8,128)(2,1)S(1)} %collective-permute-done.15.refs_11_), channel_id=1, source_target_pairs={{0,4},{4,0},{8,12},{12,8},{1,5},{5,1},{9,13},{13,9},{2,6},{6,2},{1... | collective-permute-start | bytes 589832 | tf_op jit(solution)/shard_map/ppermute | solution.py:27
  78.6 6.2 %collective-permute-start.21 = (bf16[768,128]{1,0:T(8,128)(2,1)S(1)}, bf16[768,128]{1,0:T(8,128)(2,1)S(1)}, u32[]{:S(2)}, u32[]{:S(2)}) collective-permute-start(bf16[768,128]{1,0:T(8,128)(2,1)S(1)} %collective-permute-done.19.refs_15_), channel_id=1, source_target_pairs={{0,4},{4,0},{8,12},{12,8},{1,5},{5,1},{9,13},{13,9},{2,6},{6,2},{1... | collective-permute-start | bytes 589832 | tf_op jit(solution)/shard_map/ppermute | solution.py:27
  82.8 7.7 %collective-permute-start.23 = (bf16[768,128]{1,0:T(8,128)(2,1)S(1)}, bf16[768,128]{1,0:T(8,128)(2,1)S(1)}, u32[]{:S(2)}, u32[]{:S(2)}) collective-permute-start(bf16[768,128]{1,0:T(8,128)(2,1)S(1)} %collective-permute-done.22.refs_0_), channel_id=1, source_target_pairs={{0,8},{4,12},{8,0},{12,4},{1,9},{5,13},{9,1},{13,5},{2,10},{6,14},... | collective-permute-start | bytes 589832 | tf_op jit(solution)/shard_map/ppermute | solution.py:27
  84.2 8.3 %collective-permute-start.25 = (bf16[768,128]{1,0:T(8,128)(2,1)S(1)}, bf16[768,128]{1,0:T(8,128)(2,1)S(1)}, u32[]{:S(2)}, u32[]{:S(2)}) collective-permute-start(bf16[768,128]{1,0:T(8,128)(2,1)S(1)} %collective-permute-done.24.refs_2_), channel_id=1, source_target_pairs={{0,8},{4,12},{8,0},{12,4},{1,9},{5,13},{9,1},{13,5},{2,10},{6,14},... | collective-permute-start | bytes 589832 | tf_op jit(solution)/shard_map/ppermute | solution.py:27
  92.6 1.4 %collective-permute-start.26 = (bf16[768,128]{1,0:T(8,128)(2,1)S(1)}, bf16[768,128]{1,0:T(8,128)(2,1)S(1)}, u32[]{:S(2)}, u32[]{:S(2)}) collective-permute-start(bf16[768,128]{1,0:T(8,128)(2,1)S(1)} %get-tuple-element.67.refs_10_), channel_id=1, source_target_pairs={{0,4},{4,0},{8,12},{12,8},{1,5},{5,1},{9,13},{13,9},{2,6},{6,2},{1... | collective-permute-start | bytes 589832 | tf_op jit(solution)/shard_map/ppermute | solution.py:27
  92.6 2.9 %collective-permute-start.27 = (bf16[768,128]{1,0:T(8,128)(2,1)S(1)}, bf16[768,128]{1,0:T(8,128)(2,1)S(1)}, u32[]{:S(2)}, u32[]{:S(2)}) collective-permute-start(bf16[768,128]{1,0:T(8,128)(2,1)S(1)} %get-tuple-element.68.refs_11_), channel_id=1, source_target_pairs={{0,4},{4,0},{8,12},{12,8},{1,5},{5,1},{9,13},{13,9},{2,6},{6,2},{1... | collective-permute-start | bytes 589832 | tf_op jit(solution)/shard_map/ppermute | solution.py:27
  93.1 2.5 %collective-permute-start.28 = (bf16[768,128]{1,0:T(8,128)(2,1)S(1)}, bf16[768,128]{1,0:T(8,128)(2,1)S(1)}, u32[]{:S(2)}, u32[]{:S(2)}) collective-permute-start(bf16[768,128]{1,0:T(8,128)(2,1)S(1)} %get-tuple-element.69.refs_14_), channel_id=1, source_target_pairs={{0,4},{4,0},{8,12},{12,8},{1,5},{5,1},{9,13},{13,9},{2,6},{6,2},{1... | collective-permute-start | bytes 589832 | tf_op jit(solution)/shard_map/ppermute | solution.py:27
  93.1 2.5 %collective-permute-start.29 = (bf16[768,128]{1,0:T(8,128)(2,1)S(1)}, bf16[768,128]{1,0:T(8,128)(2,1)S(1)}, u32[]{:S(2)}, u32[]{:S(2)}) collective-permute-start(bf16[768,128]{1,0:T(8,128)(2,1)S(1)} %get-tuple-element.70.refs_15_), channel_id=1, source_target_pairs={{0,4},{4,0},{8,12},{12,8},{1,5},{5,1},{9,13},{13,9},{2,6},{6,2},{1... | collective-permute-start | bytes 589832 | tf_op jit(solution)/shard_map/ppermute | solution.py:27
  93.6 6.7 %collective-permute-start.30 = (bf16[2,128,384]{2,1,0:T(8,128)(2,1)S(1)}, bf16[2,128,384]{2,1,0:T(8,128)(2,1)S(1)}, u32[]{:S(2)}, u32[]{:S(2)}) collective-permute-start(bf16[2,128,384]{2,1,0:T(8,128)(2,1)S(1)} %get-tuple-element.72), channel_id=1, source_target_pairs={{0,4},{4,0},{8,12},{12,8},{1,5},{5,1},{9,13},{13,9},{2,6},{6,2},{1... | collective-permute-start | bytes 589832 | tf_op jit(solution)/shard_map/ppermute | solution.py:27
  94.0 7.7 %collective-permute-start.31 = (bf16[2,128,384]{2,1,0:T(8,128)(2,1)S(1)}, bf16[2,128,384]{2,1,0:T(8,128)(2,1)S(1)}, u32[]{:S(2)}, u32[]{:S(2)}) collective-permute-start(bf16[2,128,384]{2,1,0:T(8,128)(2,1)S(1)} %get-tuple-element.73), channel_id=1, source_target_pairs={{0,8},{4,12},{8,0},{12,4},{1,9},{5,13},{9,1},{13,5},{2,10},{6,14},... | collective-permute-start | bytes 589832 | tf_op jit(solution)/shard_map/ppermute | solution.py:27
  95.5 9.9 %collective-permute-start.32 = (bf16[2,128,384]{2,1,0:T(8,128)(2,1)S(1)}, bf16[2,128,384]{2,1,0:T(8,128)(2,1)S(1)}, u32[]{:S(2)}, u32[]{:S(2)}) collective-permute-start(bf16[2,128,384]{2,1,0:T(8,128)(2,1)S(1)} %get-tuple-element.75), channel_id=1, source_target_pairs={{0,12},{4,8},{8,4},{12,0},{1,13},{5,9},{9,5},{13,1},{2,14},{6,10},... | collective-permute-start | bytes 589832 | tf_op jit(solution)/shard_map/ppermute | solution.py:27
  103.0 5.9 %collective-permute-start.36 = (bf16[96,256]{1,0:T(8,128)(2,1)S(1)}, bf16[96,256]{1,0:T(8,128)(2,1)S(1)}, u32[]{:S(2)}, u32[]{:S(2)}) collective-permute-start(bf16[96,256]{1,0:T(8,128)(2,1)S(1)} %get-tuple-element.81), channel_id=1, source_target_pairs={{0,1},{1,2},{2,3},{3,0},{4,5},{5,6},{6,7},{7,4},{8,9},{9,10},{10,1... | collective-permute-start | bytes 147464 | tf_op jit(solution)/shard_map/ppermute | solution.py:36
  103.6 9.5 %collective-permute-start.33 = (bf16[128,384]{1,0:T(8,128)(2,1)S(1)}, bf16[128,384]{1,0:T(8,128)(2,1)S(1)}, u32[]{:S(2)}, u32[]{:S(2)}) collective-permute-start(bf16[128,384]{1,0:T(8,128)(2,1)S(1)} %get-tuple-element.77), channel_id=1, source_target_pairs={{0,4},{4,0},{8,12},{12,8},{1,5},{5,1},{9,13},{13,9},{2,6},{6,2},{1... | collective-permute-start | bytes 294920 | tf_op jit(solution)/shard_map/ppermute | solution.py:27
  103.6 9.5 %collective-permute-start.34 = (bf16[128,384]{1,0:T(8,128)(2,1)S(1)}, bf16[128,384]{1,0:T(8,128)(2,1)S(1)}, u32[]{:S(2)}, u32[]{:S(2)}) collective-permute-start(bf16[128,384]{1,0:T(8,128)(2,1)S(1)} %get-tuple-element.78), channel_id=1, source_target_pairs={{0,8},{4,12},{8,0},{12,4},{1,9},{5,13},{9,1},{13,5},{2,10},{6,14},... | collective-permute-start | bytes 294920 | tf_op jit(solution)/shard_map/ppermute | solution.py:27
  105.1 7.9 %collective-permute-start.35 = (bf16[128,384]{1,0:T(8,128)(2,1)S(1)}, bf16[128,384]{1,0:T(8,128)(2,1)S(1)}, u32[]{:S(2)}, u32[]{:S(2)}) collective-permute-start(bf16[128,384]{1,0:T(8,128)(2,1)S(1)} %get-tuple-element.79), channel_id=1, source_target_pairs={{0,12},{4,8},{8,4},{12,0},{1,13},{5,9},{9,5},{13,1},{2,14},{6,10},... | collective-permute-start | bytes 294920 | tf_op jit(solution)/shard_map/ppermute | solution.py:27
  105.4 6.1 %collective-permute-start.37 = (bf16[96,256]{1,0:T(8,128)(2,1)S(1)}, bf16[96,256]{1,0:T(8,128)(2,1)S(1)}, u32[]{:S(2)}, u32[]{:S(2)}) collective-permute-start(bf16[96,256]{1,0:T(8,128)(2,1)S(1)} %get-tuple-element.82), channel_id=1, source_target_pairs={{0,2},{1,3},{2,0},{3,1},{4,6},{5,7},{6,4},{7,5},{8,10},{9,11},{10,... | collective-permute-start | bytes 147464 | tf_op jit(solution)/shard_map/ppermute | solution.py:36
  108.9 4.1 %collective-permute-start.38 = (bf16[96,256]{1,0:T(8,128)(2,1)S(1)}, bf16[96,256]{1,0:T(8,128)(2,1)S(1)}, u32[]{:S(2)}, u32[]{:S(2)}) collective-permute-start(bf16[96,256]{1,0:T(8,128)(2,1)S(1)} %get-tuple-element.83), channel_id=1, source_target_pairs={{0,3},{1,0},{2,1},{3,2},{4,7},{5,4},{6,5},{7,6},{8,11},{9,8},{10,9... | collective-permute-start | bytes 147464 | tf_op jit(solution)/shard_map/ppermute | solution.py:36

commit v15 on v14

--- a/solution.py
+++ b/solution.py
@@ -668,7 +668,7 @@
             if step == 0:
                 chunks = rings[part][1:]
                 if part:
-                    (last_chunk,) = tie(chunks[1:], [relays[0][0][0], lefts[1]])
+                    (last_chunk,) = tie(chunks[1:], [relays[0][0][1], relays[1][0][0]])
                     chunks = [chunks[0], last_chunk]
                 large += chunks
             large += [weights[part]]
@@ -682,9 +682,12 @@
             if step == 0:
                 weights[part] = results[2]
             (outputs if part else lefts).append(results[1])
-            piece = handed_over(results[0])
+            piece = results[0]
+            if step and not part:
+                (piece,) = tie([piece], [relays[0][0][0]])
+            piece = handed_over(piece)
             relays[step].append([piece, None if part and not step else swap(piece, 2)])
-    (piece,) = tie([relays[0][1][0]], [outputs[1]])
+    (piece,) = tie([relays[0][1][0]], [outputs[1], relays[1][0][1]])
     relays[0][1] = [piece, swap(piece, 2)]
     beside = call(
         second_pair_kernel,

time: 115 us -> 115 us (level)
  waiting for transfers between devices: 51.6 us -> 53.7 us
  starting transfers between devices: 33 us -> 31 us
    ppermute x26, waiting for transfers between devices: 11.9 us -> 15 us  [swap(): lax.ppermute(value, 'seq', [(source, source ^ bit) for source in range(co...]
    ppermute x4, waiting for transfers between devices: 9.51 us -> 6.81 us  [handed_over(): return lax.ppermute(value, 'pipe', [(0, 1), (1, 0)])]
    ppermute x6, waiting for transfers between devices: 24.8 us -> 26.8 us  [ring_step(): return lax.ppermute(value, 'dp', pairs)]
    ppermute x26, starting transfers between devices: 14.2 us -> 12.3 us  [swap(): lax.ppermute(value, 'seq', [(source, source ^ bit) for source in range(co...]
    pallas_call x24 -> x25, Pallas kernels: 28.9 us -> 28.9 us  [call(): pl.pallas_call(kernel, out_shape=out_shape, in_specs=in_specs, scratch_sh...]
  transfers between devices with their start and end apart: 39 -> 39, of which waited for: 20 -> 23; matrix products, arithmetic and copies ran while one was open for 0% -> 0% of each run, Pallas kernels for 22% -> 22%
where the time goes in v15:
time: 115 us
  waiting for transfers between devices  53.7 us (47%)
  starting transfers between devices  31 us (27%)
  Pallas kernels  28.9 us (25%)
    pallas_call x25, Pallas kernels, call(): pl.pallas_call(kernel, out_shape=out_shape, in_specs=in_specs, scratch_sh...  28.9 us
    ppermute x6, waiting for transfers between devices, ring_step(): return lax.ppermute(value, 'dp', pairs)  26.8 us
    ppermute x26, waiting for transfers between devices, swap(): lax.ppermute(value, 'seq', [(source, source ^ bit) for source in range(co...  15 us
    ppermute x26, starting transfers between devices, swap(): lax.ppermute(value, 'seq', [(source, source ^ bit) for source in range(co...  12.3 us
    ppermute x6, starting transfers between devices, ring_step(): return lax.ppermute(value, 'dp', pairs)  10.5 us
    ppermute x4, waiting for transfers between devices, handed_over(): return lax.ppermute(value, 'pipe', [(0, 1), (1, 0)])  6.81 us
    ppermute x4, starting transfers between devices, handed_over(): return lax.ppermute(value, 'pipe', [(0, 1), (1, 0)])  5.13 us
    ppermute x3, waiting for transfers between devices, shifted(): lax.ppermute(value, axis, [(source, (source + shift) % count) for source...  5.08 us
  transfers between devices with their start and end apart: 39, of which 23 were waited for; matrix products, arithmetic and copies ran while one was open for 0% of the time, Pallas kernels for 22%

profile of v15, /device:TPU:0, one launch (start us, length us, event | category | flops | bytes accessed | tf_op | source)
XLA Modules:
  0.0 114.9 jit_solution(4656611350016093031)
XLA Ops:
  0.7 1.5 %pack.1 = (bf16[2,96,384]{2,1,0:T(8,128)(2,1)S(1)}, bf16[2,96,384]{2,1,0:T(8,128)(2,1)S(1)}, bf16[2,96,384]{2,1,0:T(8,128)(2,1)S(1)}, bf16[2,96,384]{2,1,0:T(8,128)(2,1)S(1)}) custom-call(bf16[1,96,1536]{2,1,0:T(8,128)(2,1)} %wq.1, bf16[1,96,1536]{2,1,0:T(8,128)(2,1)} %wkv.1), custom_call_target="tpu_custom_call" | custom-call | tf_op jit(solution)/shard_map/pack/pallas_call | solution.py:502
  2.1 0.5 collective-permute-start
  2.7 1.0 collective-permute-done.refs_1_
  3.7 3.0 %collective-permute-start.1 = (bf16[2,2,96,384]{3,2,1,0:T(8,128)(2,1)S(1)}, bf16[2,2,96,384]{3,2,1,0:T(8,128)(2,1)S(1)}, u32[]{:S(2)}, u32[]{:S(2)}) collective-permute-start(bf16[2,2,96,384]{3,2,1,0:T(8,128)(2,1)S(1)} %near.1), channel_id=1, source_target_pairs={{0,1},{1,3},{3,2},{2,0},{4,5},{5,7},{7,6},{6,4},{8,9},{9,11},{11,1... | collective-permute-start | bytes 884744 | tf_op jit(solution)/shard_map/ppermute | solution.py:46
  6.7 1.5 %collective-permute-start.2 = (bf16[2,96,384]{2,1,0:T(8,128)(2,1)S(1)}, bf16[2,96,384]{2,1,0:T(8,128)(2,1)S(1)}, u32[]{:S(2)}, u32[]{:S(2)}) collective-permute-start(bf16[2,96,384]{2,1,0:T(8,128)(2,1)S(1)} %get-tuple-element.46), channel_id=1, source_target_pairs={{0,8},{4,12},{8,0},{12,4},{1,9},{5,13},{9,1},{13,5},{2,10},{6,14},... | collective-permute-start | bytes 442376 | tf_op jit(solution)/shard_map/ppermute | solution.py:27
  8.2 5.2 %collective-permute-done.2.refs_1_ = bf16[2,96,384]{2,1,0:T(8,128)(2,1)S(1)} collective-permute-done((bf16[2,96,384]{2,1,0:T(8,128)(2,1)S(1)}, bf16[2,96,384]{2,1,0:T(8,128)(2,1)S(1)}, u32[]{:S(2)}, u32[]{:S(2)}) %collective-permute-start.2) | collective-permute-done | bytes 147488 | tf_op jit(solution)/shard_map/ppermute | solution.py:27
  13.4 1.1 collective-permute-done.3.refs_2_
  14.5 0.5 collective-permute-done.1.refs_0_.near
  15.1 1.6 %collective-permute-start.4 = (bf16[272,1536]{1,0:T(8,128)(2,1)S(1)}, bf16[272,1536]{1,0:T(8,128)(2,1)S(1)}, u32[]{:S(2)}, u32[]{:S(2)}) collective-permute-start(bf16[272,1536]{1,0:T(8,128)(2,1)S(1)} %first.1.refs_0_), channel_id=1, source_target_pairs={{0,8},{4,12},{8,0},{12,4},{1,9},{5,13},{9,1},{13,5},{2,10},{6,14},... | collective-permute-start | bytes 2506760 | tf_op jit(solution)/shard_map/ppermute | solution.py:27
  16.7 1.9 %collective-permute-start.5 = (bf16[2,2,96,384]{3,2,1,0:T(8,128)(2,1)S(1)}, bf16[2,2,96,384]{3,2,1,0:T(8,128)(2,1)S(1)}, u32[]{:S(2)}, u32[]{:S(2)}) collective-permute-start(bf16[2,2,96,384]{3,2,1,0:T(8,128)(2,1)S(1)} %far.1), channel_id=1, source_target_pairs={{0,1},{1,3},{3,2},{2,0},{4,5},{5,7},{7,6},{6,4},{8,9},{9,11},{11,1... | collective-permute-start | bytes 884744 | tf_op jit(solution)/shard_map/ppermute | solution.py:46
  18.6 7.9 %collective-permute-done.5.far = bf16[2,2,96,384]{3,2,1,0:T(8,128)(2,1)S(1)} collective-permute-done((bf16[2,2,96,384]{3,2,1,0:T(8,128)(2,1)S(1)}, bf16[2,2,96,384]{3,2,1,0:T(8,128)(2,1)S(1)}, u32[]{:S(2)}, u32[]{:S(2)}) %collective-permute-start.5) | collective-permute-done | bytes 294944 | tf_op jit(solution)/shard_map/ppermute | solution.py:46
  26.5 1.7 %collective-permute-start.6 = (bf16[4,96,384]{2,1,0:T(8,128)(2,1)S(1)}, bf16[4,96,384]{2,1,0:T(8,128)(2,1)S(1)}, u32[]{:S(2)}, u32[]{:S(2)}) collective-permute-start(bf16[4,96,384]{2,1,0:T(8,128)(2,1)S(1)} %part0.1.chunk), channel_id=1, source_target_pairs={{0,1},{1,3},{3,2},{2,0},{4,5},{5,7},{7,6},{6,4},{8,9},{9,11},{11,1... | collective-permute-start | bytes 884744 | tf_op jit(solution)/shard_map/ppermute | solution.py:46
  28.3 1.7 %collective-permute-start.7 = (bf16[4,96,384]{2,1,0:T(8,128)(2,1)S(1)}, bf16[4,96,384]{2,1,0:T(8,128)(2,1)S(1)}, u32[]{:S(2)}, u32[]{:S(2)}) collective-permute-start(bf16[4,96,384]{2,1,0:T(8,128)(2,1)S(1)} %part1.1.chunk), channel_id=1, source_target_pairs={{0,1},{1,3},{3,2},{2,0},{4,5},{5,7},{7,6},{6,4},{8,9},{9,11},{11,1... | collective-permute-start | bytes 884744 | tf_op jit(solution)/shard_map/ppermute | solution.py:46
  30.0 7.4 %collective-permute-done.6.refs_1_.refs_9_ = bf16[4,96,384]{2,1,0:T(8,128)(2,1)S(1)} collective-permute-done((bf16[4,96,384]{2,1,0:T(8,128)(2,1)S(1)}, bf16[4,96,384]{2,1,0:T(8,128)(2,1)S(1)}, u32[]{:S(2)}, u32[]{:S(2)}) %collective-permute-start.6) | collective-permute-done | bytes 294944 | tf_op jit(solution)/shard_map/ppermute | solution.py:46
  37.4 4.4 %collective-permute-done.7.refs_2_.refs_9_ = bf16[4,96,384]{2,1,0:T(8,128)(2,1)S(1)} collective-permute-done((bf16[4,96,384]{2,1,0:T(8,128)(2,1)S(1)}, bf16[4,96,384]{2,1,0:T(8,128)(2,1)S(1)}, u32[]{:S(2)}, u32[]{:S(2)}) %collective-permute-start.7) | collective-permute-done | bytes 294944 | tf_op jit(solution)/shard_map/ppermute | solution.py:46
  41.8 1.6 %collective-permute-start.12 = (bf16[4,96,384]{2,1,0:T(8,128)(2,1)S(1)}, bf16[4,96,384]{2,1,0:T(8,128)(2,1)S(1)}, u32[]{:S(2)}, u32[]{:S(2)}) collective-permute-start(bf16[4,96,384]{2,1,0:T(8,128)(2,1)S(1)} %collective-permute-done.6.refs_1_.refs_9_), channel_id=1, source_target_pairs={{0,1},{1,3},{3,2},{2,0},{4,5},{5,7},{7,6},{6,4},{8,9},{9,11},{11,1... | collective-permute-start | bytes 884744 | tf_op jit(solution)/shard_map/ppermute | solution.py:46
  43.5 0.6 collective-permute-start.8
  44.2 0.1 copy-done.6
  44.3 3.3 %norm.1 = (bf16[512,1536]{1,0:T(8,128)(2,1)S(1)}, bf16[512,1536]{1,0:T(8,128)(2,1)S(1)}, f32[512,128]{1,0:T(8,128)S(1)}, f32[512,128]{1,0:T(8,128)S(1)}, f32[512...) custom-call(s32[1,4]{1,0:T(1,128)S(1)} %bitcast.5, ...), custom_call_target="tpu_custom_call" | custom-call | tf_op jit(solution)/shard_map/norm/pallas_call | solution.py:502
  47.6 4.5 %collective-permute-done.12.refs_10_ = bf16[4,96,384]{2,1,0:T(8,128)(2,1)S(1)} collective-permute-done((bf16[4,96,384]{2,1,0:T(8,128)(2,1)S(1)}, bf16[4,96,384]{2,1,0:T(8,128)(2,1)S(1)}, u32[]{:S(2)}, u32[]{:S(2)}) %collective-permute-start.12) | collective-permute-done | bytes 294944 | tf_op jit(solution)/shard_map/ppermute | solution.py:46
  52.1 2.7 %step0a.1 = (bf16[768,128]{1,0:T(8,128)(2,1)S(1)}, bf16[512,256]{1,0:T(8,128)(2,1)S(1)}, bf16[1536,384]{1,0:T(8,128)(2,1)S(1)}) custom-call(f32[1,16]{1,0:T(1,128)S(1)} %copy-done.8, s32[1,4]{1,0:T(1,128)S(1)} %bitcast.6, f32[1,1536]{1,0:T(1,128)S(1)} %copy-done.1, f32[1,1536]{1,0:T(1,128)S(1)} %copy-done.2, ...), custom_call_target="tpu_custom_call", output_to_operand_aliasing={{2}: (11, {})} | custom-call | flops 805306368 | bytes 1572864 | tf_op jit(solution)/shard_map/step0a/pallas_call | solution.py:502
  54.9 1.6 %collective-permute-start.13 = (bf16[768,128]{1,0:T(8,128)(2,1)S(1)}, bf16[768,128]{1,0:T(8,128)(2,1)S(1)}, u32[]{:S(2)}, u32[]{:S(2)}) collective-permute-start(bf16[768,128]{1,0:T(8,128)(2,1)S(1)} %get-tuple-element.51), channel_id=1, source_target_pairs={{0,16},{16,0},{1,17},{17,1},{2,18},{18,2},{3,19},{19,3},{4,20},{20... | collective-permute-start | bytes 589832 | tf_op jit(solution)/shard_map/ppermute | solution.py:31
  56.5 0.6 collective-permute-start.11
  57.1 2.7 %step1a.1 = (bf16[768,128]{1,0:T(8,128)(2,1)S(1)}, bf16[512,256]{1,0:T(8,128)(2,1)S(1)}) custom-call(f32[1,16]{1,0:T(1,128)S(1)} %copy-done.8, s32[1,4]{1,0:T(1,128)S(1)} %bitcast.7, f32[1,1536]{1,0:T(1,128)S(1)} %copy-done.1, f32[1,1536]{1,0:T(1,128)S(1)} %copy-done.2, f32[1,1536]{1,0:T(1,128)S(1)} %copy-done.4, s32[4,1,512]{2,1,0:T(1,128)S(1)} %copy-done.3, ...), custom_call_target="tpu_custom_call" | custom-call | flops 805306368 | bytes 1572864 | tf_op jit(solution)/shard_map/step1a/pallas_call | solution.py:502
  59.7 1.7 %collective-permute-done.13.refs_1_.refs_10_ = bf16[768,128]{1,0:T(8,128)(2,1)S(1)} collective-permute-done((bf16[768,128]{1,0:T(8,128)(2,1)S(1)}, bf16[768,128]{1,0:T(8,128)(2,1)S(1)}, u32[]{:S(2)}, u32[]{:S(2)}) %collective-permute-start.13) | collective-permute-done | bytes 196640 | tf_op jit(solution)/shard_map/ppermute | solution.py:31
  61.4 1.5 %collective-permute-start.15 = (bf16[768,128]{1,0:T(8,128)(2,1)S(1)}, bf16[768,128]{1,0:T(8,128)(2,1)S(1)}, u32[]{:S(2)}, u32[]{:S(2)}) collective-permute-start(bf16[768,128]{1,0:T(8,128)(2,1)S(1)} %tie.6), channel_id=1, source_target_pairs={{0,16},{16,0},{1,17},{17,1},{2,18},{18,2},{3,19},{19,3},{4,20},{20... | collective-permute-start | bytes 589832 | tf_op jit(solution)/shard_map/ppermute | solution.py:31
  63.0 0.5 collective-permute-start.14
  63.6 2.1 %collective-permute-done.11.refs_0_ = bf16[4,96,384]{2,1,0:T(8,128)(2,1)S(1)} collective-permute-done((bf16[4,96,384]{2,1,0:T(8,128)(2,1)S(1)}, bf16[4,96,384]{2,1,0:T(8,128)(2,1)S(1)}, u32[]{:S(2)}, u32[]{:S(2)}) %collective-permute-start.11) | collective-permute-done | bytes 294944 | tf_op jit(solution)/shard_map/ppermute | solution.py:46
  65.7 1.4 %collective-permute-done.15.refs_2_.refs_0_ = bf16[768,128]{1,0:T(8,128)(2,1)S(1)} collective-permute-done((bf16[768,128]{1,0:T(8,128)(2,1)S(1)}, bf16[768,128]{1,0:T(8,128)(2,1)S(1)}, u32[]{:S(2)}, u32[]{:S(2)}) %collective-permute-start.15) | collective-permute-done | bytes 196640 | tf_op jit(solution)/shard_map/ppermute | solution.py:31
  67.1 1.5 %collective-permute-done.14.refs_1_.refs_11_ = bf16[768,128]{1,0:T(8,128)(2,1)S(1)} collective-permute-done((bf16[768,128]{1,0:T(8,128)(2,1)S(1)}, bf16[768,128]{1,0:T(8,128)(2,1)S(1)}, u32[]{:S(2)}, u32[]{:S(2)}) %collective-permute-start.14) | collective-permute-done | bytes 196640 | tf_op jit(solution)/shard_map/ppermute | solution.py:27
  68.6 2.8 %step0b.1 = (bf16[768,128]{1,0:T(8,128)(2,1)S(1)}, bf16[4,128,384]{2,1,0:T(8,128)(2,1)S(1)}, bf16[1536,384]{1,0:T(8,128)(2,1)S(1)}) custom-call(f32[1,16]{1,0:T(1,128)S(1)} %copy-done.8, s32[1,4]{1,0:T(1,128)S(1)} %bitcast.8, f32[1,1536]{1,0:T(1,128)S(1)} %copy-done.1, f32[1,1536]{1,0:T(1,128)S(1)} %copy-done.2, ...), custom_call_target="tpu_custom_call", output_to_operand_aliasing={{2}: (11, {})} | custom-call | flops 805306368 | bytes 1572864 | tf_op jit(solution)/shard_map/step0b/pallas_call | solution.py:502
  71.4 0.1 beside.1
  71.5 0.1 collective-permute-start.16
  71.6 0.6 collective-permute-start.19
  72.2 0.6 collective-permute-start.20
  72.8 2.7 %step1b.1 = (bf16[768,128]{1,0:T(8,128)(2,1)S(1)}, bf16[4,128,384]{2,1,0:T(8,128)(2,1)S(1)}) custom-call(f32[1,16]{1,0:T(1,128)S(1)} %copy-done.8, s32[1,4]{1,0:T(1,128)S(1)} %bitcast.9, f32[1,1536]{1,0:T(1,128)S(1)} %copy-done.1, f32[1,1536]{1,0:T(1,128)S(1)} %copy-done.2, f32[1,1536]{1,0:T(1,128)S(1)} %copy-done.4, s32[4,1,512]{2,1,0:T(1,128)S(1)} %copy-done.3, ...), custom_call_target="tpu_custom_call" | custom-call | flops 805306368 | bytes 1572864 | tf_op jit(solution)/shard_map/step1b/pallas_call | solution.py:502
  75.5 3.4 %collective-permute-done.19.refs_0_ = bf16[768,128]{1,0:T(8,128)(2,1)S(1)} collective-permute-done((bf16[768,128]{1,0:T(8,128)(2,1)S(1)}, bf16[768,128]{1,0:T(8,128)(2,1)S(1)}, u32[]{:S(2)}, u32[]{:S(2)}) %collective-permute-start.19) | collective-permute-done | bytes 196640 | tf_op jit(solution)/shard_map/ppermute | solution.py:31
  78.9 0.2 collective-permute-done.20.refs_2_.refs_1_
  79.2 0.6 collective-permute-start.21
  79.8 1.5 %collective-permute-start.24 = (bf16[768,128]{1,0:T(8,128)(2,1)S(1)}, bf16[768,128]{1,0:T(8,128)(2,1)S(1)}, u32[]{:S(2)}, u32[]{:S(2)}) collective-permute-start(bf16[768,128]{1,0:T(8,128)(2,1)S(1)} %get-tuple-element.65), channel_id=1, source_target_pairs={{0,16},{16,0},{1,17},{17,1},{2,18},{18,2},{3,19},{19,3},{4,20},{20... | collective-permute-start | bytes 589832 | tf_op jit(solution)/shard_map/ppermute | solution.py:31
  81.2 0.5 collective-permute-start.22
  81.7 3.7 %collective-permute-done.21.refs_15_ = bf16[768,128]{1,0:T(8,128)(2,1)S(1)} collective-permute-done((bf16[768,128]{1,0:T(8,128)(2,1)S(1)}, bf16[768,128]{1,0:T(8,128)(2,1)S(1)}, u32[]{:S(2)}, u32[]{:S(2)}) %collective-permute-start.21) | collective-permute-done | bytes 196640 | tf_op jit(solution)/shard_map/ppermute | solution.py:27
  85.4 0.3 collective-permute-done.24.refs_2_
  85.7 1.5 %collective-permute-start.25 = (bf16[768,128]{1,0:T(8,128)(2,1)S(1)}, bf16[768,128]{1,0:T(8,128)(2,1)S(1)}, u32[]{:S(2)}, u32[]{:S(2)}) collective-permute-start(bf16[768,128]{1,0:T(8,128)(2,1)S(1)} %collective-permute-done.24.refs_2_), channel_id=1, source_target_pairs={{0,8},{4,12},{8,0},{12,4},{1,9},{5,13},{9,1},{13,5},{2,10},{6,14},... | collective-permute-start | bytes 589832 | tf_op jit(solution)/shard_map/ppermute | solution.py:27
  87.2 4.9 %step2ab.1.refs_2_.refs_0_ = bf16[4,128,384]{2,1,0:T(8,128)(2,1)S(1)} custom-call(f32[1,16]{1,0:T(1,128)S(1)} %copy-done.8, s32[1,4]{1,0:T(1,128)S(1)} %bitcast.10, f32[1,1536]{1,0:T(1,128)S(1)} %copy-done.1, f32[1,1536]{1,0:T(1,128)S(1)} %copy-done.2, f32[1,1536]{1,0:T(1,128)S(1)} %copy-done.4, s32[4,1,512]{2,1,0:T(1,128)S(1)} %copy-done.3, ...), custom_call_target="tpu_custom_call" | custom-call | flops 1610612736 | bytes 3145728 | tf_op jit(solution)/shard_map/step2ab/pallas_call | solution.py:502
  92.0 0.5 early.1
  92.5 0.2 collective-permute-done.25.refs_3_
  92.7 0.5 collective-permute-start.27
  93.3 0.5 collective-permute-start.29
  93.8 0.4 collective-permute-done.26.refs_12_
  94.2 0.5 collective-permute-start.31
  94.7 1.0 collective-permute-start.32
  95.7 4.7 %step3ab.1.refs_1_ = bf16[4,128,384]{2,1,0:T(8,128)(2,1)S(1)} custom-call(f32[1,16]{1,0:T(1,128)S(1)} %copy-done.8, s32[1,4]{1,0:T(1,128)S(1)} %bitcast.11, f32[1,1536]{1,0:T(1,128)S(1)} %copy-done.1, f32[1,1536]{1,0:T(1,128)S(1)} %copy-done.2, f32[1,1536]{1,0:T(1,128)S(1)} %copy-done.4, s32[4,1,512]{2,1,0:T(1,128)S(1)} %copy-done.3, ...), custom_call_target="tpu_custom_call" | custom-call | flops 1610612736 | bytes 3145728 | tf_op jit(solution)/shard_map/step3ab/pallas_call | solution.py:502
  100.4 1.6 %collective-permute-done.31.refs_7_ = bf16[2,128,384]{2,1,0:T(8,128)(2,1)S(1)} collective-permute-done((bf16[2,128,384]{2,1,0:T(8,128)(2,1)S(1)}, bf16[2,128,384]{2,1,0:T(8,128)(2,1)S(1)}, u32[]{:S(2)}, u32[]{:S(2)}) %collective-permute-start.31) | collective-permute-done | bytes 196640 | tf_op jit(solution)/shard_map/ppermute | solution.py:27
  101.9 1.2 %settle.1 = (bf16[128,384]{1,0:T(8,128)(2,1)S(1)}, bf16[128,384]{1,0:T(8,128)(2,1)S(1)}, bf16[128,384]{1,0:T(8,128)(2,1)S(1)}, bf16[128,384]{1,0:T(8,128)(2,1)S(...) custom-call(bf16[4,128,384]{2,1,0:T(8,128)(2,1)S(1)} %step2ab.1.refs, ...), custom_call_target="tpu_custom_call" | custom-call | tf_op jit(solution)/shard_map/settle/pallas_call | solution.py:502
  103.2 0.9 collective-permute-start.36
  104.1 0.5 collective-permute-start.34
  104.5 1.4 %collective-permute-start.35 = (bf16[128,384]{1,0:T(8,128)(2,1)S(1)}, bf16[128,384]{1,0:T(8,128)(2,1)S(1)}, u32[]{:S(2)}, u32[]{:S(2)}) collective-permute-start(bf16[128,384]{1,0:T(8,128)(2,1)S(1)} %get-tuple-element.79), channel_id=1, source_target_pairs={{0,12},{4,8},{8,4},{12,0},{1,13},{5,9},{9,5},{13,1},{2,14},{6,10},... | collective-permute-start | bytes 294920 | tf_op jit(solution)/shard_map/ppermute | solution.py:27
  105.9 1.9 %collective-permute-start.37 = (bf16[96,256]{1,0:T(8,128)(2,1)S(1)}, bf16[96,256]{1,0:T(8,128)(2,1)S(1)}, u32[]{:S(2)}, u32[]{:S(2)}) collective-permute-start(bf16[96,256]{1,0:T(8,128)(2,1)S(1)} %get-tuple-element.82), channel_id=1, source_target_pairs={{0,2},{1,3},{2,0},{3,1},{4,6},{5,7},{6,4},{7,5},{8,10},{9,11},{10,... | collective-permute-start | bytes 147464 | tf_op jit(solution)/shard_map/ppermute | solution.py:36
  107.8 1.3 %collective-permute-done.36.refs_7_ = bf16[96,256]{1,0:T(8,128)(2,1)S(1)} collective-permute-done((bf16[96,256]{1,0:T(8,128)(2,1)S(1)}, bf16[96,256]{1,0:T(8,128)(2,1)S(1)}, u32[]{:S(2)}, u32[]{:S(2)}) %collective-permute-start.36) | collective-permute-done | bytes 49184 | tf_op jit(solution)/shard_map/ppermute | solution.py:36
  109.1 0.3 collective-permute-start.38
  109.4 2.7 %collective-permute-done.37.refs_8_ = bf16[96,256]{1,0:T(8,128)(2,1)S(1)} collective-permute-done((bf16[96,256]{1,0:T(8,128)(2,1)S(1)}, bf16[96,256]{1,0:T(8,128)(2,1)S(1)}, u32[]{:S(2)}, u32[]{:S(2)}) %collective-permute-start.37) | collective-permute-done | bytes 49184 | tf_op jit(solution)/shard_map/ppermute | solution.py:36
  112.1 1.1 collective-permute-done.38.refs_9_
  113.2 1.5 %finish.1 = (bf16[3,128,1536]{2,1,0:T(8,128)(2,1)}, f32[96,256]{1,0:T(8,128)}) custom-call(bf16[3,128,1536]{2,1,0:T(8,128)(2,1)} %get-tuple-element.74.refs_0_, bf16[2,128,384]{2,1,0:T(8,128)(2,1)S(1)} %collective-permute-done.32.refs_1_, bf16[128,384]{1,0:T(8,128)(2,1)S(1)} %get-tuple-element.76.refs_2_, ...), custom_call_target="tpu_custom_call", output_to_operand_aliasing={{0}: (0, {})} | custom-call | tf_op jit(solution)/shard_map/finish/pallas_call | solution.py:502
  (59 shorter events, 0.5 us)
Async XLA Ops:
  0.6 14.4 %copy-start = (bf16[1,3,1,128,1536]{4,3,2,1,0:T(8,128)(2,1)S(1)}, bf16[1,3,1,128,1536]{4,3,2,1,0:T(8,128)(2,1)}, u32[]{:S(2)}) copy-start(bf16[1,3,1,128,1536]{4,3,2,1,0:T(8,128)(2,1)} %incoming.3) | copy-start | bytes 3538948
  0.6 14.4 %copy-start.9 = (s32[4,1,128]{2,1,0:T(1,128)S(1)}, s32[4,1,128]{2,1,0:T(1,128)}, u32[]{:S(2)}) copy-start(s32[4,1,128]{2,1,0:T(1,128)} %contacts.1) | copy-start | bytes 6148
  2.1 1.5 %collective-permute-start = (bf16[2,96,384]{2,1,0:T(8,128)(2,1)S(1)}, bf16[2,96,384]{2,1,0:T(8,128)(2,1)S(1)}, u32[]{:S(2)}, u32[]{:S(2)}) collective-permute-start(bf16[2,96,384]{2,1,0:T(8,128)(2,1)S(1)} %get-tuple-element.45), channel_id=1, source_target_pairs={{0,4},{4,0},{8,12},{12,8},{1,5},{5,1},{9,13},{13,9},{2,6},{6,2},{1... | collective-permute-start | bytes 442376 | tf_op jit(solution)/shard_map/ppermute | solution.py:27
  3.7 11.3 %collective-permute-start.1 = (bf16[2,2,96,384]{3,2,1,0:T(8,128)(2,1)S(1)}, bf16[2,2,96,384]{3,2,1,0:T(8,128)(2,1)S(1)}, u32[]{:S(2)}, u32[]{:S(2)}) collective-permute-start(bf16[2,2,96,384]{3,2,1,0:T(8,128)(2,1)S(1)} %near.1), channel_id=1, source_target_pairs={{0,1},{1,3},{3,2},{2,0},{4,5},{5,7},{7,6},{6,4},{8,9},{9,11},{11,1... | collective-permute-start | bytes 884744 | tf_op jit(solution)/shard_map/ppermute | solution.py:46
  6.7 6.7 %collective-permute-start.2 = (bf16[2,96,384]{2,1,0:T(8,128)(2,1)S(1)}, bf16[2,96,384]{2,1,0:T(8,128)(2,1)S(1)}, u32[]{:S(2)}, u32[]{:S(2)}) collective-permute-start(bf16[2,96,384]{2,1,0:T(8,128)(2,1)S(1)} %get-tuple-element.46), channel_id=1, source_target_pairs={{0,8},{4,12},{8,0},{12,4},{1,9},{5,13},{9,1},{13,5},{2,10},{6,14},... | collective-permute-start | bytes 442376 | tf_op jit(solution)/shard_map/ppermute | solution.py:27
  8.2 6.3 %collective-permute-start.3 = (bf16[2,96,384]{2,1,0:T(8,128)(2,1)S(1)}, bf16[2,96,384]{2,1,0:T(8,128)(2,1)S(1)}, u32[]{:S(2)}, u32[]{:S(2)}) collective-permute-start(bf16[2,96,384]{2,1,0:T(8,128)(2,1)S(1)} %get-tuple-element.47), channel_id=1, source_target_pairs={{0,12},{4,8},{8,4},{12,0},{1,13},{5,9},{9,5},{13,1},{2,14},{6,10},... | collective-permute-start | bytes 442376 | tf_op jit(solution)/shard_map/ppermute | solution.py:27
  15.1 26.7 %collective-permute-start.4 = (bf16[272,1536]{1,0:T(8,128)(2,1)S(1)}, bf16[272,1536]{1,0:T(8,128)(2,1)S(1)}, u32[]{:S(2)}, u32[]{:S(2)}) collective-permute-start(bf16[272,1536]{1,0:T(8,128)(2,1)S(1)} %first.1.refs_0_), channel_id=1, source_target_pairs={{0,8},{4,12},{8,0},{12,4},{1,9},{5,13},{9,1},{13,5},{2,10},{6,14},... | collective-permute-start | bytes 2506760 | tf_op jit(solution)/shard_map/ppermute | solution.py:27
  16.7 9.8 %collective-permute-start.5 = (bf16[2,2,96,384]{3,2,1,0:T(8,128)(2,1)S(1)}, bf16[2,2,96,384]{3,2,1,0:T(8,128)(2,1)S(1)}, u32[]{:S(2)}, u32[]{:S(2)}) collective-permute-start(bf16[2,2,96,384]{3,2,1,0:T(8,128)(2,1)S(1)} %far.1), channel_id=1, source_target_pairs={{0,1},{1,3},{3,2},{2,0},{4,5},{5,7},{7,6},{6,4},{8,9},{9,11},{11,1... | collective-permute-start | bytes 884744 | tf_op jit(solution)/shard_map/ppermute | solution.py:46
  26.5 10.9 %collective-permute-start.6 = (bf16[4,96,384]{2,1,0:T(8,128)(2,1)S(1)}, bf16[4,96,384]{2,1,0:T(8,128)(2,1)S(1)}, u32[]{:S(2)}, u32[]{:S(2)}) collective-permute-start(bf16[4,96,384]{2,1,0:T(8,128)(2,1)S(1)} %part0.1.chunk), channel_id=1, source_target_pairs={{0,1},{1,3},{3,2},{2,0},{4,5},{5,7},{7,6},{6,4},{8,9},{9,11},{11,1... | collective-permute-start | bytes 884744 | tf_op jit(solution)/shard_map/ppermute | solution.py:46
  28.3 15.1 %copy-start.5 = (bf16[1,3,1,128,256]{4,3,2,1,0:T(8,128)(2,1)S(1)}, bf16[1,3,1,128,256]{4,3,2,1,0:T(8,128)(2,1)}, u32[]{:S(2)}) copy-start(bf16[1,3,1,128,256]{4,3,2,1,0:T(8,128)(2,1)} %cotangent.1) | copy-start | bytes 589828
  28.3 13.5 %collective-permute-start.7 = (bf16[4,96,384]{2,1,0:T(8,128)(2,1)S(1)}, bf16[4,96,384]{2,1,0:T(8,128)(2,1)S(1)}, u32[]{:S(2)}, u32[]{:S(2)}) collective-permute-start(bf16[4,96,384]{2,1,0:T(8,128)(2,1)S(1)} %part1.1.chunk), channel_id=1, source_target_pairs={{0,1},{1,3},{3,2},{2,0},{4,5},{5,7},{7,6},{6,4},{8,9},{9,11},{11,1... | collective-permute-start | bytes 884744 | tf_op jit(solution)/shard_map/ppermute | solution.py:46
  30.0 14.1 %collective-permute-start.9 = (bf16[272,1536]{1,0:T(8,128)(2,1)S(1)}, bf16[272,1536]{1,0:T(8,128)(2,1)S(1)}, u32[]{:S(2)}, u32[]{:S(2)}) collective-permute-start(bf16[272,1536]{1,0:T(8,128)(2,1)S(1)} %first.1.refs_0_), channel_id=1, source_target_pairs={{0,4},{4,0},{8,12},{12,8},{1,5},{5,1},{9,13},{13,9},{2,6},{6,2},{1... | collective-permute-start | bytes 2506760 | tf_op jit(solution)/shard_map/ppermute | solution.py:27
  41.8 2.4 %collective-permute-start.10 = (bf16[272,1536]{1,0:T(8,128)(2,1)S(1)}, bf16[272,1536]{1,0:T(8,128)(2,1)S(1)}, u32[]{:S(2)}, u32[]{:S(2)}) collective-permute-start(bf16[272,1536]{1,0:T(8,128)(2,1)S(1)} %tie.5.dep.refs_1_), channel_id=1, source_target_pairs={{0,4},{4,0},{8,12},{12,8},{1,5},{5,1},{9,13},{13,9},{2,6},{6,2},{1... | collective-permute-start | bytes 2506760 | tf_op jit(solution)/shard_map/ppermute | solution.py:27
  41.8 10.3 %collective-permute-start.12 = (bf16[4,96,384]{2,1,0:T(8,128)(2,1)S(1)}, bf16[4,96,384]{2,1,0:T(8,128)(2,1)S(1)}, u32[]{:S(2)}, u32[]{:S(2)}) collective-permute-start(bf16[4,96,384]{2,1,0:T(8,128)(2,1)S(1)} %collective-permute-done.6.refs_1_.refs_9_), channel_id=1, source_target_pairs={{0,1},{1,3},{3,2},{2,0},{4,5},{5,7},{7,6},{6,4},{8,9},{9,11},{11,1... | collective-permute-start | bytes 884744 | tf_op jit(solution)/shard_map/ppermute | solution.py:46
  43.4 0.8 copy-start.1
  43.4 0.7 copy-start.2
  43.4 0.8 copy-start.6
  43.5 0.8 copy-start.7
  43.5 28.0 %collective-permute-start.8 = (bf16[256,1536]{1,0:T(8,128)(2,1)S(1)}, bf16[256,1536]{1,0:T(8,128)(2,1)S(1)}, u32[]{:S(2)}, u32[]{:S(2)}) collective-permute-start(bf16[256,1536]{1,0:T(8,128)(2,1)S(1)} %second.1.mine.refs_6_.refs_3_.refs_2_), channel_id=1, source_target_pairs={{0,8},{4,12},{8,0},{12,4},{1,9},{5,13},{9,1},{13,5},{2,10},{6,14},... | collective-permute-start | bytes 2359304 | tf_op jit(solution)/shard_map/ppermute | solution.py:27
  44.3 7.9 %copy-start.3 = (s32[4,1,512]{2,1,0:T(1,128)S(1)}, s32[4,1,512]{2,1,0:T(1,128)}, u32[]{:S(2)}) copy-start(s32[4,1,512]{2,1,0:T(1,128)} %refs_5_.11) | copy-start | bytes 24580
  44.3 7.9 %copy-start.4 = (f32[1,1536]{1,0:T(1,128)S(1)}, f32[1,1536]{1,0:T(1,128)}, u32[]{:S(2)}) copy-start(f32[1,1536]{1,0:T(1,128)} %refs_4_.11) | copy-start | bytes 18436
  44.3 7.9 %copy-start.8 = (f32[1,16]{1,0:T(1,128)S(1)}, f32[1,16]{1,0:T(1,128)}, u32[]{:S(2)}) copy-start(f32[1,16]{1,0:T(1,128)} %refs_0_.11) | copy-start | bytes 196
  54.9 6.5 %collective-permute-start.13 = (bf16[768,128]{1,0:T(8,128)(2,1)S(1)}, bf16[768,128]{1,0:T(8,128)(2,1)S(1)}, u32[]{:S(2)}, u32[]{:S(2)}) collective-permute-start(bf16[768,128]{1,0:T(8,128)(2,1)S(1)} %get-tuple-element.51), channel_id=1, source_target_pairs={{0,16},{16,0},{1,17},{17,1},{2,18},{18,2},{3,19},{19,3},{4,20},{20... | collective-permute-start | bytes 589832 | tf_op jit(solution)/shard_map/ppermute | solution.py:31
  56.5 9.2 %collective-permute-start.11 = (bf16[4,96,384]{2,1,0:T(8,128)(2,1)S(1)}, bf16[4,96,384]{2,1,0:T(8,128)(2,1)S(1)}, u32[]{:S(2)}, u32[]{:S(2)}) collective-permute-start(bf16[4,96,384]{2,1,0:T(8,128)(2,1)S(1)} %collective-permute-done.7.refs_2_.refs_9_), channel_id=1, source_target_pairs={{0,1},{1,3},{3,2},{2,0},{4,5},{5,7},{7,6},{6,4},{8,9},{9,11},{11,1... | collective-permute-start | bytes 884744 | tf_op jit(solution)/shard_map/ppermute | solution.py:46
  61.4 5.7 %collective-permute-start.15 = (bf16[768,128]{1,0:T(8,128)(2,1)S(1)}, bf16[768,128]{1,0:T(8,128)(2,1)S(1)}, u32[]{:S(2)}, u32[]{:S(2)}) collective-permute-start(bf16[768,128]{1,0:T(8,128)(2,1)S(1)} %tie.6), channel_id=1, source_target_pairs={{0,16},{16,0},{1,17},{17,1},{2,18},{18,2},{3,19},{19,3},{4,20},{20... | collective-permute-start | bytes 589832 | tf_op jit(solution)/shard_map/ppermute | solution.py:31
  63.0 5.7 %collective-permute-start.14 = (bf16[768,128]{1,0:T(8,128)(2,1)S(1)}, bf16[768,128]{1,0:T(8,128)(2,1)S(1)}, u32[]{:S(2)}, u32[]{:S(2)}) collective-permute-start(bf16[768,128]{1,0:T(8,128)(2,1)S(1)} %collective-permute-done.13.refs_1_.refs_10_), channel_id=1, source_target_pairs={{0,8},{4,12},{8,0},{12,4},{1,9},{5,13},{9,1},{13,5},{2,10},{6,14},... | collective-permute-start | bytes 589832 | tf_op jit(solution)/shard_map/ppermute | solution.py:27
  71.5 15.6 %collective-permute-start.16 = (bf16[2,256,1536]{2,1,0:T(8,128)(2,1)S(1)}, bf16[2,256,1536]{2,1,0:T(8,128)(2,1)S(1)}, u32[]{:S(2)}, u32[]{:S(2)}) collective-permute-start(bf16[2,256,1536]{2,1,0:T(8,128)(2,1)S(1)} %beside.1), channel_id=1, source_target_pairs={{0,4},{4,0},{8,12},{12,8},{1,5},{5,1},{9,13},{13,9},{2,6},{6,2},{1... | collective-permute-start | bytes 4718600 | tf_op jit(solution)/shard_map/ppermute | solution.py:27
  71.6 7.3 %collective-permute-start.19 = (bf16[768,128]{1,0:T(8,128)(2,1)S(1)}, bf16[768,128]{1,0:T(8,128)(2,1)S(1)}, u32[]{:S(2)}, u32[]{:S(2)}) collective-permute-start(bf16[768,128]{1,0:T(8,128)(2,1)S(1)} %get-tuple-element.60), channel_id=1, source_target_pairs={{0,16},{16,0},{1,17},{17,1},{2,18},{18,2},{3,19},{19,3},{4,20},{20... | collective-permute-start | bytes 589832 | tf_op jit(solution)/shard_map/ppermute | solution.py:31
  72.2 7.0 %collective-permute-start.20 = (bf16[768,128]{1,0:T(8,128)(2,1)S(1)}, bf16[768,128]{1,0:T(8,128)(2,1)S(1)}, u32[]{:S(2)}, u32[]{:S(2)}) collective-permute-start(bf16[768,128]{1,0:T(8,128)(2,1)S(1)} %collective-permute-done.15.refs_2_.refs_0_), channel_id=1, source_target_pairs={{0,8},{4,12},{8,0},{12,4},{1,9},{5,13},{9,1},{13,5},{2,10},{6,14},... | collective-permute-start | bytes 589832 | tf_op jit(solution)/shard_map/ppermute | solution.py:27
  72.8 8.4 %collective-permute-start.17 = (bf16[768,128]{1,0:T(8,128)(2,1)S(1)}, bf16[768,128]{1,0:T(8,128)(2,1)S(1)}, u32[]{:S(2)}, u32[]{:S(2)}) collective-permute-start(bf16[768,128]{1,0:T(8,128)(2,1)S(1)} %collective-permute-done.13.refs_1_.refs_10_), channel_id=1, source_target_pairs={{0,4},{4,0},{8,12},{12,8},{1,5},{5,1},{9,13},{13,9},{2,6},{6,2},{1... | collective-permute-start | bytes 589832 | tf_op jit(solution)/shard_map/ppermute | solution.py:27
  79.2 6.2 %collective-permute-start.21 = (bf16[768,128]{1,0:T(8,128)(2,1)S(1)}, bf16[768,128]{1,0:T(8,128)(2,1)S(1)}, u32[]{:S(2)}, u32[]{:S(2)}) collective-permute-start(bf16[768,128]{1,0:T(8,128)(2,1)S(1)} %tie.8.refs_14_), channel_id=1, source_target_pairs={{0,8},{4,12},{8,0},{12,4},{1,9},{5,13},{9,1},{13,5},{2,10},{6,14},... | collective-permute-start | bytes 589832 | tf_op jit(solution)/shard_map/ppermute | solution.py:27
  79.8 5.9 %collective-permute-start.24 = (bf16[768,128]{1,0:T(8,128)(2,1)S(1)}, bf16[768,128]{1,0:T(8,128)(2,1)S(1)}, u32[]{:S(2)}, u32[]{:S(2)}) collective-permute-start(bf16[768,128]{1,0:T(8,128)(2,1)S(1)} %get-tuple-element.65), channel_id=1, source_target_pairs={{0,16},{16,0},{1,17},{17,1},{2,18},{18,2},{3,19},{19,3},{4,20},{20... | collective-permute-start | bytes 589832 | tf_op jit(solution)/shard_map/ppermute | solution.py:31
  81.2 5.9 %collective-permute-start.18 = (bf16[768,128]{1,0:T(8,128)(2,1)S(1)}, bf16[768,128]{1,0:T(8,128)(2,1)S(1)}, u32[]{:S(2)}, u32[]{:S(2)}) collective-permute-start(bf16[768,128]{1,0:T(8,128)(2,1)S(1)} %collective-permute-done.14.refs_1_.refs_11_), channel_id=1, source_target_pairs={{0,4},{4,0},{8,12},{12,8},{1,5},{5,1},{9,13},{13,9},{2,6},{6,2},{1... | collective-permute-start | bytes 589832 | tf_op jit(solution)/shard_map/ppermute | solution.py:27
  81.2 5.9 %collective-permute-start.22 = (bf16[768,128]{1,0:T(8,128)(2,1)S(1)}, bf16[768,128]{1,0:T(8,128)(2,1)S(1)}, u32[]{:S(2)}, u32[]{:S(2)}) collective-permute-start(bf16[768,128]{1,0:T(8,128)(2,1)S(1)} %tie.8.refs_14_), channel_id=1, source_target_pairs={{0,4},{4,0},{8,12},{12,8},{1,5},{5,1},{9,13},{13,9},{2,6},{6,2},{1... | collective-permute-start | bytes 589832 | tf_op jit(solution)/shard_map/ppermute | solution.py:27
  85.4 1.8 %collective-permute-start.23 = (bf16[768,128]{1,0:T(8,128)(2,1)S(1)}, bf16[768,128]{1,0:T(8,128)(2,1)S(1)}, u32[]{:S(2)}, u32[]{:S(2)}) collective-permute-start(bf16[768,128]{1,0:T(8,128)(2,1)S(1)} %collective-permute-done.21.refs_15_), channel_id=1, source_target_pairs={{0,4},{4,0},{8,12},{12,8},{1,5},{5,1},{9,13},{13,9},{2,6},{6,2},{1... | collective-permute-start | bytes 589832 | tf_op jit(solution)/shard_map/ppermute | solution.py:27
  85.7 7.1 %collective-permute-start.25 = (bf16[768,128]{1,0:T(8,128)(2,1)S(1)}, bf16[768,128]{1,0:T(8,128)(2,1)S(1)}, u32[]{:S(2)}, u32[]{:S(2)}) collective-permute-start(bf16[768,128]{1,0:T(8,128)(2,1)S(1)} %collective-permute-done.24.refs_2_), channel_id=1, source_target_pairs={{0,8},{4,12},{8,0},{12,4},{1,9},{5,13},{9,1},{13,5},{2,10},{6,14},... | collective-permute-start | bytes 589832 | tf_op jit(solution)/shard_map/ppermute | solution.py:27
  92.7 1.4 %collective-permute-start.26 = (bf16[768,128]{1,0:T(8,128)(2,1)S(1)}, bf16[768,128]{1,0:T(8,128)(2,1)S(1)}, u32[]{:S(2)}, u32[]{:S(2)}) collective-permute-start(bf16[768,128]{1,0:T(8,128)(2,1)S(1)} %get-tuple-element.67.refs_10_), channel_id=1, source_target_pairs={{0,4},{4,0},{8,12},{12,8},{1,5},{5,1},{9,13},{13,9},{2,6},{6,2},{1... | collective-permute-start | bytes 589832 | tf_op jit(solution)/shard_map/ppermute | solution.py:27
  92.7 2.0 %collective-permute-start.27 = (bf16[768,128]{1,0:T(8,128)(2,1)S(1)}, bf16[768,128]{1,0:T(8,128)(2,1)S(1)}, u32[]{:S(2)}, u32[]{:S(2)}) collective-permute-start(bf16[768,128]{1,0:T(8,128)(2,1)S(1)} %get-tuple-element.68.refs_11_), channel_id=1, source_target_pairs={{0,4},{4,0},{8,12},{12,8},{1,5},{5,1},{9,13},{13,9},{2,6},{6,2},{1... | collective-permute-start | bytes 589832 | tf_op jit(solution)/shard_map/ppermute | solution.py:27
  93.2 2.4 %collective-permute-start.28 = (bf16[768,128]{1,0:T(8,128)(2,1)S(1)}, bf16[768,128]{1,0:T(8,128)(2,1)S(1)}, u32[]{:S(2)}, u32[]{:S(2)}) collective-permute-start(bf16[768,128]{1,0:T(8,128)(2,1)S(1)} %get-tuple-element.69.refs_14_), channel_id=1, source_target_pairs={{0,4},{4,0},{8,12},{12,8},{1,5},{5,1},{9,13},{13,9},{2,6},{6,2},{1... | collective-permute-start | bytes 589832 | tf_op jit(solution)/shard_map/ppermute | solution.py:27
  93.3 2.4 %collective-permute-start.29 = (bf16[768,128]{1,0:T(8,128)(2,1)S(1)}, bf16[768,128]{1,0:T(8,128)(2,1)S(1)}, u32[]{:S(2)}, u32[]{:S(2)}) collective-permute-start(bf16[768,128]{1,0:T(8,128)(2,1)S(1)} %get-tuple-element.70.refs_15_), channel_id=1, source_target_pairs={{0,4},{4,0},{8,12},{12,8},{1,5},{5,1},{9,13},{13,9},{2,6},{6,2},{1... | collective-permute-start | bytes 589832 | tf_op jit(solution)/shard_map/ppermute | solution.py:27
  93.8 6.6 %collective-permute-start.30 = (bf16[2,128,384]{2,1,0:T(8,128)(2,1)S(1)}, bf16[2,128,384]{2,1,0:T(8,128)(2,1)S(1)}, u32[]{:S(2)}, u32[]{:S(2)}) collective-permute-start(bf16[2,128,384]{2,1,0:T(8,128)(2,1)S(1)} %get-tuple-element.72), channel_id=1, source_target_pairs={{0,4},{4,0},{8,12},{12,8},{1,5},{5,1},{9,13},{13,9},{2,6},{6,2},{1... | collective-permute-start | bytes 589832 | tf_op jit(solution)/shard_map/ppermute | solution.py:27
  94.2 7.7 %collective-permute-start.31 = (bf16[2,128,384]{2,1,0:T(8,128)(2,1)S(1)}, bf16[2,128,384]{2,1,0:T(8,128)(2,1)S(1)}, u32[]{:S(2)}, u32[]{:S(2)}) collective-permute-start(bf16[2,128,384]{2,1,0:T(8,128)(2,1)S(1)} %get-tuple-element.73), channel_id=1, source_target_pairs={{0,8},{4,12},{8,0},{12,4},{1,9},{5,13},{9,1},{13,5},{2,10},{6,14},... | collective-permute-start | bytes 589832 | tf_op jit(solution)/shard_map/ppermute | solution.py:27
  94.7 11.2 %collective-permute-start.32 = (bf16[2,128,384]{2,1,0:T(8,128)(2,1)S(1)}, bf16[2,128,384]{2,1,0:T(8,128)(2,1)S(1)}, u32[]{:S(2)}, u32[]{:S(2)}) collective-permute-start(bf16[2,128,384]{2,1,0:T(8,128)(2,1)S(1)} %get-tuple-element.75), channel_id=1, source_target_pairs={{0,12},{4,8},{8,4},{12,0},{1,13},{5,9},{9,5},{13,1},{2,14},{6,10},... | collective-permute-start | bytes 589832 | tf_op jit(solution)/shard_map/ppermute | solution.py:27
  103.2 5.9 %collective-permute-start.36 = (bf16[96,256]{1,0:T(8,128)(2,1)S(1)}, bf16[96,256]{1,0:T(8,128)(2,1)S(1)}, u32[]{:S(2)}, u32[]{:S(2)}) collective-permute-start(bf16[96,256]{1,0:T(8,128)(2,1)S(1)} %get-tuple-element.81), channel_id=1, source_target_pairs={{0,1},{1,2},{2,3},{3,0},{4,5},{5,6},{6,7},{7,4},{8,9},{9,10},{10,1... | collective-permute-start | bytes 147464 | tf_op jit(solution)/shard_map/ppermute | solution.py:36
  104.1 9.1 %collective-permute-start.33 = (bf16[128,384]{1,0:T(8,128)(2,1)S(1)}, bf16[128,384]{1,0:T(8,128)(2,1)S(1)}, u32[]{:S(2)}, u32[]{:S(2)}) collective-permute-start(bf16[128,384]{1,0:T(8,128)(2,1)S(1)} %get-tuple-element.77), channel_id=1, source_target_pairs={{0,4},{4,0},{8,12},{12,8},{1,5},{5,1},{9,13},{13,9},{2,6},{6,2},{1... | collective-permute-start | bytes 294920 | tf_op jit(solution)/shard_map/ppermute | solution.py:27
  104.1 9.1 %collective-permute-start.34 = (bf16[128,384]{1,0:T(8,128)(2,1)S(1)}, bf16[128,384]{1,0:T(8,128)(2,1)S(1)}, u32[]{:S(2)}, u32[]{:S(2)}) collective-permute-start(bf16[128,384]{1,0:T(8,128)(2,1)S(1)} %get-tuple-element.78), channel_id=1, source_target_pairs={{0,8},{4,12},{8,0},{12,4},{1,9},{5,13},{9,1},{13,5},{2,10},{6,14},... | collective-permute-start | bytes 294920 | tf_op jit(solution)/shard_map/ppermute | solution.py:27
  104.5 8.7 %collective-permute-start.35 = (bf16[128,384]{1,0:T(8,128)(2,1)S(1)}, bf16[128,384]{1,0:T(8,128)(2,1)S(1)}, u32[]{:S(2)}, u32[]{:S(2)}) collective-permute-start(bf16[128,384]{1,0:T(8,128)(2,1)S(1)} %get-tuple-element.79), channel_id=1, source_target_pairs={{0,12},{4,8},{8,4},{12,0},{1,13},{5,9},{9,5},{13,1},{2,14},{6,10},... | collective-permute-start | bytes 294920 | tf_op jit(solution)/shard_map/ppermute | solution.py:27
  105.9 6.2 %collective-permute-start.37 = (bf16[96,256]{1,0:T(8,128)(2,1)S(1)}, bf16[96,256]{1,0:T(8,128)(2,1)S(1)}, u32[]{:S(2)}, u32[]{:S(2)}) collective-permute-start(bf16[96,256]{1,0:T(8,128)(2,1)S(1)} %get-tuple-element.82), channel_id=1, source_target_pairs={{0,2},{1,3},{2,0},{3,1},{4,6},{5,7},{6,4},{7,5},{8,10},{9,11},{10,... | collective-permute-start | bytes 147464 | tf_op jit(solution)/shard_map/ppermute | solution.py:36
  109.1 4.1 %collective-permute-start.38 = (bf16[96,256]{1,0:T(8,128)(2,1)S(1)}, bf16[96,256]{1,0:T(8,128)(2,1)S(1)}, u32[]{:S(2)}, u32[]{:S(2)}) collective-permute-start(bf16[96,256]{1,0:T(8,128)(2,1)S(1)} %get-tuple-element.83), channel_id=1, source_target_pairs={{0,3},{1,0},{2,1},{3,2},{4,7},{5,4},{6,5},{7,6},{8,11},{9,8},{10,9... | collective-permute-start | bytes 147464 | tf_op jit(solution)/shard_map/ppermute | solution.py:36

commit v16 on v14

--- a/solution.py
+++ b/solution.py
@@ -684,8 +684,6 @@
             (outputs if part else lefts).append(results[1])
             piece = handed_over(results[0])
             relays[step].append([piece, None if part and not step else swap(piece, 2)])
-    (piece,) = tie([relays[0][1][0]], [outputs[1]])
-    relays[0][1] = [piece, swap(piece, 2)]
     beside = call(
         second_pair_kernel,
         "beside",
@@ -697,6 +695,8 @@
     )
     second = [second[0], second[1], swap(beside, 1)]
 
+    (piece,) = tie([relays[0][1][0]], [outputs[1], second[2]])
+    relays[0][1] = [piece, swap(piece, 2)]
     def complete(crossing):
         return [
             piece

time: 115 us -> 112 us (0.974)
  waiting for transfers between devices: 51.6 us -> 49.2 us
    ppermute x4, waiting for transfers between devices: 9.51 us -> 4.82 us  [handed_over(): return lax.ppermute(value, 'pipe', [(0, 1), (1, 0)])]
    ppermute x26, waiting for transfers between devices: 11.9 us -> 14.3 us  [swap(): lax.ppermute(value, 'seq', [(source, source ^ bit) for source in range(co...]
  transfers between devices with their start and end apart: 39 -> 39, of which waited for: 20 -> 19; matrix products, arithmetic and copies ran while one was open for 0% -> 0% of each run, Pallas kernels for 22% -> 23%
where the time goes in v16:
time: 112 us
  waiting for transfers between devices  49.2 us (44%)
  starting transfers between devices  32.9 us (29%)
  Pallas kernels  28.9 us (26%)
  between operations  1.14 us (1%)
    pallas_call x24, Pallas kernels, call(): pl.pallas_call(kernel, out_shape=out_shape, in_specs=in_specs, scratch_sh...  28.9 us
    ppermute x6, waiting for transfers between devices, ring_step(): return lax.ppermute(value, 'dp', pairs)  24.8 us
    ppermute x26, waiting for transfers between devices, swap(): lax.ppermute(value, 'seq', [(source, source ^ bit) for source in range(co...  14.3 us
    ppermute x26, starting transfers between devices, swap(): lax.ppermute(value, 'seq', [(source, source ^ bit) for source in range(co...  14 us
    ppermute x6, starting transfers between devices, ring_step(): return lax.ppermute(value, 'dp', pairs)  10.9 us
    ppermute x3, waiting for transfers between devices, shifted(): lax.ppermute(value, axis, [(source, (source + shift) % count) for source...  5.28 us
    ppermute x4, starting transfers between devices, handed_over(): return lax.ppermute(value, 'pipe', [(0, 1), (1, 0)])  5.14 us
    ppermute x4, waiting for transfers between devices, handed_over(): return lax.ppermute(value, 'pipe', [(0, 1), (1, 0)])  4.82 us
  transfers between devices with their start and end apart: 39, of which 19 were waited for; matrix products, arithmetic and copies ran while one was open for 0% of the time, Pallas kernels for 23%

profile of v16, /device:TPU:0, one launch (start us, length us, event | category | flops | bytes accessed | tf_op | source)
XLA Modules:
  0.0 112.2 jit_solution(6789279874759241115)
XLA Ops:
  0.7 1.5 %pack.1 = (bf16[2,96,384]{2,1,0:T(8,128)(2,1)S(1)}, bf16[2,96,384]{2,1,0:T(8,128)(2,1)S(1)}, bf16[2,96,384]{2,1,0:T(8,128)(2,1)S(1)}, bf16[2,96,384]{2,1,0:T(8,128)(2,1)S(1)}) custom-call(bf16[1,96,1536]{2,1,0:T(8,128)(2,1)} %wq.1, bf16[1,96,1536]{2,1,0:T(8,128)(2,1)} %wkv.1), custom_call_target="tpu_custom_call" | custom-call | tf_op jit(solution)/shard_map/pack/pallas_call | solution.py:502
  2.1 0.5 collective-permute-start
  2.7 1.0 collective-permute-done.refs_1_
  3.7 3.0 %collective-permute-start.1 = (bf16[2,2,96,384]{3,2,1,0:T(8,128)(2,1)S(1)}, bf16[2,2,96,384]{3,2,1,0:T(8,128)(2,1)S(1)}, u32[]{:S(2)}, u32[]{:S(2)}) collective-permute-start(bf16[2,2,96,384]{3,2,1,0:T(8,128)(2,1)S(1)} %near.1), channel_id=1, source_target_pairs={{0,1},{1,3},{3,2},{2,0},{4,5},{5,7},{7,6},{6,4},{8,9},{9,11},{11,1... | collective-permute-start | bytes 884744 | tf_op jit(solution)/shard_map/ppermute | solution.py:46
  6.7 1.5 %collective-permute-start.2 = (bf16[2,96,384]{2,1,0:T(8,128)(2,1)S(1)}, bf16[2,96,384]{2,1,0:T(8,128)(2,1)S(1)}, u32[]{:S(2)}, u32[]{:S(2)}) collective-permute-start(bf16[2,96,384]{2,1,0:T(8,128)(2,1)S(1)} %get-tuple-element.46), channel_id=1, source_target_pairs={{0,8},{4,12},{8,0},{12,4},{1,9},{5,13},{9,1},{13,5},{2,10},{6,14},... | collective-permute-start | bytes 442376 | tf_op jit(solution)/shard_map/ppermute | solution.py:27
  8.2 5.2 %collective-permute-done.2.refs_1_ = bf16[2,96,384]{2,1,0:T(8,128)(2,1)S(1)} collective-permute-done((bf16[2,96,384]{2,1,0:T(8,128)(2,1)S(1)}, bf16[2,96,384]{2,1,0:T(8,128)(2,1)S(1)}, u32[]{:S(2)}, u32[]{:S(2)}) %collective-permute-start.2) | collective-permute-done | bytes 147488 | tf_op jit(solution)/shard_map/ppermute | solution.py:27
  13.4 1.1 collective-permute-done.3.refs_2_
  14.5 0.5 collective-permute-done.1.refs_0_.near
  15.1 0.1 first.1.refs_0_
  15.1 1.6 %collective-permute-start.4 = (bf16[272,1536]{1,0:T(8,128)(2,1)S(1)}, bf16[272,1536]{1,0:T(8,128)(2,1)S(1)}, u32[]{:S(2)}, u32[]{:S(2)}) collective-permute-start(bf16[272,1536]{1,0:T(8,128)(2,1)S(1)} %first.1.refs_0_), channel_id=1, source_target_pairs={{0,8},{4,12},{8,0},{12,4},{1,9},{5,13},{9,1},{13,5},{2,10},{6,14},... | collective-permute-start | bytes 2506760 | tf_op jit(solution)/shard_map/ppermute | solution.py:27
  16.7 1.9 %collective-permute-start.5 = (bf16[2,2,96,384]{3,2,1,0:T(8,128)(2,1)S(1)}, bf16[2,2,96,384]{3,2,1,0:T(8,128)(2,1)S(1)}, u32[]{:S(2)}, u32[]{:S(2)}) collective-permute-start(bf16[2,2,96,384]{3,2,1,0:T(8,128)(2,1)S(1)} %far.1), channel_id=1, source_target_pairs={{0,1},{1,3},{3,2},{2,0},{4,5},{5,7},{7,6},{6,4},{8,9},{9,11},{11,1... | collective-permute-start | bytes 884744 | tf_op jit(solution)/shard_map/ppermute | solution.py:46
  18.6 7.9 %collective-permute-done.5.far = bf16[2,2,96,384]{3,2,1,0:T(8,128)(2,1)S(1)} collective-permute-done((bf16[2,2,96,384]{3,2,1,0:T(8,128)(2,1)S(1)}, bf16[2,2,96,384]{3,2,1,0:T(8,128)(2,1)S(1)}, u32[]{:S(2)}, u32[]{:S(2)}) %collective-permute-start.5) | collective-permute-done | bytes 294944 | tf_op jit(solution)/shard_map/ppermute | solution.py:46
  26.5 1.7 %collective-permute-start.6 = (bf16[4,96,384]{2,1,0:T(8,128)(2,1)S(1)}, bf16[4,96,384]{2,1,0:T(8,128)(2,1)S(1)}, u32[]{:S(2)}, u32[]{:S(2)}) collective-permute-start(bf16[4,96,384]{2,1,0:T(8,128)(2,1)S(1)} %part0.1.chunk), channel_id=1, source_target_pairs={{0,1},{1,3},{3,2},{2,0},{4,5},{5,7},{7,6},{6,4},{8,9},{9,11},{11,1... | collective-permute-start | bytes 884744 | tf_op jit(solution)/shard_map/ppermute | solution.py:46
  28.3 0.0 copy-start.5
  28.3 1.7 %collective-permute-start.7 = (bf16[4,96,384]{2,1,0:T(8,128)(2,1)S(1)}, bf16[4,96,384]{2,1,0:T(8,128)(2,1)S(1)}, u32[]{:S(2)}, u32[]{:S(2)}) collective-permute-start(bf16[4,96,384]{2,1,0:T(8,128)(2,1)S(1)} %part1.1.chunk), channel_id=1, source_target_pairs={{0,1},{1,3},{3,2},{2,0},{4,5},{5,7},{7,6},{6,4},{8,9},{9,11},{11,1... | collective-permute-start | bytes 884744 | tf_op jit(solution)/shard_map/ppermute | solution.py:46
  30.0 7.4 %collective-permute-done.6.refs_1_.refs_9_ = bf16[4,96,384]{2,1,0:T(8,128)(2,1)S(1)} collective-permute-done((bf16[4,96,384]{2,1,0:T(8,128)(2,1)S(1)}, bf16[4,96,384]{2,1,0:T(8,128)(2,1)S(1)}, u32[]{:S(2)}, u32[]{:S(2)}) %collective-permute-start.6) | collective-permute-done | bytes 294944 | tf_op jit(solution)/shard_map/ppermute | solution.py:46
  37.4 4.4 %collective-permute-done.7.refs_2_.refs_9_ = bf16[4,96,384]{2,1,0:T(8,128)(2,1)S(1)} collective-permute-done((bf16[4,96,384]{2,1,0:T(8,128)(2,1)S(1)}, bf16[4,96,384]{2,1,0:T(8,128)(2,1)S(1)}, u32[]{:S(2)}, u32[]{:S(2)}) %collective-permute-start.7) | collective-permute-done | bytes 294944 | tf_op jit(solution)/shard_map/ppermute | solution.py:46
  41.9 0.7 collective-permute-start.8
  42.6 1.4 %collective-permute-start.12 = (bf16[4,96,384]{2,1,0:T(8,128)(2,1)S(1)}, bf16[4,96,384]{2,1,0:T(8,128)(2,1)S(1)}, u32[]{:S(2)}, u32[]{:S(2)}) collective-permute-start(bf16[4,96,384]{2,1,0:T(8,128)(2,1)S(1)} %collective-permute-done.6.refs_1_.refs_9_), channel_id=1, source_target_pairs={{0,1},{1,3},{3,2},{2,0},{4,5},{5,7},{7,6},{6,4},{8,9},{9,11},{11,1... | collective-permute-start | bytes 884744 | tf_op jit(solution)/shard_map/ppermute | solution.py:46
  44.0 1.2 %collective-permute-start.11 = (bf16[4,96,384]{2,1,0:T(8,128)(2,1)S(1)}, bf16[4,96,384]{2,1,0:T(8,128)(2,1)S(1)}, u32[]{:S(2)}, u32[]{:S(2)}) collective-permute-start(bf16[4,96,384]{2,1,0:T(8,128)(2,1)S(1)} %collective-permute-done.7.refs_2_.refs_9_), channel_id=1, source_target_pairs={{0,1},{1,3},{3,2},{2,0},{4,5},{5,7},{7,6},{6,4},{8,9},{9,11},{11,1... | collective-permute-start | bytes 884744 | tf_op jit(solution)/shard_map/ppermute | solution.py:46
  45.2 0.1 place0.1.refs_11_
  45.3 3.3 %norm.1 = (bf16[512,1536]{1,0:T(8,128)(2,1)S(1)}, bf16[512,1536]{1,0:T(8,128)(2,1)S(1)}, f32[512,128]{1,0:T(8,128)S(1)}, f32[512,128]{1,0:T(8,128)S(1)}, f32[512...) custom-call(s32[1,4]{1,0:T(1,128)S(1)} %bitcast.5, ...), custom_call_target="tpu_custom_call" | custom-call | tf_op jit(solution)/shard_map/norm/pallas_call | solution.py:502
  48.7 4.6 %collective-permute-done.12.refs_10_ = bf16[4,96,384]{2,1,0:T(8,128)(2,1)S(1)} collective-permute-done((bf16[4,96,384]{2,1,0:T(8,128)(2,1)S(1)}, bf16[4,96,384]{2,1,0:T(8,128)(2,1)S(1)}, u32[]{:S(2)}, u32[]{:S(2)}) %collective-permute-start.12) | collective-permute-done | bytes 294944 | tf_op jit(solution)/shard_map/ppermute | solution.py:46
  53.3 2.7 %step0a.1 = (bf16[768,128]{1,0:T(8,128)(2,1)S(1)}, bf16[512,256]{1,0:T(8,128)(2,1)S(1)}, bf16[1536,384]{1,0:T(8,128)(2,1)S(1)}) custom-call(f32[1,16]{1,0:T(1,128)S(1)} %copy-done.8, s32[1,4]{1,0:T(1,128)S(1)} %bitcast.6, f32[1,1536]{1,0:T(1,128)S(1)} %copy-done.1, f32[1,1536]{1,0:T(1,128)S(1)} %copy-done.2, ...), custom_call_target="tpu_custom_call", output_to_operand_aliasing={{2}: (11, {})} | custom-call | flops 805306368 | bytes 1572864 | tf_op jit(solution)/shard_map/step0a/pallas_call | solution.py:502
  56.1 1.5 %collective-permute-start.13 = (bf16[768,128]{1,0:T(8,128)(2,1)S(1)}, bf16[768,128]{1,0:T(8,128)(2,1)S(1)}, u32[]{:S(2)}, u32[]{:S(2)}) collective-permute-start(bf16[768,128]{1,0:T(8,128)(2,1)S(1)} %get-tuple-element.51), channel_id=1, source_target_pairs={{0,16},{16,0},{1,17},{17,1},{2,18},{18,2},{3,19},{19,3},{4,20},{20... | collective-permute-start | bytes 589832 | tf_op jit(solution)/shard_map/ppermute | solution.py:31
  57.6 0.1 place1.1.refs_11_
  57.7 2.7 %step1a.1 = (bf16[768,128]{1,0:T(8,128)(2,1)S(1)}, bf16[512,256]{1,0:T(8,128)(2,1)S(1)}) custom-call(f32[1,16]{1,0:T(1,128)S(1)} %copy-done.8, s32[1,4]{1,0:T(1,128)S(1)} %bitcast.7, f32[1,1536]{1,0:T(1,128)S(1)} %copy-done.1, f32[1,1536]{1,0:T(1,128)S(1)} %copy-done.2, f32[1,1536]{1,0:T(1,128)S(1)} %copy-done.4, s32[4,1,512]{2,1,0:T(1,128)S(1)} %copy-done.3, ...), custom_call_target="tpu_custom_call" | custom-call | flops 805306368 | bytes 1572864 | tf_op jit(solution)/shard_map/step1a/pallas_call | solution.py:502
  60.4 1.4 %collective-permute-done.13.refs_1_.refs_10_ = bf16[768,128]{1,0:T(8,128)(2,1)S(1)} collective-permute-done((bf16[768,128]{1,0:T(8,128)(2,1)S(1)}, bf16[768,128]{1,0:T(8,128)(2,1)S(1)}, u32[]{:S(2)}, u32[]{:S(2)}) %collective-permute-start.13) | collective-permute-done | bytes 196640 | tf_op jit(solution)/shard_map/ppermute | solution.py:31
  61.8 2.8 %step0b.1 = (bf16[768,128]{1,0:T(8,128)(2,1)S(1)}, bf16[4,128,384]{2,1,0:T(8,128)(2,1)S(1)}, bf16[1536,384]{1,0:T(8,128)(2,1)S(1)}) custom-call(f32[1,16]{1,0:T(1,128)S(1)} %copy-done.8, s32[1,4]{1,0:T(1,128)S(1)} %bitcast.8, f32[1,1536]{1,0:T(1,128)S(1)} %copy-done.1, f32[1,1536]{1,0:T(1,128)S(1)} %copy-done.2, ...), custom_call_target="tpu_custom_call", output_to_operand_aliasing={{2}: (11, {})} | custom-call | flops 805306368 | bytes 1572864 | tf_op jit(solution)/shard_map/step0b/pallas_call | solution.py:502
  64.6 0.1 beside.1
  64.7 0.1 collective-permute-start.14
  64.8 1.5 %collective-permute-start.18 = (bf16[768,128]{1,0:T(8,128)(2,1)S(1)}, bf16[768,128]{1,0:T(8,128)(2,1)S(1)}, u32[]{:S(2)}, u32[]{:S(2)}) collective-permute-start(bf16[768,128]{1,0:T(8,128)(2,1)S(1)} %get-tuple-element.60), channel_id=1, source_target_pairs={{0,16},{16,0},{1,17},{17,1},{2,18},{18,2},{3,19},{19,3},{4,20},{20... | collective-permute-start | bytes 589832 | tf_op jit(solution)/shard_map/ppermute | solution.py:31
  66.3 0.6 collective-permute-start.22
  66.9 1.4 %collective-permute-start.15 = (bf16[768,128]{1,0:T(8,128)(2,1)S(1)}, bf16[768,128]{1,0:T(8,128)(2,1)S(1)}, u32[]{:S(2)}, u32[]{:S(2)}) collective-permute-start(bf16[768,128]{1,0:T(8,128)(2,1)S(1)} %collective-permute-done.13.refs_1_.refs_10_), channel_id=1, source_target_pairs={{0,8},{4,12},{8,0},{12,4},{1,9},{5,13},{9,1},{13,5},{2,10},{6,14},... | collective-permute-start | bytes 589832 | tf_op jit(solution)/shard_map/ppermute | solution.py:27
  68.3 2.7 %step1b.1 = (bf16[768,128]{1,0:T(8,128)(2,1)S(1)}, bf16[4,128,384]{2,1,0:T(8,128)(2,1)S(1)}) custom-call(f32[1,16]{1,0:T(1,128)S(1)} %copy-done.8, s32[1,4]{1,0:T(1,128)S(1)} %bitcast.9, f32[1,1536]{1,0:T(1,128)S(1)} %copy-done.1, f32[1,1536]{1,0:T(1,128)S(1)} %copy-done.2, f32[1,1536]{1,0:T(1,128)S(1)} %copy-done.4, s32[4,1,512]{2,1,0:T(1,128)S(1)} %copy-done.3, ...), custom_call_target="tpu_custom_call" | custom-call | flops 805306368 | bytes 1572864 | tf_op jit(solution)/shard_map/step1b/pallas_call | solution.py:502
  71.1 1.5 %collective-permute-done.18.refs_0_ = bf16[768,128]{1,0:T(8,128)(2,1)S(1)} collective-permute-done((bf16[768,128]{1,0:T(8,128)(2,1)S(1)}, bf16[768,128]{1,0:T(8,128)(2,1)S(1)}, u32[]{:S(2)}, u32[]{:S(2)}) %collective-permute-start.18) | collective-permute-done | bytes 196640 | tf_op jit(solution)/shard_map/ppermute | solution.py:31
  72.6 1.4 %collective-permute-start.19 = (bf16[768,128]{1,0:T(8,128)(2,1)S(1)}, bf16[768,128]{1,0:T(8,128)(2,1)S(1)}, u32[]{:S(2)}, u32[]{:S(2)}) collective-permute-start(bf16[768,128]{1,0:T(8,128)(2,1)S(1)} %tie.6.refs_14_), channel_id=1, source_target_pairs={{0,8},{4,12},{8,0},{12,4},{1,9},{5,13},{9,1},{13,5},{2,10},{6,14},... | collective-permute-start | bytes 589832 | tf_op jit(solution)/shard_map/ppermute | solution.py:27
  74.0 1.5 %collective-permute-start.24 = (bf16[768,128]{1,0:T(8,128)(2,1)S(1)}, bf16[768,128]{1,0:T(8,128)(2,1)S(1)}, u32[]{:S(2)}, u32[]{:S(2)}) collective-permute-start(bf16[768,128]{1,0:T(8,128)(2,1)S(1)} %get-tuple-element.65), channel_id=1, source_target_pairs={{0,16},{16,0},{1,17},{17,1},{2,18},{18,2},{3,19},{19,3},{4,20},{20... | collective-permute-start | bytes 589832 | tf_op jit(solution)/shard_map/ppermute | solution.py:31
  75.5 0.2 collective-permute-start.17
  75.8 0.6 collective-permute-done.22.refs_0_
  76.3 2.3 %collective-permute-done.19.refs_15_ = bf16[768,128]{1,0:T(8,128)(2,1)S(1)} collective-permute-done((bf16[768,128]{1,0:T(8,128)(2,1)S(1)}, bf16[768,128]{1,0:T(8,128)(2,1)S(1)}, u32[]{:S(2)}, u32[]{:S(2)}) %collective-permute-start.19) | collective-permute-done | bytes 196640 | tf_op jit(solution)/shard_map/ppermute | solution.py:27
  78.6 1.4 %collective-permute-start.23 = (bf16[768,128]{1,0:T(8,128)(2,1)S(1)}, bf16[768,128]{1,0:T(8,128)(2,1)S(1)}, u32[]{:S(2)}, u32[]{:S(2)}) collective-permute-start(bf16[768,128]{1,0:T(8,128)(2,1)S(1)} %collective-permute-done.22.refs_0_), channel_id=1, source_target_pairs={{0,8},{4,12},{8,0},{12,4},{1,9},{5,13},{9,1},{13,5},{2,10},{6,14},... | collective-permute-start | bytes 589832 | tf_op jit(solution)/shard_map/ppermute | solution.py:27
  80.0 1.3 %collective-permute-done.24.refs_2_ = bf16[768,128]{1,0:T(8,128)(2,1)S(1)} collective-permute-done((bf16[768,128]{1,0:T(8,128)(2,1)S(1)}, bf16[768,128]{1,0:T(8,128)(2,1)S(1)}, u32[]{:S(2)}, u32[]{:S(2)}) %collective-permute-start.24) | collective-permute-done | bytes 196640 | tf_op jit(solution)/shard_map/ppermute | solution.py:31
  81.3 0.7 collective-permute-start.25
  82.0 4.9 %step2ab.1.refs_2_.refs_0_ = bf16[4,128,384]{2,1,0:T(8,128)(2,1)S(1)} custom-call(f32[1,16]{1,0:T(1,128)S(1)} %copy-done.8, s32[1,4]{1,0:T(1,128)S(1)} %bitcast.10, f32[1,1536]{1,0:T(1,128)S(1)} %copy-done.1, f32[1,1536]{1,0:T(1,128)S(1)} %copy-done.2, f32[1,1536]{1,0:T(1,128)S(1)} %copy-done.4, s32[4,1,512]{2,1,0:T(1,128)S(1)} %copy-done.3, ...), custom_call_target="tpu_custom_call" | custom-call | flops 1610612736 | bytes 3145728 | tf_op jit(solution)/shard_map/step2ab/pallas_call | solution.py:502
  86.9 0.5 early.1
  87.4 2.8 %collective-permute-done.25.refs_3_ = bf16[768,128]{1,0:T(8,128)(2,1)S(1)} collective-permute-done((bf16[768,128]{1,0:T(8,128)(2,1)S(1)}, bf16[768,128]{1,0:T(8,128)(2,1)S(1)}, u32[]{:S(2)}, u32[]{:S(2)}) %collective-permute-start.25) | collective-permute-done | bytes 196640 | tf_op jit(solution)/shard_map/ppermute | solution.py:27
  90.1 0.5 collective-permute-start.27
  90.7 0.5 collective-permute-start.29
  91.2 0.4 collective-permute-done.26.refs_12_
  91.6 1.4 %collective-permute-start.31 = (bf16[2,128,384]{2,1,0:T(8,128)(2,1)S(1)}, bf16[2,128,384]{2,1,0:T(8,128)(2,1)S(1)}, u32[]{:S(2)}, u32[]{:S(2)}) collective-permute-start(bf16[2,128,384]{2,1,0:T(8,128)(2,1)S(1)} %get-tuple-element.73), channel_id=1, source_target_pairs={{0,8},{4,12},{8,0},{12,4},{1,9},{5,13},{9,1},{13,5},{2,10},{6,14},... | collective-permute-start | bytes 589832 | tf_op jit(solution)/shard_map/ppermute | solution.py:27
  93.0 0.1 collective-permute-start.32
  93.1 4.7 %step3ab.1.refs_1_ = bf16[4,128,384]{2,1,0:T(8,128)(2,1)S(1)} custom-call(f32[1,16]{1,0:T(1,128)S(1)} %copy-done.8, s32[1,4]{1,0:T(1,128)S(1)} %bitcast.11, f32[1,1536]{1,0:T(1,128)S(1)} %copy-done.1, f32[1,1536]{1,0:T(1,128)S(1)} %copy-done.2, f32[1,1536]{1,0:T(1,128)S(1)} %copy-done.4, s32[4,1,512]{2,1,0:T(1,128)S(1)} %copy-done.3, ...), custom_call_target="tpu_custom_call" | custom-call | flops 1610612736 | bytes 3145728 | tf_op jit(solution)/shard_map/step3ab/pallas_call | solution.py:502
  97.8 1.5 %collective-permute-done.31.refs_7_ = bf16[2,128,384]{2,1,0:T(8,128)(2,1)S(1)} collective-permute-done((bf16[2,128,384]{2,1,0:T(8,128)(2,1)S(1)}, bf16[2,128,384]{2,1,0:T(8,128)(2,1)S(1)}, u32[]{:S(2)}, u32[]{:S(2)}) %collective-permute-start.31) | collective-permute-done | bytes 196640 | tf_op jit(solution)/shard_map/ppermute | solution.py:27
  99.3 1.2 %settle.1 = (bf16[128,384]{1,0:T(8,128)(2,1)S(1)}, bf16[128,384]{1,0:T(8,128)(2,1)S(1)}, bf16[128,384]{1,0:T(8,128)(2,1)S(1)}, bf16[128,384]{1,0:T(8,128)(2,1)S(...) custom-call(bf16[4,128,384]{2,1,0:T(8,128)(2,1)S(1)} %step2ab.1.refs, ...), custom_call_target="tpu_custom_call" | custom-call | tf_op jit(solution)/shard_map/settle/pallas_call | solution.py:502
  100.5 0.6 collective-permute-start.36
  101.1 1.5 %collective-permute-start.34 = (bf16[128,384]{1,0:T(8,128)(2,1)S(1)}, bf16[128,384]{1,0:T(8,128)(2,1)S(1)}, u32[]{:S(2)}, u32[]{:S(2)}) collective-permute-start(bf16[128,384]{1,0:T(8,128)(2,1)S(1)} %get-tuple-element.78), channel_id=1, source_target_pairs={{0,8},{4,12},{8,0},{12,4},{1,9},{5,13},{9,1},{13,5},{2,10},{6,14},... | collective-permute-start | bytes 294920 | tf_op jit(solution)/shard_map/ppermute | solution.py:27
  102.6 0.3 collective-permute-start.35
  103.0 2.1 %collective-permute-start.37 = (bf16[96,256]{1,0:T(8,128)(2,1)S(1)}, bf16[96,256]{1,0:T(8,128)(2,1)S(1)}, u32[]{:S(2)}, u32[]{:S(2)}) collective-permute-start(bf16[96,256]{1,0:T(8,128)(2,1)S(1)} %get-tuple-element.82), channel_id=1, source_target_pairs={{0,2},{1,3},{2,0},{3,1},{4,6},{5,7},{6,4},{7,5},{8,10},{9,11},{10,... | collective-permute-start | bytes 147464 | tf_op jit(solution)/shard_map/ppermute | solution.py:36
  105.1 1.4 %collective-permute-done.36.refs_7_ = bf16[96,256]{1,0:T(8,128)(2,1)S(1)} collective-permute-done((bf16[96,256]{1,0:T(8,128)(2,1)S(1)}, bf16[96,256]{1,0:T(8,128)(2,1)S(1)}, u32[]{:S(2)}, u32[]{:S(2)}) %collective-permute-start.36) | collective-permute-done | bytes 49184 | tf_op jit(solution)/shard_map/ppermute | solution.py:36
  106.5 0.2 collective-permute-start.38
  106.7 2.3 %collective-permute-done.37.refs_8_ = bf16[96,256]{1,0:T(8,128)(2,1)S(1)} collective-permute-done((bf16[96,256]{1,0:T(8,128)(2,1)S(1)}, bf16[96,256]{1,0:T(8,128)(2,1)S(1)}, u32[]{:S(2)}, u32[]{:S(2)}) %collective-permute-start.37) | collective-permute-done | bytes 49184 | tf_op jit(solution)/shard_map/ppermute | solution.py:36
  109.1 1.5 %collective-permute-done.38.refs_9_ = bf16[96,256]{1,0:T(8,128)(2,1)S(1)} collective-permute-done((bf16[96,256]{1,0:T(8,128)(2,1)S(1)}, bf16[96,256]{1,0:T(8,128)(2,1)S(1)}, u32[]{:S(2)}, u32[]{:S(2)}) %collective-permute-start.38) | collective-permute-done | bytes 49184 | tf_op jit(solution)/shard_map/ppermute | solution.py:36
  110.6 1.5 %finish.1 = (bf16[3,128,1536]{2,1,0:T(8,128)(2,1)}, f32[96,256]{1,0:T(8,128)}) custom-call(bf16[3,128,1536]{2,1,0:T(8,128)(2,1)} %get-tuple-element.74.refs_0_, bf16[2,128,384]{2,1,0:T(8,128)(2,1)S(1)} %collective-permute-done.32.refs_1_, bf16[128,384]{1,0:T(8,128)(2,1)S(1)} %get-tuple-element.76.refs_2_, ...), custom_call_target="tpu_custom_call", output_to_operand_aliasing={{0}: (0, {})} | custom-call | tf_op jit(solution)/shard_map/finish/pallas_call | solution.py:502
  (58 shorter events, 0.3 us)
Async XLA Ops:
  0.6 14.4 %copy-start = (bf16[1,3,1,128,1536]{4,3,2,1,0:T(8,128)(2,1)S(1)}, bf16[1,3,1,128,1536]{4,3,2,1,0:T(8,128)(2,1)}, u32[]{:S(2)}) copy-start(bf16[1,3,1,128,1536]{4,3,2,1,0:T(8,128)(2,1)} %incoming.3) | copy-start | bytes 3538948
  0.6 14.4 %copy-start.9 = (s32[4,1,128]{2,1,0:T(1,128)S(1)}, s32[4,1,128]{2,1,0:T(1,128)}, u32[]{:S(2)}) copy-start(s32[4,1,128]{2,1,0:T(1,128)} %contacts.1) | copy-start | bytes 6148
  2.1 1.5 %collective-permute-start = (bf16[2,96,384]{2,1,0:T(8,128)(2,1)S(1)}, bf16[2,96,384]{2,1,0:T(8,128)(2,1)S(1)}, u32[]{:S(2)}, u32[]{:S(2)}) collective-permute-start(bf16[2,96,384]{2,1,0:T(8,128)(2,1)S(1)} %get-tuple-element.45), channel_id=1, source_target_pairs={{0,4},{4,0},{8,12},{12,8},{1,5},{5,1},{9,13},{13,9},{2,6},{6,2},{1... | collective-permute-start | bytes 442376 | tf_op jit(solution)/shard_map/ppermute | solution.py:27
  3.7 11.3 %collective-permute-start.1 = (bf16[2,2,96,384]{3,2,1,0:T(8,128)(2,1)S(1)}, bf16[2,2,96,384]{3,2,1,0:T(8,128)(2,1)S(1)}, u32[]{:S(2)}, u32[]{:S(2)}) collective-permute-start(bf16[2,2,96,384]{3,2,1,0:T(8,128)(2,1)S(1)} %near.1), channel_id=1, source_target_pairs={{0,1},{1,3},{3,2},{2,0},{4,5},{5,7},{7,6},{6,4},{8,9},{9,11},{11,1... | collective-permute-start | bytes 884744 | tf_op jit(solution)/shard_map/ppermute | solution.py:46
  6.7 6.7 %collective-permute-start.2 = (bf16[2,96,384]{2,1,0:T(8,128)(2,1)S(1)}, bf16[2,96,384]{2,1,0:T(8,128)(2,1)S(1)}, u32[]{:S(2)}, u32[]{:S(2)}) collective-permute-start(bf16[2,96,384]{2,1,0:T(8,128)(2,1)S(1)} %get-tuple-element.46), channel_id=1, source_target_pairs={{0,8},{4,12},{8,0},{12,4},{1,9},{5,13},{9,1},{13,5},{2,10},{6,14},... | collective-permute-start | bytes 442376 | tf_op jit(solution)/shard_map/ppermute | solution.py:27
  8.2 6.3 %collective-permute-start.3 = (bf16[2,96,384]{2,1,0:T(8,128)(2,1)S(1)}, bf16[2,96,384]{2,1,0:T(8,128)(2,1)S(1)}, u32[]{:S(2)}, u32[]{:S(2)}) collective-permute-start(bf16[2,96,384]{2,1,0:T(8,128)(2,1)S(1)} %get-tuple-element.47), channel_id=1, source_target_pairs={{0,12},{4,8},{8,4},{12,0},{1,13},{5,9},{9,5},{13,1},{2,14},{6,10},... | collective-permute-start | bytes 442376 | tf_op jit(solution)/shard_map/ppermute | solution.py:27
  15.1 26.7 %collective-permute-start.4 = (bf16[272,1536]{1,0:T(8,128)(2,1)S(1)}, bf16[272,1536]{1,0:T(8,128)(2,1)S(1)}, u32[]{:S(2)}, u32[]{:S(2)}) collective-permute-start(bf16[272,1536]{1,0:T(8,128)(2,1)S(1)} %first.1.refs_0_), channel_id=1, source_target_pairs={{0,8},{4,12},{8,0},{12,4},{1,9},{5,13},{9,1},{13,5},{2,10},{6,14},... | collective-permute-start | bytes 2506760 | tf_op jit(solution)/shard_map/ppermute | solution.py:27
  16.7 9.8 %collective-permute-start.5 = (bf16[2,2,96,384]{3,2,1,0:T(8,128)(2,1)S(1)}, bf16[2,2,96,384]{3,2,1,0:T(8,128)(2,1)S(1)}, u32[]{:S(2)}, u32[]{:S(2)}) collective-permute-start(bf16[2,2,96,384]{3,2,1,0:T(8,128)(2,1)S(1)} %far.1), channel_id=1, source_target_pairs={{0,1},{1,3},{3,2},{2,0},{4,5},{5,7},{7,6},{6,4},{8,9},{9,11},{11,1... | collective-permute-start | bytes 884744 | tf_op jit(solution)/shard_map/ppermute | solution.py:46
  26.5 10.9 %collective-permute-start.6 = (bf16[4,96,384]{2,1,0:T(8,128)(2,1)S(1)}, bf16[4,96,384]{2,1,0:T(8,128)(2,1)S(1)}, u32[]{:S(2)}, u32[]{:S(2)}) collective-permute-start(bf16[4,96,384]{2,1,0:T(8,128)(2,1)S(1)} %part0.1.chunk), channel_id=1, source_target_pairs={{0,1},{1,3},{3,2},{2,0},{4,5},{5,7},{7,6},{6,4},{8,9},{9,11},{11,1... | collective-permute-start | bytes 884744 | tf_op jit(solution)/shard_map/ppermute | solution.py:46
  28.3 13.5 %copy-start.5 = (bf16[1,3,1,128,256]{4,3,2,1,0:T(8,128)(2,1)S(1)}, bf16[1,3,1,128,256]{4,3,2,1,0:T(8,128)(2,1)}, u32[]{:S(2)}) copy-start(bf16[1,3,1,128,256]{4,3,2,1,0:T(8,128)(2,1)} %cotangent.1) | copy-start | bytes 589828
  28.3 13.5 %collective-permute-start.7 = (bf16[4,96,384]{2,1,0:T(8,128)(2,1)S(1)}, bf16[4,96,384]{2,1,0:T(8,128)(2,1)S(1)}, u32[]{:S(2)}, u32[]{:S(2)}) collective-permute-start(bf16[4,96,384]{2,1,0:T(8,128)(2,1)S(1)} %part1.1.chunk), channel_id=1, source_target_pairs={{0,1},{1,3},{3,2},{2,0},{4,5},{5,7},{7,6},{6,4},{8,9},{9,11},{11,1... | collective-permute-start | bytes 884744 | tf_op jit(solution)/shard_map/ppermute | solution.py:46
  30.0 15.2 %collective-permute-start.9 = (bf16[272,1536]{1,0:T(8,128)(2,1)S(1)}, bf16[272,1536]{1,0:T(8,128)(2,1)S(1)}, u32[]{:S(2)}, u32[]{:S(2)}) collective-permute-start(bf16[272,1536]{1,0:T(8,128)(2,1)S(1)} %first.1.refs_0_), channel_id=1, source_target_pairs={{0,4},{4,0},{8,12},{12,8},{1,5},{5,1},{9,13},{13,9},{2,6},{6,2},{1... | collective-permute-start | bytes 2506760 | tf_op jit(solution)/shard_map/ppermute | solution.py:27
  41.8 3.4 %collective-permute-start.10 = (bf16[272,1536]{1,0:T(8,128)(2,1)S(1)}, bf16[272,1536]{1,0:T(8,128)(2,1)S(1)}, u32[]{:S(2)}, u32[]{:S(2)}) collective-permute-start(bf16[272,1536]{1,0:T(8,128)(2,1)S(1)} %tie.4.dep.refs_1_), channel_id=1, source_target_pairs={{0,4},{4,0},{8,12},{12,8},{1,5},{5,1},{9,13},{13,9},{2,6},{6,2},{1... | collective-permute-start | bytes 2506760 | tf_op jit(solution)/shard_map/ppermute | solution.py:27
  41.9 3.4 %copy-start.1 = (f32[1,1536]{1,0:T(1,128)S(1)}, f32[1,1536]{1,0:T(1,128)}, u32[]{:S(2)}) copy-start(f32[1,1536]{1,0:T(1,128)} %refs_2_.11) | copy-start | bytes 18436
  41.9 3.4 %copy-start.2 = (f32[1,1536]{1,0:T(1,128)S(1)}, f32[1,1536]{1,0:T(1,128)}, u32[]{:S(2)}) copy-start(f32[1,1536]{1,0:T(1,128)} %refs_3_.11) | copy-start | bytes 18436
  41.9 3.4 %copy-start.6 = (bf16[1,16,1536]{2,1,0:T(8,128)(2,1)S(1)}, bf16[1,16,1536]{2,1,0:T(8,128)(2,1)}, u32[]{:S(2)}) copy-start(bf16[1,16,1536]{2,1,0:T(8,128)(2,1)} %table.1) | copy-start | bytes 147460
  41.9 3.4 %copy-start.7 = (s32[4,1]{0,1:T(1,128)S(1)}, s32[4,1]{0,1:T(1,128)}, u32[]{:S(2)}) copy-start(s32[4,1]{0,1:T(1,128)} %param.15) | copy-start | bytes 52
  41.9 22.7 %collective-permute-start.8 = (bf16[256,1536]{1,0:T(8,128)(2,1)S(1)}, bf16[256,1536]{1,0:T(8,128)(2,1)S(1)}, u32[]{:S(2)}, u32[]{:S(2)}) collective-permute-start(bf16[256,1536]{1,0:T(8,128)(2,1)S(1)} %second.1.mine.refs_6_.refs_3_.refs_2_), channel_id=1, source_target_pairs={{0,8},{4,12},{8,0},{12,4},{1,9},{5,13},{9,1},{13,5},{2,10},{6,14},... | collective-permute-start | bytes 2359304 | tf_op jit(solution)/shard_map/ppermute | solution.py:27
  42.6 10.7 %collective-permute-start.12 = (bf16[4,96,384]{2,1,0:T(8,128)(2,1)S(1)}, bf16[4,96,384]{2,1,0:T(8,128)(2,1)S(1)}, u32[]{:S(2)}, u32[]{:S(2)}) collective-permute-start(bf16[4,96,384]{2,1,0:T(8,128)(2,1)S(1)} %collective-permute-done.6.refs_1_.refs_9_), channel_id=1, source_target_pairs={{0,1},{1,3},{3,2},{2,0},{4,5},{5,7},{7,6},{6,4},{8,9},{9,11},{11,1... | collective-permute-start | bytes 884744 | tf_op jit(solution)/shard_map/ppermute | solution.py:46
  44.0 16.4 %collective-permute-start.11 = (bf16[4,96,384]{2,1,0:T(8,128)(2,1)S(1)}, bf16[4,96,384]{2,1,0:T(8,128)(2,1)S(1)}, u32[]{:S(2)}, u32[]{:S(2)}) collective-permute-start(bf16[4,96,384]{2,1,0:T(8,128)(2,1)S(1)} %collective-permute-done.7.refs_2_.refs_9_), channel_id=1, source_target_pairs={{0,1},{1,3},{3,2},{2,0},{4,5},{5,7},{7,6},{6,4},{8,9},{9,11},{11,1... | collective-permute-start | bytes 884744 | tf_op jit(solution)/shard_map/ppermute | solution.py:46
  45.3 8.0 %copy-start.3 = (s32[4,1,512]{2,1,0:T(1,128)S(1)}, s32[4,1,512]{2,1,0:T(1,128)}, u32[]{:S(2)}) copy-start(s32[4,1,512]{2,1,0:T(1,128)} %refs_5_.11) | copy-start | bytes 24580
  45.3 8.0 %copy-start.4 = (f32[1,1536]{1,0:T(1,128)S(1)}, f32[1,1536]{1,0:T(1,128)}, u32[]{:S(2)}) copy-start(f32[1,1536]{1,0:T(1,128)} %refs_4_.11) | copy-start | bytes 18436
  45.3 8.0 %copy-start.8 = (f32[1,16]{1,0:T(1,128)S(1)}, f32[1,16]{1,0:T(1,128)}, u32[]{:S(2)}) copy-start(f32[1,16]{1,0:T(1,128)} %refs_0_.11) | copy-start | bytes 196
  56.1 5.7 %collective-permute-start.13 = (bf16[768,128]{1,0:T(8,128)(2,1)S(1)}, bf16[768,128]{1,0:T(8,128)(2,1)S(1)}, u32[]{:S(2)}, u32[]{:S(2)}) collective-permute-start(bf16[768,128]{1,0:T(8,128)(2,1)S(1)} %get-tuple-element.51), channel_id=1, source_target_pairs={{0,16},{16,0},{1,17},{17,1},{2,18},{18,2},{3,19},{19,3},{4,20},{20... | collective-permute-start | bytes 589832 | tf_op jit(solution)/shard_map/ppermute | solution.py:31
  64.7 7.8 %collective-permute-start.14 = (bf16[2,256,1536]{2,1,0:T(8,128)(2,1)S(1)}, bf16[2,256,1536]{2,1,0:T(8,128)(2,1)S(1)}, u32[]{:S(2)}, u32[]{:S(2)}) collective-permute-start(bf16[2,256,1536]{2,1,0:T(8,128)(2,1)S(1)} %beside.1), channel_id=1, source_target_pairs={{0,4},{4,0},{8,12},{12,8},{1,5},{5,1},{9,13},{13,9},{2,6},{6,2},{1... | collective-permute-start | bytes 4718600 | tf_op jit(solution)/shard_map/ppermute | solution.py:27
  64.8 7.8 %collective-permute-start.18 = (bf16[768,128]{1,0:T(8,128)(2,1)S(1)}, bf16[768,128]{1,0:T(8,128)(2,1)S(1)}, u32[]{:S(2)}, u32[]{:S(2)}) collective-permute-start(bf16[768,128]{1,0:T(8,128)(2,1)S(1)} %get-tuple-element.60), channel_id=1, source_target_pairs={{0,16},{16,0},{1,17},{17,1},{2,18},{18,2},{3,19},{19,3},{4,20},{20... | collective-permute-start | bytes 589832 | tf_op jit(solution)/shard_map/ppermute | solution.py:31
  66.3 10.0 %collective-permute-start.22 = (bf16[768,128]{1,0:T(8,128)(2,1)S(1)}, bf16[768,128]{1,0:T(8,128)(2,1)S(1)}, u32[]{:S(2)}, u32[]{:S(2)}) collective-permute-start(bf16[768,128]{1,0:T(8,128)(2,1)S(1)} %get-tuple-element.64), channel_id=1, source_target_pairs={{0,16},{16,0},{1,17},{17,1},{2,18},{18,2},{3,19},{19,3},{4,20},{20... | collective-permute-start | bytes 589832 | tf_op jit(solution)/shard_map/ppermute | solution.py:31
  66.9 8.6 %collective-permute-start.15 = (bf16[768,128]{1,0:T(8,128)(2,1)S(1)}, bf16[768,128]{1,0:T(8,128)(2,1)S(1)}, u32[]{:S(2)}, u32[]{:S(2)}) collective-permute-start(bf16[768,128]{1,0:T(8,128)(2,1)S(1)} %collective-permute-done.13.refs_1_.refs_10_), channel_id=1, source_target_pairs={{0,8},{4,12},{8,0},{12,4},{1,9},{5,13},{9,1},{13,5},{2,10},{6,14},... | collective-permute-start | bytes 589832 | tf_op jit(solution)/shard_map/ppermute | solution.py:27
  72.6 6.0 %collective-permute-start.19 = (bf16[768,128]{1,0:T(8,128)(2,1)S(1)}, bf16[768,128]{1,0:T(8,128)(2,1)S(1)}, u32[]{:S(2)}, u32[]{:S(2)}) collective-permute-start(bf16[768,128]{1,0:T(8,128)(2,1)S(1)} %tie.6.refs_14_), channel_id=1, source_target_pairs={{0,8},{4,12},{8,0},{12,4},{1,9},{5,13},{9,1},{13,5},{2,10},{6,14},... | collective-permute-start | bytes 589832 | tf_op jit(solution)/shard_map/ppermute | solution.py:27
  74.0 4.6 %collective-permute-start.16 = (bf16[768,128]{1,0:T(8,128)(2,1)S(1)}, bf16[768,128]{1,0:T(8,128)(2,1)S(1)}, u32[]{:S(2)}, u32[]{:S(2)}) collective-permute-start(bf16[768,128]{1,0:T(8,128)(2,1)S(1)} %collective-permute-done.13.refs_1_.refs_10_), channel_id=1, source_target_pairs={{0,4},{4,0},{8,12},{12,8},{1,5},{5,1},{9,13},{13,9},{2,6},{6,2},{1... | collective-permute-start | bytes 589832 | tf_op jit(solution)/shard_map/ppermute | solution.py:27
  74.0 7.3 %collective-permute-start.24 = (bf16[768,128]{1,0:T(8,128)(2,1)S(1)}, bf16[768,128]{1,0:T(8,128)(2,1)S(1)}, u32[]{:S(2)}, u32[]{:S(2)}) collective-permute-start(bf16[768,128]{1,0:T(8,128)(2,1)S(1)} %get-tuple-element.65), channel_id=1, source_target_pairs={{0,16},{16,0},{1,17},{17,1},{2,18},{18,2},{3,19},{19,3},{4,20},{20... | collective-permute-start | bytes 589832 | tf_op jit(solution)/shard_map/ppermute | solution.py:31
  75.5 6.5 %collective-permute-start.17 = (bf16[768,128]{1,0:T(8,128)(2,1)S(1)}, bf16[768,128]{1,0:T(8,128)(2,1)S(1)}, u32[]{:S(2)}, u32[]{:S(2)}) collective-permute-start(bf16[768,128]{1,0:T(8,128)(2,1)S(1)} %collective-permute-done.15.refs_11_), channel_id=1, source_target_pairs={{0,4},{4,0},{8,12},{12,8},{1,5},{5,1},{9,13},{13,9},{2,6},{6,2},{1... | collective-permute-start | bytes 589832 | tf_op jit(solution)/shard_map/ppermute | solution.py:27
  76.3 5.7 %collective-permute-start.20 = (bf16[768,128]{1,0:T(8,128)(2,1)S(1)}, bf16[768,128]{1,0:T(8,128)(2,1)S(1)}, u32[]{:S(2)}, u32[]{:S(2)}) collective-permute-start(bf16[768,128]{1,0:T(8,128)(2,1)S(1)} %tie.6.refs_14_), channel_id=1, source_target_pairs={{0,4},{4,0},{8,12},{12,8},{1,5},{5,1},{9,13},{13,9},{2,6},{6,2},{1... | collective-permute-start | bytes 589832 | tf_op jit(solution)/shard_map/ppermute | solution.py:27
  78.6 3.4 %collective-permute-start.21 = (bf16[768,128]{1,0:T(8,128)(2,1)S(1)}, bf16[768,128]{1,0:T(8,128)(2,1)S(1)}, u32[]{:S(2)}, u32[]{:S(2)}) collective-permute-start(bf16[768,128]{1,0:T(8,128)(2,1)S(1)} %collective-permute-done.19.refs_15_), channel_id=1, source_target_pairs={{0,4},{4,0},{8,12},{12,8},{1,5},{5,1},{9,13},{13,9},{2,6},{6,2},{1... | collective-permute-start | bytes 589832 | tf_op jit(solution)/shard_map/ppermute | solution.py:27
  78.6 8.8 %collective-permute-start.23 = (bf16[768,128]{1,0:T(8,128)(2,1)S(1)}, bf16[768,128]{1,0:T(8,128)(2,1)S(1)}, u32[]{:S(2)}, u32[]{:S(2)}) collective-permute-start(bf16[768,128]{1,0:T(8,128)(2,1)S(1)} %collective-permute-done.22.refs_0_), channel_id=1, source_target_pairs={{0,8},{4,12},{8,0},{12,4},{1,9},{5,13},{9,1},{13,5},{2,10},{6,14},... | collective-permute-start | bytes 589832 | tf_op jit(solution)/shard_map/ppermute | solution.py:27
  81.3 8.8 %collective-permute-start.25 = (bf16[768,128]{1,0:T(8,128)(2,1)S(1)}, bf16[768,128]{1,0:T(8,128)(2,1)S(1)}, u32[]{:S(2)}, u32[]{:S(2)}) collective-permute-start(bf16[768,128]{1,0:T(8,128)(2,1)S(1)} %collective-permute-done.24.refs_2_), channel_id=1, source_target_pairs={{0,8},{4,12},{8,0},{12,4},{1,9},{5,13},{9,1},{13,5},{2,10},{6,14},... | collective-permute-start | bytes 589832 | tf_op jit(solution)/shard_map/ppermute | solution.py:27
  90.1 1.4 %collective-permute-start.26 = (bf16[768,128]{1,0:T(8,128)(2,1)S(1)}, bf16[768,128]{1,0:T(8,128)(2,1)S(1)}, u32[]{:S(2)}, u32[]{:S(2)}) collective-permute-start(bf16[768,128]{1,0:T(8,128)(2,1)S(1)} %get-tuple-element.67.refs_10_), channel_id=1, source_target_pairs={{0,4},{4,0},{8,12},{12,8},{1,5},{5,1},{9,13},{13,9},{2,6},{6,2},{1... | collective-permute-start | bytes 589832 | tf_op jit(solution)/shard_map/ppermute | solution.py:27
  90.1 2.9 %collective-permute-start.27 = (bf16[768,128]{1,0:T(8,128)(2,1)S(1)}, bf16[768,128]{1,0:T(8,128)(2,1)S(1)}, u32[]{:S(2)}, u32[]{:S(2)}) collective-permute-start(bf16[768,128]{1,0:T(8,128)(2,1)S(1)} %get-tuple-element.68.refs_11_), channel_id=1, source_target_pairs={{0,4},{4,0},{8,12},{12,8},{1,5},{5,1},{9,13},{13,9},{2,6},{6,2},{1... | collective-permute-start | bytes 589832 | tf_op jit(solution)/shard_map/ppermute | solution.py:27
  90.6 2.5 %collective-permute-start.28 = (bf16[768,128]{1,0:T(8,128)(2,1)S(1)}, bf16[768,128]{1,0:T(8,128)(2,1)S(1)}, u32[]{:S(2)}, u32[]{:S(2)}) collective-permute-start(bf16[768,128]{1,0:T(8,128)(2,1)S(1)} %get-tuple-element.69.refs_14_), channel_id=1, source_target_pairs={{0,4},{4,0},{8,12},{12,8},{1,5},{5,1},{9,13},{13,9},{2,6},{6,2},{1... | collective-permute-start | bytes 589832 | tf_op jit(solution)/shard_map/ppermute | solution.py:27
  90.7 2.5 %collective-permute-start.29 = (bf16[768,128]{1,0:T(8,128)(2,1)S(1)}, bf16[768,128]{1,0:T(8,128)(2,1)S(1)}, u32[]{:S(2)}, u32[]{:S(2)}) collective-permute-start(bf16[768,128]{1,0:T(8,128)(2,1)S(1)} %get-tuple-element.70.refs_15_), channel_id=1, source_target_pairs={{0,4},{4,0},{8,12},{12,8},{1,5},{5,1},{9,13},{13,9},{2,6},{6,2},{1... | collective-permute-start | bytes 589832 | tf_op jit(solution)/shard_map/ppermute | solution.py:27
  91.2 6.7 %collective-permute-start.30 = (bf16[2,128,384]{2,1,0:T(8,128)(2,1)S(1)}, bf16[2,128,384]{2,1,0:T(8,128)(2,1)S(1)}, u32[]{:S(2)}, u32[]{:S(2)}) collective-permute-start(bf16[2,128,384]{2,1,0:T(8,128)(2,1)S(1)} %get-tuple-element.72), channel_id=1, source_target_pairs={{0,4},{4,0},{8,12},{12,8},{1,5},{5,1},{9,13},{13,9},{2,6},{6,2},{1... | collective-permute-start | bytes 589832 | tf_op jit(solution)/shard_map/ppermute | solution.py:27
  91.6 7.7 %collective-permute-start.31 = (bf16[2,128,384]{2,1,0:T(8,128)(2,1)S(1)}, bf16[2,128,384]{2,1,0:T(8,128)(2,1)S(1)}, u32[]{:S(2)}, u32[]{:S(2)}) collective-permute-start(bf16[2,128,384]{2,1,0:T(8,128)(2,1)S(1)} %get-tuple-element.73), channel_id=1, source_target_pairs={{0,8},{4,12},{8,0},{12,4},{1,9},{5,13},{9,1},{13,5},{2,10},{6,14},... | collective-permute-start | bytes 589832 | tf_op jit(solution)/shard_map/ppermute | solution.py:27
  93.0 9.9 %collective-permute-start.32 = (bf16[2,128,384]{2,1,0:T(8,128)(2,1)S(1)}, bf16[2,128,384]{2,1,0:T(8,128)(2,1)S(1)}, u32[]{:S(2)}, u32[]{:S(2)}) collective-permute-start(bf16[2,128,384]{2,1,0:T(8,128)(2,1)S(1)} %get-tuple-element.75), channel_id=1, source_target_pairs={{0,12},{4,8},{8,4},{12,0},{1,13},{5,9},{9,5},{13,1},{2,14},{6,10},... | collective-permute-start | bytes 589832 | tf_op jit(solution)/shard_map/ppermute | solution.py:27
  100.5 5.9 %collective-permute-start.36 = (bf16[96,256]{1,0:T(8,128)(2,1)S(1)}, bf16[96,256]{1,0:T(8,128)(2,1)S(1)}, u32[]{:S(2)}, u32[]{:S(2)}) collective-permute-start(bf16[96,256]{1,0:T(8,128)(2,1)S(1)} %get-tuple-element.81), channel_id=1, source_target_pairs={{0,1},{1,2},{2,3},{3,0},{4,5},{5,6},{6,7},{7,4},{8,9},{9,10},{10,1... | collective-permute-start | bytes 147464 | tf_op jit(solution)/shard_map/ppermute | solution.py:36
  101.1 9.5 %collective-permute-start.33 = (bf16[128,384]{1,0:T(8,128)(2,1)S(1)}, bf16[128,384]{1,0:T(8,128)(2,1)S(1)}, u32[]{:S(2)}, u32[]{:S(2)}) collective-permute-start(bf16[128,384]{1,0:T(8,128)(2,1)S(1)} %get-tuple-element.77), channel_id=1, source_target_pairs={{0,4},{4,0},{8,12},{12,8},{1,5},{5,1},{9,13},{13,9},{2,6},{6,2},{1... | collective-permute-start | bytes 294920 | tf_op jit(solution)/shard_map/ppermute | solution.py:27
  101.1 9.5 %collective-permute-start.34 = (bf16[128,384]{1,0:T(8,128)(2,1)S(1)}, bf16[128,384]{1,0:T(8,128)(2,1)S(1)}, u32[]{:S(2)}, u32[]{:S(2)}) collective-permute-start(bf16[128,384]{1,0:T(8,128)(2,1)S(1)} %get-tuple-element.78), channel_id=1, source_target_pairs={{0,8},{4,12},{8,0},{12,4},{1,9},{5,13},{9,1},{13,5},{2,10},{6,14},... | collective-permute-start | bytes 294920 | tf_op jit(solution)/shard_map/ppermute | solution.py:27
  102.6 7.9 %collective-permute-start.35 = (bf16[128,384]{1,0:T(8,128)(2,1)S(1)}, bf16[128,384]{1,0:T(8,128)(2,1)S(1)}, u32[]{:S(2)}, u32[]{:S(2)}) collective-permute-start(bf16[128,384]{1,0:T(8,128)(2,1)S(1)} %get-tuple-element.79), channel_id=1, source_target_pairs={{0,12},{4,8},{8,4},{12,0},{1,13},{5,9},{9,5},{13,1},{2,14},{6,10},... | collective-permute-start | bytes 294920 | tf_op jit(solution)/shard_map/ppermute | solution.py:27
  103.0 6.1 %collective-permute-start.37 = (bf16[96,256]{1,0:T(8,128)(2,1)S(1)}, bf16[96,256]{1,0:T(8,128)(2,1)S(1)}, u32[]{:S(2)}, u32[]{:S(2)}) collective-permute-start(bf16[96,256]{1,0:T(8,128)(2,1)S(1)} %get-tuple-element.82), channel_id=1, source_target_pairs={{0,2},{1,3},{2,0},{3,1},{4,6},{5,7},{6,4},{7,5},{8,10},{9,11},{10,... | collective-permute-start | bytes 147464 | tf_op jit(solution)/shard_map/ppermute | solution.py:36
  106.5 4.1 %collective-permute-start.38 = (bf16[96,256]{1,0:T(8,128)(2,1)S(1)}, bf16[96,256]{1,0:T(8,128)(2,1)S(1)}, u32[]{:S(2)}, u32[]{:S(2)}) collective-permute-start(bf16[96,256]{1,0:T(8,128)(2,1)S(1)} %get-tuple-element.83), channel_id=1, source_target_pairs={{0,3},{1,0},{2,1},{3,2},{4,7},{5,4},{6,5},{7,6},{8,11},{9,8},{10,9... | collective-permute-start | bytes 147464 | tf_op jit(solution)/shard_map/ppermute | solution.py:36

commit v17 on v16

--- a/solution.py
+++ b/solution.py
@@ -22,18 +22,13 @@
     return lax.ppermute(value, axis, [(source, (source + 1) % count) for source in range(count)])
 
 
-def swap(value, bit):
-    count = lax.axis_size("seq")
-    return lax.ppermute(value, "seq", [(source, source ^ bit) for source in range(count)])
+def swap(value, bit, axis="seq"):
+    count = lax.axis_size(axis)
+    return lax.ppermute(value, axis, [(source, source ^ bit) for source in range(count)])
 
 
 def handed_over(value):
     return lax.ppermute(value, "pipe", [(0, 1), (1, 0)])
-
-
-def shifted(value, axis, shift):
-    count = lax.axis_size(axis)
-    return lax.ppermute(value, axis, [(source, (source + shift) % count) for source in range(count)])
 
 
 def fold(index):
@@ -105,9 +100,10 @@
         weights[pl.ds(pl.multiple_of(at * rows, 16), rows)] = block[...]
 
 
-def place_kernel(part, hops, near, far, chunk, weights):
+def place_kernel(part, hops, near, far, chunk, next_chunk, weights):
     place(0, hops, [near.at[0, part], near.at[1, part], far.at[0, part], far.at[1, part]], weights)
     place(1, hops, [chunk.at[m] for m in range(4)], weights)
+    place(2, hops, [next_chunk.at[m] for m in range(4)], weights)
 
 
 def first_kernel(turns, far, incoming, contacts, out, states):
@@ -235,7 +231,7 @@
         second, embed, relay = opened(take(3)), take(1)[0], take(2 * pieces)
     else:
         scaled, scales, own_hidden = take(3)
-    chunks = take(2) if step == 0 else None
+    chunks = take(1) if step == 0 else None
     weights = take(len(parts))
     left = take(1)[0] if parts == (1,) else None
     sends = take(1)[0] if len(parts) == 1 else None
@@ -254,8 +250,7 @@
     _, batch = turn_and_batch(step, turns)
 
     if step == 0:
-        for hop, chunk in zip((2, 3), chunks):
-            place(hop, hops, [chunk.at[m] for m in range(pieces)], weights[0])
+        place(hops - 1, hops, [chunks[0].at[m] for m in range(pieces)], weights[0])
 
     def normalize(relayed):
         total = jnp.zeros((frames, 128), jnp.float32)
@@ -436,7 +431,7 @@
     g_rows = cols // hops
     own_grad[...] = total[pl.ds(pl.multiple_of(rep * g_rows, 8), g_rows)]
     for shift in range(1, hops):
-        at = pl.multiple_of(lax.rem(rep + shift, hops) * g_rows, 8)
+        at = pl.multiple_of((rep ^ shift) * g_rows, 8)
         grads[shift - 1][...] = total[pl.ds(at, g_rows)].astype(jnp.bfloat16)
     copy.wait()
 
@@ -543,7 +538,7 @@
     near_next = ring_step(near)
     far = paired("far", [near_next], blocks[2:])
     far_next = ring_step(far)
-    rings, partial = [], []
+    rings = []
     for part in range(2):
         chunk = call(
             functools.partial(part_kernel, part),
@@ -554,19 +549,9 @@
             out_specs=vmem,
         )
         rings.append([chunk])
-        partial.append(
-            call(
-                functools.partial(place_kernel, part, hops),
-                "place%d" % part,
-                pltpu.VMEM((width, cols), kind),
-                [vmem] * 3,
-                [pin(near), pin(far), pin(chunk)],
-                out_specs=vmem,
-            )
-        )
-    for hop in range(2):
-        for ring in rings:
-            ring.append(ring_step(ring[-1]))
+    for ring in rings:
+        ring.append(ring_step(ring[-1]))
+    rings[0].append(ring_step(rings[0][-1]))
 
     def tie(values, deps):
         return call(
@@ -618,6 +603,21 @@
         out_specs=vmem,
     )
     second = [mine, swap(mine, 2)]
+
+    (rings[1][1],) = tie([rings[1][1]], [prepared[0]])
+    rings[1].append(ring_step(rings[1][1]))
+    partial = []
+    for part, ring in enumerate(rings):
+        partial.append(
+            call(
+                functools.partial(place_kernel, part, hops),
+                "place%d" % part,
+                pltpu.VMEM((width, cols), kind),
+                [vmem] * 4,
+                [pin(near), pin(far), pin(ring[0]), pin(ring[1])],
+                out_specs=vmem,
+            )
+        )
 
     common = [key_bias, timesteps, norm_gain, time_freq, attn_gate, keyframes]
 
@@ -666,10 +666,9 @@
         for step in range(2):
             large = [prepared[step], prepared[2 + step], prepared[4 + step]]
             if step == 0:
-                chunks = rings[part][1:]
+                chunks = rings[part][2:]
                 if part:
-                    (last_chunk,) = tie(chunks[1:], [relays[0][0][0], lefts[1]])
-                    chunks = [chunks[0], last_chunk]
+                    chunks = list(tie(chunks, [relays[0][0][0], lefts[1]]))
                 large += chunks
             large += [weights[part]]
             aliases = {len(common) + len(large) - 1: 2} if step == 0 else {}
@@ -744,7 +743,7 @@
     )
     late, grads, held = settled[:seq_count], settled[seq_count:-1], settled[-1]
     late = [late[0]] + [swap(late[m], m) for m in range(1, seq_count)]
-    grads = [grads[0]] + [shifted(grads[k], "dp", k) for k in range(1, hops)]
+    grads = [grads[0]] + [swap(grads[k], k, "dp") for k in range(1, hops)]
     section_out, grad_rows = call(
         functools.partial(finish_kernel, seq_count, hops),
         "finish",

time: 112 us -> 113 us (level)
  starting transfers between devices: 32.9 us -> 34.9 us
  waiting for transfers between devices: 49.2 us -> 47.7 us
    ppermute x29, starting transfers between devices: 16.9 us -> 18.5 us  [swap(): lax.ppermute(value, axis, [(source, source ^ bit) for source in range(cou...]
    pallas_call x24 -> x25, Pallas kernels: 28.9 us -> 28.9 us  [call(): pl.pallas_call(kernel, out_shape=out_shape, in_specs=in_specs, scratch_sh...]
where the time goes in v17:
time: 113 us
  waiting for transfers between devices  47.7 us (42%)
  starting transfers between devices  34.9 us (31%)
  Pallas kernels  28.9 us (26%)
    pallas_call x25, Pallas kernels, call(): pl.pallas_call(kernel, out_shape=out_shape, in_specs=in_specs, scratch_sh...  28.9 us
    ppermute x6, waiting for transfers between devices, ring_step(): return lax.ppermute(value, 'dp', pairs)  24.3 us
    ppermute x29, waiting for transfers between devices, swap(): lax.ppermute(value, axis, [(source, source ^ bit) for source in range(cou...  18.6 us
    ppermute x29, starting transfers between devices, swap(): lax.ppermute(value, axis, [(source, source ^ bit) for source in range(cou...  18.5 us
    ppermute x6, starting transfers between devices, ring_step(): return lax.ppermute(value, 'dp', pairs)  11.3 us
    ppermute x4, starting transfers between devices, handed_over(): return lax.ppermute(value, 'pipe', [(0, 1), (1, 0)])  5.14 us
    ppermute x4, waiting for transfers between devices, handed_over(): return lax.ppermute(value, 'pipe', [(0, 1), (1, 0)])  4.83 us
  transfers between devices with their start and end apart: 39, of which 19 were waited for; matrix products, arithmetic and copies ran while one was open for 0% of the time, Pallas kernels for 23%

profile of v17, /device:TPU:0, one launch (start us, length us, event | category | flops | bytes accessed | tf_op | source)
XLA Modules:
  0.0 112.7 jit_solution(7347320739081418802)
XLA Ops:
  0.7 1.5 %pack.1 = (bf16[2,96,384]{2,1,0:T(8,128)(2,1)S(1)}, bf16[2,96,384]{2,1,0:T(8,128)(2,1)S(1)}, bf16[2,96,384]{2,1,0:T(8,128)(2,1)S(1)}, bf16[2,96,384]{2,1,0:T(8,128)(2,1)S(1)}) custom-call(bf16[1,96,1536]{2,1,0:T(8,128)(2,1)} %wq.1, bf16[1,96,1536]{2,1,0:T(8,128)(2,1)} %wkv.1), custom_call_target="tpu_custom_call" | custom-call | tf_op jit(solution)/shard_map/pack/pallas_call | solution.py:497
  2.1 0.5 collective-permute-start
  2.7 1.0 collective-permute-done.refs_1_
  3.7 3.0 %collective-permute-start.1 = (bf16[2,2,96,384]{3,2,1,0:T(8,128)(2,1)S(1)}, bf16[2,2,96,384]{3,2,1,0:T(8,128)(2,1)S(1)}, u32[]{:S(2)}, u32[]{:S(2)}) collective-permute-start(bf16[2,2,96,384]{3,2,1,0:T(8,128)(2,1)S(1)} %near.1), channel_id=1, source_target_pairs={{0,1},{1,3},{3,2},{2,0},{4,5},{5,7},{7,6},{6,4},{8,9},{9,11},{11,1... | collective-permute-start | bytes 884744 | tf_op jit(solution)/shard_map/ppermute | solution.py:41
  6.7 1.5 %collective-permute-start.2 = (bf16[2,96,384]{2,1,0:T(8,128)(2,1)S(1)}, bf16[2,96,384]{2,1,0:T(8,128)(2,1)S(1)}, u32[]{:S(2)}, u32[]{:S(2)}) collective-permute-start(bf16[2,96,384]{2,1,0:T(8,128)(2,1)S(1)} %get-tuple-element.46), channel_id=1, source_target_pairs={{0,8},{4,12},{8,0},{12,4},{1,9},{5,13},{9,1},{13,5},{2,10},{6,14},... | collective-permute-start | bytes 442376 | tf_op jit(solution)/shard_map/ppermute | solution.py:27
  8.2 5.2 %collective-permute-done.2.refs_1_ = bf16[2,96,384]{2,1,0:T(8,128)(2,1)S(1)} collective-permute-done((bf16[2,96,384]{2,1,0:T(8,128)(2,1)S(1)}, bf16[2,96,384]{2,1,0:T(8,128)(2,1)S(1)}, u32[]{:S(2)}, u32[]{:S(2)}) %collective-permute-start.2) | collective-permute-done | bytes 147488 | tf_op jit(solution)/shard_map/ppermute | solution.py:27
  13.4 1.1 collective-permute-done.3.refs_2_
  14.5 0.5 collective-permute-done.1.refs_0_.near
  15.1 0.1 first.1.refs_0_
  15.1 1.6 %collective-permute-start.4 = (bf16[272,1536]{1,0:T(8,128)(2,1)S(1)}, bf16[272,1536]{1,0:T(8,128)(2,1)S(1)}, u32[]{:S(2)}, u32[]{:S(2)}) collective-permute-start(bf16[272,1536]{1,0:T(8,128)(2,1)S(1)} %first.1.refs_0_), channel_id=1, source_target_pairs={{0,8},{4,12},{8,0},{12,4},{1,9},{5,13},{9,1},{13,5},{2,10},{6,14},... | collective-permute-start | bytes 2506760 | tf_op jit(solution)/shard_map/ppermute | solution.py:27
  16.7 1.9 %collective-permute-start.5 = (bf16[2,2,96,384]{3,2,1,0:T(8,128)(2,1)S(1)}, bf16[2,2,96,384]{3,2,1,0:T(8,128)(2,1)S(1)}, u32[]{:S(2)}, u32[]{:S(2)}) collective-permute-start(bf16[2,2,96,384]{3,2,1,0:T(8,128)(2,1)S(1)} %far.1), channel_id=1, source_target_pairs={{0,1},{1,3},{3,2},{2,0},{4,5},{5,7},{7,6},{6,4},{8,9},{9,11},{11,1... | collective-permute-start | bytes 884744 | tf_op jit(solution)/shard_map/ppermute | solution.py:41
  18.6 7.9 %collective-permute-done.5.far = bf16[2,2,96,384]{3,2,1,0:T(8,128)(2,1)S(1)} collective-permute-done((bf16[2,2,96,384]{3,2,1,0:T(8,128)(2,1)S(1)}, bf16[2,2,96,384]{3,2,1,0:T(8,128)(2,1)S(1)}, u32[]{:S(2)}, u32[]{:S(2)}) %collective-permute-start.5) | collective-permute-done | bytes 294944 | tf_op jit(solution)/shard_map/ppermute | solution.py:41
  26.5 1.7 %collective-permute-start.6 = (bf16[4,96,384]{2,1,0:T(8,128)(2,1)S(1)}, bf16[4,96,384]{2,1,0:T(8,128)(2,1)S(1)}, u32[]{:S(2)}, u32[]{:S(2)}) collective-permute-start(bf16[4,96,384]{2,1,0:T(8,128)(2,1)S(1)} %part0.1.chunk), channel_id=1, source_target_pairs={{0,1},{1,3},{3,2},{2,0},{4,5},{5,7},{7,6},{6,4},{8,9},{9,11},{11,1... | collective-permute-start | bytes 884744 | tf_op jit(solution)/shard_map/ppermute | solution.py:41
  28.3 1.7 %collective-permute-start.7 = (bf16[4,96,384]{2,1,0:T(8,128)(2,1)S(1)}, bf16[4,96,384]{2,1,0:T(8,128)(2,1)S(1)}, u32[]{:S(2)}, u32[]{:S(2)}) collective-permute-start(bf16[4,96,384]{2,1,0:T(8,128)(2,1)S(1)} %part1.1.chunk), channel_id=1, source_target_pairs={{0,1},{1,3},{3,2},{2,0},{4,5},{5,7},{7,6},{6,4},{8,9},{9,11},{11,1... | collective-permute-start | bytes 884744 | tf_op jit(solution)/shard_map/ppermute | solution.py:41
  30.0 7.4 %collective-permute-done.6.refs_1_.next_chunk = bf16[4,96,384]{2,1,0:T(8,128)(2,1)S(1)} collective-permute-done((bf16[4,96,384]{2,1,0:T(8,128)(2,1)S(1)}, bf16[4,96,384]{2,1,0:T(8,128)(2,1)S(1)}, u32[]{:S(2)}, u32[]{:S(2)}) %collective-permute-start.6) | collective-permute-done | bytes 294944 | tf_op jit(solution)/shard_map/ppermute | solution.py:41
  37.4 4.4 %collective-permute-done.7.refs_2_.refs_0_ = bf16[4,96,384]{2,1,0:T(8,128)(2,1)S(1)} collective-permute-done((bf16[4,96,384]{2,1,0:T(8,128)(2,1)S(1)}, bf16[4,96,384]{2,1,0:T(8,128)(2,1)S(1)}, u32[]{:S(2)}, u32[]{:S(2)}) %collective-permute-start.7) | collective-permute-done | bytes 294944 | tf_op jit(solution)/shard_map/ppermute | solution.py:41
  41.8 0.1 collective-permute-start.10
  42.0 0.7 collective-permute-start.8
  42.6 1.4 %collective-permute-start.12 = (bf16[4,96,384]{2,1,0:T(8,128)(2,1)S(1)}, bf16[4,96,384]{2,1,0:T(8,128)(2,1)S(1)}, u32[]{:S(2)}, u32[]{:S(2)}) collective-permute-start(bf16[4,96,384]{2,1,0:T(8,128)(2,1)S(1)} %collective-permute-done.6.refs_1_.next_chunk), channel_id=1, source_target_pairs={{0,1},{1,3},{3,2},{2,0},{4,5},{5,7},{7,6},{6,4},{8,9},{9,11},{11,1... | collective-permute-start | bytes 884744 | tf_op jit(solution)/shard_map/ppermute | solution.py:41
  44.0 0.2 collective-permute-done.10.refs_3_
  44.3 3.3 %norm.1 = (bf16[512,1536]{1,0:T(8,128)(2,1)S(1)}, bf16[512,1536]{1,0:T(8,128)(2,1)S(1)}, f32[512,128]{1,0:T(8,128)S(1)}, f32[512,128]{1,0:T(8,128)S(1)}, f32[512...) custom-call(s32[1,4]{1,0:T(1,128)S(1)} %bitcast.5, ...), custom_call_target="tpu_custom_call" | custom-call | tf_op jit(solution)/shard_map/norm/pallas_call | solution.py:497
  47.7 1.6 %collective-permute-start.11 = (bf16[4,96,384]{2,1,0:T(8,128)(2,1)S(1)}, bf16[4,96,384]{2,1,0:T(8,128)(2,1)S(1)}, u32[]{:S(2)}, u32[]{:S(2)}) collective-permute-start(bf16[4,96,384]{2,1,0:T(8,128)(2,1)S(1)} %tie.6.next_chunk), channel_id=1, source_target_pairs={{0,1},{1,3},{3,2},{2,0},{4,5},{5,7},{7,6},{6,4},{8,9},{9,11},{11,1... | collective-permute-start | bytes 884744 | tf_op jit(solution)/shard_map/ppermute | solution.py:41
  49.2 0.1 place0.1.refs_10_
  49.3 4.0 %collective-permute-done.12.refs_9_ = bf16[4,96,384]{2,1,0:T(8,128)(2,1)S(1)} collective-permute-done((bf16[4,96,384]{2,1,0:T(8,128)(2,1)S(1)}, bf16[4,96,384]{2,1,0:T(8,128)(2,1)S(1)}, u32[]{:S(2)}, u32[]{:S(2)}) %collective-permute-start.12) | collective-permute-done | bytes 294944 | tf_op jit(solution)/shard_map/ppermute | solution.py:41
  53.4 2.7 %step0a.1 = (bf16[768,128]{1,0:T(8,128)(2,1)S(1)}, bf16[512,256]{1,0:T(8,128)(2,1)S(1)}, bf16[1536,384]{1,0:T(8,128)(2,1)S(1)}) custom-call(f32[1,16]{1,0:T(1,128)S(1)} %copy-done.8, s32[1,4]{1,0:T(1,128)S(1)} %bitcast.6, f32[1,1536]{1,0:T(1,128)S(1)} %copy-done.1, f32[1,1536]{1,0:T(1,128)S(1)} %copy-done.2, ...), custom_call_target="tpu_custom_call", output_to_operand_aliasing={{2}: (10, {})} | custom-call | flops 805306368 | bytes 1572864 | tf_op jit(solution)/shard_map/step0a/pallas_call | solution.py:497
  56.1 1.5 %collective-permute-start.13 = (bf16[768,128]{1,0:T(8,128)(2,1)S(1)}, bf16[768,128]{1,0:T(8,128)(2,1)S(1)}, u32[]{:S(2)}, u32[]{:S(2)}) collective-permute-start(bf16[768,128]{1,0:T(8,128)(2,1)S(1)} %get-tuple-element.51), channel_id=1, source_target_pairs={{0,16},{16,0},{1,17},{17,1},{2,18},{18,2},{3,19},{19,3},{4,20},{20... | collective-permute-start | bytes 589832 | tf_op jit(solution)/shard_map/ppermute | solution.py:31
  57.6 0.1 place1.1.refs_10_
  57.7 2.7 %step1a.1 = (bf16[768,128]{1,0:T(8,128)(2,1)S(1)}, bf16[512,256]{1,0:T(8,128)(2,1)S(1)}) custom-call(f32[1,16]{1,0:T(1,128)S(1)} %copy-done.8, s32[1,4]{1,0:T(1,128)S(1)} %bitcast.7, f32[1,1536]{1,0:T(1,128)S(1)} %copy-done.1, f32[1,1536]{1,0:T(1,128)S(1)} %copy-done.2, f32[1,1536]{1,0:T(1,128)S(1)} %copy-done.4, s32[4,1,512]{2,1,0:T(1,128)S(1)} %copy-done.3, ...), custom_call_target="tpu_custom_call" | custom-call | flops 805306368 | bytes 1572864 | tf_op jit(solution)/shard_map/step1a/pallas_call | solution.py:497
  60.4 1.4 %collective-permute-done.13.refs_1_.refs_10_ = bf16[768,128]{1,0:T(8,128)(2,1)S(1)} collective-permute-done((bf16[768,128]{1,0:T(8,128)(2,1)S(1)}, bf16[768,128]{1,0:T(8,128)(2,1)S(1)}, u32[]{:S(2)}, u32[]{:S(2)}) %collective-permute-start.13) | collective-permute-done | bytes 196640 | tf_op jit(solution)/shard_map/ppermute | solution.py:31
  61.9 2.8 %step0b.1 = (bf16[768,128]{1,0:T(8,128)(2,1)S(1)}, bf16[4,128,384]{2,1,0:T(8,128)(2,1)S(1)}, bf16[1536,384]{1,0:T(8,128)(2,1)S(1)}) custom-call(f32[1,16]{1,0:T(1,128)S(1)} %copy-done.8, s32[1,4]{1,0:T(1,128)S(1)} %bitcast.8, f32[1,1536]{1,0:T(1,128)S(1)} %copy-done.1, f32[1,1536]{1,0:T(1,128)S(1)} %copy-done.2, ...), custom_call_target="tpu_custom_call", output_to_operand_aliasing={{2}: (10, {})} | custom-call | flops 805306368 | bytes 1572864 | tf_op jit(solution)/shard_map/step0b/pallas_call | solution.py:497
  64.6 0.1 beside.1
  64.7 0.1 collective-permute-start.14
  64.8 1.5 %collective-permute-start.18 = (bf16[768,128]{1,0:T(8,128)(2,1)S(1)}, bf16[768,128]{1,0:T(8,128)(2,1)S(1)}, u32[]{:S(2)}, u32[]{:S(2)}) collective-permute-start(bf16[768,128]{1,0:T(8,128)(2,1)S(1)} %get-tuple-element.60), channel_id=1, source_target_pairs={{0,16},{16,0},{1,17},{17,1},{2,18},{18,2},{3,19},{19,3},{4,20},{20... | collective-permute-start | bytes 589832 | tf_op jit(solution)/shard_map/ppermute | solution.py:31
  66.4 0.6 collective-permute-start.22
  66.9 1.4 %collective-permute-start.15 = (bf16[768,128]{1,0:T(8,128)(2,1)S(1)}, bf16[768,128]{1,0:T(8,128)(2,1)S(1)}, u32[]{:S(2)}, u32[]{:S(2)}) collective-permute-start(bf16[768,128]{1,0:T(8,128)(2,1)S(1)} %collective-permute-done.13.refs_1_.refs_10_), channel_id=1, source_target_pairs={{0,8},{4,12},{8,0},{12,4},{1,9},{5,13},{9,1},{13,5},{2,10},{6,14},... | collective-permute-start | bytes 589832 | tf_op jit(solution)/shard_map/ppermute | solution.py:27
  68.4 2.7 %step1b.1 = (bf16[768,128]{1,0:T(8,128)(2,1)S(1)}, bf16[4,128,384]{2,1,0:T(8,128)(2,1)S(1)}) custom-call(f32[1,16]{1,0:T(1,128)S(1)} %copy-done.8, s32[1,4]{1,0:T(1,128)S(1)} %bitcast.9, f32[1,1536]{1,0:T(1,128)S(1)} %copy-done.1, f32[1,1536]{1,0:T(1,128)S(1)} %copy-done.2, f32[1,1536]{1,0:T(1,128)S(1)} %copy-done.4, s32[4,1,512]{2,1,0:T(1,128)S(1)} %copy-done.3, ...), custom_call_target="tpu_custom_call" | custom-call | flops 805306368 | bytes 1572864 | tf_op jit(solution)/shard_map/step1b/pallas_call | solution.py:497
  71.1 1.5 %collective-permute-done.18.refs_0_ = bf16[768,128]{1,0:T(8,128)(2,1)S(1)} collective-permute-done((bf16[768,128]{1,0:T(8,128)(2,1)S(1)}, bf16[768,128]{1,0:T(8,128)(2,1)S(1)}, u32[]{:S(2)}, u32[]{:S(2)}) %collective-permute-start.18) | collective-permute-done | bytes 196640 | tf_op jit(solution)/shard_map/ppermute | solution.py:31
  72.6 1.4 %collective-permute-start.19 = (bf16[768,128]{1,0:T(8,128)(2,1)S(1)}, bf16[768,128]{1,0:T(8,128)(2,1)S(1)}, u32[]{:S(2)}, u32[]{:S(2)}) collective-permute-start(bf16[768,128]{1,0:T(8,128)(2,1)S(1)} %tie.8.refs_14_), channel_id=1, source_target_pairs={{0,8},{4,12},{8,0},{12,4},{1,9},{5,13},{9,1},{13,5},{2,10},{6,14},... | collective-permute-start | bytes 589832 | tf_op jit(solution)/shard_map/ppermute | solution.py:27
  74.0 1.5 %collective-permute-start.24 = (bf16[768,128]{1,0:T(8,128)(2,1)S(1)}, bf16[768,128]{1,0:T(8,128)(2,1)S(1)}, u32[]{:S(2)}, u32[]{:S(2)}) collective-permute-start(bf16[768,128]{1,0:T(8,128)(2,1)S(1)} %get-tuple-element.65), channel_id=1, source_target_pairs={{0,16},{16,0},{1,17},{17,1},{2,18},{18,2},{3,19},{19,3},{4,20},{20... | collective-permute-start | bytes 589832 | tf_op jit(solution)/shard_map/ppermute | solution.py:31
  75.6 0.2 collective-permute-start.17
  75.8 0.6 collective-permute-done.22.refs_0_
  76.4 2.3 %collective-permute-done.19.refs_15_ = bf16[768,128]{1,0:T(8,128)(2,1)S(1)} collective-permute-done((bf16[768,128]{1,0:T(8,128)(2,1)S(1)}, bf16[768,128]{1,0:T(8,128)(2,1)S(1)}, u32[]{:S(2)}, u32[]{:S(2)}) %collective-permute-start.19) | collective-permute-done | bytes 196640 | tf_op jit(solution)/shard_map/ppermute | solution.py:27
  78.6 1.4 %collective-permute-start.23 = (bf16[768,128]{1,0:T(8,128)(2,1)S(1)}, bf16[768,128]{1,0:T(8,128)(2,1)S(1)}, u32[]{:S(2)}, u32[]{:S(2)}) collective-permute-start(bf16[768,128]{1,0:T(8,128)(2,1)S(1)} %collective-permute-done.22.refs_0_), channel_id=1, source_target_pairs={{0,8},{4,12},{8,0},{12,4},{1,9},{5,13},{9,1},{13,5},{2,10},{6,14},... | collective-permute-start | bytes 589832 | tf_op jit(solution)/shard_map/ppermute | solution.py:27
  80.1 1.3 %collective-permute-done.24.refs_2_ = bf16[768,128]{1,0:T(8,128)(2,1)S(1)} collective-permute-done((bf16[768,128]{1,0:T(8,128)(2,1)S(1)}, bf16[768,128]{1,0:T(8,128)(2,1)S(1)}, u32[]{:S(2)}, u32[]{:S(2)}) %collective-permute-start.24) | collective-permute-done | bytes 196640 | tf_op jit(solution)/shard_map/ppermute | solution.py:31
  81.4 0.7 collective-permute-start.25
  82.0 4.9 %step2ab.1.refs_2_.refs_0_ = bf16[4,128,384]{2,1,0:T(8,128)(2,1)S(1)} custom-call(f32[1,16]{1,0:T(1,128)S(1)} %copy-done.8, s32[1,4]{1,0:T(1,128)S(1)} %bitcast.10, f32[1,1536]{1,0:T(1,128)S(1)} %copy-done.1, f32[1,1536]{1,0:T(1,128)S(1)} %copy-done.2, f32[1,1536]{1,0:T(1,128)S(1)} %copy-done.4, s32[4,1,512]{2,1,0:T(1,128)S(1)} %copy-done.3, ...), custom_call_target="tpu_custom_call" | custom-call | flops 1610612736 | bytes 3145728 | tf_op jit(solution)/shard_map/step2ab/pallas_call | solution.py:497
  86.9 0.5 early.1
  87.4 2.8 %collective-permute-done.25.refs_3_ = bf16[768,128]{1,0:T(8,128)(2,1)S(1)} collective-permute-done((bf16[768,128]{1,0:T(8,128)(2,1)S(1)}, bf16[768,128]{1,0:T(8,128)(2,1)S(1)}, u32[]{:S(2)}, u32[]{:S(2)}) %collective-permute-start.25) | collective-permute-done | bytes 196640 | tf_op jit(solution)/shard_map/ppermute | solution.py:27
  90.2 0.5 collective-permute-start.27
  90.7 0.5 collective-permute-start.29
  91.2 0.4 collective-permute-done.26.refs_12_
  91.6 1.4 %collective-permute-start.31 = (bf16[2,128,384]{2,1,0:T(8,128)(2,1)S(1)}, bf16[2,128,384]{2,1,0:T(8,128)(2,1)S(1)}, u32[]{:S(2)}, u32[]{:S(2)}) collective-permute-start(bf16[2,128,384]{2,1,0:T(8,128)(2,1)S(1)} %get-tuple-element.73), channel_id=1, source_target_pairs={{0,8},{4,12},{8,0},{12,4},{1,9},{5,13},{9,1},{13,5},{2,10},{6,14},... | collective-permute-start | bytes 589832 | tf_op jit(solution)/shard_map/ppermute | solution.py:27
  93.0 0.1 collective-permute-start.32
  93.2 4.7 %step3ab.1.refs_1_ = bf16[4,128,384]{2,1,0:T(8,128)(2,1)S(1)} custom-call(f32[1,16]{1,0:T(1,128)S(1)} %copy-done.8, s32[1,4]{1,0:T(1,128)S(1)} %bitcast.11, f32[1,1536]{1,0:T(1,128)S(1)} %copy-done.1, f32[1,1536]{1,0:T(1,128)S(1)} %copy-done.2, f32[1,1536]{1,0:T(1,128)S(1)} %copy-done.4, s32[4,1,512]{2,1,0:T(1,128)S(1)} %copy-done.3, ...), custom_call_target="tpu_custom_call" | custom-call | flops 1610612736 | bytes 3145728 | tf_op jit(solution)/shard_map/step3ab/pallas_call | solution.py:497
  97.8 1.5 %collective-permute-done.31.refs_7_ = bf16[2,128,384]{2,1,0:T(8,128)(2,1)S(1)} collective-permute-done((bf16[2,128,384]{2,1,0:T(8,128)(2,1)S(1)}, bf16[2,128,384]{2,1,0:T(8,128)(2,1)S(1)}, u32[]{:S(2)}, u32[]{:S(2)}) %collective-permute-start.31) | collective-permute-done | bytes 196640 | tf_op jit(solution)/shard_map/ppermute | solution.py:27
  99.3 1.2 %settle.1 = (bf16[128,384]{1,0:T(8,128)(2,1)S(1)}, bf16[128,384]{1,0:T(8,128)(2,1)S(1)}, bf16[128,384]{1,0:T(8,128)(2,1)S(1)}, bf16[128,384]{1,0:T(8,128)(2,1)S(...) custom-call(bf16[4,128,384]{2,1,0:T(8,128)(2,1)S(1)} %step2ab.1.refs, ...), custom_call_target="tpu_custom_call" | custom-call | tf_op jit(solution)/shard_map/settle/pallas_call | solution.py:497
  100.6 0.6 collective-permute-start.36
  101.2 1.5 %collective-permute-start.34 = (bf16[128,384]{1,0:T(8,128)(2,1)S(1)}, bf16[128,384]{1,0:T(8,128)(2,1)S(1)}, u32[]{:S(2)}, u32[]{:S(2)}) collective-permute-start(bf16[128,384]{1,0:T(8,128)(2,1)S(1)} %get-tuple-element.78), channel_id=1, source_target_pairs={{0,8},{4,12},{8,0},{12,4},{1,9},{5,13},{9,1},{13,5},{2,10},{6,14},... | collective-permute-start | bytes 294920 | tf_op jit(solution)/shard_map/ppermute | solution.py:27
  102.7 0.3 collective-permute-start.35
  103.0 2.1 %collective-permute-start.37 = (bf16[96,256]{1,0:T(8,128)(2,1)S(1)}, bf16[96,256]{1,0:T(8,128)(2,1)S(1)}, u32[]{:S(2)}, u32[]{:S(2)}) collective-permute-start(bf16[96,256]{1,0:T(8,128)(2,1)S(1)} %get-tuple-element.82), channel_id=1, source_target_pairs={{0,2},{1,3},{2,0},{3,1},{4,6},{5,7},{6,4},{7,5},{8,10},{9,11},{10,... | collective-permute-start | bytes 147464 | tf_op jit(solution)/shard_map/ppermute | solution.py:27
  105.1 1.8 %collective-permute-start.38 = (bf16[96,256]{1,0:T(8,128)(2,1)S(1)}, bf16[96,256]{1,0:T(8,128)(2,1)S(1)}, u32[]{:S(2)}, u32[]{:S(2)}) collective-permute-start(bf16[96,256]{1,0:T(8,128)(2,1)S(1)} %get-tuple-element.83), channel_id=1, source_target_pairs={{0,3},{1,2},{2,1},{3,0},{4,7},{5,6},{6,5},{7,4},{8,11},{9,10},{10,... | collective-permute-start | bytes 147464 | tf_op jit(solution)/shard_map/ppermute | solution.py:27
  106.9 2.5 %collective-permute-done.37.refs_8_ = bf16[96,256]{1,0:T(8,128)(2,1)S(1)} collective-permute-done((bf16[96,256]{1,0:T(8,128)(2,1)S(1)}, bf16[96,256]{1,0:T(8,128)(2,1)S(1)}, u32[]{:S(2)}, u32[]{:S(2)}) %collective-permute-start.37) | collective-permute-done | bytes 49184 | tf_op jit(solution)/shard_map/ppermute | solution.py:27
  109.4 1.6 %collective-permute-done.38.refs_9_ = bf16[96,256]{1,0:T(8,128)(2,1)S(1)} collective-permute-done((bf16[96,256]{1,0:T(8,128)(2,1)S(1)}, bf16[96,256]{1,0:T(8,128)(2,1)S(1)}, u32[]{:S(2)}, u32[]{:S(2)}) %collective-permute-start.38) | collective-permute-done | bytes 49184 | tf_op jit(solution)/shard_map/ppermute | solution.py:27
  111.0 1.5 %finish.1 = (bf16[3,128,1536]{2,1,0:T(8,128)(2,1)}, f32[96,256]{1,0:T(8,128)}) custom-call(bf16[3,128,1536]{2,1,0:T(8,128)(2,1)} %get-tuple-element.74.refs_0_, bf16[2,128,384]{2,1,0:T(8,128)(2,1)S(1)} %collective-permute-done.32.refs_1_, bf16[128,384]{1,0:T(8,128)(2,1)S(1)} %get-tuple-element.76.refs_2_, ...), custom_call_target="tpu_custom_call", output_to_operand_aliasing={{0}: (0, {})} | custom-call | tf_op jit(solution)/shard_map/finish/pallas_call | solution.py:497
  (59 shorter events, 0.3 us)
Async XLA Ops:
  0.6 14.4 %copy-start = (bf16[1,3,1,128,1536]{4,3,2,1,0:T(8,128)(2,1)S(1)}, bf16[1,3,1,128,1536]{4,3,2,1,0:T(8,128)(2,1)}, u32[]{:S(2)}) copy-start(bf16[1,3,1,128,1536]{4,3,2,1,0:T(8,128)(2,1)} %incoming.3) | copy-start | bytes 3538948
  0.6 14.4 %copy-start.9 = (s32[4,1,128]{2,1,0:T(1,128)S(1)}, s32[4,1,128]{2,1,0:T(1,128)}, u32[]{:S(2)}) copy-start(s32[4,1,128]{2,1,0:T(1,128)} %contacts.1) | copy-start | bytes 6148
  2.1 1.5 %collective-permute-start = (bf16[2,96,384]{2,1,0:T(8,128)(2,1)S(1)}, bf16[2,96,384]{2,1,0:T(8,128)(2,1)S(1)}, u32[]{:S(2)}, u32[]{:S(2)}) collective-permute-start(bf16[2,96,384]{2,1,0:T(8,128)(2,1)S(1)} %get-tuple-element.45), channel_id=1, source_target_pairs={{0,4},{4,0},{8,12},{12,8},{1,5},{5,1},{9,13},{13,9},{2,6},{6,2},{1... | collective-permute-start | bytes 442376 | tf_op jit(solution)/shard_map/ppermute | solution.py:27
  3.7 11.3 %collective-permute-start.1 = (bf16[2,2,96,384]{3,2,1,0:T(8,128)(2,1)S(1)}, bf16[2,2,96,384]{3,2,1,0:T(8,128)(2,1)S(1)}, u32[]{:S(2)}, u32[]{:S(2)}) collective-permute-start(bf16[2,2,96,384]{3,2,1,0:T(8,128)(2,1)S(1)} %near.1), channel_id=1, source_target_pairs={{0,1},{1,3},{3,2},{2,0},{4,5},{5,7},{7,6},{6,4},{8,9},{9,11},{11,1... | collective-permute-start | bytes 884744 | tf_op jit(solution)/shard_map/ppermute | solution.py:41
  6.7 6.7 %collective-permute-start.2 = (bf16[2,96,384]{2,1,0:T(8,128)(2,1)S(1)}, bf16[2,96,384]{2,1,0:T(8,128)(2,1)S(1)}, u32[]{:S(2)}, u32[]{:S(2)}) collective-permute-start(bf16[2,96,384]{2,1,0:T(8,128)(2,1)S(1)} %get-tuple-element.46), channel_id=1, source_target_pairs={{0,8},{4,12},{8,0},{12,4},{1,9},{5,13},{9,1},{13,5},{2,10},{6,14},... | collective-permute-start | bytes 442376 | tf_op jit(solution)/shard_map/ppermute | solution.py:27
  8.2 6.3 %collective-permute-start.3 = (bf16[2,96,384]{2,1,0:T(8,128)(2,1)S(1)}, bf16[2,96,384]{2,1,0:T(8,128)(2,1)S(1)}, u32[]{:S(2)}, u32[]{:S(2)}) collective-permute-start(bf16[2,96,384]{2,1,0:T(8,128)(2,1)S(1)} %get-tuple-element.47), channel_id=1, source_target_pairs={{0,12},{4,8},{8,4},{12,0},{1,13},{5,9},{9,5},{13,1},{2,14},{6,10},... | collective-permute-start | bytes 442376 | tf_op jit(solution)/shard_map/ppermute | solution.py:27
  15.1 26.7 %collective-permute-start.4 = (bf16[272,1536]{1,0:T(8,128)(2,1)S(1)}, bf16[272,1536]{1,0:T(8,128)(2,1)S(1)}, u32[]{:S(2)}, u32[]{:S(2)}) collective-permute-start(bf16[272,1536]{1,0:T(8,128)(2,1)S(1)} %first.1.refs_0_), channel_id=1, source_target_pairs={{0,8},{4,12},{8,0},{12,4},{1,9},{5,13},{9,1},{13,5},{2,10},{6,14},... | collective-permute-start | bytes 2506760 | tf_op jit(solution)/shard_map/ppermute | solution.py:27
  16.7 9.8 %collective-permute-start.5 = (bf16[2,2,96,384]{3,2,1,0:T(8,128)(2,1)S(1)}, bf16[2,2,96,384]{3,2,1,0:T(8,128)(2,1)S(1)}, u32[]{:S(2)}, u32[]{:S(2)}) collective-permute-start(bf16[2,2,96,384]{3,2,1,0:T(8,128)(2,1)S(1)} %far.1), channel_id=1, source_target_pairs={{0,1},{1,3},{3,2},{2,0},{4,5},{5,7},{7,6},{6,4},{8,9},{9,11},{11,1... | collective-permute-start | bytes 884744 | tf_op jit(solution)/shard_map/ppermute | solution.py:41
  26.5 10.9 %collective-permute-start.6 = (bf16[4,96,384]{2,1,0:T(8,128)(2,1)S(1)}, bf16[4,96,384]{2,1,0:T(8,128)(2,1)S(1)}, u32[]{:S(2)}, u32[]{:S(2)}) collective-permute-start(bf16[4,96,384]{2,1,0:T(8,128)(2,1)S(1)} %part0.1.chunk), channel_id=1, source_target_pairs={{0,1},{1,3},{3,2},{2,0},{4,5},{5,7},{7,6},{6,4},{8,9},{9,11},{11,1... | collective-permute-start | bytes 884744 | tf_op jit(solution)/shard_map/ppermute | solution.py:41
  28.3 13.6 %copy-start.5 = (bf16[1,3,1,128,256]{4,3,2,1,0:T(8,128)(2,1)S(1)}, bf16[1,3,1,128,256]{4,3,2,1,0:T(8,128)(2,1)}, u32[]{:S(2)}) copy-start(bf16[1,3,1,128,256]{4,3,2,1,0:T(8,128)(2,1)} %cotangent.1) | copy-start | bytes 589828
  28.3 13.5 %collective-permute-start.7 = (bf16[4,96,384]{2,1,0:T(8,128)(2,1)S(1)}, bf16[4,96,384]{2,1,0:T(8,128)(2,1)S(1)}, u32[]{:S(2)}, u32[]{:S(2)}) collective-permute-start(bf16[4,96,384]{2,1,0:T(8,128)(2,1)S(1)} %part1.1.chunk), channel_id=1, source_target_pairs={{0,1},{1,3},{3,2},{2,0},{4,5},{5,7},{7,6},{6,4},{8,9},{9,11},{11,1... | collective-permute-start | bytes 884744 | tf_op jit(solution)/shard_map/ppermute | solution.py:41
  30.0 14.0 %collective-permute-start.9 = (bf16[272,1536]{1,0:T(8,128)(2,1)S(1)}, bf16[272,1536]{1,0:T(8,128)(2,1)S(1)}, u32[]{:S(2)}, u32[]{:S(2)}) collective-permute-start(bf16[272,1536]{1,0:T(8,128)(2,1)S(1)} %first.1.refs_0_), channel_id=1, source_target_pairs={{0,4},{4,0},{8,12},{12,8},{1,5},{5,1},{9,13},{13,9},{2,6},{6,2},{1... | collective-permute-start | bytes 2506760 | tf_op jit(solution)/shard_map/ppermute | solution.py:27
  41.8 2.5 %copy-start.1 = (f32[1,1536]{1,0:T(1,128)S(1)}, f32[1,1536]{1,0:T(1,128)}, u32[]{:S(2)}) copy-start(f32[1,1536]{1,0:T(1,128)} %refs_2_.11) | copy-start | bytes 18436
  41.8 2.5 %copy-start.2 = (f32[1,1536]{1,0:T(1,128)S(1)}, f32[1,1536]{1,0:T(1,128)}, u32[]{:S(2)}) copy-start(f32[1,1536]{1,0:T(1,128)} %refs_3_.11) | copy-start | bytes 18436
  41.8 2.5 %copy-start.6 = (bf16[1,16,1536]{2,1,0:T(8,128)(2,1)S(1)}, bf16[1,16,1536]{2,1,0:T(8,128)(2,1)}, u32[]{:S(2)}) copy-start(bf16[1,16,1536]{2,1,0:T(8,128)(2,1)} %table.1) | copy-start | bytes 147460
  41.8 2.4 %copy-start.7 = (s32[4,1]{0,1:T(1,128)S(1)}, s32[4,1]{0,1:T(1,128)}, u32[]{:S(2)}) copy-start(s32[4,1]{0,1:T(1,128)} %param.15) | copy-start | bytes 52
  41.8 2.4 %collective-permute-start.10 = (bf16[272,1536]{1,0:T(8,128)(2,1)S(1)}, bf16[272,1536]{1,0:T(8,128)(2,1)S(1)}, u32[]{:S(2)}, u32[]{:S(2)}) collective-permute-start(bf16[272,1536]{1,0:T(8,128)(2,1)S(1)} %tie.5.dep.refs_1_), channel_id=1, source_target_pairs={{0,4},{4,0},{8,12},{12,8},{1,5},{5,1},{9,13},{13,9},{2,6},{6,2},{1... | collective-permute-start | bytes 2506760 | tf_op jit(solution)/shard_map/ppermute | solution.py:27
  42.0 22.7 %collective-permute-start.8 = (bf16[256,1536]{1,0:T(8,128)(2,1)S(1)}, bf16[256,1536]{1,0:T(8,128)(2,1)S(1)}, u32[]{:S(2)}, u32[]{:S(2)}) collective-permute-start(bf16[256,1536]{1,0:T(8,128)(2,1)S(1)} %second.1.mine.refs_6_.refs_3_.refs_2_), channel_id=1, source_target_pairs={{0,8},{4,12},{8,0},{12,4},{1,9},{5,13},{9,1},{13,5},{2,10},{6,14},... | collective-permute-start | bytes 2359304 | tf_op jit(solution)/shard_map/ppermute | solution.py:27
  42.6 10.7 %collective-permute-start.12 = (bf16[4,96,384]{2,1,0:T(8,128)(2,1)S(1)}, bf16[4,96,384]{2,1,0:T(8,128)(2,1)S(1)}, u32[]{:S(2)}, u32[]{:S(2)}) collective-permute-start(bf16[4,96,384]{2,1,0:T(8,128)(2,1)S(1)} %collective-permute-done.6.refs_1_.next_chunk), channel_id=1, source_target_pairs={{0,1},{1,3},{3,2},{2,0},{4,5},{5,7},{7,6},{6,4},{8,9},{9,11},{11,1... | collective-permute-start | bytes 884744 | tf_op jit(solution)/shard_map/ppermute | solution.py:41
  47.6 5.7 %copy-start.3 = (s32[4,1,512]{2,1,0:T(1,128)S(1)}, s32[4,1,512]{2,1,0:T(1,128)}, u32[]{:S(2)}) copy-start(s32[4,1,512]{2,1,0:T(1,128)} %refs_5_.11) | copy-start | bytes 24580
  47.6 5.7 %copy-start.4 = (f32[1,1536]{1,0:T(1,128)S(1)}, f32[1,1536]{1,0:T(1,128)}, u32[]{:S(2)}) copy-start(f32[1,1536]{1,0:T(1,128)} %refs_4_.11) | copy-start | bytes 18436
  47.7 5.7 %copy-start.8 = (f32[1,16]{1,0:T(1,128)S(1)}, f32[1,16]{1,0:T(1,128)}, u32[]{:S(2)}) copy-start(f32[1,16]{1,0:T(1,128)} %refs_0_.11) | copy-start | bytes 196
  47.7 14.2 %collective-permute-start.11 = (bf16[4,96,384]{2,1,0:T(8,128)(2,1)S(1)}, bf16[4,96,384]{2,1,0:T(8,128)(2,1)S(1)}, u32[]{:S(2)}, u32[]{:S(2)}) collective-permute-start(bf16[4,96,384]{2,1,0:T(8,128)(2,1)S(1)} %tie.6.next_chunk), channel_id=1, source_target_pairs={{0,1},{1,3},{3,2},{2,0},{4,5},{5,7},{7,6},{6,4},{8,9},{9,11},{11,1... | collective-permute-start | bytes 884744 | tf_op jit(solution)/shard_map/ppermute | solution.py:41
  56.1 5.7 %collective-permute-start.13 = (bf16[768,128]{1,0:T(8,128)(2,1)S(1)}, bf16[768,128]{1,0:T(8,128)(2,1)S(1)}, u32[]{:S(2)}, u32[]{:S(2)}) collective-permute-start(bf16[768,128]{1,0:T(8,128)(2,1)S(1)} %get-tuple-element.51), channel_id=1, source_target_pairs={{0,16},{16,0},{1,17},{17,1},{2,18},{18,2},{3,19},{19,3},{4,20},{20... | collective-permute-start | bytes 589832 | tf_op jit(solution)/shard_map/ppermute | solution.py:31
  64.7 7.8 %collective-permute-start.14 = (bf16[2,256,1536]{2,1,0:T(8,128)(2,1)S(1)}, bf16[2,256,1536]{2,1,0:T(8,128)(2,1)S(1)}, u32[]{:S(2)}, u32[]{:S(2)}) collective-permute-start(bf16[2,256,1536]{2,1,0:T(8,128)(2,1)S(1)} %beside.1), channel_id=1, source_target_pairs={{0,4},{4,0},{8,12},{12,8},{1,5},{5,1},{9,13},{13,9},{2,6},{6,2},{1... | collective-permute-start | bytes 4718600 | tf_op jit(solution)/shard_map/ppermute | solution.py:27
  64.8 7.8 %collective-permute-start.18 = (bf16[768,128]{1,0:T(8,128)(2,1)S(1)}, bf16[768,128]{1,0:T(8,128)(2,1)S(1)}, u32[]{:S(2)}, u32[]{:S(2)}) collective-permute-start(bf16[768,128]{1,0:T(8,128)(2,1)S(1)} %get-tuple-element.60), channel_id=1, source_target_pairs={{0,16},{16,0},{1,17},{17,1},{2,18},{18,2},{3,19},{19,3},{4,20},{20... | collective-permute-start | bytes 589832 | tf_op jit(solution)/shard_map/ppermute | solution.py:31
  66.4 10.0 %collective-permute-start.22 = (bf16[768,128]{1,0:T(8,128)(2,1)S(1)}, bf16[768,128]{1,0:T(8,128)(2,1)S(1)}, u32[]{:S(2)}, u32[]{:S(2)}) collective-permute-start(bf16[768,128]{1,0:T(8,128)(2,1)S(1)} %get-tuple-element.64), channel_id=1, source_target_pairs={{0,16},{16,0},{1,17},{17,1},{2,18},{18,2},{3,19},{19,3},{4,20},{20... | collective-permute-start | bytes 589832 | tf_op jit(solution)/shard_map/ppermute | solution.py:31
  66.9 8.6 %collective-permute-start.15 = (bf16[768,128]{1,0:T(8,128)(2,1)S(1)}, bf16[768,128]{1,0:T(8,128)(2,1)S(1)}, u32[]{:S(2)}, u32[]{:S(2)}) collective-permute-start(bf16[768,128]{1,0:T(8,128)(2,1)S(1)} %collective-permute-done.13.refs_1_.refs_10_), channel_id=1, source_target_pairs={{0,8},{4,12},{8,0},{12,4},{1,9},{5,13},{9,1},{13,5},{2,10},{6,14},... | collective-permute-start | bytes 589832 | tf_op jit(solution)/shard_map/ppermute | solution.py:27
  72.6 6.0 %collective-permute-start.19 = (bf16[768,128]{1,0:T(8,128)(2,1)S(1)}, bf16[768,128]{1,0:T(8,128)(2,1)S(1)}, u32[]{:S(2)}, u32[]{:S(2)}) collective-permute-start(bf16[768,128]{1,0:T(8,128)(2,1)S(1)} %tie.8.refs_14_), channel_id=1, source_target_pairs={{0,8},{4,12},{8,0},{12,4},{1,9},{5,13},{9,1},{13,5},{2,10},{6,14},... | collective-permute-start | bytes 589832 | tf_op jit(solution)/shard_map/ppermute | solution.py:27
  74.0 4.6 %collective-permute-start.16 = (bf16[768,128]{1,0:T(8,128)(2,1)S(1)}, bf16[768,128]{1,0:T(8,128)(2,1)S(1)}, u32[]{:S(2)}, u32[]{:S(2)}) collective-permute-start(bf16[768,128]{1,0:T(8,128)(2,1)S(1)} %collective-permute-done.13.refs_1_.refs_10_), channel_id=1, source_target_pairs={{0,4},{4,0},{8,12},{12,8},{1,5},{5,1},{9,13},{13,9},{2,6},{6,2},{1... | collective-permute-start | bytes 589832 | tf_op jit(solution)/shard_map/ppermute | solution.py:27
  74.0 7.3 %collective-permute-start.24 = (bf16[768,128]{1,0:T(8,128)(2,1)S(1)}, bf16[768,128]{1,0:T(8,128)(2,1)S(1)}, u32[]{:S(2)}, u32[]{:S(2)}) collective-permute-start(bf16[768,128]{1,0:T(8,128)(2,1)S(1)} %get-tuple-element.65), channel_id=1, source_target_pairs={{0,16},{16,0},{1,17},{17,1},{2,18},{18,2},{3,19},{19,3},{4,20},{20... | collective-permute-start | bytes 589832 | tf_op jit(solution)/shard_map/ppermute | solution.py:31
  75.6 6.4 %collective-permute-start.17 = (bf16[768,128]{1,0:T(8,128)(2,1)S(1)}, bf16[768,128]{1,0:T(8,128)(2,1)S(1)}, u32[]{:S(2)}, u32[]{:S(2)}) collective-permute-start(bf16[768,128]{1,0:T(8,128)(2,1)S(1)} %collective-permute-done.15.refs_11_), channel_id=1, source_target_pairs={{0,4},{4,0},{8,12},{12,8},{1,5},{5,1},{9,13},{13,9},{2,6},{6,2},{1... | collective-permute-start | bytes 589832 | tf_op jit(solution)/shard_map/ppermute | solution.py:27
  76.4 5.7 %collective-permute-start.20 = (bf16[768,128]{1,0:T(8,128)(2,1)S(1)}, bf16[768,128]{1,0:T(8,128)(2,1)S(1)}, u32[]{:S(2)}, u32[]{:S(2)}) collective-permute-start(bf16[768,128]{1,0:T(8,128)(2,1)S(1)} %tie.8.refs_14_), channel_id=1, source_target_pairs={{0,4},{4,0},{8,12},{12,8},{1,5},{5,1},{9,13},{13,9},{2,6},{6,2},{1... | collective-permute-start | bytes 589832 | tf_op jit(solution)/shard_map/ppermute | solution.py:27
  78.6 3.4 %collective-permute-start.21 = (bf16[768,128]{1,0:T(8,128)(2,1)S(1)}, bf16[768,128]{1,0:T(8,128)(2,1)S(1)}, u32[]{:S(2)}, u32[]{:S(2)}) collective-permute-start(bf16[768,128]{1,0:T(8,128)(2,1)S(1)} %collective-permute-done.19.refs_15_), channel_id=1, source_target_pairs={{0,4},{4,0},{8,12},{12,8},{1,5},{5,1},{9,13},{13,9},{2,6},{6,2},{1... | collective-permute-start | bytes 589832 | tf_op jit(solution)/shard_map/ppermute | solution.py:27
  78.6 8.8 %collective-permute-start.23 = (bf16[768,128]{1,0:T(8,128)(2,1)S(1)}, bf16[768,128]{1,0:T(8,128)(2,1)S(1)}, u32[]{:S(2)}, u32[]{:S(2)}) collective-permute-start(bf16[768,128]{1,0:T(8,128)(2,1)S(1)} %collective-permute-done.22.refs_0_), channel_id=1, source_target_pairs={{0,8},{4,12},{8,0},{12,4},{1,9},{5,13},{9,1},{13,5},{2,10},{6,14},... | collective-permute-start | bytes 589832 | tf_op jit(solution)/shard_map/ppermute | solution.py:27
  81.4 8.8 %collective-permute-start.25 = (bf16[768,128]{1,0:T(8,128)(2,1)S(1)}, bf16[768,128]{1,0:T(8,128)(2,1)S(1)}, u32[]{:S(2)}, u32[]{:S(2)}) collective-permute-start(bf16[768,128]{1,0:T(8,128)(2,1)S(1)} %collective-permute-done.24.refs_2_), channel_id=1, source_target_pairs={{0,8},{4,12},{8,0},{12,4},{1,9},{5,13},{9,1},{13,5},{2,10},{6,14},... | collective-permute-start | bytes 589832 | tf_op jit(solution)/shard_map/ppermute | solution.py:27
  90.2 1.4 %collective-permute-start.26 = (bf16[768,128]{1,0:T(8,128)(2,1)S(1)}, bf16[768,128]{1,0:T(8,128)(2,1)S(1)}, u32[]{:S(2)}, u32[]{:S(2)}) collective-permute-start(bf16[768,128]{1,0:T(8,128)(2,1)S(1)} %get-tuple-element.67.refs_10_), channel_id=1, source_target_pairs={{0,4},{4,0},{8,12},{12,8},{1,5},{5,1},{9,13},{13,9},{2,6},{6,2},{1... | collective-permute-start | bytes 589832 | tf_op jit(solution)/shard_map/ppermute | solution.py:27
  90.2 2.9 %collective-permute-start.27 = (bf16[768,128]{1,0:T(8,128)(2,1)S(1)}, bf16[768,128]{1,0:T(8,128)(2,1)S(1)}, u32[]{:S(2)}, u32[]{:S(2)}) collective-permute-start(bf16[768,128]{1,0:T(8,128)(2,1)S(1)} %get-tuple-element.68.refs_11_), channel_id=1, source_target_pairs={{0,4},{4,0},{8,12},{12,8},{1,5},{5,1},{9,13},{13,9},{2,6},{6,2},{1... | collective-permute-start | bytes 589832 | tf_op jit(solution)/shard_map/ppermute | solution.py:27
  90.7 2.5 %collective-permute-start.28 = (bf16[768,128]{1,0:T(8,128)(2,1)S(1)}, bf16[768,128]{1,0:T(8,128)(2,1)S(1)}, u32[]{:S(2)}, u32[]{:S(2)}) collective-permute-start(bf16[768,128]{1,0:T(8,128)(2,1)S(1)} %get-tuple-element.69.refs_14_), channel_id=1, source_target_pairs={{0,4},{4,0},{8,12},{12,8},{1,5},{5,1},{9,13},{13,9},{2,6},{6,2},{1... | collective-permute-start | bytes 589832 | tf_op jit(solution)/shard_map/ppermute | solution.py:27
  90.7 2.5 %collective-permute-start.29 = (bf16[768,128]{1,0:T(8,128)(2,1)S(1)}, bf16[768,128]{1,0:T(8,128)(2,1)S(1)}, u32[]{:S(2)}, u32[]{:S(2)}) collective-permute-start(bf16[768,128]{1,0:T(8,128)(2,1)S(1)} %get-tuple-element.70.refs_15_), channel_id=1, source_target_pairs={{0,4},{4,0},{8,12},{12,8},{1,5},{5,1},{9,13},{13,9},{2,6},{6,2},{1... | collective-permute-start | bytes 589832 | tf_op jit(solution)/shard_map/ppermute | solution.py:27
  91.2 6.7 %collective-permute-start.30 = (bf16[2,128,384]{2,1,0:T(8,128)(2,1)S(1)}, bf16[2,128,384]{2,1,0:T(8,128)(2,1)S(1)}, u32[]{:S(2)}, u32[]{:S(2)}) collective-permute-start(bf16[2,128,384]{2,1,0:T(8,128)(2,1)S(1)} %get-tuple-element.72), channel_id=1, source_target_pairs={{0,4},{4,0},{8,12},{12,8},{1,5},{5,1},{9,13},{13,9},{2,6},{6,2},{1... | collective-permute-start | bytes 589832 | tf_op jit(solution)/shard_map/ppermute | solution.py:27
  91.6 7.7 %collective-permute-start.31 = (bf16[2,128,384]{2,1,0:T(8,128)(2,1)S(1)}, bf16[2,128,384]{2,1,0:T(8,128)(2,1)S(1)}, u32[]{:S(2)}, u32[]{:S(2)}) collective-permute-start(bf16[2,128,384]{2,1,0:T(8,128)(2,1)S(1)} %get-tuple-element.73), channel_id=1, source_target_pairs={{0,8},{4,12},{8,0},{12,4},{1,9},{5,13},{9,1},{13,5},{2,10},{6,14},... | collective-permute-start | bytes 589832 | tf_op jit(solution)/shard_map/ppermute | solution.py:27
  93.0 10.0 %collective-permute-start.32 = (bf16[2,128,384]{2,1,0:T(8,128)(2,1)S(1)}, bf16[2,128,384]{2,1,0:T(8,128)(2,1)S(1)}, u32[]{:S(2)}, u32[]{:S(2)}) collective-permute-start(bf16[2,128,384]{2,1,0:T(8,128)(2,1)S(1)} %get-tuple-element.75), channel_id=1, source_target_pairs={{0,12},{4,8},{8,4},{12,0},{1,13},{5,9},{9,5},{13,1},{2,14},{6,10},... | collective-permute-start | bytes 589832 | tf_op jit(solution)/shard_map/ppermute | solution.py:27
  100.6 4.5 %collective-permute-start.36 = (bf16[96,256]{1,0:T(8,128)(2,1)S(1)}, bf16[96,256]{1,0:T(8,128)(2,1)S(1)}, u32[]{:S(2)}, u32[]{:S(2)}) collective-permute-start(bf16[96,256]{1,0:T(8,128)(2,1)S(1)} %get-tuple-element.81), channel_id=1, source_target_pairs={{0,1},{1,0},{2,3},{3,2},{4,5},{5,4},{6,7},{7,6},{8,9},{9,8},{10,11... | collective-permute-start | bytes 147464 | tf_op jit(solution)/shard_map/ppermute | solution.py:27
  101.1 9.9 %collective-permute-start.33 = (bf16[128,384]{1,0:T(8,128)(2,1)S(1)}, bf16[128,384]{1,0:T(8,128)(2,1)S(1)}, u32[]{:S(2)}, u32[]{:S(2)}) collective-permute-start(bf16[128,384]{1,0:T(8,128)(2,1)S(1)} %get-tuple-element.77), channel_id=1, source_target_pairs={{0,4},{4,0},{8,12},{12,8},{1,5},{5,1},{9,13},{13,9},{2,6},{6,2},{1... | collective-permute-start | bytes 294920 | tf_op jit(solution)/shard_map/ppermute | solution.py:27
  101.2 9.9 %collective-permute-start.34 = (bf16[128,384]{1,0:T(8,128)(2,1)S(1)}, bf16[128,384]{1,0:T(8,128)(2,1)S(1)}, u32[]{:S(2)}, u32[]{:S(2)}) collective-permute-start(bf16[128,384]{1,0:T(8,128)(2,1)S(1)} %get-tuple-element.78), channel_id=1, source_target_pairs={{0,8},{4,12},{8,0},{12,4},{1,9},{5,13},{9,1},{13,5},{2,10},{6,14},... | collective-permute-start | bytes 294920 | tf_op jit(solution)/shard_map/ppermute | solution.py:27
  102.7 8.3 %collective-permute-start.35 = (bf16[128,384]{1,0:T(8,128)(2,1)S(1)}, bf16[128,384]{1,0:T(8,128)(2,1)S(1)}, u32[]{:S(2)}, u32[]{:S(2)}) collective-permute-start(bf16[128,384]{1,0:T(8,128)(2,1)S(1)} %get-tuple-element.79), channel_id=1, source_target_pairs={{0,12},{4,8},{8,4},{12,0},{1,13},{5,9},{9,5},{13,1},{2,14},{6,10},... | collective-permute-start | bytes 294920 | tf_op jit(solution)/shard_map/ppermute | solution.py:27
  103.0 6.4 %collective-permute-start.37 = (bf16[96,256]{1,0:T(8,128)(2,1)S(1)}, bf16[96,256]{1,0:T(8,128)(2,1)S(1)}, u32[]{:S(2)}, u32[]{:S(2)}) collective-permute-start(bf16[96,256]{1,0:T(8,128)(2,1)S(1)} %get-tuple-element.82), channel_id=1, source_target_pairs={{0,2},{1,3},{2,0},{3,1},{4,6},{5,7},{6,4},{7,5},{8,10},{9,11},{10,... | collective-permute-start | bytes 147464 | tf_op jit(solution)/shard_map/ppermute | solution.py:27
  105.1 5.9 %collective-permute-start.38 = (bf16[96,256]{1,0:T(8,128)(2,1)S(1)}, bf16[96,256]{1,0:T(8,128)(2,1)S(1)}, u32[]{:S(2)}, u32[]{:S(2)}) collective-permute-start(bf16[96,256]{1,0:T(8,128)(2,1)S(1)} %get-tuple-element.83), channel_id=1, source_target_pairs={{0,3},{1,2},{2,1},{3,0},{4,7},{5,6},{6,5},{7,4},{8,11},{9,10},{10,... | collective-permute-start | bytes 147464 | tf_op jit(solution)/shard_map/ppermute | solution.py:27

commit v18 on v16

--- a/solution.py
+++ b/solution.py
@@ -403,41 +403,35 @@
     grad[...] = total
 
 
-def settle_kernel(turns, pieces, halves, hops, feats, *refs):
-    refs = list(refs)
-
-    def take(count):
-        taken, refs[:count] = refs[:count], []
-        return taken
-
-    before, now, second, early = take(halves), take(halves), opened(take(3)), take(pieces - 1)
-    early_grad = take(1)[0]
-    late, own_grad, grads = take(pieces), take(1)[0], take(hops - 1)
-    section_out = take(1)[0]
-    rows_out, total, sem = take(3)
-    section, seq, rep = lax.axis_index("pipe"), lax.axis_index("seq"), lax.axis_index("dp")
+def share_kernel(turns, pieces, hops, feats, *refs):
+    before, now, second, early_grad = refs[0], refs[1], opened(refs[2:5]), refs[5]
+    own_grad, grads, total = refs[6], refs[7:-1], refs[-1]
+    section, rep = lax.axis_index("pipe"), lax.axis_index("dp")
+    rows, cols = before.shape[1:]
+    output = jnp.where(section == 0, before[...], now[...]).reshape(pieces * rows, cols)
+    share = grad_of(output, second, turns - 1, rows, feats)
+    total[...] = (share + early_grad[...]) * float(turns * hops * rows * pieces) ** (-0.5)
+    g_rows = cols // hops
+    own_grad[...] = total[pl.ds(pl.multiple_of(rep * g_rows, 8), g_rows)]
+    for shift in range(1, hops):
+        at = pl.multiple_of(lax.rem(rep + shift, hops) * g_rows, 8)
+        grads[shift - 1][...] = total[pl.ds(at, g_rows)].astype(jnp.bfloat16)
+
+
+def settle_kernel(turns, pieces, *refs):
+    before, now, early = refs[0], refs[1], refs[2 : pieces + 1]
+    late, (section_out, rows_out, sem) = refs[pieces + 1 : -3], refs[-3:]
+    section, seq = lax.axis_index("pipe"), lax.axis_index("seq")
     offsets = offsets_of(pieces)
-    part = pieces // halves
     rows, cols = early[0].shape[1:]
+    for p in range(pieces):
+        late[offsets[p]][...] = jnp.where(section == 0, before[p], now[p])
     for m in range(pieces - 1):
         lanes = pl.ds(pl.multiple_of((seq ^ m) * cols, 128), cols)
         for turn in range(turns - 1):
             rows_out[turn, :, lanes] = early[m][turn]
     copy = pltpu.make_async_copy(rows_out, section_out.at[pl.ds(0, turns - 1)], sem)
     copy.start()
-    blocks = []
-    for p in range(pieces):
-        block = jnp.where(section == 0, before[p // part][p % part], now[p // part][p % part])
-        late[offsets[p]][...] = block
-        blocks.append(block)
-    share = grad_of(jnp.concatenate(blocks, axis=0), second, turns - 1, rows, feats)
-    factor = float(turns * hops * rows * pieces) ** (-0.5)
-    total[...] = (share + early_grad[...]) * factor
-    g_rows = cols // hops
-    own_grad[...] = total[pl.ds(pl.multiple_of(rep * g_rows, 8), g_rows)]
-    for shift in range(1, hops):
-        at = pl.multiple_of(lax.rem(rep + shift, hops) * g_rows, 8)
-        grads[shift - 1][...] = total[pl.ds(at, g_rows)].astype(jnp.bfloat16)
     copy.wait()
 
 
@@ -724,25 +718,29 @@
     outputs.append(output)
 
     g_shape = (cols // hops, feats)
-    operands = outputs[-2:] + second + early[:-1] + [early_grad]
-    settled = call(
-        functools.partial(settle_kernel, turns, seq_count, 1, hops, feats),
-        "settle",
-        [shape((rows, cols), kind)] * seq_count
-        + [shape(g_shape, jnp.float32)]
-        + [shape(g_shape, kind)] * (hops - 1)
-        + [shape((turns, rows, width), kind)],
+    operands = outputs[-2:] + second + [early_grad]
+    grads = call(
+        functools.partial(share_kernel, turns, seq_count, hops, feats),
+        "share",
+        [shape(g_shape, jnp.float32)] + [shape(g_shape, kind)] * (hops - 1),
         [vmem] * len(operands),
         operands,
-        [
-            pltpu.VMEM((turns - 1, rows, width), kind),
-            pltpu.VMEM((cols, feats), jnp.float32),
-            pltpu.SemaphoreType.DMA,
-        ],
+        [pltpu.VMEM((cols, feats), jnp.float32)],
         8,
-        out_specs=[vmem] * (seq_count + hops) + [anywhere],
-    )
-    late, grads, held = settled[:seq_count], settled[seq_count:-1], settled[-1]
+        out_specs=[vmem] * hops,
+    )
+    operands = outputs[-2:] + early[:-1]
+    settled = call(
+        functools.partial(settle_kernel, turns, seq_count),
+        "settle",
+        [shape((rows, cols), kind)] * seq_count + [shape((turns, rows, width), kind)],
+        [vmem] * len(operands),
+        operands,
+        [pltpu.VMEM((turns - 1, rows, width), kind), pltpu.SemaphoreType.DMA],
+        8,
+        out_specs=[vmem] * seq_count + [anywhere],
+    )
+    late, held = settled[:seq_count], settled[-1]
     late = [late[0]] + [swap(late[m], m) for m in range(1, seq_count)]
     grads = [grads[0]] + [shifted(grads[k], "dp", k) for k in range(1, hops)]
     section_out, grad_rows = call(

time: 112 us -> 111 us (level)
  waiting for transfers between devices: 49.2 us -> 46.9 us
    ppermute x3, waiting for transfers between devices: 5.28 us -> 4.02 us  [shifted(): lax.ppermute(value, axis, [(source, (source + shift) % count) for source...]
    pallas_call x24 -> x25, Pallas kernels: 28.9 us -> 29 us  [call(): pl.pallas_call(kernel, out_shape=out_shape, in_specs=in_specs, scratch_sh...]
where the time goes in v18:
time: 111 us; the launch traced here: 110 us
  waiting for transfers between devices  46.9 us (42%)
  starting transfers between devices  33.2 us (30%)
  Pallas kernels  29 us (26%)
  between operations  1.15 us (1%)
    pallas_call x25, Pallas kernels, call(): pl.pallas_call(kernel, out_shape=out_shape, in_specs=in_specs, scratch_sh...  29 us
    ppermute x6, waiting for transfers between devices, ring_step(): return lax.ppermute(value, 'dp', pairs)  24.8 us
    ppermute x26, starting transfers between devices, swap(): lax.ppermute(value, 'seq', [(source, source ^ bit) for source in range(co...  14.1 us
    ppermute x26, waiting for transfers between devices, swap(): lax.ppermute(value, 'seq', [(source, source ^ bit) for source in range(co...  13.3 us
    ppermute x6, starting transfers between devices, ring_step(): return lax.ppermute(value, 'dp', pairs)  10.9 us
    ppermute x4, starting transfers between devices, handed_over(): return lax.ppermute(value, 'pipe', [(0, 1), (1, 0)])  5.14 us
    ppermute x4, waiting for transfers between devices, handed_over(): return lax.ppermute(value, 'pipe', [(0, 1), (1, 0)])  4.82 us
    ppermute x3, waiting for transfers between devices, shifted(): lax.ppermute(value, axis, [(source, (source + shift) % count) for source...  4.02 us
  transfers between devices with their start and end apart: 39, of which 19 were waited for; matrix products, arithmetic and copies ran while one was open for 0% of the time, Pallas kernels for 23%

profile of v18, /device:TPU:0, one launch (start us, length us, event | category | flops | bytes accessed | tf_op | source)
XLA Modules:
  0.0 110.4 jit_solution(10021046455116920550)
XLA Ops:
  0.7 1.5 %pack.1 = (bf16[2,96,384]{2,1,0:T(8,128)(2,1)S(1)}, bf16[2,96,384]{2,1,0:T(8,128)(2,1)S(1)}, bf16[2,96,384]{2,1,0:T(8,128)(2,1)S(1)}, bf16[2,96,384]{2,1,0:T(8,128)(2,1)S(1)}) custom-call(bf16[1,96,1536]{2,1,0:T(8,128)(2,1)} %wq.1, bf16[1,96,1536]{2,1,0:T(8,128)(2,1)} %wkv.1), custom_call_target="tpu_custom_call" | custom-call | tf_op jit(solution)/shard_map/pack/pallas_call | solution.py:496
  2.1 0.5 collective-permute-start
  2.7 1.0 collective-permute-done.refs_1_
  3.7 3.0 %collective-permute-start.1 = (bf16[2,2,96,384]{3,2,1,0:T(8,128)(2,1)S(1)}, bf16[2,2,96,384]{3,2,1,0:T(8,128)(2,1)S(1)}, u32[]{:S(2)}, u32[]{:S(2)}) collective-permute-start(bf16[2,2,96,384]{3,2,1,0:T(8,128)(2,1)S(1)} %near.1), channel_id=1, source_target_pairs={{0,1},{1,3},{3,2},{2,0},{4,5},{5,7},{7,6},{6,4},{8,9},{9,11},{11,1... | collective-permute-start | bytes 884744 | tf_op jit(solution)/shard_map/ppermute | solution.py:46
  6.7 1.5 %collective-permute-start.2 = (bf16[2,96,384]{2,1,0:T(8,128)(2,1)S(1)}, bf16[2,96,384]{2,1,0:T(8,128)(2,1)S(1)}, u32[]{:S(2)}, u32[]{:S(2)}) collective-permute-start(bf16[2,96,384]{2,1,0:T(8,128)(2,1)S(1)} %get-tuple-element.46), channel_id=1, source_target_pairs={{0,8},{4,12},{8,0},{12,4},{1,9},{5,13},{9,1},{13,5},{2,10},{6,14},... | collective-permute-start | bytes 442376 | tf_op jit(solution)/shard_map/ppermute | solution.py:27
  8.2 5.2 %collective-permute-done.2.refs_1_ = bf16[2,96,384]{2,1,0:T(8,128)(2,1)S(1)} collective-permute-done((bf16[2,96,384]{2,1,0:T(8,128)(2,1)S(1)}, bf16[2,96,384]{2,1,0:T(8,128)(2,1)S(1)}, u32[]{:S(2)}, u32[]{:S(2)}) %collective-permute-start.2) | collective-permute-done | bytes 147488 | tf_op jit(solution)/shard_map/ppermute | solution.py:27
  13.4 1.1 collective-permute-done.3.refs_2_
  14.5 0.5 collective-permute-done.1.refs_0_.near
  15.1 1.6 %collective-permute-start.4 = (bf16[272,1536]{1,0:T(8,128)(2,1)S(1)}, bf16[272,1536]{1,0:T(8,128)(2,1)S(1)}, u32[]{:S(2)}, u32[]{:S(2)}) collective-permute-start(bf16[272,1536]{1,0:T(8,128)(2,1)S(1)} %first.1.refs_0_), channel_id=1, source_target_pairs={{0,8},{4,12},{8,0},{12,4},{1,9},{5,13},{9,1},{13,5},{2,10},{6,14},... | collective-permute-start | bytes 2506760 | tf_op jit(solution)/shard_map/ppermute | solution.py:27
  16.7 1.9 %collective-permute-start.5 = (bf16[2,2,96,384]{3,2,1,0:T(8,128)(2,1)S(1)}, bf16[2,2,96,384]{3,2,1,0:T(8,128)(2,1)S(1)}, u32[]{:S(2)}, u32[]{:S(2)}) collective-permute-start(bf16[2,2,96,384]{3,2,1,0:T(8,128)(2,1)S(1)} %far.1), channel_id=1, source_target_pairs={{0,1},{1,3},{3,2},{2,0},{4,5},{5,7},{7,6},{6,4},{8,9},{9,11},{11,1... | collective-permute-start | bytes 884744 | tf_op jit(solution)/shard_map/ppermute | solution.py:46
  18.6 7.9 %collective-permute-done.5.far = bf16[2,2,96,384]{3,2,1,0:T(8,128)(2,1)S(1)} collective-permute-done((bf16[2,2,96,384]{3,2,1,0:T(8,128)(2,1)S(1)}, bf16[2,2,96,384]{3,2,1,0:T(8,128)(2,1)S(1)}, u32[]{:S(2)}, u32[]{:S(2)}) %collective-permute-start.5) | collective-permute-done | bytes 294944 | tf_op jit(solution)/shard_map/ppermute | solution.py:46
  26.5 1.7 %collective-permute-start.6 = (bf16[4,96,384]{2,1,0:T(8,128)(2,1)S(1)}, bf16[4,96,384]{2,1,0:T(8,128)(2,1)S(1)}, u32[]{:S(2)}, u32[]{:S(2)}) collective-permute-start(bf16[4,96,384]{2,1,0:T(8,128)(2,1)S(1)} %part0.1.chunk), channel_id=1, source_target_pairs={{0,1},{1,3},{3,2},{2,0},{4,5},{5,7},{7,6},{6,4},{8,9},{9,11},{11,1... | collective-permute-start | bytes 884744 | tf_op jit(solution)/shard_map/ppermute | solution.py:46
  28.3 1.7 %collective-permute-start.7 = (bf16[4,96,384]{2,1,0:T(8,128)(2,1)S(1)}, bf16[4,96,384]{2,1,0:T(8,128)(2,1)S(1)}, u32[]{:S(2)}, u32[]{:S(2)}) collective-permute-start(bf16[4,96,384]{2,1,0:T(8,128)(2,1)S(1)} %part1.1.chunk), channel_id=1, source_target_pairs={{0,1},{1,3},{3,2},{2,0},{4,5},{5,7},{7,6},{6,4},{8,9},{9,11},{11,1... | collective-permute-start | bytes 884744 | tf_op jit(solution)/shard_map/ppermute | solution.py:46
  30.0 7.4 %collective-permute-done.6.refs_1_.refs_9_ = bf16[4,96,384]{2,1,0:T(8,128)(2,1)S(1)} collective-permute-done((bf16[4,96,384]{2,1,0:T(8,128)(2,1)S(1)}, bf16[4,96,384]{2,1,0:T(8,128)(2,1)S(1)}, u32[]{:S(2)}, u32[]{:S(2)}) %collective-permute-start.6) | collective-permute-done | bytes 294944 | tf_op jit(solution)/shard_map/ppermute | solution.py:46
  37.4 4.4 %collective-permute-done.7.refs_2_.refs_9_ = bf16[4,96,384]{2,1,0:T(8,128)(2,1)S(1)} collective-permute-done((bf16[4,96,384]{2,1,0:T(8,128)(2,1)S(1)}, bf16[4,96,384]{2,1,0:T(8,128)(2,1)S(1)}, u32[]{:S(2)}, u32[]{:S(2)}) %collective-permute-start.7) | collective-permute-done | bytes 294944 | tf_op jit(solution)/shard_map/ppermute | solution.py:46
  41.9 0.7 collective-permute-start.8
  42.6 1.4 %collective-permute-start.12 = (bf16[4,96,384]{2,1,0:T(8,128)(2,1)S(1)}, bf16[4,96,384]{2,1,0:T(8,128)(2,1)S(1)}, u32[]{:S(2)}, u32[]{:S(2)}) collective-permute-start(bf16[4,96,384]{2,1,0:T(8,128)(2,1)S(1)} %collective-permute-done.6.refs_1_.refs_9_), channel_id=1, source_target_pairs={{0,1},{1,3},{3,2},{2,0},{4,5},{5,7},{7,6},{6,4},{8,9},{9,11},{11,1... | collective-permute-start | bytes 884744 | tf_op jit(solution)/shard_map/ppermute | solution.py:46
  44.0 1.2 %collective-permute-start.11 = (bf16[4,96,384]{2,1,0:T(8,128)(2,1)S(1)}, bf16[4,96,384]{2,1,0:T(8,128)(2,1)S(1)}, u32[]{:S(2)}, u32[]{:S(2)}) collective-permute-start(bf16[4,96,384]{2,1,0:T(8,128)(2,1)S(1)} %collective-permute-done.7.refs_2_.refs_9_), channel_id=1, source_target_pairs={{0,1},{1,3},{3,2},{2,0},{4,5},{5,7},{7,6},{6,4},{8,9},{9,11},{11,1... | collective-permute-start | bytes 884744 | tf_op jit(solution)/shard_map/ppermute | solution.py:46
  45.2 0.1 place0.1.refs_11_
  45.3 3.3 %norm.1 = (bf16[512,1536]{1,0:T(8,128)(2,1)S(1)}, bf16[512,1536]{1,0:T(8,128)(2,1)S(1)}, f32[512,128]{1,0:T(8,128)S(1)}, f32[512,128]{1,0:T(8,128)S(1)}, f32[512...) custom-call(s32[1,4]{1,0:T(1,128)S(1)} %bitcast.5, ...), custom_call_target="tpu_custom_call" | custom-call | tf_op jit(solution)/shard_map/norm/pallas_call | solution.py:496
  48.7 4.6 %collective-permute-done.12.refs_10_ = bf16[4,96,384]{2,1,0:T(8,128)(2,1)S(1)} collective-permute-done((bf16[4,96,384]{2,1,0:T(8,128)(2,1)S(1)}, bf16[4,96,384]{2,1,0:T(8,128)(2,1)S(1)}, u32[]{:S(2)}, u32[]{:S(2)}) %collective-permute-start.12) | collective-permute-done | bytes 294944 | tf_op jit(solution)/shard_map/ppermute | solution.py:46
  53.3 2.7 %step0a.1 = (bf16[768,128]{1,0:T(8,128)(2,1)S(1)}, bf16[512,256]{1,0:T(8,128)(2,1)S(1)}, bf16[1536,384]{1,0:T(8,128)(2,1)S(1)}) custom-call(f32[1,16]{1,0:T(1,128)S(1)} %copy-done.8, s32[1,4]{1,0:T(1,128)S(1)} %bitcast.6, f32[1,1536]{1,0:T(1,128)S(1)} %copy-done.1, f32[1,1536]{1,0:T(1,128)S(1)} %copy-done.2, ...), custom_call_target="tpu_custom_call", output_to_operand_aliasing={{2}: (11, {})} | custom-call | flops 805306368 | bytes 1572864 | tf_op jit(solution)/shard_map/step0a/pallas_call | solution.py:496
  56.1 1.5 %collective-permute-start.13 = (bf16[768,128]{1,0:T(8,128)(2,1)S(1)}, bf16[768,128]{1,0:T(8,128)(2,1)S(1)}, u32[]{:S(2)}, u32[]{:S(2)}) collective-permute-start(bf16[768,128]{1,0:T(8,128)(2,1)S(1)} %get-tuple-element.51), channel_id=1, source_target_pairs={{0,16},{16,0},{1,17},{17,1},{2,18},{18,2},{3,19},{19,3},{4,20},{20... | collective-permute-start | bytes 589832 | tf_op jit(solution)/shard_map/ppermute | solution.py:31
  57.6 0.1 place1.1.refs_11_
  57.7 2.7 %step1a.1 = (bf16[768,128]{1,0:T(8,128)(2,1)S(1)}, bf16[512,256]{1,0:T(8,128)(2,1)S(1)}) custom-call(f32[1,16]{1,0:T(1,128)S(1)} %copy-done.8, s32[1,4]{1,0:T(1,128)S(1)} %bitcast.7, f32[1,1536]{1,0:T(1,128)S(1)} %copy-done.1, f32[1,1536]{1,0:T(1,128)S(1)} %copy-done.2, f32[1,1536]{1,0:T(1,128)S(1)} %copy-done.4, s32[4,1,512]{2,1,0:T(1,128)S(1)} %copy-done.3, ...), custom_call_target="tpu_custom_call" | custom-call | flops 805306368 | bytes 1572864 | tf_op jit(solution)/shard_map/step1a/pallas_call | solution.py:496
  60.4 1.4 %collective-permute-done.13.refs_1_.refs_10_ = bf16[768,128]{1,0:T(8,128)(2,1)S(1)} collective-permute-done((bf16[768,128]{1,0:T(8,128)(2,1)S(1)}, bf16[768,128]{1,0:T(8,128)(2,1)S(1)}, u32[]{:S(2)}, u32[]{:S(2)}) %collective-permute-start.13) | collective-permute-done | bytes 196640 | tf_op jit(solution)/shard_map/ppermute | solution.py:31
  61.8 2.8 %step0b.1 = (bf16[768,128]{1,0:T(8,128)(2,1)S(1)}, bf16[4,128,384]{2,1,0:T(8,128)(2,1)S(1)}, bf16[1536,384]{1,0:T(8,128)(2,1)S(1)}) custom-call(f32[1,16]{1,0:T(1,128)S(1)} %copy-done.8, s32[1,4]{1,0:T(1,128)S(1)} %bitcast.8, f32[1,1536]{1,0:T(1,128)S(1)} %copy-done.1, f32[1,1536]{1,0:T(1,128)S(1)} %copy-done.2, ...), custom_call_target="tpu_custom_call", output_to_operand_aliasing={{2}: (11, {})} | custom-call | flops 805306368 | bytes 1572864 | tf_op jit(solution)/shard_map/step0b/pallas_call | solution.py:496
  64.6 0.1 beside.1
  64.7 0.1 collective-permute-start.14
  64.8 1.5 %collective-permute-start.18 = (bf16[768,128]{1,0:T(8,128)(2,1)S(1)}, bf16[768,128]{1,0:T(8,128)(2,1)S(1)}, u32[]{:S(2)}, u32[]{:S(2)}) collective-permute-start(bf16[768,128]{1,0:T(8,128)(2,1)S(1)} %get-tuple-element.60), channel_id=1, source_target_pairs={{0,16},{16,0},{1,17},{17,1},{2,18},{18,2},{3,19},{19,3},{4,20},{20... | collective-permute-start | bytes 589832 | tf_op jit(solution)/shard_map/ppermute | solution.py:31
  66.3 0.6 collective-permute-start.22
  66.9 1.4 %collective-permute-start.15 = (bf16[768,128]{1,0:T(8,128)(2,1)S(1)}, bf16[768,128]{1,0:T(8,128)(2,1)S(1)}, u32[]{:S(2)}, u32[]{:S(2)}) collective-permute-start(bf16[768,128]{1,0:T(8,128)(2,1)S(1)} %collective-permute-done.13.refs_1_.refs_10_), channel_id=1, source_target_pairs={{0,8},{4,12},{8,0},{12,4},{1,9},{5,13},{9,1},{13,5},{2,10},{6,14},... | collective-permute-start | bytes 589832 | tf_op jit(solution)/shard_map/ppermute | solution.py:27
  68.3 2.7 %step1b.1 = (bf16[768,128]{1,0:T(8,128)(2,1)S(1)}, bf16[4,128,384]{2,1,0:T(8,128)(2,1)S(1)}) custom-call(f32[1,16]{1,0:T(1,128)S(1)} %copy-done.8, s32[1,4]{1,0:T(1,128)S(1)} %bitcast.9, f32[1,1536]{1,0:T(1,128)S(1)} %copy-done.1, f32[1,1536]{1,0:T(1,128)S(1)} %copy-done.2, f32[1,1536]{1,0:T(1,128)S(1)} %copy-done.4, s32[4,1,512]{2,1,0:T(1,128)S(1)} %copy-done.3, ...), custom_call_target="tpu_custom_call" | custom-call | flops 805306368 | bytes 1572864 | tf_op jit(solution)/shard_map/step1b/pallas_call | solution.py:496
  71.1 1.5 %collective-permute-done.18.refs_0_ = bf16[768,128]{1,0:T(8,128)(2,1)S(1)} collective-permute-done((bf16[768,128]{1,0:T(8,128)(2,1)S(1)}, bf16[768,128]{1,0:T(8,128)(2,1)S(1)}, u32[]{:S(2)}, u32[]{:S(2)}) %collective-permute-start.18) | collective-permute-done | bytes 196640 | tf_op jit(solution)/shard_map/ppermute | solution.py:31
  72.6 1.4 %collective-permute-start.19 = (bf16[768,128]{1,0:T(8,128)(2,1)S(1)}, bf16[768,128]{1,0:T(8,128)(2,1)S(1)}, u32[]{:S(2)}, u32[]{:S(2)}) collective-permute-start(bf16[768,128]{1,0:T(8,128)(2,1)S(1)} %tie.6.refs_14_), channel_id=1, source_target_pairs={{0,8},{4,12},{8,0},{12,4},{1,9},{5,13},{9,1},{13,5},{2,10},{6,14},... | collective-permute-start | bytes 589832 | tf_op jit(solution)/shard_map/ppermute | solution.py:27
  74.0 1.5 %collective-permute-start.24 = (bf16[768,128]{1,0:T(8,128)(2,1)S(1)}, bf16[768,128]{1,0:T(8,128)(2,1)S(1)}, u32[]{:S(2)}, u32[]{:S(2)}) collective-permute-start(bf16[768,128]{1,0:T(8,128)(2,1)S(1)} %get-tuple-element.65), channel_id=1, source_target_pairs={{0,16},{16,0},{1,17},{17,1},{2,18},{18,2},{3,19},{19,3},{4,20},{20... | collective-permute-start | bytes 589832 | tf_op jit(solution)/shard_map/ppermute | solution.py:31
  75.5 0.2 collective-permute-start.17
  75.8 0.6 collective-permute-done.22.refs_0_
  76.3 2.3 %collective-permute-done.19.refs_15_ = bf16[768,128]{1,0:T(8,128)(2,1)S(1)} collective-permute-done((bf16[768,128]{1,0:T(8,128)(2,1)S(1)}, bf16[768,128]{1,0:T(8,128)(2,1)S(1)}, u32[]{:S(2)}, u32[]{:S(2)}) %collective-permute-start.19) | collective-permute-done | bytes 196640 | tf_op jit(solution)/shard_map/ppermute | solution.py:27
  78.6 1.4 %collective-permute-start.23 = (bf16[768,128]{1,0:T(8,128)(2,1)S(1)}, bf16[768,128]{1,0:T(8,128)(2,1)S(1)}, u32[]{:S(2)}, u32[]{:S(2)}) collective-permute-start(bf16[768,128]{1,0:T(8,128)(2,1)S(1)} %collective-permute-done.22.refs_0_), channel_id=1, source_target_pairs={{0,8},{4,12},{8,0},{12,4},{1,9},{5,13},{9,1},{13,5},{2,10},{6,14},... | collective-permute-start | bytes 589832 | tf_op jit(solution)/shard_map/ppermute | solution.py:27
  80.0 1.3 %collective-permute-done.24.refs_2_ = bf16[768,128]{1,0:T(8,128)(2,1)S(1)} collective-permute-done((bf16[768,128]{1,0:T(8,128)(2,1)S(1)}, bf16[768,128]{1,0:T(8,128)(2,1)S(1)}, u32[]{:S(2)}, u32[]{:S(2)}) %collective-permute-start.24) | collective-permute-done | bytes 196640 | tf_op jit(solution)/shard_map/ppermute | solution.py:31
  81.3 0.7 collective-permute-start.25
  82.0 4.9 %step2ab.1.refs_2_.refs_0_ = bf16[4,128,384]{2,1,0:T(8,128)(2,1)S(1)} custom-call(f32[1,16]{1,0:T(1,128)S(1)} %copy-done.8, s32[1,4]{1,0:T(1,128)S(1)} %bitcast.10, f32[1,1536]{1,0:T(1,128)S(1)} %copy-done.1, f32[1,1536]{1,0:T(1,128)S(1)} %copy-done.2, f32[1,1536]{1,0:T(1,128)S(1)} %copy-done.4, s32[4,1,512]{2,1,0:T(1,128)S(1)} %copy-done.3, ...), custom_call_target="tpu_custom_call" | custom-call | flops 1610612736 | bytes 3145728 | tf_op jit(solution)/shard_map/step2ab/pallas_call | solution.py:496
  86.9 0.5 early.1
  87.4 2.8 %collective-permute-done.25.refs_3_ = bf16[768,128]{1,0:T(8,128)(2,1)S(1)} collective-permute-done((bf16[768,128]{1,0:T(8,128)(2,1)S(1)}, bf16[768,128]{1,0:T(8,128)(2,1)S(1)}, u32[]{:S(2)}, u32[]{:S(2)}) %collective-permute-start.25) | collective-permute-done | bytes 196640 | tf_op jit(solution)/shard_map/ppermute | solution.py:27
  90.1 0.5 collective-permute-start.27
  90.7 0.5 collective-permute-start.29
  91.2 0.4 collective-permute-done.26.refs_12_
  91.6 1.4 %collective-permute-start.31 = (bf16[2,128,384]{2,1,0:T(8,128)(2,1)S(1)}, bf16[2,128,384]{2,1,0:T(8,128)(2,1)S(1)}, u32[]{:S(2)}, u32[]{:S(2)}) collective-permute-start(bf16[2,128,384]{2,1,0:T(8,128)(2,1)S(1)} %get-tuple-element.73), channel_id=1, source_target_pairs={{0,8},{4,12},{8,0},{12,4},{1,9},{5,13},{9,1},{13,5},{2,10},{6,14},... | collective-permute-start | bytes 589832 | tf_op jit(solution)/shard_map/ppermute | solution.py:27
  93.0 0.1 collective-permute-start.32
  93.1 4.7 %step3ab.1.refs_1_ = bf16[4,128,384]{2,1,0:T(8,128)(2,1)S(1)} custom-call(f32[1,16]{1,0:T(1,128)S(1)} %copy-done.8, s32[1,4]{1,0:T(1,128)S(1)} %bitcast.11, f32[1,1536]{1,0:T(1,128)S(1)} %copy-done.1, f32[1,1536]{1,0:T(1,128)S(1)} %copy-done.2, f32[1,1536]{1,0:T(1,128)S(1)} %copy-done.4, s32[4,1,512]{2,1,0:T(1,128)S(1)} %copy-done.3, ...), custom_call_target="tpu_custom_call" | custom-call | flops 1610612736 | bytes 3145728 | tf_op jit(solution)/shard_map/step3ab/pallas_call | solution.py:496
  97.8 0.4 share.1
  98.2 0.7 collective-permute-start.36
  98.8 0.5 collective-permute-done.31.refs_4_
  99.3 1.0 settle.1
  100.3 0.1 collective-permute-start.33
  100.4 1.5 %collective-permute-start.34 = (bf16[128,384]{1,0:T(8,128)(2,1)S(1)}, bf16[128,384]{1,0:T(8,128)(2,1)S(1)}, u32[]{:S(2)}, u32[]{:S(2)}) collective-permute-start(bf16[128,384]{1,0:T(8,128)(2,1)S(1)} %get-tuple-element.78), channel_id=1, source_target_pairs={{0,8},{4,12},{8,0},{12,4},{1,9},{5,13},{9,1},{13,5},{2,10},{6,14},... | collective-permute-start | bytes 294920 | tf_op jit(solution)/shard_map/ppermute | solution.py:27
  101.9 0.4 collective-permute-start.35
  102.2 1.6 %collective-permute-start.37 = (bf16[96,256]{1,0:T(8,128)(2,1)S(1)}, bf16[96,256]{1,0:T(8,128)(2,1)S(1)}, u32[]{:S(2)}, u32[]{:S(2)}) collective-permute-start(bf16[96,256]{1,0:T(8,128)(2,1)S(1)} %get-tuple-element.82), channel_id=1, source_target_pairs={{0,2},{1,3},{2,0},{3,1},{4,6},{5,7},{6,4},{7,5},{8,10},{9,11},{10,... | collective-permute-start | bytes 147464 | tf_op jit(solution)/shard_map/ppermute | solution.py:36
  103.8 0.4 collective-permute-done.36.refs_7_
  104.3 0.8 collective-permute-start.38
  105.1 3.4 %collective-permute-done.37.refs_8_ = bf16[96,256]{1,0:T(8,128)(2,1)S(1)} collective-permute-done((bf16[96,256]{1,0:T(8,128)(2,1)S(1)}, bf16[96,256]{1,0:T(8,128)(2,1)S(1)}, u32[]{:S(2)}, u32[]{:S(2)}) %collective-permute-start.37) | collective-permute-done | bytes 49184 | tf_op jit(solution)/shard_map/ppermute | solution.py:36
  108.5 0.2 collective-permute-done.38.refs_9_
  108.7 1.5 %finish.1 = (bf16[3,128,1536]{2,1,0:T(8,128)(2,1)}, f32[96,256]{1,0:T(8,128)}) custom-call(bf16[3,128,1536]{2,1,0:T(8,128)(2,1)} %get-tuple-element.74.refs_0_, bf16[2,128,384]{2,1,0:T(8,128)(2,1)S(1)} %collective-permute-done.32.refs_1_, bf16[128,384]{1,0:T(8,128)(2,1)S(1)} %get-tuple-element.76.refs_2_, ...), custom_call_target="tpu_custom_call", output_to_operand_aliasing={{0}: (0, {})} | custom-call | tf_op jit(solution)/shard_map/finish/pallas_call | solution.py:496
  (59 shorter events, 0.3 us)
Async XLA Ops:
  0.6 14.4 %copy-start = (bf16[1,3,1,128,1536]{4,3,2,1,0:T(8,128)(2,1)S(1)}, bf16[1,3,1,128,1536]{4,3,2,1,0:T(8,128)(2,1)}, u32[]{:S(2)}) copy-start(bf16[1,3,1,128,1536]{4,3,2,1,0:T(8,128)(2,1)} %incoming.3) | copy-start | bytes 3538948
  0.6 14.4 %copy-start.9 = (s32[4,1,128]{2,1,0:T(1,128)S(1)}, s32[4,1,128]{2,1,0:T(1,128)}, u32[]{:S(2)}) copy-start(s32[4,1,128]{2,1,0:T(1,128)} %contacts.1) | copy-start | bytes 6148
  2.1 1.5 %collective-permute-start = (bf16[2,96,384]{2,1,0:T(8,128)(2,1)S(1)}, bf16[2,96,384]{2,1,0:T(8,128)(2,1)S(1)}, u32[]{:S(2)}, u32[]{:S(2)}) collective-permute-start(bf16[2,96,384]{2,1,0:T(8,128)(2,1)S(1)} %get-tuple-element.45), channel_id=1, source_target_pairs={{0,4},{4,0},{8,12},{12,8},{1,5},{5,1},{9,13},{13,9},{2,6},{6,2},{1... | collective-permute-start | bytes 442376 | tf_op jit(solution)/shard_map/ppermute | solution.py:27
  3.7 11.3 %collective-permute-start.1 = (bf16[2,2,96,384]{3,2,1,0:T(8,128)(2,1)S(1)}, bf16[2,2,96,384]{3,2,1,0:T(8,128)(2,1)S(1)}, u32[]{:S(2)}, u32[]{:S(2)}) collective-permute-start(bf16[2,2,96,384]{3,2,1,0:T(8,128)(2,1)S(1)} %near.1), channel_id=1, source_target_pairs={{0,1},{1,3},{3,2},{2,0},{4,5},{5,7},{7,6},{6,4},{8,9},{9,11},{11,1... | collective-permute-start | bytes 884744 | tf_op jit(solution)/shard_map/ppermute | solution.py:46
  6.7 6.7 %collective-permute-start.2 = (bf16[2,96,384]{2,1,0:T(8,128)(2,1)S(1)}, bf16[2,96,384]{2,1,0:T(8,128)(2,1)S(1)}, u32[]{:S(2)}, u32[]{:S(2)}) collective-permute-start(bf16[2,96,384]{2,1,0:T(8,128)(2,1)S(1)} %get-tuple-element.46), channel_id=1, source_target_pairs={{0,8},{4,12},{8,0},{12,4},{1,9},{5,13},{9,1},{13,5},{2,10},{6,14},... | collective-permute-start | bytes 442376 | tf_op jit(solution)/shard_map/ppermute | solution.py:27
  8.2 6.3 %collective-permute-start.3 = (bf16[2,96,384]{2,1,0:T(8,128)(2,1)S(1)}, bf16[2,96,384]{2,1,0:T(8,128)(2,1)S(1)}, u32[]{:S(2)}, u32[]{:S(2)}) collective-permute-start(bf16[2,96,384]{2,1,0:T(8,128)(2,1)S(1)} %get-tuple-element.47), channel_id=1, source_target_pairs={{0,12},{4,8},{8,4},{12,0},{1,13},{5,9},{9,5},{13,1},{2,14},{6,10},... | collective-permute-start | bytes 442376 | tf_op jit(solution)/shard_map/ppermute | solution.py:27
  15.1 26.7 %collective-permute-start.4 = (bf16[272,1536]{1,0:T(8,128)(2,1)S(1)}, bf16[272,1536]{1,0:T(8,128)(2,1)S(1)}, u32[]{:S(2)}, u32[]{:S(2)}) collective-permute-start(bf16[272,1536]{1,0:T(8,128)(2,1)S(1)} %first.1.refs_0_), channel_id=1, source_target_pairs={{0,8},{4,12},{8,0},{12,4},{1,9},{5,13},{9,1},{13,5},{2,10},{6,14},... | collective-permute-start | bytes 2506760 | tf_op jit(solution)/shard_map/ppermute | solution.py:27
  16.7 9.8 %collective-permute-start.5 = (bf16[2,2,96,384]{3,2,1,0:T(8,128)(2,1)S(1)}, bf16[2,2,96,384]{3,2,1,0:T(8,128)(2,1)S(1)}, u32[]{:S(2)}, u32[]{:S(2)}) collective-permute-start(bf16[2,2,96,384]{3,2,1,0:T(8,128)(2,1)S(1)} %far.1), channel_id=1, source_target_pairs={{0,1},{1,3},{3,2},{2,0},{4,5},{5,7},{7,6},{6,4},{8,9},{9,11},{11,1... | collective-permute-start | bytes 884744 | tf_op jit(solution)/shard_map/ppermute | solution.py:46
  26.5 10.9 %collective-permute-start.6 = (bf16[4,96,384]{2,1,0:T(8,128)(2,1)S(1)}, bf16[4,96,384]{2,1,0:T(8,128)(2,1)S(1)}, u32[]{:S(2)}, u32[]{:S(2)}) collective-permute-start(bf16[4,96,384]{2,1,0:T(8,128)(2,1)S(1)} %part0.1.chunk), channel_id=1, source_target_pairs={{0,1},{1,3},{3,2},{2,0},{4,5},{5,7},{7,6},{6,4},{8,9},{9,11},{11,1... | collective-permute-start | bytes 884744 | tf_op jit(solution)/shard_map/ppermute | solution.py:46
  28.3 13.5 %copy-start.5 = (bf16[1,3,1,128,256]{4,3,2,1,0:T(8,128)(2,1)S(1)}, bf16[1,3,1,128,256]{4,3,2,1,0:T(8,128)(2,1)}, u32[]{:S(2)}) copy-start(bf16[1,3,1,128,256]{4,3,2,1,0:T(8,128)(2,1)} %cotangent.1) | copy-start | bytes 589828
  28.3 13.5 %collective-permute-start.7 = (bf16[4,96,384]{2,1,0:T(8,128)(2,1)S(1)}, bf16[4,96,384]{2,1,0:T(8,128)(2,1)S(1)}, u32[]{:S(2)}, u32[]{:S(2)}) collective-permute-start(bf16[4,96,384]{2,1,0:T(8,128)(2,1)S(1)} %part1.1.chunk), channel_id=1, source_target_pairs={{0,1},{1,3},{3,2},{2,0},{4,5},{5,7},{7,6},{6,4},{8,9},{9,11},{11,1... | collective-permute-start | bytes 884744 | tf_op jit(solution)/shard_map/ppermute | solution.py:46
  30.0 15.2 %collective-permute-start.9 = (bf16[272,1536]{1,0:T(8,128)(2,1)S(1)}, bf16[272,1536]{1,0:T(8,128)(2,1)S(1)}, u32[]{:S(2)}, u32[]{:S(2)}) collective-permute-start(bf16[272,1536]{1,0:T(8,128)(2,1)S(1)} %first.1.refs_0_), channel_id=1, source_target_pairs={{0,4},{4,0},{8,12},{12,8},{1,5},{5,1},{9,13},{13,9},{2,6},{6,2},{1... | collective-permute-start | bytes 2506760 | tf_op jit(solution)/shard_map/ppermute | solution.py:27
  41.8 3.4 %collective-permute-start.10 = (bf16[272,1536]{1,0:T(8,128)(2,1)S(1)}, bf16[272,1536]{1,0:T(8,128)(2,1)S(1)}, u32[]{:S(2)}, u32[]{:S(2)}) collective-permute-start(bf16[272,1536]{1,0:T(8,128)(2,1)S(1)} %tie.4.dep.refs_1_), channel_id=1, source_target_pairs={{0,4},{4,0},{8,12},{12,8},{1,5},{5,1},{9,13},{13,9},{2,6},{6,2},{1... | collective-permute-start | bytes 2506760 | tf_op jit(solution)/shard_map/ppermute | solution.py:27
  41.9 3.4 %copy-start.1 = (f32[1,1536]{1,0:T(1,128)S(1)}, f32[1,1536]{1,0:T(1,128)}, u32[]{:S(2)}) copy-start(f32[1,1536]{1,0:T(1,128)} %refs_2_.11) | copy-start | bytes 18436
  41.9 3.4 %copy-start.2 = (f32[1,1536]{1,0:T(1,128)S(1)}, f32[1,1536]{1,0:T(1,128)}, u32[]{:S(2)}) copy-start(f32[1,1536]{1,0:T(1,128)} %refs_3_.11) | copy-start | bytes 18436
  41.9 3.4 %copy-start.6 = (bf16[1,16,1536]{2,1,0:T(8,128)(2,1)S(1)}, bf16[1,16,1536]{2,1,0:T(8,128)(2,1)}, u32[]{:S(2)}) copy-start(bf16[1,16,1536]{2,1,0:T(8,128)(2,1)} %table.1) | copy-start | bytes 147460
  41.9 3.4 %copy-start.7 = (s32[4,1]{0,1:T(1,128)S(1)}, s32[4,1]{0,1:T(1,128)}, u32[]{:S(2)}) copy-start(s32[4,1]{0,1:T(1,128)} %param.15) | copy-start | bytes 52
  41.9 22.7 %collective-permute-start.8 = (bf16[256,1536]{1,0:T(8,128)(2,1)S(1)}, bf16[256,1536]{1,0:T(8,128)(2,1)S(1)}, u32[]{:S(2)}, u32[]{:S(2)}) collective-permute-start(bf16[256,1536]{1,0:T(8,128)(2,1)S(1)} %second.1.mine.refs_6_.refs_3_.refs_2_), channel_id=1, source_target_pairs={{0,8},{4,12},{8,0},{12,4},{1,9},{5,13},{9,1},{13,5},{2,10},{6,14},... | collective-permute-start | bytes 2359304 | tf_op jit(solution)/shard_map/ppermute | solution.py:27
  42.6 10.7 %collective-permute-start.12 = (bf16[4,96,384]{2,1,0:T(8,128)(2,1)S(1)}, bf16[4,96,384]{2,1,0:T(8,128)(2,1)S(1)}, u32[]{:S(2)}, u32[]{:S(2)}) collective-permute-start(bf16[4,96,384]{2,1,0:T(8,128)(2,1)S(1)} %collective-permute-done.6.refs_1_.refs_9_), channel_id=1, source_target_pairs={{0,1},{1,3},{3,2},{2,0},{4,5},{5,7},{7,6},{6,4},{8,9},{9,11},{11,1... | collective-permute-start | bytes 884744 | tf_op jit(solution)/shard_map/ppermute | solution.py:46
  44.0 16.4 %collective-permute-start.11 = (bf16[4,96,384]{2,1,0:T(8,128)(2,1)S(1)}, bf16[4,96,384]{2,1,0:T(8,128)(2,1)S(1)}, u32[]{:S(2)}, u32[]{:S(2)}) collective-permute-start(bf16[4,96,384]{2,1,0:T(8,128)(2,1)S(1)} %collective-permute-done.7.refs_2_.refs_9_), channel_id=1, source_target_pairs={{0,1},{1,3},{3,2},{2,0},{4,5},{5,7},{7,6},{6,4},{8,9},{9,11},{11,1... | collective-permute-start | bytes 884744 | tf_op jit(solution)/shard_map/ppermute | solution.py:46
  45.3 8.0 %copy-start.3 = (s32[4,1,512]{2,1,0:T(1,128)S(1)}, s32[4,1,512]{2,1,0:T(1,128)}, u32[]{:S(2)}) copy-start(s32[4,1,512]{2,1,0:T(1,128)} %refs_5_.11) | copy-start | bytes 24580
  45.3 8.0 %copy-start.4 = (f32[1,1536]{1,0:T(1,128)S(1)}, f32[1,1536]{1,0:T(1,128)}, u32[]{:S(2)}) copy-start(f32[1,1536]{1,0:T(1,128)} %refs_4_.11) | copy-start | bytes 18436
  45.3 8.0 %copy-start.8 = (f32[1,16]{1,0:T(1,128)S(1)}, f32[1,16]{1,0:T(1,128)}, u32[]{:S(2)}) copy-start(f32[1,16]{1,0:T(1,128)} %refs_0_.11) | copy-start | bytes 196
  56.1 5.7 %collective-permute-start.13 = (bf16[768,128]{1,0:T(8,128)(2,1)S(1)}, bf16[768,128]{1,0:T(8,128)(2,1)S(1)}, u32[]{:S(2)}, u32[]{:S(2)}) collective-permute-start(bf16[768,128]{1,0:T(8,128)(2,1)S(1)} %get-tuple-element.51), channel_id=1, source_target_pairs={{0,16},{16,0},{1,17},{17,1},{2,18},{18,2},{3,19},{19,3},{4,20},{20... | collective-permute-start | bytes 589832 | tf_op jit(solution)/shard_map/ppermute | solution.py:31
  64.7 7.8 %collective-permute-start.14 = (bf16[2,256,1536]{2,1,0:T(8,128)(2,1)S(1)}, bf16[2,256,1536]{2,1,0:T(8,128)(2,1)S(1)}, u32[]{:S(2)}, u32[]{:S(2)}) collective-permute-start(bf16[2,256,1536]{2,1,0:T(8,128)(2,1)S(1)} %beside.1), channel_id=1, source_target_pairs={{0,4},{4,0},{8,12},{12,8},{1,5},{5,1},{9,13},{13,9},{2,6},{6,2},{1... | collective-permute-start | bytes 4718600 | tf_op jit(solution)/shard_map/ppermute | solution.py:27
  64.8 7.8 %collective-permute-start.18 = (bf16[768,128]{1,0:T(8,128)(2,1)S(1)}, bf16[768,128]{1,0:T(8,128)(2,1)S(1)}, u32[]{:S(2)}, u32[]{:S(2)}) collective-permute-start(bf16[768,128]{1,0:T(8,128)(2,1)S(1)} %get-tuple-element.60), channel_id=1, source_target_pairs={{0,16},{16,0},{1,17},{17,1},{2,18},{18,2},{3,19},{19,3},{4,20},{20... | collective-permute-start | bytes 589832 | tf_op jit(solution)/shard_map/ppermute | solution.py:31
  66.3 10.0 %collective-permute-start.22 = (bf16[768,128]{1,0:T(8,128)(2,1)S(1)}, bf16[768,128]{1,0:T(8,128)(2,1)S(1)}, u32[]{:S(2)}, u32[]{:S(2)}) collective-permute-start(bf16[768,128]{1,0:T(8,128)(2,1)S(1)} %get-tuple-element.64), channel_id=1, source_target_pairs={{0,16},{16,0},{1,17},{17,1},{2,18},{18,2},{3,19},{19,3},{4,20},{20... | collective-permute-start | bytes 589832 | tf_op jit(solution)/shard_map/ppermute | solution.py:31
  66.9 8.6 %collective-permute-start.15 = (bf16[768,128]{1,0:T(8,128)(2,1)S(1)}, bf16[768,128]{1,0:T(8,128)(2,1)S(1)}, u32[]{:S(2)}, u32[]{:S(2)}) collective-permute-start(bf16[768,128]{1,0:T(8,128)(2,1)S(1)} %collective-permute-done.13.refs_1_.refs_10_), channel_id=1, source_target_pairs={{0,8},{4,12},{8,0},{12,4},{1,9},{5,13},{9,1},{13,5},{2,10},{6,14},... | collective-permute-start | bytes 589832 | tf_op jit(solution)/shard_map/ppermute | solution.py:27
  72.6 6.0 %collective-permute-start.19 = (bf16[768,128]{1,0:T(8,128)(2,1)S(1)}, bf16[768,128]{1,0:T(8,128)(2,1)S(1)}, u32[]{:S(2)}, u32[]{:S(2)}) collective-permute-start(bf16[768,128]{1,0:T(8,128)(2,1)S(1)} %tie.6.refs_14_), channel_id=1, source_target_pairs={{0,8},{4,12},{8,0},{12,4},{1,9},{5,13},{9,1},{13,5},{2,10},{6,14},... | collective-permute-start | bytes 589832 | tf_op jit(solution)/shard_map/ppermute | solution.py:27
  74.0 4.6 %collective-permute-start.16 = (bf16[768,128]{1,0:T(8,128)(2,1)S(1)}, bf16[768,128]{1,0:T(8,128)(2,1)S(1)}, u32[]{:S(2)}, u32[]{:S(2)}) collective-permute-start(bf16[768,128]{1,0:T(8,128)(2,1)S(1)} %collective-permute-done.13.refs_1_.refs_10_), channel_id=1, source_target_pairs={{0,4},{4,0},{8,12},{12,8},{1,5},{5,1},{9,13},{13,9},{2,6},{6,2},{1... | collective-permute-start | bytes 589832 | tf_op jit(solution)/shard_map/ppermute | solution.py:27
  74.0 7.3 %collective-permute-start.24 = (bf16[768,128]{1,0:T(8,128)(2,1)S(1)}, bf16[768,128]{1,0:T(8,128)(2,1)S(1)}, u32[]{:S(2)}, u32[]{:S(2)}) collective-permute-start(bf16[768,128]{1,0:T(8,128)(2,1)S(1)} %get-tuple-element.65), channel_id=1, source_target_pairs={{0,16},{16,0},{1,17},{17,1},{2,18},{18,2},{3,19},{19,3},{4,20},{20... | collective-permute-start | bytes 589832 | tf_op jit(solution)/shard_map/ppermute | solution.py:31
  75.5 6.5 %collective-permute-start.17 = (bf16[768,128]{1,0:T(8,128)(2,1)S(1)}, bf16[768,128]{1,0:T(8,128)(2,1)S(1)}, u32[]{:S(2)}, u32[]{:S(2)}) collective-permute-start(bf16[768,128]{1,0:T(8,128)(2,1)S(1)} %collective-permute-done.15.refs_11_), channel_id=1, source_target_pairs={{0,4},{4,0},{8,12},{12,8},{1,5},{5,1},{9,13},{13,9},{2,6},{6,2},{1... | collective-permute-start | bytes 589832 | tf_op jit(solution)/shard_map/ppermute | solution.py:27
  76.3 5.7 %collective-permute-start.20 = (bf16[768,128]{1,0:T(8,128)(2,1)S(1)}, bf16[768,128]{1,0:T(8,128)(2,1)S(1)}, u32[]{:S(2)}, u32[]{:S(2)}) collective-permute-start(bf16[768,128]{1,0:T(8,128)(2,1)S(1)} %tie.6.refs_14_), channel_id=1, source_target_pairs={{0,4},{4,0},{8,12},{12,8},{1,5},{5,1},{9,13},{13,9},{2,6},{6,2},{1... | collective-permute-start | bytes 589832 | tf_op jit(solution)/shard_map/ppermute | solution.py:27
  78.6 3.4 %collective-permute-start.21 = (bf16[768,128]{1,0:T(8,128)(2,1)S(1)}, bf16[768,128]{1,0:T(8,128)(2,1)S(1)}, u32[]{:S(2)}, u32[]{:S(2)}) collective-permute-start(bf16[768,128]{1,0:T(8,128)(2,1)S(1)} %collective-permute-done.19.refs_15_), channel_id=1, source_target_pairs={{0,4},{4,0},{8,12},{12,8},{1,5},{5,1},{9,13},{13,9},{2,6},{6,2},{1... | collective-permute-start | bytes 589832 | tf_op jit(solution)/shard_map/ppermute | solution.py:27
  78.6 8.8 %collective-permute-start.23 = (bf16[768,128]{1,0:T(8,128)(2,1)S(1)}, bf16[768,128]{1,0:T(8,128)(2,1)S(1)}, u32[]{:S(2)}, u32[]{:S(2)}) collective-permute-start(bf16[768,128]{1,0:T(8,128)(2,1)S(1)} %collective-permute-done.22.refs_0_), channel_id=1, source_target_pairs={{0,8},{4,12},{8,0},{12,4},{1,9},{5,13},{9,1},{13,5},{2,10},{6,14},... | collective-permute-start | bytes 589832 | tf_op jit(solution)/shard_map/ppermute | solution.py:27
  81.3 8.8 %collective-permute-start.25 = (bf16[768,128]{1,0:T(8,128)(2,1)S(1)}, bf16[768,128]{1,0:T(8,128)(2,1)S(1)}, u32[]{:S(2)}, u32[]{:S(2)}) collective-permute-start(bf16[768,128]{1,0:T(8,128)(2,1)S(1)} %collective-permute-done.24.refs_2_), channel_id=1, source_target_pairs={{0,8},{4,12},{8,0},{12,4},{1,9},{5,13},{9,1},{13,5},{2,10},{6,14},... | collective-permute-start | bytes 589832 | tf_op jit(solution)/shard_map/ppermute | solution.py:27
  90.1 1.4 %collective-permute-start.26 = (bf16[768,128]{1,0:T(8,128)(2,1)S(1)}, bf16[768,128]{1,0:T(8,128)(2,1)S(1)}, u32[]{:S(2)}, u32[]{:S(2)}) collective-permute-start(bf16[768,128]{1,0:T(8,128)(2,1)S(1)} %get-tuple-element.67.refs_10_), channel_id=1, source_target_pairs={{0,4},{4,0},{8,12},{12,8},{1,5},{5,1},{9,13},{13,9},{2,6},{6,2},{1... | collective-permute-start | bytes 589832 | tf_op jit(solution)/shard_map/ppermute | solution.py:27
  90.1 2.9 %collective-permute-start.27 = (bf16[768,128]{1,0:T(8,128)(2,1)S(1)}, bf16[768,128]{1,0:T(8,128)(2,1)S(1)}, u32[]{:S(2)}, u32[]{:S(2)}) collective-permute-start(bf16[768,128]{1,0:T(8,128)(2,1)S(1)} %get-tuple-element.68.refs_11_), channel_id=1, source_target_pairs={{0,4},{4,0},{8,12},{12,8},{1,5},{5,1},{9,13},{13,9},{2,6},{6,2},{1... | collective-permute-start | bytes 589832 | tf_op jit(solution)/shard_map/ppermute | solution.py:27
  90.6 2.5 %collective-permute-start.28 = (bf16[768,128]{1,0:T(8,128)(2,1)S(1)}, bf16[768,128]{1,0:T(8,128)(2,1)S(1)}, u32[]{:S(2)}, u32[]{:S(2)}) collective-permute-start(bf16[768,128]{1,0:T(8,128)(2,1)S(1)} %get-tuple-element.69.refs_14_), channel_id=1, source_target_pairs={{0,4},{4,0},{8,12},{12,8},{1,5},{5,1},{9,13},{13,9},{2,6},{6,2},{1... | collective-permute-start | bytes 589832 | tf_op jit(solution)/shard_map/ppermute | solution.py:27
  90.7 2.5 %collective-permute-start.29 = (bf16[768,128]{1,0:T(8,128)(2,1)S(1)}, bf16[768,128]{1,0:T(8,128)(2,1)S(1)}, u32[]{:S(2)}, u32[]{:S(2)}) collective-permute-start(bf16[768,128]{1,0:T(8,128)(2,1)S(1)} %get-tuple-element.70.refs_15_), channel_id=1, source_target_pairs={{0,4},{4,0},{8,12},{12,8},{1,5},{5,1},{9,13},{13,9},{2,6},{6,2},{1... | collective-permute-start | bytes 589832 | tf_op jit(solution)/shard_map/ppermute | solution.py:27
  91.2 7.7 %collective-permute-start.30 = (bf16[2,128,384]{2,1,0:T(8,128)(2,1)S(1)}, bf16[2,128,384]{2,1,0:T(8,128)(2,1)S(1)}, u32[]{:S(2)}, u32[]{:S(2)}) collective-permute-start(bf16[2,128,384]{2,1,0:T(8,128)(2,1)S(1)} %get-tuple-element.72), channel_id=1, source_target_pairs={{0,4},{4,0},{8,12},{12,8},{1,5},{5,1},{9,13},{13,9},{2,6},{6,2},{1... | collective-permute-start | bytes 589832 | tf_op jit(solution)/shard_map/ppermute | solution.py:27
  91.6 7.7 %collective-permute-start.31 = (bf16[2,128,384]{2,1,0:T(8,128)(2,1)S(1)}, bf16[2,128,384]{2,1,0:T(8,128)(2,1)S(1)}, u32[]{:S(2)}, u32[]{:S(2)}) collective-permute-start(bf16[2,128,384]{2,1,0:T(8,128)(2,1)S(1)} %get-tuple-element.73), channel_id=1, source_target_pairs={{0,8},{4,12},{8,0},{12,4},{1,9},{5,13},{9,1},{13,5},{2,10},{6,14},... | collective-permute-start | bytes 589832 | tf_op jit(solution)/shard_map/ppermute | solution.py:27
  93.0 9.2 %collective-permute-start.32 = (bf16[2,128,384]{2,1,0:T(8,128)(2,1)S(1)}, bf16[2,128,384]{2,1,0:T(8,128)(2,1)S(1)}, u32[]{:S(2)}, u32[]{:S(2)}) collective-permute-start(bf16[2,128,384]{2,1,0:T(8,128)(2,1)S(1)} %get-tuple-element.75), channel_id=1, source_target_pairs={{0,12},{4,8},{8,4},{12,0},{1,13},{5,9},{9,5},{13,1},{2,14},{6,10},... | collective-permute-start | bytes 589832 | tf_op jit(solution)/shard_map/ppermute | solution.py:27
  98.2 6.1 %collective-permute-start.36 = (bf16[96,256]{1,0:T(8,128)(2,1)S(1)}, bf16[96,256]{1,0:T(8,128)(2,1)S(1)}, u32[]{:S(2)}, u32[]{:S(2)}) collective-permute-start(bf16[96,256]{1,0:T(8,128)(2,1)S(1)} %get-tuple-element.81), channel_id=1, source_target_pairs={{0,1},{1,2},{2,3},{3,0},{4,5},{5,6},{6,7},{7,4},{8,9},{9,10},{10,1... | collective-permute-start | bytes 147464 | tf_op jit(solution)/shard_map/ppermute | solution.py:36
  100.3 8.4 %collective-permute-start.33 = (bf16[128,384]{1,0:T(8,128)(2,1)S(1)}, bf16[128,384]{1,0:T(8,128)(2,1)S(1)}, u32[]{:S(2)}, u32[]{:S(2)}) collective-permute-start(bf16[128,384]{1,0:T(8,128)(2,1)S(1)} %get-tuple-element.77), channel_id=1, source_target_pairs={{0,4},{4,0},{8,12},{12,8},{1,5},{5,1},{9,13},{13,9},{2,6},{6,2},{1... | collective-permute-start | bytes 294920 | tf_op jit(solution)/shard_map/ppermute | solution.py:27
  100.4 8.3 %collective-permute-start.34 = (bf16[128,384]{1,0:T(8,128)(2,1)S(1)}, bf16[128,384]{1,0:T(8,128)(2,1)S(1)}, u32[]{:S(2)}, u32[]{:S(2)}) collective-permute-start(bf16[128,384]{1,0:T(8,128)(2,1)S(1)} %get-tuple-element.78), channel_id=1, source_target_pairs={{0,8},{4,12},{8,0},{12,4},{1,9},{5,13},{9,1},{13,5},{2,10},{6,14},... | collective-permute-start | bytes 294920 | tf_op jit(solution)/shard_map/ppermute | solution.py:27
  101.9 6.8 %collective-permute-start.35 = (bf16[128,384]{1,0:T(8,128)(2,1)S(1)}, bf16[128,384]{1,0:T(8,128)(2,1)S(1)}, u32[]{:S(2)}, u32[]{:S(2)}) collective-permute-start(bf16[128,384]{1,0:T(8,128)(2,1)S(1)} %get-tuple-element.79), channel_id=1, source_target_pairs={{0,12},{4,8},{8,4},{12,0},{1,13},{5,9},{9,5},{13,1},{2,14},{6,10},... | collective-permute-start | bytes 294920 | tf_op jit(solution)/shard_map/ppermute | solution.py:27
  102.2 6.2 %collective-permute-start.37 = (bf16[96,256]{1,0:T(8,128)(2,1)S(1)}, bf16[96,256]{1,0:T(8,128)(2,1)S(1)}, u32[]{:S(2)}, u32[]{:S(2)}) collective-permute-start(bf16[96,256]{1,0:T(8,128)(2,1)S(1)} %get-tuple-element.82), channel_id=1, source_target_pairs={{0,2},{1,3},{2,0},{3,1},{4,6},{5,7},{6,4},{7,5},{8,10},{9,11},{10,... | collective-permute-start | bytes 147464 | tf_op jit(solution)/shard_map/ppermute | solution.py:36
  104.3 4.4 %collective-permute-start.38 = (bf16[96,256]{1,0:T(8,128)(2,1)S(1)}, bf16[96,256]{1,0:T(8,128)(2,1)S(1)}, u32[]{:S(2)}, u32[]{:S(2)}) collective-permute-start(bf16[96,256]{1,0:T(8,128)(2,1)S(1)} %get-tuple-element.83), channel_id=1, source_target_pairs={{0,3},{1,0},{2,1},{3,2},{4,7},{5,4},{6,5},{7,6},{8,11},{9,8},{10,9... | collective-permute-start | bytes 147464 | tf_op jit(solution)/shard_map/ppermute | solution.py:36

commit v19 on v18

--- a/solution.py
+++ b/solution.py
@@ -91,10 +91,13 @@
         out[at] = ref[...]
 
 
-def part_kernel(part, near, far, out):
+def part_kernel(part, near, far, *outs):
     for at in range(2):
-        out[at] = near[at, part]
-        out[at + 2] = far[at, part]
+        outs[0][at] = near[at, part]
+        if len(outs) == 1:
+            outs[0][at + 2] = far[at, part]
+        else:
+            outs[1][at] = far[at, part]
 
 
 def place(hop, hops, blocks, weights):
@@ -105,9 +108,14 @@
         weights[pl.ds(pl.multiple_of(at * rows, 16), rows)] = block[...]
 
 
-def place_kernel(part, hops, near, far, chunk, weights):
+def blocks_in(chunk):
+    return [ref.at[m] for ref in chunk for m in range(ref.shape[0])]
+
+
+def place_kernel(part, hops, near, far, *refs):
+    chunk, weights = refs[:-1], refs[-1]
     place(0, hops, [near.at[0, part], near.at[1, part], far.at[0, part], far.at[1, part]], weights)
-    place(1, hops, [chunk.at[m] for m in range(4)], weights)
+    place(1, hops, blocks_in(chunk), weights)
 
 
 def first_kernel(turns, far, incoming, contacts, out, states):
@@ -235,7 +243,8 @@
         second, embed, relay = opened(take(3)), take(1)[0], take(2 * pieces)
     else:
         scaled, scales, own_hidden = take(3)
-    chunks = take(2) if step == 0 else None
+    streams = cfg["streams"]
+    chunks = [take(streams), take(streams)] if step == 0 else None
     weights = take(len(parts))
     left = take(1)[0] if parts == (1,) else None
     sends = take(1)[0] if len(parts) == 1 else None
@@ -255,7 +264,7 @@
 
     if step == 0:
         for hop, chunk in zip((2, 3), chunks):
-            place(hop, hops, [chunk.at[m] for m in range(pieces)], weights[0])
+            place(hop, hops, blocks_in(chunk), weights[0])
 
     def normalize(relayed):
         total = jnp.zeros((frames, 128), jnp.float32)
@@ -537,30 +546,32 @@
     near_next = ring_step(near)
     far = paired("far", [near_next], blocks[2:])
     far_next = ring_step(far)
+    streams = (2, 1)
     rings, partial = [], []
     for part in range(2):
+        count = streams[part]
         chunk = call(
             functools.partial(part_kernel, part),
             "part%d" % part,
-            pltpu.VMEM((seq_count, w_rows, cols), kind),
+            [pltpu.VMEM((seq_count // count, w_rows, cols), kind)] * count,
             [vmem, vmem],
             [near_next, far_next],
-            out_specs=vmem,
-        )
-        rings.append([chunk])
+            out_specs=[vmem] * count,
+        )
+        rings.append([list(chunk)])
         partial.append(
             call(
                 functools.partial(place_kernel, part, hops),
                 "place%d" % part,
                 pltpu.VMEM((width, cols), kind),
-                [vmem] * 3,
-                [pin(near), pin(far), pin(chunk)],
+                [vmem] * (2 + count),
+                [pin(near), pin(far)] + [pin(value) for value in chunk],
                 out_specs=vmem,
             )
         )
-    for hop in range(2):
-        for ring in rings:
-            ring.append(ring_step(ring[-1]))
+    for ring in rings:
+        ring.append([ring_step(value) for value in ring[-1]])
+    rings[0].append([ring_step(value) for value in rings[0][-1]])
 
     def tie(values, deps):
         return call(
@@ -584,7 +595,7 @@
     )
     across = swap(mine, 2)
     beside = swap(mine, 1)
-    (across,) = tie([across], [ring[1] for ring in rings])
+    (across,) = tie([across], rings[0][1] + rings[1][1])
     first = [mine, across, beside, swap(across, 1)]
     prepared = call(
         functools.partial(norm_kernel, turns, seq_count),
@@ -613,6 +624,9 @@
     )
     second = [mine, swap(mine, 2)]
 
+    rings[1][1] = list(tie(rings[1][1], [prepared[0]]))
+    rings[1].append([ring_step(value) for value in rings[1][1]])
+
     common = [key_bias, timesteps, norm_gain, time_freq, attn_gate, keyframes]
 
     def run_step(step, parts, large, out_shape, aliases):
@@ -626,6 +640,7 @@
             "heads": heads,
             "group": heads // kv_heads,
             "turns": turns,
+            "streams": streams[parts[0]],
         }
         scratch = [
             pltpu.VMEM((frames, len(parts) * (cols + 128)), kind),
@@ -660,10 +675,10 @@
         for step in range(2):
             large = [prepared[step], prepared[2 + step], prepared[4 + step]]
             if step == 0:
-                chunks = rings[part][1:]
+                chunks = rings[part][1] + rings[part][2]
                 if part:
-                    (last_chunk,) = tie(chunks[1:], [relays[0][0][0], lefts[1]])
-                    chunks = [chunks[0], last_chunk]
+                    last = tie(rings[part][2], [relays[0][0][0], lefts[1]])
+                    chunks = rings[part][1] + list(last)
                 large += chunks
             large += [weights[part]]
             aliases = {len(common) + len(large) - 1: 2} if step == 0 else {}

time: 111 us -> 110 us (level)
  waiting for transfers between devices: 46.9 us -> 45.6 us
  starting transfers between devices: 33.2 us -> 34.4 us
    ppermute x6 -> x8, waiting for transfers between devices: 24.8 us -> 23.9 us  [ring_step(): return lax.ppermute(value, 'dp', pairs)]
    ppermute x6 -> x8, starting transfers between devices: 10.9 us -> 11.7 us  [ring_step(): return lax.ppermute(value, 'dp', pairs)]
    pallas_call x25 -> x26, Pallas kernels: 29 us -> 29.1 us  [call(): pl.pallas_call(kernel, out_shape=out_shape, in_specs=in_specs, scratch_sh...]
  transfers between devices with their start and end apart: 39 -> 41, of which waited for: 19 -> 20; matrix products, arithmetic and copies ran while one was open for 0% -> 0% of each run, Pallas kernels for 23% -> 23%
where the time goes in v19:
time: 110 us
  waiting for transfers between devices  45.6 us (41%)
  starting transfers between devices  34.4 us (31%)
  Pallas kernels  29.1 us (26%)
  between operations  1.16 us (1%)
    pallas_call x26, Pallas kernels, call(): pl.pallas_call(kernel, out_shape=out_shape, in_specs=in_specs, scratch_sh...  29.1 us
    ppermute x8, waiting for transfers between devices, ring_step(): return lax.ppermute(value, 'dp', pairs)  23.9 us
    ppermute x26, starting transfers between devices, swap(): lax.ppermute(value, 'seq', [(source, source ^ bit) for source in range(co...  14 us
    ppermute x26, waiting for transfers between devices, swap(): lax.ppermute(value, 'seq', [(source, source ^ bit) for source in range(co...  13.1 us
    ppermute x8, starting transfers between devices, ring_step(): return lax.ppermute(value, 'dp', pairs)  11.7 us
    ppermute x4, starting transfers between devices, handed_over(): return lax.ppermute(value, 'pipe', [(0, 1), (1, 0)])  5.08 us
    ppermute x4, waiting for transfers between devices, handed_over(): return lax.ppermute(value, 'pipe', [(0, 1), (1, 0)])  4.99 us
    ppermute x3, waiting for transfers between devices, shifted(): lax.ppermute(value, axis, [(source, (source + shift) % count) for source...  3.68 us
  transfers between devices with their start and end apart: 41, of which 20 were waited for; matrix products, arithmetic and copies ran while one was open for 0% of the time, Pallas kernels for 23%

profile of v19, /device:TPU:0, one launch (start us, length us, event | category | flops | bytes accessed | tf_op | source)
XLA Modules:
  0.0 110.3 jit_solution(16179374935493752196)
XLA Ops:
  0.7 1.5 %pack.1 = (bf16[2,96,384]{2,1,0:T(8,128)(2,1)S(1)}, bf16[2,96,384]{2,1,0:T(8,128)(2,1)S(1)}, bf16[2,96,384]{2,1,0:T(8,128)(2,1)S(1)}, bf16[2,96,384]{2,1,0:T(8,128)(2,1)S(1)}) custom-call(bf16[1,96,1536]{2,1,0:T(8,128)(2,1)} %wq.1, bf16[1,96,1536]{2,1,0:T(8,128)(2,1)} %wkv.1), custom_call_target="tpu_custom_call" | custom-call | tf_op jit(solution)/shard_map/pack/pallas_call | solution.py:505
  2.1 0.5 collective-permute-start
  2.7 1.0 collective-permute-done.refs_1_
  3.7 3.0 %collective-permute-start.1 = (bf16[2,2,96,384]{3,2,1,0:T(8,128)(2,1)S(1)}, bf16[2,2,96,384]{3,2,1,0:T(8,128)(2,1)S(1)}, u32[]{:S(2)}, u32[]{:S(2)}) collective-permute-start(bf16[2,2,96,384]{3,2,1,0:T(8,128)(2,1)S(1)} %near.1), channel_id=1, source_target_pairs={{0,1},{1,3},{3,2},{2,0},{4,5},{5,7},{7,6},{6,4},{8,9},{9,11},{11,1... | collective-permute-start | bytes 884744 | tf_op jit(solution)/shard_map/ppermute | solution.py:46
  6.7 1.5 %collective-permute-start.2 = (bf16[2,96,384]{2,1,0:T(8,128)(2,1)S(1)}, bf16[2,96,384]{2,1,0:T(8,128)(2,1)S(1)}, u32[]{:S(2)}, u32[]{:S(2)}) collective-permute-start(bf16[2,96,384]{2,1,0:T(8,128)(2,1)S(1)} %get-tuple-element.48), channel_id=1, source_target_pairs={{0,8},{4,12},{8,0},{12,4},{1,9},{5,13},{9,1},{13,5},{2,10},{6,14},... | collective-permute-start | bytes 442376 | tf_op jit(solution)/shard_map/ppermute | solution.py:27
  8.2 5.2 %collective-permute-done.2.refs_1_ = bf16[2,96,384]{2,1,0:T(8,128)(2,1)S(1)} collective-permute-done((bf16[2,96,384]{2,1,0:T(8,128)(2,1)S(1)}, bf16[2,96,384]{2,1,0:T(8,128)(2,1)S(1)}, u32[]{:S(2)}, u32[]{:S(2)}) %collective-permute-start.2) | collective-permute-done | bytes 147488 | tf_op jit(solution)/shard_map/ppermute | solution.py:27
  13.4 1.1 collective-permute-done.3.refs_2_
  14.5 0.5 collective-permute-done.1.refs_0_.near
  15.1 1.6 %collective-permute-start.4 = (bf16[272,1536]{1,0:T(8,128)(2,1)S(1)}, bf16[272,1536]{1,0:T(8,128)(2,1)S(1)}, u32[]{:S(2)}, u32[]{:S(2)}) collective-permute-start(bf16[272,1536]{1,0:T(8,128)(2,1)S(1)} %first.1.refs_0_), channel_id=1, source_target_pairs={{0,8},{4,12},{8,0},{12,4},{1,9},{5,13},{9,1},{13,5},{2,10},{6,14},... | collective-permute-start | bytes 2506760 | tf_op jit(solution)/shard_map/ppermute | solution.py:27
  16.7 1.9 %collective-permute-start.5 = (bf16[2,2,96,384]{3,2,1,0:T(8,128)(2,1)S(1)}, bf16[2,2,96,384]{3,2,1,0:T(8,128)(2,1)S(1)}, u32[]{:S(2)}, u32[]{:S(2)}) collective-permute-start(bf16[2,2,96,384]{3,2,1,0:T(8,128)(2,1)S(1)} %far.1), channel_id=1, source_target_pairs={{0,1},{1,3},{3,2},{2,0},{4,5},{5,7},{7,6},{6,4},{8,9},{9,11},{11,1... | collective-permute-start | bytes 884744 | tf_op jit(solution)/shard_map/ppermute | solution.py:46
  18.6 7.9 %collective-permute-done.5.far = bf16[2,2,96,384]{3,2,1,0:T(8,128)(2,1)S(1)} collective-permute-done((bf16[2,2,96,384]{3,2,1,0:T(8,128)(2,1)S(1)}, bf16[2,2,96,384]{3,2,1,0:T(8,128)(2,1)S(1)}, u32[]{:S(2)}, u32[]{:S(2)}) %collective-permute-start.5) | collective-permute-done | bytes 294944 | tf_op jit(solution)/shard_map/ppermute | solution.py:46
  26.5 1.7 %collective-permute-start.8 = (bf16[4,96,384]{2,1,0:T(8,128)(2,1)S(1)}, bf16[4,96,384]{2,1,0:T(8,128)(2,1)S(1)}, u32[]{:S(2)}, u32[]{:S(2)}) collective-permute-start(bf16[4,96,384]{2,1,0:T(8,128)(2,1)S(1)} %part1.1.refs_0_), channel_id=1, source_target_pairs={{0,1},{1,3},{3,2},{2,0},{4,5},{5,7},{7,6},{6,4},{8,9},{9,11},{11,1... | collective-permute-start | bytes 884744 | tf_op jit(solution)/shard_map/ppermute | solution.py:46
  28.3 1.7 %collective-permute-start.6 = (bf16[2,96,384]{2,1,0:T(8,128)(2,1)S(1)}, bf16[2,96,384]{2,1,0:T(8,128)(2,1)S(1)}, u32[]{:S(2)}, u32[]{:S(2)}) collective-permute-start(bf16[2,96,384]{2,1,0:T(8,128)(2,1)S(1)} %get-tuple-element.50.refs_0_), channel_id=1, source_target_pairs={{0,1},{1,3},{3,2},{2,0},{4,5},{5,7},{7,6},{6,4},{8,9},{9,11},{11,1... | collective-permute-start | bytes 442376 | tf_op jit(solution)/shard_map/ppermute | solution.py:46
  30.1 10.1 %collective-permute-done.6.refs_1_.refs_9_ = bf16[2,96,384]{2,1,0:T(8,128)(2,1)S(1)} collective-permute-done((bf16[2,96,384]{2,1,0:T(8,128)(2,1)S(1)}, bf16[2,96,384]{2,1,0:T(8,128)(2,1)S(1)}, u32[]{:S(2)}, u32[]{:S(2)}) %collective-permute-start.6) | collective-permute-done | bytes 147488 | tf_op jit(solution)/shard_map/ppermute | solution.py:46
  40.2 1.6 %collective-permute-done.7.refs_2_.refs_10_ = bf16[2,96,384]{2,1,0:T(8,128)(2,1)S(1)} collective-permute-done((bf16[2,96,384]{2,1,0:T(8,128)(2,1)S(1)}, bf16[2,96,384]{2,1,0:T(8,128)(2,1)S(1)}, u32[]{:S(2)}, u32[]{:S(2)}) %collective-permute-start.7) | collective-permute-done | bytes 147488 | tf_op jit(solution)/shard_map/ppermute | solution.py:46
  41.9 0.1 collective-permute-start.11
  42.0 0.7 collective-permute-start.9
  42.6 1.4 %collective-permute-start.13 = (bf16[2,96,384]{2,1,0:T(8,128)(2,1)S(1)}, bf16[2,96,384]{2,1,0:T(8,128)(2,1)S(1)}, u32[]{:S(2)}, u32[]{:S(2)}) collective-permute-start(bf16[2,96,384]{2,1,0:T(8,128)(2,1)S(1)} %collective-permute-done.6.refs_1_.refs_9_), channel_id=1, source_target_pairs={{0,1},{1,3},{3,2},{2,0},{4,5},{5,7},{7,6},{6,4},{8,9},{9,11},{11,1... | collective-permute-start | bytes 442376 | tf_op jit(solution)/shard_map/ppermute | solution.py:46
  44.1 1.2 %collective-permute-start.14 = (bf16[2,96,384]{2,1,0:T(8,128)(2,1)S(1)}, bf16[2,96,384]{2,1,0:T(8,128)(2,1)S(1)}, u32[]{:S(2)}, u32[]{:S(2)}) collective-permute-start(bf16[2,96,384]{2,1,0:T(8,128)(2,1)S(1)} %collective-permute-done.7.refs_2_.refs_10_), channel_id=1, source_target_pairs={{0,1},{1,3},{3,2},{2,0},{4,5},{5,7},{7,6},{6,4},{8,9},{9,11},{11,1... | collective-permute-start | bytes 442376 | tf_op jit(solution)/shard_map/ppermute | solution.py:46
  45.3 3.3 %norm.1 = (bf16[512,1536]{1,0:T(8,128)(2,1)S(1)}, bf16[512,1536]{1,0:T(8,128)(2,1)S(1)}, f32[512,128]{1,0:T(8,128)S(1)}, f32[512,128]{1,0:T(8,128)S(1)}, f32[512...) custom-call(s32[1,4]{1,0:T(1,128)S(1)} %bitcast.5, ...), custom_call_target="tpu_custom_call" | custom-call | tf_op jit(solution)/shard_map/norm/pallas_call | solution.py:505
  48.7 0.8 collective-permute-start.12
  49.5 0.7 collective-permute-done.13.refs_11_
  50.2 3.0 %collective-permute-done.14.refs_12_ = bf16[2,96,384]{2,1,0:T(8,128)(2,1)S(1)} collective-permute-done((bf16[2,96,384]{2,1,0:T(8,128)(2,1)S(1)}, bf16[2,96,384]{2,1,0:T(8,128)(2,1)S(1)}, u32[]{:S(2)}, u32[]{:S(2)}) %collective-permute-start.14) | collective-permute-done | bytes 147488 | tf_op jit(solution)/shard_map/ppermute | solution.py:46
  53.2 2.8 %step0a.1 = (bf16[768,128]{1,0:T(8,128)(2,1)S(1)}, bf16[512,256]{1,0:T(8,128)(2,1)S(1)}, bf16[1536,384]{1,0:T(8,128)(2,1)S(1)}) custom-call(f32[1,16]{1,0:T(1,128)S(1)} %copy-done.8, s32[1,4]{1,0:T(1,128)S(1)} %bitcast.6, f32[1,1536]{1,0:T(1,128)S(1)} %copy-done.1, f32[1,1536]{1,0:T(1,128)S(1)} %copy-done.2, ...), custom_call_target="tpu_custom_call", output_to_operand_aliasing={{2}: (13, {})} | custom-call | flops 805306368 | bytes 1572864 | tf_op jit(solution)/shard_map/step0a/pallas_call | solution.py:505
  56.0 1.5 %collective-permute-start.15 = (bf16[768,128]{1,0:T(8,128)(2,1)S(1)}, bf16[768,128]{1,0:T(8,128)(2,1)S(1)}, u32[]{:S(2)}, u32[]{:S(2)}) collective-permute-start(bf16[768,128]{1,0:T(8,128)(2,1)S(1)} %get-tuple-element.55), channel_id=1, source_target_pairs={{0,16},{16,0},{1,17},{17,1},{2,18},{18,2},{3,19},{19,3},{4,20},{20... | collective-permute-start | bytes 589832 | tf_op jit(solution)/shard_map/ppermute | solution.py:31
  57.5 2.7 %step1a.1 = (bf16[768,128]{1,0:T(8,128)(2,1)S(1)}, bf16[512,256]{1,0:T(8,128)(2,1)S(1)}) custom-call(f32[1,16]{1,0:T(1,128)S(1)} %copy-done.8, s32[1,4]{1,0:T(1,128)S(1)} %bitcast.7, f32[1,1536]{1,0:T(1,128)S(1)} %copy-done.1, f32[1,1536]{1,0:T(1,128)S(1)} %copy-done.2, f32[1,1536]{1,0:T(1,128)S(1)} %copy-done.4, s32[4,1,512]{2,1,0:T(1,128)S(1)} %copy-done.3, ...), custom_call_target="tpu_custom_call" | custom-call | flops 805306368 | bytes 1572864 | tf_op jit(solution)/shard_map/step1a/pallas_call | solution.py:505
  60.2 1.5 %collective-permute-done.15.refs_1_.refs_10_ = bf16[768,128]{1,0:T(8,128)(2,1)S(1)} collective-permute-done((bf16[768,128]{1,0:T(8,128)(2,1)S(1)}, bf16[768,128]{1,0:T(8,128)(2,1)S(1)}, u32[]{:S(2)}, u32[]{:S(2)}) %collective-permute-start.15) | collective-permute-done | bytes 196640 | tf_op jit(solution)/shard_map/ppermute | solution.py:31
  61.7 2.8 %step0b.1 = (bf16[768,128]{1,0:T(8,128)(2,1)S(1)}, bf16[4,128,384]{2,1,0:T(8,128)(2,1)S(1)}, bf16[1536,384]{1,0:T(8,128)(2,1)S(1)}) custom-call(f32[1,16]{1,0:T(1,128)S(1)} %copy-done.8, s32[1,4]{1,0:T(1,128)S(1)} %bitcast.8, f32[1,1536]{1,0:T(1,128)S(1)} %copy-done.1, f32[1,1536]{1,0:T(1,128)S(1)} %copy-done.2, ...), custom_call_target="tpu_custom_call", output_to_operand_aliasing={{2}: (11, {})} | custom-call | flops 805306368 | bytes 1572864 | tf_op jit(solution)/shard_map/step0b/pallas_call | solution.py:505
  64.5 0.1 beside.1
  64.7 0.1 collective-permute-start.16
  64.7 1.5 %collective-permute-start.20 = (bf16[768,128]{1,0:T(8,128)(2,1)S(1)}, bf16[768,128]{1,0:T(8,128)(2,1)S(1)}, u32[]{:S(2)}, u32[]{:S(2)}) collective-permute-start(bf16[768,128]{1,0:T(8,128)(2,1)S(1)} %get-tuple-element.64), channel_id=1, source_target_pairs={{0,16},{16,0},{1,17},{17,1},{2,18},{18,2},{3,19},{19,3},{4,20},{20... | collective-permute-start | bytes 589832 | tf_op jit(solution)/shard_map/ppermute | solution.py:31
  66.2 0.6 collective-permute-start.24
  66.8 1.4 %collective-permute-start.17 = (bf16[768,128]{1,0:T(8,128)(2,1)S(1)}, bf16[768,128]{1,0:T(8,128)(2,1)S(1)}, u32[]{:S(2)}, u32[]{:S(2)}) collective-permute-start(bf16[768,128]{1,0:T(8,128)(2,1)S(1)} %collective-permute-done.15.refs_1_.refs_10_), channel_id=1, source_target_pairs={{0,8},{4,12},{8,0},{12,4},{1,9},{5,13},{9,1},{13,5},{2,10},{6,14},... | collective-permute-start | bytes 589832 | tf_op jit(solution)/shard_map/ppermute | solution.py:27
  68.2 2.7 %step1b.1 = (bf16[768,128]{1,0:T(8,128)(2,1)S(1)}, bf16[4,128,384]{2,1,0:T(8,128)(2,1)S(1)}) custom-call(f32[1,16]{1,0:T(1,128)S(1)} %copy-done.8, s32[1,4]{1,0:T(1,128)S(1)} %bitcast.9, f32[1,1536]{1,0:T(1,128)S(1)} %copy-done.1, f32[1,1536]{1,0:T(1,128)S(1)} %copy-done.2, f32[1,1536]{1,0:T(1,128)S(1)} %copy-done.4, s32[4,1,512]{2,1,0:T(1,128)S(1)} %copy-done.3, ...), custom_call_target="tpu_custom_call" | custom-call | flops 805306368 | bytes 1572864 | tf_op jit(solution)/shard_map/step1b/pallas_call | solution.py:505
  70.9 1.6 %collective-permute-done.20.refs_0_ = bf16[768,128]{1,0:T(8,128)(2,1)S(1)} collective-permute-done((bf16[768,128]{1,0:T(8,128)(2,1)S(1)}, bf16[768,128]{1,0:T(8,128)(2,1)S(1)}, u32[]{:S(2)}, u32[]{:S(2)}) %collective-permute-start.20) | collective-permute-done | bytes 196640 | tf_op jit(solution)/shard_map/ppermute | solution.py:31
  72.5 1.4 %collective-permute-start.21 = (bf16[768,128]{1,0:T(8,128)(2,1)S(1)}, bf16[768,128]{1,0:T(8,128)(2,1)S(1)}, u32[]{:S(2)}, u32[]{:S(2)}) collective-permute-start(bf16[768,128]{1,0:T(8,128)(2,1)S(1)} %tie.8.refs_14_), channel_id=1, source_target_pairs={{0,8},{4,12},{8,0},{12,4},{1,9},{5,13},{9,1},{13,5},{2,10},{6,14},... | collective-permute-start | bytes 589832 | tf_op jit(solution)/shard_map/ppermute | solution.py:27
  73.9 1.5 %collective-permute-start.26 = (bf16[768,128]{1,0:T(8,128)(2,1)S(1)}, bf16[768,128]{1,0:T(8,128)(2,1)S(1)}, u32[]{:S(2)}, u32[]{:S(2)}) collective-permute-start(bf16[768,128]{1,0:T(8,128)(2,1)S(1)} %get-tuple-element.69), channel_id=1, source_target_pairs={{0,16},{16,0},{1,17},{17,1},{2,18},{18,2},{3,19},{19,3},{4,20},{20... | collective-permute-start | bytes 589832 | tf_op jit(solution)/shard_map/ppermute | solution.py:31
  75.4 0.2 collective-permute-start.19
  75.7 0.6 collective-permute-done.24.refs_0_
  76.3 2.3 %collective-permute-done.21.refs_15_ = bf16[768,128]{1,0:T(8,128)(2,1)S(1)} collective-permute-done((bf16[768,128]{1,0:T(8,128)(2,1)S(1)}, bf16[768,128]{1,0:T(8,128)(2,1)S(1)}, u32[]{:S(2)}, u32[]{:S(2)}) %collective-permute-start.21) | collective-permute-done | bytes 196640 | tf_op jit(solution)/shard_map/ppermute | solution.py:27
  78.5 1.4 %collective-permute-start.25 = (bf16[768,128]{1,0:T(8,128)(2,1)S(1)}, bf16[768,128]{1,0:T(8,128)(2,1)S(1)}, u32[]{:S(2)}, u32[]{:S(2)}) collective-permute-start(bf16[768,128]{1,0:T(8,128)(2,1)S(1)} %collective-permute-done.24.refs_0_), channel_id=1, source_target_pairs={{0,8},{4,12},{8,0},{12,4},{1,9},{5,13},{9,1},{13,5},{2,10},{6,14},... | collective-permute-start | bytes 589832 | tf_op jit(solution)/shard_map/ppermute | solution.py:27
  79.9 1.3 %collective-permute-done.26.refs_2_ = bf16[768,128]{1,0:T(8,128)(2,1)S(1)} collective-permute-done((bf16[768,128]{1,0:T(8,128)(2,1)S(1)}, bf16[768,128]{1,0:T(8,128)(2,1)S(1)}, u32[]{:S(2)}, u32[]{:S(2)}) %collective-permute-start.26) | collective-permute-done | bytes 196640 | tf_op jit(solution)/shard_map/ppermute | solution.py:31
  81.2 0.7 collective-permute-start.27
  81.9 4.9 %step2ab.1.refs_2_.refs_0_ = bf16[4,128,384]{2,1,0:T(8,128)(2,1)S(1)} custom-call(f32[1,16]{1,0:T(1,128)S(1)} %copy-done.8, s32[1,4]{1,0:T(1,128)S(1)} %bitcast.10, f32[1,1536]{1,0:T(1,128)S(1)} %copy-done.1, f32[1,1536]{1,0:T(1,128)S(1)} %copy-done.2, f32[1,1536]{1,0:T(1,128)S(1)} %copy-done.4, s32[4,1,512]{2,1,0:T(1,128)S(1)} %copy-done.3, ...), custom_call_target="tpu_custom_call" | custom-call | flops 1610612736 | bytes 3145728 | tf_op jit(solution)/shard_map/step2ab/pallas_call | solution.py:505
  86.8 0.5 early.1
  87.3 2.8 %collective-permute-done.27.refs_3_ = bf16[768,128]{1,0:T(8,128)(2,1)S(1)} collective-permute-done((bf16[768,128]{1,0:T(8,128)(2,1)S(1)}, bf16[768,128]{1,0:T(8,128)(2,1)S(1)}, u32[]{:S(2)}, u32[]{:S(2)}) %collective-permute-start.27) | collective-permute-done | bytes 196640 | tf_op jit(solution)/shard_map/ppermute | solution.py:27
  90.1 0.5 collective-permute-start.29
  90.6 0.5 collective-permute-start.31
  91.1 0.4 collective-permute-done.28.refs_12_
  91.5 1.4 %collective-permute-start.33 = (bf16[2,128,384]{2,1,0:T(8,128)(2,1)S(1)}, bf16[2,128,384]{2,1,0:T(8,128)(2,1)S(1)}, u32[]{:S(2)}, u32[]{:S(2)}) collective-permute-start(bf16[2,128,384]{2,1,0:T(8,128)(2,1)S(1)} %get-tuple-element.77), channel_id=1, source_target_pairs={{0,8},{4,12},{8,0},{12,4},{1,9},{5,13},{9,1},{13,5},{2,10},{6,14},... | collective-permute-start | bytes 589832 | tf_op jit(solution)/shard_map/ppermute | solution.py:27
  92.9 0.1 collective-permute-start.34
  93.0 4.7 %step3ab.1.refs_1_ = bf16[4,128,384]{2,1,0:T(8,128)(2,1)S(1)} custom-call(f32[1,16]{1,0:T(1,128)S(1)} %copy-done.8, s32[1,4]{1,0:T(1,128)S(1)} %bitcast.11, f32[1,1536]{1,0:T(1,128)S(1)} %copy-done.1, f32[1,1536]{1,0:T(1,128)S(1)} %copy-done.2, f32[1,1536]{1,0:T(1,128)S(1)} %copy-done.4, s32[4,1,512]{2,1,0:T(1,128)S(1)} %copy-done.3, ...), custom_call_target="tpu_custom_call" | custom-call | flops 1610612736 | bytes 3145728 | tf_op jit(solution)/shard_map/step3ab/pallas_call | solution.py:505
  97.7 0.4 share.1
  98.1 0.9 collective-permute-start.38
  98.9 0.3 collective-permute-done.33.refs_4_
  99.3 1.0 settle.1
  100.3 1.5 %collective-permute-start.36 = (bf16[128,384]{1,0:T(8,128)(2,1)S(1)}, bf16[128,384]{1,0:T(8,128)(2,1)S(1)}, u32[]{:S(2)}, u32[]{:S(2)}) collective-permute-start(bf16[128,384]{1,0:T(8,128)(2,1)S(1)} %get-tuple-element.82), channel_id=1, source_target_pairs={{0,8},{4,12},{8,0},{12,4},{1,9},{5,13},{9,1},{13,5},{2,10},{6,14},... | collective-permute-start | bytes 294920 | tf_op jit(solution)/shard_map/ppermute | solution.py:27
  101.8 0.4 collective-permute-start.37
  102.2 1.8 %collective-permute-start.39 = (bf16[96,256]{1,0:T(8,128)(2,1)S(1)}, bf16[96,256]{1,0:T(8,128)(2,1)S(1)}, u32[]{:S(2)}, u32[]{:S(2)}) collective-permute-start(bf16[96,256]{1,0:T(8,128)(2,1)S(1)} %get-tuple-element.86), channel_id=1, source_target_pairs={{0,2},{1,3},{2,0},{3,1},{4,6},{5,7},{6,4},{7,5},{8,10},{9,11},{10,... | collective-permute-start | bytes 147464 | tf_op jit(solution)/shard_map/ppermute | solution.py:36
  103.9 0.3 collective-permute-done.38.refs_7_
  104.2 1.0 collective-permute-start.40
  105.2 3.2 %collective-permute-done.39.refs_8_ = bf16[96,256]{1,0:T(8,128)(2,1)S(1)} collective-permute-done((bf16[96,256]{1,0:T(8,128)(2,1)S(1)}, bf16[96,256]{1,0:T(8,128)(2,1)S(1)}, u32[]{:S(2)}, u32[]{:S(2)}) %collective-permute-start.39) | collective-permute-done | bytes 49184 | tf_op jit(solution)/shard_map/ppermute | solution.py:36
  108.4 0.2 collective-permute-done.40.refs_9_
  108.7 1.5 %finish.1 = (bf16[3,128,1536]{2,1,0:T(8,128)(2,1)}, f32[96,256]{1,0:T(8,128)}) custom-call(bf16[3,128,1536]{2,1,0:T(8,128)(2,1)} %get-tuple-element.78.refs_0_, bf16[2,128,384]{2,1,0:T(8,128)(2,1)S(1)} %collective-permute-done.34.refs_1_, bf16[128,384]{1,0:T(8,128)(2,1)S(1)} %get-tuple-element.80.refs_2_, ...), custom_call_target="tpu_custom_call", output_to_operand_aliasing={{0}: (0, {})} | custom-call | tf_op jit(solution)/shard_map/finish/pallas_call | solution.py:505
  (64 shorter events, 0.6 us)
Async XLA Ops:
  0.6 14.4 %copy-start = (bf16[1,3,1,128,1536]{4,3,2,1,0:T(8,128)(2,1)S(1)}, bf16[1,3,1,128,1536]{4,3,2,1,0:T(8,128)(2,1)}, u32[]{:S(2)}) copy-start(bf16[1,3,1,128,1536]{4,3,2,1,0:T(8,128)(2,1)} %incoming.3) | copy-start | bytes 3538948
  0.6 14.4 %copy-start.9 = (s32[4,1,128]{2,1,0:T(1,128)S(1)}, s32[4,1,128]{2,1,0:T(1,128)}, u32[]{:S(2)}) copy-start(s32[4,1,128]{2,1,0:T(1,128)} %contacts.1) | copy-start | bytes 6148
  2.1 1.5 %collective-permute-start = (bf16[2,96,384]{2,1,0:T(8,128)(2,1)S(1)}, bf16[2,96,384]{2,1,0:T(8,128)(2,1)S(1)}, u32[]{:S(2)}, u32[]{:S(2)}) collective-permute-start(bf16[2,96,384]{2,1,0:T(8,128)(2,1)S(1)} %get-tuple-element.47), channel_id=1, source_target_pairs={{0,4},{4,0},{8,12},{12,8},{1,5},{5,1},{9,13},{13,9},{2,6},{6,2},{1... | collective-permute-start | bytes 442376 | tf_op jit(solution)/shard_map/ppermute | solution.py:27
  3.7 11.3 %collective-permute-start.1 = (bf16[2,2,96,384]{3,2,1,0:T(8,128)(2,1)S(1)}, bf16[2,2,96,384]{3,2,1,0:T(8,128)(2,1)S(1)}, u32[]{:S(2)}, u32[]{:S(2)}) collective-permute-start(bf16[2,2,96,384]{3,2,1,0:T(8,128)(2,1)S(1)} %near.1), channel_id=1, source_target_pairs={{0,1},{1,3},{3,2},{2,0},{4,5},{5,7},{7,6},{6,4},{8,9},{9,11},{11,1... | collective-permute-start | bytes 884744 | tf_op jit(solution)/shard_map/ppermute | solution.py:46
  6.7 6.7 %collective-permute-start.2 = (bf16[2,96,384]{2,1,0:T(8,128)(2,1)S(1)}, bf16[2,96,384]{2,1,0:T(8,128)(2,1)S(1)}, u32[]{:S(2)}, u32[]{:S(2)}) collective-permute-start(bf16[2,96,384]{2,1,0:T(8,128)(2,1)S(1)} %get-tuple-element.48), channel_id=1, source_target_pairs={{0,8},{4,12},{8,0},{12,4},{1,9},{5,13},{9,1},{13,5},{2,10},{6,14},... | collective-permute-start | bytes 442376 | tf_op jit(solution)/shard_map/ppermute | solution.py:27
  8.2 6.3 %collective-permute-start.3 = (bf16[2,96,384]{2,1,0:T(8,128)(2,1)S(1)}, bf16[2,96,384]{2,1,0:T(8,128)(2,1)S(1)}, u32[]{:S(2)}, u32[]{:S(2)}) collective-permute-start(bf16[2,96,384]{2,1,0:T(8,128)(2,1)S(1)} %get-tuple-element.49), channel_id=1, source_target_pairs={{0,12},{4,8},{8,4},{12,0},{1,13},{5,9},{9,5},{13,1},{2,14},{6,10},... | collective-permute-start | bytes 442376 | tf_op jit(solution)/shard_map/ppermute | solution.py:27
  15.1 26.7 %collective-permute-start.4 = (bf16[272,1536]{1,0:T(8,128)(2,1)S(1)}, bf16[272,1536]{1,0:T(8,128)(2,1)S(1)}, u32[]{:S(2)}, u32[]{:S(2)}) collective-permute-start(bf16[272,1536]{1,0:T(8,128)(2,1)S(1)} %first.1.refs_0_), channel_id=1, source_target_pairs={{0,8},{4,12},{8,0},{12,4},{1,9},{5,13},{9,1},{13,5},{2,10},{6,14},... | collective-permute-start | bytes 2506760 | tf_op jit(solution)/shard_map/ppermute | solution.py:27
  16.7 9.8 %collective-permute-start.5 = (bf16[2,2,96,384]{3,2,1,0:T(8,128)(2,1)S(1)}, bf16[2,2,96,384]{3,2,1,0:T(8,128)(2,1)S(1)}, u32[]{:S(2)}, u32[]{:S(2)}) collective-permute-start(bf16[2,2,96,384]{3,2,1,0:T(8,128)(2,1)S(1)} %far.1), channel_id=1, source_target_pairs={{0,1},{1,3},{3,2},{2,0},{4,5},{5,7},{7,6},{6,4},{8,9},{9,11},{11,1... | collective-permute-start | bytes 884744 | tf_op jit(solution)/shard_map/ppermute | solution.py:46
  26.5 15.3 %collective-permute-start.8 = (bf16[4,96,384]{2,1,0:T(8,128)(2,1)S(1)}, bf16[4,96,384]{2,1,0:T(8,128)(2,1)S(1)}, u32[]{:S(2)}, u32[]{:S(2)}) collective-permute-start(bf16[4,96,384]{2,1,0:T(8,128)(2,1)S(1)} %part1.1.refs_0_), channel_id=1, source_target_pairs={{0,1},{1,3},{3,2},{2,0},{4,5},{5,7},{7,6},{6,4},{8,9},{9,11},{11,1... | collective-permute-start | bytes 884744 | tf_op jit(solution)/shard_map/ppermute | solution.py:46
  28.3 13.6 %copy-start.5 = (bf16[1,3,1,128,256]{4,3,2,1,0:T(8,128)(2,1)S(1)}, bf16[1,3,1,128,256]{4,3,2,1,0:T(8,128)(2,1)}, u32[]{:S(2)}) copy-start(bf16[1,3,1,128,256]{4,3,2,1,0:T(8,128)(2,1)} %cotangent.1) | copy-start | bytes 589828
  28.3 11.9 %collective-permute-start.6 = (bf16[2,96,384]{2,1,0:T(8,128)(2,1)S(1)}, bf16[2,96,384]{2,1,0:T(8,128)(2,1)S(1)}, u32[]{:S(2)}, u32[]{:S(2)}) collective-permute-start(bf16[2,96,384]{2,1,0:T(8,128)(2,1)S(1)} %get-tuple-element.50.refs_0_), channel_id=1, source_target_pairs={{0,1},{1,3},{3,2},{2,0},{4,5},{5,7},{7,6},{6,4},{8,9},{9,11},{11,1... | collective-permute-start | bytes 442376 | tf_op jit(solution)/shard_map/ppermute | solution.py:46
  30.0 11.8 %collective-permute-start.7 = (bf16[2,96,384]{2,1,0:T(8,128)(2,1)S(1)}, bf16[2,96,384]{2,1,0:T(8,128)(2,1)S(1)}, u32[]{:S(2)}, u32[]{:S(2)}) collective-permute-start(bf16[2,96,384]{2,1,0:T(8,128)(2,1)S(1)} %get-tuple-element.51.refs_1_), channel_id=1, source_target_pairs={{0,1},{1,3},{3,2},{2,0},{4,5},{5,7},{7,6},{6,4},{8,9},{9,11},{11,1... | collective-permute-start | bytes 442376 | tf_op jit(solution)/shard_map/ppermute | solution.py:46
  30.1 15.2 %collective-permute-start.10 = (bf16[272,1536]{1,0:T(8,128)(2,1)S(1)}, bf16[272,1536]{1,0:T(8,128)(2,1)S(1)}, u32[]{:S(2)}, u32[]{:S(2)}) collective-permute-start(bf16[272,1536]{1,0:T(8,128)(2,1)S(1)} %first.1.refs_0_), channel_id=1, source_target_pairs={{0,4},{4,0},{8,12},{12,8},{1,5},{5,1},{9,13},{13,9},{2,6},{6,2},{1... | collective-permute-start | bytes 2506760 | tf_op jit(solution)/shard_map/ppermute | solution.py:27
  41.8 3.4 %copy-start.1 = (f32[1,1536]{1,0:T(1,128)S(1)}, f32[1,1536]{1,0:T(1,128)}, u32[]{:S(2)}) copy-start(f32[1,1536]{1,0:T(1,128)} %refs_2_.11) | copy-start | bytes 18436
  41.8 3.4 %copy-start.2 = (f32[1,1536]{1,0:T(1,128)S(1)}, f32[1,1536]{1,0:T(1,128)}, u32[]{:S(2)}) copy-start(f32[1,1536]{1,0:T(1,128)} %refs_3_.11) | copy-start | bytes 18436
  41.8 3.4 %copy-start.6 = (bf16[1,16,1536]{2,1,0:T(8,128)(2,1)S(1)}, bf16[1,16,1536]{2,1,0:T(8,128)(2,1)}, u32[]{:S(2)}) copy-start(bf16[1,16,1536]{2,1,0:T(8,128)(2,1)} %table.1) | copy-start | bytes 147460
  41.8 3.4 %copy-start.7 = (s32[4,1]{0,1:T(1,128)S(1)}, s32[4,1]{0,1:T(1,128)}, u32[]{:S(2)}) copy-start(s32[4,1]{0,1:T(1,128)} %param.15) | copy-start | bytes 52
  41.9 3.4 %collective-permute-start.11 = (bf16[272,1536]{1,0:T(8,128)(2,1)S(1)}, bf16[272,1536]{1,0:T(8,128)(2,1)S(1)}, u32[]{:S(2)}, u32[]{:S(2)}) collective-permute-start(bf16[272,1536]{1,0:T(8,128)(2,1)S(1)} %tie.5.dep.refs_1_), channel_id=1, source_target_pairs={{0,4},{4,0},{8,12},{12,8},{1,5},{5,1},{9,13},{13,9},{2,6},{6,2},{1... | collective-permute-start | bytes 2506760 | tf_op jit(solution)/shard_map/ppermute | solution.py:27
  42.0 22.5 %collective-permute-start.9 = (bf16[256,1536]{1,0:T(8,128)(2,1)S(1)}, bf16[256,1536]{1,0:T(8,128)(2,1)S(1)}, u32[]{:S(2)}, u32[]{:S(2)}) collective-permute-start(bf16[256,1536]{1,0:T(8,128)(2,1)S(1)} %second.1.mine.refs_6_.refs_3_.refs_2_), channel_id=1, source_target_pairs={{0,8},{4,12},{8,0},{12,4},{1,9},{5,13},{9,1},{13,5},{2,10},{6,14},... | collective-permute-start | bytes 2359304 | tf_op jit(solution)/shard_map/ppermute | solution.py:27
  42.6 7.6 %collective-permute-start.13 = (bf16[2,96,384]{2,1,0:T(8,128)(2,1)S(1)}, bf16[2,96,384]{2,1,0:T(8,128)(2,1)S(1)}, u32[]{:S(2)}, u32[]{:S(2)}) collective-permute-start(bf16[2,96,384]{2,1,0:T(8,128)(2,1)S(1)} %collective-permute-done.6.refs_1_.refs_9_), channel_id=1, source_target_pairs={{0,1},{1,3},{3,2},{2,0},{4,5},{5,7},{7,6},{6,4},{8,9},{9,11},{11,1... | collective-permute-start | bytes 442376 | tf_op jit(solution)/shard_map/ppermute | solution.py:46
  44.1 9.2 %collective-permute-start.14 = (bf16[2,96,384]{2,1,0:T(8,128)(2,1)S(1)}, bf16[2,96,384]{2,1,0:T(8,128)(2,1)S(1)}, u32[]{:S(2)}, u32[]{:S(2)}) collective-permute-start(bf16[2,96,384]{2,1,0:T(8,128)(2,1)S(1)} %collective-permute-done.7.refs_2_.refs_10_), channel_id=1, source_target_pairs={{0,1},{1,3},{3,2},{2,0},{4,5},{5,7},{7,6},{6,4},{8,9},{9,11},{11,1... | collective-permute-start | bytes 442376 | tf_op jit(solution)/shard_map/ppermute | solution.py:46
  48.6 4.6 %copy-start.3 = (s32[4,1,512]{2,1,0:T(1,128)S(1)}, s32[4,1,512]{2,1,0:T(1,128)}, u32[]{:S(2)}) copy-start(s32[4,1,512]{2,1,0:T(1,128)} %refs_5_.11) | copy-start | bytes 24580
  48.7 4.6 %copy-start.4 = (f32[1,1536]{1,0:T(1,128)S(1)}, f32[1,1536]{1,0:T(1,128)}, u32[]{:S(2)}) copy-start(f32[1,1536]{1,0:T(1,128)} %refs_4_.11) | copy-start | bytes 18436
  48.7 4.6 %copy-start.8 = (f32[1,16]{1,0:T(1,128)S(1)}, f32[1,16]{1,0:T(1,128)}, u32[]{:S(2)}) copy-start(f32[1,16]{1,0:T(1,128)} %refs_0_.11) | copy-start | bytes 196
  48.7 13.0 %collective-permute-start.12 = (bf16[4,96,384]{2,1,0:T(8,128)(2,1)S(1)}, bf16[4,96,384]{2,1,0:T(8,128)(2,1)S(1)}, u32[]{:S(2)}, u32[]{:S(2)}) collective-permute-start(bf16[4,96,384]{2,1,0:T(8,128)(2,1)S(1)} %tie.6.refs_9_), channel_id=1, source_target_pairs={{0,1},{1,3},{3,2},{2,0},{4,5},{5,7},{7,6},{6,4},{8,9},{9,11},{11,1... | collective-permute-start | bytes 884744 | tf_op jit(solution)/shard_map/ppermute | solution.py:46
  56.0 5.7 %collective-permute-start.15 = (bf16[768,128]{1,0:T(8,128)(2,1)S(1)}, bf16[768,128]{1,0:T(8,128)(2,1)S(1)}, u32[]{:S(2)}, u32[]{:S(2)}) collective-permute-start(bf16[768,128]{1,0:T(8,128)(2,1)S(1)} %get-tuple-element.55), channel_id=1, source_target_pairs={{0,16},{16,0},{1,17},{17,1},{2,18},{18,2},{3,19},{19,3},{4,20},{20... | collective-permute-start | bytes 589832 | tf_op jit(solution)/shard_map/ppermute | solution.py:31
  64.7 7.8 %collective-permute-start.16 = (bf16[2,256,1536]{2,1,0:T(8,128)(2,1)S(1)}, bf16[2,256,1536]{2,1,0:T(8,128)(2,1)S(1)}, u32[]{:S(2)}, u32[]{:S(2)}) collective-permute-start(bf16[2,256,1536]{2,1,0:T(8,128)(2,1)S(1)} %beside.1), channel_id=1, source_target_pairs={{0,4},{4,0},{8,12},{12,8},{1,5},{5,1},{9,13},{13,9},{2,6},{6,2},{1... | collective-permute-start | bytes 4718600 | tf_op jit(solution)/shard_map/ppermute | solution.py:27
  64.7 7.8 %collective-permute-start.20 = (bf16[768,128]{1,0:T(8,128)(2,1)S(1)}, bf16[768,128]{1,0:T(8,128)(2,1)S(1)}, u32[]{:S(2)}, u32[]{:S(2)}) collective-permute-start(bf16[768,128]{1,0:T(8,128)(2,1)S(1)} %get-tuple-element.64), channel_id=1, source_target_pairs={{0,16},{16,0},{1,17},{17,1},{2,18},{18,2},{3,19},{19,3},{4,20},{20... | collective-permute-start | bytes 589832 | tf_op jit(solution)/shard_map/ppermute | solution.py:31
  66.2 10.0 %collective-permute-start.24 = (bf16[768,128]{1,0:T(8,128)(2,1)S(1)}, bf16[768,128]{1,0:T(8,128)(2,1)S(1)}, u32[]{:S(2)}, u32[]{:S(2)}) collective-permute-start(bf16[768,128]{1,0:T(8,128)(2,1)S(1)} %get-tuple-element.68), channel_id=1, source_target_pairs={{0,16},{16,0},{1,17},{17,1},{2,18},{18,2},{3,19},{19,3},{4,20},{20... | collective-permute-start | bytes 589832 | tf_op jit(solution)/shard_map/ppermute | solution.py:31
  66.8 8.6 %collective-permute-start.17 = (bf16[768,128]{1,0:T(8,128)(2,1)S(1)}, bf16[768,128]{1,0:T(8,128)(2,1)S(1)}, u32[]{:S(2)}, u32[]{:S(2)}) collective-permute-start(bf16[768,128]{1,0:T(8,128)(2,1)S(1)} %collective-permute-done.15.refs_1_.refs_10_), channel_id=1, source_target_pairs={{0,8},{4,12},{8,0},{12,4},{1,9},{5,13},{9,1},{13,5},{2,10},{6,14},... | collective-permute-start | bytes 589832 | tf_op jit(solution)/shard_map/ppermute | solution.py:27
  72.5 6.0 %collective-permute-start.21 = (bf16[768,128]{1,0:T(8,128)(2,1)S(1)}, bf16[768,128]{1,0:T(8,128)(2,1)S(1)}, u32[]{:S(2)}, u32[]{:S(2)}) collective-permute-start(bf16[768,128]{1,0:T(8,128)(2,1)S(1)} %tie.8.refs_14_), channel_id=1, source_target_pairs={{0,8},{4,12},{8,0},{12,4},{1,9},{5,13},{9,1},{13,5},{2,10},{6,14},... | collective-permute-start | bytes 589832 | tf_op jit(solution)/shard_map/ppermute | solution.py:27
  73.9 4.6 %collective-permute-start.18 = (bf16[768,128]{1,0:T(8,128)(2,1)S(1)}, bf16[768,128]{1,0:T(8,128)(2,1)S(1)}, u32[]{:S(2)}, u32[]{:S(2)}) collective-permute-start(bf16[768,128]{1,0:T(8,128)(2,1)S(1)} %collective-permute-done.15.refs_1_.refs_10_), channel_id=1, source_target_pairs={{0,4},{4,0},{8,12},{12,8},{1,5},{5,1},{9,13},{13,9},{2,6},{6,2},{1... | collective-permute-start | bytes 589832 | tf_op jit(solution)/shard_map/ppermute | solution.py:27
  73.9 7.3 %collective-permute-start.26 = (bf16[768,128]{1,0:T(8,128)(2,1)S(1)}, bf16[768,128]{1,0:T(8,128)(2,1)S(1)}, u32[]{:S(2)}, u32[]{:S(2)}) collective-permute-start(bf16[768,128]{1,0:T(8,128)(2,1)S(1)} %get-tuple-element.69), channel_id=1, source_target_pairs={{0,16},{16,0},{1,17},{17,1},{2,18},{18,2},{3,19},{19,3},{4,20},{20... | collective-permute-start | bytes 589832 | tf_op jit(solution)/shard_map/ppermute | solution.py:31
  75.4 6.4 %collective-permute-start.19 = (bf16[768,128]{1,0:T(8,128)(2,1)S(1)}, bf16[768,128]{1,0:T(8,128)(2,1)S(1)}, u32[]{:S(2)}, u32[]{:S(2)}) collective-permute-start(bf16[768,128]{1,0:T(8,128)(2,1)S(1)} %collective-permute-done.17.refs_11_), channel_id=1, source_target_pairs={{0,4},{4,0},{8,12},{12,8},{1,5},{5,1},{9,13},{13,9},{2,6},{6,2},{1... | collective-permute-start | bytes 589832 | tf_op jit(solution)/shard_map/ppermute | solution.py:27
  76.3 5.6 %collective-permute-start.22 = (bf16[768,128]{1,0:T(8,128)(2,1)S(1)}, bf16[768,128]{1,0:T(8,128)(2,1)S(1)}, u32[]{:S(2)}, u32[]{:S(2)}) collective-permute-start(bf16[768,128]{1,0:T(8,128)(2,1)S(1)} %tie.8.refs_14_), channel_id=1, source_target_pairs={{0,4},{4,0},{8,12},{12,8},{1,5},{5,1},{9,13},{13,9},{2,6},{6,2},{1... | collective-permute-start | bytes 589832 | tf_op jit(solution)/shard_map/ppermute | solution.py:27
  78.5 3.4 %collective-permute-start.23 = (bf16[768,128]{1,0:T(8,128)(2,1)S(1)}, bf16[768,128]{1,0:T(8,128)(2,1)S(1)}, u32[]{:S(2)}, u32[]{:S(2)}) collective-permute-start(bf16[768,128]{1,0:T(8,128)(2,1)S(1)} %collective-permute-done.21.refs_15_), channel_id=1, source_target_pairs={{0,4},{4,0},{8,12},{12,8},{1,5},{5,1},{9,13},{13,9},{2,6},{6,2},{1... | collective-permute-start | bytes 589832 | tf_op jit(solution)/shard_map/ppermute | solution.py:27
  78.5 8.8 %collective-permute-start.25 = (bf16[768,128]{1,0:T(8,128)(2,1)S(1)}, bf16[768,128]{1,0:T(8,128)(2,1)S(1)}, u32[]{:S(2)}, u32[]{:S(2)}) collective-permute-start(bf16[768,128]{1,0:T(8,128)(2,1)S(1)} %collective-permute-done.24.refs_0_), channel_id=1, source_target_pairs={{0,8},{4,12},{8,0},{12,4},{1,9},{5,13},{9,1},{13,5},{2,10},{6,14},... | collective-permute-start | bytes 589832 | tf_op jit(solution)/shard_map/ppermute | solution.py:27
  81.2 8.8 %collective-permute-start.27 = (bf16[768,128]{1,0:T(8,128)(2,1)S(1)}, bf16[768,128]{1,0:T(8,128)(2,1)S(1)}, u32[]{:S(2)}, u32[]{:S(2)}) collective-permute-start(bf16[768,128]{1,0:T(8,128)(2,1)S(1)} %collective-permute-done.26.refs_2_), channel_id=1, source_target_pairs={{0,8},{4,12},{8,0},{12,4},{1,9},{5,13},{9,1},{13,5},{2,10},{6,14},... | collective-permute-start | bytes 589832 | tf_op jit(solution)/shard_map/ppermute | solution.py:27
  90.1 1.4 %collective-permute-start.28 = (bf16[768,128]{1,0:T(8,128)(2,1)S(1)}, bf16[768,128]{1,0:T(8,128)(2,1)S(1)}, u32[]{:S(2)}, u32[]{:S(2)}) collective-permute-start(bf16[768,128]{1,0:T(8,128)(2,1)S(1)} %get-tuple-element.71.refs_10_), channel_id=1, source_target_pairs={{0,4},{4,0},{8,12},{12,8},{1,5},{5,1},{9,13},{13,9},{2,6},{6,2},{1... | collective-permute-start | bytes 589832 | tf_op jit(solution)/shard_map/ppermute | solution.py:27
  90.1 2.8 %collective-permute-start.29 = (bf16[768,128]{1,0:T(8,128)(2,1)S(1)}, bf16[768,128]{1,0:T(8,128)(2,1)S(1)}, u32[]{:S(2)}, u32[]{:S(2)}) collective-permute-start(bf16[768,128]{1,0:T(8,128)(2,1)S(1)} %get-tuple-element.72.refs_11_), channel_id=1, source_target_pairs={{0,4},{4,0},{8,12},{12,8},{1,5},{5,1},{9,13},{13,9},{2,6},{6,2},{1... | collective-permute-start | bytes 589832 | tf_op jit(solution)/shard_map/ppermute | solution.py:27
  90.6 2.4 %collective-permute-start.30 = (bf16[768,128]{1,0:T(8,128)(2,1)S(1)}, bf16[768,128]{1,0:T(8,128)(2,1)S(1)}, u32[]{:S(2)}, u32[]{:S(2)}) collective-permute-start(bf16[768,128]{1,0:T(8,128)(2,1)S(1)} %get-tuple-element.73.refs_14_), channel_id=1, source_target_pairs={{0,4},{4,0},{8,12},{12,8},{1,5},{5,1},{9,13},{13,9},{2,6},{6,2},{1... | collective-permute-start | bytes 589832 | tf_op jit(solution)/shard_map/ppermute | solution.py:27
  90.6 2.4 %collective-permute-start.31 = (bf16[768,128]{1,0:T(8,128)(2,1)S(1)}, bf16[768,128]{1,0:T(8,128)(2,1)S(1)}, u32[]{:S(2)}, u32[]{:S(2)}) collective-permute-start(bf16[768,128]{1,0:T(8,128)(2,1)S(1)} %get-tuple-element.74.refs_15_), channel_id=1, source_target_pairs={{0,4},{4,0},{8,12},{12,8},{1,5},{5,1},{9,13},{13,9},{2,6},{6,2},{1... | collective-permute-start | bytes 589832 | tf_op jit(solution)/shard_map/ppermute | solution.py:27
  91.1 7.9 %collective-permute-start.32 = (bf16[2,128,384]{2,1,0:T(8,128)(2,1)S(1)}, bf16[2,128,384]{2,1,0:T(8,128)(2,1)S(1)}, u32[]{:S(2)}, u32[]{:S(2)}) collective-permute-start(bf16[2,128,384]{2,1,0:T(8,128)(2,1)S(1)} %get-tuple-element.76), channel_id=1, source_target_pairs={{0,4},{4,0},{8,12},{12,8},{1,5},{5,1},{9,13},{13,9},{2,6},{6,2},{1... | collective-permute-start | bytes 589832 | tf_op jit(solution)/shard_map/ppermute | solution.py:27
  91.5 7.7 %collective-permute-start.33 = (bf16[2,128,384]{2,1,0:T(8,128)(2,1)S(1)}, bf16[2,128,384]{2,1,0:T(8,128)(2,1)S(1)}, u32[]{:S(2)}, u32[]{:S(2)}) collective-permute-start(bf16[2,128,384]{2,1,0:T(8,128)(2,1)S(1)} %get-tuple-element.77), channel_id=1, source_target_pairs={{0,8},{4,12},{8,0},{12,4},{1,9},{5,13},{9,1},{13,5},{2,10},{6,14},... | collective-permute-start | bytes 589832 | tf_op jit(solution)/shard_map/ppermute | solution.py:27
  92.9 9.3 %collective-permute-start.34 = (bf16[2,128,384]{2,1,0:T(8,128)(2,1)S(1)}, bf16[2,128,384]{2,1,0:T(8,128)(2,1)S(1)}, u32[]{:S(2)}, u32[]{:S(2)}) collective-permute-start(bf16[2,128,384]{2,1,0:T(8,128)(2,1)S(1)} %get-tuple-element.79), channel_id=1, source_target_pairs={{0,12},{4,8},{8,4},{12,0},{1,13},{5,9},{9,5},{13,1},{2,14},{6,10},... | collective-permute-start | bytes 589832 | tf_op jit(solution)/shard_map/ppermute | solution.py:27
  98.1 6.1 %collective-permute-start.38 = (bf16[96,256]{1,0:T(8,128)(2,1)S(1)}, bf16[96,256]{1,0:T(8,128)(2,1)S(1)}, u32[]{:S(2)}, u32[]{:S(2)}) collective-permute-start(bf16[96,256]{1,0:T(8,128)(2,1)S(1)} %get-tuple-element.85), channel_id=1, source_target_pairs={{0,1},{1,2},{2,3},{3,0},{4,5},{5,6},{6,7},{7,4},{8,9},{9,10},{10,1... | collective-permute-start | bytes 147464 | tf_op jit(solution)/shard_map/ppermute | solution.py:36
  100.2 8.4 %collective-permute-start.35 = (bf16[128,384]{1,0:T(8,128)(2,1)S(1)}, bf16[128,384]{1,0:T(8,128)(2,1)S(1)}, u32[]{:S(2)}, u32[]{:S(2)}) collective-permute-start(bf16[128,384]{1,0:T(8,128)(2,1)S(1)} %get-tuple-element.81), channel_id=1, source_target_pairs={{0,4},{4,0},{8,12},{12,8},{1,5},{5,1},{9,13},{13,9},{2,6},{6,2},{1... | collective-permute-start | bytes 294920 | tf_op jit(solution)/shard_map/ppermute | solution.py:27
  100.3 8.3 %collective-permute-start.36 = (bf16[128,384]{1,0:T(8,128)(2,1)S(1)}, bf16[128,384]{1,0:T(8,128)(2,1)S(1)}, u32[]{:S(2)}, u32[]{:S(2)}) collective-permute-start(bf16[128,384]{1,0:T(8,128)(2,1)S(1)} %get-tuple-element.82), channel_id=1, source_target_pairs={{0,8},{4,12},{8,0},{12,4},{1,9},{5,13},{9,1},{13,5},{2,10},{6,14},... | collective-permute-start | bytes 294920 | tf_op jit(solution)/shard_map/ppermute | solution.py:27
  101.8 6.9 %collective-permute-start.37 = (bf16[128,384]{1,0:T(8,128)(2,1)S(1)}, bf16[128,384]{1,0:T(8,128)(2,1)S(1)}, u32[]{:S(2)}, u32[]{:S(2)}) collective-permute-start(bf16[128,384]{1,0:T(8,128)(2,1)S(1)} %get-tuple-element.83), channel_id=1, source_target_pairs={{0,12},{4,8},{8,4},{12,0},{1,13},{5,9},{9,5},{13,1},{2,14},{6,10},... | collective-permute-start | bytes 294920 | tf_op jit(solution)/shard_map/ppermute | solution.py:27
  102.2 6.2 %collective-permute-start.39 = (bf16[96,256]{1,0:T(8,128)(2,1)S(1)}, bf16[96,256]{1,0:T(8,128)(2,1)S(1)}, u32[]{:S(2)}, u32[]{:S(2)}) collective-permute-start(bf16[96,256]{1,0:T(8,128)(2,1)S(1)} %get-tuple-element.86), channel_id=1, source_target_pairs={{0,2},{1,3},{2,0},{3,1},{4,6},{5,7},{6,4},{7,5},{8,10},{9,11},{10,... | collective-permute-start | bytes 147464 | tf_op jit(solution)/shard_map/ppermute | solution.py:36
  104.2 4.4 %collective-permute-start.40 = (bf16[96,256]{1,0:T(8,128)(2,1)S(1)}, bf16[96,256]{1,0:T(8,128)(2,1)S(1)}, u32[]{:S(2)}, u32[]{:S(2)}) collective-permute-start(bf16[96,256]{1,0:T(8,128)(2,1)S(1)} %get-tuple-element.87), channel_id=1, source_target_pairs={{0,3},{1,0},{2,1},{3,2},{4,7},{5,4},{6,5},{7,6},{8,11},{9,8},{10,9... | collective-permute-start | bytes 147464 | tf_op jit(solution)/shard_map/ppermute | solution.py:36

commit v20 on v19

--- a/solution.py
+++ b/solution.py
@@ -91,13 +91,19 @@
         out[at] = ref[...]
 
 
+def far_kernel(dep, first, second, *outs):
+    for part, out in enumerate(outs):
+        out[0] = first[part]
+        out[1] = second[part]
+
+
 def part_kernel(part, near, far, *outs):
     for at in range(2):
         outs[0][at] = near[at, part]
         if len(outs) == 1:
-            outs[0][at + 2] = far[at, part]
+            outs[0][at + 2] = far[at]
         else:
-            outs[1][at] = far[at, part]
+            outs[1][at] = far[at]
 
 
 def place(hop, hops, blocks, weights):
@@ -114,7 +120,7 @@
 
 def place_kernel(part, hops, near, far, *refs):
     chunk, weights = refs[:-1], refs[-1]
-    place(0, hops, [near.at[0, part], near.at[1, part], far.at[0, part], far.at[1, part]], weights)
+    place(0, hops, [near.at[0, part], near.at[1, part], far.at[0], far.at[1]], weights)
     place(1, hops, blocks_in(chunk), weights)
 
 
@@ -544,8 +550,15 @@
 
     near = paired("near", [], blocks[:2])
     near_next = ring_step(near)
-    far = paired("far", [near_next], blocks[2:])
-    far_next = ring_step(far)
+    far = call(
+        far_kernel,
+        "far",
+        [pltpu.VMEM((2, w_rows, cols), kind)] * 2,
+        [anywhere, vmem, vmem],
+        [near_next] + blocks[2:],
+        out_specs=[vmem] * 2,
+    )
+    far_next = [ring_step(value) for value in far]
     streams = (2, 1)
     rings, partial = [], []
     for part in range(2):
@@ -555,7 +568,7 @@
             "part%d" % part,
             [pltpu.VMEM((seq_count // count, w_rows, cols), kind)] * count,
             [vmem, vmem],
-            [near_next, far_next],
+            [near_next, far_next[part]],
             out_specs=[vmem] * count,
         )
         rings.append([list(chunk)])
@@ -565,7 +578,7 @@
                 "place%d" % part,
                 pltpu.VMEM((width, cols), kind),
                 [vmem] * (2 + count),
-                [pin(near), pin(far)] + [pin(value) for value in chunk],
+                [pin(near), pin(far[part])] + [pin(value) for value in chunk],
                 out_specs=vmem,
             )
         )
@@ -589,7 +602,7 @@
         "first",
         pltpu.VMEM((2 * rows + 16, width), kind),
         [anywhere, vmem, vmem],
-        [far, incoming, contacts],
+        [far[0], incoming, contacts],
         [pltpu.VMEM((16, 128), jnp.float32)],
         out_specs=vmem,
     )

time: 110 us -> 108 us (0.982)
  waiting for transfers between devices: 45.6 us -> 37.9 us
  starting transfers between devices: 34.4 us -> 39.9 us
    ppermute x8 -> x9, waiting for transfers between devices: 23.9 us -> 16.3 us  [ring_step(): return lax.ppermute(value, 'dp', pairs)]
    ppermute x8 -> x9, starting transfers between devices: 11.7 us -> 16 us  [ring_step(): return lax.ppermute(value, 'dp', pairs)]
  transfers between devices with their start and end apart: 41 -> 42, of which waited for: 20 -> 19; matrix products, arithmetic and copies ran while one was open for 0% -> 0% of each run, Pallas kernels for 23% -> 24%
where the time goes in v20:
time: 108 us
  starting transfers between devices  39.9 us (37%)
  waiting for transfers between devices  37.9 us (35%)
  Pallas kernels  29.1 us (27%)
  between operations  1.16 us (1%)
    pallas_call x26, Pallas kernels, call(): pl.pallas_call(kernel, out_shape=out_shape, in_specs=in_specs, scratch_sh...  29.1 us
    ppermute x9, waiting for transfers between devices, ring_step(): return lax.ppermute(value, 'dp', pairs)  16.3 us
    ppermute x9, starting transfers between devices, ring_step(): return lax.ppermute(value, 'dp', pairs)  16 us
    ppermute x26, starting transfers between devices, swap(): lax.ppermute(value, 'seq', [(source, source ^ bit) for source in range(co...  14.3 us
    ppermute x26, waiting for transfers between devices, swap(): lax.ppermute(value, 'seq', [(source, source ^ bit) for source in range(co...  12.7 us
    ppermute x4, waiting for transfers between devices, handed_over(): return lax.ppermute(value, 'pipe', [(0, 1), (1, 0)])  5.21 us
    ppermute x4, starting transfers between devices, handed_over(): return lax.ppermute(value, 'pipe', [(0, 1), (1, 0)])  5.19 us
    ppermute x3, starting transfers between devices, shifted(): lax.ppermute(value, axis, [(source, (source + shift) % count) for source...  4.44 us
  transfers between devices with their start and end apart: 42, of which 19 were waited for; matrix products, arithmetic and copies ran while one was open for 0% of the time, Pallas kernels for 24%

profile of v20, /device:TPU:0, one launch (start us, length us, event | category | flops | bytes accessed | tf_op | source)
XLA Modules:
  0.0 108.1 jit_solution(9558917171745850101)
XLA Ops:
  0.7 1.5 %pack.1 = (bf16[2,96,384]{2,1,0:T(8,128)(2,1)S(1)}, bf16[2,96,384]{2,1,0:T(8,128)(2,1)S(1)}, bf16[2,96,384]{2,1,0:T(8,128)(2,1)S(1)}, bf16[2,96,384]{2,1,0:T(8,128)(2,1)S(1)}) custom-call(bf16[1,96,1536]{2,1,0:T(8,128)(2,1)} %wq.1, bf16[1,96,1536]{2,1,0:T(8,128)(2,1)} %wkv.1), custom_call_target="tpu_custom_call" | custom-call | tf_op jit(solution)/shard_map/pack/pallas_call | solution.py:511
  2.1 0.5 collective-permute-start
  2.7 1.0 collective-permute-done.refs_1_
  3.7 3.0 %collective-permute-start.1 = (bf16[2,2,96,384]{3,2,1,0:T(8,128)(2,1)S(1)}, bf16[2,2,96,384]{3,2,1,0:T(8,128)(2,1)S(1)}, u32[]{:S(2)}, u32[]{:S(2)}) collective-permute-start(bf16[2,2,96,384]{3,2,1,0:T(8,128)(2,1)S(1)} %near.1), channel_id=1, source_target_pairs={{0,1},{1,3},{3,2},{2,0},{4,5},{5,7},{7,6},{6,4},{8,9},{9,11},{11,1... | collective-permute-start | bytes 884744 | tf_op jit(solution)/shard_map/ppermute | solution.py:46
  6.7 1.5 %collective-permute-start.2 = (bf16[2,96,384]{2,1,0:T(8,128)(2,1)S(1)}, bf16[2,96,384]{2,1,0:T(8,128)(2,1)S(1)}, u32[]{:S(2)}, u32[]{:S(2)}) collective-permute-start(bf16[2,96,384]{2,1,0:T(8,128)(2,1)S(1)} %get-tuple-element.50), channel_id=1, source_target_pairs={{0,8},{4,12},{8,0},{12,4},{1,9},{5,13},{9,1},{13,5},{2,10},{6,14},... | collective-permute-start | bytes 442376 | tf_op jit(solution)/shard_map/ppermute | solution.py:27
  8.2 5.2 %collective-permute-done.2.first = bf16[2,96,384]{2,1,0:T(8,128)(2,1)S(1)} collective-permute-done((bf16[2,96,384]{2,1,0:T(8,128)(2,1)S(1)}, bf16[2,96,384]{2,1,0:T(8,128)(2,1)S(1)}, u32[]{:S(2)}, u32[]{:S(2)}) %collective-permute-start.2) | collective-permute-done | bytes 147488 | tf_op jit(solution)/shard_map/ppermute | solution.py:27
  13.4 1.1 collective-permute-done.3.second
  14.5 0.5 collective-permute-done.1.dep.near
  15.1 1.6 %collective-permute-start.4 = (bf16[272,1536]{1,0:T(8,128)(2,1)S(1)}, bf16[272,1536]{1,0:T(8,128)(2,1)S(1)}, u32[]{:S(2)}, u32[]{:S(2)}) collective-permute-start(bf16[272,1536]{1,0:T(8,128)(2,1)S(1)} %first.1.refs_0_), channel_id=1, source_target_pairs={{0,8},{4,12},{8,0},{12,4},{1,9},{5,13},{9,1},{13,5},{2,10},{6,14},... | collective-permute-start | bytes 2506760 | tf_op jit(solution)/shard_map/ppermute | solution.py:27
  16.7 1.9 %collective-permute-start.8 = (bf16[2,96,384]{2,1,0:T(8,128)(2,1)S(1)}, bf16[2,96,384]{2,1,0:T(8,128)(2,1)S(1)}, u32[]{:S(2)}, u32[]{:S(2)}) collective-permute-start(bf16[2,96,384]{2,1,0:T(8,128)(2,1)S(1)} %get-tuple-element.55.far), channel_id=1, source_target_pairs={{0,1},{1,3},{3,2},{2,0},{4,5},{5,7},{7,6},{6,4},{8,9},{9,11},{11,1... | collective-permute-start | bytes 442376 | tf_op jit(solution)/shard_map/ppermute | solution.py:46
  18.6 2.3 %collective-permute-start.5 = (bf16[2,96,384]{2,1,0:T(8,128)(2,1)S(1)}, bf16[2,96,384]{2,1,0:T(8,128)(2,1)S(1)}, u32[]{:S(2)}, u32[]{:S(2)}) collective-permute-start(bf16[2,96,384]{2,1,0:T(8,128)(2,1)S(1)} %get-tuple-element.52.far), channel_id=1, source_target_pairs={{0,1},{1,3},{3,2},{2,0},{4,5},{5,7},{7,6},{6,4},{8,9},{9,11},{11,1... | collective-permute-start | bytes 442376 | tf_op jit(solution)/shard_map/ppermute | solution.py:46
  20.9 3.2 %collective-permute-done.8.far = bf16[2,96,384]{2,1,0:T(8,128)(2,1)S(1)} collective-permute-done((bf16[2,96,384]{2,1,0:T(8,128)(2,1)S(1)}, bf16[2,96,384]{2,1,0:T(8,128)(2,1)S(1)}, u32[]{:S(2)}, u32[]{:S(2)}) %collective-permute-start.8) | collective-permute-done | bytes 147488 | tf_op jit(solution)/shard_map/ppermute | solution.py:46
  24.2 1.2 %collective-permute-start.9 = (bf16[4,96,384]{2,1,0:T(8,128)(2,1)S(1)}, bf16[4,96,384]{2,1,0:T(8,128)(2,1)S(1)}, u32[]{:S(2)}, u32[]{:S(2)}) collective-permute-start(bf16[4,96,384]{2,1,0:T(8,128)(2,1)S(1)} %part1.1.refs_0_), channel_id=1, source_target_pairs={{0,1},{1,3},{3,2},{2,0},{4,5},{5,7},{7,6},{6,4},{8,9},{9,11},{11,1... | collective-permute-start | bytes 884744 | tf_op jit(solution)/shard_map/ppermute | solution.py:46
  25.4 1.5 %collective-permute-done.5.far = bf16[2,96,384]{2,1,0:T(8,128)(2,1)S(1)} collective-permute-done((bf16[2,96,384]{2,1,0:T(8,128)(2,1)S(1)}, bf16[2,96,384]{2,1,0:T(8,128)(2,1)S(1)}, u32[]{:S(2)}, u32[]{:S(2)}) %collective-permute-start.5) | collective-permute-done | bytes 147488 | tf_op jit(solution)/shard_map/ppermute | solution.py:46
  27.0 1.6 %collective-permute-start.6 = (bf16[2,96,384]{2,1,0:T(8,128)(2,1)S(1)}, bf16[2,96,384]{2,1,0:T(8,128)(2,1)S(1)}, u32[]{:S(2)}, u32[]{:S(2)}) collective-permute-start(bf16[2,96,384]{2,1,0:T(8,128)(2,1)S(1)} %get-tuple-element.53.refs_0_), channel_id=1, source_target_pairs={{0,1},{1,3},{3,2},{2,0},{4,5},{5,7},{7,6},{6,4},{8,9},{9,11},{11,1... | collective-permute-start | bytes 442376 | tf_op jit(solution)/shard_map/ppermute | solution.py:46
  28.6 2.4 %collective-permute-start.7 = (bf16[2,96,384]{2,1,0:T(8,128)(2,1)S(1)}, bf16[2,96,384]{2,1,0:T(8,128)(2,1)S(1)}, u32[]{:S(2)}, u32[]{:S(2)}) collective-permute-start(bf16[2,96,384]{2,1,0:T(8,128)(2,1)S(1)} %get-tuple-element.54.refs_1_), channel_id=1, source_target_pairs={{0,1},{1,3},{3,2},{2,0},{4,5},{5,7},{7,6},{6,4},{8,9},{9,11},{11,1... | collective-permute-start | bytes 442376 | tf_op jit(solution)/shard_map/ppermute | solution.py:46
  31.0 6.6 %collective-permute-done.6.refs_1_.refs_9_ = bf16[2,96,384]{2,1,0:T(8,128)(2,1)S(1)} collective-permute-done((bf16[2,96,384]{2,1,0:T(8,128)(2,1)S(1)}, bf16[2,96,384]{2,1,0:T(8,128)(2,1)S(1)}, u32[]{:S(2)}, u32[]{:S(2)}) %collective-permute-start.6) | collective-permute-done | bytes 147488 | tf_op jit(solution)/shard_map/ppermute | solution.py:46
  37.6 1.6 %collective-permute-done.7.refs_2_.refs_10_ = bf16[2,96,384]{2,1,0:T(8,128)(2,1)S(1)} collective-permute-done((bf16[2,96,384]{2,1,0:T(8,128)(2,1)S(1)}, bf16[2,96,384]{2,1,0:T(8,128)(2,1)S(1)}, u32[]{:S(2)}, u32[]{:S(2)}) %collective-permute-start.7) | collective-permute-done | bytes 147488 | tf_op jit(solution)/shard_map/ppermute | solution.py:46
  39.3 0.6 collective-permute-start.10
  39.9 1.7 %collective-permute-start.14 = (bf16[2,96,384]{2,1,0:T(8,128)(2,1)S(1)}, bf16[2,96,384]{2,1,0:T(8,128)(2,1)S(1)}, u32[]{:S(2)}, u32[]{:S(2)}) collective-permute-start(bf16[2,96,384]{2,1,0:T(8,128)(2,1)S(1)} %collective-permute-done.6.refs_1_.refs_9_), channel_id=1, source_target_pairs={{0,1},{1,3},{3,2},{2,0},{4,5},{5,7},{7,6},{6,4},{8,9},{9,11},{11,1... | collective-permute-start | bytes 442376 | tf_op jit(solution)/shard_map/ppermute | solution.py:46
  41.6 1.6 %collective-permute-start.15 = (bf16[2,96,384]{2,1,0:T(8,128)(2,1)S(1)}, bf16[2,96,384]{2,1,0:T(8,128)(2,1)S(1)}, u32[]{:S(2)}, u32[]{:S(2)}) collective-permute-start(bf16[2,96,384]{2,1,0:T(8,128)(2,1)S(1)} %collective-permute-done.7.refs_2_.refs_10_), channel_id=1, source_target_pairs={{0,1},{1,3},{3,2},{2,0},{4,5},{5,7},{7,6},{6,4},{8,9},{9,11},{11,1... | collective-permute-start | bytes 442376 | tf_op jit(solution)/shard_map/ppermute | solution.py:46
  43.3 3.3 %norm.1 = (bf16[512,1536]{1,0:T(8,128)(2,1)S(1)}, bf16[512,1536]{1,0:T(8,128)(2,1)S(1)}, f32[512,128]{1,0:T(8,128)S(1)}, f32[512,128]{1,0:T(8,128)S(1)}, f32[512...) custom-call(s32[1,4]{1,0:T(1,128)S(1)} %bitcast.5, ...), custom_call_target="tpu_custom_call" | custom-call | tf_op jit(solution)/shard_map/norm/pallas_call | solution.py:511
  46.7 0.3 collective-permute-start.13
  47.0 0.5 collective-permute-done.14.refs_11_
  47.5 2.4 %collective-permute-done.15.refs_12_ = bf16[2,96,384]{2,1,0:T(8,128)(2,1)S(1)} collective-permute-done((bf16[2,96,384]{2,1,0:T(8,128)(2,1)S(1)}, bf16[2,96,384]{2,1,0:T(8,128)(2,1)S(1)}, u32[]{:S(2)}, u32[]{:S(2)}) %collective-permute-start.15) | collective-permute-done | bytes 147488 | tf_op jit(solution)/shard_map/ppermute | solution.py:46
  50.0 2.8 %step0a.1 = (bf16[768,128]{1,0:T(8,128)(2,1)S(1)}, bf16[512,256]{1,0:T(8,128)(2,1)S(1)}, bf16[1536,384]{1,0:T(8,128)(2,1)S(1)}) custom-call(f32[1,16]{1,0:T(1,128)S(1)} %copy-done.8, s32[1,4]{1,0:T(1,128)S(1)} %bitcast.6, f32[1,1536]{1,0:T(1,128)S(1)} %copy-done.1, f32[1,1536]{1,0:T(1,128)S(1)} %copy-done.2, ...), custom_call_target="tpu_custom_call", output_to_operand_aliasing={{2}: (13, {})} | custom-call | flops 805306368 | bytes 1572864 | tf_op jit(solution)/shard_map/step0a/pallas_call | solution.py:511
  52.7 1.6 %collective-permute-start.16 = (bf16[768,128]{1,0:T(8,128)(2,1)S(1)}, bf16[768,128]{1,0:T(8,128)(2,1)S(1)}, u32[]{:S(2)}, u32[]{:S(2)}) collective-permute-start(bf16[768,128]{1,0:T(8,128)(2,1)S(1)} %get-tuple-element.59), channel_id=1, source_target_pairs={{0,16},{16,0},{1,17},{17,1},{2,18},{18,2},{3,19},{19,3},{4,20},{20... | collective-permute-start | bytes 589832 | tf_op jit(solution)/shard_map/ppermute | solution.py:31
  54.4 2.7 %step1a.1 = (bf16[768,128]{1,0:T(8,128)(2,1)S(1)}, bf16[512,256]{1,0:T(8,128)(2,1)S(1)}) custom-call(f32[1,16]{1,0:T(1,128)S(1)} %copy-done.8, s32[1,4]{1,0:T(1,128)S(1)} %bitcast.7, f32[1,1536]{1,0:T(1,128)S(1)} %copy-done.1, f32[1,1536]{1,0:T(1,128)S(1)} %copy-done.2, f32[1,1536]{1,0:T(1,128)S(1)} %copy-done.4, s32[4,1,512]{2,1,0:T(1,128)S(1)} %copy-done.3, ...), custom_call_target="tpu_custom_call" | custom-call | flops 805306368 | bytes 1572864 | tf_op jit(solution)/shard_map/step1a/pallas_call | solution.py:511
  57.0 1.9 %collective-permute-done.16.refs_1_.refs_10_ = bf16[768,128]{1,0:T(8,128)(2,1)S(1)} collective-permute-done((bf16[768,128]{1,0:T(8,128)(2,1)S(1)}, bf16[768,128]{1,0:T(8,128)(2,1)S(1)}, u32[]{:S(2)}, u32[]{:S(2)}) %collective-permute-start.16) | collective-permute-done | bytes 196640 | tf_op jit(solution)/shard_map/ppermute | solution.py:31
  59.0 2.8 %step0b.1 = (bf16[768,128]{1,0:T(8,128)(2,1)S(1)}, bf16[4,128,384]{2,1,0:T(8,128)(2,1)S(1)}, bf16[1536,384]{1,0:T(8,128)(2,1)S(1)}) custom-call(f32[1,16]{1,0:T(1,128)S(1)} %copy-done.8, s32[1,4]{1,0:T(1,128)S(1)} %bitcast.8, f32[1,1536]{1,0:T(1,128)S(1)} %copy-done.1, f32[1,1536]{1,0:T(1,128)S(1)} %copy-done.2, ...), custom_call_target="tpu_custom_call", output_to_operand_aliasing={{2}: (11, {})} | custom-call | flops 805306368 | bytes 1572864 | tf_op jit(solution)/shard_map/step0b/pallas_call | solution.py:511
  61.8 0.1 beside.1
  62.0 1.6 %collective-permute-start.21 = (bf16[768,128]{1,0:T(8,128)(2,1)S(1)}, bf16[768,128]{1,0:T(8,128)(2,1)S(1)}, u32[]{:S(2)}, u32[]{:S(2)}) collective-permute-start(bf16[768,128]{1,0:T(8,128)(2,1)S(1)} %get-tuple-element.68), channel_id=1, source_target_pairs={{0,16},{16,0},{1,17},{17,1},{2,18},{18,2},{3,19},{19,3},{4,20},{20... | collective-permute-start | bytes 589832 | tf_op jit(solution)/shard_map/ppermute | solution.py:31
  63.6 0.5 collective-permute-start.25
  64.1 1.5 %collective-permute-start.18 = (bf16[768,128]{1,0:T(8,128)(2,1)S(1)}, bf16[768,128]{1,0:T(8,128)(2,1)S(1)}, u32[]{:S(2)}, u32[]{:S(2)}) collective-permute-start(bf16[768,128]{1,0:T(8,128)(2,1)S(1)} %collective-permute-done.16.refs_1_.refs_10_), channel_id=1, source_target_pairs={{0,8},{4,12},{8,0},{12,4},{1,9},{5,13},{9,1},{13,5},{2,10},{6,14},... | collective-permute-start | bytes 589832 | tf_op jit(solution)/shard_map/ppermute | solution.py:27
  65.6 2.7 %step1b.1 = (bf16[768,128]{1,0:T(8,128)(2,1)S(1)}, bf16[4,128,384]{2,1,0:T(8,128)(2,1)S(1)}) custom-call(f32[1,16]{1,0:T(1,128)S(1)} %copy-done.8, s32[1,4]{1,0:T(1,128)S(1)} %bitcast.9, f32[1,1536]{1,0:T(1,128)S(1)} %copy-done.1, f32[1,1536]{1,0:T(1,128)S(1)} %copy-done.2, f32[1,1536]{1,0:T(1,128)S(1)} %copy-done.4, s32[4,1,512]{2,1,0:T(1,128)S(1)} %copy-done.3, ...), custom_call_target="tpu_custom_call" | custom-call | flops 805306368 | bytes 1572864 | tf_op jit(solution)/shard_map/step1b/pallas_call | solution.py:511
  68.3 1.5 %collective-permute-done.21.refs_0_ = bf16[768,128]{1,0:T(8,128)(2,1)S(1)} collective-permute-done((bf16[768,128]{1,0:T(8,128)(2,1)S(1)}, bf16[768,128]{1,0:T(8,128)(2,1)S(1)}, u32[]{:S(2)}, u32[]{:S(2)}) %collective-permute-start.21) | collective-permute-done | bytes 196640 | tf_op jit(solution)/shard_map/ppermute | solution.py:31
  69.8 1.5 %collective-permute-start.22 = (bf16[768,128]{1,0:T(8,128)(2,1)S(1)}, bf16[768,128]{1,0:T(8,128)(2,1)S(1)}, u32[]{:S(2)}, u32[]{:S(2)}) collective-permute-start(bf16[768,128]{1,0:T(8,128)(2,1)S(1)} %tie.8.refs_14_), channel_id=1, source_target_pairs={{0,8},{4,12},{8,0},{12,4},{1,9},{5,13},{9,1},{13,5},{2,10},{6,14},... | collective-permute-start | bytes 589832 | tf_op jit(solution)/shard_map/ppermute | solution.py:27
  71.2 1.5 %collective-permute-start.27 = (bf16[768,128]{1,0:T(8,128)(2,1)S(1)}, bf16[768,128]{1,0:T(8,128)(2,1)S(1)}, u32[]{:S(2)}, u32[]{:S(2)}) collective-permute-start(bf16[768,128]{1,0:T(8,128)(2,1)S(1)} %get-tuple-element.73), channel_id=1, source_target_pairs={{0,16},{16,0},{1,17},{17,1},{2,18},{18,2},{3,19},{19,3},{4,20},{20... | collective-permute-start | bytes 589832 | tf_op jit(solution)/shard_map/ppermute | solution.py:31
  72.8 0.2 collective-permute-start.20
  73.0 0.5 collective-permute-done.25.refs_0_
  73.5 2.3 %collective-permute-done.22.refs_15_ = bf16[768,128]{1,0:T(8,128)(2,1)S(1)} collective-permute-done((bf16[768,128]{1,0:T(8,128)(2,1)S(1)}, bf16[768,128]{1,0:T(8,128)(2,1)S(1)}, u32[]{:S(2)}, u32[]{:S(2)}) %collective-permute-start.22) | collective-permute-done | bytes 196640 | tf_op jit(solution)/shard_map/ppermute | solution.py:27
  75.8 1.5 %collective-permute-start.26 = (bf16[768,128]{1,0:T(8,128)(2,1)S(1)}, bf16[768,128]{1,0:T(8,128)(2,1)S(1)}, u32[]{:S(2)}, u32[]{:S(2)}) collective-permute-start(bf16[768,128]{1,0:T(8,128)(2,1)S(1)} %collective-permute-done.25.refs_0_), channel_id=1, source_target_pairs={{0,8},{4,12},{8,0},{12,4},{1,9},{5,13},{9,1},{13,5},{2,10},{6,14},... | collective-permute-start | bytes 589832 | tf_op jit(solution)/shard_map/ppermute | solution.py:27
  77.3 1.3 %collective-permute-done.27.refs_2_ = bf16[768,128]{1,0:T(8,128)(2,1)S(1)} collective-permute-done((bf16[768,128]{1,0:T(8,128)(2,1)S(1)}, bf16[768,128]{1,0:T(8,128)(2,1)S(1)}, u32[]{:S(2)}, u32[]{:S(2)}) %collective-permute-start.27) | collective-permute-done | bytes 196640 | tf_op jit(solution)/shard_map/ppermute | solution.py:31
  78.6 0.7 collective-permute-start.28
  79.2 4.9 %step2ab.1.refs_2_.refs_0_ = bf16[4,128,384]{2,1,0:T(8,128)(2,1)S(1)} custom-call(f32[1,16]{1,0:T(1,128)S(1)} %copy-done.8, s32[1,4]{1,0:T(1,128)S(1)} %bitcast.10, f32[1,1536]{1,0:T(1,128)S(1)} %copy-done.1, f32[1,1536]{1,0:T(1,128)S(1)} %copy-done.2, f32[1,1536]{1,0:T(1,128)S(1)} %copy-done.4, s32[4,1,512]{2,1,0:T(1,128)S(1)} %copy-done.3, ...), custom_call_target="tpu_custom_call" | custom-call | flops 1610612736 | bytes 3145728 | tf_op jit(solution)/shard_map/step2ab/pallas_call | solution.py:511
  84.1 0.5 early.1
  84.6 2.7 %collective-permute-done.28.refs_3_ = bf16[768,128]{1,0:T(8,128)(2,1)S(1)} collective-permute-done((bf16[768,128]{1,0:T(8,128)(2,1)S(1)}, bf16[768,128]{1,0:T(8,128)(2,1)S(1)}, u32[]{:S(2)}, u32[]{:S(2)}) %collective-permute-start.28) | collective-permute-done | bytes 196640 | tf_op jit(solution)/shard_map/ppermute | solution.py:27
  87.3 0.5 collective-permute-start.30
  87.8 0.5 collective-permute-start.32
  88.3 0.4 collective-permute-done.29.refs_12_
  88.8 1.5 %collective-permute-start.34 = (bf16[2,128,384]{2,1,0:T(8,128)(2,1)S(1)}, bf16[2,128,384]{2,1,0:T(8,128)(2,1)S(1)}, u32[]{:S(2)}, u32[]{:S(2)}) collective-permute-start(bf16[2,128,384]{2,1,0:T(8,128)(2,1)S(1)} %get-tuple-element.81), channel_id=1, source_target_pairs={{0,8},{4,12},{8,0},{12,4},{1,9},{5,13},{9,1},{13,5},{2,10},{6,14},... | collective-permute-start | bytes 589832 | tf_op jit(solution)/shard_map/ppermute | solution.py:27
  90.2 0.1 collective-permute-start.35
  90.4 4.7 %step3ab.1.refs_1_ = bf16[4,128,384]{2,1,0:T(8,128)(2,1)S(1)} custom-call(f32[1,16]{1,0:T(1,128)S(1)} %copy-done.8, s32[1,4]{1,0:T(1,128)S(1)} %bitcast.11, f32[1,1536]{1,0:T(1,128)S(1)} %copy-done.1, f32[1,1536]{1,0:T(1,128)S(1)} %copy-done.2, f32[1,1536]{1,0:T(1,128)S(1)} %copy-done.4, s32[4,1,512]{2,1,0:T(1,128)S(1)} %copy-done.3, ...), custom_call_target="tpu_custom_call" | custom-call | flops 1610612736 | bytes 3145728 | tf_op jit(solution)/shard_map/step3ab/pallas_call | solution.py:511
  95.0 0.4 share.1
  95.4 1.1 collective-permute-start.39
  96.5 1.0 settle.1
  97.5 0.3 collective-permute-start.36
  97.8 1.5 %collective-permute-start.37 = (bf16[128,384]{1,0:T(8,128)(2,1)S(1)}, bf16[128,384]{1,0:T(8,128)(2,1)S(1)}, u32[]{:S(2)}, u32[]{:S(2)}) collective-permute-start(bf16[128,384]{1,0:T(8,128)(2,1)S(1)} %get-tuple-element.86), channel_id=1, source_target_pairs={{0,8},{4,12},{8,0},{12,4},{1,9},{5,13},{9,1},{13,5},{2,10},{6,14},... | collective-permute-start | bytes 294920 | tf_op jit(solution)/shard_map/ppermute | solution.py:27
  99.3 0.1 collective-permute-start.38
  99.4 2.5 %collective-permute-start.40 = (bf16[96,256]{1,0:T(8,128)(2,1)S(1)}, bf16[96,256]{1,0:T(8,128)(2,1)S(1)}, u32[]{:S(2)}, u32[]{:S(2)}) collective-permute-start(bf16[96,256]{1,0:T(8,128)(2,1)S(1)} %get-tuple-element.90), channel_id=1, source_target_pairs={{0,2},{1,3},{2,0},{3,1},{4,6},{5,7},{6,4},{7,5},{8,10},{9,11},{10,... | collective-permute-start | bytes 147464 | tf_op jit(solution)/shard_map/ppermute | solution.py:36
  101.9 0.9 collective-permute-start.41
  102.8 3.0 %collective-permute-done.40.refs_8_ = bf16[96,256]{1,0:T(8,128)(2,1)S(1)} collective-permute-done((bf16[96,256]{1,0:T(8,128)(2,1)S(1)}, bf16[96,256]{1,0:T(8,128)(2,1)S(1)}, u32[]{:S(2)}, u32[]{:S(2)}) %collective-permute-start.40) | collective-permute-done | bytes 49184 | tf_op jit(solution)/shard_map/ppermute | solution.py:36
  105.8 0.6 collective-permute-done.41.refs_9_
  106.4 1.5 %finish.1 = (bf16[3,128,1536]{2,1,0:T(8,128)(2,1)}, f32[96,256]{1,0:T(8,128)}) custom-call(bf16[3,128,1536]{2,1,0:T(8,128)(2,1)} %get-tuple-element.82.refs_0_, bf16[2,128,384]{2,1,0:T(8,128)(2,1)S(1)} %collective-permute-done.35.refs_1_, bf16[128,384]{1,0:T(8,128)(2,1)S(1)} %get-tuple-element.84.refs_2_, ...), custom_call_target="tpu_custom_call", output_to_operand_aliasing={{0}: (0, {})} | custom-call | tf_op jit(solution)/shard_map/finish/pallas_call | solution.py:511
  (66 shorter events, 0.7 us)
Async XLA Ops:
  0.6 14.4 %copy-start = (bf16[1,3,1,128,1536]{4,3,2,1,0:T(8,128)(2,1)S(1)}, bf16[1,3,1,128,1536]{4,3,2,1,0:T(8,128)(2,1)}, u32[]{:S(2)}) copy-start(bf16[1,3,1,128,1536]{4,3,2,1,0:T(8,128)(2,1)} %incoming.3) | copy-start | bytes 3538948
  0.6 14.4 %copy-start.9 = (s32[4,1,128]{2,1,0:T(1,128)S(1)}, s32[4,1,128]{2,1,0:T(1,128)}, u32[]{:S(2)}) copy-start(s32[4,1,128]{2,1,0:T(1,128)} %contacts.1) | copy-start | bytes 6148
  2.1 1.5 %collective-permute-start = (bf16[2,96,384]{2,1,0:T(8,128)(2,1)S(1)}, bf16[2,96,384]{2,1,0:T(8,128)(2,1)S(1)}, u32[]{:S(2)}, u32[]{:S(2)}) collective-permute-start(bf16[2,96,384]{2,1,0:T(8,128)(2,1)S(1)} %get-tuple-element.49), channel_id=1, source_target_pairs={{0,4},{4,0},{8,12},{12,8},{1,5},{5,1},{9,13},{13,9},{2,6},{6,2},{1... | collective-permute-start | bytes 442376 | tf_op jit(solution)/shard_map/ppermute | solution.py:27
  3.7 11.3 %collective-permute-start.1 = (bf16[2,2,96,384]{3,2,1,0:T(8,128)(2,1)S(1)}, bf16[2,2,96,384]{3,2,1,0:T(8,128)(2,1)S(1)}, u32[]{:S(2)}, u32[]{:S(2)}) collective-permute-start(bf16[2,2,96,384]{3,2,1,0:T(8,128)(2,1)S(1)} %near.1), channel_id=1, source_target_pairs={{0,1},{1,3},{3,2},{2,0},{4,5},{5,7},{7,6},{6,4},{8,9},{9,11},{11,1... | collective-permute-start | bytes 884744 | tf_op jit(solution)/shard_map/ppermute | solution.py:46
  6.7 6.7 %collective-permute-start.2 = (bf16[2,96,384]{2,1,0:T(8,128)(2,1)S(1)}, bf16[2,96,384]{2,1,0:T(8,128)(2,1)S(1)}, u32[]{:S(2)}, u32[]{:S(2)}) collective-permute-start(bf16[2,96,384]{2,1,0:T(8,128)(2,1)S(1)} %get-tuple-element.50), channel_id=1, source_target_pairs={{0,8},{4,12},{8,0},{12,4},{1,9},{5,13},{9,1},{13,5},{2,10},{6,14},... | collective-permute-start | bytes 442376 | tf_op jit(solution)/shard_map/ppermute | solution.py:27
  8.2 6.3 %collective-permute-start.3 = (bf16[2,96,384]{2,1,0:T(8,128)(2,1)S(1)}, bf16[2,96,384]{2,1,0:T(8,128)(2,1)S(1)}, u32[]{:S(2)}, u32[]{:S(2)}) collective-permute-start(bf16[2,96,384]{2,1,0:T(8,128)(2,1)S(1)} %get-tuple-element.51), channel_id=1, source_target_pairs={{0,12},{4,8},{8,4},{12,0},{1,13},{5,9},{9,5},{13,1},{2,14},{6,10},... | collective-permute-start | bytes 442376 | tf_op jit(solution)/shard_map/ppermute | solution.py:27
  15.1 24.0 %collective-permute-start.4 = (bf16[272,1536]{1,0:T(8,128)(2,1)S(1)}, bf16[272,1536]{1,0:T(8,128)(2,1)S(1)}, u32[]{:S(2)}, u32[]{:S(2)}) collective-permute-start(bf16[272,1536]{1,0:T(8,128)(2,1)S(1)} %first.1.refs_0_), channel_id=1, source_target_pairs={{0,8},{4,12},{8,0},{12,4},{1,9},{5,13},{9,1},{13,5},{2,10},{6,14},... | collective-permute-start | bytes 2506760 | tf_op jit(solution)/shard_map/ppermute | solution.py:27
  16.7 7.4 %collective-permute-start.8 = (bf16[2,96,384]{2,1,0:T(8,128)(2,1)S(1)}, bf16[2,96,384]{2,1,0:T(8,128)(2,1)S(1)}, u32[]{:S(2)}, u32[]{:S(2)}) collective-permute-start(bf16[2,96,384]{2,1,0:T(8,128)(2,1)S(1)} %get-tuple-element.55.far), channel_id=1, source_target_pairs={{0,1},{1,3},{3,2},{2,0},{4,5},{5,7},{7,6},{6,4},{8,9},{9,11},{11,1... | collective-permute-start | bytes 442376 | tf_op jit(solution)/shard_map/ppermute | solution.py:46
  18.6 8.3 %collective-permute-start.5 = (bf16[2,96,384]{2,1,0:T(8,128)(2,1)S(1)}, bf16[2,96,384]{2,1,0:T(8,128)(2,1)S(1)}, u32[]{:S(2)}, u32[]{:S(2)}) collective-permute-start(bf16[2,96,384]{2,1,0:T(8,128)(2,1)S(1)} %get-tuple-element.52.far), channel_id=1, source_target_pairs={{0,1},{1,3},{3,2},{2,0},{4,5},{5,7},{7,6},{6,4},{8,9},{9,11},{11,1... | collective-permute-start | bytes 442376 | tf_op jit(solution)/shard_map/ppermute | solution.py:46
  24.2 15.0 %collective-permute-start.9 = (bf16[4,96,384]{2,1,0:T(8,128)(2,1)S(1)}, bf16[4,96,384]{2,1,0:T(8,128)(2,1)S(1)}, u32[]{:S(2)}, u32[]{:S(2)}) collective-permute-start(bf16[4,96,384]{2,1,0:T(8,128)(2,1)S(1)} %part1.1.refs_0_), channel_id=1, source_target_pairs={{0,1},{1,3},{3,2},{2,0},{4,5},{5,7},{7,6},{6,4},{8,9},{9,11},{11,1... | collective-permute-start | bytes 884744 | tf_op jit(solution)/shard_map/ppermute | solution.py:46
  27.0 12.3 %copy-start.5 = (bf16[1,3,1,128,256]{4,3,2,1,0:T(8,128)(2,1)S(1)}, bf16[1,3,1,128,256]{4,3,2,1,0:T(8,128)(2,1)}, u32[]{:S(2)}) copy-start(bf16[1,3,1,128,256]{4,3,2,1,0:T(8,128)(2,1)} %cotangent.1) | copy-start | bytes 589828
  27.0 10.6 %collective-permute-start.6 = (bf16[2,96,384]{2,1,0:T(8,128)(2,1)S(1)}, bf16[2,96,384]{2,1,0:T(8,128)(2,1)S(1)}, u32[]{:S(2)}, u32[]{:S(2)}) collective-permute-start(bf16[2,96,384]{2,1,0:T(8,128)(2,1)S(1)} %get-tuple-element.53.refs_0_), channel_id=1, source_target_pairs={{0,1},{1,3},{3,2},{2,0},{4,5},{5,7},{7,6},{6,4},{8,9},{9,11},{11,1... | collective-permute-start | bytes 442376 | tf_op jit(solution)/shard_map/ppermute | solution.py:46
  28.6 10.5 %collective-permute-start.7 = (bf16[2,96,384]{2,1,0:T(8,128)(2,1)S(1)}, bf16[2,96,384]{2,1,0:T(8,128)(2,1)S(1)}, u32[]{:S(2)}, u32[]{:S(2)}) collective-permute-start(bf16[2,96,384]{2,1,0:T(8,128)(2,1)S(1)} %get-tuple-element.54.refs_1_), channel_id=1, source_target_pairs={{0,1},{1,3},{3,2},{2,0},{4,5},{5,7},{7,6},{6,4},{8,9},{9,11},{11,1... | collective-permute-start | bytes 442376 | tf_op jit(solution)/shard_map/ppermute | solution.py:46
  31.0 12.3 %collective-permute-start.11 = (bf16[272,1536]{1,0:T(8,128)(2,1)S(1)}, bf16[272,1536]{1,0:T(8,128)(2,1)S(1)}, u32[]{:S(2)}, u32[]{:S(2)}) collective-permute-start(bf16[272,1536]{1,0:T(8,128)(2,1)S(1)} %first.1.refs_0_), channel_id=1, source_target_pairs={{0,4},{4,0},{8,12},{12,8},{1,5},{5,1},{9,13},{13,9},{2,6},{6,2},{1... | collective-permute-start | bytes 2506760 | tf_op jit(solution)/shard_map/ppermute | solution.py:27
  39.2 4.1 %copy-start.1 = (f32[1,1536]{1,0:T(1,128)S(1)}, f32[1,1536]{1,0:T(1,128)}, u32[]{:S(2)}) copy-start(f32[1,1536]{1,0:T(1,128)} %refs_2_.11) | copy-start | bytes 18436
  39.2 4.1 %copy-start.2 = (f32[1,1536]{1,0:T(1,128)S(1)}, f32[1,1536]{1,0:T(1,128)}, u32[]{:S(2)}) copy-start(f32[1,1536]{1,0:T(1,128)} %refs_3_.11) | copy-start | bytes 18436
  39.2 4.1 %copy-start.6 = (bf16[1,16,1536]{2,1,0:T(8,128)(2,1)S(1)}, bf16[1,16,1536]{2,1,0:T(8,128)(2,1)}, u32[]{:S(2)}) copy-start(bf16[1,16,1536]{2,1,0:T(8,128)(2,1)} %table.1) | copy-start | bytes 147460
  39.2 4.1 %copy-start.7 = (s32[4,1]{0,1:T(1,128)S(1)}, s32[4,1]{0,1:T(1,128)}, u32[]{:S(2)}) copy-start(s32[4,1]{0,1:T(1,128)} %param.15) | copy-start | bytes 52
  39.2 4.1 %collective-permute-start.12 = (bf16[272,1536]{1,0:T(8,128)(2,1)S(1)}, bf16[272,1536]{1,0:T(8,128)(2,1)S(1)}, u32[]{:S(2)}, u32[]{:S(2)}) collective-permute-start(bf16[272,1536]{1,0:T(8,128)(2,1)S(1)} %tie.5.dep.refs_1_), channel_id=1, source_target_pairs={{0,4},{4,0},{8,12},{12,8},{1,5},{5,1},{9,13},{13,9},{2,6},{6,2},{1... | collective-permute-start | bytes 2506760 | tf_op jit(solution)/shard_map/ppermute | solution.py:27
  39.3 22.5 %collective-permute-start.10 = (bf16[256,1536]{1,0:T(8,128)(2,1)S(1)}, bf16[256,1536]{1,0:T(8,128)(2,1)S(1)}, u32[]{:S(2)}, u32[]{:S(2)}) collective-permute-start(bf16[256,1536]{1,0:T(8,128)(2,1)S(1)} %second.1.mine.refs_6_.refs_3_.refs_2_), channel_id=1, source_target_pairs={{0,8},{4,12},{8,0},{12,4},{1,9},{5,13},{9,1},{13,5},{2,10},{6,14},... | collective-permute-start | bytes 2359304 | tf_op jit(solution)/shard_map/ppermute | solution.py:27
  39.9 7.6 %collective-permute-start.14 = (bf16[2,96,384]{2,1,0:T(8,128)(2,1)S(1)}, bf16[2,96,384]{2,1,0:T(8,128)(2,1)S(1)}, u32[]{:S(2)}, u32[]{:S(2)}) collective-permute-start(bf16[2,96,384]{2,1,0:T(8,128)(2,1)S(1)} %collective-permute-done.6.refs_1_.refs_9_), channel_id=1, source_target_pairs={{0,1},{1,3},{3,2},{2,0},{4,5},{5,7},{7,6},{6,4},{8,9},{9,11},{11,1... | collective-permute-start | bytes 442376 | tf_op jit(solution)/shard_map/ppermute | solution.py:46
  41.6 8.3 %collective-permute-start.15 = (bf16[2,96,384]{2,1,0:T(8,128)(2,1)S(1)}, bf16[2,96,384]{2,1,0:T(8,128)(2,1)S(1)}, u32[]{:S(2)}, u32[]{:S(2)}) collective-permute-start(bf16[2,96,384]{2,1,0:T(8,128)(2,1)S(1)} %collective-permute-done.7.refs_2_.refs_10_), channel_id=1, source_target_pairs={{0,1},{1,3},{3,2},{2,0},{4,5},{5,7},{7,6},{6,4},{8,9},{9,11},{11,1... | collective-permute-start | bytes 442376 | tf_op jit(solution)/shard_map/ppermute | solution.py:46
  46.7 3.3 %copy-start.3 = (s32[4,1,512]{2,1,0:T(1,128)S(1)}, s32[4,1,512]{2,1,0:T(1,128)}, u32[]{:S(2)}) copy-start(s32[4,1,512]{2,1,0:T(1,128)} %refs_5_.11) | copy-start | bytes 24580
  46.7 3.3 %copy-start.4 = (f32[1,1536]{1,0:T(1,128)S(1)}, f32[1,1536]{1,0:T(1,128)}, u32[]{:S(2)}) copy-start(f32[1,1536]{1,0:T(1,128)} %refs_4_.11) | copy-start | bytes 18436
  46.7 3.3 %copy-start.8 = (f32[1,16]{1,0:T(1,128)S(1)}, f32[1,16]{1,0:T(1,128)}, u32[]{:S(2)}) copy-start(f32[1,16]{1,0:T(1,128)} %refs_0_.11) | copy-start | bytes 196
  46.7 12.3 %collective-permute-start.13 = (bf16[4,96,384]{2,1,0:T(8,128)(2,1)S(1)}, bf16[4,96,384]{2,1,0:T(8,128)(2,1)S(1)}, u32[]{:S(2)}, u32[]{:S(2)}) collective-permute-start(bf16[4,96,384]{2,1,0:T(8,128)(2,1)S(1)} %tie.6.refs_9_), channel_id=1, source_target_pairs={{0,1},{1,3},{3,2},{2,0},{4,5},{5,7},{7,6},{6,4},{8,9},{9,11},{11,1... | collective-permute-start | bytes 884744 | tf_op jit(solution)/shard_map/ppermute | solution.py:46
  52.7 6.3 %collective-permute-start.16 = (bf16[768,128]{1,0:T(8,128)(2,1)S(1)}, bf16[768,128]{1,0:T(8,128)(2,1)S(1)}, u32[]{:S(2)}, u32[]{:S(2)}) collective-permute-start(bf16[768,128]{1,0:T(8,128)(2,1)S(1)} %get-tuple-element.59), channel_id=1, source_target_pairs={{0,16},{16,0},{1,17},{17,1},{2,18},{18,2},{3,19},{19,3},{4,20},{20... | collective-permute-start | bytes 589832 | tf_op jit(solution)/shard_map/ppermute | solution.py:31
  61.9 7.8 %collective-permute-start.17 = (bf16[2,256,1536]{2,1,0:T(8,128)(2,1)S(1)}, bf16[2,256,1536]{2,1,0:T(8,128)(2,1)S(1)}, u32[]{:S(2)}, u32[]{:S(2)}) collective-permute-start(bf16[2,256,1536]{2,1,0:T(8,128)(2,1)S(1)} %beside.1), channel_id=1, source_target_pairs={{0,4},{4,0},{8,12},{12,8},{1,5},{5,1},{9,13},{13,9},{2,6},{6,2},{1... | collective-permute-start | bytes 4718600 | tf_op jit(solution)/shard_map/ppermute | solution.py:27
  62.0 7.8 %collective-permute-start.21 = (bf16[768,128]{1,0:T(8,128)(2,1)S(1)}, bf16[768,128]{1,0:T(8,128)(2,1)S(1)}, u32[]{:S(2)}, u32[]{:S(2)}) collective-permute-start(bf16[768,128]{1,0:T(8,128)(2,1)S(1)} %get-tuple-element.68), channel_id=1, source_target_pairs={{0,16},{16,0},{1,17},{17,1},{2,18},{18,2},{3,19},{19,3},{4,20},{20... | collective-permute-start | bytes 589832 | tf_op jit(solution)/shard_map/ppermute | solution.py:31
  63.6 9.9 %collective-permute-start.25 = (bf16[768,128]{1,0:T(8,128)(2,1)S(1)}, bf16[768,128]{1,0:T(8,128)(2,1)S(1)}, u32[]{:S(2)}, u32[]{:S(2)}) collective-permute-start(bf16[768,128]{1,0:T(8,128)(2,1)S(1)} %get-tuple-element.72), channel_id=1, source_target_pairs={{0,16},{16,0},{1,17},{17,1},{2,18},{18,2},{3,19},{19,3},{4,20},{20... | collective-permute-start | bytes 589832 | tf_op jit(solution)/shard_map/ppermute | solution.py:31
  64.1 8.7 %collective-permute-start.18 = (bf16[768,128]{1,0:T(8,128)(2,1)S(1)}, bf16[768,128]{1,0:T(8,128)(2,1)S(1)}, u32[]{:S(2)}, u32[]{:S(2)}) collective-permute-start(bf16[768,128]{1,0:T(8,128)(2,1)S(1)} %collective-permute-done.16.refs_1_.refs_10_), channel_id=1, source_target_pairs={{0,8},{4,12},{8,0},{12,4},{1,9},{5,13},{9,1},{13,5},{2,10},{6,14},... | collective-permute-start | bytes 589832 | tf_op jit(solution)/shard_map/ppermute | solution.py:27
  69.8 6.0 %collective-permute-start.22 = (bf16[768,128]{1,0:T(8,128)(2,1)S(1)}, bf16[768,128]{1,0:T(8,128)(2,1)S(1)}, u32[]{:S(2)}, u32[]{:S(2)}) collective-permute-start(bf16[768,128]{1,0:T(8,128)(2,1)S(1)} %tie.8.refs_14_), channel_id=1, source_target_pairs={{0,8},{4,12},{8,0},{12,4},{1,9},{5,13},{9,1},{13,5},{2,10},{6,14},... | collective-permute-start | bytes 589832 | tf_op jit(solution)/shard_map/ppermute | solution.py:27
  71.2 4.5 %collective-permute-start.19 = (bf16[768,128]{1,0:T(8,128)(2,1)S(1)}, bf16[768,128]{1,0:T(8,128)(2,1)S(1)}, u32[]{:S(2)}, u32[]{:S(2)}) collective-permute-start(bf16[768,128]{1,0:T(8,128)(2,1)S(1)} %collective-permute-done.16.refs_1_.refs_10_), channel_id=1, source_target_pairs={{0,4},{4,0},{8,12},{12,8},{1,5},{5,1},{9,13},{13,9},{2,6},{6,2},{1... | collective-permute-start | bytes 589832 | tf_op jit(solution)/shard_map/ppermute | solution.py:27
  71.2 7.3 %collective-permute-start.27 = (bf16[768,128]{1,0:T(8,128)(2,1)S(1)}, bf16[768,128]{1,0:T(8,128)(2,1)S(1)}, u32[]{:S(2)}, u32[]{:S(2)}) collective-permute-start(bf16[768,128]{1,0:T(8,128)(2,1)S(1)} %get-tuple-element.73), channel_id=1, source_target_pairs={{0,16},{16,0},{1,17},{17,1},{2,18},{18,2},{3,19},{19,3},{4,20},{20... | collective-permute-start | bytes 589832 | tf_op jit(solution)/shard_map/ppermute | solution.py:31
  72.8 6.5 %collective-permute-start.20 = (bf16[768,128]{1,0:T(8,128)(2,1)S(1)}, bf16[768,128]{1,0:T(8,128)(2,1)S(1)}, u32[]{:S(2)}, u32[]{:S(2)}) collective-permute-start(bf16[768,128]{1,0:T(8,128)(2,1)S(1)} %collective-permute-done.18.refs_11_), channel_id=1, source_target_pairs={{0,4},{4,0},{8,12},{12,8},{1,5},{5,1},{9,13},{13,9},{2,6},{6,2},{1... | collective-permute-start | bytes 589832 | tf_op jit(solution)/shard_map/ppermute | solution.py:27
  73.5 5.7 %collective-permute-start.23 = (bf16[768,128]{1,0:T(8,128)(2,1)S(1)}, bf16[768,128]{1,0:T(8,128)(2,1)S(1)}, u32[]{:S(2)}, u32[]{:S(2)}) collective-permute-start(bf16[768,128]{1,0:T(8,128)(2,1)S(1)} %tie.8.refs_14_), channel_id=1, source_target_pairs={{0,4},{4,0},{8,12},{12,8},{1,5},{5,1},{9,13},{13,9},{2,6},{6,2},{1... | collective-permute-start | bytes 589832 | tf_op jit(solution)/shard_map/ppermute | solution.py:27
  75.8 3.5 %collective-permute-start.24 = (bf16[768,128]{1,0:T(8,128)(2,1)S(1)}, bf16[768,128]{1,0:T(8,128)(2,1)S(1)}, u32[]{:S(2)}, u32[]{:S(2)}) collective-permute-start(bf16[768,128]{1,0:T(8,128)(2,1)S(1)} %collective-permute-done.22.refs_15_), channel_id=1, source_target_pairs={{0,4},{4,0},{8,12},{12,8},{1,5},{5,1},{9,13},{13,9},{2,6},{6,2},{1... | collective-permute-start | bytes 589832 | tf_op jit(solution)/shard_map/ppermute | solution.py:27
  75.8 8.9 %collective-permute-start.26 = (bf16[768,128]{1,0:T(8,128)(2,1)S(1)}, bf16[768,128]{1,0:T(8,128)(2,1)S(1)}, u32[]{:S(2)}, u32[]{:S(2)}) collective-permute-start(bf16[768,128]{1,0:T(8,128)(2,1)S(1)} %collective-permute-done.25.refs_0_), channel_id=1, source_target_pairs={{0,8},{4,12},{8,0},{12,4},{1,9},{5,13},{9,1},{13,5},{2,10},{6,14},... | collective-permute-start | bytes 589832 | tf_op jit(solution)/shard_map/ppermute | solution.py:27
  78.6 8.7 %collective-permute-start.28 = (bf16[768,128]{1,0:T(8,128)(2,1)S(1)}, bf16[768,128]{1,0:T(8,128)(2,1)S(1)}, u32[]{:S(2)}, u32[]{:S(2)}) collective-permute-start(bf16[768,128]{1,0:T(8,128)(2,1)S(1)} %collective-permute-done.27.refs_2_), channel_id=1, source_target_pairs={{0,8},{4,12},{8,0},{12,4},{1,9},{5,13},{9,1},{13,5},{2,10},{6,14},... | collective-permute-start | bytes 589832 | tf_op jit(solution)/shard_map/ppermute | solution.py:27
  87.3 1.4 %collective-permute-start.29 = (bf16[768,128]{1,0:T(8,128)(2,1)S(1)}, bf16[768,128]{1,0:T(8,128)(2,1)S(1)}, u32[]{:S(2)}, u32[]{:S(2)}) collective-permute-start(bf16[768,128]{1,0:T(8,128)(2,1)S(1)} %get-tuple-element.75.refs_10_), channel_id=1, source_target_pairs={{0,4},{4,0},{8,12},{12,8},{1,5},{5,1},{9,13},{13,9},{2,6},{6,2},{1... | collective-permute-start | bytes 589832 | tf_op jit(solution)/shard_map/ppermute | solution.py:27
  87.3 2.9 %collective-permute-start.30 = (bf16[768,128]{1,0:T(8,128)(2,1)S(1)}, bf16[768,128]{1,0:T(8,128)(2,1)S(1)}, u32[]{:S(2)}, u32[]{:S(2)}) collective-permute-start(bf16[768,128]{1,0:T(8,128)(2,1)S(1)} %get-tuple-element.76.refs_11_), channel_id=1, source_target_pairs={{0,4},{4,0},{8,12},{12,8},{1,5},{5,1},{9,13},{13,9},{2,6},{6,2},{1... | collective-permute-start | bytes 589832 | tf_op jit(solution)/shard_map/ppermute | solution.py:27
  87.8 2.5 %collective-permute-start.31 = (bf16[768,128]{1,0:T(8,128)(2,1)S(1)}, bf16[768,128]{1,0:T(8,128)(2,1)S(1)}, u32[]{:S(2)}, u32[]{:S(2)}) collective-permute-start(bf16[768,128]{1,0:T(8,128)(2,1)S(1)} %get-tuple-element.77.refs_14_), channel_id=1, source_target_pairs={{0,4},{4,0},{8,12},{12,8},{1,5},{5,1},{9,13},{13,9},{2,6},{6,2},{1... | collective-permute-start | bytes 589832 | tf_op jit(solution)/shard_map/ppermute | solution.py:27
  87.8 2.5 %collective-permute-start.32 = (bf16[768,128]{1,0:T(8,128)(2,1)S(1)}, bf16[768,128]{1,0:T(8,128)(2,1)S(1)}, u32[]{:S(2)}, u32[]{:S(2)}) collective-permute-start(bf16[768,128]{1,0:T(8,128)(2,1)S(1)} %get-tuple-element.78.refs_15_), channel_id=1, source_target_pairs={{0,4},{4,0},{8,12},{12,8},{1,5},{5,1},{9,13},{13,9},{2,6},{6,2},{1... | collective-permute-start | bytes 589832 | tf_op jit(solution)/shard_map/ppermute | solution.py:27
  88.3 8.1 %collective-permute-start.33 = (bf16[2,128,384]{2,1,0:T(8,128)(2,1)S(1)}, bf16[2,128,384]{2,1,0:T(8,128)(2,1)S(1)}, u32[]{:S(2)}, u32[]{:S(2)}) collective-permute-start(bf16[2,128,384]{2,1,0:T(8,128)(2,1)S(1)} %get-tuple-element.80), channel_id=1, source_target_pairs={{0,4},{4,0},{8,12},{12,8},{1,5},{5,1},{9,13},{13,9},{2,6},{6,2},{1... | collective-permute-start | bytes 589832 | tf_op jit(solution)/shard_map/ppermute | solution.py:27
  88.8 7.7 %collective-permute-start.34 = (bf16[2,128,384]{2,1,0:T(8,128)(2,1)S(1)}, bf16[2,128,384]{2,1,0:T(8,128)(2,1)S(1)}, u32[]{:S(2)}, u32[]{:S(2)}) collective-permute-start(bf16[2,128,384]{2,1,0:T(8,128)(2,1)S(1)} %get-tuple-element.81), channel_id=1, source_target_pairs={{0,8},{4,12},{8,0},{12,4},{1,9},{5,13},{9,1},{13,5},{2,10},{6,14},... | collective-permute-start | bytes 589832 | tf_op jit(solution)/shard_map/ppermute | solution.py:27
  90.2 9.2 %collective-permute-start.35 = (bf16[2,128,384]{2,1,0:T(8,128)(2,1)S(1)}, bf16[2,128,384]{2,1,0:T(8,128)(2,1)S(1)}, u32[]{:S(2)}, u32[]{:S(2)}) collective-permute-start(bf16[2,128,384]{2,1,0:T(8,128)(2,1)S(1)} %get-tuple-element.83), channel_id=1, source_target_pairs={{0,12},{4,8},{8,4},{12,0},{1,13},{5,9},{9,5},{13,1},{2,14},{6,10},... | collective-permute-start | bytes 589832 | tf_op jit(solution)/shard_map/ppermute | solution.py:27
  95.4 6.5 %collective-permute-start.39 = (bf16[96,256]{1,0:T(8,128)(2,1)S(1)}, bf16[96,256]{1,0:T(8,128)(2,1)S(1)}, u32[]{:S(2)}, u32[]{:S(2)}) collective-permute-start(bf16[96,256]{1,0:T(8,128)(2,1)S(1)} %get-tuple-element.89), channel_id=1, source_target_pairs={{0,1},{1,2},{2,3},{3,0},{4,5},{5,6},{6,7},{7,4},{8,9},{9,10},{10,1... | collective-permute-start | bytes 147464 | tf_op jit(solution)/shard_map/ppermute | solution.py:36
  97.5 8.9 %collective-permute-start.36 = (bf16[128,384]{1,0:T(8,128)(2,1)S(1)}, bf16[128,384]{1,0:T(8,128)(2,1)S(1)}, u32[]{:S(2)}, u32[]{:S(2)}) collective-permute-start(bf16[128,384]{1,0:T(8,128)(2,1)S(1)} %get-tuple-element.85), channel_id=1, source_target_pairs={{0,4},{4,0},{8,12},{12,8},{1,5},{5,1},{9,13},{13,9},{2,6},{6,2},{1... | collective-permute-start | bytes 294920 | tf_op jit(solution)/shard_map/ppermute | solution.py:27
  97.8 8.6 %collective-permute-start.37 = (bf16[128,384]{1,0:T(8,128)(2,1)S(1)}, bf16[128,384]{1,0:T(8,128)(2,1)S(1)}, u32[]{:S(2)}, u32[]{:S(2)}) collective-permute-start(bf16[128,384]{1,0:T(8,128)(2,1)S(1)} %get-tuple-element.86), channel_id=1, source_target_pairs={{0,8},{4,12},{8,0},{12,4},{1,9},{5,13},{9,1},{13,5},{2,10},{6,14},... | collective-permute-start | bytes 294920 | tf_op jit(solution)/shard_map/ppermute | solution.py:27
  99.3 7.2 %collective-permute-start.38 = (bf16[128,384]{1,0:T(8,128)(2,1)S(1)}, bf16[128,384]{1,0:T(8,128)(2,1)S(1)}, u32[]{:S(2)}, u32[]{:S(2)}) collective-permute-start(bf16[128,384]{1,0:T(8,128)(2,1)S(1)} %get-tuple-element.87), channel_id=1, source_target_pairs={{0,12},{4,8},{8,4},{12,0},{1,13},{5,9},{9,5},{13,1},{2,14},{6,10},... | collective-permute-start | bytes 294920 | tf_op jit(solution)/shard_map/ppermute | solution.py:27
  99.4 6.4 %collective-permute-start.40 = (bf16[96,256]{1,0:T(8,128)(2,1)S(1)}, bf16[96,256]{1,0:T(8,128)(2,1)S(1)}, u32[]{:S(2)}, u32[]{:S(2)}) collective-permute-start(bf16[96,256]{1,0:T(8,128)(2,1)S(1)} %get-tuple-element.90), channel_id=1, source_target_pairs={{0,2},{1,3},{2,0},{3,1},{4,6},{5,7},{6,4},{7,5},{8,10},{9,11},{10,... | collective-permute-start | bytes 147464 | tf_op jit(solution)/shard_map/ppermute | solution.py:36
  101.9 4.5 %collective-permute-start.41 = (bf16[96,256]{1,0:T(8,128)(2,1)S(1)}, bf16[96,256]{1,0:T(8,128)(2,1)S(1)}, u32[]{:S(2)}, u32[]{:S(2)}) collective-permute-start(bf16[96,256]{1,0:T(8,128)(2,1)S(1)} %get-tuple-element.91), channel_id=1, source_target_pairs={{0,3},{1,0},{2,1},{3,2},{4,7},{5,4},{6,5},{7,6},{8,11},{9,8},{10,9... | collective-permute-start | bytes 147464 | tf_op jit(solution)/shard_map/ppermute | solution.py:36

commit v21 on v20

--- a/solution.py
+++ b/solution.py
@@ -548,6 +548,17 @@
             out_specs=vmem,
         )
 
+    def tie(values, deps):
+        return call(
+            tie_kernel,
+            "tie",
+            [shape(value.shape, kind) for value in values],
+            [anywhere] * (len(values) + len(deps)),
+            list(values) + list(deps),
+            out_specs=[anywhere] * len(values),
+            input_output_aliases={i: i for i in range(len(values))},
+        )
+
     near = paired("near", [], blocks[:2])
     near_next = ring_step(near)
     far = call(
@@ -559,6 +570,7 @@
         out_specs=[vmem] * 2,
     )
     far_next = [ring_step(value) for value in far]
+    (far_next[1],) = tie([far_next[1]], [far_next[0]])
     streams = (2, 1)
     rings, partial = [], []
     for part in range(2):
@@ -585,17 +597,6 @@
     for ring in rings:
         ring.append([ring_step(value) for value in ring[-1]])
     rings[0].append([ring_step(value) for value in rings[0][-1]])
-
-    def tie(values, deps):
-        return call(
-            tie_kernel,
-            "tie",
-            [shape(value.shape, kind) for value in values],
-            [anywhere] * (len(values) + len(deps)),
-            list(values) + list(deps),
-            out_specs=[anywhere] * len(values),
-            input_output_aliases={i: i for i in range(len(values))},
-        )
 
     mine = call(
         functools.partial(first_kernel, turns),

time: 108 us -> 111 us (1.028)
  waiting for transfers between devices: 37.9 us -> 44.7 us
  starting transfers between devices: 39.9 us -> 35.6 us
    ppermute x9, waiting for transfers between devices: 16.3 us -> 22.1 us  [ring_step(): return lax.ppermute(value, 'dp', pairs)]
    ppermute x9, starting transfers between devices: 16 us -> 13.8 us  [ring_step(): return lax.ppermute(value, 'dp', pairs)]
    ppermute x3, starting transfers between devices: 4.44 us -> 2.61 us  [shifted(): lax.ppermute(value, axis, [(source, (source + shift) % count) for source...]
    pallas_call x26 -> x27, Pallas kernels: 29.1 us -> 29.1 us  [call(): pl.pallas_call(kernel, out_shape=out_shape, in_specs=in_specs, scratch_sh...]
  transfers between devices with their start and end apart: 42 -> 42, of which waited for: 19 -> 21; matrix products, arithmetic and copies ran while one was open for 0% -> 0% of each run, Pallas kernels for 24% -> 23%
where the time goes in v21:
time: 111 us
  waiting for transfers between devices  44.7 us (40%)
  starting transfers between devices  35.6 us (32%)
  Pallas kernels  29.1 us (26%)
  between operations  1.16 us (1%)
    pallas_call x27, Pallas kernels, call(): pl.pallas_call(kernel, out_shape=out_shape, in_specs=in_specs, scratch_sh...  29.1 us
    ppermute x9, waiting for transfers between devices, ring_step(): return lax.ppermute(value, 'dp', pairs)  22.1 us
    ppermute x26, starting transfers between devices, swap(): lax.ppermute(value, 'seq', [(source, source ^ bit) for source in range(co...  14 us
    ppermute x9, starting transfers between devices, ring_step(): return lax.ppermute(value, 'dp', pairs)  13.8 us
    ppermute x26, waiting for transfers between devices, swap(): lax.ppermute(value, 'seq', [(source, source ^ bit) for source in range(co...  13.4 us
    ppermute x4, starting transfers between devices, handed_over(): return lax.ppermute(value, 'pipe', [(0, 1), (1, 0)])  5.19 us
    ppermute x4, waiting for transfers between devices, handed_over(): return lax.ppermute(value, 'pipe', [(0, 1), (1, 0)])  4.84 us
    ppermute x3, waiting for transfers between devices, shifted(): lax.ppermute(value, axis, [(source, (source + shift) % count) for source...  4.37 us
  transfers between devices with their start and end apart: 42, of which 21 were waited for; matrix products, arithmetic and copies ran while one was open for 0% of the time, Pallas kernels for 23%

profile of v21, /device:TPU:0, one launch (start us, length us, event | category | flops | bytes accessed | tf_op | source)
XLA Modules:
  0.0 110.7 jit_solution(2741456996172277487)
XLA Ops:
  0.7 1.5 %pack.1 = (bf16[2,96,384]{2,1,0:T(8,128)(2,1)S(1)}, bf16[2,96,384]{2,1,0:T(8,128)(2,1)S(1)}, bf16[2,96,384]{2,1,0:T(8,128)(2,1)S(1)}, bf16[2,96,384]{2,1,0:T(8,128)(2,1)S(1)}) custom-call(bf16[1,96,1536]{2,1,0:T(8,128)(2,1)} %wq.1, bf16[1,96,1536]{2,1,0:T(8,128)(2,1)} %wkv.1), custom_call_target="tpu_custom_call" | custom-call | tf_op jit(solution)/shard_map/pack/pallas_call | solution.py:511
  2.1 0.5 collective-permute-start
  2.7 1.0 collective-permute-done.refs_1_
  3.7 3.0 %collective-permute-start.1 = (bf16[2,2,96,384]{3,2,1,0:T(8,128)(2,1)S(1)}, bf16[2,2,96,384]{3,2,1,0:T(8,128)(2,1)S(1)}, u32[]{:S(2)}, u32[]{:S(2)}) collective-permute-start(bf16[2,2,96,384]{3,2,1,0:T(8,128)(2,1)S(1)} %near.1), channel_id=1, source_target_pairs={{0,1},{1,3},{3,2},{2,0},{4,5},{5,7},{7,6},{6,4},{8,9},{9,11},{11,1... | collective-permute-start | bytes 884744 | tf_op jit(solution)/shard_map/ppermute | solution.py:46
  6.7 1.5 %collective-permute-start.2 = (bf16[2,96,384]{2,1,0:T(8,128)(2,1)S(1)}, bf16[2,96,384]{2,1,0:T(8,128)(2,1)S(1)}, u32[]{:S(2)}, u32[]{:S(2)}) collective-permute-start(bf16[2,96,384]{2,1,0:T(8,128)(2,1)S(1)} %get-tuple-element.50), channel_id=1, source_target_pairs={{0,8},{4,12},{8,0},{12,4},{1,9},{5,13},{9,1},{13,5},{2,10},{6,14},... | collective-permute-start | bytes 442376 | tf_op jit(solution)/shard_map/ppermute | solution.py:27
  8.2 5.2 %collective-permute-done.2.first = bf16[2,96,384]{2,1,0:T(8,128)(2,1)S(1)} collective-permute-done((bf16[2,96,384]{2,1,0:T(8,128)(2,1)S(1)}, bf16[2,96,384]{2,1,0:T(8,128)(2,1)S(1)}, u32[]{:S(2)}, u32[]{:S(2)}) %collective-permute-start.2) | collective-permute-done | bytes 147488 | tf_op jit(solution)/shard_map/ppermute | solution.py:27
  13.4 1.1 collective-permute-done.3.second
  14.5 0.5 collective-permute-done.1.dep.near
  15.1 1.6 %collective-permute-start.4 = (bf16[272,1536]{1,0:T(8,128)(2,1)S(1)}, bf16[272,1536]{1,0:T(8,128)(2,1)S(1)}, u32[]{:S(2)}, u32[]{:S(2)}) collective-permute-start(bf16[272,1536]{1,0:T(8,128)(2,1)S(1)} %first.1.refs_0_), channel_id=1, source_target_pairs={{0,8},{4,12},{8,0},{12,4},{1,9},{5,13},{9,1},{13,5},{2,10},{6,14},... | collective-permute-start | bytes 2506760 | tf_op jit(solution)/shard_map/ppermute | solution.py:27
  16.7 1.9 %collective-permute-start.5 = (bf16[2,96,384]{2,1,0:T(8,128)(2,1)S(1)}, bf16[2,96,384]{2,1,0:T(8,128)(2,1)S(1)}, u32[]{:S(2)}, u32[]{:S(2)}) collective-permute-start(bf16[2,96,384]{2,1,0:T(8,128)(2,1)S(1)} %get-tuple-element.52.far), channel_id=1, source_target_pairs={{0,1},{1,3},{3,2},{2,0},{4,5},{5,7},{7,6},{6,4},{8,9},{9,11},{11,1... | collective-permute-start | bytes 442376 | tf_op jit(solution)/shard_map/ppermute | solution.py:46
  18.6 2.3 %collective-permute-start.8 = (bf16[2,96,384]{2,1,0:T(8,128)(2,1)S(1)}, bf16[2,96,384]{2,1,0:T(8,128)(2,1)S(1)}, u32[]{:S(2)}, u32[]{:S(2)}) collective-permute-start(bf16[2,96,384]{2,1,0:T(8,128)(2,1)S(1)} %get-tuple-element.55.far), channel_id=1, source_target_pairs={{0,1},{1,3},{3,2},{2,0},{4,5},{5,7},{7,6},{6,4},{8,9},{9,11},{11,1... | collective-permute-start | bytes 442376 | tf_op jit(solution)/shard_map/ppermute | solution.py:46
  20.9 3.2 %collective-permute-done.5.far.refs_1_ = bf16[2,96,384]{2,1,0:T(8,128)(2,1)S(1)} collective-permute-done((bf16[2,96,384]{2,1,0:T(8,128)(2,1)S(1)}, bf16[2,96,384]{2,1,0:T(8,128)(2,1)S(1)}, u32[]{:S(2)}, u32[]{:S(2)}) %collective-permute-start.5) | collective-permute-done | bytes 147488 | tf_op jit(solution)/shard_map/ppermute | solution.py:46
  24.2 2.3 %collective-permute-done.8.refs_0_ = bf16[2,96,384]{2,1,0:T(8,128)(2,1)S(1)} collective-permute-done((bf16[2,96,384]{2,1,0:T(8,128)(2,1)S(1)}, bf16[2,96,384]{2,1,0:T(8,128)(2,1)S(1)}, u32[]{:S(2)}, u32[]{:S(2)}) %collective-permute-start.8) | collective-permute-done | bytes 147488 | tf_op jit(solution)/shard_map/ppermute | solution.py:46
  26.5 1.7 %collective-permute-start.9 = (bf16[4,96,384]{2,1,0:T(8,128)(2,1)S(1)}, bf16[4,96,384]{2,1,0:T(8,128)(2,1)S(1)}, u32[]{:S(2)}, u32[]{:S(2)}) collective-permute-start(bf16[4,96,384]{2,1,0:T(8,128)(2,1)S(1)} %part1.1.refs_0_), channel_id=1, source_target_pairs={{0,1},{1,3},{3,2},{2,0},{4,5},{5,7},{7,6},{6,4},{8,9},{9,11},{11,1... | collective-permute-start | bytes 884744 | tf_op jit(solution)/shard_map/ppermute | solution.py:46
  28.3 1.7 %collective-permute-start.6 = (bf16[2,96,384]{2,1,0:T(8,128)(2,1)S(1)}, bf16[2,96,384]{2,1,0:T(8,128)(2,1)S(1)}, u32[]{:S(2)}, u32[]{:S(2)}) collective-permute-start(bf16[2,96,384]{2,1,0:T(8,128)(2,1)S(1)} %get-tuple-element.53.refs_0_), channel_id=1, source_target_pairs={{0,1},{1,3},{3,2},{2,0},{4,5},{5,7},{7,6},{6,4},{8,9},{9,11},{11,1... | collective-permute-start | bytes 442376 | tf_op jit(solution)/shard_map/ppermute | solution.py:46
  30.1 10.4 %collective-permute-done.6.refs_1_.refs_9_ = bf16[2,96,384]{2,1,0:T(8,128)(2,1)S(1)} collective-permute-done((bf16[2,96,384]{2,1,0:T(8,128)(2,1)S(1)}, bf16[2,96,384]{2,1,0:T(8,128)(2,1)S(1)}, u32[]{:S(2)}, u32[]{:S(2)}) %collective-permute-start.6) | collective-permute-done | bytes 147488 | tf_op jit(solution)/shard_map/ppermute | solution.py:46
  40.4 1.6 %collective-permute-done.7.refs_2_.refs_10_ = bf16[2,96,384]{2,1,0:T(8,128)(2,1)S(1)} collective-permute-done((bf16[2,96,384]{2,1,0:T(8,128)(2,1)S(1)}, bf16[2,96,384]{2,1,0:T(8,128)(2,1)S(1)}, u32[]{:S(2)}, u32[]{:S(2)}) %collective-permute-start.7) | collective-permute-done | bytes 147488 | tf_op jit(solution)/shard_map/ppermute | solution.py:46
  42.2 0.6 collective-permute-start.10
  42.8 1.2 %collective-permute-start.14 = (bf16[2,96,384]{2,1,0:T(8,128)(2,1)S(1)}, bf16[2,96,384]{2,1,0:T(8,128)(2,1)S(1)}, u32[]{:S(2)}, u32[]{:S(2)}) collective-permute-start(bf16[2,96,384]{2,1,0:T(8,128)(2,1)S(1)} %collective-permute-done.6.refs_1_.refs_9_), channel_id=1, source_target_pairs={{0,1},{1,3},{3,2},{2,0},{4,5},{5,7},{7,6},{6,4},{8,9},{9,11},{11,1... | collective-permute-start | bytes 442376 | tf_op jit(solution)/shard_map/ppermute | solution.py:46
  44.1 1.2 %collective-permute-start.15 = (bf16[2,96,384]{2,1,0:T(8,128)(2,1)S(1)}, bf16[2,96,384]{2,1,0:T(8,128)(2,1)S(1)}, u32[]{:S(2)}, u32[]{:S(2)}) collective-permute-start(bf16[2,96,384]{2,1,0:T(8,128)(2,1)S(1)} %collective-permute-done.7.refs_2_.refs_10_), channel_id=1, source_target_pairs={{0,1},{1,3},{3,2},{2,0},{4,5},{5,7},{7,6},{6,4},{8,9},{9,11},{11,1... | collective-permute-start | bytes 442376 | tf_op jit(solution)/shard_map/ppermute | solution.py:46
  45.3 3.3 %norm.1 = (bf16[512,1536]{1,0:T(8,128)(2,1)S(1)}, bf16[512,1536]{1,0:T(8,128)(2,1)S(1)}, f32[512,128]{1,0:T(8,128)S(1)}, f32[512,128]{1,0:T(8,128)S(1)}, f32[512...) custom-call(s32[1,4]{1,0:T(1,128)S(1)} %bitcast.5, ...), custom_call_target="tpu_custom_call" | custom-call | tf_op jit(solution)/shard_map/norm/pallas_call | solution.py:511
  48.7 0.8 collective-permute-start.13
  49.5 0.9 collective-permute-done.14.refs_11_
  50.4 3.2 %collective-permute-done.15.refs_12_ = bf16[2,96,384]{2,1,0:T(8,128)(2,1)S(1)} collective-permute-done((bf16[2,96,384]{2,1,0:T(8,128)(2,1)S(1)}, bf16[2,96,384]{2,1,0:T(8,128)(2,1)S(1)}, u32[]{:S(2)}, u32[]{:S(2)}) %collective-permute-start.15) | collective-permute-done | bytes 147488 | tf_op jit(solution)/shard_map/ppermute | solution.py:46
  53.6 2.8 %step0a.1 = (bf16[768,128]{1,0:T(8,128)(2,1)S(1)}, bf16[512,256]{1,0:T(8,128)(2,1)S(1)}, bf16[1536,384]{1,0:T(8,128)(2,1)S(1)}) custom-call(f32[1,16]{1,0:T(1,128)S(1)} %copy-done.8, s32[1,4]{1,0:T(1,128)S(1)} %bitcast.6, f32[1,1536]{1,0:T(1,128)S(1)} %copy-done.1, f32[1,1536]{1,0:T(1,128)S(1)} %copy-done.2, ...), custom_call_target="tpu_custom_call", output_to_operand_aliasing={{2}: (13, {})} | custom-call | flops 805306368 | bytes 1572864 | tf_op jit(solution)/shard_map/step0a/pallas_call | solution.py:511
  56.3 1.6 %collective-permute-start.16 = (bf16[768,128]{1,0:T(8,128)(2,1)S(1)}, bf16[768,128]{1,0:T(8,128)(2,1)S(1)}, u32[]{:S(2)}, u32[]{:S(2)}) collective-permute-start(bf16[768,128]{1,0:T(8,128)(2,1)S(1)} %get-tuple-element.59), channel_id=1, source_target_pairs={{0,16},{16,0},{1,17},{17,1},{2,18},{18,2},{3,19},{19,3},{4,20},{20... | collective-permute-start | bytes 589832 | tf_op jit(solution)/shard_map/ppermute | solution.py:31
  58.0 2.7 %step1a.1 = (bf16[768,128]{1,0:T(8,128)(2,1)S(1)}, bf16[512,256]{1,0:T(8,128)(2,1)S(1)}) custom-call(f32[1,16]{1,0:T(1,128)S(1)} %copy-done.8, s32[1,4]{1,0:T(1,128)S(1)} %bitcast.7, f32[1,1536]{1,0:T(1,128)S(1)} %copy-done.1, f32[1,1536]{1,0:T(1,128)S(1)} %copy-done.2, f32[1,1536]{1,0:T(1,128)S(1)} %copy-done.4, s32[4,1,512]{2,1,0:T(1,128)S(1)} %copy-done.3, ...), custom_call_target="tpu_custom_call" | custom-call | flops 805306368 | bytes 1572864 | tf_op jit(solution)/shard_map/step1a/pallas_call | solution.py:511
  60.6 1.4 %collective-permute-done.16.refs_1_.refs_10_ = bf16[768,128]{1,0:T(8,128)(2,1)S(1)} collective-permute-done((bf16[768,128]{1,0:T(8,128)(2,1)S(1)}, bf16[768,128]{1,0:T(8,128)(2,1)S(1)}, u32[]{:S(2)}, u32[]{:S(2)}) %collective-permute-start.16) | collective-permute-done | bytes 196640 | tf_op jit(solution)/shard_map/ppermute | solution.py:31
  62.1 2.8 %step0b.1 = (bf16[768,128]{1,0:T(8,128)(2,1)S(1)}, bf16[4,128,384]{2,1,0:T(8,128)(2,1)S(1)}, bf16[1536,384]{1,0:T(8,128)(2,1)S(1)}) custom-call(f32[1,16]{1,0:T(1,128)S(1)} %copy-done.8, s32[1,4]{1,0:T(1,128)S(1)} %bitcast.8, f32[1,1536]{1,0:T(1,128)S(1)} %copy-done.1, f32[1,1536]{1,0:T(1,128)S(1)} %copy-done.2, ...), custom_call_target="tpu_custom_call", output_to_operand_aliasing={{2}: (11, {})} | custom-call | flops 805306368 | bytes 1572864 | tf_op jit(solution)/shard_map/step0b/pallas_call | solution.py:511
  64.9 0.1 beside.1
  65.1 1.6 %collective-permute-start.21 = (bf16[768,128]{1,0:T(8,128)(2,1)S(1)}, bf16[768,128]{1,0:T(8,128)(2,1)S(1)}, u32[]{:S(2)}, u32[]{:S(2)}) collective-permute-start(bf16[768,128]{1,0:T(8,128)(2,1)S(1)} %get-tuple-element.68), channel_id=1, source_target_pairs={{0,16},{16,0},{1,17},{17,1},{2,18},{18,2},{3,19},{19,3},{4,20},{20... | collective-permute-start | bytes 589832 | tf_op jit(solution)/shard_map/ppermute | solution.py:31
  66.7 0.5 collective-permute-start.25
  67.2 1.4 %collective-permute-start.18 = (bf16[768,128]{1,0:T(8,128)(2,1)S(1)}, bf16[768,128]{1,0:T(8,128)(2,1)S(1)}, u32[]{:S(2)}, u32[]{:S(2)}) collective-permute-start(bf16[768,128]{1,0:T(8,128)(2,1)S(1)} %collective-permute-done.16.refs_1_.refs_10_), channel_id=1, source_target_pairs={{0,8},{4,12},{8,0},{12,4},{1,9},{5,13},{9,1},{13,5},{2,10},{6,14},... | collective-permute-start | bytes 589832 | tf_op jit(solution)/shard_map/ppermute | solution.py:27
  68.6 2.7 %step1b.1 = (bf16[768,128]{1,0:T(8,128)(2,1)S(1)}, bf16[4,128,384]{2,1,0:T(8,128)(2,1)S(1)}) custom-call(f32[1,16]{1,0:T(1,128)S(1)} %copy-done.8, s32[1,4]{1,0:T(1,128)S(1)} %bitcast.9, f32[1,1536]{1,0:T(1,128)S(1)} %copy-done.1, f32[1,1536]{1,0:T(1,128)S(1)} %copy-done.2, f32[1,1536]{1,0:T(1,128)S(1)} %copy-done.4, s32[4,1,512]{2,1,0:T(1,128)S(1)} %copy-done.3, ...), custom_call_target="tpu_custom_call" | custom-call | flops 805306368 | bytes 1572864 | tf_op jit(solution)/shard_map/step1b/pallas_call | solution.py:511
  71.3 1.5 %collective-permute-done.21.refs_0_ = bf16[768,128]{1,0:T(8,128)(2,1)S(1)} collective-permute-done((bf16[768,128]{1,0:T(8,128)(2,1)S(1)}, bf16[768,128]{1,0:T(8,128)(2,1)S(1)}, u32[]{:S(2)}, u32[]{:S(2)}) %collective-permute-start.21) | collective-permute-done | bytes 196640 | tf_op jit(solution)/shard_map/ppermute | solution.py:31
  72.8 1.4 %collective-permute-start.22 = (bf16[768,128]{1,0:T(8,128)(2,1)S(1)}, bf16[768,128]{1,0:T(8,128)(2,1)S(1)}, u32[]{:S(2)}, u32[]{:S(2)}) collective-permute-start(bf16[768,128]{1,0:T(8,128)(2,1)S(1)} %tie.10.refs_14_), channel_id=1, source_target_pairs={{0,8},{4,12},{8,0},{12,4},{1,9},{5,13},{9,1},{13,5},{2,10},{6,14},... | collective-permute-start | bytes 589832 | tf_op jit(solution)/shard_map/ppermute | solution.py:27
  74.3 1.5 %collective-permute-start.27 = (bf16[768,128]{1,0:T(8,128)(2,1)S(1)}, bf16[768,128]{1,0:T(8,128)(2,1)S(1)}, u32[]{:S(2)}, u32[]{:S(2)}) collective-permute-start(bf16[768,128]{1,0:T(8,128)(2,1)S(1)} %get-tuple-element.73), channel_id=1, source_target_pairs={{0,16},{16,0},{1,17},{17,1},{2,18},{18,2},{3,19},{19,3},{4,20},{20... | collective-permute-start | bytes 589832 | tf_op jit(solution)/shard_map/ppermute | solution.py:31
  75.8 0.2 collective-permute-start.20
  76.0 0.6 collective-permute-done.25.refs_0_
  76.6 2.3 %collective-permute-done.22.refs_15_ = bf16[768,128]{1,0:T(8,128)(2,1)S(1)} collective-permute-done((bf16[768,128]{1,0:T(8,128)(2,1)S(1)}, bf16[768,128]{1,0:T(8,128)(2,1)S(1)}, u32[]{:S(2)}, u32[]{:S(2)}) %collective-permute-start.22) | collective-permute-done | bytes 196640 | tf_op jit(solution)/shard_map/ppermute | solution.py:27
  78.9 1.4 %collective-permute-start.26 = (bf16[768,128]{1,0:T(8,128)(2,1)S(1)}, bf16[768,128]{1,0:T(8,128)(2,1)S(1)}, u32[]{:S(2)}, u32[]{:S(2)}) collective-permute-start(bf16[768,128]{1,0:T(8,128)(2,1)S(1)} %collective-permute-done.25.refs_0_), channel_id=1, source_target_pairs={{0,8},{4,12},{8,0},{12,4},{1,9},{5,13},{9,1},{13,5},{2,10},{6,14},... | collective-permute-start | bytes 589832 | tf_op jit(solution)/shard_map/ppermute | solution.py:27
  80.3 1.3 %collective-permute-done.27.refs_2_ = bf16[768,128]{1,0:T(8,128)(2,1)S(1)} collective-permute-done((bf16[768,128]{1,0:T(8,128)(2,1)S(1)}, bf16[768,128]{1,0:T(8,128)(2,1)S(1)}, u32[]{:S(2)}, u32[]{:S(2)}) %collective-permute-start.27) | collective-permute-done | bytes 196640 | tf_op jit(solution)/shard_map/ppermute | solution.py:31
  81.6 0.7 collective-permute-start.28
  82.2 4.9 %step2ab.1.refs_2_.refs_0_ = bf16[4,128,384]{2,1,0:T(8,128)(2,1)S(1)} custom-call(f32[1,16]{1,0:T(1,128)S(1)} %copy-done.8, s32[1,4]{1,0:T(1,128)S(1)} %bitcast.10, f32[1,1536]{1,0:T(1,128)S(1)} %copy-done.1, f32[1,1536]{1,0:T(1,128)S(1)} %copy-done.2, f32[1,1536]{1,0:T(1,128)S(1)} %copy-done.4, s32[4,1,512]{2,1,0:T(1,128)S(1)} %copy-done.3, ...), custom_call_target="tpu_custom_call" | custom-call | flops 1610612736 | bytes 3145728 | tf_op jit(solution)/shard_map/step2ab/pallas_call | solution.py:511
  87.1 0.5 early.1
  87.7 2.7 %collective-permute-done.28.refs_3_ = bf16[768,128]{1,0:T(8,128)(2,1)S(1)} collective-permute-done((bf16[768,128]{1,0:T(8,128)(2,1)S(1)}, bf16[768,128]{1,0:T(8,128)(2,1)S(1)}, u32[]{:S(2)}, u32[]{:S(2)}) %collective-permute-start.28) | collective-permute-done | bytes 196640 | tf_op jit(solution)/shard_map/ppermute | solution.py:27
  90.4 0.5 collective-permute-start.30
  90.9 0.5 collective-permute-start.32
  91.4 0.4 collective-permute-done.29.refs_12_
  91.8 1.4 %collective-permute-start.34 = (bf16[2,128,384]{2,1,0:T(8,128)(2,1)S(1)}, bf16[2,128,384]{2,1,0:T(8,128)(2,1)S(1)}, u32[]{:S(2)}, u32[]{:S(2)}) collective-permute-start(bf16[2,128,384]{2,1,0:T(8,128)(2,1)S(1)} %get-tuple-element.81), channel_id=1, source_target_pairs={{0,8},{4,12},{8,0},{12,4},{1,9},{5,13},{9,1},{13,5},{2,10},{6,14},... | collective-permute-start | bytes 589832 | tf_op jit(solution)/shard_map/ppermute | solution.py:27
  93.3 0.1 collective-permute-start.35
  93.4 4.7 %step3ab.1.refs_1_ = bf16[4,128,384]{2,1,0:T(8,128)(2,1)S(1)} custom-call(f32[1,16]{1,0:T(1,128)S(1)} %copy-done.8, s32[1,4]{1,0:T(1,128)S(1)} %bitcast.11, f32[1,1536]{1,0:T(1,128)S(1)} %copy-done.1, f32[1,1536]{1,0:T(1,128)S(1)} %copy-done.2, f32[1,1536]{1,0:T(1,128)S(1)} %copy-done.4, s32[4,1,512]{2,1,0:T(1,128)S(1)} %copy-done.3, ...), custom_call_target="tpu_custom_call" | custom-call | flops 1610612736 | bytes 3145728 | tf_op jit(solution)/shard_map/step3ab/pallas_call | solution.py:511
  98.0 0.4 share.1
  98.4 0.5 collective-permute-start.39
  98.9 0.6 collective-permute-done.34.refs_4_
  99.6 1.0 settle.1
  100.6 1.5 %collective-permute-start.37 = (bf16[128,384]{1,0:T(8,128)(2,1)S(1)}, bf16[128,384]{1,0:T(8,128)(2,1)S(1)}, u32[]{:S(2)}, u32[]{:S(2)}) collective-permute-start(bf16[128,384]{1,0:T(8,128)(2,1)S(1)} %get-tuple-element.86), channel_id=1, source_target_pairs={{0,8},{4,12},{8,0},{12,4},{1,9},{5,13},{9,1},{13,5},{2,10},{6,14},... | collective-permute-start | bytes 294920 | tf_op jit(solution)/shard_map/ppermute | solution.py:27
  102.1 0.4 collective-permute-start.38
  102.5 1.4 %collective-permute-start.40 = (bf16[96,256]{1,0:T(8,128)(2,1)S(1)}, bf16[96,256]{1,0:T(8,128)(2,1)S(1)}, u32[]{:S(2)}, u32[]{:S(2)}) collective-permute-start(bf16[96,256]{1,0:T(8,128)(2,1)S(1)} %get-tuple-element.90), channel_id=1, source_target_pairs={{0,2},{1,3},{2,0},{3,1},{4,6},{5,7},{6,4},{7,5},{8,10},{9,11},{10,... | collective-permute-start | bytes 147464 | tf_op jit(solution)/shard_map/ppermute | solution.py:36
  103.9 0.7 collective-permute-done.39.refs_7_
  104.5 0.7 collective-permute-start.41
  105.3 3.5 %collective-permute-done.40.refs_8_ = bf16[96,256]{1,0:T(8,128)(2,1)S(1)} collective-permute-done((bf16[96,256]{1,0:T(8,128)(2,1)S(1)}, bf16[96,256]{1,0:T(8,128)(2,1)S(1)}, u32[]{:S(2)}, u32[]{:S(2)}) %collective-permute-start.40) | collective-permute-done | bytes 49184 | tf_op jit(solution)/shard_map/ppermute | solution.py:36
  108.7 0.2 collective-permute-done.41.refs_9_
  109.0 1.5 %finish.1 = (bf16[3,128,1536]{2,1,0:T(8,128)(2,1)}, f32[96,256]{1,0:T(8,128)}) custom-call(bf16[3,128,1536]{2,1,0:T(8,128)(2,1)} %get-tuple-element.82.refs_0_, bf16[2,128,384]{2,1,0:T(8,128)(2,1)S(1)} %collective-permute-done.35.refs_1_, bf16[128,384]{1,0:T(8,128)(2,1)S(1)} %get-tuple-element.84.refs_2_, ...), custom_call_target="tpu_custom_call", output_to_operand_aliasing={{0}: (0, {})} | custom-call | tf_op jit(solution)/shard_map/finish/pallas_call | solution.py:511
  (67 shorter events, 0.8 us)
Async XLA Ops:
  0.6 14.4 %copy-start = (bf16[1,3,1,128,1536]{4,3,2,1,0:T(8,128)(2,1)S(1)}, bf16[1,3,1,128,1536]{4,3,2,1,0:T(8,128)(2,1)}, u32[]{:S(2)}) copy-start(bf16[1,3,1,128,1536]{4,3,2,1,0:T(8,128)(2,1)} %incoming.3) | copy-start | bytes 3538948
  0.6 14.4 %copy-start.9 = (s32[4,1,128]{2,1,0:T(1,128)S(1)}, s32[4,1,128]{2,1,0:T(1,128)}, u32[]{:S(2)}) copy-start(s32[4,1,128]{2,1,0:T(1,128)} %contacts.1) | copy-start | bytes 6148
  2.1 1.5 %collective-permute-start = (bf16[2,96,384]{2,1,0:T(8,128)(2,1)S(1)}, bf16[2,96,384]{2,1,0:T(8,128)(2,1)S(1)}, u32[]{:S(2)}, u32[]{:S(2)}) collective-permute-start(bf16[2,96,384]{2,1,0:T(8,128)(2,1)S(1)} %get-tuple-element.49), channel_id=1, source_target_pairs={{0,4},{4,0},{8,12},{12,8},{1,5},{5,1},{9,13},{13,9},{2,6},{6,2},{1... | collective-permute-start | bytes 442376 | tf_op jit(solution)/shard_map/ppermute | solution.py:27
  3.7 11.3 %collective-permute-start.1 = (bf16[2,2,96,384]{3,2,1,0:T(8,128)(2,1)S(1)}, bf16[2,2,96,384]{3,2,1,0:T(8,128)(2,1)S(1)}, u32[]{:S(2)}, u32[]{:S(2)}) collective-permute-start(bf16[2,2,96,384]{3,2,1,0:T(8,128)(2,1)S(1)} %near.1), channel_id=1, source_target_pairs={{0,1},{1,3},{3,2},{2,0},{4,5},{5,7},{7,6},{6,4},{8,9},{9,11},{11,1... | collective-permute-start | bytes 884744 | tf_op jit(solution)/shard_map/ppermute | solution.py:46
  6.7 6.7 %collective-permute-start.2 = (bf16[2,96,384]{2,1,0:T(8,128)(2,1)S(1)}, bf16[2,96,384]{2,1,0:T(8,128)(2,1)S(1)}, u32[]{:S(2)}, u32[]{:S(2)}) collective-permute-start(bf16[2,96,384]{2,1,0:T(8,128)(2,1)S(1)} %get-tuple-element.50), channel_id=1, source_target_pairs={{0,8},{4,12},{8,0},{12,4},{1,9},{5,13},{9,1},{13,5},{2,10},{6,14},... | collective-permute-start | bytes 442376 | tf_op jit(solution)/shard_map/ppermute | solution.py:27
  8.2 6.3 %collective-permute-start.3 = (bf16[2,96,384]{2,1,0:T(8,128)(2,1)S(1)}, bf16[2,96,384]{2,1,0:T(8,128)(2,1)S(1)}, u32[]{:S(2)}, u32[]{:S(2)}) collective-permute-start(bf16[2,96,384]{2,1,0:T(8,128)(2,1)S(1)} %get-tuple-element.51), channel_id=1, source_target_pairs={{0,12},{4,8},{8,4},{12,0},{1,13},{5,9},{9,5},{13,1},{2,14},{6,10},... | collective-permute-start | bytes 442376 | tf_op jit(solution)/shard_map/ppermute | solution.py:27
  15.1 26.9 %collective-permute-start.4 = (bf16[272,1536]{1,0:T(8,128)(2,1)S(1)}, bf16[272,1536]{1,0:T(8,128)(2,1)S(1)}, u32[]{:S(2)}, u32[]{:S(2)}) collective-permute-start(bf16[272,1536]{1,0:T(8,128)(2,1)S(1)} %first.1.refs_0_), channel_id=1, source_target_pairs={{0,8},{4,12},{8,0},{12,4},{1,9},{5,13},{9,1},{13,5},{2,10},{6,14},... | collective-permute-start | bytes 2506760 | tf_op jit(solution)/shard_map/ppermute | solution.py:27
  16.7 7.4 %collective-permute-start.5 = (bf16[2,96,384]{2,1,0:T(8,128)(2,1)S(1)}, bf16[2,96,384]{2,1,0:T(8,128)(2,1)S(1)}, u32[]{:S(2)}, u32[]{:S(2)}) collective-permute-start(bf16[2,96,384]{2,1,0:T(8,128)(2,1)S(1)} %get-tuple-element.52.far), channel_id=1, source_target_pairs={{0,1},{1,3},{3,2},{2,0},{4,5},{5,7},{7,6},{6,4},{8,9},{9,11},{11,1... | collective-permute-start | bytes 442376 | tf_op jit(solution)/shard_map/ppermute | solution.py:46
  18.6 7.9 %collective-permute-start.8 = (bf16[2,96,384]{2,1,0:T(8,128)(2,1)S(1)}, bf16[2,96,384]{2,1,0:T(8,128)(2,1)S(1)}, u32[]{:S(2)}, u32[]{:S(2)}) collective-permute-start(bf16[2,96,384]{2,1,0:T(8,128)(2,1)S(1)} %get-tuple-element.55.far), channel_id=1, source_target_pairs={{0,1},{1,3},{3,2},{2,0},{4,5},{5,7},{7,6},{6,4},{8,9},{9,11},{11,1... | collective-permute-start | bytes 442376 | tf_op jit(solution)/shard_map/ppermute | solution.py:46
  26.5 15.5 %collective-permute-start.9 = (bf16[4,96,384]{2,1,0:T(8,128)(2,1)S(1)}, bf16[4,96,384]{2,1,0:T(8,128)(2,1)S(1)}, u32[]{:S(2)}, u32[]{:S(2)}) collective-permute-start(bf16[4,96,384]{2,1,0:T(8,128)(2,1)S(1)} %part1.1.refs_0_), channel_id=1, source_target_pairs={{0,1},{1,3},{3,2},{2,0},{4,5},{5,7},{7,6},{6,4},{8,9},{9,11},{11,1... | collective-permute-start | bytes 884744 | tf_op jit(solution)/shard_map/ppermute | solution.py:46
  28.3 13.8 %copy-start.5 = (bf16[1,3,1,128,256]{4,3,2,1,0:T(8,128)(2,1)S(1)}, bf16[1,3,1,128,256]{4,3,2,1,0:T(8,128)(2,1)}, u32[]{:S(2)}) copy-start(bf16[1,3,1,128,256]{4,3,2,1,0:T(8,128)(2,1)} %cotangent.1) | copy-start | bytes 589828
  28.3 12.1 %collective-permute-start.6 = (bf16[2,96,384]{2,1,0:T(8,128)(2,1)S(1)}, bf16[2,96,384]{2,1,0:T(8,128)(2,1)S(1)}, u32[]{:S(2)}, u32[]{:S(2)}) collective-permute-start(bf16[2,96,384]{2,1,0:T(8,128)(2,1)S(1)} %get-tuple-element.53.refs_0_), channel_id=1, source_target_pairs={{0,1},{1,3},{3,2},{2,0},{4,5},{5,7},{7,6},{6,4},{8,9},{9,11},{11,1... | collective-permute-start | bytes 442376 | tf_op jit(solution)/shard_map/ppermute | solution.py:46
  30.0 12.0 %collective-permute-start.7 = (bf16[2,96,384]{2,1,0:T(8,128)(2,1)S(1)}, bf16[2,96,384]{2,1,0:T(8,128)(2,1)S(1)}, u32[]{:S(2)}, u32[]{:S(2)}) collective-permute-start(bf16[2,96,384]{2,1,0:T(8,128)(2,1)S(1)} %get-tuple-element.54.refs_1_), channel_id=1, source_target_pairs={{0,1},{1,3},{3,2},{2,0},{4,5},{5,7},{7,6},{6,4},{8,9},{9,11},{11,1... | collective-permute-start | bytes 442376 | tf_op jit(solution)/shard_map/ppermute | solution.py:46
  30.1 15.2 %collective-permute-start.11 = (bf16[272,1536]{1,0:T(8,128)(2,1)S(1)}, bf16[272,1536]{1,0:T(8,128)(2,1)S(1)}, u32[]{:S(2)}, u32[]{:S(2)}) collective-permute-start(bf16[272,1536]{1,0:T(8,128)(2,1)S(1)} %first.1.refs_0_), channel_id=1, source_target_pairs={{0,4},{4,0},{8,12},{12,8},{1,5},{5,1},{9,13},{13,9},{2,6},{6,2},{1... | collective-permute-start | bytes 2506760 | tf_op jit(solution)/shard_map/ppermute | solution.py:27
  42.0 3.2 %copy-start.1 = (f32[1,1536]{1,0:T(1,128)S(1)}, f32[1,1536]{1,0:T(1,128)}, u32[]{:S(2)}) copy-start(f32[1,1536]{1,0:T(1,128)} %refs_2_.11) | copy-start | bytes 18436
  42.0 3.2 %copy-start.2 = (f32[1,1536]{1,0:T(1,128)S(1)}, f32[1,1536]{1,0:T(1,128)}, u32[]{:S(2)}) copy-start(f32[1,1536]{1,0:T(1,128)} %refs_3_.11) | copy-start | bytes 18436
  42.0 3.2 %copy-start.6 = (bf16[1,16,1536]{2,1,0:T(8,128)(2,1)S(1)}, bf16[1,16,1536]{2,1,0:T(8,128)(2,1)}, u32[]{:S(2)}) copy-start(bf16[1,16,1536]{2,1,0:T(8,128)(2,1)} %table.1) | copy-start | bytes 147460
  42.1 3.2 %copy-start.7 = (s32[4,1]{0,1:T(1,128)S(1)}, s32[4,1]{0,1:T(1,128)}, u32[]{:S(2)}) copy-start(s32[4,1]{0,1:T(1,128)} %param.15) | copy-start | bytes 52
  42.1 3.2 %collective-permute-start.12 = (bf16[272,1536]{1,0:T(8,128)(2,1)S(1)}, bf16[272,1536]{1,0:T(8,128)(2,1)S(1)}, u32[]{:S(2)}, u32[]{:S(2)}) collective-permute-start(bf16[272,1536]{1,0:T(8,128)(2,1)S(1)} %tie.7.dep.refs_1_), channel_id=1, source_target_pairs={{0,4},{4,0},{8,12},{12,8},{1,5},{5,1},{9,13},{13,9},{2,6},{6,2},{1... | collective-permute-start | bytes 2506760 | tf_op jit(solution)/shard_map/ppermute | solution.py:27
  42.2 22.7 %collective-permute-start.10 = (bf16[256,1536]{1,0:T(8,128)(2,1)S(1)}, bf16[256,1536]{1,0:T(8,128)(2,1)S(1)}, u32[]{:S(2)}, u32[]{:S(2)}) collective-permute-start(bf16[256,1536]{1,0:T(8,128)(2,1)S(1)} %second.1.mine.refs_6_.refs_3_.refs_2_), channel_id=1, source_target_pairs={{0,8},{4,12},{8,0},{12,4},{1,9},{5,13},{9,1},{13,5},{2,10},{6,14},... | collective-permute-start | bytes 2359304 | tf_op jit(solution)/shard_map/ppermute | solution.py:27
  42.8 7.6 %collective-permute-start.14 = (bf16[2,96,384]{2,1,0:T(8,128)(2,1)S(1)}, bf16[2,96,384]{2,1,0:T(8,128)(2,1)S(1)}, u32[]{:S(2)}, u32[]{:S(2)}) collective-permute-start(bf16[2,96,384]{2,1,0:T(8,128)(2,1)S(1)} %collective-permute-done.6.refs_1_.refs_9_), channel_id=1, source_target_pairs={{0,1},{1,3},{3,2},{2,0},{4,5},{5,7},{7,6},{6,4},{8,9},{9,11},{11,1... | collective-permute-start | bytes 442376 | tf_op jit(solution)/shard_map/ppermute | solution.py:46
  44.1 9.5 %collective-permute-start.15 = (bf16[2,96,384]{2,1,0:T(8,128)(2,1)S(1)}, bf16[2,96,384]{2,1,0:T(8,128)(2,1)S(1)}, u32[]{:S(2)}, u32[]{:S(2)}) collective-permute-start(bf16[2,96,384]{2,1,0:T(8,128)(2,1)S(1)} %collective-permute-done.7.refs_2_.refs_10_), channel_id=1, source_target_pairs={{0,1},{1,3},{3,2},{2,0},{4,5},{5,7},{7,6},{6,4},{8,9},{9,11},{11,1... | collective-permute-start | bytes 442376 | tf_op jit(solution)/shard_map/ppermute | solution.py:46
  48.6 4.9 %copy-start.3 = (s32[4,1,512]{2,1,0:T(1,128)S(1)}, s32[4,1,512]{2,1,0:T(1,128)}, u32[]{:S(2)}) copy-start(s32[4,1,512]{2,1,0:T(1,128)} %refs_5_.11) | copy-start | bytes 24580
  48.6 4.9 %copy-start.4 = (f32[1,1536]{1,0:T(1,128)S(1)}, f32[1,1536]{1,0:T(1,128)}, u32[]{:S(2)}) copy-start(f32[1,1536]{1,0:T(1,128)} %refs_4_.11) | copy-start | bytes 18436
  48.7 4.9 %copy-start.8 = (f32[1,16]{1,0:T(1,128)S(1)}, f32[1,16]{1,0:T(1,128)}, u32[]{:S(2)}) copy-start(f32[1,16]{1,0:T(1,128)} %refs_0_.11) | copy-start | bytes 196
  48.7 13.4 %collective-permute-start.13 = (bf16[4,96,384]{2,1,0:T(8,128)(2,1)S(1)}, bf16[4,96,384]{2,1,0:T(8,128)(2,1)S(1)}, u32[]{:S(2)}, u32[]{:S(2)}) collective-permute-start(bf16[4,96,384]{2,1,0:T(8,128)(2,1)S(1)} %tie.8.refs_9_), channel_id=1, source_target_pairs={{0,1},{1,3},{3,2},{2,0},{4,5},{5,7},{7,6},{6,4},{8,9},{9,11},{11,1... | collective-permute-start | bytes 884744 | tf_op jit(solution)/shard_map/ppermute | solution.py:46
  56.3 5.7 %collective-permute-start.16 = (bf16[768,128]{1,0:T(8,128)(2,1)S(1)}, bf16[768,128]{1,0:T(8,128)(2,1)S(1)}, u32[]{:S(2)}, u32[]{:S(2)}) collective-permute-start(bf16[768,128]{1,0:T(8,128)(2,1)S(1)} %get-tuple-element.59), channel_id=1, source_target_pairs={{0,16},{16,0},{1,17},{17,1},{2,18},{18,2},{3,19},{19,3},{4,20},{20... | collective-permute-start | bytes 589832 | tf_op jit(solution)/shard_map/ppermute | solution.py:31
  65.0 7.8 %collective-permute-start.17 = (bf16[2,256,1536]{2,1,0:T(8,128)(2,1)S(1)}, bf16[2,256,1536]{2,1,0:T(8,128)(2,1)S(1)}, u32[]{:S(2)}, u32[]{:S(2)}) collective-permute-start(bf16[2,256,1536]{2,1,0:T(8,128)(2,1)S(1)} %beside.1), channel_id=1, source_target_pairs={{0,4},{4,0},{8,12},{12,8},{1,5},{5,1},{9,13},{13,9},{2,6},{6,2},{1... | collective-permute-start | bytes 4718600 | tf_op jit(solution)/shard_map/ppermute | solution.py:27
  65.1 7.8 %collective-permute-start.21 = (bf16[768,128]{1,0:T(8,128)(2,1)S(1)}, bf16[768,128]{1,0:T(8,128)(2,1)S(1)}, u32[]{:S(2)}, u32[]{:S(2)}) collective-permute-start(bf16[768,128]{1,0:T(8,128)(2,1)S(1)} %get-tuple-element.68), channel_id=1, source_target_pairs={{0,16},{16,0},{1,17},{17,1},{2,18},{18,2},{3,19},{19,3},{4,20},{20... | collective-permute-start | bytes 589832 | tf_op jit(solution)/shard_map/ppermute | solution.py:31
  66.7 9.9 %collective-permute-start.25 = (bf16[768,128]{1,0:T(8,128)(2,1)S(1)}, bf16[768,128]{1,0:T(8,128)(2,1)S(1)}, u32[]{:S(2)}, u32[]{:S(2)}) collective-permute-start(bf16[768,128]{1,0:T(8,128)(2,1)S(1)} %get-tuple-element.72), channel_id=1, source_target_pairs={{0,16},{16,0},{1,17},{17,1},{2,18},{18,2},{3,19},{19,3},{4,20},{20... | collective-permute-start | bytes 589832 | tf_op jit(solution)/shard_map/ppermute | solution.py:31
  67.2 8.6 %collective-permute-start.18 = (bf16[768,128]{1,0:T(8,128)(2,1)S(1)}, bf16[768,128]{1,0:T(8,128)(2,1)S(1)}, u32[]{:S(2)}, u32[]{:S(2)}) collective-permute-start(bf16[768,128]{1,0:T(8,128)(2,1)S(1)} %collective-permute-done.16.refs_1_.refs_10_), channel_id=1, source_target_pairs={{0,8},{4,12},{8,0},{12,4},{1,9},{5,13},{9,1},{13,5},{2,10},{6,14},... | collective-permute-start | bytes 589832 | tf_op jit(solution)/shard_map/ppermute | solution.py:27
  72.8 6.0 %collective-permute-start.22 = (bf16[768,128]{1,0:T(8,128)(2,1)S(1)}, bf16[768,128]{1,0:T(8,128)(2,1)S(1)}, u32[]{:S(2)}, u32[]{:S(2)}) collective-permute-start(bf16[768,128]{1,0:T(8,128)(2,1)S(1)} %tie.10.refs_14_), channel_id=1, source_target_pairs={{0,8},{4,12},{8,0},{12,4},{1,9},{5,13},{9,1},{13,5},{2,10},{6,14},... | collective-permute-start | bytes 589832 | tf_op jit(solution)/shard_map/ppermute | solution.py:27
  74.3 4.6 %collective-permute-start.19 = (bf16[768,128]{1,0:T(8,128)(2,1)S(1)}, bf16[768,128]{1,0:T(8,128)(2,1)S(1)}, u32[]{:S(2)}, u32[]{:S(2)}) collective-permute-start(bf16[768,128]{1,0:T(8,128)(2,1)S(1)} %collective-permute-done.16.refs_1_.refs_10_), channel_id=1, source_target_pairs={{0,4},{4,0},{8,12},{12,8},{1,5},{5,1},{9,13},{13,9},{2,6},{6,2},{1... | collective-permute-start | bytes 589832 | tf_op jit(solution)/shard_map/ppermute | solution.py:27
  74.3 7.3 %collective-permute-start.27 = (bf16[768,128]{1,0:T(8,128)(2,1)S(1)}, bf16[768,128]{1,0:T(8,128)(2,1)S(1)}, u32[]{:S(2)}, u32[]{:S(2)}) collective-permute-start(bf16[768,128]{1,0:T(8,128)(2,1)S(1)} %get-tuple-element.73), channel_id=1, source_target_pairs={{0,16},{16,0},{1,17},{17,1},{2,18},{18,2},{3,19},{19,3},{4,20},{20... | collective-permute-start | bytes 589832 | tf_op jit(solution)/shard_map/ppermute | solution.py:31
  75.8 6.5 %collective-permute-start.20 = (bf16[768,128]{1,0:T(8,128)(2,1)S(1)}, bf16[768,128]{1,0:T(8,128)(2,1)S(1)}, u32[]{:S(2)}, u32[]{:S(2)}) collective-permute-start(bf16[768,128]{1,0:T(8,128)(2,1)S(1)} %collective-permute-done.18.refs_11_), channel_id=1, source_target_pairs={{0,4},{4,0},{8,12},{12,8},{1,5},{5,1},{9,13},{13,9},{2,6},{6,2},{1... | collective-permute-start | bytes 589832 | tf_op jit(solution)/shard_map/ppermute | solution.py:27
  76.6 5.6 %collective-permute-start.23 = (bf16[768,128]{1,0:T(8,128)(2,1)S(1)}, bf16[768,128]{1,0:T(8,128)(2,1)S(1)}, u32[]{:S(2)}, u32[]{:S(2)}) collective-permute-start(bf16[768,128]{1,0:T(8,128)(2,1)S(1)} %tie.10.refs_14_), channel_id=1, source_target_pairs={{0,4},{4,0},{8,12},{12,8},{1,5},{5,1},{9,13},{13,9},{2,6},{6,2},{1... | collective-permute-start | bytes 589832 | tf_op jit(solution)/shard_map/ppermute | solution.py:27
  78.9 3.4 %collective-permute-start.24 = (bf16[768,128]{1,0:T(8,128)(2,1)S(1)}, bf16[768,128]{1,0:T(8,128)(2,1)S(1)}, u32[]{:S(2)}, u32[]{:S(2)}) collective-permute-start(bf16[768,128]{1,0:T(8,128)(2,1)S(1)} %collective-permute-done.22.refs_15_), channel_id=1, source_target_pairs={{0,4},{4,0},{8,12},{12,8},{1,5},{5,1},{9,13},{13,9},{2,6},{6,2},{1... | collective-permute-start | bytes 589832 | tf_op jit(solution)/shard_map/ppermute | solution.py:27
  78.9 8.8 %collective-permute-start.26 = (bf16[768,128]{1,0:T(8,128)(2,1)S(1)}, bf16[768,128]{1,0:T(8,128)(2,1)S(1)}, u32[]{:S(2)}, u32[]{:S(2)}) collective-permute-start(bf16[768,128]{1,0:T(8,128)(2,1)S(1)} %collective-permute-done.25.refs_0_), channel_id=1, source_target_pairs={{0,8},{4,12},{8,0},{12,4},{1,9},{5,13},{9,1},{13,5},{2,10},{6,14},... | collective-permute-start | bytes 589832 | tf_op jit(solution)/shard_map/ppermute | solution.py:27
  81.6 8.8 %collective-permute-start.28 = (bf16[768,128]{1,0:T(8,128)(2,1)S(1)}, bf16[768,128]{1,0:T(8,128)(2,1)S(1)}, u32[]{:S(2)}, u32[]{:S(2)}) collective-permute-start(bf16[768,128]{1,0:T(8,128)(2,1)S(1)} %collective-permute-done.27.refs_2_), channel_id=1, source_target_pairs={{0,8},{4,12},{8,0},{12,4},{1,9},{5,13},{9,1},{13,5},{2,10},{6,14},... | collective-permute-start | bytes 589832 | tf_op jit(solution)/shard_map/ppermute | solution.py:27
  90.4 1.4 %collective-permute-start.29 = (bf16[768,128]{1,0:T(8,128)(2,1)S(1)}, bf16[768,128]{1,0:T(8,128)(2,1)S(1)}, u32[]{:S(2)}, u32[]{:S(2)}) collective-permute-start(bf16[768,128]{1,0:T(8,128)(2,1)S(1)} %get-tuple-element.75.refs_10_), channel_id=1, source_target_pairs={{0,4},{4,0},{8,12},{12,8},{1,5},{5,1},{9,13},{13,9},{2,6},{6,2},{1... | collective-permute-start | bytes 589832 | tf_op jit(solution)/shard_map/ppermute | solution.py:27
  90.4 2.9 %collective-permute-start.30 = (bf16[768,128]{1,0:T(8,128)(2,1)S(1)}, bf16[768,128]{1,0:T(8,128)(2,1)S(1)}, u32[]{:S(2)}, u32[]{:S(2)}) collective-permute-start(bf16[768,128]{1,0:T(8,128)(2,1)S(1)} %get-tuple-element.76.refs_11_), channel_id=1, source_target_pairs={{0,4},{4,0},{8,12},{12,8},{1,5},{5,1},{9,13},{13,9},{2,6},{6,2},{1... | collective-permute-start | bytes 589832 | tf_op jit(solution)/shard_map/ppermute | solution.py:27
  90.9 2.5 %collective-permute-start.31 = (bf16[768,128]{1,0:T(8,128)(2,1)S(1)}, bf16[768,128]{1,0:T(8,128)(2,1)S(1)}, u32[]{:S(2)}, u32[]{:S(2)}) collective-permute-start(bf16[768,128]{1,0:T(8,128)(2,1)S(1)} %get-tuple-element.77.refs_14_), channel_id=1, source_target_pairs={{0,4},{4,0},{8,12},{12,8},{1,5},{5,1},{9,13},{13,9},{2,6},{6,2},{1... | collective-permute-start | bytes 589832 | tf_op jit(solution)/shard_map/ppermute | solution.py:27
  90.9 2.5 %collective-permute-start.32 = (bf16[768,128]{1,0:T(8,128)(2,1)S(1)}, bf16[768,128]{1,0:T(8,128)(2,1)S(1)}, u32[]{:S(2)}, u32[]{:S(2)}) collective-permute-start(bf16[768,128]{1,0:T(8,128)(2,1)S(1)} %get-tuple-element.78.refs_15_), channel_id=1, source_target_pairs={{0,4},{4,0},{8,12},{12,8},{1,5},{5,1},{9,13},{13,9},{2,6},{6,2},{1... | collective-permute-start | bytes 589832 | tf_op jit(solution)/shard_map/ppermute | solution.py:27
  91.4 7.5 %collective-permute-start.33 = (bf16[2,128,384]{2,1,0:T(8,128)(2,1)S(1)}, bf16[2,128,384]{2,1,0:T(8,128)(2,1)S(1)}, u32[]{:S(2)}, u32[]{:S(2)}) collective-permute-start(bf16[2,128,384]{2,1,0:T(8,128)(2,1)S(1)} %get-tuple-element.80), channel_id=1, source_target_pairs={{0,4},{4,0},{8,12},{12,8},{1,5},{5,1},{9,13},{13,9},{2,6},{6,2},{1... | collective-permute-start | bytes 589832 | tf_op jit(solution)/shard_map/ppermute | solution.py:27
  91.8 7.7 %collective-permute-start.34 = (bf16[2,128,384]{2,1,0:T(8,128)(2,1)S(1)}, bf16[2,128,384]{2,1,0:T(8,128)(2,1)S(1)}, u32[]{:S(2)}, u32[]{:S(2)}) collective-permute-start(bf16[2,128,384]{2,1,0:T(8,128)(2,1)S(1)} %get-tuple-element.81), channel_id=1, source_target_pairs={{0,8},{4,12},{8,0},{12,4},{1,9},{5,13},{9,1},{13,5},{2,10},{6,14},... | collective-permute-start | bytes 589832 | tf_op jit(solution)/shard_map/ppermute | solution.py:27
  93.3 9.2 %collective-permute-start.35 = (bf16[2,128,384]{2,1,0:T(8,128)(2,1)S(1)}, bf16[2,128,384]{2,1,0:T(8,128)(2,1)S(1)}, u32[]{:S(2)}, u32[]{:S(2)}) collective-permute-start(bf16[2,128,384]{2,1,0:T(8,128)(2,1)S(1)} %get-tuple-element.83), channel_id=1, source_target_pairs={{0,12},{4,8},{8,4},{12,0},{1,13},{5,9},{9,5},{13,1},{2,14},{6,10},... | collective-permute-start | bytes 589832 | tf_op jit(solution)/shard_map/ppermute | solution.py:27
  98.4 6.1 %collective-permute-start.39 = (bf16[96,256]{1,0:T(8,128)(2,1)S(1)}, bf16[96,256]{1,0:T(8,128)(2,1)S(1)}, u32[]{:S(2)}, u32[]{:S(2)}) collective-permute-start(bf16[96,256]{1,0:T(8,128)(2,1)S(1)} %get-tuple-element.89), channel_id=1, source_target_pairs={{0,1},{1,2},{2,3},{3,0},{4,5},{5,6},{6,7},{7,4},{8,9},{9,10},{10,1... | collective-permute-start | bytes 147464 | tf_op jit(solution)/shard_map/ppermute | solution.py:36
  100.6 8.4 %collective-permute-start.36 = (bf16[128,384]{1,0:T(8,128)(2,1)S(1)}, bf16[128,384]{1,0:T(8,128)(2,1)S(1)}, u32[]{:S(2)}, u32[]{:S(2)}) collective-permute-start(bf16[128,384]{1,0:T(8,128)(2,1)S(1)} %get-tuple-element.85), channel_id=1, source_target_pairs={{0,4},{4,0},{8,12},{12,8},{1,5},{5,1},{9,13},{13,9},{2,6},{6,2},{1... | collective-permute-start | bytes 294920 | tf_op jit(solution)/shard_map/ppermute | solution.py:27
  100.6 8.3 %collective-permute-start.37 = (bf16[128,384]{1,0:T(8,128)(2,1)S(1)}, bf16[128,384]{1,0:T(8,128)(2,1)S(1)}, u32[]{:S(2)}, u32[]{:S(2)}) collective-permute-start(bf16[128,384]{1,0:T(8,128)(2,1)S(1)} %get-tuple-element.86), channel_id=1, source_target_pairs={{0,8},{4,12},{8,0},{12,4},{1,9},{5,13},{9,1},{13,5},{2,10},{6,14},... | collective-permute-start | bytes 294920 | tf_op jit(solution)/shard_map/ppermute | solution.py:27
  102.1 6.9 %collective-permute-start.38 = (bf16[128,384]{1,0:T(8,128)(2,1)S(1)}, bf16[128,384]{1,0:T(8,128)(2,1)S(1)}, u32[]{:S(2)}, u32[]{:S(2)}) collective-permute-start(bf16[128,384]{1,0:T(8,128)(2,1)S(1)} %get-tuple-element.87), channel_id=1, source_target_pairs={{0,12},{4,8},{8,4},{12,0},{1,13},{5,9},{9,5},{13,1},{2,14},{6,10},... | collective-permute-start | bytes 294920 | tf_op jit(solution)/shard_map/ppermute | solution.py:27
  102.5 6.2 %collective-permute-start.40 = (bf16[96,256]{1,0:T(8,128)(2,1)S(1)}, bf16[96,256]{1,0:T(8,128)(2,1)S(1)}, u32[]{:S(2)}, u32[]{:S(2)}) collective-permute-start(bf16[96,256]{1,0:T(8,128)(2,1)S(1)} %get-tuple-element.90), channel_id=1, source_target_pairs={{0,2},{1,3},{2,0},{3,1},{4,6},{5,7},{6,4},{7,5},{8,10},{9,11},{10,... | collective-permute-start | bytes 147464 | tf_op jit(solution)/shard_map/ppermute | solution.py:36
  104.5 4.4 %collective-permute-start.41 = (bf16[96,256]{1,0:T(8,128)(2,1)S(1)}, bf16[96,256]{1,0:T(8,128)(2,1)S(1)}, u32[]{:S(2)}, u32[]{:S(2)}) collective-permute-start(bf16[96,256]{1,0:T(8,128)(2,1)S(1)} %get-tuple-element.91), channel_id=1, source_target_pairs={{0,3},{1,0},{2,1},{3,2},{4,7},{5,4},{6,5},{7,6},{8,11},{9,8},{10,9... | collective-permute-start | bytes 147464 | tf_op jit(solution)/shard_map/ppermute | solution.py:36
